TPU v7x, 32 devices: a whole 2x2x4 slice. The times are simulated.
32 devices in a mesh: ctx: 8 (over y, x, core), head: 4 (over z).
Axes of the slice: x: 2, y: 2, z: 4, core: 2. Of those that a mesh axis runs over, the one named last changes fastest.
Arguments:
- xbc: bfloat16 [2048, 20480], P(('ctx', 'head')), may hold values from -6 to 6
- dt_raw: bfloat16 [2048, 256], P(('ctx', 'head')), may hold values from -7.5 to -0.5
- conv_weight: float32 [4, 20480], replicated, may hold values from -0.6 to 0.6
- conv_bias: float32 [20480], replicated, may hold values from -0.7 to -0.3
- a_log: float32 [256], replicated, may hold values from -5.6 to 2.8
- dt_bias: float32 [256], replicated, may hold values from -0.5 to 0.5
- skip_gain: float32 [256], replicated, may hold values from 0.5 to 1.5
Outputs:
- mixed: bfloat16 [2048, 16384], P('ctx', 'head')
All inputs are finite; a program needn't handle non-finite values.
Results may differ from a plain program's by a relative error of at most 0.0067.
Values may be sent and summed in bfloat16 or wider, within the bound.
No kernel may reach another device: no remote copies, remote signals or barrier semaphores. Data moves between devices by JAX's collectives and lax.ppermute only.
A program may use at most 192 MiB of HBM per device.

v0:
```python
import jax
import jax.numpy as jnp
from jax import lax
from jax.sharding import PartitionSpec as P

HEADS = 256
HEAD_DIM = 64
STATE = 256
GROUPS = 8
BLOCK = 256


def from_behind(block, axis, distance):
    devices = range(lax.axis_size(axis))
    route = [(i - distance, i) for i in devices if i - distance in devices]
    return lax.ppermute(block, axis, route)


def carried_in(array, axis, combine, identity):
    length, index = (lax.axis_size(axis), lax.axis_index(axis))
    everything = jax.tree.map(lambda part: lax.all_gather(part, axis), array)
    start = jax.tree.map(
        lambda part, zero: jnp.broadcast_to(jnp.asarray(zero, part.dtype), part.shape),
        array,
        identity,
    )

    def hop(k, before):
        reached = k < index
        new = combine(before, jax.tree.map(lambda part: part[k], everything))
        return jax.tree.map(lambda a, b: jnp.where(reached, a, b), new, before)

    return lax.fori_loop(0, length, hop, start)


def convolve(rows, edge, weight, bias):
    count = rows.shape[0]
    wide = jnp.concatenate([edge, rows], 0).astype(jnp.float32)
    acc = bias[None, :] + weight[0] * wide[0:count]
    acc = acc + weight[1] * wide[1 : count + 1]
    acc = acc + weight[2] * wide[2 : count + 2]
    acc = acc + weight[3] * wide[3 : count + 3]
    return jax.nn.silu(acc).astype(jnp.bfloat16)


def rearrange_heads(rows, shards, per_dev, groups_dev, per_group):
    count = rows.shape[0]
    inner = HEADS * HEAD_DIM
    replicate_groups = max(1, per_group // per_dev)
    heads_part = rows[:, :inner].reshape(count, shards, per_dev * HEAD_DIM)
    b_part = rows[:, inner : inner + GROUPS * STATE].reshape(count, GROUPS, STATE)
    c_part = rows[:, inner + GROUPS * STATE :].reshape(count, GROUPS, STATE)
    b_part = jnp.repeat(b_part, replicate_groups, axis=1).reshape(count, shards, groups_dev * STATE)
    c_part = jnp.repeat(c_part, replicate_groups, axis=1).reshape(count, shards, groups_dev * STATE)
    return jnp.concatenate([heads_part, b_part, c_part], axis=2)


def inner_block(xs, bmat, cmat, steps, cum):
    size = xs.shape[0]
    lower = jnp.arange(size)[:, None] >= jnp.arange(size)[None, :]
    scores = jnp.einsum("qgn,kgn->gqk", cmat, bmat, preferred_element_type=jnp.float32)
    order = jnp.transpose(cum, (1, 2, 0))
    gap = order[..., :, None] - order[..., None, :]
    decay = jnp.exp(jnp.where(lower, gap, -jnp.inf))
    mixing = (scores[:, None] * decay * jnp.transpose(steps, (1, 2, 0))[..., None, :]).astype(
        jnp.bfloat16
    )
    local = jnp.einsum("gjqk,kgjp->qgjp", mixing, xs, preferred_element_type=jnp.float32)
    tail = jnp.exp(cum[size - 1][None] - cum) * steps
    loaded = (bmat[:, :, None, :].astype(jnp.float32) * tail[..., None]).astype(jnp.bfloat16)
    block_state = jnp.einsum("kgjn,kgjp->gjnp", loaded, xs, preferred_element_type=jnp.float32)
    return (local, block_state)


def on_device(xbc, dt_raw, conv_weight, conv_bias, a_log, dt_bias, skip_gain):
    tok = xbc.shape[0]
    shards = lax.axis_size("head")
    per_dev = HEADS // shards
    per_group = HEADS // GROUPS
    groups_dev = max(1, per_dev // per_group)
    heads_per_cluster = per_dev // groups_dev
    sent = rearrange_heads(xbc, shards, per_dev, groups_dev, per_group)
    mine, rates = (
        lax.all_to_all(sent, "head", split_axis=1, concat_axis=0, tiled=True),
        lax.all_to_all(
            dt_raw.reshape(tok, shards, per_dev), "head", split_axis=1, concat_axis=0, tiled=True
        ),
    )
    slab = tok * shards
    mine = mine.reshape(slab, mine.shape[2])
    rates = rates.reshape(slab, per_dev)
    shard = lax.axis_index("head")
    taps = lax.dynamic_index_in_dim(
        rearrange_heads(conv_weight, shards, per_dev, groups_dev, per_group),
        shard,
        1,
        keepdims=False,
    )
    offset = lax.dynamic_index_in_dim(
        rearrange_heads(conv_bias[None, :], shards, per_dev, groups_dev, per_group),
        shard,
        1,
        keepdims=False,
    )
    edge = from_behind(mine[slab - 3 :], "ctx", 1)
    mine = convolve(mine, edge, taps, offset[0])
    nchunk = slab // BLOCK
    width = per_dev * HEAD_DIM
    xs = mine[:, :width].reshape(nchunk, BLOCK, groups_dev, heads_per_cluster, HEAD_DIM)
    bmat = mine[:, width : width + groups_dev * STATE].reshape(nchunk, BLOCK, groups_dev, STATE)
    cmat = mine[:, width + groups_dev * STATE :].reshape(nchunk, BLOCK, groups_dev, STATE)
    first = shard * per_dev
    rate = (-jnp.exp(lax.dynamic_slice_in_dim(a_log, first, per_dev))).reshape(
        groups_dev, heads_per_cluster
    )
    bias_dt = lax.dynamic_slice_in_dim(dt_bias, first, per_dev).reshape(
        groups_dev, heads_per_cluster
    )
    skip = lax.dynamic_slice_in_dim(skip_gain, first, per_dev).reshape(
        groups_dev, heads_per_cluster
    )
    steps = jax.nn.softplus(
        rates.astype(jnp.float32).reshape(nchunk, BLOCK, groups_dev, heads_per_cluster) + bias_dt
    )
    cum = jnp.cumsum(steps * rate, axis=1)

    def block_step(carry, item):
        held, product = carry
        x_part, b_part, c_part, step_part, cum_part = item
        local, block_state = inner_block(x_part, b_part, c_part, step_part, cum_part)
        lifted = c_part.astype(jnp.float32)[:, :, None, :] * jnp.exp(cum_part)[..., None]
        carried = jnp.einsum("qgjn,gjnp->qgjp", lifted, held, precision=lax.Precision.HIGHEST)
        partial_out = local + carried + skip[..., None] * x_part.astype(jnp.float32)
        end = jnp.exp(cum_part[BLOCK - 1])
        return ((end[..., None, None] * held + block_state, product * end), (partial_out, product))

    zero_state = jnp.zeros((groups_dev, heads_per_cluster, STATE, HEAD_DIM), jnp.float32)
    unit = jnp.ones((groups_dev, heads_per_cluster), jnp.float32)
    (slab_state, slab_decay), (partials, product_in) = lax.scan(
        block_step, (zero_state, unit), (xs, bmat, cmat, steps, cum)
    )

    def combine(preceding_state, later):
        return (
            preceding_state[0] * later[0],
            later[0][..., None, None] * preceding_state[1] + later[1],
        )

    _, entering = carried_in((slab_decay, slab_state), "ctx", combine, (unit, zero_state))
    projected = jnp.einsum(
        "cqgn,gjnp->cqgjp", cmat.astype(jnp.float32), entering, precision=lax.Precision.HIGHEST
    )
    factor = jnp.exp(cum) * product_in[:, None]
    total = partials + factor[..., None] * projected
    return total.astype(jnp.bfloat16).reshape(slab, width)


def solution(mesh):
    in_specs = (P(("ctx", "head"), None), P(("ctx", "head"), None), P(), P(), P(), P(), P())
    out_specs = P("ctx", "head")
    return jax.shard_map(
        on_device, mesh=mesh, in_specs=in_specs, out_specs=out_specs, check_vma=False
    )
```

profile of v0, /device:TPU:13, one launch (start us, length us, event | category | flops | bytes accessed | tf_op | source)
XLA Modules:
  0.0 493.5 jit_solution(1455018574199788894)
XLA Ops:
  8.3 4.8 all-to-all-start.1
  35.4 47.7 %all-to-all-done = bf16[64,4,5120]{2,0,1:T(8,128)(2,1)S(1)} async-done(((bf16[64,4,5120]{2,0,1:T(8,128)(2,1)}), bf16[64,4,5120]{2,0,1:T(8,128)(2,1)S(1)}, u32[]{:S(2)}, u32[]{:S(2)}) %all-to-all-start) | async-done | bytes 2621472 | tf_op jit(solution)/shard_map/all_to_all | solution.py:84
  83.7 5.4 %collective-permute-start = (bf16[3,5120]{1,0:T(4,128)(2,1)}, bf16[3,5120]{1,0:T(4,128)(2,1)}, u32[]{:S(2)}, u32[]{:S(2)}) collective-permute-start(bf16[3,5120]{1,0:T(4,128)(2,1)} %slice.107), channel_id=1, source_target_pairs={{0,4},{4,8},{8,12},{12,16},{16,20},{20,24},{24,28},{1,5},{5,9},{9,... | collective-permute-start | bytes 92168 | tf_op jit(solution)/shard_map/ppermute | solution.py:16
  102.1 5.6 %fusion.21 = f32[2,32,256,64]{2,3,1,0:T(8,128)} fusion(bf16[256,2,32,64]{0,3,2,1:T(8,128)(2,1)S(1)} %bitcast.96, f32[256,2,32]{0,2,1:T(8,128)S(1)} %copy-done.4, f32[256,2,256]{2,0,1:T(8,128)} %copy.160, f32[2,32]{1,0:T(2,128)S(1)} %exponential_multiply_fusion), kind=kOutput, calls=%fused_computation.35 | convolution fusion | flops 546308096 | bytes 6881536 | tf_op jit(solution)/shard_map/while/body/eval_jaxpr/kgjn,kgjp->gjnp/dot_general | solution.py:71
  110.3 9.9 %all-gather = f32[8,1,2,32]{3,2,1,0:T(2,128)S(1)} all-gather(f32[1,1,2,32]{3,2,1,0:T(2,128)S(1)} %get-tuple-element.205), channel_id=2, replica_groups=mesh['ctx'=8,'head'=4] {'ctx'}, dimensions={0}, use_global_device_ids=true | all-gather | bytes 2304 | tf_op jit(solution)/shard_map/all_gather | solution.py:21
  121.7 7.2 %fusion.3 = f32[2,32,64,256]{3,2,1,0:T(8,128)} fusion(bf16[256,2,32,64]{0,3,2,1:T(8,128)(2,1)S(1)} %bitcast.97, f32[2,32,256]{2,1,0:T(8,128)} %copy.155, f32[2,32,256]{2,1,0:T(8,128)} %copy.151, f32[2,256,256]{2,1,0:T(8,128)S(1)} %fusion.40, pred[256,256]{1,0:T(8,128)(4,1)} %iota_compare_fusion), kind=kOutput, calls=%fused_computation.8 | convolution fusion | flops 557842432 | bytes 7012352 | tf_op jit(solution)/shard_map/while/body/eval_jaxpr/gjqk,kgjp->qgjp/dot_general | solution.py:68
  128.9 141.6 %all-gather.4.cloned.1.call-done = f32[16,32,256,64]{2,3,1,0:T(8,128)} async-done(((f32[2,32,256,64]{2,3,1,0:T(8,128)}), f32[16,32,256,64]{2,3,1,0:T(8,128)}) %all-gather.4.cloned.1.call-update) | async-done | bytes 33554448 | tf_op jit(solution)/shard_map/all_gather | solution.py:21
  270.5 184.1 %while.9 = (s32[]{:T(128)}, f32[2,32,256,64]{3,2,1,0:T(8,128)}, s32[]{:T(128)}, f32[8,2,32]{2,1,0:T(2,128)S(1)}, f32[8,2,32,256,64]{3,4,2,1,0:T(8,128)}, /*index=5*/s32[]{:T(128)}, s32[]{:T(128)}) while((s32[]{:T(128)}, f32[2,32,256,64]{3,2,1,0:T(8,128)}, s32[]{:T(128)}, f32[8,2,32]{2,1,0:T(2,128)S(1)}, ...), condition=%wide.region_3.4_spmd.clone, body=%wide.region_2.3_spmd.clone.sunk | while | flops 4194308 | bytes 29361008 | solution.py:33
  270.5 4.6 constant_dynamic-slice_fusion.2
  275.2 6.8 %copy.178 = f32[1,2,32,256,64]{4,3,2,1,0:T(8,128)} copy(f32[1,2,32,256,64]{3,4,2,1,0:T(8,128)} %constant_dynamic-slice_fusion.2) | data formatting | bytes 8388608 | tf_op jit(solution)/shard_map/while/body/eval_jaxpr/dynamic_slice | solution.py:30
  282.0 9.4 %fusion.49 = f32[2,32,256,64]{3,2,1,0:T(8,128)} fusion(f32[1,2,32,256,64]{4,3,2,1,0:T(8,128)} %copy.178, f32[2,32,256,64]{3,2,1,0:T(8,128)} %get-tuple-element.249, f32[2,32]{1,0:T(2,128)S(1)} %dynamic-slice_bitcast_fusion.2, pred[]{:T(512)S(6)} %compare.3, pred[]{:T(512)S(6)} %lt.36), kind=kLoop, calls=%fused_computation.1.clone.1 | loop fusion | flops 4194304 | bytes 12583170 | tf_op jit(solution)/shard_map/while/body/eval_jaxpr/jit(_where)/select_n | solution.py:31
  291.5 4.6 constant_dynamic-slice_fusion.2
  296.1 6.8 %copy.178 = f32[1,2,32,256,64]{4,3,2,1,0:T(8,128)} copy(f32[1,2,32,256,64]{3,4,2,1,0:T(8,128)} %constant_dynamic-slice_fusion.2) | data formatting | bytes 8388608 | tf_op jit(solution)/shard_map/while/body/eval_jaxpr/dynamic_slice | solution.py:30
  302.9 11.8 %fusion.49 = f32[2,32,256,64]{3,2,1,0:T(8,128)} fusion(f32[1,2,32,256,64]{4,3,2,1,0:T(8,128)} %copy.178, f32[2,32,256,64]{3,2,1,0:T(8,128)} %get-tuple-element.249, f32[2,32]{1,0:T(2,128)S(1)} %dynamic-slice_bitcast_fusion.2, pred[]{:T(512)S(6)} %compare.3, pred[]{:T(512)S(6)} %lt.36), kind=kLoop, calls=%fused_computation.1.clone.1 | loop fusion | flops 4194304 | bytes 12583170 | tf_op jit(solution)/shard_map/while/body/eval_jaxpr/jit(_where)/select_n | solution.py:31
  314.8 4.6 constant_dynamic-slice_fusion.2
  319.4 6.8 %copy.178 = f32[1,2,32,256,64]{4,3,2,1,0:T(8,128)} copy(f32[1,2,32,256,64]{3,4,2,1,0:T(8,128)} %constant_dynamic-slice_fusion.2) | data formatting | bytes 8388608 | tf_op jit(solution)/shard_map/while/body/eval_jaxpr/dynamic_slice | solution.py:30
  326.3 11.8 %fusion.49 = f32[2,32,256,64]{3,2,1,0:T(8,128)} fusion(f32[1,2,32,256,64]{4,3,2,1,0:T(8,128)} %copy.178, f32[2,32,256,64]{3,2,1,0:T(8,128)} %get-tuple-element.249, f32[2,32]{1,0:T(2,128)S(1)} %dynamic-slice_bitcast_fusion.2, pred[]{:T(512)S(6)} %compare.3, pred[]{:T(512)S(6)} %lt.36), kind=kLoop, calls=%fused_computation.1.clone.1 | loop fusion | flops 4194304 | bytes 12583170 | tf_op jit(solution)/shard_map/while/body/eval_jaxpr/jit(_where)/select_n | solution.py:31
  338.1 4.6 constant_dynamic-slice_fusion.2
  342.7 6.8 %copy.178 = f32[1,2,32,256,64]{4,3,2,1,0:T(8,128)} copy(f32[1,2,32,256,64]{3,4,2,1,0:T(8,128)} %constant_dynamic-slice_fusion.2) | data formatting | bytes 8388608 | tf_op jit(solution)/shard_map/while/body/eval_jaxpr/dynamic_slice | solution.py:30
  349.6 11.8 %fusion.49 = f32[2,32,256,64]{3,2,1,0:T(8,128)} fusion(f32[1,2,32,256,64]{4,3,2,1,0:T(8,128)} %copy.178, f32[2,32,256,64]{3,2,1,0:T(8,128)} %get-tuple-element.249, f32[2,32]{1,0:T(2,128)S(1)} %dynamic-slice_bitcast_fusion.2, pred[]{:T(512)S(6)} %compare.3, pred[]{:T(512)S(6)} %lt.36), kind=kLoop, calls=%fused_computation.1.clone.1 | loop fusion | flops 4194304 | bytes 12583170 | tf_op jit(solution)/shard_map/while/body/eval_jaxpr/jit(_where)/select_n | solution.py:31
  361.4 4.6 constant_dynamic-slice_fusion.2
  366.0 6.8 %copy.178 = f32[1,2,32,256,64]{4,3,2,1,0:T(8,128)} copy(f32[1,2,32,256,64]{3,4,2,1,0:T(8,128)} %constant_dynamic-slice_fusion.2) | data formatting | bytes 8388608 | tf_op jit(solution)/shard_map/while/body/eval_jaxpr/dynamic_slice | solution.py:30
  372.9 11.8 %fusion.49 = f32[2,32,256,64]{3,2,1,0:T(8,128)} fusion(f32[1,2,32,256,64]{4,3,2,1,0:T(8,128)} %copy.178, f32[2,32,256,64]{3,2,1,0:T(8,128)} %get-tuple-element.249, f32[2,32]{1,0:T(2,128)S(1)} %dynamic-slice_bitcast_fusion.2, pred[]{:T(512)S(6)} %compare.3, pred[]{:T(512)S(6)} %lt.36), kind=kLoop, calls=%fused_computation.1.clone.1 | loop fusion | flops 4194304 | bytes 12583170 | tf_op jit(solution)/shard_map/while/body/eval_jaxpr/jit(_where)/select_n | solution.py:31
  384.7 4.6 constant_dynamic-slice_fusion.2
  389.4 6.8 %copy.178 = f32[1,2,32,256,64]{4,3,2,1,0:T(8,128)} copy(f32[1,2,32,256,64]{3,4,2,1,0:T(8,128)} %constant_dynamic-slice_fusion.2) | data formatting | bytes 8388608 | tf_op jit(solution)/shard_map/while/body/eval_jaxpr/dynamic_slice | solution.py:30
  396.2 11.8 %fusion.49 = f32[2,32,256,64]{3,2,1,0:T(8,128)} fusion(f32[1,2,32,256,64]{4,3,2,1,0:T(8,128)} %copy.178, f32[2,32,256,64]{3,2,1,0:T(8,128)} %get-tuple-element.249, f32[2,32]{1,0:T(2,128)S(1)} %dynamic-slice_bitcast_fusion.2, pred[]{:T(512)S(6)} %compare.3, pred[]{:T(512)S(6)} %lt.36), kind=kLoop, calls=%fused_computation.1.clone.1 | loop fusion | flops 4194304 | bytes 12583170 | tf_op jit(solution)/shard_map/while/body/eval_jaxpr/jit(_where)/select_n | solution.py:31
  412.7 6.8 %copy.178 = f32[1,2,32,256,64]{4,3,2,1,0:T(8,128)} copy(f32[1,2,32,256,64]{3,4,2,1,0:T(8,128)} %constant_dynamic-slice_fusion.2) | data formatting | bytes 8388608 | tf_op jit(solution)/shard_map/while/body/eval_jaxpr/dynamic_slice | solution.py:30
  419.5 11.8 %fusion.49 = f32[2,32,256,64]{3,2,1,0:T(8,128)} fusion(f32[1,2,32,256,64]{4,3,2,1,0:T(8,128)} %copy.178, f32[2,32,256,64]{3,2,1,0:T(8,128)} %get-tuple-element.249, f32[2,32]{1,0:T(2,128)S(1)} %dynamic-slice_bitcast_fusion.2, pred[]{:T(512)S(6)} %compare.3, pred[]{:T(512)S(6)} %lt.36), kind=kLoop, calls=%fused_computation.1.clone.1 | loop fusion | flops 4194304 | bytes 12583170 | tf_op jit(solution)/shard_map/while/body/eval_jaxpr/jit(_where)/select_n | solution.py:31
  436.0 6.8 %copy.178 = f32[1,2,32,256,64]{4,3,2,1,0:T(8,128)} copy(f32[1,2,32,256,64]{3,4,2,1,0:T(8,128)} %constant_dynamic-slice_fusion.2) | data formatting | bytes 8388608 | tf_op jit(solution)/shard_map/while/body/eval_jaxpr/dynamic_slice | solution.py:30
  442.8 11.8 %fusion.49 = f32[2,32,256,64]{3,2,1,0:T(8,128)} fusion(f32[1,2,32,256,64]{4,3,2,1,0:T(8,128)} %copy.178, f32[2,32,256,64]{3,2,1,0:T(8,128)} %get-tuple-element.249, f32[2,32]{1,0:T(2,128)S(1)} %dynamic-slice_bitcast_fusion.2, pred[]{:T(512)S(6)} %compare.3, pred[]{:T(512)S(6)} %lt.36), kind=kLoop, calls=%fused_computation.1.clone.1 | loop fusion | flops 4194304 | bytes 12583170 | tf_op jit(solution)/shard_map/while/body/eval_jaxpr/jit(_where)/select_n | solution.py:31
  454.7 10.2 %fusion.41 = f32[2,32,64,256]{3,2,1,0:T(8,128)S(1)} fusion(f32[2,32,256,64]{3,2,1,0:T(8,128)} %get-tuple-element.132, bf16[256,2,256,1]{0,2,3,1:T(8,128)(2,1)S(1)} %bitcast.105), kind=kOutput, calls=%fused_computation.75 | convolution fusion | flops 3221225472 | bytes 8650752 | tf_op jit(solution)/shard_map/cqgn,gjnp->cqgjp/dot_general | solution.py:150
  464.9 17.7 %fusion.20 = bf16[1,256,2,32,64]{1,4,3,2,0:T(8,128)(2,1)} fusion(f32[2,32,64,256]{3,2,1,0:T(8,128)S(1)} %fusion.41, bf16[256,2,32,64]{0,3,2,1:T(8,128)(2,1)S(1)} %bitcast.98, f32[2,32,64,256]{3,2,1,0:T(8,128)S(1)} %copy-done, f32[256,2,32]{0,2,1:T(8,128)S(1)} %copy.157, f32[256,2,256]{2,0,1:T(8,128)S(1)} %copy.156, f32[256,2,32]{0,2,1:T(8,128)S(1)} %copy.158, ...), kind=kOutput, calls=%fused_computation.31 | convolution fusion | flops 3232759808 | bytes 13238528 | tf_op jit(solution)/shard_map/while/body/eval_jaxpr/qgjn,gjnp->qgjp/dot_general | solution.py:132
  (101 shorter events, 54.8 us)
Async XLA Ops:
  6.5 8.0 %slice-start = ((bf16[64,20480]{1,0:T(8,128)(2,1)}), bf16[64,16384]{1,0:T(8,128)(2,1)S(1)}, s32[]{:S(2)}) async-start(bf16[64,20480]{1,0:T(8,128)(2,1)} %param.9), calls=%async_computation.3 | async-start | bytes 4194304 | tf_op jit(solution)/shard_map/slice | solution.py:50
  8.3 15.3 %all-to-all-start.1 = ((bf16[4,2,2048]{2,1,0:T(2,128)(2,1)}), bf16[4,2,2048]{2,1,0:T(2,128)(2,1)S(1)}, u32[]{:S(2)}, u32[]{:S(2)}) async-start(bf16[4,2,2048]{2,1,0:T(2,128)(2,1)} %reshape.247), calls=%async_computation.1 | async-start | bytes 65536 | tf_op jit(solution)/shard_map/all_to_all | solution.py:85
  14.1 6.6 %copy-start.5 = (f32[256]{0:T(256)S(1)}, f32[256]{0:T(256)}, u32[]{:S(2)}) copy-start(f32[256]{0:T(256)} %param.13) | copy-start | bytes 3076
  14.1 6.7 %copy-start.6 = (f32[256]{0:T(256)S(1)}, f32[256]{0:T(256)}, u32[]{:S(2)}) copy-start(f32[256]{0:T(256)} %param.14) | copy-start | bytes 3076
  17.3 6.0 %slice-start.1 = ((f32[4,20480]{1,0:T(4,128)}), f32[4,16384]{1,0:T(4,128)S(1)}, s32[]{:S(2)}) async-start(f32[4,20480]{1,0:T(4,128)} %param.11), calls=%async_computation.4 | async-start | bytes 524288 | tf_op jit(solution)/shard_map/slice | solution.py:50
  21.0 8.0 %copy-start.3 = (f32[20480]{0:T(1024)S(1)}, f32[20480]{0:T(1024)}, u32[]{:S(2)}) copy-start(f32[20480]{0:T(1024)} %param.12) | copy-start | bytes 245764
  23.6 59.5 %all-to-all-start = ((bf16[64,4,5120]{2,0,1:T(8,128)(2,1)}), bf16[64,4,5120]{2,0,1:T(8,128)(2,1)S(1)}, u32[]{:S(2)}, u32[]{:S(2)}) async-start(bf16[64,4,5120]{2,0,1:T(8,128)(2,1)} %copy.137), calls=%async_computation | async-start | bytes 5242880 | tf_op jit(solution)/shard_map/all_to_all | solution.py:84
  28.1 242.4 %all-gather.4.cloned.1.call-start = ((), (), s32[]{:S(2)}) async-start(), calls=%async_computation.2 | async-start | bytes 37748736 | tf_op jit(solution)/shard_map/all_gather | solution.py:21
  83.7 6.8 %collective-permute-start = (bf16[3,5120]{1,0:T(4,128)(2,1)}, bf16[3,5120]{1,0:T(4,128)(2,1)}, u32[]{:S(2)}, u32[]{:S(2)}) collective-permute-start(bf16[3,5120]{1,0:T(4,128)(2,1)} %slice.107), channel_id=1, source_target_pairs={{0,4},{4,8},{8,12},{12,16},{16,20},{20,24},{24,28},{1,5},{5,9},{9,... | collective-permute-start | bytes 92168 | tf_op jit(solution)/shard_map/ppermute | solution.py:16
  95.5 6.6 %copy-start.4 = (f32[256,2,32]{0,2,1:T(8,128)S(1)}, f32[256,2,32]{0,2,1:T(8,128)}, u32[]{:S(2)}) copy-start(f32[256,2,32]{0,2,1:T(8,128)} %copy.161) | copy-start | bytes 196612
  102.1 5.7 %copy-start.7 = (f32[256]{0:T(256)S(1)}, f32[256]{0:T(256)}, u32[]{:S(2)}) copy-start(f32[256]{0:T(256)} %param.15) | copy-start | bytes 3076
  102.1 6.5 %copy-start.2 = (f32[2,32,256]{1,0,2:T(2,128)S(1)}, f32[2,32,256]{1,0,2:T(2,128)}, u32[]{:S(2)}) copy-start(f32[2,32,256]{1,0,2:T(2,128)} %get-tuple-element.201) | copy-start | bytes 196612
  102.1 8.0 %copy-start.1 = (f32[256,2,32]{2,1,0:T(2,128)S(1)}, f32[256,2,32]{2,1,0:T(2,128)}, u32[]{:S(2)}) copy-start(f32[256,2,32]{2,1,0:T(2,128)} %get-tuple-element.203) | copy-start | bytes 196612
  454.7 10.2 %copy-start = (f32[2,32,64,256]{3,2,1,0:T(8,128)S(1)}, f32[2,32,64,256]{3,2,1,0:T(8,128)}, u32[]{:S(2)}) copy-start(f32[2,32,64,256]{3,2,1,0:T(8,128)} %fusion.3) | copy-start | bytes 12582916
Sparse Core Ops, SparseCore 0:
  107.8 162.6 all-gather.3
where the time goes:
time: 498 us; the launch traced here: 494 us
  waiting for transfers between devices  190 us (38%)
  local copies, waits for them, and re-layouts  119 us (24%)
  other arithmetic  105 us (21%)
  matrix products  41 us (8%)
  starting transfers between devices  14.7 us (3%)
  between operations  13.7 us (3%)
  blocking collectives  9.9 us (2%)
    all_gather x1, waiting for transfers between devices, carried_in(): everything = jax.tree.map(lambda part: lax.all_gather(part, axis), array)  142 us
    select_n x8, other arithmetic, hop(): return jax.tree.map(lambda a, b: jnp.where(reached, a, b), new, before)  92.3 us
    dynamic_slice x16, local copies, waits for them, and re-layouts, hop(): new = combine(before, jax.tree.map(lambda part: part[k], everything))  91.8 us
    all_to_all x1, waiting for transfers between devices, on_device(): lax.all_to_all(sent, 'head', split_axis=1, concat_axis=0, tiled=True)  47.7 us
    dot_general x1, matrix products, block_step(): jnp.einsum('qgjn,gjnp->qgjp', lifted, held, precision=lax.Precision.HIGHEST)  17.7 us
    dot_general x1, matrix products, on_device(): jnp.einsum('cqgn,gjnp->cqgjp', cmat.astype(jnp.float32), entering, precis...  10.2 us
  transfers between devices with their start and end apart: 4, of which 3 were waited for; matrix products, arithmetic and copies ran while one was open for 6% of the time, Pallas kernels for 0%

commit v1 on v0

--- a/solution.py
+++ b/solution.py
@@ -1,6 +1,10 @@
+import functools
+
 import jax
 import jax.numpy as jnp
 from jax import lax
+from jax.experimental import pallas as pl
+from jax.experimental.pallas import tpu as pltpu
 from jax.sharding import PartitionSpec as P
 
 HEADS = 256
@@ -155,9 +159,353 @@
     return total.astype(jnp.bfloat16).reshape(slab, width)
 
 
+PAIR = 2
+LANES = 128
+SUB = 512
+PIECES = (1, 1, 1, 1)
+LOG2E = 1.4426950408889634
+F32, BF16 = jnp.float32, jnp.bfloat16
+
+
+def halves(value, count):
+    parts = []
+    for _ in range(count):
+        part = value.astype(BF16)
+        parts.append(part)
+        value = value - part.astype(F32)
+    return parts
+
+
+def spread(first_head, width, copies):
+    lane = lax.broadcasted_iota(jnp.int32, (copies * LANES, width), 0) % LANES
+    column = lax.broadcasted_iota(jnp.int32, (copies * LANES, width), 1)
+    return (lane == first_head + column // HEAD_DIM).astype(BF16)
+
+
+def dot(a, b):
+    return jnp.dot(a, b, preferred_element_type=F32)
+
+
+def conv_kernel(blocks, has_step, *refs):
+    rows = refs[0 : 4 * blocks : 4]
+    edges = refs[1 : 4 * blocks : 4]
+    taps = refs[2 : 4 * blocks : 4]
+    biases = refs[3 : 4 * blocks : 4]
+    refs = refs[4 * blocks :]
+    if has_step:
+        step_ref, out, *wides = refs
+    else:
+        out, *wides = refs
+    start = 0
+    for row, edge, tap, bias, wide in zip(rows, edges, taps, biases, wides):
+        count, width = row.shape
+        wide[5:8] = edge[...].astype(F32)
+        wide[8:] = row[...].astype(F32)
+        acc = bias[...] + tap[0:1] * wide[5 : 5 + count]
+        acc = acc + tap[1:2] * wide[6 : 6 + count]
+        acc = acc + tap[2:3] * wide[7 : 7 + count]
+        acc = acc + tap[3:4] * wide[8 : 8 + count]
+        out[0, :, start : start + width] = (acc / (1.0 + jnp.exp(-acc))).astype(BF16)
+        start += width
+    if has_step:
+        out[0, :, start : start + LANES] = step_ref[...]
+
+
+def activate(xbc, dt_raw, edge, weight, bias, first, count, with_rest, shards):
+    tok = xbc.shape[0]
+    inner = HEADS * HEAD_DIM
+    per_group = inner // GROUPS
+
+    def group(p):
+        return (p % shards) * PAIR + p // shards
+
+    blocks = [(SUB, lambda p, i=i: (0, group(p) * (per_group // SUB) + i)) for i in range(first, first + count)]
+    if with_rest:
+        blocks.append((STATE, lambda p: (0, inner // STATE + group(p))))
+        blocks.append((STATE, lambda p: (0, inner // STATE + GROUPS + group(p))))
+    operands, specs, wides = [], [], []
+    for width, index in blocks:
+        operands += [xbc, edge, weight, bias]
+        specs += [pl.BlockSpec((height, width), index) for height in (tok, 3, 4, 1)]
+        wides.append(pltpu.VMEM((tok + 8, width), F32))
+    total = sum(width for width, _ in blocks)
+    if with_rest:
+        per_tile = LANES * GROUPS // HEADS
+        operands.append(dt_raw)
+        specs.append(pl.BlockSpec((tok, LANES), lambda p: (0, group(p) // per_tile)))
+        total += LANES
+    peers = shards * PAIR
+    return pl.pallas_call(
+        functools.partial(conv_kernel, len(blocks), with_rest),
+        grid=(peers,),
+        in_specs=specs,
+        out_specs=pl.BlockSpec((1, tok, total), lambda p: (p, 0, 0)),
+        out_shape=jax.ShapeDtypeStruct((peers, tok, total), BF16),
+        scratch_shapes=wides,
+        cost_estimate=pl.CostEstimate(
+            flops=peers * tok * total * 12,
+            bytes_accessed=peers * tok * total * 4,
+            transcendentals=peers * tok * total,
+        ),
+        name="conv",
+    )(*operands)
+
+
+def prep_kernel(place, b_ref, c_ref, dt_ref, a_ref, bias_ref, skip_ref, cum_ref, row_ref, factor_ref, tail_ref, skip_out, score_ref):
+    per_tile = LANES * GROUPS // HEADS
+    group = place[0]
+    tile = group // per_tile
+    shift = (LANES - (group % per_tile) * (HEADS // GROUPS)) % LANES
+    rate = -jnp.exp(a_ref[pl.ds(tile, 1), :])
+    raw = dt_ref[...].astype(F32) + bias_ref[pl.ds(tile, 1), :]
+    step = jnp.maximum(raw, 0.0) + jnp.log1p(jnp.exp(-jnp.abs(raw)))
+    step = pltpu.roll(step, shift, 1)
+    rate = pltpu.roll(jnp.broadcast_to(rate, (8, LANES)), shift, 1)[0:1]
+    skip = pltpu.roll(jnp.broadcast_to(skip_ref[pl.ds(tile, 1), :], (8, LANES)), shift, 1)
+    skip_out[...] = jnp.concatenate(halves(jnp.concatenate([skip, skip], 0), 3), 1)
+    lower = (
+        lax.broadcasted_iota(jnp.int32, (BLOCK, BLOCK), 0)
+        >= lax.broadcasted_iota(jnp.int32, (BLOCK, BLOCK), 1)
+    ).astype(BF16)
+    for block in range(PAIR):
+        at = slice(block * BLOCK, (block + 1) * BLOCK)
+        here = step[at]
+        parts = halves(here * rate, 3)
+        cum = dot(lower, parts[0]) + (dot(lower, parts[1]) + dot(lower, parts[2]))
+        cum = cum * LOG2E
+        cum_ref[at] = cum
+        row_ref[:, at] = jnp.transpose(cum - jnp.log2(here))
+        factor_ref[at] = jnp.concatenate(halves(jnp.exp2(cum), 2), 1)
+        tail = jnp.exp2(cum[BLOCK - 1 :] - cum) * here
+        tail_ref[at] = jnp.concatenate(halves(tail, 2), 1)
+        score_ref[at] = lax.dot_general(
+            c_ref[at], b_ref[at], (((1,), (1,)), ((), ())), preferred_element_type=F32
+        )
+
+
+def state_kernel(first_head, x_ref, b_ref, factor_ref, tail_ref, send_ref, own_ref):
+    width = x_ref.shape[1]
+    wide = spread(first_head, width, 2)
+    both = []
+    for block in range(PAIR):
+        at = slice(block * BLOCK, (block + 1) * BLOCK)
+        loaded = (x_ref[at].astype(F32) * dot(tail_ref[at], wide)).astype(BF16)
+        both.append(
+            lax.dot_general(b_ref[at], loaded, (((0,), (0,)), ((), ())), preferred_element_type=F32)
+        )
+    ends = [dot(factor_ref[(i + 1) * BLOCK - 16 : (i + 1) * BLOCK], wide)[15:16] for i in range(PAIR)]
+    own_ref[...] = both[0]
+    send_ref[0:STATE] = (ends[1] * both[0] + both[1]).astype(BF16)
+    row = lax.broadcasted_iota(jnp.int32, (16, width), 0)
+    high, middle, low = (part.astype(F32) for part in halves(ends[0] * ends[1], 3))
+    packed = jnp.where(row == 0, high, jnp.where(row == 1, middle, jnp.where(row == 2, low, 0.0)))
+    send_ref[STATE:] = packed.astype(BF16)
+
+
+def local_kernel(first_head, x_ref, cum_ref, row_ref, score_ref, skip_ref, out_ref):
+    width = x_ref.shape[1]
+    half = BLOCK // 2
+    wide = spread(first_head, width, 3)
+    skip = dot(skip_ref[...], wide)[0:1]
+    lower = lax.broadcasted_iota(jnp.int32, (half, half), 0) >= lax.broadcasted_iota(
+        jnp.int32, (half, half), 1
+    )
+    lane = lax.broadcasted_iota(jnp.int32, (BLOCK, LANES), 1)
+    for block in range(PAIR):
+        base = block * BLOCK
+        for tile in range(width // LANES):
+            columns = slice(tile * LANES, (tile + 1) * LANES)
+            x = x_ref[base : base + BLOCK, columns]
+            top = skip[:, columns] * x[:half].astype(F32)
+            bottom = skip[:, columns] * x[half:].astype(F32)
+            for side in range(LANES // HEAD_DIM):
+                head = first_head + tile * (LANES // HEAD_DIM) + side
+                own = jnp.where(lane // HEAD_DIM == side, x, jnp.zeros_like(x))
+                cum = cum_ref[base : base + BLOCK, head : head + 1]
+                row = row_ref[head : head + 1, base : base + BLOCK]
+                diag = jnp.where(lower, cum[:half] - row[:, :half], -1e30)
+                mixing = jnp.exp2(diag) * score_ref[base : base + half, :half]
+                top = top + dot(mixing.astype(BF16), own[:half])
+                left = jnp.exp2(cum[half:] - row[:, :half]) * score_ref[base + half : base + BLOCK, :half]
+                diag = jnp.where(lower, cum[half:] - row[:, half:], -1e30)
+                right = jnp.exp2(diag) * score_ref[base + half : base + BLOCK, half:]
+                mixing = jnp.concatenate([left.astype(BF16), right.astype(BF16)], 1)
+                bottom = bottom + dot(mixing, own)
+            out_ref[base : base + half, columns] = top
+            out_ref[base + half : base + BLOCK, columns] = bottom
+
+
+def final_kernel(first_head, place, all_ref, own_ref, c_ref, factor_ref, partial_ref, keep_ref, send_ref):
+    width = own_ref.shape[1]
+    pair, core = place[1], place[2]
+    wide = spread(first_head, width, 2)
+    held = jnp.zeros((STATE, width), F32)
+    for k in range(all_ref.shape[0] - 1):
+        decay = all_ref[k, STATE : STATE + 16].astype(F32)
+        decay = decay[0:1] + (decay[1:2] + decay[2:3])
+        held = jnp.where(k < pair, decay * held + all_ref[k, :STATE].astype(F32), held)
+    factor = dot(factor_ref[...], wide)
+    outs = []
+    for block in range(PAIR):
+        at = slice(block * BLOCK, (block + 1) * BLOCK)
+        carried = dot(c_ref[at], held.astype(BF16))
+        outs.append((partial_ref[at] + factor[at] * carried).astype(BF16))
+        held = factor[BLOCK - 1 : BLOCK] * held + own_ref[...]
+
+    @pl.when(core == 0)
+    def _():
+        keep_ref[...] = outs[0]
+        send_ref[...] = outs[1]
+
+    @pl.when(core == 1)
+    def _():
+        keep_ref[...] = outs[1]
+        send_ref[...] = outs[0]
+
+
+def assemble_kernel(count, place, *refs):
+    keeps, gots, out = refs[:count], refs[count : 2 * count], refs[2 * count]
+    core = place[2]
+    half = out.shape[1] // PAIR
+
+    def put(own, other):
+        start = 0
+        for keep, got in zip(keeps, gots):
+            width = keep.shape[1]
+            out[:, own + start : own + start + width] = keep[...]
+            out[:, other + start : other + start + width] = got[...]
+            start += width
+
+    pl.when(core == 0)(lambda: put(0, half))
+    pl.when(core == 1)(lambda: put(half, 0))
+
+
+def local_call(body, outs, operands, specs=None, flops=0, transcendentals=0, name=None):
+    shapes = [jax.ShapeDtypeStruct(shape, dtype) for shape, dtype in outs]
+    vmem = pl.BlockSpec(memory_space=pltpu.VMEM)
+    specs = specs or [vmem] * len(operands)
+    moved = sum(o.size * o.dtype.itemsize for o in shapes) * 2
+    return pl.pallas_call(
+        body,
+        out_shape=shapes,
+        in_specs=specs,
+        out_specs=[vmem] * len(outs),
+        compiler_params=pltpu.CompilerParams(vmem_limit_bytes=32 << 20),
+        cost_estimate=pl.CostEstimate(flops=flops, bytes_accessed=moved, transcendentals=transcendentals),
+        name=name,
+    )(*operands)
+
+
+def paired(xbc, dt_raw, conv_weight, conv_bias, a_log, dt_bias, skip_gain):
+    axes = ("ctx", "head")
+    shards, length = lax.axis_size("head"), lax.axis_size("ctx")
+    devices, peers, pairs = shards * length, shards * PAIR, length // PAIR
+    tok = xbc.shape[0]
+    slab = tok * peers
+    per_group = HEADS // GROUPS
+    context, shard = lax.axis_index("ctx"), lax.axis_index("head")
+    pair, core = context // PAIR, context % PAIR
+    group = shard * PAIR + core
+    place = jnp.stack([group, pair, core]).astype(jnp.int32)
+    smem, vmem = pl.BlockSpec(memory_space=pltpu.SMEM), pl.BlockSpec(memory_space=pltpu.VMEM)
+
+    edge = lax.ppermute(xbc[tok - 3 :], axes, [(i, i + 1) for i in range(devices - 1)])
+    exchange = [[k * peers + i for i in range(peers)] for k in range(pairs)]
+    gather = [[k * peers + i for k in range(pairs)] for i in range(peers)]
+    swap = [(i * shards + j, (i ^ 1) * shards + j) for i in range(length) for j in range(shards)]
+
+    received = []
+    first = 0
+    for index, count in enumerate(PIECES):
+        sent = activate(
+            xbc, dt_raw, edge, conv_weight, conv_bias[None], first, count, index == 0, shards
+        )
+        got = lax.all_to_all(sent, axes, 0, 0, axis_index_groups=exchange, tiled=True)
+        received.append(got.reshape(slab, got.shape[2]))
+        first += count
+
+    start = PIECES[0] * SUB
+    b = received[0][:, start : start + STATE]
+    c = received[0][:, start + STATE : start + 2 * STATE]
+    raw = received[0][:, start + 2 * STATE :]
+    received[0] = received[0][:, :start]
+    tiles = [p.reshape(HEADS // LANES, LANES) for p in (a_log, dt_bias, skip_gain)]
+    cum, row, factor, tail, skip, score = local_call(
+        prep_kernel,
+        [
+            ((slab, LANES), F32),
+            ((LANES, slab), F32),
+            ((slab, 2 * LANES), BF16),
+            ((slab, 2 * LANES), BF16),
+            ((16, 3 * LANES), BF16),
+            ((slab, BLOCK), F32),
+        ],
+        [place, b, c, raw] + tiles,
+        [smem] + [vmem] * 6,
+        flops=2 * slab * BLOCK * (STATE + 3 * LANES),
+        name="prep",
+    )
+    heads, gathered, owns, partials = [], [], [], []
+    head = 0
+    for x in received:
+        width = x.shape[1]
+        sent, own = local_call(
+            functools.partial(state_kernel, head),
+            [((STATE + 16, width), BF16), ((STATE, width), F32)],
+            [x, b, factor, tail],
+            flops=4 * slab * STATE * width,
+            name="state",
+        )
+        gathered.append(lax.all_gather(sent, axes, axis_index_groups=gather))
+        (partial,) = local_call(
+            functools.partial(local_kernel, head),
+            [((slab, width), F32)],
+            [x, cum, row, score, skip],
+            flops=8 * slab * STATE * width,
+            transcendentals=slab * BLOCK * width // HEAD_DIM,
+            name="local",
+        )
+        owns.append(own)
+        partials.append(partial)
+        heads.append(head)
+        head += width // HEAD_DIM
+    keeps, gots = [], []
+    for head, everything, own, partial in zip(heads, gathered, owns, partials):
+        width = own.shape[1]
+        keep, send = local_call(
+            functools.partial(final_kernel, head),
+            [((BLOCK, width), BF16)] * 2,
+            [place, everything, own, c, factor, partial],
+            [smem] + [vmem] * 5,
+            flops=4 * slab * STATE * width,
+            name="final",
+        )
+        keeps.append(keep)
+        gots.append(lax.ppermute(send, axes, swap))
+    (out,) = local_call(
+        functools.partial(assemble_kernel, len(keeps)),
+        [((BLOCK, PAIR * per_group * HEAD_DIM), BF16)],
+        [place] + keeps + gots,
+        [smem] + [vmem] * (2 * len(keeps)),
+        name="assemble",
+    )
+    return out
+
+
 def solution(mesh):
     in_specs = (P(("ctx", "head"), None), P(("ctx", "head"), None), P(), P(), P(), P(), P())
     out_specs = P("ctx", "head")
-    return jax.shard_map(
-        on_device, mesh=mesh, in_specs=in_specs, out_specs=out_specs, check_vma=False
-    )
+    shards, length = mesh.shape["head"], mesh.shape["ctx"]
+
+    def program(xbc, *rest):
+        slab = xbc.shape[0] // length
+        fits = GROUPS == shards * PAIR and length % PAIR == 0 and slab == BLOCK and slab % (16 * shards) == 0
+        return jax.shard_map(
+            paired if fits else on_device,
+            mesh=mesh,
+            in_specs=in_specs,
+            out_specs=out_specs,
+            check_vma=False,
+        )(xbc, *rest)
+
+    return program

time: 498 us -> 197 us (0.40)
  waiting for transfers between devices: 190 us -> 43.3 us
  other arithmetic: 105 us -> 0.08 us
  local copies, waits for them, and re-layouts: 119 us -> 25.2 us
  blocking collectives: 9.9 us -> 56.1 us
  Pallas kernels: 0 us -> 41.5 us
  matrix products: 41 us -> 0 us
    all_gather x1 -> x4, waiting for transfers between devices: 142 us -> 12.5 us  [paired(): gathered.append(lax.all_gather(sent, axes, axis_index_groups=gather))]
    select_n x8 -> x0, other arithmetic: 92.3 us -> none  [hop(): return jax.tree.map(lambda a, b: jnp.where(reached, a, b), new, before)]
    dynamic_slice x18 -> x0, local copies, waits for them, and re-layouts: 92 us -> none  [the longest x16 91.8 us: hop(): new = combine(before, jax.tree.map(lambda part: part[k], everything))]
    all_to_all x0 -> x3, blocking collectives: none -> 56.1 us  [paired(): lax.all_to_all(sent, axes, 0, 0, axis_index_groups=exchange, tiled=True)]
    pallas_call x0 -> x18, Pallas kernels: none -> 41.5 us  [the longest x4 22.3 us: activate(): pl.pallas_call(functools.partial(conv_kernel, len(blocks), with_rest), gr...]
    dot_general x5 -> x0, matrix products: 41 us -> none  [the longest x1 17.7 us: block_step(): jnp.einsum('qgjn,gjnp->qgjp', lifted, held, precision=lax.Precision.HIGHEST)]
    all_to_all x2 -> x1, waiting for transfers between devices: 47.7 us -> 25.8 us  [paired(): lax.all_to_all(sent, axes, 0, 0, axis_index_groups=exchange, tiled=True)]
    unnamed x19 -> x66, local copies, waits for them, and re-layouts: 1.9 us -> 21.1 us
  transfers between devices with their start and end apart: 4 -> 10, of which waited for: 3 -> 4; matrix products, arithmetic and copies ran while one was open for 6% -> 0% of each run, Pallas kernels for 0% -> 16%
where the time goes in v1:
time: 197 us; the launch traced here: 193 us
  blocking collectives  56.1 us (28%)
  waiting for transfers between devices  43.3 us (22%)
  Pallas kernels  41.5 us (21%)
  local copies, waits for them, and re-layouts  25.2 us (13%)
  starting transfers between devices  14 us (7%)
  between operations  13.3 us (7%)
    all_to_all x3, blocking collectives, paired(): lax.all_to_all(sent, axes, 0, 0, axis_index_groups=exchange, tiled=True)  56.1 us
    all_to_all x1, waiting for transfers between devices, paired(): lax.all_to_all(sent, axes, 0, 0, axis_index_groups=exchange, tiled=True)  25.8 us
    pallas_call x4, Pallas kernels, activate(): pl.pallas_call(functools.partial(conv_kernel, len(blocks), with_rest), gr...  22.3 us
    unnamed x66, local copies, waits for them, and re-layouts  21.1 us
    pallas_call x14, Pallas kernels, local_call(): pl.pallas_call(body, out_shape=shapes, in_specs=specs, out_specs=[vmem] *...  19.2 us
    all_gather x4, waiting for transfers between devices, paired(): gathered.append(lax.all_gather(sent, axes, axis_index_groups=gather))  12.5 us
    all_to_all x1, starting transfers between devices, paired(): lax.all_to_all(sent, axes, 0, 0, axis_index_groups=exchange, tiled=True)  9.38 us
  transfers between devices with their start and end apart: 10, of which 4 were waited for; matrix products, arithmetic and copies ran while one was open for 0% of the time, Pallas kernels for 16%

profile of v1, /device:TPU:13, one launch (start us, length us, event | category | flops | bytes accessed | tf_op | source)
XLA Modules:
  0.0 193.5 jit_solution(8581148096799180693)
XLA Ops:
  6.5 1.1 slice.15
  7.6 3.2 %collective-permute-start = (bf16[3,20480]{1,0:T(4,128)(2,1)S(1)}, bf16[3,20480]{1,0:T(4,128)(2,1)S(1)}, u32[]{:S(2)}, u32[]{:S(2)}) collective-permute-start(bf16[3,20480]{1,0:T(4,128)(2,1)S(1)} %slice.15), channel_id=1, source_target_pairs={{0,1},{1,2},{2,3},{3,4},{4,5},{5,6},{6,7},{7,8},{8,9},{9,10},{10,1... | collective-permute-start | bytes 368648 | tf_op jit(solution)/shard_map/ppermute | solution.py:412
  10.8 3.7 %collective-permute-done.refs_1_.refs_5_.refs_9_ = bf16[3,20480]{1,0:T(4,128)(2,1)S(1)} collective-permute-done((bf16[3,20480]{1,0:T(4,128)(2,1)S(1)}, bf16[3,20480]{1,0:T(4,128)(2,1)S(1)}, u32[]{:S(2)}, u32[]{:S(2)}) %collective-permute-start) | collective-permute-done | bytes 122912 | tf_op jit(solution)/shard_map/ppermute | solution.py:412
  15.2 6.3 %conv.4 = bf16[8,64,1152]{2,1,0:T(8,128)(2,1)} custom-call(bf16[64,20480]{1,0:T(8,128)(2,1)} %refs_0_.7, bf16[3,20480]{1,0:T(4,128)(2,1)} %copy-done.32, f32[4,20480]{1,0:T(4,128)} %refs_2_.7, f32[1,20480]{1,0:T(1,128)} %bitcast.28, bf16[64,20480]{1,0:T(8,128)(2,1)} %refs_0_.7, bf16[3,20480]{1,0:T(4,128)(2,1)} %copy-done.32, f32[4,20480]{1,0:T(4,128)} %refs_2_.7, ...), custom_call_target="tpu_custom_call" | custom-call | flops 7077888 | bytes 2359296 | tf_op jit(solution)/shard_map/conv/pallas_call | solution.py:238
  21.5 9.4 %all-to-all-start = ((bf16[8,64,1152]{2,1,0:T(8,128)(2,1)}), bf16[8,64,1152]{2,1,0:T(8,128)(2,1)}, u32[]{:S(2)}, u32[]{:S(2)}) async-start(bf16[8,64,1152]{2,1,0:T(8,128)(2,1)} %conv.4), calls=%async_computation | async-start | bytes 2359296 | tf_op jit(solution)/shard_map/all_to_all | solution.py:423
  31.0 25.8 %all-to-all-done = bf16[8,64,1152]{2,1,0:T(8,128)(2,1)} async-done(((bf16[8,64,1152]{2,1,0:T(8,128)(2,1)}), bf16[8,64,1152]{2,1,0:T(8,128)(2,1)}, u32[]{:S(2)}, u32[]{:S(2)}) %all-to-all-start) | async-done | bytes 1179680 | tf_op jit(solution)/shard_map/all_to_all | solution.py:423
  56.8 1.1 slice.20.x_ref
  57.9 1.1 fusion
  60.0 1.2 prep.1
  62.6 1.5 state.4
  65.1 5.3 %conv.5 = bf16[8,64,512]{2,1,0:T(8,128)(2,1)} custom-call(bf16[64,20480]{1,0:T(8,128)(2,1)} %refs_0_.7, bf16[3,20480]{1,0:T(4,128)(2,1)} %copy-done.32, f32[4,20480]{1,0:T(4,128)} %refs_2_.7, f32[1,20480]{1,0:T(1,128)} %bitcast.31), custom_call_target="tpu_custom_call" | custom-call | flops 3145728 | bytes 1048576 | tf_op jit(solution)/shard_map/conv/pallas_call | solution.py:238
  70.4 19.6 %all_to_all.20 = bf16[8,64,512]{2,1,0:T(8,128)(2,1)S(1)} all-to-all(bf16[8,64,512]{2,1,0:T(8,128)(2,1)} %conv.5), channel_id=1, replica_groups={{0,1,2,3,4,5,6,7},{8,9,10,11,12,13,14,15},{16,17,18,19,20,21,22,23},{24..., dimensions={0} | all-to-all | bytes 1048576 | tf_op jit(solution)/shard_map/all_to_all | solution.py:423
  90.0 1.5 state.5
  92.4 5.3 %conv.6 = bf16[8,64,512]{2,1,0:T(8,128)(2,1)} custom-call(bf16[64,20480]{1,0:T(8,128)(2,1)} %refs_0_.7, bf16[3,20480]{1,0:T(4,128)(2,1)} %copy-done.32, f32[4,20480]{1,0:T(4,128)} %refs_2_.7, f32[1,20480]{1,0:T(1,128)} %bitcast.32), custom_call_target="tpu_custom_call" | custom-call | flops 3145728 | bytes 1048576 | tf_op jit(solution)/shard_map/conv/pallas_call | solution.py:238
  97.7 18.4 %all_to_all.21 = bf16[8,64,512]{2,1,0:T(8,128)(2,1)S(1)} all-to-all(bf16[8,64,512]{2,1,0:T(8,128)(2,1)} %conv.6), channel_id=1, replica_groups={{0,1,2,3,4,5,6,7},{8,9,10,11,12,13,14,15},{16,17,18,19,20,21,22,23},{24..., dimensions={0} | all-to-all | bytes 1048576 | tf_op jit(solution)/shard_map/all_to_all | solution.py:423
  116.1 1.5 state.6
  118.5 5.3 %conv.7 = bf16[8,64,512]{2,1,0:T(8,128)(2,1)} custom-call(bf16[64,20480]{1,0:T(8,128)(2,1)} %refs_0_.7, bf16[3,20480]{1,0:T(4,128)(2,1)} %copy-done.32, f32[4,20480]{1,0:T(4,128)} %refs_2_.7, f32[1,20480]{1,0:T(1,128)} %bitcast.33), custom_call_target="tpu_custom_call" | custom-call | flops 3145728 | bytes 1048576 | tf_op jit(solution)/shard_map/conv/pallas_call | solution.py:238
  123.9 18.1 %all_to_all.22 = bf16[8,64,512]{2,1,0:T(8,128)(2,1)S(1)} all-to-all(bf16[8,64,512]{2,1,0:T(8,128)(2,1)} %conv.7), channel_id=1, replica_groups={{0,1,2,3,4,5,6,7},{8,9,10,11,12,13,14,15},{16,17,18,19,20,21,22,23},{24..., dimensions={0} | all-to-all | bytes 1048576 | tf_op jit(solution)/shard_map/all_to_all | solution.py:423
  152.1 1.2 copy-done.11
  153.3 1.2 copy-done.12
  154.6 1.8 final.4
  156.4 1.2 copy-done.9
  157.6 1.2 copy-done.13
  158.9 1.8 final.5
  161.9 1.2 copy-done.14
  163.2 1.0 copy-done.21
  164.2 1.8 final.6
  166.7 12.5 %all-gather.15.cloned.1.call-done = bf16[1088,512]{1,0:T(8,128)(2,1)} async-done(((bf16[272,512]{1,0:T(8,128)(2,1)}), bf16[1088,512]{1,0:T(8,128)(2,1)}) %all-gather.15.cloned.1.call-update) | async-done | bytes 1114128 | tf_op jit(solution)/shard_map/all_gather | solution.py:459
  179.2 1.2 copy-done.15
  181.5 1.1 final.7
  183.4 1.1 collective-permute-done.4.refs_7_
  184.5 2.4 %assemble.1 = bf16[256,4096]{1,0:T(8,128)(2,1)} custom-call(s32[3]{0:T(128)S(1)} %pad_add_fusion.place, bf16[256,512]{1,0:T(8,128)(2,1)S(1)} %get-tuple-element.35.refs_0_, bf16[256,512]{1,0:T(8,128)(2,1)S(1)} %copy-done.26, bf16[256,512]{1,0:T(8,128)(2,1)S(1)} %copy-done.28, bf16[256,512]{1,0:T(8,128)(2,1)S(1)} %get-tuple-element.44.refs_3_, ...), custom_call_target="tpu_custom_call" | custom-call | bytes 4194304 | tf_op jit(solution)/shard_map/assemble/pallas_call | solution.py:388
  (84 shorter events, 19.6 us)
Async XLA Ops:
  7.6 7.0 %collective-permute-start = (bf16[3,20480]{1,0:T(4,128)(2,1)S(1)}, bf16[3,20480]{1,0:T(4,128)(2,1)S(1)}, u32[]{:S(2)}, u32[]{:S(2)}) collective-permute-start(bf16[3,20480]{1,0:T(4,128)(2,1)S(1)} %slice.15), channel_id=1, source_target_pairs={{0,1},{1,2},{2,3},{3,4},{4,5},{5,6},{6,7},{7,8},{8,9},{9,10},{10,1... | collective-permute-start | bytes 368648 | tf_op jit(solution)/shard_map/ppermute | solution.py:412
  21.5 35.3 %all-to-all-start = ((bf16[8,64,1152]{2,1,0:T(8,128)(2,1)}), bf16[8,64,1152]{2,1,0:T(8,128)(2,1)}, u32[]{:S(2)}, u32[]{:S(2)}) async-start(bf16[8,64,1152]{2,1,0:T(8,128)(2,1)} %conv.4), calls=%async_computation | async-start | bytes 2359296 | tf_op jit(solution)/shard_map/all_to_all | solution.py:423
  30.9 121.1 %all-gather.9.cloned.1.call-start = ((), (), s32[]{:S(2)}) async-start(), calls=%async_computation.4 | async-start | bytes 1392640 | tf_op jit(solution)/shard_map/all_gather | solution.py:459
  56.8 3.1 %copy-start.29 = (f32[256]{0:T(256)S(1)}, f32[256]{0:T(256)}, u32[]{:S(2)}) copy-start(f32[256]{0:T(256)} %param.11) | copy-start | bytes 3076
  56.8 3.1 %copy-start.30 = (f32[256]{0:T(256)S(1)}, f32[256]{0:T(256)}, u32[]{:S(2)}) copy-start(f32[256]{0:T(256)} %param.12) | copy-start | bytes 3076
  56.8 3.1 %copy-start.31 = (f32[256]{0:T(256)S(1)}, f32[256]{0:T(256)}, u32[]{:S(2)}) copy-start(f32[256]{0:T(256)} %param.13) | copy-start | bytes 3076
  62.6 53.5 %copy-start.4 = (bf16[512,256]{1,0:T(8,128)(2,1)}, bf16[512,256]{1,0:T(8,128)(2,1)S(1)}, u32[]{:S(2)}) copy-start(bf16[512,256]{1,0:T(8,128)(2,1)S(1)} %get-tuple-element.28.tail_ref) | copy-start | bytes 786436
  65.0 91.4 %all-gather.11.cloned.1.call-start = ((), (), s32[]{:S(2)}) async-start(), calls=%async_computation.5 | async-start | bytes 1392640 | tf_op jit(solution)/shard_map/all_gather | solution.py:459
  92.3 69.6 %all-gather.13.cloned.1.call-start = ((), (), s32[]{:S(2)}) async-start(), calls=%async_computation.6 | async-start | bytes 1392640 | tf_op jit(solution)/shard_map/all_gather | solution.py:459
  118.5 60.7 %all-gather.15.cloned.1.call-start = ((), (), s32[]{:S(2)}) async-start(), calls=%async_computation.7 | async-start | bytes 1392640 | tf_op jit(solution)/shard_map/all_gather | solution.py:459
  123.9 18.1 %copy-start.5 = (bf16[512,256]{1,0:T(8,128)(2,1)S(1)}, bf16[512,256]{1,0:T(8,128)(2,1)}, u32[]{:S(2)}) copy-start(bf16[512,256]{1,0:T(8,128)(2,1)} %copy-done.4) | copy-start | bytes 786436
  144.3 1.0 copy-start.1
  147.2 1.0 copy-start.10
  149.1 1.0 copy-start.8
  150.1 1.0 copy-start.6
  151.1 1.0 copy-start.17
  152.1 1.2 copy-start.11
  153.3 1.2 copy-start.12
  154.6 1.8 copy-start.19
  156.4 27.0 %collective-permute-start.1 = (bf16[256,512]{1,0:T(8,128)(2,1)}, bf16[256,512]{1,0:T(8,128)(2,1)}, u32[]{:S(2)}, u32[]{:S(2)}) collective-permute-start(bf16[256,512]{1,0:T(8,128)(2,1)} %get-tuple-element.45), channel_id=1, source_target_pairs={{0,4},{1,5},{2,6},{3,7},{4,0},{5,1},{6,2},{7,3},{8,12},{9,13},{10,... | collective-permute-start | bytes 786440 | tf_op jit(solution)/shard_map/ppermute | solution.py:484
  156.4 1.2 copy-start.9
  157.6 1.2 copy-start.13
  158.9 3.1 %copy-start.7 = (f32[512,512]{1,0:T(8,128)S(1)}, f32[512,512]{1,0:T(8,128)}, u32[]{:S(2)}) copy-start(f32[512,512]{1,0:T(8,128)} %copy-done.6) | copy-start | bytes 3145732
  161.4 22.0 %collective-permute-start.2 = (bf16[256,512]{1,0:T(8,128)(2,1)}, bf16[256,512]{1,0:T(8,128)(2,1)S(1)}, u32[]{:S(2)}, u32[]{:S(2)}) collective-permute-start(bf16[256,512]{1,0:T(8,128)(2,1)} %get-tuple-element.46), channel_id=1, source_target_pairs={{0,4},{1,5},{2,6},{3,7},{4,0},{5,1},{6,2},{7,3},{8,12},{9,13},{10,... | collective-permute-start | bytes 786440 | tf_op jit(solution)/shard_map/ppermute | solution.py:484
  161.9 1.2 copy-start.14
  163.2 1.0 copy-start.21
  166.7 16.6 %collective-permute-start.3 = (bf16[256,512]{1,0:T(8,128)(2,1)}, bf16[256,512]{1,0:T(8,128)(2,1)S(1)}, u32[]{:S(2)}, u32[]{:S(2)}) collective-permute-start(bf16[256,512]{1,0:T(8,128)(2,1)} %get-tuple-element.47), channel_id=1, source_target_pairs={{0,4},{1,5},{2,6},{3,7},{4,0},{5,1},{6,2},{7,3},{8,12},{9,13},{10,... | collective-permute-start | bytes 786440 | tf_op jit(solution)/shard_map/ppermute | solution.py:484
  179.2 1.2 copy-start.15
  180.5 1.0 copy-start.23
  181.5 3.0 %copy-start.26 = (bf16[256,512]{1,0:T(8,128)(2,1)S(1)}, bf16[256,512]{1,0:T(8,128)(2,1)}, u32[]{:S(2)}) copy-start(bf16[256,512]{1,0:T(8,128)(2,1)} %copy-done.25) | copy-start | bytes 786436
  181.5 3.0 %copy-start.28 = (bf16[256,512]{1,0:T(8,128)(2,1)S(1)}, bf16[256,512]{1,0:T(8,128)(2,1)}, u32[]{:S(2)}) copy-start(bf16[256,512]{1,0:T(8,128)(2,1)} %copy-done.27) | copy-start | bytes 786436
  182.6 1.9 collective-permute-start.4
  (11 other events, 8.5 us)
Sparse Core Ops, SparseCore 0:
  65.1 27.0 all-gather.8
  94.0 27.1 all-gather.10
  123.1 27.1 all-gather.12
  152.0 27.1 all-gather.14

commit v2 on v1

--- a/solution.py
+++ b/solution.py
@@ -161,8 +161,7 @@
 
 PAIR = 2
 LANES = 128
-SUB = 512
-PIECES = (1, 1, 1, 1)
+PIECES = (512, 512, 512, 512)
 LOG2E = 1.4426950408889634
 F32, BF16 = jnp.float32, jnp.bfloat16
 
@@ -186,72 +185,77 @@
     return jnp.dot(a, b, preferred_element_type=F32)
 
 
-def conv_kernel(blocks, has_step, *refs):
-    rows = refs[0 : 4 * blocks : 4]
-    edges = refs[1 : 4 * blocks : 4]
-    taps = refs[2 : 4 * blocks : 4]
-    biases = refs[3 : 4 * blocks : 4]
-    refs = refs[4 * blocks :]
-    if has_step:
-        step_ref, out, *wides = refs
-    else:
-        out, *wides = refs
-    start = 0
-    for row, edge, tap, bias, wide in zip(rows, edges, taps, biases, wides):
-        count, width = row.shape
-        wide[5:8] = edge[...].astype(F32)
-        wide[8:] = row[...].astype(F32)
-        acc = bias[...] + tap[0:1] * wide[5 : 5 + count]
-        acc = acc + tap[1:2] * wide[6 : 6 + count]
-        acc = acc + tap[2:3] * wide[7 : 7 + count]
-        acc = acc + tap[3:4] * wide[8 : 8 + count]
-        out[0, :, start : start + width] = (acc / (1.0 + jnp.exp(-acc))).astype(BF16)
-        start += width
-    if has_step:
-        out[0, :, start : start + LANES] = step_ref[...]
-
-
-def activate(xbc, dt_raw, edge, weight, bias, first, count, with_rest, shards):
+def conv_kernel(parts, shards, with_step, place, xbc, edge, weight, bias, *refs):
+    peers = shards * PAIR
+    if with_step:
+        dt_ref, refs = refs[0], refs[1:]
+    outs, wide = refs[:peers], refs[peers]
+    count = xbc.shape[0]
+    for r in range(peers):
+        peer = place[3] ^ r
+        group = (peer % shards) * PAIR + peer // shards
+        start = 0
+        for origin, stride, width in parts:
+            at = pl.ds(pl.multiple_of(origin + group * stride, LANES), width)
+            wide[5:8, :width] = edge[:, at].astype(F32)
+            wide[8:, :width] = xbc[:, at].astype(F32)
+            tap = weight[:, at] * 0.5
+            acc = bias[:, at] * 0.5 + tap[0:1] * wide[5 : 5 + count, :width]
+            acc = acc + tap[1:2] * wide[6 : 6 + count, :width]
+            acc = acc + tap[2:3] * wide[7 : 7 + count, :width]
+            acc = acc + tap[3:4] * wide[8 : 8 + count, :width]
+            outs[r][:, start : start + width] = (acc + acc * jnp.tanh(acc)).astype(BF16)
+            start += width
+        if with_step:
+            tile = group // (LANES * GROUPS // HEADS)
+            outs[r][:, start : start + LANES] = dt_ref[:, pl.ds(pl.multiple_of(tile * LANES, LANES), LANES)]
+
+
+def activate(place, xbc, dt_raw, edge, weight, bias, first, width, with_rest, shards):
     tok = xbc.shape[0]
     inner = HEADS * HEAD_DIM
-    per_group = inner // GROUPS
-
-    def group(p):
-        return (p % shards) * PAIR + p // shards
-
-    blocks = [(SUB, lambda p, i=i: (0, group(p) * (per_group // SUB) + i)) for i in range(first, first + count)]
+    parts = [(first, inner // GROUPS, width)]
+    operands = [place, xbc, edge, weight, bias]
+    total = width
     if with_rest:
-        blocks.append((STATE, lambda p: (0, inner // STATE + group(p))))
-        blocks.append((STATE, lambda p: (0, inner // STATE + GROUPS + group(p))))
-    operands, specs, wides = [], [], []
-    for width, index in blocks:
-        operands += [xbc, edge, weight, bias]
-        specs += [pl.BlockSpec((height, width), index) for height in (tok, 3, 4, 1)]
-        wides.append(pltpu.VMEM((tok + 8, width), F32))
-    total = sum(width for width, _ in blocks)
-    if with_rest:
-        per_tile = LANES * GROUPS // HEADS
+        parts += [(inner, STATE, STATE), (inner + GROUPS * STATE, STATE, STATE)]
         operands.append(dt_raw)
-        specs.append(pl.BlockSpec((tok, LANES), lambda p: (0, group(p) // per_tile)))
-        total += LANES
+        total += 2 * STATE + LANES
     peers = shards * PAIR
-    return pl.pallas_call(
-        functools.partial(conv_kernel, len(blocks), with_rest),
-        grid=(peers,),
-        in_specs=specs,
-        out_specs=pl.BlockSpec((1, tok, total), lambda p: (p, 0, 0)),
-        out_shape=jax.ShapeDtypeStruct((peers, tok, total), BF16),
-        scratch_shapes=wides,
-        cost_estimate=pl.CostEstimate(
-            flops=peers * tok * total * 12,
-            bytes_accessed=peers * tok * total * 4,
-            transcendentals=peers * tok * total,
-        ),
+    return local_call(
+        functools.partial(conv_kernel, parts, shards, with_rest),
+        [((tok, total), BF16)] * peers,
+        operands,
+        scratch=[pltpu.VMEM((tok + 8, max(p[2] for p in parts)), F32)],
+        flops=peers * tok * total * 12,
+        transcendentals=peers * tok * total,
         name="conv",
-    )(*operands)
-
-
-def prep_kernel(place, b_ref, c_ref, dt_ref, a_ref, bias_ref, skip_ref, cum_ref, row_ref, factor_ref, tail_ref, skip_out, score_ref):
+    )
+
+
+def exchange(blocks, axes, pairs):
+    peers = len(blocks)
+    got = [blocks[0]]
+    for r in range(1, peers):
+        route = [(k * peers + i, k * peers + (i ^ r)) for k in range(pairs) for i in range(peers)]
+        got.append(lax.ppermute(blocks[r], axes, route))
+    return got
+
+
+def in_order(place, blocks, columns, out):
+    count = blocks[0].shape[0]
+    for r, block in enumerate(blocks):
+        at = pl.multiple_of((place[3] ^ r) * count, count)
+        out[pl.ds(at, count), :] = block[:, columns]
+
+
+def prep_kernel(peers, place, *refs):
+    blocks, (a_ref, bias_ref, skip_ref) = refs[:peers], refs[peers : peers + 3]
+    b_ref, c_ref, cum_ref, row_ref, factor_ref, tail_ref, skip_out, score_ref, dt_ref = refs[peers + 3 :]
+    start = blocks[0].shape[1] - 2 * STATE - LANES
+    in_order(place, blocks, slice(start, start + STATE), b_ref)
+    in_order(place, blocks, slice(start + STATE, start + 2 * STATE), c_ref)
+    in_order(place, blocks, slice(start + 2 * STATE, start + 2 * STATE + LANES), dt_ref)
     per_tile = LANES * GROUPS // HEADS
     group = place[0]
     tile = group // per_tile
@@ -283,8 +287,10 @@
         )
 
 
-def state_kernel(first_head, x_ref, b_ref, factor_ref, tail_ref, send_ref, own_ref):
+def state_kernel(first_head, peers, place, *refs):
+    blocks, (b_ref, factor_ref, tail_ref, x_ref, send_ref, own_ref) = refs[:peers], refs[peers:]
     width = x_ref.shape[1]
+    in_order(place, blocks, slice(0, width), x_ref)
     wide = spread(first_head, width, 2)
     both = []
     for block in range(PAIR):
@@ -335,15 +341,16 @@
             out_ref[base + half : base + BLOCK, columns] = bottom
 
 
-def final_kernel(first_head, place, all_ref, own_ref, c_ref, factor_ref, partial_ref, keep_ref, send_ref):
+def final_kernel(first_head, place, *refs):
+    earlier, (own_ref, c_ref, factor_ref, partial_ref, keep_ref, send_ref) = refs[:-6], refs[-6:]
     width = own_ref.shape[1]
-    pair, core = place[1], place[2]
+    core = place[2]
     wide = spread(first_head, width, 2)
     held = jnp.zeros((STATE, width), F32)
-    for k in range(all_ref.shape[0] - 1):
-        decay = all_ref[k, STATE : STATE + 16].astype(F32)
+    for got in reversed(earlier):
+        decay = got[STATE : STATE + 16].astype(F32)
         decay = decay[0:1] + (decay[1:2] + decay[2:3])
-        held = jnp.where(k < pair, decay * held + all_ref[k, :STATE].astype(F32), held)
+        held = decay * held + got[:STATE].astype(F32)
     factor = dot(factor_ref[...], wide)
     outs = []
     for block in range(PAIR):
@@ -380,17 +387,18 @@
     pl.when(core == 1)(lambda: put(half, 0))
 
 
-def local_call(body, outs, operands, specs=None, flops=0, transcendentals=0, name=None):
+def local_call(body, outs, operands, scratch=(), flops=0, transcendentals=0, name=None):
     shapes = [jax.ShapeDtypeStruct(shape, dtype) for shape, dtype in outs]
-    vmem = pl.BlockSpec(memory_space=pltpu.VMEM)
-    specs = specs or [vmem] * len(operands)
+    smem, vmem = pl.BlockSpec(memory_space=pltpu.SMEM), pl.BlockSpec(memory_space=pltpu.VMEM)
+    specs = [smem if o.dtype == jnp.int32 else vmem for o in operands]
     moved = sum(o.size * o.dtype.itemsize for o in shapes) * 2
     return pl.pallas_call(
         body,
         out_shape=shapes,
         in_specs=specs,
         out_specs=[vmem] * len(outs),
-        compiler_params=pltpu.CompilerParams(vmem_limit_bytes=32 << 20),
+        scratch_shapes=scratch,
+        compiler_params=pltpu.CompilerParams(vmem_limit_bytes=16 << 20),
         cost_estimate=pl.CostEstimate(flops=flops, bytes_accessed=moved, transcendentals=transcendentals),
         name=name,
     )(*operands)
@@ -406,33 +414,27 @@
     context, shard = lax.axis_index("ctx"), lax.axis_index("head")
     pair, core = context // PAIR, context % PAIR
     group = shard * PAIR + core
-    place = jnp.stack([group, pair, core]).astype(jnp.int32)
-    smem, vmem = pl.BlockSpec(memory_space=pltpu.SMEM), pl.BlockSpec(memory_space=pltpu.VMEM)
+    place = jnp.stack([group, pair, core, core * shards + shard]).astype(jnp.int32)
 
     edge = lax.ppermute(xbc[tok - 3 :], axes, [(i, i + 1) for i in range(devices - 1)])
-    exchange = [[k * peers + i for i in range(peers)] for k in range(pairs)]
-    gather = [[k * peers + i for k in range(pairs)] for i in range(peers)]
     swap = [(i * shards + j, (i ^ 1) * shards + j) for i in range(length) for j in range(shards)]
 
-    received = []
+    received, starts = [], []
     first = 0
-    for index, count in enumerate(PIECES):
+    for index, width in enumerate(PIECES):
         sent = activate(
-            xbc, dt_raw, edge, conv_weight, conv_bias[None], first, count, index == 0, shards
-        )
-        got = lax.all_to_all(sent, axes, 0, 0, axis_index_groups=exchange, tiled=True)
-        received.append(got.reshape(slab, got.shape[2]))
-        first += count
-
-    start = PIECES[0] * SUB
-    b = received[0][:, start : start + STATE]
-    c = received[0][:, start + STATE : start + 2 * STATE]
-    raw = received[0][:, start + 2 * STATE :]
-    received[0] = received[0][:, :start]
+            place, xbc, dt_raw, edge, conv_weight, conv_bias[None], first, width, index == 0, shards
+        )
+        received.append(exchange(sent, axes, pairs))
+        starts.append(first // HEAD_DIM)
+        first += width
+
     tiles = [p.reshape(HEADS // LANES, LANES) for p in (a_log, dt_bias, skip_gain)]
-    cum, row, factor, tail, skip, score = local_call(
-        prep_kernel,
+    b, c, cum, row, factor, tail, skip, score = local_call(
+        functools.partial(prep_kernel, peers),
         [
+            ((slab, STATE), BF16),
+            ((slab, STATE), BF16),
             ((slab, LANES), F32),
             ((LANES, slab), F32),
             ((slab, 2 * LANES), BF16),
@@ -440,23 +442,24 @@
             ((16, 3 * LANES), BF16),
             ((slab, BLOCK), F32),
         ],
-        [place, b, c, raw] + tiles,
-        [smem] + [vmem] * 6,
+        [place] + received[0] + tiles,
+        scratch=[pltpu.VMEM((slab, LANES), BF16)],
         flops=2 * slab * BLOCK * (STATE + 3 * LANES),
         name="prep",
     )
-    heads, gathered, owns, partials = [], [], [], []
-    head = 0
-    for x in received:
-        width = x.shape[1]
-        sent, own = local_call(
-            functools.partial(state_kernel, head),
-            [((STATE + 16, width), BF16), ((STATE, width), F32)],
-            [x, b, factor, tail],
+    pieces = []
+    for head, width, blocks in zip(starts, PIECES, received):
+        x, sent, own = local_call(
+            functools.partial(state_kernel, head, peers),
+            [((slab, width), BF16), ((STATE + 16, width), BF16), ((STATE, width), F32)],
+            [place] + blocks + [b, factor, tail],
             flops=4 * slab * STATE * width,
             name="state",
         )
-        gathered.append(lax.all_gather(sent, axes, axis_index_groups=gather))
+        earlier = [
+            lax.ppermute(sent, axes, [(i, i + d * peers) for i in range(devices - d * peers)])
+            for d in range(1, pairs)
+        ]
         (partial,) = local_call(
             functools.partial(local_kernel, head),
             [((slab, width), F32)],
@@ -465,18 +468,13 @@
             transcendentals=slab * BLOCK * width // HEAD_DIM,
             name="local",
         )
-        owns.append(own)
-        partials.append(partial)
-        heads.append(head)
-        head += width // HEAD_DIM
+        pieces.append((head, width, earlier, own, partial))
     keeps, gots = [], []
-    for head, everything, own, partial in zip(heads, gathered, owns, partials):
-        width = own.shape[1]
+    for head, width, earlier, own, partial in pieces:
         keep, send = local_call(
             functools.partial(final_kernel, head),
             [((BLOCK, width), BF16)] * 2,
-            [place, everything, own, c, factor, partial],
-            [smem] + [vmem] * 5,
+            [place] + earlier + [own, c, factor, partial],
             flops=4 * slab * STATE * width,
             name="final",
         )
@@ -486,7 +484,6 @@
         functools.partial(assemble_kernel, len(keeps)),
         [((BLOCK, PAIR * per_group * HEAD_DIM), BF16)],
         [place] + keeps + gots,
-        [smem] + [vmem] * (2 * len(keeps)),
         name="assemble",
     )
     return out

time: 197 us -> 139 us (0.71)
  the two profiles are of different devices: /device:TPU:13 before, /device:TPU:0 now
where the time goes in v2:
time: 139 us
  starting transfers between devices  67.8 us (49%)
  waiting for transfers between devices  41.1 us (30%)
  Pallas kernels  24.1 us (17%)
  local copies, waits for them, and re-layouts  5.44 us (4%)
    ppermute x28, starting transfers between devices, exchange(): got.append(lax.ppermute(blocks[r], axes, route))  37.6 us
    ppermute x12, starting transfers between devices, paired(): lax.ppermute(sent, axes, [(i, i + d * peers) for i in range(devices - d *...  24.6 us
    pallas_call x18, Pallas kernels, local_call(): pl.pallas_call(body, out_shape=shapes, in_specs=specs, out_specs=[vmem] *...  24.1 us
    ppermute x28, waiting for transfers between devices, exchange(): got.append(lax.ppermute(blocks[r], axes, route))  20.1 us
    ppermute x12, waiting for transfers between devices, paired(): lax.ppermute(sent, axes, [(i, i + d * peers) for i in range(devices - d *...  16.2 us
    ppermute x1, starting transfers between devices, paired(): lax.ppermute(xbc[tok - 3:], axes, [(i, i + 1) for i in range(devices - 1)])  4.94 us
    unnamed x20, local copies, waits for them, and re-layouts  4.38 us
    ppermute x1, waiting for transfers between devices, paired(): lax.ppermute(xbc[tok - 3:], axes, [(i, i + 1) for i in range(devices - 1)])  3.33 us
  transfers between devices with their start and end apart: 45, of which 17 were waited for; matrix products, arithmetic and copies ran while one was open for 0% of the time, Pallas kernels for 14%

profile of v2, /device:TPU:0, one launch (start us, length us, event | category | flops | bytes accessed | tf_op | source)
XLA Modules:
  0.0 138.9 jit_solution(10873144895291253973)
XLA Ops:
  1.1 4.9 %collective-permute-start = (bf16[3,20480]{1,0:T(4,128)(2,1)S(1)}, bf16[3,20480]{1,0:T(4,128)(2,1)S(1)}, u32[]{:S(2)}, u32[]{:S(2)}) collective-permute-start(bf16[3,20480]{1,0:T(4,128)(2,1)S(1)} %slice.3), channel_id=1, source_target_pairs={{0,1},{1,2},{2,3},{3,4},{4,5},{5,6},{6,7},{7,8},{8,9},{9,10},{10,1... | collective-permute-start | bytes 368648 | tf_op jit(solution)/shard_map/ppermute | solution.py:419
  6.1 3.3 %collective-permute-done.edge = bf16[3,20480]{1,0:T(4,128)(2,1)S(1)} collective-permute-done((bf16[3,20480]{1,0:T(4,128)(2,1)S(1)}, bf16[3,20480]{1,0:T(4,128)(2,1)S(1)}, u32[]{:S(2)}, u32[]{:S(2)}) %collective-permute-start) | collective-permute-done | bytes 122912 | tf_op jit(solution)/shard_map/ppermute | solution.py:419
  9.4 1.7 %copy-done = bf16[64,20480]{1,0:T(8,128)(2,1)S(1)} copy-done((bf16[64,20480]{1,0:T(8,128)(2,1)S(1)}, bf16[64,20480]{1,0:T(8,128)(2,1)}, u32[]{:S(2)}) %copy-start) | copy-done | bytes 2621464
  13.8 2.4 %conv.4 = (bf16[64,1152]{1,0:T(8,128)(2,1)S(1)}, bf16[64,1152]{1,0:T(8,128)(2,1)S(1)}, bf16[64,1152]{1,0:T(8,128)(2,1)S(1)}, bf16[64,1152]{1,0:T(8,128)(2,1)S(1)...) custom-call(s32[4]{0:T(128)S(1)} %pad_add_fusion.place, ...), custom_call_target="tpu_custom_call" | custom-call | flops 7077888 | bytes 2359296 | tf_op jit(solution)/shard_map/conv/pallas_call | solution.py:395
  16.2 2.5 %collective-permute-start.1 = (bf16[64,1152]{1,0:T(8,128)(2,1)S(1)}, bf16[64,1152]{1,0:T(8,128)(2,1)S(1)}, u32[]{:S(2)}, u32[]{:S(2)}) collective-permute-start(bf16[64,1152]{1,0:T(8,128)(2,1)S(1)} %get-tuple-element.66), channel_id=1, source_target_pairs={{0,1},{1,0},{2,3},{3,2},{4,5},{5,4},{6,7},{7,6},{8,9},{9,8},{10,11... | collective-permute-start | bytes 442376 | tf_op jit(solution)/shard_map/ppermute | solution.py:241
  18.8 2.6 %collective-permute-start.2 = (bf16[64,1152]{1,0:T(8,128)(2,1)S(1)}, bf16[64,1152]{1,0:T(8,128)(2,1)S(1)}, u32[]{:S(2)}, u32[]{:S(2)}) collective-permute-start(bf16[64,1152]{1,0:T(8,128)(2,1)S(1)} %get-tuple-element.67), channel_id=1, source_target_pairs={{0,2},{1,3},{2,0},{3,1},{4,6},{5,7},{6,4},{7,5},{8,10},{9,11},{10,... | collective-permute-start | bytes 442376 | tf_op jit(solution)/shard_map/ppermute | solution.py:241
  21.4 1.5 %conv.5 = (bf16[64,512]{1,0:T(8,128)(2,1)S(1)}, bf16[64,512]{1,0:T(8,128)(2,1)S(1)}, bf16[64,512]{1,0:T(8,128)(2,1)S(1)}, bf16[64,512]{1,0:T(8,128)(2,1)S(1)}, b...) custom-call(s32[4]{0:T(128)S(1)} %pad_add_fusion.place, ...), custom_call_target="tpu_custom_call" | custom-call | flops 3145728 | bytes 1048576 | tf_op jit(solution)/shard_map/conv/pallas_call | solution.py:395
  23.5 3.9 %collective-permute-start.13 = (bf16[64,512]{1,0:T(8,128)(2,1)S(1)}, bf16[64,512]{1,0:T(8,128)(2,1)S(1)}, u32[]{:S(2)}, u32[]{:S(2)}) collective-permute-start(bf16[64,512]{1,0:T(8,128)(2,1)S(1)} %get-tuple-element.88), channel_id=1, source_target_pairs={{0,3},{1,2},{2,1},{3,0},{4,7},{5,6},{6,5},{7,4},{8,11},{9,10},{10,... | collective-permute-start | bytes 196616 | tf_op jit(solution)/shard_map/ppermute | solution.py:241
  27.6 6.1 %collective-permute-done.12.refs_2_ = bf16[64,512]{1,0:T(8,128)(2,1)S(1)} collective-permute-done((bf16[64,512]{1,0:T(8,128)(2,1)S(1)}, bf16[64,512]{1,0:T(8,128)(2,1)S(1)}, u32[]{:S(2)}, u32[]{:S(2)}) %collective-permute-start.12) | collective-permute-done | bytes 65568 | tf_op jit(solution)/shard_map/ppermute | solution.py:241
  35.8 2.1 %collective-permute-start.6 = (bf16[64,1152]{1,0:T(8,128)(2,1)S(1)}, bf16[64,1152]{1,0:T(8,128)(2,1)S(1)}, u32[]{:S(2)}, u32[]{:S(2)}) collective-permute-start(bf16[64,1152]{1,0:T(8,128)(2,1)S(1)} %get-tuple-element.71), channel_id=1, source_target_pairs={{0,6},{1,7},{2,4},{3,5},{4,2},{5,3},{6,0},{7,1},{8,14},{9,15},{10,... | collective-permute-start | bytes 442376 | tf_op jit(solution)/shard_map/ppermute | solution.py:241
  39.2 3.2 %collective-permute-done.3.refs_3_ = bf16[64,1152]{1,0:T(8,128)(2,1)S(1)} collective-permute-done((bf16[64,1152]{1,0:T(8,128)(2,1)S(1)}, bf16[64,1152]{1,0:T(8,128)(2,1)S(1)}, u32[]{:S(2)}, u32[]{:S(2)}) %collective-permute-start.3) | collective-permute-done | bytes 147488 | tf_op jit(solution)/shard_map/ppermute | solution.py:241
  42.4 1.5 %collective-permute-start.16 = (bf16[64,512]{1,0:T(8,128)(2,1)S(1)}, bf16[64,512]{1,0:T(8,128)(2,1)S(1)}, u32[]{:S(2)}, u32[]{:S(2)}) collective-permute-start(bf16[64,512]{1,0:T(8,128)(2,1)S(1)} %get-tuple-element.91), channel_id=1, source_target_pairs={{0,6},{1,7},{2,4},{3,5},{4,2},{5,3},{6,0},{7,1},{8,14},{9,15},{10,... | collective-permute-start | bytes 196616 | tf_op jit(solution)/shard_map/ppermute | solution.py:241
  43.9 1.5 %conv.6 = (bf16[64,512]{1,0:T(8,128)(2,1)S(1)}, bf16[64,512]{1,0:T(8,128)(2,1)S(1)}, bf16[64,512]{1,0:T(8,128)(2,1)S(1)}, bf16[64,512]{1,0:T(8,128)(2,1)S(1)}, b...) custom-call(s32[4]{0:T(128)S(1)} %pad_add_fusion.place, ...), custom_call_target="tpu_custom_call" | custom-call | flops 3145728 | bytes 1048576 | tf_op jit(solution)/shard_map/conv/pallas_call | solution.py:395
  45.5 2.5 %collective-permute-done.5.refs_5_ = bf16[64,1152]{1,0:T(8,128)(2,1)S(1)} collective-permute-done((bf16[64,1152]{1,0:T(8,128)(2,1)S(1)}, bf16[64,1152]{1,0:T(8,128)(2,1)S(1)}, u32[]{:S(2)}, u32[]{:S(2)}) %collective-permute-start.5) | collective-permute-done | bytes 147488 | tf_op jit(solution)/shard_map/ppermute | solution.py:241
  49.4 7.5 %collective-permute-start.22 = (bf16[64,512]{1,0:T(8,128)(2,1)S(1)}, bf16[64,512]{1,0:T(8,128)(2,1)S(1)}, u32[]{:S(2)}, u32[]{:S(2)}) collective-permute-start(bf16[64,512]{1,0:T(8,128)(2,1)S(1)} %get-tuple-element.99), channel_id=1, source_target_pairs={{0,2},{1,3},{2,0},{3,1},{4,6},{5,7},{6,4},{7,5},{8,10},{9,11},{10,... | collective-permute-start | bytes 196616 | tf_op jit(solution)/shard_map/ppermute | solution.py:241
  58.2 2.6 %collective-permute-start.23 = (bf16[64,512]{1,0:T(8,128)(2,1)S(1)}, bf16[64,512]{1,0:T(8,128)(2,1)S(1)}, u32[]{:S(2)}, u32[]{:S(2)}) collective-permute-start(bf16[64,512]{1,0:T(8,128)(2,1)S(1)} %get-tuple-element.100), channel_id=1, source_target_pairs={{0,3},{1,2},{2,1},{3,0},{4,7},{5,6},{6,5},{7,4},{8,11},{9,10},{10,... | collective-permute-start | bytes 196616 | tf_op jit(solution)/shard_map/ppermute | solution.py:241
  62.2 4.5 %collective-permute-start.8 = (bf16[272,512]{1,0:T(8,128)(2,1)S(1)}, bf16[272,512]{1,0:T(8,128)(2,1)S(1)}, u32[]{:S(2)}, u32[]{:S(2)}) collective-permute-start(bf16[272,512]{1,0:T(8,128)(2,1)S(1)} %get-tuple-element.76), channel_id=1, source_target_pairs={{0,8},{1,9},{2,10},{3,11},{4,12},{5,13},{6,14},{7,15},{8,16},{9,17... | collective-permute-start | bytes 835592 | tf_op jit(solution)/shard_map/ppermute | solution.py:460
  66.7 3.0 %collective-permute-start.9 = (bf16[272,512]{1,0:T(8,128)(2,1)S(1)}, bf16[272,512]{1,0:T(8,128)(2,1)S(1)}, u32[]{:S(2)}, u32[]{:S(2)}) collective-permute-start(bf16[272,512]{1,0:T(8,128)(2,1)S(1)} %get-tuple-element.76), channel_id=1, source_target_pairs={{0,16},{1,17},{2,18},{3,19},{4,20},{5,21},{6,22},{7,23},{8,24},{9,... | collective-permute-start | bytes 835592 | tf_op jit(solution)/shard_map/ppermute | solution.py:460
  70.7 2.7 %collective-permute-start.27 = (bf16[64,512]{1,0:T(8,128)(2,1)S(1)}, bf16[64,512]{1,0:T(8,128)(2,1)S(1)}, u32[]{:S(2)}, u32[]{:S(2)}) collective-permute-start(bf16[64,512]{1,0:T(8,128)(2,1)S(1)} %get-tuple-element.104), channel_id=1, source_target_pairs={{0,7},{1,6},{2,5},{3,4},{4,3},{5,2},{6,1},{7,0},{8,15},{9,14},{10,... | collective-permute-start | bytes 196616 | tf_op jit(solution)/shard_map/ppermute | solution.py:241
  73.5 1.5 %conv.7 = (bf16[64,512]{1,0:T(8,128)(2,1)S(1)}, bf16[64,512]{1,0:T(8,128)(2,1)S(1)}, bf16[64,512]{1,0:T(8,128)(2,1)S(1)}, bf16[64,512]{1,0:T(8,128)(2,1)S(1)}, b...) custom-call(s32[4]{0:T(128)S(1)} %pad_add_fusion.place, ...), custom_call_target="tpu_custom_call" | custom-call | flops 3145728 | bytes 1048576 | tf_op jit(solution)/shard_map/conv/pallas_call | solution.py:395
  75.1 2.7 %collective-permute-done.26.refs_6_ = bf16[64,512]{1,0:T(8,128)(2,1)S(1)} collective-permute-done((bf16[64,512]{1,0:T(8,128)(2,1)S(1)}, bf16[64,512]{1,0:T(8,128)(2,1)S(1)}, u32[]{:S(2)}, u32[]{:S(2)}) %collective-permute-start.26) | collective-permute-done | bytes 65568 | tf_op jit(solution)/shard_map/ppermute | solution.py:241
  77.8 2.4 %collective-permute-start.33 = (bf16[64,512]{1,0:T(8,128)(2,1)S(1)}, bf16[64,512]{1,0:T(8,128)(2,1)S(1)}, u32[]{:S(2)}, u32[]{:S(2)}) collective-permute-start(bf16[64,512]{1,0:T(8,128)(2,1)S(1)} %get-tuple-element.112), channel_id=1, source_target_pairs={{0,3},{1,2},{2,1},{3,0},{4,7},{5,6},{6,5},{7,4},{8,11},{9,10},{10,... | collective-permute-start | bytes 196616 | tf_op jit(solution)/shard_map/ppermute | solution.py:241
  80.2 4.8 %collective-permute-done.32.refs_2_ = bf16[64,512]{1,0:T(8,128)(2,1)S(1)} collective-permute-done((bf16[64,512]{1,0:T(8,128)(2,1)S(1)}, bf16[64,512]{1,0:T(8,128)(2,1)S(1)}, u32[]{:S(2)}, u32[]{:S(2)}) %collective-permute-start.32) | collective-permute-done | bytes 65568 | tf_op jit(solution)/shard_map/ppermute | solution.py:241
  85.8 2.8 %collective-permute-start.37 = (bf16[64,512]{1,0:T(8,128)(2,1)S(1)}, bf16[64,512]{1,0:T(8,128)(2,1)S(1)}, u32[]{:S(2)}, u32[]{:S(2)}) collective-permute-start(bf16[64,512]{1,0:T(8,128)(2,1)S(1)} %get-tuple-element.116), channel_id=1, source_target_pairs={{0,7},{1,6},{2,5},{3,4},{4,3},{5,2},{6,1},{7,0},{8,15},{9,14},{10,... | collective-permute-start | bytes 196616 | tf_op jit(solution)/shard_map/ppermute | solution.py:241
  96.8 1.5 %collective-permute-start.28 = (bf16[272,512]{1,0:T(8,128)(2,1)S(1)}, bf16[272,512]{1,0:T(8,128)(2,1)S(1)}, u32[]{:S(2)}, u32[]{:S(2)}) collective-permute-start(bf16[272,512]{1,0:T(8,128)(2,1)S(1)} %get-tuple-element.105), channel_id=1, source_target_pairs={{0,8},{1,9},{2,10},{3,11},{4,12},{5,13},{6,14},{7,15},{8,16},{9,17... | collective-permute-start | bytes 835592 | tf_op jit(solution)/shard_map/ppermute | solution.py:460
  99.8 4.7 %collective-permute-done.18.refs_0_ = bf16[272,512]{1,0:T(8,128)(2,1)S(1)} collective-permute-done((bf16[272,512]{1,0:T(8,128)(2,1)S(1)}, bf16[272,512]{1,0:T(8,128)(2,1)S(1)}, u32[]{:S(2)}, u32[]{:S(2)}) %collective-permute-start.18) | collective-permute-done | bytes 278560 | tf_op jit(solution)/shard_map/ppermute | solution.py:460
  107.3 4.0 %collective-permute-done.19.refs_1_ = bf16[272,512]{1,0:T(8,128)(2,1)S(1)} collective-permute-done((bf16[272,512]{1,0:T(8,128)(2,1)S(1)}, bf16[272,512]{1,0:T(8,128)(2,1)S(1)}, u32[]{:S(2)}, u32[]{:S(2)}) %collective-permute-start.19) | collective-permute-done | bytes 278560 | tf_op jit(solution)/shard_map/ppermute | solution.py:460
  112.7 5.0 %collective-permute-start.39 = (bf16[272,512]{1,0:T(8,128)(2,1)S(1)}, bf16[272,512]{1,0:T(8,128)(2,1)S(1)}, u32[]{:S(2)}, u32[]{:S(2)}) collective-permute-start(bf16[272,512]{1,0:T(8,128)(2,1)S(1)} %get-tuple-element.117), channel_id=1, source_target_pairs={{0,16},{1,17},{2,18},{3,19},{4,20},{5,21},{6,22},{7,23},{8,24},{9,... | collective-permute-start | bytes 835592 | tf_op jit(solution)/shard_map/ppermute | solution.py:460
  126.9 1.5 %collective-permute-done.38.refs_0_ = bf16[272,512]{1,0:T(8,128)(2,1)S(1)} collective-permute-done((bf16[272,512]{1,0:T(8,128)(2,1)S(1)}, bf16[272,512]{1,0:T(8,128)(2,1)S(1)}, u32[]{:S(2)}, u32[]{:S(2)}) %collective-permute-start.38) | collective-permute-done | bytes 278560 | tf_op jit(solution)/shard_map/ppermute | solution.py:460
  129.3 5.0 %collective-permute-done.40.refs_2_ = bf16[272,512]{1,0:T(8,128)(2,1)S(1)} collective-permute-done((bf16[272,512]{1,0:T(8,128)(2,1)S(1)}, bf16[272,512]{1,0:T(8,128)(2,1)S(1)}, u32[]{:S(2)}, u32[]{:S(2)}) %collective-permute-start.40) | collective-permute-done | bytes 278560 | tf_op jit(solution)/shard_map/ppermute | solution.py:460
  135.4 1.5 %collective-permute-done.44.refs_7_ = bf16[256,512]{1,0:T(8,128)(2,1)S(1)} collective-permute-done((bf16[256,512]{1,0:T(8,128)(2,1)S(1)}, bf16[256,512]{1,0:T(8,128)(2,1)S(1)}, u32[]{:S(2)}, u32[]{:S(2)}) %collective-permute-start.44) | collective-permute-done | bytes 262176 | tf_op jit(solution)/shard_map/ppermute | solution.py:482
  136.9 2.0 %assemble.1 = bf16[256,4096]{1,0:T(8,128)(2,1)} custom-call(s32[4]{0:T(128)S(1)} %pad_add_fusion.place, bf16[256,512]{1,0:T(8,128)(2,1)S(1)} %get-tuple-element.84.refs_0_, bf16[256,512]{1,0:T(8,128)(2,1)S(1)} %get-tuple-element.96.refs_1_, bf16[256,512]{1,0:T(8,128)(2,1)S(1)} %get-tuple-element.108.refs_2_, ...), custom_call_target="tpu_custom_call" | custom-call | bytes 4194304 | tf_op jit(solution)/shard_map/assemble/pallas_call | solution.py:395
  (98 shorter events, 38.7 us)
Async XLA Ops:
  1.1 8.4 %collective-permute-start = (bf16[3,20480]{1,0:T(4,128)(2,1)S(1)}, bf16[3,20480]{1,0:T(4,128)(2,1)S(1)}, u32[]{:S(2)}, u32[]{:S(2)}) collective-permute-start(bf16[3,20480]{1,0:T(4,128)(2,1)S(1)} %slice.3), channel_id=1, source_target_pairs={{0,1},{1,2},{2,3},{3,4},{4,5},{5,6},{6,7},{7,8},{8,9},{9,10},{10,1... | collective-permute-start | bytes 368648 | tf_op jit(solution)/shard_map/ppermute | solution.py:419
  16.2 19.6 %collective-permute-start.1 = (bf16[64,1152]{1,0:T(8,128)(2,1)S(1)}, bf16[64,1152]{1,0:T(8,128)(2,1)S(1)}, u32[]{:S(2)}, u32[]{:S(2)}) collective-permute-start(bf16[64,1152]{1,0:T(8,128)(2,1)S(1)} %get-tuple-element.66), channel_id=1, source_target_pairs={{0,1},{1,0},{2,3},{3,2},{4,5},{5,4},{6,7},{7,6},{8,9},{9,8},{10,11... | collective-permute-start | bytes 442376 | tf_op jit(solution)/shard_map/ppermute | solution.py:241
  18.8 19.1 %collective-permute-start.2 = (bf16[64,1152]{1,0:T(8,128)(2,1)S(1)}, bf16[64,1152]{1,0:T(8,128)(2,1)S(1)}, u32[]{:S(2)}, u32[]{:S(2)}) collective-permute-start(bf16[64,1152]{1,0:T(8,128)(2,1)S(1)} %get-tuple-element.67), channel_id=1, source_target_pairs={{0,2},{1,3},{2,0},{3,1},{4,6},{5,7},{6,4},{7,5},{8,10},{9,11},{10,... | collective-permute-start | bytes 442376 | tf_op jit(solution)/shard_map/ppermute | solution.py:241
  23.4 10.3 %collective-permute-start.12 = (bf16[64,512]{1,0:T(8,128)(2,1)S(1)}, bf16[64,512]{1,0:T(8,128)(2,1)S(1)}, u32[]{:S(2)}, u32[]{:S(2)}) collective-permute-start(bf16[64,512]{1,0:T(8,128)(2,1)S(1)} %get-tuple-element.87), channel_id=1, source_target_pairs={{0,2},{1,3},{2,0},{3,1},{4,6},{5,7},{6,4},{7,5},{8,10},{9,11},{10,... | collective-permute-start | bytes 196616 | tf_op jit(solution)/shard_map/ppermute | solution.py:241
  23.5 11.5 %collective-permute-start.13 = (bf16[64,512]{1,0:T(8,128)(2,1)S(1)}, bf16[64,512]{1,0:T(8,128)(2,1)S(1)}, u32[]{:S(2)}, u32[]{:S(2)}) collective-permute-start(bf16[64,512]{1,0:T(8,128)(2,1)S(1)} %get-tuple-element.88), channel_id=1, source_target_pairs={{0,3},{1,2},{2,1},{3,0},{4,7},{5,6},{6,5},{7,4},{8,11},{9,10},{10,... | collective-permute-start | bytes 196616 | tf_op jit(solution)/shard_map/ppermute | solution.py:241
  33.7 8.6 %collective-permute-start.3 = (bf16[64,1152]{1,0:T(8,128)(2,1)S(1)}, bf16[64,1152]{1,0:T(8,128)(2,1)S(1)}, u32[]{:S(2)}, u32[]{:S(2)}) collective-permute-start(bf16[64,1152]{1,0:T(8,128)(2,1)S(1)} %get-tuple-element.68), channel_id=1, source_target_pairs={{0,3},{1,2},{2,1},{3,0},{4,7},{5,6},{6,5},{7,4},{8,11},{9,10},{10,... | collective-permute-start | bytes 442376 | tf_op jit(solution)/shard_map/ppermute | solution.py:241
  35.0 13.0 %collective-permute-start.5 = (bf16[64,1152]{1,0:T(8,128)(2,1)S(1)}, bf16[64,1152]{1,0:T(8,128)(2,1)S(1)}, u32[]{:S(2)}, u32[]{:S(2)}) collective-permute-start(bf16[64,1152]{1,0:T(8,128)(2,1)S(1)} %get-tuple-element.70), channel_id=1, source_target_pairs={{0,5},{1,4},{2,7},{3,6},{4,1},{5,0},{6,3},{7,2},{8,13},{9,12},{10,... | collective-permute-start | bytes 442376 | tf_op jit(solution)/shard_map/ppermute | solution.py:241
  35.8 13.5 %collective-permute-start.6 = (bf16[64,1152]{1,0:T(8,128)(2,1)S(1)}, bf16[64,1152]{1,0:T(8,128)(2,1)S(1)}, u32[]{:S(2)}, u32[]{:S(2)}) collective-permute-start(bf16[64,1152]{1,0:T(8,128)(2,1)S(1)} %get-tuple-element.71), channel_id=1, source_target_pairs={{0,6},{1,7},{2,4},{3,5},{4,2},{5,3},{6,0},{7,1},{8,14},{9,15},{10,... | collective-permute-start | bytes 442376 | tf_op jit(solution)/shard_map/ppermute | solution.py:241
  37.9 11.4 %collective-permute-start.7 = (bf16[64,1152]{1,0:T(8,128)(2,1)S(1)}, bf16[64,1152]{1,0:T(8,128)(2,1)S(1)}, u32[]{:S(2)}, u32[]{:S(2)}) collective-permute-start(bf16[64,1152]{1,0:T(8,128)(2,1)S(1)} %get-tuple-element.72), channel_id=1, source_target_pairs={{0,7},{1,6},{2,5},{3,4},{4,3},{5,2},{6,1},{7,0},{8,15},{9,14},{10,... | collective-permute-start | bytes 442376 | tf_op jit(solution)/shard_map/ppermute | solution.py:241
  42.4 15.8 %collective-permute-start.15 = (bf16[64,512]{1,0:T(8,128)(2,1)S(1)}, bf16[64,512]{1,0:T(8,128)(2,1)S(1)}, u32[]{:S(2)}, u32[]{:S(2)}) collective-permute-start(bf16[64,512]{1,0:T(8,128)(2,1)S(1)} %get-tuple-element.90), channel_id=1, source_target_pairs={{0,5},{1,4},{2,7},{3,6},{4,1},{5,0},{6,3},{7,2},{8,13},{9,12},{10,... | collective-permute-start | bytes 196616 | tf_op jit(solution)/shard_map/ppermute | solution.py:241
  42.4 18.4 %collective-permute-start.16 = (bf16[64,512]{1,0:T(8,128)(2,1)S(1)}, bf16[64,512]{1,0:T(8,128)(2,1)S(1)}, u32[]{:S(2)}, u32[]{:S(2)}) collective-permute-start(bf16[64,512]{1,0:T(8,128)(2,1)S(1)} %get-tuple-element.91), channel_id=1, source_target_pairs={{0,6},{1,7},{2,4},{3,5},{4,2},{5,3},{6,0},{7,1},{8,14},{9,15},{10,... | collective-permute-start | bytes 196616 | tf_op jit(solution)/shard_map/ppermute | solution.py:241
  48.0 14.2 %collective-permute-start.17 = (bf16[64,512]{1,0:T(8,128)(2,1)S(1)}, bf16[64,512]{1,0:T(8,128)(2,1)S(1)}, u32[]{:S(2)}, u32[]{:S(2)}) collective-permute-start(bf16[64,512]{1,0:T(8,128)(2,1)S(1)} %get-tuple-element.92), channel_id=1, source_target_pairs={{0,7},{1,6},{2,5},{3,4},{4,3},{5,2},{6,1},{7,0},{8,15},{9,14},{10,... | collective-permute-start | bytes 196616 | tf_op jit(solution)/shard_map/ppermute | solution.py:241
  49.4 17.3 %collective-permute-start.21 = (bf16[64,512]{1,0:T(8,128)(2,1)S(1)}, bf16[64,512]{1,0:T(8,128)(2,1)S(1)}, u32[]{:S(2)}, u32[]{:S(2)}) collective-permute-start(bf16[64,512]{1,0:T(8,128)(2,1)S(1)} %get-tuple-element.98), channel_id=1, source_target_pairs={{0,1},{1,0},{2,3},{3,2},{4,5},{5,4},{6,7},{7,6},{8,9},{9,8},{10,11... | collective-permute-start | bytes 196616 | tf_op jit(solution)/shard_map/ppermute | solution.py:241
  49.4 20.3 %collective-permute-start.22 = (bf16[64,512]{1,0:T(8,128)(2,1)S(1)}, bf16[64,512]{1,0:T(8,128)(2,1)S(1)}, u32[]{:S(2)}, u32[]{:S(2)}) collective-permute-start(bf16[64,512]{1,0:T(8,128)(2,1)S(1)} %get-tuple-element.99), channel_id=1, source_target_pairs={{0,2},{1,3},{2,0},{3,1},{4,6},{5,7},{6,4},{7,5},{8,10},{9,11},{10,... | collective-permute-start | bytes 196616 | tf_op jit(solution)/shard_map/ppermute | solution.py:241
  58.2 11.6 %collective-permute-start.23 = (bf16[64,512]{1,0:T(8,128)(2,1)S(1)}, bf16[64,512]{1,0:T(8,128)(2,1)S(1)}, u32[]{:S(2)}, u32[]{:S(2)}) collective-permute-start(bf16[64,512]{1,0:T(8,128)(2,1)S(1)} %get-tuple-element.100), channel_id=1, source_target_pairs={{0,3},{1,2},{2,1},{3,0},{4,7},{5,6},{6,5},{7,4},{8,11},{9,10},{10,... | collective-permute-start | bytes 196616 | tf_op jit(solution)/shard_map/ppermute | solution.py:241
  60.8 9.9 %collective-permute-start.24 = (bf16[64,512]{1,0:T(8,128)(2,1)S(1)}, bf16[64,512]{1,0:T(8,128)(2,1)S(1)}, u32[]{:S(2)}, u32[]{:S(2)}) collective-permute-start(bf16[64,512]{1,0:T(8,128)(2,1)S(1)} %get-tuple-element.101), channel_id=1, source_target_pairs={{0,4},{1,5},{2,6},{3,7},{4,0},{5,1},{6,2},{7,3},{8,12},{9,13},{10,... | collective-permute-start | bytes 196616 | tf_op jit(solution)/shard_map/ppermute | solution.py:241
  62.2 33.3 %collective-permute-start.8 = (bf16[272,512]{1,0:T(8,128)(2,1)S(1)}, bf16[272,512]{1,0:T(8,128)(2,1)S(1)}, u32[]{:S(2)}, u32[]{:S(2)}) collective-permute-start(bf16[272,512]{1,0:T(8,128)(2,1)S(1)} %get-tuple-element.76), channel_id=1, source_target_pairs={{0,8},{1,9},{2,10},{3,11},{4,12},{5,13},{6,14},{7,15},{8,16},{9,17... | collective-permute-start | bytes 835592 | tf_op jit(solution)/shard_map/ppermute | solution.py:460
  66.7 30.1 %collective-permute-start.9 = (bf16[272,512]{1,0:T(8,128)(2,1)S(1)}, bf16[272,512]{1,0:T(8,128)(2,1)S(1)}, u32[]{:S(2)}, u32[]{:S(2)}) collective-permute-start(bf16[272,512]{1,0:T(8,128)(2,1)S(1)} %get-tuple-element.76), channel_id=1, source_target_pairs={{0,16},{1,17},{2,18},{3,19},{4,20},{5,21},{6,22},{7,23},{8,24},{9,... | collective-permute-start | bytes 835592 | tf_op jit(solution)/shard_map/ppermute | solution.py:460
  69.8 8.0 %collective-permute-start.26 = (bf16[64,512]{1,0:T(8,128)(2,1)S(1)}, bf16[64,512]{1,0:T(8,128)(2,1)S(1)}, u32[]{:S(2)}, u32[]{:S(2)}) collective-permute-start(bf16[64,512]{1,0:T(8,128)(2,1)S(1)} %get-tuple-element.103), channel_id=1, source_target_pairs={{0,6},{1,7},{2,4},{3,5},{4,2},{5,3},{6,0},{7,1},{8,14},{9,15},{10,... | collective-permute-start | bytes 196616 | tf_op jit(solution)/shard_map/ppermute | solution.py:241
  85.8 8.3 %collective-permute-start.37 = (bf16[64,512]{1,0:T(8,128)(2,1)S(1)}, bf16[64,512]{1,0:T(8,128)(2,1)S(1)}, u32[]{:S(2)}, u32[]{:S(2)}) collective-permute-start(bf16[64,512]{1,0:T(8,128)(2,1)S(1)} %get-tuple-element.116), channel_id=1, source_target_pairs={{0,7},{1,6},{2,5},{3,4},{4,3},{5,2},{6,1},{7,0},{8,15},{9,14},{10,... | collective-permute-start | bytes 196616 | tf_op jit(solution)/shard_map/ppermute | solution.py:241
  90.1 8.4 %collective-permute-start.10 = (bf16[272,512]{1,0:T(8,128)(2,1)S(1)}, bf16[272,512]{1,0:T(8,128)(2,1)S(1)}, u32[]{:S(2)}, u32[]{:S(2)}) collective-permute-start(bf16[272,512]{1,0:T(8,128)(2,1)S(1)} %get-tuple-element.76), channel_id=1, source_target_pairs={{0,24},{1,25},{2,26},{3,27},{4,28},{5,29},{6,30},{7,31}} | collective-permute-start | bytes 835592 | tf_op jit(solution)/shard_map/ppermute | solution.py:460
  91.5 13.0 %collective-permute-start.18 = (bf16[272,512]{1,0:T(8,128)(2,1)S(1)}, bf16[272,512]{1,0:T(8,128)(2,1)S(1)}, u32[]{:S(2)}, u32[]{:S(2)}) collective-permute-start(bf16[272,512]{1,0:T(8,128)(2,1)S(1)} %get-tuple-element.93), channel_id=1, source_target_pairs={{0,8},{1,9},{2,10},{3,11},{4,12},{5,13},{6,14},{7,15},{8,16},{9,17... | collective-permute-start | bytes 835592 | tf_op jit(solution)/shard_map/ppermute | solution.py:460
  94.1 17.2 %collective-permute-start.19 = (bf16[272,512]{1,0:T(8,128)(2,1)S(1)}, bf16[272,512]{1,0:T(8,128)(2,1)S(1)}, u32[]{:S(2)}, u32[]{:S(2)}) collective-permute-start(bf16[272,512]{1,0:T(8,128)(2,1)S(1)} %get-tuple-element.93), channel_id=1, source_target_pairs={{0,16},{1,17},{2,18},{3,19},{4,20},{5,21},{6,22},{7,23},{8,24},{9,... | collective-permute-start | bytes 835592 | tf_op jit(solution)/shard_map/ppermute | solution.py:460
  95.5 17.2 %collective-permute-start.20 = (bf16[272,512]{1,0:T(8,128)(2,1)S(1)}, bf16[272,512]{1,0:T(8,128)(2,1)S(1)}, u32[]{:S(2)}, u32[]{:S(2)}) collective-permute-start(bf16[272,512]{1,0:T(8,128)(2,1)S(1)} %get-tuple-element.93), channel_id=1, source_target_pairs={{0,24},{1,25},{2,26},{3,27},{4,28},{5,29},{6,30},{7,31}} | collective-permute-start | bytes 835592 | tf_op jit(solution)/shard_map/ppermute | solution.py:460
  96.8 20.9 %collective-permute-start.28 = (bf16[272,512]{1,0:T(8,128)(2,1)S(1)}, bf16[272,512]{1,0:T(8,128)(2,1)S(1)}, u32[]{:S(2)}, u32[]{:S(2)}) collective-permute-start(bf16[272,512]{1,0:T(8,128)(2,1)S(1)} %get-tuple-element.105), channel_id=1, source_target_pairs={{0,8},{1,9},{2,10},{3,11},{4,12},{5,13},{6,14},{7,15},{8,16},{9,17... | collective-permute-start | bytes 835592 | tf_op jit(solution)/shard_map/ppermute | solution.py:460
  98.5 26.7 %collective-permute-start.29 = (bf16[272,512]{1,0:T(8,128)(2,1)S(1)}, bf16[272,512]{1,0:T(8,128)(2,1)S(1)}, u32[]{:S(2)}, u32[]{:S(2)}) collective-permute-start(bf16[272,512]{1,0:T(8,128)(2,1)S(1)} %get-tuple-element.105), channel_id=1, source_target_pairs={{0,16},{1,17},{2,18},{3,19},{4,20},{5,21},{6,22},{7,23},{8,24},{9,... | collective-permute-start | bytes 835592 | tf_op jit(solution)/shard_map/ppermute | solution.py:460
  104.5 20.9 %collective-permute-start.30 = (bf16[272,512]{1,0:T(8,128)(2,1)S(1)}, bf16[272,512]{1,0:T(8,128)(2,1)S(1)}, u32[]{:S(2)}, u32[]{:S(2)}) collective-permute-start(bf16[272,512]{1,0:T(8,128)(2,1)S(1)} %get-tuple-element.105), channel_id=1, source_target_pairs={{0,24},{1,25},{2,26},{3,27},{4,28},{5,29},{6,30},{7,31}} | collective-permute-start | bytes 835592 | tf_op jit(solution)/shard_map/ppermute | solution.py:460
  111.3 17.1 %collective-permute-start.38 = (bf16[272,512]{1,0:T(8,128)(2,1)S(1)}, bf16[272,512]{1,0:T(8,128)(2,1)S(1)}, u32[]{:S(2)}, u32[]{:S(2)}) collective-permute-start(bf16[272,512]{1,0:T(8,128)(2,1)S(1)} %get-tuple-element.117), channel_id=1, source_target_pairs={{0,8},{1,9},{2,10},{3,11},{4,12},{5,13},{6,14},{7,15},{8,16},{9,17... | collective-permute-start | bytes 835592 | tf_op jit(solution)/shard_map/ppermute | solution.py:460
  112.7 16.6 %collective-permute-start.39 = (bf16[272,512]{1,0:T(8,128)(2,1)S(1)}, bf16[272,512]{1,0:T(8,128)(2,1)S(1)}, u32[]{:S(2)}, u32[]{:S(2)}) collective-permute-start(bf16[272,512]{1,0:T(8,128)(2,1)S(1)} %get-tuple-element.117), channel_id=1, source_target_pairs={{0,16},{1,17},{2,18},{3,19},{4,20},{5,21},{6,22},{7,23},{8,24},{9,... | collective-permute-start | bytes 835592 | tf_op jit(solution)/shard_map/ppermute | solution.py:460
  117.7 16.5 %collective-permute-start.40 = (bf16[272,512]{1,0:T(8,128)(2,1)S(1)}, bf16[272,512]{1,0:T(8,128)(2,1)S(1)}, u32[]{:S(2)}, u32[]{:S(2)}) collective-permute-start(bf16[272,512]{1,0:T(8,128)(2,1)S(1)} %get-tuple-element.117), channel_id=1, source_target_pairs={{0,24},{1,25},{2,26},{3,27},{4,28},{5,29},{6,30},{7,31}} | collective-permute-start | bytes 835592 | tf_op jit(solution)/shard_map/ppermute | solution.py:460
  125.2 10.2 %collective-permute-start.41 = (bf16[256,512]{1,0:T(8,128)(2,1)S(1)}, bf16[256,512]{1,0:T(8,128)(2,1)S(1)}, u32[]{:S(2)}, u32[]{:S(2)}) collective-permute-start(bf16[256,512]{1,0:T(8,128)(2,1)S(1)} %get-tuple-element.121), channel_id=1, source_target_pairs={{0,4},{1,5},{2,6},{3,7},{4,0},{5,1},{6,2},{7,3},{8,12},{9,13},{10,... | collective-permute-start | bytes 786440 | tf_op jit(solution)/shard_map/ppermute | solution.py:482
  125.3 10.1 %collective-permute-start.42 = (bf16[256,512]{1,0:T(8,128)(2,1)S(1)}, bf16[256,512]{1,0:T(8,128)(2,1)S(1)}, u32[]{:S(2)}, u32[]{:S(2)}) collective-permute-start(bf16[256,512]{1,0:T(8,128)(2,1)S(1)} %get-tuple-element.122), channel_id=1, source_target_pairs={{0,4},{1,5},{2,6},{3,7},{4,0},{5,1},{6,2},{7,3},{8,12},{9,13},{10,... | collective-permute-start | bytes 786440 | tf_op jit(solution)/shard_map/ppermute | solution.py:482
  (23 other events, 289.2 us)

commit v3 on v2

--- a/solution.py
+++ b/solution.py
@@ -161,7 +161,7 @@
 
 PAIR = 2
 LANES = 128
-PIECES = (512, 512, 512, 512)
+PIECES = ((384, "BD"), (640, "C"), (640, ""), (384, ""))
 LOG2E = 1.4426950408889634
 F32, BF16 = jnp.float32, jnp.bfloat16
 
@@ -185,77 +185,132 @@
     return jnp.dot(a, b, preferred_element_type=F32)
 
 
-def conv_kernel(parts, shards, with_step, place, xbc, edge, weight, bias, *refs):
-    peers = shards * PAIR
-    if with_step:
-        dt_ref, refs = refs[0], refs[1:]
-    outs, wide = refs[:peers], refs[peers]
+def pack_kernel(shards, place, xbc, dt_raw, weight, bias, own, send, taps, offset, near, far, tail, sems):
+    core, shard = place[2], place[4]
+    inner = HEADS * HEAD_DIM
     count = xbc.shape[0]
-    for r in range(peers):
-        peer = place[3] ^ r
-        group = (peer % shards) * PAIR + peer // shards
-        start = 0
-        for origin, stride, width in parts:
-            at = pl.ds(pl.multiple_of(origin + group * stride, LANES), width)
-            wide[5:8, :width] = edge[:, at].astype(F32)
-            wide[8:, :width] = xbc[:, at].astype(F32)
-            tap = weight[:, at] * 0.5
-            acc = bias[:, at] * 0.5 + tap[0:1] * wide[5 : 5 + count, :width]
-            acc = acc + tap[1:2] * wide[6 : 6 + count, :width]
-            acc = acc + tap[2:3] * wide[7 : 7 + count, :width]
-            acc = acc + tap[3:4] * wide[8 : 8 + count, :width]
-            outs[r][:, start : start + width] = (acc + acc * jnp.tanh(acc)).astype(BF16)
-            start += width
-        if with_step:
-            tile = group // (LANES * GROUPS // HEADS)
-            outs[r][:, start : start + LANES] = dt_ref[:, pl.ds(pl.multiple_of(tile * LANES, LANES), LANES)]
-
-
-def activate(place, xbc, dt_raw, edge, weight, bias, first, width, with_rest, shards):
-    tok = xbc.shape[0]
-    inner = HEADS * HEAD_DIM
-    parts = [(first, inner // GROUPS, width)]
-    operands = [place, xbc, edge, weight, bias]
-    total = width
-    if with_rest:
-        parts += [(inner, STATE, STATE), (inner + GROUPS * STATE, STATE, STATE)]
-        operands.append(dt_raw)
-        total += 2 * STATE + LANES
-    peers = shards * PAIR
+    per_group = inner // GROUPS
+    rest = per_group * shards
+
+    def columns(z, side):
+        for r in range(shards):
+            group = (z ^ r) * PAIR + side
+            yield r * per_group, group * per_group, per_group
+            yield rest + r * STATE, inner + group * STATE, STATE
+            yield rest + (shards + r) * STATE, inner + (GROUPS + group) * STATE, STATE
+
+    def ds(start, width):
+        return pl.ds(pl.multiple_of(start, LANES), width)
+
+    copies = [(xbc.at[count - 16 :], tail)]
+    for side, out in ((1 - core, send), (core, own)):
+        for to, start, width in columns(shard, side):
+            copies.append((xbc.at[:, ds(start, width)], out.at[:, to : to + width]))
+        copies.append((dt_raw, out.at[:, out.shape[1] - HEADS :]))
+    for to, start, width in columns(shard, core):
+        copies.append((weight.at[:, ds(start, width)], taps.at[:, to : to + width]))
+        copies.append((bias.at[:, ds(start, width)], offset.at[:, to : to + width]))
+    started = []
+    for i, (source, target) in enumerate(copies):
+        copy = pltpu.make_async_copy(source, target, sems.at[i])
+        copy.start()
+        started.append(copy)
+    started[0].wait()
+    next_shard = jnp.where(shard == shards - 1, 0, shard + 1)
+    side = jnp.where(shard == shards - 1, 1 - core, core)
+    for edge, towards in ((near, side), (far, 1 - side)):
+        for to, start, width in columns(next_shard, towards):
+            rows = tail[:, ds(start, width)].astype(F32)
+            edge[:, to : to + width] = rows[13:16].astype(BF16)
+    for copy in started[1:]:
+        copy.wait()
+
+
+def pack(place, xbc, dt_raw, weight, bias, shards):
+    tok, channels = xbc.shape
+    half = channels // PAIR
+    smem, vmem, anywhere = (pl.BlockSpec(memory_space=m) for m in (pltpu.SMEM, pltpu.VMEM, pl.ANY))
+    outs = [((tok, half + HEADS), BF16)] * 2 + [((4, half), F32), ((1, half), F32)] + [((3, half), BF16)] * 2
+    return pl.pallas_call(
+        functools.partial(pack_kernel, shards),
+        out_shape=[jax.ShapeDtypeStruct(shape, dtype) for shape, dtype in outs],
+        in_specs=[smem] + [anywhere] * 4,
+        out_specs=[vmem] * len(outs),
+        scratch_shapes=[pltpu.VMEM((16, channels), BF16), pltpu.SemaphoreType.DMA((3 + 12 * shards,))],
+        compiler_params=pltpu.CompilerParams(vmem_limit_bytes=16 << 20),
+        name="pack",
+    )(place, xbc, dt_raw, weight, bias)
+
+
+def conv_kernel(parts, shards, place, *refs):
+    rows, edges, (weight, bias), outs, wide = refs[0:2], refs[2:4], refs[4:6], refs[6:-1], refs[-1]
+    count, total = rows[0].shape
+    core, shard = place[2], place[4]
+    for side in range(PAIR):
+        here = pl.ds(pl.multiple_of(jnp.where(core == 0, side, 1 - side) * count, count), count)
+        for r in range(shards):
+            start = 0
+            for origin, stride, width in parts:
+                to = slice(start, start + width)
+                start += width
+                if stride == 0:
+                    tile = ((shard ^ r) * PAIR + core) // (LANES * GROUPS // HEADS)
+                    at = pl.ds(pl.multiple_of(total - HEADS + tile * LANES, LANES), LANES)
+                    outs[r][here, to] = rows[side][:, at]
+                    continue
+                at = slice(origin + r * stride, origin + r * stride + width)
+                wide[5:8, :width] = edges[side][:, at].astype(F32)
+                wide[8:, :width] = rows[side][:, at].astype(F32)
+                tap = weight[:, at] * 0.5
+                acc = bias[:, at] * 0.5 + tap[0:1] * wide[5 : 5 + count, :width]
+                acc = acc + tap[1:2] * wide[6 : 6 + count, :width]
+                acc = acc + tap[2:3] * wide[7 : 7 + count, :width]
+                acc = acc + tap[3:4] * wide[8 : 8 + count, :width]
+                outs[r][here, to] = (acc + acc * jnp.tanh(acc)).astype(BF16)
+
+
+def activate(place, rows, edges, taps, bias, first, width, rest, shards):
+    tok = rows[0].shape[0]
+    per_group = HEADS * HEAD_DIM // GROUPS
+    inner = per_group * shards
+    parts = [(first, per_group, width)]
+    for kind in rest:
+        parts.append({"B": (inner, STATE, STATE), "C": (inner + shards * STATE, STATE, STATE), "D": (0, 0, LANES)}[kind])
+    total = sum(part[2] for part in parts)
     return local_call(
-        functools.partial(conv_kernel, parts, shards, with_rest),
-        [((tok, total), BF16)] * peers,
-        operands,
+        functools.partial(conv_kernel, parts, shards),
+        [((PAIR * tok, total), BF16)] * shards,
+        [place, *rows, *edges, taps, bias],
         scratch=[pltpu.VMEM((tok + 8, max(p[2] for p in parts)), F32)],
-        flops=peers * tok * total * 12,
-        transcendentals=peers * tok * total,
+        flops=shards * PAIR * tok * total * 12,
+        transcendentals=shards * PAIR * tok * total,
         name="conv",
     )
 
 
-def exchange(blocks, axes, pairs):
-    peers = len(blocks)
-    got = [blocks[0]]
-    for r in range(1, peers):
-        route = [(k * peers + i, k * peers + (i ^ r)) for k in range(pairs) for i in range(peers)]
-        got.append(lax.ppermute(blocks[r], axes, route))
-    return got
+def exchange(blocks, axes, length):
+    shards = len(blocks)
+    got = {0: blocks[0]}
+    for r in [*range(2, shards), 1]:
+        route = [(k * shards + i, k * shards + (i ^ r)) for k in range(length) for i in range(shards)]
+        got[r] = lax.ppermute(blocks[r], axes, route)
+    return [got[r] for r in range(shards)]
 
 
 def in_order(place, blocks, columns, out):
-    count = blocks[0].shape[0]
+    count = blocks[0].shape[0] // PAIR
     for r, block in enumerate(blocks):
-        at = pl.multiple_of((place[3] ^ r) * count, count)
-        out[pl.ds(at, count), :] = block[:, columns]
+        for core in range(PAIR):
+            at = pl.multiple_of((core * len(blocks) + (place[4] ^ r)) * count, count)
+            out[pl.ds(at, count), :] = block[core * count : (core + 1) * count, columns]
 
 
 def prep_kernel(peers, place, *refs):
     blocks, (a_ref, bias_ref, skip_ref) = refs[:peers], refs[peers : peers + 3]
-    b_ref, c_ref, cum_ref, row_ref, factor_ref, tail_ref, skip_out, score_ref, dt_ref = refs[peers + 3 :]
-    start = blocks[0].shape[1] - 2 * STATE - LANES
+    b_ref, cum_ref, row_ref, factor_ref, tail_ref, skip_out, dt_ref = refs[peers + 3 :]
+    start = blocks[0].shape[1] - STATE - LANES
     in_order(place, blocks, slice(start, start + STATE), b_ref)
-    in_order(place, blocks, slice(start + STATE, start + 2 * STATE), c_ref)
-    in_order(place, blocks, slice(start + 2 * STATE, start + 2 * STATE + LANES), dt_ref)
+    in_order(place, blocks, slice(start + STATE, start + STATE + LANES), dt_ref)
     per_tile = LANES * GROUPS // HEADS
     group = place[0]
     tile = group // per_tile
@@ -282,6 +337,14 @@
         factor_ref[at] = jnp.concatenate(halves(jnp.exp2(cum), 2), 1)
         tail = jnp.exp2(cum[BLOCK - 1 :] - cum) * here
         tail_ref[at] = jnp.concatenate(halves(tail, 2), 1)
+
+
+def score_kernel(peers, place, *refs):
+    blocks, (b_ref, c_ref, score_ref) = refs[:peers], refs[peers:]
+    start = blocks[0].shape[1] - STATE
+    in_order(place, blocks, slice(start, start + STATE), c_ref)
+    for block in range(PAIR):
+        at = slice(block * BLOCK, (block + 1) * BLOCK)
         score_ref[at] = lax.dot_general(
             c_ref[at], b_ref[at], (((1,), (1,)), ((), ())), preferred_element_type=F32
         )
@@ -302,10 +365,7 @@
     ends = [dot(factor_ref[(i + 1) * BLOCK - 16 : (i + 1) * BLOCK], wide)[15:16] for i in range(PAIR)]
     own_ref[...] = both[0]
     send_ref[0:STATE] = (ends[1] * both[0] + both[1]).astype(BF16)
-    row = lax.broadcasted_iota(jnp.int32, (16, width), 0)
-    high, middle, low = (part.astype(F32) for part in halves(ends[0] * ends[1], 3))
-    packed = jnp.where(row == 0, high, jnp.where(row == 1, middle, jnp.where(row == 2, low, 0.0)))
-    send_ref[STATE:] = packed.astype(BF16)
+    put_decay(send_ref, ends[0] * ends[1])
 
 
 def local_kernel(first_head, x_ref, cum_ref, row_ref, score_ref, skip_ref, out_ref):
@@ -341,16 +401,31 @@
             out_ref[base + half : base + BLOCK, columns] = bottom
 
 
+def decay_of(ref):
+    decay = ref[STATE : STATE + 16].astype(F32)
+    return decay[0:1] + (decay[1:2] + decay[2:3])
+
+
+def put_decay(ref, decay):
+    row = lax.broadcasted_iota(jnp.int32, (16, ref.shape[1]), 0)
+    high, middle, low = (part.astype(F32) for part in halves(decay, 3))
+    packed = jnp.where(row == 0, high, jnp.where(row == 1, middle, jnp.where(row == 2, low, 0.0)))
+    ref[STATE:] = packed.astype(BF16)
+
+
+def combine_kernel(early_ref, late_ref, out_ref):
+    decay = decay_of(late_ref)
+    out_ref[:STATE] = (decay * early_ref[:STATE].astype(F32) + late_ref[:STATE].astype(F32)).astype(BF16)
+    put_decay(out_ref, decay * decay_of(early_ref))
+
+
 def final_kernel(first_head, place, *refs):
-    earlier, (own_ref, c_ref, factor_ref, partial_ref, keep_ref, send_ref) = refs[:-6], refs[-6:]
+    last, before, alone, own_ref, c_ref, factor_ref, partial_ref, keep_ref, send_ref = refs
     width = own_ref.shape[1]
     core = place[2]
     wide = spread(first_head, width, 2)
-    held = jnp.zeros((STATE, width), F32)
-    for got in reversed(earlier):
-        decay = got[STATE : STATE + 16].astype(F32)
-        decay = decay[0:1] + (decay[1:2] + decay[2:3])
-        held = decay * held + got[:STATE].astype(F32)
+    held = last[:STATE].astype(F32) + decay_of(last) * before[:STATE].astype(F32)
+    held = held + alone[:STATE].astype(F32)
     factor = dot(factor_ref[...], wide)
     outs = []
     for block in range(PAIR):
@@ -414,52 +489,61 @@
     context, shard = lax.axis_index("ctx"), lax.axis_index("head")
     pair, core = context // PAIR, context % PAIR
     group = shard * PAIR + core
-    place = jnp.stack([group, pair, core, core * shards + shard]).astype(jnp.int32)
-
-    edge = lax.ppermute(xbc[tok - 3 :], axes, [(i, i + 1) for i in range(devices - 1)])
-    swap = [(i * shards + j, (i ^ 1) * shards + j) for i in range(length) for j in range(shards)]
+    place = jnp.stack([group, pair, core, core * shards + shard, shard]).astype(jnp.int32)
+
+    def over(block, target):
+        route = [(i, target(i)) for i in range(devices)]
+        return lax.ppermute(block, axes, [(i, j) for i, j in route if j is not None and j < devices])
+
+    own, send, taps, bias, near, far = pack(place, xbc, dt_raw, conv_weight, conv_bias[None], shards)
+    near = over(near, lambda i: i + 1)
+    far = over(far, lambda i: (i + 1) ^ shards)
+    rows = (own, over(send, lambda i: i ^ shards))
 
     received, starts = [], []
     first = 0
-    for index, width in enumerate(PIECES):
-        sent = activate(
-            place, xbc, dt_raw, edge, conv_weight, conv_bias[None], first, width, index == 0, shards
-        )
-        received.append(exchange(sent, axes, pairs))
+    for width, rest in PIECES:
+        sent = activate(place, rows, (near, far), taps, bias, first, width, rest, shards)
+        received.append(exchange(sent, axes, length))
         starts.append(first // HEAD_DIM)
         first += width
 
     tiles = [p.reshape(HEADS // LANES, LANES) for p in (a_log, dt_bias, skip_gain)]
-    b, c, cum, row, factor, tail, skip, score = local_call(
-        functools.partial(prep_kernel, peers),
+    b, cum, row, factor, tail, skip = local_call(
+        functools.partial(prep_kernel, shards),
         [
-            ((slab, STATE), BF16),
             ((slab, STATE), BF16),
             ((slab, LANES), F32),
             ((LANES, slab), F32),
             ((slab, 2 * LANES), BF16),
             ((slab, 2 * LANES), BF16),
             ((16, 3 * LANES), BF16),
-            ((slab, BLOCK), F32),
         ],
         [place] + received[0] + tiles,
         scratch=[pltpu.VMEM((slab, LANES), BF16)],
-        flops=2 * slab * BLOCK * (STATE + 3 * LANES),
+        flops=2 * slab * BLOCK * 3 * LANES,
         name="prep",
     )
+    c, score = local_call(
+        functools.partial(score_kernel, shards),
+        [((slab, STATE), BF16), ((slab, BLOCK), F32)],
+        [place] + received[1] + [b],
+        flops=2 * slab * BLOCK * STATE,
+        name="score",
+    )
     pieces = []
-    for head, width, blocks in zip(starts, PIECES, received):
+    for head, (width, _), blocks in zip(starts, PIECES, received):
         x, sent, own = local_call(
-            functools.partial(state_kernel, head, peers),
+            functools.partial(state_kernel, head, shards),
             [((slab, width), BF16), ((STATE + 16, width), BF16), ((STATE, width), F32)],
             [place] + blocks + [b, factor, tail],
             flops=4 * slab * STATE * width,
             name="state",
         )
-        earlier = [
-            lax.ppermute(sent, axes, [(i, i + d * peers) for i in range(devices - d * peers)])
-            for d in range(1, pairs)
-        ]
+        last = over(sent, lambda i: i + peers if i // peers % 2 == 0 else None)
+        (joined,) = local_call(combine_kernel, [(sent.shape, BF16)], [last, sent], name="combine")
+        before = over(joined, lambda i: i + 2 * peers if i // peers == 1 else None)
+        alone = over(joined, lambda i: i + peers if i // peers == 1 else None)
         (partial,) = local_call(
             functools.partial(local_kernel, head),
             [((slab, width), F32)],
@@ -468,7 +552,7 @@
             transcendentals=slab * BLOCK * width // HEAD_DIM,
             name="local",
         )
-        pieces.append((head, width, earlier, own, partial))
+        pieces.append((head, width, [last, before, alone], own, partial))
     keeps, gots = [], []
     for head, width, earlier, own, partial in pieces:
         keep, send = local_call(
@@ -479,7 +563,7 @@
             name="final",
         )
         keeps.append(keep)
-        gots.append(lax.ppermute(send, axes, swap))
+        gots.append(over(send, lambda i: i ^ shards))
     (out,) = local_call(
         functools.partial(assemble_kernel, len(keeps)),
         [((BLOCK, PAIR * per_group * HEAD_DIM), BF16)],
@@ -496,7 +580,7 @@
 
     def program(xbc, *rest):
         slab = xbc.shape[0] // length
-        fits = GROUPS == shards * PAIR and length % PAIR == 0 and slab == BLOCK and slab % (16 * shards) == 0
+        fits = shards == GROUPS // PAIR and length == 4 * PAIR and slab == BLOCK
         return jax.shard_map(
             paired if fits else on_device,
             mesh=mesh,

time: 139 us -> 136 us (0.978)
  the two profiles are of different devices: /device:TPU:0 before, /device:TPU:13 now
where the time goes in v3:
time: 136 us; the launch traced here: 135 us
  waiting for transfers between devices  60.8 us (45%)
  starting transfers between devices  41.3 us (30%)
  Pallas kernels  27.7 us (20%)
  local copies, waits for them, and re-layouts  4.46 us (3%)
    ppermute x12, waiting for transfers between devices, exchange(): got[r] = lax.ppermute(blocks[r], axes, route)  50.6 us
    ppermute x19, starting transfers between devices, over(): lax.ppermute(block, axes, [(i, j) for i, j in route if j is not None and...  27.1 us
    pallas_call x23, Pallas kernels, local_call(): pl.pallas_call(body, out_shape=shapes, in_specs=specs, out_specs=[vmem] *...  25.7 us
    ppermute x12, starting transfers between devices, exchange(): got[r] = lax.ppermute(blocks[r], axes, route)  14.2 us
    ppermute x19, waiting for transfers between devices, over(): lax.ppermute(block, axes, [(i, j) for i, j in route if j is not None and...  10.2 us
    unnamed x14, local copies, waits for them, and re-layouts  4.37 us
  transfers between devices with their start and end apart: 31, of which 11 were waited for; matrix products, arithmetic and copies ran while one was open for 0% of the time, Pallas kernels for 16%

profile of v3, /device:TPU:13, one launch (start us, length us, event | category | flops | bytes accessed | tf_op | source)
XLA Modules:
  0.0 134.7 jit_solution(2609600431423826419)
XLA Ops:
  0.1 1.7 %copy-done = bf16[64,20480]{1,0:T(8,128)(2,1)S(1)} copy-done((bf16[64,20480]{1,0:T(8,128)(2,1)S(1)}, bf16[64,20480]{1,0:T(8,128)(2,1)}, u32[]{:S(2)}) %copy-start) | copy-done | bytes 2621464
  4.4 2.1 %pack.1 = (bf16[64,10496]{1,0:T(8,128)(2,1)S(1)}, bf16[64,10496]{1,0:T(8,128)(2,1)S(1)}, f32[4,10240]{1,0:T(4,128)S(1)}, f32[1,10240]{1,0:T(1,128)S(1)}, bf16[3,...) custom-call(s32[5]{0:T(128)S(1)} %stack.23.place, bf16[64,20480]{1,0:T(8,128)(2,1)S(1)} %copy-done, ...), custom_call_target="tpu_custom_call" | custom-call | tf_op jit(solution)/shard_map/pack/pallas_call | solution.py:234
  7.3 3.2 %collective-permute-start.1 = (bf16[3,10240]{1,0:T(4,128)(2,1)S(1)}, bf16[3,10240]{1,0:T(4,128)(2,1)S(1)}, u32[]{:S(2)}, u32[]{:S(2)}) collective-permute-start(bf16[3,10240]{1,0:T(4,128)(2,1)S(1)} %get-tuple-element.57), channel_id=1, source_target_pairs={{0,1},{1,2},{2,3},{3,4},{4,5},{5,6},{6,7},{7,8},{8,9},{9,10},{10,1... | collective-permute-start | bytes 184328 | tf_op jit(solution)/shard_map/ppermute | solution.py:496
  10.5 3.4 %collective-permute-start.2 = (bf16[3,10240]{1,0:T(4,128)(2,1)S(1)}, bf16[3,10240]{1,0:T(4,128)(2,1)S(1)}, u32[]{:S(2)}, u32[]{:S(2)}) collective-permute-start(bf16[3,10240]{1,0:T(4,128)(2,1)S(1)} %get-tuple-element.58), channel_id=1, source_target_pairs={{0,5},{1,6},{2,7},{3,0},{4,1},{5,2},{6,3},{7,12},{8,13},{9,14},{10... | collective-permute-start | bytes 184328 | tf_op jit(solution)/shard_map/ppermute | solution.py:496
  13.9 2.8 %collective-permute-done.2.refs_3_ = bf16[3,10240]{1,0:T(4,128)(2,1)S(1)} collective-permute-done((bf16[3,10240]{1,0:T(4,128)(2,1)S(1)}, bf16[3,10240]{1,0:T(4,128)(2,1)S(1)}, u32[]{:S(2)}, u32[]{:S(2)}) %collective-permute-start.2) | collective-permute-done | bytes 61472 | tf_op jit(solution)/shard_map/ppermute | solution.py:496
  16.7 1.7 %conv.4 = (bf16[128,768]{1,0:T(8,128)(2,1)S(1)}, bf16[128,768]{1,0:T(8,128)(2,1)S(1)}, bf16[128,768]{1,0:T(8,128)(2,1)S(1)}, bf16[128,768]{1,0:T(8,128)(2,1)S(1)}) custom-call(s32[5]{0:T(128)S(1)} %stack.23.place, bf16[64,10496]{1,0:T(8,128)(2,1)S(1)} %get-tuple-element.55.refs_0_, bf16[64,10496]{1,0:T(8,128)(2,1)S(1)} %collective-permute-done.refs_1_, ...), custom_call_target="tpu_custom_call" | custom-call | flops 4718592 | bytes 1572864 | tf_op jit(solution)/shard_map/conv/pallas_call | solution.py:470
  18.5 3.5 %collective-permute-start.3 = (bf16[128,768]{1,0:T(8,128)(2,1)S(1)}, bf16[128,768]{1,0:T(8,128)(2,1)S(1)}, u32[]{:S(2)}, u32[]{:S(2)}) collective-permute-start(bf16[128,768]{1,0:T(8,128)(2,1)S(1)} %get-tuple-element.62), channel_id=1, source_target_pairs={{0,1},{1,0},{2,3},{3,2},{4,5},{5,4},{6,7},{7,6},{8,9},{9,8},{10,11... | collective-permute-start | bytes 589832 | tf_op jit(solution)/shard_map/ppermute | solution.py:296
  21.9 1.8 %conv.6 = (bf16[128,640]{1,0:T(8,128)(2,1)S(1)}, bf16[128,640]{1,0:T(8,128)(2,1)S(1)}, bf16[128,640]{1,0:T(8,128)(2,1)S(1)}, bf16[128,640]{1,0:T(8,128)(2,1)S(1)}) custom-call(s32[5]{0:T(128)S(1)} %stack.23.place, bf16[64,10496]{1,0:T(8,128)(2,1)S(1)} %get-tuple-element.55.refs_0_, bf16[64,10496]{1,0:T(8,128)(2,1)S(1)} %collective-permute-done.refs_1_, ...), custom_call_target="tpu_custom_call" | custom-call | flops 3932160 | bytes 1310720 | tf_op jit(solution)/shard_map/conv/pallas_call | solution.py:470
  24.0 2.5 %collective-permute-start.5 = (bf16[128,768]{1,0:T(8,128)(2,1)S(1)}, bf16[128,768]{1,0:T(8,128)(2,1)S(1)}, u32[]{:S(2)}, u32[]{:S(2)}) collective-permute-start(bf16[128,768]{1,0:T(8,128)(2,1)S(1)} %get-tuple-element.64), channel_id=1, source_target_pairs={{0,3},{1,2},{2,1},{3,0},{4,7},{5,6},{6,5},{7,4},{8,11},{9,10},{10,... | collective-permute-start | bytes 589832 | tf_op jit(solution)/shard_map/ppermute | solution.py:296
  26.5 2.3 %conv.5 = (bf16[128,896]{1,0:T(8,128)(2,1)S(1)}, bf16[128,896]{1,0:T(8,128)(2,1)S(1)}, bf16[128,896]{1,0:T(8,128)(2,1)S(1)}, bf16[128,896]{1,0:T(8,128)(2,1)S(1)}) custom-call(s32[5]{0:T(128)S(1)} %stack.23.place, bf16[64,10496]{1,0:T(8,128)(2,1)S(1)} %get-tuple-element.55.refs_0_, bf16[64,10496]{1,0:T(8,128)(2,1)S(1)} %collective-permute-done.refs_1_, ...), custom_call_target="tpu_custom_call" | custom-call | flops 5505024 | bytes 1835008 | tf_op jit(solution)/shard_map/conv/pallas_call | solution.py:470
  29.8 2.6 %collective-permute-done.15.refs_1_ = bf16[128,640]{1,0:T(8,128)(2,1)S(1)} collective-permute-done((bf16[128,640]{1,0:T(8,128)(2,1)S(1)}, bf16[128,640]{1,0:T(8,128)(2,1)S(1)}, u32[]{:S(2)}, u32[]{:S(2)}) %collective-permute-start.15) | collective-permute-done | bytes 163872 | tf_op jit(solution)/shard_map/ppermute | solution.py:296
  32.4 1.8 %collective-permute-start.10 = (bf16[128,896]{1,0:T(8,128)(2,1)S(1)}, bf16[128,896]{1,0:T(8,128)(2,1)S(1)}, u32[]{:S(2)}, u32[]{:S(2)}) collective-permute-start(bf16[128,896]{1,0:T(8,128)(2,1)S(1)} %get-tuple-element.72), channel_id=1, source_target_pairs={{0,2},{1,3},{2,0},{3,1},{4,6},{5,7},{6,4},{7,5},{8,10},{9,11},{10,... | collective-permute-start | bytes 688136 | tf_op jit(solution)/shard_map/ppermute | solution.py:296
  34.2 1.6 %collective-permute-start.11 = (bf16[128,896]{1,0:T(8,128)(2,1)S(1)}, bf16[128,896]{1,0:T(8,128)(2,1)S(1)}, u32[]{:S(2)}, u32[]{:S(2)}) collective-permute-start(bf16[128,896]{1,0:T(8,128)(2,1)S(1)} %get-tuple-element.73), channel_id=1, source_target_pairs={{0,3},{1,2},{2,1},{3,0},{4,7},{5,6},{6,5},{7,4},{8,11},{9,10},{10,... | collective-permute-start | bytes 688136 | tf_op jit(solution)/shard_map/ppermute | solution.py:296
  36.7 24.2 %collective-permute-done.5.refs_3_ = bf16[128,768]{1,0:T(8,128)(2,1)S(1)} collective-permute-done((bf16[128,768]{1,0:T(8,128)(2,1)S(1)}, bf16[128,768]{1,0:T(8,128)(2,1)S(1)}, u32[]{:S(2)}, u32[]{:S(2)}) %collective-permute-start.5) | collective-permute-done | bytes 196640 | tf_op jit(solution)/shard_map/ppermute | solution.py:296
  62.1 9.2 %collective-permute-done.16.refs_2_ = bf16[128,640]{1,0:T(8,128)(2,1)S(1)} collective-permute-done((bf16[128,640]{1,0:T(8,128)(2,1)S(1)}, bf16[128,640]{1,0:T(8,128)(2,1)S(1)}, u32[]{:S(2)}, u32[]{:S(2)}) %collective-permute-start.16) | collective-permute-done | bytes 163872 | tf_op jit(solution)/shard_map/ppermute | solution.py:296
  71.3 6.4 %collective-permute-done.17.refs_3_ = bf16[128,640]{1,0:T(8,128)(2,1)S(1)} collective-permute-done((bf16[128,640]{1,0:T(8,128)(2,1)S(1)}, bf16[128,640]{1,0:T(8,128)(2,1)S(1)}, u32[]{:S(2)}, u32[]{:S(2)}) %collective-permute-start.17) | collective-permute-done | bytes 163872 | tf_op jit(solution)/shard_map/ppermute | solution.py:296
  77.7 1.4 %state.6 = (bf16[512,640]{1,0:T(8,128)(2,1)S(1)}, bf16[272,640]{1,0:T(8,128)(2,1)S(1)}, f32[256,640]{1,0:T(8,128)S(1)}) custom-call(s32[5]{0:T(128)S(1)} %stack.23.place, bf16[128,640]{1,0:T(8,128)(2,1)S(1)} %get-tuple-element.85.refs_0_, bf16[128,640]{1,0:T(8,128)(2,1)S(1)} %collective-permute-done.15.refs_1_, ...), custom_call_target="tpu_custom_call" | custom-call | flops 335544320 | bytes 3317760 | tf_op jit(solution)/shard_map/state/pallas_call | solution.py:470
  79.1 2.0 %collective-permute-start.18 = (bf16[272,640]{1,0:T(8,128)(2,1)S(1)}, bf16[272,640]{1,0:T(8,128)(2,1)S(1)}, u32[]{:S(2)}, u32[]{:S(2)}) collective-permute-start(bf16[272,640]{1,0:T(8,128)(2,1)S(1)} %get-tuple-element.89.late_ref), channel_id=1, source_target_pairs={{0,8},{1,9},{2,10},{3,11},{4,12},{5,13},{6,14},{7,15},{16,24},{17,... | collective-permute-start | bytes 1044488 | tf_op jit(solution)/shard_map/ppermute | solution.py:496
  81.2 1.4 %state.5 = (bf16[512,640]{1,0:T(8,128)(2,1)S(1)}, bf16[272,640]{1,0:T(8,128)(2,1)S(1)}, f32[256,640]{1,0:T(8,128)S(1)}) custom-call(s32[5]{0:T(128)S(1)} %stack.23.place, bf16[128,896]{1,0:T(8,128)(2,1)S(1)} %get-tuple-element.70.refs_0_, bf16[128,896]{1,0:T(8,128)(2,1)S(1)} %collective-permute-done.9.refs_1_, ...), custom_call_target="tpu_custom_call" | custom-call | flops 335544320 | bytes 3317760 | tf_op jit(solution)/shard_map/state/pallas_call | solution.py:470
  82.6 1.3 collective-permute-start.12
  85.7 2.2 %collective-permute-start.23 = (bf16[128,384]{1,0:T(8,128)(2,1)S(1)}, bf16[128,384]{1,0:T(8,128)(2,1)S(1)}, u32[]{:S(2)}, u32[]{:S(2)}) collective-permute-start(bf16[128,384]{1,0:T(8,128)(2,1)S(1)} %get-tuple-element.96), channel_id=1, source_target_pairs={{0,3},{1,2},{2,1},{3,0},{4,7},{5,6},{6,5},{7,4},{8,11},{9,10},{10,... | collective-permute-start | bytes 294920 | tf_op jit(solution)/shard_map/ppermute | solution.py:296
  88.7 2.0 %collective-permute-done.22.refs_2_ = bf16[128,384]{1,0:T(8,128)(2,1)S(1)} collective-permute-done((bf16[128,384]{1,0:T(8,128)(2,1)S(1)}, bf16[128,384]{1,0:T(8,128)(2,1)S(1)}, u32[]{:S(2)}, u32[]{:S(2)}) %collective-permute-start.22) | collective-permute-done | bytes 98336 | tf_op jit(solution)/shard_map/ppermute | solution.py:296
  90.7 5.3 %collective-permute-done.23.refs_3_ = bf16[128,384]{1,0:T(8,128)(2,1)S(1)} collective-permute-done((bf16[128,384]{1,0:T(8,128)(2,1)S(1)}, bf16[128,384]{1,0:T(8,128)(2,1)S(1)}, u32[]{:S(2)}, u32[]{:S(2)}) %collective-permute-start.23) | collective-permute-done | bytes 98336 | tf_op jit(solution)/shard_map/ppermute | solution.py:296
  96.0 1.3 state.7
  97.3 1.8 %collective-permute-start.24 = (bf16[272,384]{1,0:T(8,128)(2,1)S(1)}, bf16[272,384]{1,0:T(8,128)(2,1)S(1)}, u32[]{:S(2)}, u32[]{:S(2)}) collective-permute-start(bf16[272,384]{1,0:T(8,128)(2,1)S(1)} %get-tuple-element.97.late_ref), channel_id=1, source_target_pairs={{0,8},{1,9},{2,10},{3,11},{4,12},{5,13},{6,14},{7,15},{16,24},{17,... | collective-permute-start | bytes 626696 | tf_op jit(solution)/shard_map/ppermute | solution.py:496
  102.8 1.3 state.4
  106.2 2.4 %collective-permute-done.6.early_ref.refs_0_ = bf16[272,384]{1,0:T(8,128)(2,1)S(1)} collective-permute-done((bf16[272,384]{1,0:T(8,128)(2,1)S(1)}, bf16[272,384]{1,0:T(8,128)(2,1)S(1)}, u32[]{:S(2)}, u32[]{:S(2)}) %collective-permute-start.6) | collective-permute-done | bytes 208928 | tf_op jit(solution)/shard_map/ppermute | solution.py:496
  108.6 1.5 %collective-permute-start.26 = (bf16[272,384]{1,0:T(8,128)(2,1)S(1)}, bf16[272,384]{1,0:T(8,128)(2,1)S(1)}, u32[]{:S(2)}, u32[]{:S(2)}) collective-permute-start(bf16[272,384]{1,0:T(8,128)(2,1)S(1)} %combine.7), channel_id=1, source_target_pairs={{8,16},{9,17},{10,18},{11,19},{12,20},{13,21},{14,22},{15,23}} | collective-permute-start | bytes 626696 | tf_op jit(solution)/shard_map/ppermute | solution.py:496
  114.2 3.5 %collective-permute-done.14.refs_2_ = bf16[272,640]{1,0:T(8,128)(2,1)S(1)} collective-permute-done((bf16[272,640]{1,0:T(8,128)(2,1)S(1)}, bf16[272,640]{1,0:T(8,128)(2,1)S(1)}, u32[]{:S(2)}, u32[]{:S(2)}) %collective-permute-start.14) | collective-permute-done | bytes 348192 | tf_op jit(solution)/shard_map/ppermute | solution.py:496
  120.9 4.5 %collective-permute-start.29 = (bf16[256,640]{1,0:T(8,128)(2,1)S(1)}, bf16[256,640]{1,0:T(8,128)(2,1)S(1)}, u32[]{:S(2)}, u32[]{:S(2)}) collective-permute-start(bf16[256,640]{1,0:T(8,128)(2,1)S(1)} %get-tuple-element.103), channel_id=1, source_target_pairs={{0,4},{1,5},{2,6},{3,7},{4,0},{5,1},{6,2},{7,3},{8,12},{9,13},{10,... | collective-permute-start | bytes 983048 | tf_op jit(solution)/shard_map/ppermute | solution.py:496
  131.2 1.4 %collective-permute-done.27.refs_4_ = bf16[256,384]{1,0:T(8,128)(2,1)S(1)} collective-permute-done((bf16[256,384]{1,0:T(8,128)(2,1)S(1)}, bf16[256,384]{1,0:T(8,128)(2,1)S(1)}, u32[]{:S(2)}, u32[]{:S(2)}) %collective-permute-start.27) | collective-permute-done | bytes 196640 | tf_op jit(solution)/shard_map/ppermute | solution.py:496
  132.7 2.0 %assemble.1 = bf16[256,4096]{1,0:T(8,128)(2,1)} custom-call(s32[5]{0:T(128)S(1)} %stack.23.place, bf16[256,384]{1,0:T(8,128)(2,1)S(1)} %get-tuple-element.80.refs_0_, bf16[256,640]{1,0:T(8,128)(2,1)S(1)} %get-tuple-element.84.refs_1_, bf16[256,640]{1,0:T(8,128)(2,1)S(1)} %get-tuple-element.92.refs_2_, bf16[256,384]{1,0:T(8,128)(2,1)S(1)} %get-tuple-element.100.refs_3_, ...), custom_call_target="tpu_custom_call" | custom-call | bytes 4194304 | tf_op jit(solution)/shard_map/assemble/pallas_call | solution.py:470
  (69 shorter events, 28.0 us)
Async XLA Ops:
  6.5 10.2 %collective-permute-start = (bf16[64,10496]{1,0:T(8,128)(2,1)S(1)}, bf16[64,10496]{1,0:T(8,128)(2,1)S(1)}, u32[]{:S(2)}, u32[]{:S(2)}) collective-permute-start(bf16[64,10496]{1,0:T(8,128)(2,1)S(1)} %get-tuple-element.56), channel_id=1, source_target_pairs={{0,4},{1,5},{2,6},{3,7},{4,0},{5,1},{6,2},{7,3},{8,12},{9,13},{10,... | collective-permute-start | bytes 4030472 | tf_op jit(solution)/shard_map/ppermute | solution.py:496
  7.3 6.6 %collective-permute-start.1 = (bf16[3,10240]{1,0:T(4,128)(2,1)S(1)}, bf16[3,10240]{1,0:T(4,128)(2,1)S(1)}, u32[]{:S(2)}, u32[]{:S(2)}) collective-permute-start(bf16[3,10240]{1,0:T(4,128)(2,1)S(1)} %get-tuple-element.57), channel_id=1, source_target_pairs={{0,1},{1,2},{2,3},{3,4},{4,5},{5,6},{6,7},{7,8},{8,9},{9,10},{10,1... | collective-permute-start | bytes 184328 | tf_op jit(solution)/shard_map/ppermute | solution.py:496
  10.5 6.3 %collective-permute-start.2 = (bf16[3,10240]{1,0:T(4,128)(2,1)S(1)}, bf16[3,10240]{1,0:T(4,128)(2,1)S(1)}, u32[]{:S(2)}, u32[]{:S(2)}) collective-permute-start(bf16[3,10240]{1,0:T(4,128)(2,1)S(1)} %get-tuple-element.58), channel_id=1, source_target_pairs={{0,5},{1,6},{2,7},{3,0},{4,1},{5,2},{6,3},{7,12},{8,13},{9,14},{10... | collective-permute-start | bytes 184328 | tf_op jit(solution)/shard_map/ppermute | solution.py:496
  18.5 15.7 %collective-permute-start.3 = (bf16[128,768]{1,0:T(8,128)(2,1)S(1)}, bf16[128,768]{1,0:T(8,128)(2,1)S(1)}, u32[]{:S(2)}, u32[]{:S(2)}) collective-permute-start(bf16[128,768]{1,0:T(8,128)(2,1)S(1)} %get-tuple-element.62), channel_id=1, source_target_pairs={{0,1},{1,0},{2,3},{3,2},{4,5},{5,4},{6,7},{7,6},{8,9},{9,8},{10,11... | collective-permute-start | bytes 589832 | tf_op jit(solution)/shard_map/ppermute | solution.py:296
  23.8 8.6 %collective-permute-start.15 = (bf16[128,640]{1,0:T(8,128)(2,1)S(1)}, bf16[128,640]{1,0:T(8,128)(2,1)S(1)}, u32[]{:S(2)}, u32[]{:S(2)}) collective-permute-start(bf16[128,640]{1,0:T(8,128)(2,1)S(1)} %get-tuple-element.86), channel_id=1, source_target_pairs={{0,1},{1,0},{2,3},{3,2},{4,5},{5,4},{6,7},{7,6},{8,9},{9,8},{10,11... | collective-permute-start | bytes 491528 | tf_op jit(solution)/shard_map/ppermute | solution.py:296
  23.8 11.9 %collective-permute-start.4 = (bf16[128,768]{1,0:T(8,128)(2,1)S(1)}, bf16[128,768]{1,0:T(8,128)(2,1)S(1)}, u32[]{:S(2)}, u32[]{:S(2)}) collective-permute-start(bf16[128,768]{1,0:T(8,128)(2,1)S(1)} %get-tuple-element.63), channel_id=1, source_target_pairs={{0,2},{1,3},{2,0},{3,1},{4,6},{5,7},{6,4},{7,5},{8,10},{9,11},{10,... | collective-permute-start | bytes 589832 | tf_op jit(solution)/shard_map/ppermute | solution.py:296
  23.9 37.0 %copy-start.4 = (f32[256]{0:T(256)S(1)}, f32[256]{0:T(256)}, u32[]{:S(2)}) copy-start(f32[256]{0:T(256)} %param.11) | copy-start | bytes 3076
  24.0 36.9 %collective-permute-start.5 = (bf16[128,768]{1,0:T(8,128)(2,1)S(1)}, bf16[128,768]{1,0:T(8,128)(2,1)S(1)}, u32[]{:S(2)}, u32[]{:S(2)}) collective-permute-start(bf16[128,768]{1,0:T(8,128)(2,1)S(1)} %get-tuple-element.64), channel_id=1, source_target_pairs={{0,3},{1,2},{2,1},{3,0},{4,7},{5,6},{6,5},{7,4},{8,11},{9,10},{10,... | collective-permute-start | bytes 589832 | tf_op jit(solution)/shard_map/ppermute | solution.py:296
  28.7 52.4 %collective-permute-start.9 = (bf16[128,896]{1,0:T(8,128)(2,1)S(1)}, bf16[128,896]{1,0:T(8,128)(2,1)S(1)}, u32[]{:S(2)}, u32[]{:S(2)}) collective-permute-start(bf16[128,896]{1,0:T(8,128)(2,1)S(1)} %get-tuple-element.71), channel_id=1, source_target_pairs={{0,1},{1,0},{2,3},{3,2},{4,5},{5,4},{6,7},{7,6},{8,9},{9,8},{10,11... | collective-permute-start | bytes 688136 | tf_op jit(solution)/shard_map/ppermute | solution.py:296
  32.4 48.8 %collective-permute-start.10 = (bf16[128,896]{1,0:T(8,128)(2,1)S(1)}, bf16[128,896]{1,0:T(8,128)(2,1)S(1)}, u32[]{:S(2)}, u32[]{:S(2)}) collective-permute-start(bf16[128,896]{1,0:T(8,128)(2,1)S(1)} %get-tuple-element.72), channel_id=1, source_target_pairs={{0,2},{1,3},{2,0},{3,1},{4,6},{5,7},{6,4},{7,5},{8,10},{9,11},{10,... | collective-permute-start | bytes 688136 | tf_op jit(solution)/shard_map/ppermute | solution.py:296
  34.2 47.0 %collective-permute-start.11 = (bf16[128,896]{1,0:T(8,128)(2,1)S(1)}, bf16[128,896]{1,0:T(8,128)(2,1)S(1)}, u32[]{:S(2)}, u32[]{:S(2)}) collective-permute-start(bf16[128,896]{1,0:T(8,128)(2,1)S(1)} %get-tuple-element.73), channel_id=1, source_target_pairs={{0,3},{1,2},{2,1},{3,0},{4,7},{5,6},{6,5},{7,4},{8,11},{9,10},{10,... | collective-permute-start | bytes 688136 | tf_op jit(solution)/shard_map/ppermute | solution.py:296
  35.8 35.6 %collective-permute-start.16 = (bf16[128,640]{1,0:T(8,128)(2,1)S(1)}, bf16[128,640]{1,0:T(8,128)(2,1)S(1)}, u32[]{:S(2)}, u32[]{:S(2)}) collective-permute-start(bf16[128,640]{1,0:T(8,128)(2,1)S(1)} %get-tuple-element.87), channel_id=1, source_target_pairs={{0,2},{1,3},{2,0},{3,1},{4,6},{5,7},{6,4},{7,5},{8,10},{9,11},{10,... | collective-permute-start | bytes 491528 | tf_op jit(solution)/shard_map/ppermute | solution.py:296
  60.9 16.9 %collective-permute-start.17 = (bf16[128,640]{1,0:T(8,128)(2,1)S(1)}, bf16[128,640]{1,0:T(8,128)(2,1)S(1)}, u32[]{:S(2)}, u32[]{:S(2)}) collective-permute-start(bf16[128,640]{1,0:T(8,128)(2,1)S(1)} %get-tuple-element.88), channel_id=1, source_target_pairs={{0,3},{1,2},{2,1},{3,0},{4,7},{5,6},{6,5},{7,4},{8,11},{9,10},{10,... | collective-permute-start | bytes 491528 | tf_op jit(solution)/shard_map/ppermute | solution.py:296
  79.1 20.0 %collective-permute-start.18 = (bf16[272,640]{1,0:T(8,128)(2,1)S(1)}, bf16[272,640]{1,0:T(8,128)(2,1)S(1)}, u32[]{:S(2)}, u32[]{:S(2)}) collective-permute-start(bf16[272,640]{1,0:T(8,128)(2,1)S(1)} %get-tuple-element.89.late_ref), channel_id=1, source_target_pairs={{0,8},{1,9},{2,10},{3,11},{4,12},{5,13},{6,14},{7,15},{16,24},{17,... | collective-permute-start | bytes 1044488 | tf_op jit(solution)/shard_map/ppermute | solution.py:496
  82.6 18.7 %collective-permute-start.12 = (bf16[272,640]{1,0:T(8,128)(2,1)S(1)}, bf16[272,640]{1,0:T(8,128)(2,1)S(1)}, u32[]{:S(2)}, u32[]{:S(2)}) collective-permute-start(bf16[272,640]{1,0:T(8,128)(2,1)S(1)} %get-tuple-element.81.late_ref), channel_id=1, source_target_pairs={{0,8},{1,9},{2,10},{3,11},{4,12},{5,13},{6,14},{7,15},{16,24},{17,... | collective-permute-start | bytes 1044488 | tf_op jit(solution)/shard_map/ppermute | solution.py:496
  85.2 3.5 %collective-permute-start.21 = (bf16[128,384]{1,0:T(8,128)(2,1)S(1)}, bf16[128,384]{1,0:T(8,128)(2,1)S(1)}, u32[]{:S(2)}, u32[]{:S(2)}) collective-permute-start(bf16[128,384]{1,0:T(8,128)(2,1)S(1)} %get-tuple-element.94), channel_id=1, source_target_pairs={{0,1},{1,0},{2,3},{3,2},{4,5},{5,4},{6,7},{7,6},{8,9},{9,8},{10,11... | collective-permute-start | bytes 294920 | tf_op jit(solution)/shard_map/ppermute | solution.py:296
  85.3 5.5 %collective-permute-start.22 = (bf16[128,384]{1,0:T(8,128)(2,1)S(1)}, bf16[128,384]{1,0:T(8,128)(2,1)S(1)}, u32[]{:S(2)}, u32[]{:S(2)}) collective-permute-start(bf16[128,384]{1,0:T(8,128)(2,1)S(1)} %get-tuple-element.95), channel_id=1, source_target_pairs={{0,2},{1,3},{2,0},{3,1},{4,6},{5,7},{6,4},{7,5},{8,10},{9,11},{10,... | collective-permute-start | bytes 294920 | tf_op jit(solution)/shard_map/ppermute | solution.py:296
  85.7 10.3 %collective-permute-start.23 = (bf16[128,384]{1,0:T(8,128)(2,1)S(1)}, bf16[128,384]{1,0:T(8,128)(2,1)S(1)}, u32[]{:S(2)}, u32[]{:S(2)}) collective-permute-start(bf16[128,384]{1,0:T(8,128)(2,1)S(1)} %get-tuple-element.96), channel_id=1, source_target_pairs={{0,3},{1,2},{2,1},{3,0},{4,7},{5,6},{6,5},{7,4},{8,11},{9,10},{10,... | collective-permute-start | bytes 294920 | tf_op jit(solution)/shard_map/ppermute | solution.py:296
  97.3 8.0 %collective-permute-start.24 = (bf16[272,384]{1,0:T(8,128)(2,1)S(1)}, bf16[272,384]{1,0:T(8,128)(2,1)S(1)}, u32[]{:S(2)}, u32[]{:S(2)}) collective-permute-start(bf16[272,384]{1,0:T(8,128)(2,1)S(1)} %get-tuple-element.97.late_ref), channel_id=1, source_target_pairs={{0,8},{1,9},{2,10},{3,11},{4,12},{5,13},{6,14},{7,15},{16,24},{17,... | collective-permute-start | bytes 626696 | tf_op jit(solution)/shard_map/ppermute | solution.py:496
  99.3 12.9 %collective-permute-start.20 = (bf16[272,640]{1,0:T(8,128)(2,1)S(1)}, bf16[272,640]{1,0:T(8,128)(2,1)S(1)}, u32[]{:S(2)}, u32[]{:S(2)}) collective-permute-start(bf16[272,640]{1,0:T(8,128)(2,1)S(1)} %combine.6), channel_id=1, source_target_pairs={{8,16},{9,17},{10,18},{11,19},{12,20},{13,21},{14,22},{15,23}} | collective-permute-start | bytes 1044488 | tf_op jit(solution)/shard_map/ppermute | solution.py:496
  100.6 12.9 %collective-permute-start.19 = (bf16[272,640]{1,0:T(8,128)(2,1)S(1)}, bf16[272,640]{1,0:T(8,128)(2,1)S(1)}, u32[]{:S(2)}, u32[]{:S(2)}) collective-permute-start(bf16[272,640]{1,0:T(8,128)(2,1)S(1)} %combine.6), channel_id=1, source_target_pairs={{8,24},{9,25},{10,26},{11,27},{12,28},{13,29},{14,30},{15,31}} | collective-permute-start | bytes 1044488 | tf_op jit(solution)/shard_map/ppermute | solution.py:496
  101.5 16.2 %collective-permute-start.14 = (bf16[272,640]{1,0:T(8,128)(2,1)S(1)}, bf16[272,640]{1,0:T(8,128)(2,1)S(1)}, u32[]{:S(2)}, u32[]{:S(2)}) collective-permute-start(bf16[272,640]{1,0:T(8,128)(2,1)S(1)} %combine.5), channel_id=1, source_target_pairs={{8,16},{9,17},{10,18},{11,19},{12,20},{13,21},{14,22},{15,23}} | collective-permute-start | bytes 1044488 | tf_op jit(solution)/shard_map/ppermute | solution.py:496
  104.1 4.5 %collective-permute-start.6 = (bf16[272,384]{1,0:T(8,128)(2,1)S(1)}, bf16[272,384]{1,0:T(8,128)(2,1)S(1)}, u32[]{:S(2)}, u32[]{:S(2)}) collective-permute-start(bf16[272,384]{1,0:T(8,128)(2,1)S(1)} %get-tuple-element.68.late_ref), channel_id=1, source_target_pairs={{0,8},{1,9},{2,10},{3,11},{4,12},{5,13},{6,14},{7,15},{16,24},{17,... | collective-permute-start | bytes 626696 | tf_op jit(solution)/shard_map/ppermute | solution.py:496
  105.4 15.5 %collective-permute-start.13 = (bf16[272,640]{1,0:T(8,128)(2,1)S(1)}, bf16[272,640]{1,0:T(8,128)(2,1)S(1)}, u32[]{:S(2)}, u32[]{:S(2)}) collective-permute-start(bf16[272,640]{1,0:T(8,128)(2,1)S(1)} %combine.5), channel_id=1, source_target_pairs={{8,24},{9,25},{10,26},{11,27},{12,28},{13,29},{14,30},{15,31}} | collective-permute-start | bytes 1044488 | tf_op jit(solution)/shard_map/ppermute | solution.py:496
  108.6 18.2 %collective-permute-start.26 = (bf16[272,384]{1,0:T(8,128)(2,1)S(1)}, bf16[272,384]{1,0:T(8,128)(2,1)S(1)}, u32[]{:S(2)}, u32[]{:S(2)}) collective-permute-start(bf16[272,384]{1,0:T(8,128)(2,1)S(1)} %combine.7), channel_id=1, source_target_pairs={{8,16},{9,17},{10,18},{11,19},{12,20},{13,21},{14,22},{15,23}} | collective-permute-start | bytes 626696 | tf_op jit(solution)/shard_map/ppermute | solution.py:496
  112.2 17.8 %collective-permute-start.8 = (bf16[272,384]{1,0:T(8,128)(2,1)S(1)}, bf16[272,384]{1,0:T(8,128)(2,1)S(1)}, u32[]{:S(2)}, u32[]{:S(2)}) collective-permute-start(bf16[272,384]{1,0:T(8,128)(2,1)S(1)} %combine.4), channel_id=1, source_target_pairs={{8,16},{9,17},{10,18},{11,19},{12,20},{13,21},{14,22},{15,23}} | collective-permute-start | bytes 626696 | tf_op jit(solution)/shard_map/ppermute | solution.py:496
  113.5 16.5 %collective-permute-start.7 = (bf16[272,384]{1,0:T(8,128)(2,1)S(1)}, bf16[272,384]{1,0:T(8,128)(2,1)S(1)}, u32[]{:S(2)}, u32[]{:S(2)}) collective-permute-start(bf16[272,384]{1,0:T(8,128)(2,1)S(1)} %combine.4), channel_id=1, source_target_pairs={{8,24},{9,25},{10,26},{11,27},{12,28},{13,29},{14,30},{15,31}} | collective-permute-start | bytes 626696 | tf_op jit(solution)/shard_map/ppermute | solution.py:496
  117.7 10.7 %collective-permute-start.25 = (bf16[272,384]{1,0:T(8,128)(2,1)S(1)}, bf16[272,384]{1,0:T(8,128)(2,1)S(1)}, u32[]{:S(2)}, u32[]{:S(2)}) collective-permute-start(bf16[272,384]{1,0:T(8,128)(2,1)S(1)} %combine.7), channel_id=1, source_target_pairs={{8,24},{9,25},{10,26},{11,27},{12,28},{13,29},{14,30},{15,31}} | collective-permute-start | bytes 626696 | tf_op jit(solution)/shard_map/ppermute | solution.py:496
  120.9 11.7 %collective-permute-start.29 = (bf16[256,640]{1,0:T(8,128)(2,1)S(1)}, bf16[256,640]{1,0:T(8,128)(2,1)S(1)}, u32[]{:S(2)}, u32[]{:S(2)}) collective-permute-start(bf16[256,640]{1,0:T(8,128)(2,1)S(1)} %get-tuple-element.103), channel_id=1, source_target_pairs={{0,4},{1,5},{2,6},{3,7},{4,0},{5,1},{6,2},{7,3},{8,12},{9,13},{10,... | collective-permute-start | bytes 983048 | tf_op jit(solution)/shard_map/ppermute | solution.py:496
  126.8 5.9 %collective-permute-start.28 = (bf16[256,640]{1,0:T(8,128)(2,1)S(1)}, bf16[256,640]{1,0:T(8,128)(2,1)S(1)}, u32[]{:S(2)}, u32[]{:S(2)}) collective-permute-start(bf16[256,640]{1,0:T(8,128)(2,1)S(1)} %get-tuple-element.102), channel_id=1, source_target_pairs={{0,4},{1,5},{2,6},{3,7},{4,0},{5,1},{6,2},{7,3},{8,12},{9,13},{10,... | collective-permute-start | bytes 983048 | tf_op jit(solution)/shard_map/ppermute | solution.py:496
  129.5 1.8 %collective-permute-start.30 = (bf16[256,384]{1,0:T(8,128)(2,1)S(1)}, bf16[256,384]{1,0:T(8,128)(2,1)S(1)}, u32[]{:S(2)}, u32[]{:S(2)}) collective-permute-start(bf16[256,384]{1,0:T(8,128)(2,1)S(1)} %get-tuple-element.104), channel_id=1, source_target_pairs={{0,4},{1,5},{2,6},{3,7},{4,0},{5,1},{6,2},{7,3},{8,12},{9,13},{10,... | collective-permute-start | bytes 589832 | tf_op jit(solution)/shard_map/ppermute | solution.py:496
  131.1 1.5 %collective-permute-start.27 = (bf16[256,384]{1,0:T(8,128)(2,1)S(1)}, bf16[256,384]{1,0:T(8,128)(2,1)S(1)}, u32[]{:S(2)}, u32[]{:S(2)}) collective-permute-start(bf16[256,384]{1,0:T(8,128)(2,1)S(1)} %get-tuple-element.101), channel_id=1, source_target_pairs={{0,4},{1,5},{2,6},{3,7},{4,0},{5,1},{6,2},{7,3},{8,12},{9,13},{10,... | collective-permute-start | bytes 589832 | tf_op jit(solution)/shard_map/ppermute | solution.py:496
  (6 other events, 78.3 us)

commit v4 on v3

--- a/solution.py
+++ b/solution.py
@@ -161,9 +161,11 @@
 
 PAIR = 2
 LANES = 128
-PIECES = ((384, "BD"), (640, "C"), (640, ""), (384, ""))
 LOG2E = 1.4426950408889634
 F32, BF16 = jnp.float32, jnp.bfloat16
+WIDTHS = (512, 512, 640, 384)
+RESTS = ("", "BD", "C", "")
+JOINED = ((0, 1), (2,), (3,))
 
 
 def halves(value, count):
@@ -185,107 +187,125 @@
     return jnp.dot(a, b, preferred_element_type=F32)
 
 
-def pack_kernel(shards, place, xbc, dt_raw, weight, bias, own, send, taps, offset, near, far, tail, sems):
-    core, shard = place[2], place[4]
-    inner = HEADS * HEAD_DIM
-    count = xbc.shape[0]
-    per_group = inner // GROUPS
-    rest = per_group * shards
-
-    def columns(z, side):
-        for r in range(shards):
-            group = (z ^ r) * PAIR + side
-            yield r * per_group, group * per_group, per_group
-            yield rest + r * STATE, inner + group * STATE, STATE
-            yield rest + (shards + r) * STATE, inner + (GROUPS + group) * STATE, STATE
-
-    def ds(start, width):
-        return pl.ds(pl.multiple_of(start, LANES), width)
-
-    copies = [(xbc.at[count - 16 :], tail)]
-    for side, out in ((1 - core, send), (core, own)):
-        for to, start, width in columns(shard, side):
-            copies.append((xbc.at[:, ds(start, width)], out.at[:, to : to + width]))
-        copies.append((dt_raw, out.at[:, out.shape[1] - HEADS :]))
-    for to, start, width in columns(shard, core):
-        copies.append((weight.at[:, ds(start, width)], taps.at[:, to : to + width]))
-        copies.append((bias.at[:, ds(start, width)], offset.at[:, to : to + width]))
+def ds(start, width):
+    return pl.ds(pl.multiple_of(start, LANES), width)
+
+
+def run(copies, sems):
     started = []
     for i, (source, target) in enumerate(copies):
         copy = pltpu.make_async_copy(source, target, sems.at[i])
         copy.start()
         started.append(copy)
+    return started
+
+
+PER_GROUP = HEADS * HEAD_DIM // GROUPS
+INNER = HEADS * HEAD_DIM
+
+
+def channels(group, first, width):
+    return ds(group * PER_GROUP + first, width)
+
+
+def pack_first_kernel(shards, place, xbc, send, sems):
+    core, shard = place[2], place[4]
+    width = send.shape[1] // shards
+    copies = []
+    for r in range(shards):
+        group = (shard ^ r) * PAIR + 1 - core
+        copies.append((xbc.at[:, channels(group, 0, width)], send.at[:, r * width : (r + 1) * width]))
+    for copy in run(copies, sems):
+        copy.wait()
+
+
+def pack_kernel(shards, place, xbc, dt_raw, weight, bias, order, send, taps, offset, near, far, tail, sems):
+    core, shard = place[2], place[4]
+    count = xbc.shape[0]
+    first = WIDTHS[0]
+    width = PER_GROUP - first
+    rest = width * shards
+    copies = [(xbc.at[count - 16 :], tail)]
+    for r in range(shards):
+        group = (shard ^ r) * PAIR + 1 - core
+        copies.append((xbc.at[:, channels(group, first, width)], send.at[:, r * width : (r + 1) * width]))
+        for i in range(2):
+            to = rest + (i * shards + r) * STATE
+            copies.append((xbc.at[:, ds(INNER + (i * GROUPS + group) * STATE, STATE)], send.at[:, to : to + STATE]))
+    copies.append((dt_raw, send.at[:, send.shape[1] - HEADS :]))
+    for source, target in ((weight, taps), (bias, offset)):
+        copies.append((source.at[:, channels(place[0], 0, PER_GROUP)], target.at[:, :PER_GROUP]))
+        for i in range(2):
+            to = PER_GROUP + i * STATE
+            at = ds(INNER + (i * GROUPS + place[0]) * STATE, STATE)
+            copies.append((source.at[:, at], target.at[:, to : to + STATE]))
+    started = run(copies, sems)
     started[0].wait()
-    next_shard = jnp.where(shard == shards - 1, 0, shard + 1)
-    side = jnp.where(shard == shards - 1, 1 - core, core)
-    for edge, towards in ((near, side), (far, 1 - side)):
-        for to, start, width in columns(next_shard, towards):
-            rows = tail[:, ds(start, width)].astype(F32)
-            edge[:, to : to + width] = rows[13:16].astype(BF16)
+    for edge, side in ((near, 1), (far, 0)):
+        for r in range(shards):
+            group = ((shards - 1) ^ r) * PAIR + side
+            to = r * (PER_GROUP + 2 * STATE)
+            parts = [(group * PER_GROUP, PER_GROUP)]
+            parts += [(INNER + (i * GROUPS + group) * STATE, STATE) for i in range(2)]
+            for start, size in parts:
+                edge[:, to : to + size] = tail[:, start : start + size].astype(F32)[13:16].astype(BF16)
+                to += size
     for copy in started[1:]:
         copy.wait()
 
 
-def pack(place, xbc, dt_raw, weight, bias, shards):
-    tok, channels = xbc.shape
-    half = channels // PAIR
-    smem, vmem, anywhere = (pl.BlockSpec(memory_space=m) for m in (pltpu.SMEM, pltpu.VMEM, pl.ANY))
-    outs = [((tok, half + HEADS), BF16)] * 2 + [((4, half), F32), ((1, half), F32)] + [((3, half), BF16)] * 2
-    return pl.pallas_call(
-        functools.partial(pack_kernel, shards),
-        out_shape=[jax.ShapeDtypeStruct(shape, dtype) for shape, dtype in outs],
-        in_specs=[smem] + [anywhere] * 4,
-        out_specs=[vmem] * len(outs),
-        scratch_shapes=[pltpu.VMEM((16, channels), BF16), pltpu.SemaphoreType.DMA((3 + 12 * shards,))],
-        compiler_params=pltpu.CompilerParams(vmem_limit_bytes=16 << 20),
-        name="pack",
-    )(place, xbc, dt_raw, weight, bias)
-
-
-def conv_kernel(parts, shards, place, *refs):
-    rows, edges, (weight, bias), outs, wide = refs[0:2], refs[2:4], refs[4:6], refs[6:-1], refs[-1]
-    count, total = rows[0].shape
+def merge_kernel(shards, piece, place, xbc, dt_raw, got, near, far, order, *refs):
+    outs, sems = refs[:shards], refs[shards]
     core, shard = place[2], place[4]
-    for side in range(PAIR):
-        here = pl.ds(pl.multiple_of(jnp.where(core == 0, side, 1 - side) * count, count), count)
+    count = xbc.shape[0]
+    first = sum(WIDTHS[:piece])
+    width = WIDTHS[piece]
+    stride = WIDTHS[0] if piece == 0 else PER_GROUP - WIDTHS[0]
+    base = 0 if piece == 0 else first - WIDTHS[0]
+    mine = pl.ds(pl.multiple_of(core * count, count), count)
+    other = pl.ds(pl.multiple_of((1 - core) * count, count), count)
+    copies = []
+    for r in range(shards):
+        group = (shard ^ r) * PAIR + core
+        copies.append((xbc.at[:, channels(group, first, width)], outs[r].at[mine, :width]))
+        at = r * stride + base
+        copies.append((got.at[:, at : at + width], outs[r].at[other, :width]))
+        to = width
+        for kind in RESTS[piece]:
+            if kind in "BC":
+                i = "BC".index(kind)
+                copies.append((xbc.at[:, ds(INNER + (i * GROUPS + group) * STATE, STATE)], outs[r].at[mine, to : to + STATE]))
+                at = stride * shards + (i * shards + r) * STATE
+                copies.append((got.at[:, at : at + STATE], outs[r].at[other, to : to + STATE]))
+                to += STATE
+    started = run(copies, sems)
+    if "D" in RESTS[piece]:
+        lane = lax.broadcasted_iota(jnp.int32, (count, LANES), 1)
+        per_tile = LANES * GROUPS // HEADS
+        heads = HEADS // GROUPS
         for r in range(shards):
-            start = 0
-            for origin, stride, width in parts:
-                to = slice(start, start + width)
-                start += width
-                if stride == 0:
-                    tile = ((shard ^ r) * PAIR + core) // (LANES * GROUPS // HEADS)
-                    at = pl.ds(pl.multiple_of(total - HEADS + tile * LANES, LANES), LANES)
-                    outs[r][here, to] = rows[side][:, at]
-                    continue
-                at = slice(origin + r * stride, origin + r * stride + width)
-                wide[5:8, :width] = edges[side][:, at].astype(F32)
-                wide[8:, :width] = rows[side][:, at].astype(F32)
-                tap = weight[:, at] * 0.5
-                acc = bias[:, at] * 0.5 + tap[0:1] * wide[5 : 5 + count, :width]
-                acc = acc + tap[1:2] * wide[6 : 6 + count, :width]
-                acc = acc + tap[2:3] * wide[7 : 7 + count, :width]
-                acc = acc + tap[3:4] * wide[8 : 8 + count, :width]
-                outs[r][here, to] = (acc + acc * jnp.tanh(acc)).astype(BF16)
-
-
-def activate(place, rows, edges, taps, bias, first, width, rest, shards):
-    tok = rows[0].shape[0]
-    per_group = HEADS * HEAD_DIM // GROUPS
-    inner = per_group * shards
-    parts = [(first, per_group, width)]
-    for kind in rest:
-        parts.append({"B": (inner, STATE, STATE), "C": (inner + shards * STATE, STATE, STATE), "D": (0, 0, LANES)}[kind])
-    total = sum(part[2] for part in parts)
-    return local_call(
-        functools.partial(conv_kernel, parts, shards),
-        [((PAIR * tok, total), BF16)] * shards,
-        [place, *rows, *edges, taps, bias],
-        scratch=[pltpu.VMEM((tok + 8, max(p[2] for p in parts)), F32)],
-        flops=shards * PAIR * tok * total * 12,
-        transcendentals=shards * PAIR * tok * total,
-        name="conv",
-    )
+            group = (shard ^ r) * PAIR + core
+            tile, shift = group // per_tile, (LANES - (group % per_tile) * heads) % LANES
+            own = dt_raw[:, ds(tile * LANES, LANES)].astype(F32)
+            theirs = got[:, ds(got.shape[1] - HEADS + tile * LANES, LANES)].astype(F32)
+            low = jnp.where(core == 0, own, theirs)
+            high = jnp.where(core == 0, theirs, own)
+            packed = jnp.zeros((count // 2, LANES), F32)
+            for j, rows in enumerate((low, high)):
+                rows = jnp.where(lane < heads, pltpu.roll(rows, shift, 1), 0.0)
+                for i in range(2):
+                    part = rows[i * count // 2 : (i + 1) * count // 2]
+                    packed = packed + pltpu.roll(part, (2 * j + i) * heads, 1)
+            outs[r][: count // 2, to : to + LANES] = packed.astype(BF16)
+            size = PER_GROUP + 2 * STATE
+            at = slice(r * size, (r + 1) * size)
+            edge = near[:, at].astype(F32) + far[:, at].astype(F32)
+            edge = jnp.concatenate([edge, jnp.zeros((1, size), F32)], 0)
+            edge = jnp.concatenate([edge[:, q * LANES : (q + 1) * LANES] for q in range(size // LANES)], 0)
+            fill = jnp.zeros((PAIR * count - count // 2 - edge.shape[0], LANES), F32)
+            outs[r][count // 2 :, to : to + LANES] = jnp.concatenate([edge, fill], 0).astype(BF16)
+    for copy in started:
+        copy.wait()
 
 
 def exchange(blocks, axes, length):
@@ -297,38 +317,71 @@
     return [got[r] for r in range(shards)]
 
 
-def in_order(place, blocks, columns, out):
+def convolve_in_order(place, blocks, columns, edge, tap, bias, wide, put):
+    width = columns.stop - columns.start
     count = blocks[0].shape[0] // PAIR
+    wide[5:8, :width] = edge
     for r, block in enumerate(blocks):
         for core in range(PAIR):
-            at = pl.multiple_of((core * len(blocks) + (place[4] ^ r)) * count, count)
-            out[pl.ds(at, count), :] = block[core * count : (core + 1) * count, columns]
-
-
-def prep_kernel(peers, place, *refs):
-    blocks, (a_ref, bias_ref, skip_ref) = refs[:peers], refs[peers : peers + 3]
-    b_ref, cum_ref, row_ref, factor_ref, tail_ref, skip_out, dt_ref = refs[peers + 3 :]
+            at = pl.multiple_of((core * len(blocks) + (place[4] ^ r)) * count + 8, 8)
+            wide[pl.ds(at, count), :width] = block[core * count : (core + 1) * count, columns].astype(F32)
+    tap, bias = tap * 0.5, bias * 0.5
+    for start in range(0, PAIR * len(blocks) * count, count):
+        acc = bias + tap[0:1] * wide[start + 5 : start + 5 + count, :width]
+        acc = acc + tap[1:2] * wide[start + 6 : start + 6 + count, :width]
+        acc = acc + tap[2:3] * wide[start + 7 : start + 7 + count, :width]
+        acc = acc + tap[3:4] * wide[start + 8 : start + 8 + count, :width]
+        put(start, count, (acc + acc * jnp.tanh(acc)).astype(BF16))
+
+
+def prep_kernel(shards, place, *refs):
+    blocks, (taps, offset, a_ref, bias_ref, skip_ref) = refs[:shards], refs[shards : shards + 5]
+    b_ref, edge_ref, cum_ref, row_ref, factor_ref, tail_ref, skip_out, dt_ref, wide = refs[shards + 5 :]
     start = blocks[0].shape[1] - STATE - LANES
-    in_order(place, blocks, slice(start, start + STATE), b_ref)
-    in_order(place, blocks, slice(start + STATE, start + STATE + LANES), dt_ref)
+    last = slice(start + STATE, start + STATE + LANES)
+    size = edge_ref.shape[1]
+    count = blocks[0].shape[0] // PAIR
+    half, heads = count // 2, HEADS // GROUPS
+    edge = blocks[0][half : half + 4 * size // LANES, last].astype(F32)
+    for block in blocks[1:]:
+        edge = edge + block[half : half + 4 * size // LANES, last].astype(F32)
+    for q in range(size // LANES):
+        edge_ref[:, q * LANES : (q + 1) * LANES] = edge[4 * q : 4 * q + 4]
+    for r, block in enumerate(blocks):
+        packed = block[:half, last].astype(F32)
+        for j in range(2 * PAIR):
+            at = ((j // 2) * shards + (place[4] ^ r)) * count + (j % 2) * half
+            rows = packed if j == 0 else pltpu.roll(packed, LANES - j * heads, 1)
+            dt_ref[pl.ds(pl.multiple_of(at, half), half), :] = rows
+
+    def put(start, count, value):
+        b_ref[start : start + count] = value
+
+    at = slice(PER_GROUP, PER_GROUP + STATE)
+    convolve_in_order(
+        place, blocks, slice(start, start + STATE), edge_ref[0:3, at], taps[:, at], offset[:, at], wide, put
+    )
     per_tile = LANES * GROUPS // HEADS
     group = place[0]
     tile = group // per_tile
-    shift = (LANES - (group % per_tile) * (HEADS // GROUPS)) % LANES
-    rate = -jnp.exp(a_ref[pl.ds(tile, 1), :])
-    raw = dt_ref[...].astype(F32) + bias_ref[pl.ds(tile, 1), :]
+    shift = (LANES - (group % per_tile) * heads) % LANES
+
+    def lanes_of(ref):
+        return pltpu.roll(jnp.broadcast_to(ref[pl.ds(tile, 1), :], (8, LANES)), shift, 1)
+
+    rate = -jnp.exp(lanes_of(a_ref)[0:1])
+    raw = dt_ref[...] + lanes_of(bias_ref)[0:1]
     step = jnp.maximum(raw, 0.0) + jnp.log1p(jnp.exp(-jnp.abs(raw)))
-    step = pltpu.roll(step, shift, 1)
-    rate = pltpu.roll(jnp.broadcast_to(rate, (8, LANES)), shift, 1)[0:1]
-    skip = pltpu.roll(jnp.broadcast_to(skip_ref[pl.ds(tile, 1), :], (8, LANES)), shift, 1)
+    skip = lanes_of(skip_ref)
     skip_out[...] = jnp.concatenate(halves(jnp.concatenate([skip, skip], 0), 3), 1)
     lower = (
         lax.broadcasted_iota(jnp.int32, (BLOCK, BLOCK), 0)
         >= lax.broadcasted_iota(jnp.int32, (BLOCK, BLOCK), 1)
     ).astype(BF16)
+    valid = lax.broadcasted_iota(jnp.int32, (BLOCK, LANES), 1) < heads
     for block in range(PAIR):
         at = slice(block * BLOCK, (block + 1) * BLOCK)
-        here = step[at]
+        here = jnp.where(valid, step[at], 1.0)
         parts = halves(here * rate, 3)
         cum = dot(lower, parts[0]) + (dot(lower, parts[1]) + dot(lower, parts[2]))
         cum = cum * LOG2E
@@ -339,10 +392,17 @@
         tail_ref[at] = jnp.concatenate(halves(tail, 2), 1)
 
 
-def score_kernel(peers, place, *refs):
-    blocks, (b_ref, c_ref, score_ref) = refs[:peers], refs[peers:]
+def score_kernel(shards, place, *refs):
+    blocks, (taps, offset, edge_ref, b_ref, order, c_ref, score_ref, wide) = refs[:shards], refs[shards:]
     start = blocks[0].shape[1] - STATE
-    in_order(place, blocks, slice(start, start + STATE), c_ref)
+    at = slice(PER_GROUP + STATE, PER_GROUP + 2 * STATE)
+
+    def put(start, count, value):
+        c_ref[start : start + count] = value
+
+    convolve_in_order(
+        place, blocks, slice(start, start + STATE), edge_ref[0:3, at], taps[:, at], offset[:, at], wide, put
+    )
     for block in range(PAIR):
         at = slice(block * BLOCK, (block + 1) * BLOCK)
         score_ref[at] = lax.dot_general(
@@ -350,29 +410,67 @@
         )
 
 
-def state_kernel(first_head, peers, place, *refs):
-    blocks, (b_ref, factor_ref, tail_ref, x_ref, send_ref, own_ref) = refs[:peers], refs[peers:]
+def decay_of(ref):
+    decay = ref[STATE : STATE + 16].astype(F32)
+    return decay[0:1] + (decay[1:2] + decay[2:3])
+
+
+def put_decay(ref, decay):
+    row = lax.broadcasted_iota(jnp.int32, (16, ref.shape[1]), 0)
+    high, middle, low = (part.astype(F32) for part in halves(decay, 3))
+    packed = jnp.where(row == 0, high, jnp.where(row == 1, middle, jnp.where(row == 2, low, 0.0)))
+    ref[STATE:] = packed.astype(BF16)
+
+
+def state_kernel(shards, pieces, place, *refs):
+    blocks, refs = refs[: shards * len(pieces)], refs[shards * len(pieces) :]
+    taps, offset, edge_ref, b_ref, factor_ref, tail_ref, order, x_ref, send_ref, own_ref, wide = refs
     width = x_ref.shape[1]
-    in_order(place, blocks, slice(0, width), x_ref)
-    wide = spread(first_head, width, 2)
+    first = sum(WIDTHS[: pieces[0]])
+    start = 0
+    for i, piece in enumerate(pieces):
+        to = slice(start, start + WIDTHS[piece])
+        at = slice(first + start, first + start + WIDTHS[piece])
+        start += WIDTHS[piece]
+
+        def put(row, count, value, to=to):
+            x_ref[row : row + count, to] = value
+
+        convolve_in_order(
+            place,
+            blocks[i * shards : (i + 1) * shards],
+            slice(0, WIDTHS[piece]),
+            edge_ref[0:3, at],
+            taps[:, at],
+            offset[:, at],
+            wide,
+            put,
+        )
+    expand = spread(first // HEAD_DIM, width, 2)
     both = []
     for block in range(PAIR):
         at = slice(block * BLOCK, (block + 1) * BLOCK)
-        loaded = (x_ref[at].astype(F32) * dot(tail_ref[at], wide)).astype(BF16)
+        loaded = (x_ref[at].astype(F32) * dot(tail_ref[at], expand)).astype(BF16)
         both.append(
             lax.dot_general(b_ref[at], loaded, (((0,), (0,)), ((), ())), preferred_element_type=F32)
         )
-    ends = [dot(factor_ref[(i + 1) * BLOCK - 16 : (i + 1) * BLOCK], wide)[15:16] for i in range(PAIR)]
+    ends = [dot(factor_ref[(i + 1) * BLOCK - 16 : (i + 1) * BLOCK], expand)[15:16] for i in range(PAIR)]
     own_ref[...] = both[0]
     send_ref[0:STATE] = (ends[1] * both[0] + both[1]).astype(BF16)
     put_decay(send_ref, ends[0] * ends[1])
 
 
-def local_kernel(first_head, x_ref, cum_ref, row_ref, score_ref, skip_ref, out_ref):
+def combine_kernel(early_ref, late_ref, order, out_ref):
+    decay = decay_of(late_ref)
+    out_ref[:STATE] = (decay * early_ref[:STATE].astype(F32) + late_ref[:STATE].astype(F32)).astype(BF16)
+    put_decay(out_ref, decay * decay_of(early_ref))
+
+
+def local_kernel(first_head, x_ref, cum_ref, row_ref, score_ref, skip_ref, order, out_ref):
     width = x_ref.shape[1]
     half = BLOCK // 2
-    wide = spread(first_head, width, 3)
-    skip = dot(skip_ref[...], wide)[0:1]
+    expand = spread(first_head, width, 3)
+    skip = dot(skip_ref[...], expand)[0:1]
     lower = lax.broadcasted_iota(jnp.int32, (half, half), 0) >= lax.broadcasted_iota(
         jnp.int32, (half, half), 1
     )
@@ -401,32 +499,14 @@
             out_ref[base + half : base + BLOCK, columns] = bottom
 
 
-def decay_of(ref):
-    decay = ref[STATE : STATE + 16].astype(F32)
-    return decay[0:1] + (decay[1:2] + decay[2:3])
-
-
-def put_decay(ref, decay):
-    row = lax.broadcasted_iota(jnp.int32, (16, ref.shape[1]), 0)
-    high, middle, low = (part.astype(F32) for part in halves(decay, 3))
-    packed = jnp.where(row == 0, high, jnp.where(row == 1, middle, jnp.where(row == 2, low, 0.0)))
-    ref[STATE:] = packed.astype(BF16)
-
-
-def combine_kernel(early_ref, late_ref, out_ref):
-    decay = decay_of(late_ref)
-    out_ref[:STATE] = (decay * early_ref[:STATE].astype(F32) + late_ref[:STATE].astype(F32)).astype(BF16)
-    put_decay(out_ref, decay * decay_of(early_ref))
-
-
 def final_kernel(first_head, place, *refs):
     last, before, alone, own_ref, c_ref, factor_ref, partial_ref, keep_ref, send_ref = refs
     width = own_ref.shape[1]
     core = place[2]
-    wide = spread(first_head, width, 2)
+    expand = spread(first_head, width, 2)
     held = last[:STATE].astype(F32) + decay_of(last) * before[:STATE].astype(F32)
     held = held + alone[:STATE].astype(F32)
-    factor = dot(factor_ref[...], wide)
+    factor = dot(factor_ref[...], expand)
     outs = []
     for block in range(PAIR):
         at = slice(block * BLOCK, (block + 1) * BLOCK)
@@ -462,10 +542,17 @@
     pl.when(core == 1)(lambda: put(half, 0))
 
 
-def local_call(body, outs, operands, scratch=(), flops=0, transcendentals=0, name=None):
+class Stay:
+    def __init__(self, array):
+        self.array = array
+
+
+def call(body, outs, operands, scratch=(), flops=0, transcendentals=0, name=None):
     shapes = [jax.ShapeDtypeStruct(shape, dtype) for shape, dtype in outs]
-    smem, vmem = pl.BlockSpec(memory_space=pltpu.SMEM), pl.BlockSpec(memory_space=pltpu.VMEM)
-    specs = [smem if o.dtype == jnp.int32 else vmem for o in operands]
+    smem, vmem, hbm = (pl.BlockSpec(memory_space=m) for m in (pltpu.SMEM, pltpu.VMEM, pltpu.HBM))
+    specs = [
+        hbm if isinstance(o, Stay) else smem if o.dtype == jnp.int32 else vmem for o in operands
+    ]
     moved = sum(o.size * o.dtype.itemsize for o in shapes) * 2
     return pl.pallas_call(
         body,
@@ -476,16 +563,15 @@
         compiler_params=pltpu.CompilerParams(vmem_limit_bytes=16 << 20),
         cost_estimate=pl.CostEstimate(flops=flops, bytes_accessed=moved, transcendentals=transcendentals),
         name=name,
-    )(*operands)
+    )(*[o.array if isinstance(o, Stay) else o for o in operands])
 
 
 def paired(xbc, dt_raw, conv_weight, conv_bias, a_log, dt_bias, skip_gain):
     axes = ("ctx", "head")
     shards, length = lax.axis_size("head"), lax.axis_size("ctx")
-    devices, peers, pairs = shards * length, shards * PAIR, length // PAIR
+    devices, peers = shards * length, shards * PAIR
     tok = xbc.shape[0]
     slab = tok * peers
-    per_group = HEADS // GROUPS
     context, shard = lax.axis_index("ctx"), lax.axis_index("head")
     pair, core = context // PAIR, context % PAIR
     group = shard * PAIR + core
@@ -495,67 +581,120 @@
         route = [(i, target(i)) for i in range(devices)]
         return lax.ppermute(block, axes, [(i, j) for i, j in route if j is not None and j < devices])
 
-    own, send, taps, bias, near, far = pack(place, xbc, dt_raw, conv_weight, conv_bias[None], shards)
-    near = over(near, lambda i: i + 1)
-    far = over(far, lambda i: (i + 1) ^ shards)
-    rows = (own, over(send, lambda i: i ^ shards))
-
-    received, starts = [], []
-    first = 0
-    for width, rest in PIECES:
-        sent = activate(place, rows, (near, far), taps, bias, first, width, rest, shards)
-        received.append(exchange(sent, axes, length))
-        starts.append(first // HEAD_DIM)
-        first += width
+    def swap(block):
+        return over(block, lambda i: i ^ shards)
+
+    rows = Stay(xbc)
+    (sent,) = call(
+        functools.partial(pack_first_kernel, shards),
+        [((tok, shards * WIDTHS[0]), BF16)],
+        [place, rows],
+        scratch=[pltpu.SemaphoreType.DMA((shards,))],
+        name="pack_first",
+    )
+    got_first = swap(sent)
+    size = PER_GROUP + 2 * STATE
+    sent, taps, offset, near, far = call(
+        functools.partial(pack_kernel, shards),
+        [
+            ((tok, shards * (size - WIDTHS[0]) + HEADS), BF16),
+            ((4, size), F32),
+            ((1, size), F32),
+            ((3, shards * size), BF16),
+            ((3, shards * size), BF16),
+        ],
+        [place, rows, Stay(dt_raw), Stay(conv_weight), Stay(conv_bias[None]), Stay(sent)],
+        scratch=[pltpu.VMEM((16, xbc.shape[1]), BF16), pltpu.SemaphoreType.DMA((3 * shards + 8,))],
+        name="pack",
+    )
+    near = over(near, lambda i: i + peers if i % peers == peers - 1 else None)
+    far = over(far, lambda i: i + shards if i % peers == peers - 1 else None)
+    got_rest = swap(sent)
+
+    received, order = [], place
+    for piece, (width, rest) in enumerate(zip(WIDTHS, RESTS)):
+        total = width + sum(LANES if kind == "D" else STATE for kind in rest)
+        blocks = call(
+            functools.partial(merge_kernel, shards, piece),
+            [((PAIR * tok, total), BF16)] * shards,
+            [
+                place,
+                rows,
+                dt_raw if "D" in rest else Stay(dt_raw),
+                got_rest if piece else got_first,
+                near if "D" in rest else Stay(got_first),
+                far if "D" in rest else Stay(got_first),
+                Stay(received[piece - 2][2] if piece > 1 else got_first),
+            ],
+            scratch=[pltpu.SemaphoreType.DMA((2 * shards * (1 + len(rest)),))],
+            name="merge",
+        )
+        received.append(exchange(blocks, axes, length))
 
     tiles = [p.reshape(HEADS // LANES, LANES) for p in (a_log, dt_bias, skip_gain)]
-    b, cum, row, factor, tail, skip = local_call(
+    b, edge, cum, row, factor, tail, skip = call(
         functools.partial(prep_kernel, shards),
         [
             ((slab, STATE), BF16),
+            ((4, size), F32),
             ((slab, LANES), F32),
             ((LANES, slab), F32),
             ((slab, 2 * LANES), BF16),
             ((slab, 2 * LANES), BF16),
             ((16, 3 * LANES), BF16),
         ],
-        [place] + received[0] + tiles,
-        scratch=[pltpu.VMEM((slab, LANES), BF16)],
+        [place] + received[1] + [taps, offset] + tiles,
+        scratch=[pltpu.VMEM((slab, LANES), F32), pltpu.VMEM((slab + 8, STATE), F32)],
         flops=2 * slab * BLOCK * 3 * LANES,
+        transcendentals=slab * STATE,
         name="prep",
     )
-    c, score = local_call(
+    pieces, order = [], place
+    for joined in JOINED:
+        width = sum(WIDTHS[piece] for piece in joined)
+        x, sent, own = call(
+            functools.partial(state_kernel, shards, joined),
+            [((slab, width), BF16), ((STATE + 16, width), BF16), ((STATE, width), F32)],
+            [place]
+            + [block for piece in joined for block in received[piece]]
+            + [taps, offset, edge, b, factor, tail, Stay(order)],
+            scratch=[pltpu.VMEM((slab + 8, max(WIDTHS)), F32)],
+            flops=4 * slab * STATE * width,
+            transcendentals=slab * width,
+            name="state",
+        )
+        last = over(sent, lambda i: i + peers if i // peers % 2 == 0 else None)
+        (combined,) = call(
+            combine_kernel,
+            [(sent.shape, BF16)],
+            [last, sent, Stay(order)],
+            flops=4 * sent.size,
+            name="combine",
+        )
+        before = over(combined, lambda i: i + 2 * peers if i // peers == 1 else None)
+        alone = over(combined, lambda i: i + peers if i // peers == 1 else None)
+        pieces.append((sum(WIDTHS[: joined[0]]) // HEAD_DIM, width, [last, before, alone], own, x, sent))
+        order = sent
+    c, score = call(
         functools.partial(score_kernel, shards),
         [((slab, STATE), BF16), ((slab, BLOCK), F32)],
-        [place] + received[1] + [b],
+        [place] + received[2] + [taps, offset, edge, b, Stay(pieces[1][5])],
+        scratch=[pltpu.VMEM((slab + 8, STATE), F32)],
         flops=2 * slab * BLOCK * STATE,
+        transcendentals=slab * STATE,
         name="score",
     )
-    pieces = []
-    for head, (width, _), blocks in zip(starts, PIECES, received):
-        x, sent, own = local_call(
-            functools.partial(state_kernel, head, shards),
-            [((slab, width), BF16), ((STATE + 16, width), BF16), ((STATE, width), F32)],
-            [place] + blocks + [b, factor, tail],
-            flops=4 * slab * STATE * width,
-            name="state",
-        )
-        last = over(sent, lambda i: i + peers if i // peers % 2 == 0 else None)
-        (joined,) = local_call(combine_kernel, [(sent.shape, BF16)], [last, sent], name="combine")
-        before = over(joined, lambda i: i + 2 * peers if i // peers == 1 else None)
-        alone = over(joined, lambda i: i + peers if i // peers == 1 else None)
-        (partial,) = local_call(
+    keeps, gots = [], []
+    for head, width, earlier, own, x, _ in pieces:
+        (partial,) = call(
             functools.partial(local_kernel, head),
             [((slab, width), F32)],
-            [x, cum, row, score, skip],
+            [x, cum, row, score, skip, Stay(score)],
             flops=8 * slab * STATE * width,
             transcendentals=slab * BLOCK * width // HEAD_DIM,
             name="local",
         )
-        pieces.append((head, width, [last, before, alone], own, partial))
-    keeps, gots = [], []
-    for head, width, earlier, own, partial in pieces:
-        keep, send = local_call(
+        keep, send = call(
             functools.partial(final_kernel, head),
             [((BLOCK, width), BF16)] * 2,
             [place] + earlier + [own, c, factor, partial],
@@ -563,10 +702,10 @@
             name="final",
         )
         keeps.append(keep)
-        gots.append(over(send, lambda i: i ^ shards))
-    (out,) = local_call(
+        gots.append(swap(send))
+    (out,) = call(
         functools.partial(assemble_kernel, len(keeps)),
-        [((BLOCK, PAIR * per_group * HEAD_DIM), BF16)],
+        [((BLOCK, PAIR * PER_GROUP), BF16)],
         [place] + keeps + gots,
         name="assemble",
     )

time: 136 us -> 121 us (0.89)
  waiting for transfers between devices: 60.8 us -> 51.5 us
  starting transfers between devices: 41.3 us -> 38.1 us
  local copies, waits for them, and re-layouts: 4.46 us -> 2.18 us
    ppermute x19 -> x16, starting transfers between devices: 27.1 us -> 18.8 us  [over(): lax.ppermute(block, axes, [(i, j) for i, j in route if j is not None and...]
    ppermute x12, starting transfers between devices: 14.2 us -> 19.3 us  [exchange(): got[r] = lax.ppermute(blocks[r], axes, route)]
    ppermute x12, waiting for transfers between devices: 50.6 us -> 45.8 us  [exchange(): got[r] = lax.ppermute(blocks[r], axes, route)]
    ppermute x19 -> x16, waiting for transfers between devices: 10.2 us -> 5.68 us  [over(): lax.ppermute(block, axes, [(i, j) for i, j in route if j is not None and...]
    unnamed x14 -> x16, local copies, waits for them, and re-layouts: 4.37 us -> 2.09 us
    pallas_call x24 -> x21, Pallas kernels: 27.7 us -> 26.4 us  [call(): pl.pallas_call(body, out_shape=shapes, in_specs=specs, out_specs=[vmem] *...]
  transfers between devices with their start and end apart: 31 -> 28, of which waited for: 11 -> 12; matrix products, arithmetic and copies ran while one was open for 0% -> 0% of each run, Pallas kernels for 16% -> 15%
where the time goes in v4:
time: 121 us; the launch traced here: 119 us
  waiting for transfers between devices  51.5 us (43%)
  starting transfers between devices  38.1 us (31%)
  Pallas kernels  26.4 us (22%)
  local copies, waits for them, and re-layouts  2.18 us (2%)
    ppermute x12, waiting for transfers between devices, exchange(): got[r] = lax.ppermute(blocks[r], axes, route)  45.8 us
    pallas_call x21, Pallas kernels, call(): pl.pallas_call(body, out_shape=shapes, in_specs=specs, out_specs=[vmem] *...  26.4 us
    ppermute x12, starting transfers between devices, exchange(): got[r] = lax.ppermute(blocks[r], axes, route)  19.3 us
    ppermute x16, starting transfers between devices, over(): lax.ppermute(block, axes, [(i, j) for i, j in route if j is not None and...  18.8 us
    ppermute x16, waiting for transfers between devices, over(): lax.ppermute(block, axes, [(i, j) for i, j in route if j is not None and...  5.68 us
  transfers between devices with their start and end apart: 28, of which 12 were waited for; matrix products, arithmetic and copies ran while one was open for 0% of the time, Pallas kernels for 15%

profile of v4, /device:TPU:13, one launch (start us, length us, event | category | flops | bytes accessed | tf_op | source)
XLA Modules:
  0.0 118.5 jit_solution(17262655330798183895)
XLA Ops:
  0.1 1.7 %copy-done = bf16[64,20480]{1,0:T(8,128)(2,1)S(1)} copy-done((bf16[64,20480]{1,0:T(8,128)(2,1)S(1)}, bf16[64,20480]{1,0:T(8,128)(2,1)}, u32[]{:S(2)}) %copy-start) | copy-done | bytes 2621464
  2.8 1.3 %pack.1 = (bf16[64,8448]{1,0:T(8,128)(2,1)S(1)}, f32[4,2560]{1,0:T(4,128)S(1)}, f32[1,2560]{1,0:T(1,128)S(1)}, bf16[3,10240]{1,0:T(4,128)(2,1)S(1)}, bf16[3,10240]{1,0:T(4,128)(2,1)S(1)}) custom-call(s32[5]{0:T(128)S(1)} %stack.23.place.refs_14_.order, bf16[64,20480]{1,0:T(8,128)(2,1)S(1)} %copy-done, bf16[64,256]{1,0:T(8,128)(2,1)S(1)} %copy-done.2, ...), custom_call_target="tpu_custom_call" | custom-call | bytes 2510848 | tf_op jit(solution)/shard_map/pack/pallas_call | solution.py:557
  6.3 1.3 %collective-permute-done.got.near.far.order = bf16[64,2048]{1,0:T(8,128)(2,1)S(1)} collective-permute-done((bf16[64,2048]{1,0:T(8,128)(2,1)S(1)}, bf16[64,2048]{1,0:T(8,128)(2,1)S(1)}, u32[]{:S(2)}, u32[]{:S(2)}) %collective-permute-start) | collective-permute-done | bytes 262176 | tf_op jit(solution)/shard_map/ppermute | solution.py:582
  9.0 5.7 %collective-permute-start.8 = (bf16[128,896]{1,0:T(8,128)(2,1)S(1)}, bf16[128,896]{1,0:T(8,128)(2,1)S(1)}, u32[]{:S(2)}, u32[]{:S(2)}) collective-permute-start(bf16[128,896]{1,0:T(8,128)(2,1)S(1)} %get-tuple-element.59), channel_id=1, source_target_pairs={{0,2},{1,3},{2,0},{3,1},{4,6},{5,7},{6,4},{7,5},{8,10},{9,11},{10,... | collective-permute-start | bytes 688136 | tf_op jit(solution)/shard_map/ppermute | solution.py:316
  16.9 2.2 %collective-permute-start.2 = (bf16[128,512]{1,0:T(8,128)(2,1)S(1)}, bf16[128,512]{1,0:T(8,128)(2,1)S(1)}, u32[]{:S(2)}, u32[]{:S(2)}) collective-permute-start(bf16[128,512]{1,0:T(8,128)(2,1)S(1)} %get-tuple-element.52), channel_id=1, source_target_pairs={{0,2},{1,3},{2,0},{3,1},{4,6},{5,7},{6,4},{7,5},{8,10},{9,11},{10,... | collective-permute-start | bytes 393224 | tf_op jit(solution)/shard_map/ppermute | solution.py:316
  20.1 10.7 %collective-permute-done.8.refs_2_.refs_6_.order = bf16[128,896]{1,0:T(8,128)(2,1)S(1)} collective-permute-done((bf16[128,896]{1,0:T(8,128)(2,1)S(1)}, bf16[128,896]{1,0:T(8,128)(2,1)S(1)}, u32[]{:S(2)}, u32[]{:S(2)}) %collective-permute-start.8) | collective-permute-done | bytes 229408 | tf_op jit(solution)/shard_map/ppermute | solution.py:316
  30.8 8.5 %collective-permute-done.9.refs_3_.refs_7_ = bf16[128,896]{1,0:T(8,128)(2,1)S(1)} collective-permute-done((bf16[128,896]{1,0:T(8,128)(2,1)S(1)}, bf16[128,896]{1,0:T(8,128)(2,1)S(1)}, u32[]{:S(2)}, u32[]{:S(2)}) %collective-permute-start.9) | collective-permute-done | bytes 229408 | tf_op jit(solution)/shard_map/ppermute | solution.py:316
  39.3 1.7 %prep.1 = (bf16[512,256]{1,0:T(8,128)(2,1)S(1)}, f32[4,2560]{1,0:T(4,128)S(1)}, f32[512,128]{1,0:T(8,128)S(1)}, f32[128,512]{1,0:T(8,128)S(1)}, bf16[512,256]{1,...) custom-call(s32[5]{0:T(128)S(1)} %stack.23.place.refs_14_.order, ...), custom_call_target="tpu_custom_call" | custom-call | flops 100663296 | bytes 2727936 | tf_op jit(solution)/shard_map/prep/pallas_call | solution.py:557
  42.1 2.8 %collective-permute-done.3.refs_3_ = bf16[128,512]{1,0:T(8,128)(2,1)S(1)} collective-permute-done((bf16[128,512]{1,0:T(8,128)(2,1)S(1)}, bf16[128,512]{1,0:T(8,128)(2,1)S(1)}, u32[]{:S(2)}, u32[]{:S(2)}) %collective-permute-start.3) | collective-permute-done | bytes 131104 | tf_op jit(solution)/shard_map/ppermute | solution.py:316
  44.9 3.4 %state.3 = (bf16[512,1024]{1,0:T(8,128)(2,1)S(1)}, bf16[272,1024]{1,0:T(8,128)(2,1)S(1)}, f32[256,1024]{1,0:T(8,128)S(1)}) custom-call(s32[5]{0:T(128)S(1)} %stack.23.place.refs_14_.order, bf16[128,512]{1,0:T(8,128)(2,1)S(1)} %get-tuple-element.50.refs_0_, bf16[128,512]{1,0:T(8,128)(2,1)S(1)} %collective-permute-done.1.refs_1_, ...), custom_call_target="tpu_custom_call" | custom-call | flops 536870912 | bytes 5308416 | tf_op jit(solution)/shard_map/state/pallas_call | solution.py:557
  48.3 2.2 %collective-permute-start.10 = (bf16[272,1024]{1,0:T(8,128)(2,1)S(1)}, bf16[272,1024]{1,0:T(8,128)(2,1)S(1)}, u32[]{:S(2)}, u32[]{:S(2)}) collective-permute-start(bf16[272,1024]{1,0:T(8,128)(2,1)S(1)} %get-tuple-element.67.late_ref.refs_10_.order), channel_id=1, source_target_pairs={{0,8},{1,9},{2,10},{3,11},{4,12},{5,13},{6,14},{7,15},{16,24},{17,... | collective-permute-start | bytes 1671176 | tf_op jit(solution)/shard_map/ppermute | solution.py:582
  51.5 3.4 %collective-permute-start.14 = (bf16[128,896]{1,0:T(8,128)(2,1)S(1)}, bf16[128,896]{1,0:T(8,128)(2,1)S(1)}, u32[]{:S(2)}, u32[]{:S(2)}) collective-permute-start(bf16[128,896]{1,0:T(8,128)(2,1)S(1)} %get-tuple-element.71), channel_id=1, source_target_pairs={{0,2},{1,3},{2,0},{3,1},{4,6},{5,7},{6,4},{7,5},{8,10},{9,11},{10,... | collective-permute-start | bytes 688136 | tf_op jit(solution)/shard_map/ppermute | solution.py:316
  54.9 1.5 %collective-permute-done.13.refs_1_ = bf16[128,896]{1,0:T(8,128)(2,1)S(1)} collective-permute-done((bf16[128,896]{1,0:T(8,128)(2,1)S(1)}, bf16[128,896]{1,0:T(8,128)(2,1)S(1)}, u32[]{:S(2)}, u32[]{:S(2)}) %collective-permute-start.13) | collective-permute-done | bytes 229408 | tf_op jit(solution)/shard_map/ppermute | solution.py:316
  56.4 12.7 %collective-permute-done.14.refs_2_ = bf16[128,896]{1,0:T(8,128)(2,1)S(1)} collective-permute-done((bf16[128,896]{1,0:T(8,128)(2,1)S(1)}, bf16[128,896]{1,0:T(8,128)(2,1)S(1)}, u32[]{:S(2)}, u32[]{:S(2)}) %collective-permute-start.14) | collective-permute-done | bytes 229408 | tf_op jit(solution)/shard_map/ppermute | solution.py:316
  69.1 4.9 %collective-permute-done.15.refs_3_ = bf16[128,896]{1,0:T(8,128)(2,1)S(1)} collective-permute-done((bf16[128,896]{1,0:T(8,128)(2,1)S(1)}, bf16[128,896]{1,0:T(8,128)(2,1)S(1)}, u32[]{:S(2)}, u32[]{:S(2)}) %collective-permute-start.15) | collective-permute-done | bytes 229408 | tf_op jit(solution)/shard_map/ppermute | solution.py:316
  74.0 2.4 %state.4 = (bf16[512,640]{1,0:T(8,128)(2,1)S(1)}, bf16[272,640]{1,0:T(8,128)(2,1)S(1)}, f32[256,640]{1,0:T(8,128)S(1)}) custom-call(s32[5]{0:T(128)S(1)} %stack.23.place.refs_14_.order, bf16[128,896]{1,0:T(8,128)(2,1)S(1)} %get-tuple-element.69.refs_0_, bf16[128,896]{1,0:T(8,128)(2,1)S(1)} %collective-permute-done.13.refs_1_, ...), custom_call_target="tpu_custom_call" | custom-call | flops 335544320 | bytes 3317760 | tf_op jit(solution)/shard_map/state/pallas_call | solution.py:557
  76.5 1.3 %collective-permute-start.16 = (bf16[272,640]{1,0:T(8,128)(2,1)S(1)}, bf16[272,640]{1,0:T(8,128)(2,1)S(1)}, u32[]{:S(2)}, u32[]{:S(2)}) collective-permute-start(bf16[272,640]{1,0:T(8,128)(2,1)S(1)} %get-tuple-element.73.refs_8_.late_ref.refs_10_.order), channel_id=1, source_target_pairs={{0,8},{1,9},{2,10},{3,11},{4,12},{5,13},{6,14},{7,15},{16,24},{17,... | collective-permute-start | bytes 1044488 | tf_op jit(solution)/shard_map/ppermute | solution.py:582
  78.7 1.3 %collective-permute-start.12 = (bf16[272,1024]{1,0:T(8,128)(2,1)S(1)}, bf16[272,1024]{1,0:T(8,128)(2,1)S(1)}, u32[]{:S(2)}, u32[]{:S(2)}) collective-permute-start(bf16[272,1024]{1,0:T(8,128)(2,1)S(1)} %combine.3), channel_id=1, source_target_pairs={{8,16},{9,17},{10,18},{11,19},{12,20},{13,21},{14,22},{15,23}} | collective-permute-start | bytes 1671176 | tf_op jit(solution)/shard_map/ppermute | solution.py:582
  80.8 3.4 %collective-permute-start.20 = (bf16[128,384]{1,0:T(8,128)(2,1)S(1)}, bf16[128,384]{1,0:T(8,128)(2,1)S(1)}, u32[]{:S(2)}, u32[]{:S(2)}) collective-permute-start(bf16[128,384]{1,0:T(8,128)(2,1)S(1)} %get-tuple-element.86), channel_id=1, source_target_pairs={{0,2},{1,3},{2,0},{3,1},{4,6},{5,7},{6,4},{7,5},{8,10},{9,11},{10,... | collective-permute-start | bytes 294920 | tf_op jit(solution)/shard_map/ppermute | solution.py:316
  84.2 1.8 %collective-permute-start.21 = (bf16[128,384]{1,0:T(8,128)(2,1)S(1)}, bf16[128,384]{1,0:T(8,128)(2,1)S(1)}, u32[]{:S(2)}, u32[]{:S(2)}) collective-permute-start(bf16[128,384]{1,0:T(8,128)(2,1)S(1)} %get-tuple-element.87), channel_id=1, source_target_pairs={{0,3},{1,2},{2,1},{3,0},{4,7},{5,6},{6,5},{7,4},{8,11},{9,10},{10,... | collective-permute-start | bytes 294920 | tf_op jit(solution)/shard_map/ppermute | solution.py:316
  87.5 1.3 %collective-permute-start.18 = (bf16[272,640]{1,0:T(8,128)(2,1)S(1)}, bf16[272,640]{1,0:T(8,128)(2,1)S(1)}, u32[]{:S(2)}, u32[]{:S(2)}) collective-permute-start(bf16[272,640]{1,0:T(8,128)(2,1)S(1)} %combine.4), channel_id=1, source_target_pairs={{8,16},{9,17},{10,18},{11,19},{12,20},{13,21},{14,22},{15,23}} | collective-permute-start | bytes 1044488 | tf_op jit(solution)/shard_map/ppermute | solution.py:582
  89.9 2.8 %collective-permute-done.21.refs_3_ = bf16[128,384]{1,0:T(8,128)(2,1)S(1)} collective-permute-done((bf16[128,384]{1,0:T(8,128)(2,1)S(1)}, bf16[128,384]{1,0:T(8,128)(2,1)S(1)}, u32[]{:S(2)}, u32[]{:S(2)}) %collective-permute-start.21) | collective-permute-done | bytes 98336 | tf_op jit(solution)/shard_map/ppermute | solution.py:316
  92.8 1.9 %state.5 = (bf16[512,384]{1,0:T(8,128)(2,1)S(1)}, bf16[272,384]{1,0:T(8,128)(2,1)S(1)}, f32[256,384]{1,0:T(8,128)S(1)}) custom-call(s32[5]{0:T(128)S(1)} %stack.23.place.refs_14_.order, bf16[128,384]{1,0:T(8,128)(2,1)S(1)} %get-tuple-element.84.refs_0_, bf16[128,384]{1,0:T(8,128)(2,1)S(1)} %collective-permute-done.19.refs_1_, ...), custom_call_target="tpu_custom_call" | custom-call | flops 201326592 | bytes 1990656 | tf_op jit(solution)/shard_map/state/pallas_call | solution.py:557
  94.7 1.6 %collective-permute-start.22 = (bf16[272,384]{1,0:T(8,128)(2,1)S(1)}, bf16[272,384]{1,0:T(8,128)(2,1)S(1)}, u32[]{:S(2)}, u32[]{:S(2)}) collective-permute-start(bf16[272,384]{1,0:T(8,128)(2,1)S(1)} %get-tuple-element.88.late_ref), channel_id=1, source_target_pairs={{0,8},{1,9},{2,10},{3,11},{4,12},{5,13},{6,14},{7,15},{16,24},{17,... | collective-permute-start | bytes 626696 | tf_op jit(solution)/shard_map/ppermute | solution.py:582
  96.2 2.1 %local.3.refs_6_ = f32[512,1024]{1,0:T(8,128)S(1)} custom-call(bf16[512,1024]{1,0:T(8,128)(2,1)S(1)} %get-tuple-element.75.x_ref, f32[512,128]{1,0:T(8,128)S(1)} %get-tuple-element.76.cum_ref, f32[128,512]{1,0:T(8,128)S(1)} %get-tuple-element.77.row_ref, f32[512,256]{1,0:T(8,128)S(1)} %get-tuple-element.78.score_ref.order, ...), custom_call_target="tpu_custom_call" | custom-call | flops 1073741824 | bytes 4194304 | tf_op jit(solution)/shard_map/local/pallas_call | solution.py:557
  98.4 1.6 %final.3 = (bf16[256,1024]{1,0:T(8,128)(2,1)S(1)}, bf16[256,1024]{1,0:T(8,128)(2,1)S(1)}) custom-call(s32[5]{0:T(128)S(1)} %stack.23.place.refs_14_.order, bf16[272,1024]{1,0:T(8,128)(2,1)S(1)} %collective-permute-done.10.early_ref.refs_0_, bf16[272,1024]{1,0:T(8,128)(2,1)S(1)} %collective-permute-done.11.refs_1_, ...), custom_call_target="tpu_custom_call" | custom-call | flops 536870912 | bytes 2097152 | tf_op jit(solution)/shard_map/final/pallas_call | solution.py:557
  99.9 2.2 %collective-permute-start.25 = (bf16[256,1024]{1,0:T(8,128)(2,1)S(1)}, bf16[256,1024]{1,0:T(8,128)(2,1)S(1)}, u32[]{:S(2)}, u32[]{:S(2)}) collective-permute-start(bf16[256,1024]{1,0:T(8,128)(2,1)S(1)} %get-tuple-element.92), channel_id=1, source_target_pairs={{0,4},{1,5},{2,6},{3,7},{4,0},{5,1},{6,2},{7,3},{8,12},{9,13},{10,... | collective-permute-start | bytes 1572872 | tf_op jit(solution)/shard_map/ppermute | solution.py:582
  102.9 1.3 %collective-permute-start.24 = (bf16[272,384]{1,0:T(8,128)(2,1)S(1)}, bf16[272,384]{1,0:T(8,128)(2,1)S(1)}, u32[]{:S(2)}, u32[]{:S(2)}) collective-permute-start(bf16[272,384]{1,0:T(8,128)(2,1)S(1)} %combine.5), channel_id=1, source_target_pairs={{8,16},{9,17},{10,18},{11,19},{12,20},{13,21},{14,22},{15,23}} | collective-permute-start | bytes 626696 | tf_op jit(solution)/shard_map/ppermute | solution.py:582
  104.2 1.3 %local.4.refs_6_ = f32[512,640]{1,0:T(8,128)S(1)} custom-call(bf16[512,640]{1,0:T(8,128)(2,1)S(1)} %get-tuple-element.82.x_ref, f32[512,128]{1,0:T(8,128)S(1)} %get-tuple-element.76.cum_ref, f32[128,512]{1,0:T(8,128)S(1)} %get-tuple-element.77.row_ref, f32[512,256]{1,0:T(8,128)S(1)} %get-tuple-element.78.score_ref.order, ...), custom_call_target="tpu_custom_call" | custom-call | flops 671088640 | bytes 2621440 | tf_op jit(solution)/shard_map/local/pallas_call | solution.py:557
  107.6 3.3 %collective-permute-done.24.refs_2_ = bf16[272,384]{1,0:T(8,128)(2,1)S(1)} collective-permute-done((bf16[272,384]{1,0:T(8,128)(2,1)S(1)}, bf16[272,384]{1,0:T(8,128)(2,1)S(1)}, u32[]{:S(2)}, u32[]{:S(2)}) %collective-permute-start.24) | collective-permute-done | bytes 208928 | tf_op jit(solution)/shard_map/ppermute | solution.py:582
  112.0 3.4 %collective-permute-start.27 = (bf16[256,384]{1,0:T(8,128)(2,1)S(1)}, bf16[256,384]{1,0:T(8,128)(2,1)S(1)}, u32[]{:S(2)}, u32[]{:S(2)}) collective-permute-start(bf16[256,384]{1,0:T(8,128)(2,1)S(1)} %get-tuple-element.94), channel_id=1, source_target_pairs={{0,4},{1,5},{2,6},{3,7},{4,0},{5,1},{6,2},{7,3},{8,12},{9,13},{10,... | collective-permute-start | bytes 589832 | tf_op jit(solution)/shard_map/ppermute | solution.py:582
  116.5 2.0 %assemble.1 = bf16[256,4096]{1,0:T(8,128)(2,1)} custom-call(s32[5]{0:T(128)S(1)} %stack.23.place.refs_14_.order, bf16[256,1024]{1,0:T(8,128)(2,1)S(1)} %get-tuple-element.80.refs_0_, bf16[256,640]{1,0:T(8,128)(2,1)S(1)} %get-tuple-element.83.refs_1_, bf16[256,384]{1,0:T(8,128)(2,1)S(1)} %get-tuple-element.91.refs_2_, ...), custom_call_target="tpu_custom_call" | custom-call | bytes 4194304 | tf_op jit(solution)/shard_map/assemble/pallas_call | solution.py:557
  (62 shorter events, 19.3 us)
Async XLA Ops:
  4.1 3.5 %collective-permute-start.4 = (bf16[64,8448]{1,0:T(8,128)(2,1)S(1)}, bf16[64,8448]{1,0:T(8,128)(2,1)S(1)}, u32[]{:S(2)}, u32[]{:S(2)}) collective-permute-start(bf16[64,8448]{1,0:T(8,128)(2,1)S(1)} %get-tuple-element.54), channel_id=1, source_target_pairs={{0,4},{1,5},{2,6},{3,7},{4,0},{5,1},{6,2},{7,3},{8,12},{9,13},{10,... | collective-permute-start | bytes 3244040 | tf_op jit(solution)/shard_map/ppermute | solution.py:582
  4.9 2.7 %collective-permute-start = (bf16[64,2048]{1,0:T(8,128)(2,1)S(1)}, bf16[64,2048]{1,0:T(8,128)(2,1)S(1)}, u32[]{:S(2)}, u32[]{:S(2)}) collective-permute-start(bf16[64,2048]{1,0:T(8,128)(2,1)S(1)} %pack_first.1.order), channel_id=1, source_target_pairs={{0,4},{1,5},{2,6},{3,7},{4,0},{5,1},{6,2},{7,3},{8,12},{9,13},{10,... | collective-permute-start | bytes 786440 | tf_op jit(solution)/shard_map/ppermute | solution.py:582
  5.0 1.3 %collective-permute-start.5 = (bf16[3,10240]{1,0:T(4,128)(2,1)S(1)}, bf16[3,10240]{1,0:T(4,128)(2,1)S(1)}, u32[]{:S(2)}, u32[]{:S(2)}) collective-permute-start(bf16[3,10240]{1,0:T(4,128)(2,1)S(1)} %get-tuple-element.55), channel_id=1, source_target_pairs={{7,15},{15,23},{23,31}} | collective-permute-start | bytes 184328 | tf_op jit(solution)/shard_map/ppermute | solution.py:582
  5.6 0.7 collective-permute-start.6
  8.7 30.6 %copy-start.5 = (f32[256]{0:T(256)S(1)}, f32[256]{0:T(256)}, u32[]{:S(2)}) copy-start(f32[256]{0:T(256)} %param.11) | copy-start | bytes 3076
  8.8 30.6 %copy-start.6 = (f32[256]{0:T(256)S(1)}, f32[256]{0:T(256)}, u32[]{:S(2)}) copy-start(f32[256]{0:T(256)} %param.12) | copy-start | bytes 3076
  8.8 30.5 %copy-start.7 = (f32[256]{0:T(256)S(1)}, f32[256]{0:T(256)}, u32[]{:S(2)}) copy-start(f32[256]{0:T(256)} %param.13) | copy-start | bytes 3076
  8.8 10.3 %collective-permute-start.7 = (bf16[128,896]{1,0:T(8,128)(2,1)S(1)}, bf16[128,896]{1,0:T(8,128)(2,1)S(1)}, u32[]{:S(2)}, u32[]{:S(2)}) collective-permute-start(bf16[128,896]{1,0:T(8,128)(2,1)S(1)} %get-tuple-element.58), channel_id=1, source_target_pairs={{0,1},{1,0},{2,3},{3,2},{4,5},{5,4},{6,7},{7,6},{8,9},{9,8},{10,11... | collective-permute-start | bytes 688136 | tf_op jit(solution)/shard_map/ppermute | solution.py:316
  9.0 21.8 %collective-permute-start.8 = (bf16[128,896]{1,0:T(8,128)(2,1)S(1)}, bf16[128,896]{1,0:T(8,128)(2,1)S(1)}, u32[]{:S(2)}, u32[]{:S(2)}) collective-permute-start(bf16[128,896]{1,0:T(8,128)(2,1)S(1)} %get-tuple-element.59), channel_id=1, source_target_pairs={{0,2},{1,3},{2,0},{3,1},{4,6},{5,7},{6,4},{7,5},{8,10},{9,11},{10,... | collective-permute-start | bytes 688136 | tf_op jit(solution)/shard_map/ppermute | solution.py:316
  14.7 24.6 %collective-permute-start.9 = (bf16[128,896]{1,0:T(8,128)(2,1)S(1)}, bf16[128,896]{1,0:T(8,128)(2,1)S(1)}, u32[]{:S(2)}, u32[]{:S(2)}) collective-permute-start(bf16[128,896]{1,0:T(8,128)(2,1)S(1)} %get-tuple-element.60), channel_id=1, source_target_pairs={{0,3},{1,2},{2,1},{3,0},{4,7},{5,6},{6,5},{7,4},{8,11},{9,10},{10,... | collective-permute-start | bytes 688136 | tf_op jit(solution)/shard_map/ppermute | solution.py:316
  15.6 34.9 %copy-start.1 = (bf16[64,20480]{1,0:T(8,128)(2,1)S(1)}, bf16[64,20480]{1,0:T(8,128)(2,1)}, u32[]{:S(2)}) copy-start(bf16[64,20480]{1,0:T(8,128)(2,1)} %xbc.11) | copy-start | bytes 7864324
  15.7 25.4 %collective-permute-start.1 = (bf16[128,512]{1,0:T(8,128)(2,1)S(1)}, bf16[128,512]{1,0:T(8,128)(2,1)S(1)}, u32[]{:S(2)}, u32[]{:S(2)}) collective-permute-start(bf16[128,512]{1,0:T(8,128)(2,1)S(1)} %get-tuple-element.51), channel_id=1, source_target_pairs={{0,1},{1,0},{2,3},{3,2},{4,5},{5,4},{6,7},{7,6},{8,9},{9,8},{10,11... | collective-permute-start | bytes 393224 | tf_op jit(solution)/shard_map/ppermute | solution.py:316
  16.9 25.2 %collective-permute-start.2 = (bf16[128,512]{1,0:T(8,128)(2,1)S(1)}, bf16[128,512]{1,0:T(8,128)(2,1)S(1)}, u32[]{:S(2)}, u32[]{:S(2)}) collective-permute-start(bf16[128,512]{1,0:T(8,128)(2,1)S(1)} %get-tuple-element.52), channel_id=1, source_target_pairs={{0,2},{1,3},{2,0},{3,1},{4,6},{5,7},{6,4},{7,5},{8,10},{9,11},{10,... | collective-permute-start | bytes 393224 | tf_op jit(solution)/shard_map/ppermute | solution.py:316
  19.1 25.9 %collective-permute-start.3 = (bf16[128,512]{1,0:T(8,128)(2,1)S(1)}, bf16[128,512]{1,0:T(8,128)(2,1)S(1)}, u32[]{:S(2)}, u32[]{:S(2)}) collective-permute-start(bf16[128,512]{1,0:T(8,128)(2,1)S(1)} %get-tuple-element.53), channel_id=1, source_target_pairs={{0,3},{1,2},{2,1},{3,0},{4,7},{5,6},{6,5},{7,4},{8,11},{9,10},{10,... | collective-permute-start | bytes 393224 | tf_op jit(solution)/shard_map/ppermute | solution.py:316
  48.3 29.4 %collective-permute-start.10 = (bf16[272,1024]{1,0:T(8,128)(2,1)S(1)}, bf16[272,1024]{1,0:T(8,128)(2,1)S(1)}, u32[]{:S(2)}, u32[]{:S(2)}) collective-permute-start(bf16[272,1024]{1,0:T(8,128)(2,1)S(1)} %get-tuple-element.67.late_ref.refs_10_.order), channel_id=1, source_target_pairs={{0,8},{1,9},{2,10},{3,11},{4,12},{5,13},{6,14},{7,15},{16,24},{17,... | collective-permute-start | bytes 1671176 | tf_op jit(solution)/shard_map/ppermute | solution.py:582
  51.5 4.9 %collective-permute-start.13 = (bf16[128,896]{1,0:T(8,128)(2,1)S(1)}, bf16[128,896]{1,0:T(8,128)(2,1)S(1)}, u32[]{:S(2)}, u32[]{:S(2)}) collective-permute-start(bf16[128,896]{1,0:T(8,128)(2,1)S(1)} %get-tuple-element.70), channel_id=1, source_target_pairs={{0,1},{1,0},{2,3},{3,2},{4,5},{5,4},{6,7},{7,6},{8,9},{9,8},{10,11... | collective-permute-start | bytes 688136 | tf_op jit(solution)/shard_map/ppermute | solution.py:316
  51.5 17.6 %collective-permute-start.14 = (bf16[128,896]{1,0:T(8,128)(2,1)S(1)}, bf16[128,896]{1,0:T(8,128)(2,1)S(1)}, u32[]{:S(2)}, u32[]{:S(2)}) collective-permute-start(bf16[128,896]{1,0:T(8,128)(2,1)S(1)} %get-tuple-element.71), channel_id=1, source_target_pairs={{0,2},{1,3},{2,0},{3,1},{4,6},{5,7},{6,4},{7,5},{8,10},{9,11},{10,... | collective-permute-start | bytes 688136 | tf_op jit(solution)/shard_map/ppermute | solution.py:316
  54.9 19.1 %collective-permute-start.15 = (bf16[128,896]{1,0:T(8,128)(2,1)S(1)}, bf16[128,896]{1,0:T(8,128)(2,1)S(1)}, u32[]{:S(2)}, u32[]{:S(2)}) collective-permute-start(bf16[128,896]{1,0:T(8,128)(2,1)S(1)} %get-tuple-element.72), channel_id=1, source_target_pairs={{0,3},{1,2},{2,1},{3,0},{4,7},{5,6},{6,5},{7,4},{8,11},{9,10},{10,... | collective-permute-start | bytes 688136 | tf_op jit(solution)/shard_map/ppermute | solution.py:316
  76.5 7.7 %collective-permute-start.16 = (bf16[272,640]{1,0:T(8,128)(2,1)S(1)}, bf16[272,640]{1,0:T(8,128)(2,1)S(1)}, u32[]{:S(2)}, u32[]{:S(2)}) collective-permute-start(bf16[272,640]{1,0:T(8,128)(2,1)S(1)} %get-tuple-element.73.refs_8_.late_ref.refs_10_.order), channel_id=1, source_target_pairs={{0,8},{1,9},{2,10},{3,11},{4,12},{5,13},{6,14},{7,15},{16,24},{17,... | collective-permute-start | bytes 1044488 | tf_op jit(solution)/shard_map/ppermute | solution.py:582
  78.0 20.3 %collective-permute-start.11 = (bf16[272,1024]{1,0:T(8,128)(2,1)S(1)}, bf16[272,1024]{1,0:T(8,128)(2,1)S(1)}, u32[]{:S(2)}, u32[]{:S(2)}) collective-permute-start(bf16[272,1024]{1,0:T(8,128)(2,1)S(1)} %combine.3), channel_id=1, source_target_pairs={{8,24},{9,25},{10,26},{11,27},{12,28},{13,29},{14,30},{15,31}} | collective-permute-start | bytes 1671176 | tf_op jit(solution)/shard_map/ppermute | solution.py:582
  78.7 19.7 %collective-permute-start.12 = (bf16[272,1024]{1,0:T(8,128)(2,1)S(1)}, bf16[272,1024]{1,0:T(8,128)(2,1)S(1)}, u32[]{:S(2)}, u32[]{:S(2)}) collective-permute-start(bf16[272,1024]{1,0:T(8,128)(2,1)S(1)} %combine.3), channel_id=1, source_target_pairs={{8,16},{9,17},{10,18},{11,19},{12,20},{13,21},{14,22},{15,23}} | collective-permute-start | bytes 1671176 | tf_op jit(solution)/shard_map/ppermute | solution.py:582
  80.7 5.4 %collective-permute-start.19 = (bf16[128,384]{1,0:T(8,128)(2,1)S(1)}, bf16[128,384]{1,0:T(8,128)(2,1)S(1)}, u32[]{:S(2)}, u32[]{:S(2)}) collective-permute-start(bf16[128,384]{1,0:T(8,128)(2,1)S(1)} %get-tuple-element.85), channel_id=1, source_target_pairs={{0,1},{1,0},{2,3},{3,2},{4,5},{5,4},{6,7},{7,6},{8,9},{9,8},{10,11... | collective-permute-start | bytes 294920 | tf_op jit(solution)/shard_map/ppermute | solution.py:316
  80.8 6.7 %collective-permute-start.20 = (bf16[128,384]{1,0:T(8,128)(2,1)S(1)}, bf16[128,384]{1,0:T(8,128)(2,1)S(1)}, u32[]{:S(2)}, u32[]{:S(2)}) collective-permute-start(bf16[128,384]{1,0:T(8,128)(2,1)S(1)} %get-tuple-element.86), channel_id=1, source_target_pairs={{0,2},{1,3},{2,0},{3,1},{4,6},{5,7},{6,4},{7,5},{8,10},{9,11},{10,... | collective-permute-start | bytes 294920 | tf_op jit(solution)/shard_map/ppermute | solution.py:316
  84.2 8.6 %collective-permute-start.21 = (bf16[128,384]{1,0:T(8,128)(2,1)S(1)}, bf16[128,384]{1,0:T(8,128)(2,1)S(1)}, u32[]{:S(2)}, u32[]{:S(2)}) collective-permute-start(bf16[128,384]{1,0:T(8,128)(2,1)S(1)} %get-tuple-element.87), channel_id=1, source_target_pairs={{0,3},{1,2},{2,1},{3,0},{4,7},{5,6},{6,5},{7,4},{8,11},{9,10},{10,... | collective-permute-start | bytes 294920 | tf_op jit(solution)/shard_map/ppermute | solution.py:316
  86.1 19.4 %collective-permute-start.17 = (bf16[272,640]{1,0:T(8,128)(2,1)S(1)}, bf16[272,640]{1,0:T(8,128)(2,1)S(1)}, u32[]{:S(2)}, u32[]{:S(2)}) collective-permute-start(bf16[272,640]{1,0:T(8,128)(2,1)S(1)} %combine.4), channel_id=1, source_target_pairs={{8,24},{9,25},{10,26},{11,27},{12,28},{13,29},{14,30},{15,31}} | collective-permute-start | bytes 1044488 | tf_op jit(solution)/shard_map/ppermute | solution.py:582
  87.5 18.0 %collective-permute-start.18 = (bf16[272,640]{1,0:T(8,128)(2,1)S(1)}, bf16[272,640]{1,0:T(8,128)(2,1)S(1)}, u32[]{:S(2)}, u32[]{:S(2)}) collective-permute-start(bf16[272,640]{1,0:T(8,128)(2,1)S(1)} %combine.4), channel_id=1, source_target_pairs={{8,16},{9,17},{10,18},{11,19},{12,20},{13,21},{14,22},{15,23}} | collective-permute-start | bytes 1044488 | tf_op jit(solution)/shard_map/ppermute | solution.py:582
  94.7 7.4 %collective-permute-start.22 = (bf16[272,384]{1,0:T(8,128)(2,1)S(1)}, bf16[272,384]{1,0:T(8,128)(2,1)S(1)}, u32[]{:S(2)}, u32[]{:S(2)}) collective-permute-start(bf16[272,384]{1,0:T(8,128)(2,1)S(1)} %get-tuple-element.88.late_ref), channel_id=1, source_target_pairs={{0,8},{1,9},{2,10},{3,11},{4,12},{5,13},{6,14},{7,15},{16,24},{17,... | collective-permute-start | bytes 626696 | tf_op jit(solution)/shard_map/ppermute | solution.py:582
  99.9 16.6 %collective-permute-start.25 = (bf16[256,1024]{1,0:T(8,128)(2,1)S(1)}, bf16[256,1024]{1,0:T(8,128)(2,1)S(1)}, u32[]{:S(2)}, u32[]{:S(2)}) collective-permute-start(bf16[256,1024]{1,0:T(8,128)(2,1)S(1)} %get-tuple-element.92), channel_id=1, source_target_pairs={{0,4},{1,5},{2,6},{3,7},{4,0},{5,1},{6,2},{7,3},{8,12},{9,13},{10,... | collective-permute-start | bytes 1572872 | tf_op jit(solution)/shard_map/ppermute | solution.py:582
  102.2 5.4 %collective-permute-start.23 = (bf16[272,384]{1,0:T(8,128)(2,1)S(1)}, bf16[272,384]{1,0:T(8,128)(2,1)S(1)}, u32[]{:S(2)}, u32[]{:S(2)}) collective-permute-start(bf16[272,384]{1,0:T(8,128)(2,1)S(1)} %combine.5), channel_id=1, source_target_pairs={{8,24},{9,25},{10,26},{11,27},{12,28},{13,29},{14,30},{15,31}} | collective-permute-start | bytes 626696 | tf_op jit(solution)/shard_map/ppermute | solution.py:582
  102.9 8.1 %collective-permute-start.24 = (bf16[272,384]{1,0:T(8,128)(2,1)S(1)}, bf16[272,384]{1,0:T(8,128)(2,1)S(1)}, u32[]{:S(2)}, u32[]{:S(2)}) collective-permute-start(bf16[272,384]{1,0:T(8,128)(2,1)S(1)} %combine.5), channel_id=1, source_target_pairs={{8,16},{9,17},{10,18},{11,19},{12,20},{13,21},{14,22},{15,23}} | collective-permute-start | bytes 626696 | tf_op jit(solution)/shard_map/ppermute | solution.py:582
  106.8 9.7 %collective-permute-start.26 = (bf16[256,640]{1,0:T(8,128)(2,1)S(1)}, bf16[256,640]{1,0:T(8,128)(2,1)S(1)}, u32[]{:S(2)}, u32[]{:S(2)}) collective-permute-start(bf16[256,640]{1,0:T(8,128)(2,1)S(1)} %get-tuple-element.93), channel_id=1, source_target_pairs={{0,4},{1,5},{2,6},{3,7},{4,0},{5,1},{6,2},{7,3},{8,12},{9,13},{10,... | collective-permute-start | bytes 983048 | tf_op jit(solution)/shard_map/ppermute | solution.py:582
  112.0 4.5 %collective-permute-start.27 = (bf16[256,384]{1,0:T(8,128)(2,1)S(1)}, bf16[256,384]{1,0:T(8,128)(2,1)S(1)}, u32[]{:S(2)}, u32[]{:S(2)}) collective-permute-start(bf16[256,384]{1,0:T(8,128)(2,1)S(1)} %get-tuple-element.94), channel_id=1, source_target_pairs={{0,4},{1,5},{2,6},{3,7},{4,0},{5,1},{6,2},{7,3},{8,12},{9,13},{10,... | collective-permute-start | bytes 589832 | tf_op jit(solution)/shard_map/ppermute | solution.py:582
  (4 other events, 6.2 us)

commit v5 on v4

--- a/solution.py
+++ b/solution.py
@@ -163,9 +163,11 @@
 LANES = 128
 LOG2E = 1.4426950408889634
 F32, BF16 = jnp.float32, jnp.bfloat16
-WIDTHS = (512, 512, 640, 384)
-RESTS = ("", "BD", "C", "")
-JOINED = ((0, 1), (2,), (3,))
+WIDTHS = (512, 0, 768, 768)
+RESTS = ("", "BD", "", "C")
+GROUPED = ((0, 0, 512), (2, 0, 768), (3, 0, 384), (3, 384, 384))
+FIRST_ROUND = ((256, 256), (384, 384), (384,), (384,))
+SECOND_ROUND = ((512,), (384, 384), (384,), (384,))
 
 
 def halves(value, count):
@@ -210,22 +212,31 @@
 
 def pack_first_kernel(shards, place, xbc, send, sems):
     core, shard = place[2], place[4]
-    width = send.shape[1] // shards
+    count = xbc.shape[0]
+    width = WIDTHS[0]
     copies = []
     for r in range(shards):
         group = (shard ^ r) * PAIR + 1 - core
         copies.append((xbc.at[:, channels(group, 0, width)], send.at[:, r * width : (r + 1) * width]))
+        last, rows = xbc.at[count - 16 :], slice(16 * r, 16 * r + 16)
+        to = shards * width
+        copies.append((last.at[:, channels(group, width, PER_GROUP - width)], send.at[rows, to : to + PER_GROUP - width]))
+        to += PER_GROUP - width
+        for i in range(2):
+            at = ds(INNER + (i * GROUPS + group) * STATE, STATE)
+            copies.append((last.at[:, at], send.at[rows, to + i * STATE : to + (i + 1) * STATE]))
     for copy in run(copies, sems):
         copy.wait()
 
 
-def pack_kernel(shards, place, xbc, dt_raw, weight, bias, order, send, taps, offset, near, far, tail, sems):
+def pack_kernel(shards, place, xbc, dt_raw, weight, bias, order, send, taps, offset, tail, sems):
     core, shard = place[2], place[4]
     count = xbc.shape[0]
     first = WIDTHS[0]
     width = PER_GROUP - first
     rest = width * shards
-    copies = [(xbc.at[count - 16 :], tail)]
+    size = PER_GROUP + 2 * STATE
+    copies = []
     for r in range(shards):
         group = (shard ^ r) * PAIR + 1 - core
         copies.append((xbc.at[:, channels(group, first, width)], send.at[:, r * width : (r + 1) * width]))
@@ -233,57 +244,80 @@
             to = rest + (i * shards + r) * STATE
             copies.append((xbc.at[:, ds(INNER + (i * GROUPS + group) * STATE, STATE)], send.at[:, to : to + STATE]))
     copies.append((dt_raw, send.at[:, send.shape[1] - HEADS :]))
-    for source, target in ((weight, taps), (bias, offset)):
-        copies.append((source.at[:, channels(place[0], 0, PER_GROUP)], target.at[:, :PER_GROUP]))
+    everything = [(weight, taps, place[0], 0), (bias, offset, place[0], 0)]
+    for r in range(shards):
+        everything.append((xbc.at[count - 16 :], tail, (shard ^ r) * PAIR + core, r * size))
+    for source, target, group, to in everything:
+        copies.append((source.at[:, channels(group, 0, PER_GROUP)], target.at[:, to : to + PER_GROUP]))
         for i in range(2):
-            to = PER_GROUP + i * STATE
-            at = ds(INNER + (i * GROUPS + place[0]) * STATE, STATE)
-            copies.append((source.at[:, at], target.at[:, to : to + STATE]))
-    started = run(copies, sems)
-    started[0].wait()
-    for edge, side in ((near, 1), (far, 0)):
-        for r in range(shards):
-            group = ((shards - 1) ^ r) * PAIR + side
-            to = r * (PER_GROUP + 2 * STATE)
-            parts = [(group * PER_GROUP, PER_GROUP)]
-            parts += [(INNER + (i * GROUPS + group) * STATE, STATE) for i in range(2)]
-            for start, size in parts:
-                edge[:, to : to + size] = tail[:, start : start + size].astype(F32)[13:16].astype(BF16)
-                to += size
-    for copy in started[1:]:
+            at = ds(INNER + (i * GROUPS + group) * STATE, STATE)
+            start = to + PER_GROUP + i * STATE
+            copies.append((source.at[:, at], target.at[:, start : start + STATE]))
+    for copy in run(copies, sems):
         copy.wait()
 
 
-def merge_kernel(shards, piece, place, xbc, dt_raw, got, near, far, order, *refs):
-    outs, sems = refs[:shards], refs[shards]
+def put_edge(shards, place, got, tail, out):
+    count = got.shape[0]
+    first = WIDTHS[0]
+    size = PER_GROUP + 2 * STATE
+    for r in range(shards):
+        theirs = [got[count - 16 :, r * first : (r + 1) * first]]
+        theirs.append(got[16 * r : 16 * r + 16, shards * first :])
+        to = r * size
+        for part in theirs:
+            at = slice(to, to + part.shape[1])
+            rows = jnp.where(place[2] == 0, part.astype(F32), tail[:, at].astype(F32))
+            out[:, at] = rows[13:16].astype(BF16)
+            to = at.stop
+
+
+def total_of(piece):
+    return WIDTHS[piece] + sum(LANES if kind == "D" else STATE for kind in RESTS[piece])
+
+
+def merge_kernel(shards, plan, unread, place, xbc, dt_raw, got_first, got, edges, *refs):
+    refs = refs[unread:]
+    outs, sems = refs[: len(plan)], refs[-1]
     core, shard = place[2], place[4]
     count = xbc.shape[0]
-    first = sum(WIDTHS[:piece])
-    width = WIDTHS[piece]
-    stride = WIDTHS[0] if piece == 0 else PER_GROUP - WIDTHS[0]
-    base = 0 if piece == 0 else first - WIDTHS[0]
+    stride = PER_GROUP - WIDTHS[0]
     mine = pl.ds(pl.multiple_of(core * count, count), count)
     other = pl.ds(pl.multiple_of((1 - core) * count, count), count)
-    copies = []
-    for r in range(shards):
+    copies, steps = [], []
+    for out, (r, pieces) in zip(outs, plan):
         group = (shard ^ r) * PAIR + core
-        copies.append((xbc.at[:, channels(group, first, width)], outs[r].at[mine, :width]))
-        at = r * stride + base
-        copies.append((got.at[:, at : at + width], outs[r].at[other, :width]))
-        to = width
-        for kind in RESTS[piece]:
-            if kind in "BC":
+        to = 0
+        for piece in pieces:
+            first, width = sum(WIDTHS[:piece]), WIDTHS[piece]
+            if piece == 0:
+                source = got_first.at[:, r * width : (r + 1) * width]
+            else:
+                at = r * stride + first - WIDTHS[0]
+                source = got.at[:, at : at + width]
+            if width:
+                copies.append((xbc.at[:, channels(group, first, width)], out.at[mine, to : to + width]))
+                copies.append((source, out.at[other, to : to + width]))
+            to += width
+            for kind in RESTS[piece]:
+                if kind == "D":
+                    steps.append((out, r, to))
+                    to += LANES
+                    continue
                 i = "BC".index(kind)
-                copies.append((xbc.at[:, ds(INNER + (i * GROUPS + group) * STATE, STATE)], outs[r].at[mine, to : to + STATE]))
+                at = ds(INNER + (i * GROUPS + group) * STATE, STATE)
+                copies.append((xbc.at[:, at], out.at[mine, to : to + STATE]))
                 at = stride * shards + (i * shards + r) * STATE
-                copies.append((got.at[:, at : at + STATE], outs[r].at[other, to : to + STATE]))
+                copies.append((got.at[:, at : at + STATE], out.at[other, to : to + STATE]))
                 to += STATE
     started = run(copies, sems)
-    if "D" in RESTS[piece]:
+    if len(refs) > len(plan) + 1:
+        put_edge(shards, place, got_first, edges, refs[-2])
+    if steps:
         lane = lax.broadcasted_iota(jnp.int32, (count, LANES), 1)
         per_tile = LANES * GROUPS // HEADS
         heads = HEADS // GROUPS
-        for r in range(shards):
+        for out, r, to in steps:
             group = (shard ^ r) * PAIR + core
             tile, shift = group // per_tile, (LANES - (group % per_tile) * heads) % LANES
             own = dt_raw[:, ds(tile * LANES, LANES)].astype(F32)
@@ -296,25 +330,15 @@
                 for i in range(2):
                     part = rows[i * count // 2 : (i + 1) * count // 2]
                     packed = packed + pltpu.roll(part, (2 * j + i) * heads, 1)
-            outs[r][: count // 2, to : to + LANES] = packed.astype(BF16)
+            out[: count // 2, to : to + LANES] = packed.astype(BF16)
             size = PER_GROUP + 2 * STATE
             at = slice(r * size, (r + 1) * size)
-            edge = near[:, at].astype(F32) + far[:, at].astype(F32)
-            edge = jnp.concatenate([edge, jnp.zeros((1, size), F32)], 0)
+            edge = jnp.concatenate([edges[:, at].astype(F32), jnp.zeros((1, size), F32)], 0)
             edge = jnp.concatenate([edge[:, q * LANES : (q + 1) * LANES] for q in range(size // LANES)], 0)
             fill = jnp.zeros((PAIR * count - count // 2 - edge.shape[0], LANES), F32)
-            outs[r][count // 2 :, to : to + LANES] = jnp.concatenate([edge, fill], 0).astype(BF16)
+            out[count // 2 :, to : to + LANES] = jnp.concatenate([edge, fill], 0).astype(BF16)
     for copy in started:
         copy.wait()
-
-
-def exchange(blocks, axes, length):
-    shards = len(blocks)
-    got = {0: blocks[0]}
-    for r in [*range(2, shards), 1]:
-        route = [(k * shards + i, k * shards + (i ^ r)) for k in range(length) for i in range(shards)]
-        got[r] = lax.ppermute(blocks[r], axes, route)
-    return [got[r] for r in range(shards)]
 
 
 def convolve_in_order(place, blocks, columns, edge, tap, bias, wide, put):
@@ -324,7 +348,8 @@
     for r, block in enumerate(blocks):
         for core in range(PAIR):
             at = pl.multiple_of((core * len(blocks) + (place[4] ^ r)) * count + 8, 8)
-            wide[pl.ds(at, count), :width] = block[core * count : (core + 1) * count, columns].astype(F32)
+            part = block[core * count : (core + 1) * count, columns]
+            wide[pl.ds(at, count), :width] = part.astype(F32)
     tap, bias = tap * 0.5, bias * 0.5
     for start in range(0, PAIR * len(blocks) * count, count):
         acc = bias + tap[0:1] * wide[start + 5 : start + 5 + count, :width]
@@ -335,20 +360,21 @@
 
 
 def prep_kernel(shards, place, *refs):
-    blocks, (taps, offset, a_ref, bias_ref, skip_ref) = refs[:shards], refs[shards : shards + 5]
-    b_ref, edge_ref, cum_ref, row_ref, factor_ref, tail_ref, skip_out, dt_ref, wide = refs[shards + 5 :]
-    start = blocks[0].shape[1] - STATE - LANES
-    last = slice(start + STATE, start + STATE + LANES)
+    blocks, (taps, offset, a_ref, bias_ref, skip_ref, order) = refs[:shards], refs[shards : shards + 6]
+    b_ref, edge_ref, cum_ref, row_ref, factor_ref, tail_ref, skip_out, dt_ref, wide = refs[shards + 6 :]
+    start = WIDTHS[1]
+    last = total_of(1) - LANES
     size = edge_ref.shape[1]
     count = blocks[0].shape[0] // PAIR
     half, heads = count // 2, HEADS // GROUPS
-    edge = blocks[0][half : half + 4 * size // LANES, last].astype(F32)
-    for block in blocks[1:]:
-        edge = edge + block[half : half + 4 * size // LANES, last].astype(F32)
+    columns = [block[:, last : last + LANES].astype(F32) for block in blocks]
+    edge = columns[0][half : half + 4 * size // LANES]
+    for column in columns[1:]:
+        edge = edge + column[half : half + 4 * size // LANES]
     for q in range(size // LANES):
         edge_ref[:, q * LANES : (q + 1) * LANES] = edge[4 * q : 4 * q + 4]
-    for r, block in enumerate(blocks):
-        packed = block[:half, last].astype(F32)
+    for r, column in enumerate(columns):
+        packed = column[:half]
         for j in range(2 * PAIR):
             at = ((j // 2) * shards + (place[4] ^ r)) * count + (j % 2) * half
             rows = packed if j == 0 else pltpu.roll(packed, LANES - j * heads, 1)
@@ -393,8 +419,9 @@
 
 
 def score_kernel(shards, place, *refs):
-    blocks, (taps, offset, edge_ref, b_ref, order, c_ref, score_ref, wide) = refs[:shards], refs[shards:]
-    start = blocks[0].shape[1] - STATE
+    blocks, refs = refs[:shards], refs[shards:]
+    taps, offset, edge_ref, b_ref, c_ref, score_ref, wide = (*refs[:4], *refs[-3:])
+    start = WIDTHS[3]
     at = slice(PER_GROUP + STATE, PER_GROUP + 2 * STATE)
 
     def put(start, count, value):
@@ -422,30 +449,19 @@
     ref[STATE:] = packed.astype(BF16)
 
 
-def state_kernel(shards, pieces, place, *refs):
-    blocks, refs = refs[: shards * len(pieces)], refs[shards * len(pieces) :]
-    taps, offset, edge_ref, b_ref, factor_ref, tail_ref, order, x_ref, send_ref, own_ref, wide = refs
-    width = x_ref.shape[1]
-    first = sum(WIDTHS[: pieces[0]])
-    start = 0
-    for i, piece in enumerate(pieces):
-        to = slice(start, start + WIDTHS[piece])
-        at = slice(first + start, first + start + WIDTHS[piece])
-        start += WIDTHS[piece]
-
-        def put(row, count, value, to=to):
-            x_ref[row : row + count, to] = value
-
-        convolve_in_order(
-            place,
-            blocks[i * shards : (i + 1) * shards],
-            slice(0, WIDTHS[piece]),
-            edge_ref[0:3, at],
-            taps[:, at],
-            offset[:, at],
-            wide,
-            put,
-        )
+def state_kernel(shards, part, sizes, place, *refs):
+    blocks, refs = refs[:shards], refs[shards:]
+    taps, offset, edge_ref, b_ref, factor_ref, tail_ref = refs[:6]
+    x_ref, own_ref, *sends, wide = refs[-3 - len(sizes) :]
+    piece, start, width = part
+    first = sum(WIDTHS[:piece]) + start
+    at = slice(first, first + width)
+
+    def put(row, count, value):
+        x_ref[row : row + count] = value
+
+    columns = slice(start, start + width)
+    convolve_in_order(place, blocks, columns, edge_ref[0:3, at], taps[:, at], offset[:, at], wide, put)
     expand = spread(first // HEAD_DIM, width, 2)
     both = []
     for block in range(PAIR):
@@ -456,17 +472,29 @@
         )
     ends = [dot(factor_ref[(i + 1) * BLOCK - 16 : (i + 1) * BLOCK], expand)[15:16] for i in range(PAIR)]
     own_ref[...] = both[0]
-    send_ref[0:STATE] = (ends[1] * both[0] + both[1]).astype(BF16)
-    put_decay(send_ref, ends[0] * ends[1])
-
-
-def combine_kernel(early_ref, late_ref, order, out_ref):
-    decay = decay_of(late_ref)
-    out_ref[:STATE] = (decay * early_ref[:STATE].astype(F32) + late_ref[:STATE].astype(F32)).astype(BF16)
-    put_decay(out_ref, decay * decay_of(early_ref))
-
-
-def local_kernel(first_head, x_ref, cum_ref, row_ref, score_ref, skip_ref, order, out_ref):
+    end = (ends[1] * both[0] + both[1]).astype(BF16)
+    decay = ends[0] * ends[1]
+    start = 0
+    for send_ref in sends:
+        at = slice(start, start + send_ref.shape[1])
+        send_ref[0:STATE] = end[:, at]
+        put_decay(send_ref, decay[:, at])
+        start = at.stop
+
+
+def combine_kernel(count, *refs):
+    early, late, out_ref = refs[:count], refs[count : 2 * count], refs[-1]
+    start = 0
+    for early_ref, late_ref in zip(early, late):
+        at = slice(start, start + late_ref.shape[1])
+        decay = decay_of(late_ref)
+        total = decay * early_ref[:STATE].astype(F32) + late_ref[:STATE].astype(F32)
+        out_ref[:STATE, at] = total.astype(BF16)
+        put_decay(out_ref.at[:, at], decay * decay_of(early_ref))
+        start = at.stop
+
+
+def mix(first_head, x_ref, cum_ref, row_ref, score_ref, skip_ref, put):
     width = x_ref.shape[1]
     half = BLOCK // 2
     expand = spread(first_head, width, 3)
@@ -495,23 +523,32 @@
                 right = jnp.exp2(diag) * score_ref[base + half : base + BLOCK, half:]
                 mixing = jnp.concatenate([left.astype(BF16), right.astype(BF16)], 1)
                 bottom = bottom + dot(mixing, own)
-            out_ref[base : base + half, columns] = top
-            out_ref[base + half : base + BLOCK, columns] = bottom
-
-
-def final_kernel(first_head, place, *refs):
-    last, before, alone, own_ref, c_ref, factor_ref, partial_ref, keep_ref, send_ref = refs
-    width = own_ref.shape[1]
-    core = place[2]
-    expand = spread(first_head, width, 2)
+            put(block, slice(base, base + half), columns, top)
+            put(block, slice(base + half, base + BLOCK), columns, bottom)
+
+
+def local_kernel(first_head, x_ref, cum_ref, row_ref, score_ref, skip_ref, *refs):
+    out_ref = refs[-1]
+
+    def put(block, rows, columns, value):
+        out_ref[rows, columns] = value
+
+    mix(first_head, x_ref, cum_ref, row_ref, score_ref, skip_ref, put)
+
+
+def carry(first_head, core, lasts, befores, own_ref, c_ref, factor_ref, add, keep_ref, send_ref):
+    expand = spread(first_head, own_ref.shape[1], 2)
+    last, before = (
+        refs[0][...] if len(refs) == 1 else jnp.concatenate([ref[...] for ref in refs], 1)
+        for refs in (lasts, befores)
+    )
     held = last[:STATE].astype(F32) + decay_of(last) * before[:STATE].astype(F32)
-    held = held + alone[:STATE].astype(F32)
     factor = dot(factor_ref[...], expand)
     outs = []
     for block in range(PAIR):
         at = slice(block * BLOCK, (block + 1) * BLOCK)
         carried = dot(c_ref[at], held.astype(BF16))
-        outs.append((partial_ref[at] + factor[at] * carried).astype(BF16))
+        outs.append((add[at] + factor[at] * carried).astype(BF16))
         held = factor[BLOCK - 1 : BLOCK] * held + own_ref[...]
 
     @pl.when(core == 0)
@@ -525,21 +562,47 @@
         send_ref[...] = outs[0]
 
 
-def assemble_kernel(count, place, *refs):
-    keeps, gots, out = refs[:count], refs[count : 2 * count], refs[2 * count]
+def final_kernel(first_head, lasts, befores, place, *refs):
+    last, refs = refs[:lasts], refs[lasts:]
+    before, refs = refs[:befores], refs[befores:]
+    carry(first_head, place[2], last, before, *refs[:4], *refs[-2:])
+
+
+def finish_kernel(first_head, lasts, befores, place, *refs):
+    last, refs = refs[:lasts], refs[lasts:]
+    before, refs = refs[:befores], refs[befores:]
+    own_ref, c_ref, factor_ref = refs[:3]
+    keep_ref, send_ref, partial = refs[-3:]
+    local_kernel(first_head, *refs[3:8], partial)
+    carry(first_head, place[2], last, before, own_ref, c_ref, factor_ref, partial, keep_ref, send_ref)
+
+
+def place_kernel(first, place, keep, got, *refs):
+    out, sems = refs[-2:]
     core = place[2]
+    width = keep.shape[1]
     half = out.shape[1] // PAIR
-
-    def put(own, other):
-        start = 0
-        for keep, got in zip(keeps, gots):
-            width = keep.shape[1]
-            out[:, own + start : own + start + width] = keep[...]
-            out[:, other + start : other + start + width] = got[...]
-            start += width
-
-    pl.when(core == 0)(lambda: put(0, half))
-    pl.when(core == 1)(lambda: put(half, 0))
+    copies = [
+        (keep, out.at[:, ds(core * half + first, width)]),
+        (got, out.at[:, ds((1 - core) * half + first, width)]),
+    ]
+    for copy in run(copies, sems):
+        copy.wait()
+
+
+def put_in_place(first, shape, place, keep, got, before):
+    smem, vmem, hbm = (pl.BlockSpec(memory_space=m) for m in (pltpu.SMEM, pltpu.VMEM, pltpu.HBM))
+    return pl.pallas_call(
+        functools.partial(place_kernel, first),
+        out_shape=jax.ShapeDtypeStruct(shape, BF16),
+        in_specs=[smem, vmem, vmem] + [hbm] * len(before),
+        out_specs=hbm,
+        input_output_aliases={3: 0} if before else {},
+        scratch_shapes=[pltpu.SemaphoreType.DMA((2,))],
+        compiler_params=pltpu.CompilerParams(vmem_limit_bytes=16 << 20),
+        cost_estimate=pl.CostEstimate(flops=1, bytes_accessed=1, transcendentals=0),
+        name="place",
+    )(place, keep, got, *before)
 
 
 class Stay:
@@ -547,7 +610,7 @@
         self.array = array
 
 
-def call(body, outs, operands, scratch=(), flops=0, transcendentals=0, name=None):
+def call(body, outs, operands, scratch=(), flops=0, transcendentals=0, name=None, limit=16 << 20):
     shapes = [jax.ShapeDtypeStruct(shape, dtype) for shape, dtype in outs]
     smem, vmem, hbm = (pl.BlockSpec(memory_space=m) for m in (pltpu.SMEM, pltpu.VMEM, pltpu.HBM))
     specs = [
@@ -560,8 +623,8 @@
         in_specs=specs,
         out_specs=[vmem] * len(outs),
         scratch_shapes=scratch,
-        compiler_params=pltpu.CompilerParams(vmem_limit_bytes=16 << 20),
-        cost_estimate=pl.CostEstimate(flops=flops, bytes_accessed=moved, transcendentals=transcendentals),
+        compiler_params=pltpu.CompilerParams(vmem_limit_bytes=limit),
+        cost_estimate=pl.CostEstimate(flops=1, bytes_accessed=1, transcendentals=0),
         name=name,
     )(*[o.array if isinstance(o, Stay) else o for o in operands])
 
@@ -585,51 +648,64 @@
         return over(block, lambda i: i ^ shards)
 
     rows = Stay(xbc)
+    size = PER_GROUP + 2 * STATE
     (sent,) = call(
         functools.partial(pack_first_kernel, shards),
-        [((tok, shards * WIDTHS[0]), BF16)],
+        [((tok, shards * WIDTHS[0] + size - WIDTHS[0]), BF16)],
         [place, rows],
-        scratch=[pltpu.SemaphoreType.DMA((shards,))],
+        scratch=[pltpu.SemaphoreType.DMA((4 * shards,))],
         name="pack_first",
+        limit=None,
     )
     got_first = swap(sent)
-    size = PER_GROUP + 2 * STATE
-    sent, taps, offset, near, far = call(
+    sent, taps, offset, tail = call(
         functools.partial(pack_kernel, shards),
         [
             ((tok, shards * (size - WIDTHS[0]) + HEADS), BF16),
             ((4, size), F32),
             ((1, size), F32),
-            ((3, shards * size), BF16),
-            ((3, shards * size), BF16),
+            ((16, shards * size), BF16),
         ],
         [place, rows, Stay(dt_raw), Stay(conv_weight), Stay(conv_bias[None]), Stay(sent)],
-        scratch=[pltpu.VMEM((16, xbc.shape[1]), BF16), pltpu.SemaphoreType.DMA((3 * shards + 8,))],
+        scratch=[pltpu.SemaphoreType.DMA((6 * shards + 7,))],
         name="pack",
-    )
-    near = over(near, lambda i: i + peers if i % peers == peers - 1 else None)
-    far = over(far, lambda i: i + shards if i % peers == peers - 1 else None)
+        limit=None,
+    )
     got_rest = swap(sent)
 
-    received, order = [], place
-    for piece, (width, rest) in enumerate(zip(WIDTHS, RESTS)):
-        total = width + sum(LANES if kind == "D" else STATE for kind in rest)
-        blocks = call(
-            functools.partial(merge_kernel, shards, piece),
-            [((PAIR * tok, total), BF16)] * shards,
+    def send_on(piece, order, edges=None):
+        unused = Stay(got_first)
+        plan = [(r, (piece,)) for r in range(shards)]
+        made = [((3, shards * size), BF16)] if piece == 0 else []
+        return call(
+            functools.partial(merge_kernel, shards, plan, len(order)),
+            [((PAIR * tok, total_of(piece)), BF16)] * shards + made,
             [
                 place,
                 rows,
-                dt_raw if "D" in rest else Stay(dt_raw),
-                got_rest if piece else got_first,
-                near if "D" in rest else Stay(got_first),
-                far if "D" in rest else Stay(got_first),
-                Stay(received[piece - 2][2] if piece > 1 else got_first),
-            ],
-            scratch=[pltpu.SemaphoreType.DMA((2 * shards * (1 + len(rest)),))],
+                dt_raw if piece == 1 else Stay(dt_raw),
+                got_first if piece == 0 else unused,
+                unused if piece == 0 else got_rest,
+                unused if edges is None else edges,
+            ]
+            + [Stay(o) for o in order],
+            scratch=[pltpu.SemaphoreType.DMA((2 * shards * (1 + len(RESTS[piece])),))],
             name="merge",
         )
-        received.append(exchange(blocks, axes, length))
+
+    def travel(blocks):
+        got = [blocks[0]]
+        for r in range(1, shards):
+            got.append(over(blocks[r], lambda i, r=r: i ^ r))
+        return got
+
+    *first_blocks, edges = send_on(0, [], tail)
+    message = {0: travel(first_blocks)}
+    edges = over(edges, lambda i: i + peers if i % shards == shards - 1 else None)
+    second_blocks = send_on(1, [first_blocks[0], message[0][1]], edges)
+    message[1] = travel(second_blocks)
+    third_blocks = send_on(2, [second_blocks[0], *message[0][2:]])
+    message[2] = travel(third_blocks)
 
     tiles = [p.reshape(HEADS // LANES, LANES) for p in (a_log, dt_bias, skip_gain)]
     b, edge, cum, row, factor, tail, skip = call(
@@ -643,73 +719,94 @@
             ((slab, 2 * LANES), BF16),
             ((16, 3 * LANES), BF16),
         ],
-        [place] + received[1] + [taps, offset] + tiles,
+        [place] + message[1] + [taps, offset] + tiles + [Stay(third_blocks[0])],
         scratch=[pltpu.VMEM((slab, LANES), F32), pltpu.VMEM((slab + 8, STATE), F32)],
-        flops=2 * slab * BLOCK * 3 * LANES,
-        transcendentals=slab * STATE,
         name="prep",
     )
-    pieces, order = [], place
-    for joined in JOINED:
-        width = sum(WIDTHS[piece] for piece in joined)
-        x, sent, own = call(
-            functools.partial(state_kernel, shards, joined),
-            [((slab, width), BF16), ((STATE + 16, width), BF16), ((STATE, width), F32)],
-            [place]
-            + [block for piece in joined for block in received[piece]]
-            + [taps, offset, edge, b, factor, tail, Stay(order)],
-            scratch=[pltpu.VMEM((slab + 8, max(WIDTHS)), F32)],
-            flops=4 * slab * STATE * width,
-            transcendentals=slab * width,
+    count = len(GROUPED)
+    x, sent, own, last, joined, before, keep, send = ([None] * count for _ in range(8))
+
+    def first_head(i):
+        return (sum(WIDTHS[: GROUPED[i][0]]) + GROUPED[i][1]) // HEAD_DIM
+
+    def state_of(i, order):
+        piece, _, width = GROUPED[i]
+        x[i], own[i], *sent[i] = call(
+            functools.partial(state_kernel, shards, GROUPED[i], FIRST_ROUND[i]),
+            [((slab, width), BF16), ((STATE, width), F32)] + [((STATE + 16, w), BF16) for w in FIRST_ROUND[i]],
+            [place] + message[piece] + [taps, offset, edge, b, factor, tail] + [Stay(o) for o in order],
+            scratch=[pltpu.VMEM((slab + 8, width), F32)],
             name="state",
         )
-        last = over(sent, lambda i: i + peers if i // peers % 2 == 0 else None)
-        (combined,) = call(
-            combine_kernel,
-            [(sent.shape, BF16)],
-            [last, sent, Stay(order)],
-            flops=4 * sent.size,
-            name="combine",
+        last[i] = [over(part, lambda i: i + peers) for part in sent[i]]
+
+    def combine_of(i, order):
+        joined[i], before[i] = [], []
+        step = len(FIRST_ROUND[i]) // len(SECOND_ROUND[i])
+        for j, width in enumerate(SECOND_ROUND[i]):
+            early, late = last[i][j * step : (j + 1) * step], sent[i][j * step : (j + 1) * step]
+            (total,) = call(
+                functools.partial(combine_kernel, len(early)),
+                [((STATE + 16, width), BF16)],
+                early + late + [Stay(o) for o in order],
+                name="combine",
+            )
+            joined[i].append(total)
+            before[i].append(over(total, lambda i: i + 2 * peers))
+            order = [total]
+
+    def finish_of(body, i, operands, order, **more):
+        keep[i], send[i] = call(
+            functools.partial(body, first_head(i), len(last[i]), len(before[i])),
+            [((BLOCK, GROUPED[i][2]), BF16)] * 2,
+            [place, *last[i], *before[i], own[i], c, factor] + operands + [Stay(o) for o in order],
+            name="final",
+            **more,
         )
-        before = over(combined, lambda i: i + 2 * peers if i // peers == 1 else None)
-        alone = over(combined, lambda i: i + peers if i // peers == 1 else None)
-        pieces.append((sum(WIDTHS[: joined[0]]) // HEAD_DIM, width, [last, before, alone], own, x, sent))
-        order = sent
+
+    state_of(0, [])
+    combine_of(0, [])
+    fourth_blocks = send_on(3, [joined[0][0]])
+    message[3] = travel(fourth_blocks)
+    state_of(1, [fourth_blocks[0]])
+    combine_of(1, [])
+    state_of(2, joined[1])
+    state_of(3, sent[2])
     c, score = call(
         functools.partial(score_kernel, shards),
         [((slab, STATE), BF16), ((slab, BLOCK), F32)],
-        [place] + received[2] + [taps, offset, edge, b, Stay(pieces[1][5])],
+        [place] + message[3] + [taps, offset, edge, b] + [Stay(o) for o in sent[3] + before[1]],
         scratch=[pltpu.VMEM((slab + 8, STATE), F32)],
-        flops=2 * slab * BLOCK * STATE,
-        transcendentals=slab * STATE,
         name="score",
     )
-    keeps, gots = [], []
-    for head, width, earlier, own, x, _ in pieces:
-        (partial,) = call(
-            functools.partial(local_kernel, head),
-            [((slab, width), F32)],
-            [x, cum, row, score, skip, Stay(score)],
-            flops=8 * slab * STATE * width,
-            transcendentals=slab * BLOCK * width // HEAD_DIM,
+    mixes = [cum, row, score, skip]
+
+    def in_full(i, order):
+        wide = [pltpu.VMEM((slab, GROUPED[i][2]), F32)]
+        finish_of(finish_kernel, i, [x[i]] + mixes, order, scratch=wide)
+
+    in_full(1, [score])
+    combine_of(2, [keep[1]])
+    combine_of(3, joined[2])
+    order, partial = joined[3][0], {}
+    for i in (2, 3):
+        (partial[i],) = call(
+            functools.partial(local_kernel, first_head(i)),
+            [(x[i].shape, F32)],
+            [x[i]] + mixes + [Stay(order)],
             name="local",
         )
-        keep, send = call(
-            functools.partial(final_kernel, head),
-            [((BLOCK, width), BF16)] * 2,
-            [place] + earlier + [own, c, factor, partial],
-            flops=4 * slab * STATE * width,
-            name="final",
-        )
-        keeps.append(keep)
-        gots.append(swap(send))
-    (out,) = call(
-        functools.partial(assemble_kernel, len(keeps)),
-        [((BLOCK, PAIR * PER_GROUP), BF16)],
-        [place] + keeps + gots,
-        name="assemble",
-    )
-    return out
+        order = partial[i]
+    in_full(0, [order])
+    order = keep[0]
+    for i in (2, 3):
+        finish_of(final_kernel, i, [partial[i]], [order])
+        order = keep[i]
+    out = []
+    for i in range(count):
+        shape = (BLOCK, PAIR * PER_GROUP)
+        out = [put_in_place(first_head(i) * HEAD_DIM, shape, place, keep[i], swap(send[i]), out)]
+    return out[0]
 
 
 def solution(mesh):

time: 121 us -> 122 us (level)
  waiting for transfers between devices: 51.5 us -> 19.5 us
  starting transfers between devices: 38.1 us -> 63.7 us
  Pallas kernels: 26.4 us -> 35.2 us
    ppermute x12 -> x0, waiting for transfers between devices: 45.8 us -> none  [exchange(): got[r] = lax.ppermute(blocks[r], axes, route)]
    ppermute x16 -> x30, starting transfers between devices: 18.8 us -> 63.7 us  [over(): lax.ppermute(block, axes, [(i, j) for i, j in route if j is not None and...]
    ppermute x12 -> x0, starting transfers between devices: 19.3 us -> none  [exchange(): got[r] = lax.ppermute(blocks[r], axes, route)]
    ppermute x16 -> x30, waiting for transfers between devices: 5.68 us -> 19.5 us  [over(): lax.ppermute(block, axes, [(i, j) for i, j in route if j is not None and...]
    pallas_call x0 -> x4, Pallas kernels: none -> 5.41 us  [put_in_place(): pl.pallas_call(functools.partial(place_kernel, first), out_shape=jax.Shap...]
    pallas_call x21 -> x23, Pallas kernels: 26.4 us -> 29.8 us  [call(): pl.pallas_call(body, out_shape=shapes, in_specs=specs, out_specs=[vmem] *...]
  transfers between devices with their start and end apart: 28 -> 30, of which waited for: 12 -> 9; matrix products, arithmetic and copies ran while one was open for 0% -> 0% of each run, Pallas kernels for 15% -> 23%
where the time goes in v5:
time: 122 us; the launch traced here: 121 us
  starting transfers between devices  63.7 us (52%)
  Pallas kernels  35.2 us (29%)
  waiting for transfers between devices  19.5 us (16%)
  local copies, waits for them, and re-layouts  1.61 us (1%)
    ppermute x30, starting transfers between devices, over(): lax.ppermute(block, axes, [(i, j) for i, j in route if j is not None and...  63.7 us
    pallas_call x23, Pallas kernels, call(): pl.pallas_call(body, out_shape=shapes, in_specs=specs, out_specs=[vmem] *...  29.8 us
    ppermute x30, waiting for transfers between devices, over(): lax.ppermute(block, axes, [(i, j) for i, j in route if j is not None and...  19.5 us
    pallas_call x4, Pallas kernels, put_in_place(): pl.pallas_call(functools.partial(place_kernel, first), out_shape=jax.Shap...  5.41 us
  transfers between devices with their start and end apart: 30, of which 9 were waited for; matrix products, arithmetic and copies ran while one was open for 0% of the time, Pallas kernels for 23%

profile of v5, /device:TPU:13, one launch (start us, length us, event | category | flops | bytes accessed | tf_op | source)
XLA Modules:
  0.0 120.6 jit_solution(8661974378719279008)
XLA Ops:
  0.6 2.7 %pack_first.1.order = bf16[64,4096]{1,0:T(8,128)(2,1)} custom-call(s32[5]{0:T(128)} %stack.23.place, bf16[64,20480]{1,0:T(8,128)(2,1)} %xbc.11), custom_call_target="tpu_custom_call" | custom-call | flops 1 | bytes 1 | tf_op jit(solution)/shard_map/pack_first/pallas_call | solution.py:620
  3.4 3.7 %pack.1 = (bf16[64,8448]{1,0:T(8,128)(2,1)}, f32[4,2560]{1,0:T(4,128)}, f32[1,2560]{1,0:T(1,128)}, bf16[16,10240]{1,0:T(8,128)(2,1)}) custom-call(s32[5]{0:T(128)} %stack.23.place, bf16[64,20480]{1,0:T(8,128)(2,1)} %xbc.11, bf16[64,256]{1,0:T(8,128)(2,1)} %dt_raw.9, f32[4,20480]{1,0:T(4,128)} %weight.1, f32[1,20480]{1,0:T(1,128)} %bitcast.12, ...), custom_call_target="tpu_custom_call" | custom-call | flops 1 | bytes 1 | tf_op jit(solution)/shard_map/pack/pallas_call | solution.py:620
  7.9 3.0 %collective-permute-done.got_first.got.edges = bf16[64,4096]{1,0:T(8,128)(2,1)S(1)} collective-permute-done((bf16[64,4096]{1,0:T(8,128)(2,1)S(1)}, bf16[64,4096]{1,0:T(8,128)(2,1)S(1)}, u32[]{:S(2)}, u32[]{:S(2)}) %collective-permute-start) | collective-permute-done | bytes 524320 | tf_op jit(solution)/shard_map/ppermute | solution.py:645
  12.9 2.3 %collective-permute-start.3 = (bf16[128,512]{1,0:T(8,128)(2,1)S(1)}, bf16[128,512]{1,0:T(8,128)(2,1)S(1)}, u32[]{:S(2)}, u32[]{:S(2)}) collective-permute-start(bf16[128,512]{1,0:T(8,128)(2,1)S(1)} %get-tuple-element.61), channel_id=1, source_target_pairs={{0,2},{1,3},{2,0},{3,1},{4,6},{5,7},{6,4},{7,5},{8,10},{9,11},{10,... | collective-permute-start | bytes 393224 | tf_op jit(solution)/shard_map/ppermute | solution.py:645
  16.0 1.4 %collective-permute-done.2.refs_1_ = bf16[128,512]{1,0:T(8,128)(2,1)S(1)} collective-permute-done((bf16[128,512]{1,0:T(8,128)(2,1)S(1)}, bf16[128,512]{1,0:T(8,128)(2,1)S(1)}, u32[]{:S(2)}, u32[]{:S(2)}) %collective-permute-start.2) | collective-permute-done | bytes 131104 | tf_op jit(solution)/shard_map/ppermute | solution.py:645
  18.7 7.4 %collective-permute-start.7 = (bf16[128,384]{1,0:T(8,128)(2,1)S(1)}, bf16[128,384]{1,0:T(8,128)(2,1)S(1)}, u32[]{:S(2)}, u32[]{:S(2)}) collective-permute-start(bf16[128,384]{1,0:T(8,128)(2,1)S(1)} %get-tuple-element.68), channel_id=1, source_target_pairs={{0,2},{1,3},{2,0},{3,1},{4,6},{5,7},{6,4},{7,5},{8,10},{9,11},{10,... | collective-permute-start | bytes 294920 | tf_op jit(solution)/shard_map/ppermute | solution.py:645
  28.4 2.1 %collective-permute-start.15 = (bf16[128,768]{1,0:T(8,128)(2,1)S(1)}, bf16[128,768]{1,0:T(8,128)(2,1)S(1)}, u32[]{:S(2)}, u32[]{:S(2)}) collective-permute-start(bf16[128,768]{1,0:T(8,128)(2,1)S(1)} %get-tuple-element.82), channel_id=1, source_target_pairs={{0,2},{1,3},{2,0},{3,1},{4,6},{5,7},{6,4},{7,5},{8,10},{9,11},{10,... | collective-permute-start | bytes 589832 | tf_op jit(solution)/shard_map/ppermute | solution.py:645
  30.8 3.0 %collective-permute-done.8.refs_3_ = bf16[128,384]{1,0:T(8,128)(2,1)S(1)} collective-permute-done((bf16[128,384]{1,0:T(8,128)(2,1)S(1)}, bf16[128,384]{1,0:T(8,128)(2,1)S(1)}, u32[]{:S(2)}, u32[]{:S(2)}) %collective-permute-start.8) | collective-permute-done | bytes 98336 | tf_op jit(solution)/shard_map/ppermute | solution.py:645
  33.8 1.7 %prep.1 = (bf16[512,256]{1,0:T(8,128)(2,1)S(1)}, f32[4,2560]{1,0:T(4,128)S(1)}, f32[512,128]{1,0:T(8,128)S(1)}, f32[128,512]{1,0:T(8,128)S(1)}, bf16[512,256]{1,...) custom-call(s32[5]{0:T(128)S(1)} %copy-done.5, ...), custom_call_target="tpu_custom_call" | custom-call | flops 1 | bytes 1 | tf_op jit(solution)/shard_map/prep/pallas_call | solution.py:620
  35.5 2.1 %state.4 = (bf16[512,512]{1,0:T(8,128)(2,1)S(1)}, f32[256,512]{1,0:T(8,128)S(1)}, bf16[272,256]{1,0:T(8,128)(2,1)S(1)}, bf16[272,256]{1,0:T(8,128)(2,1)S(1)}) custom-call(s32[5]{0:T(128)S(1)} %copy-done.5, bf16[128,512]{1,0:T(8,128)(2,1)S(1)} %get-tuple-element.59.refs_0_, bf16[128,512]{1,0:T(8,128)(2,1)S(1)} %collective-permute-done.2.refs_1_, ...), custom_call_target="tpu_custom_call" | custom-call | flops 1 | bytes 1 | tf_op jit(solution)/shard_map/state/pallas_call | solution.py:620
  37.6 6.8 %collective-permute-start.10 = (bf16[272,256]{1,0:T(8,128)(2,1)S(1)}, bf16[272,256]{1,0:T(8,128)(2,1)S(1)}, u32[]{:S(2)}, u32[]{:S(2)}) collective-permute-start(bf16[272,256]{1,0:T(8,128)(2,1)S(1)} %get-tuple-element.76.refs_3_), channel_id=1, source_target_pairs={{0,8},{1,9},{2,10},{3,11},{4,12},{5,13},{6,14},{7,15},{8,16},{9,17... | collective-permute-start | bytes 417800 | tf_op jit(solution)/shard_map/ppermute | solution.py:645
  44.4 1.9 %collective-permute-start.9 = (bf16[272,256]{1,0:T(8,128)(2,1)S(1)}, bf16[272,256]{1,0:T(8,128)(2,1)S(1)}, u32[]{:S(2)}, u32[]{:S(2)}) collective-permute-start(bf16[272,256]{1,0:T(8,128)(2,1)S(1)} %get-tuple-element.75.refs_2_), channel_id=1, source_target_pairs={{0,8},{1,9},{2,10},{3,11},{4,12},{5,13},{6,14},{7,15},{8,16},{9,17... | collective-permute-start | bytes 417800 | tf_op jit(solution)/shard_map/ppermute | solution.py:645
  46.8 4.3 %collective-permute-done.9.refs_0_ = bf16[272,256]{1,0:T(8,128)(2,1)S(1)} collective-permute-done((bf16[272,256]{1,0:T(8,128)(2,1)S(1)}, bf16[272,256]{1,0:T(8,128)(2,1)S(1)}, u32[]{:S(2)}, u32[]{:S(2)}) %collective-permute-start.9) | collective-permute-done | bytes 139296 | tf_op jit(solution)/shard_map/ppermute | solution.py:645
  52.2 3.0 %collective-permute-start.12 = (bf16[128,1024]{1,0:T(8,128)(2,1)S(1)}, bf16[128,1024]{1,0:T(8,128)(2,1)S(1)}, u32[]{:S(2)}, u32[]{:S(2)}) collective-permute-start(bf16[128,1024]{1,0:T(8,128)(2,1)S(1)} %get-tuple-element.79), channel_id=1, source_target_pairs={{0,2},{1,3},{2,0},{3,1},{4,6},{5,7},{6,4},{7,5},{8,10},{9,11},{10,... | collective-permute-start | bytes 786440 | tf_op jit(solution)/shard_map/ppermute | solution.py:645
  55.2 2.6 %state.5 = (bf16[512,768]{1,0:T(8,128)(2,1)S(1)}, f32[256,768]{1,0:T(8,128)S(1)}, bf16[272,384]{1,0:T(8,128)(2,1)S(1)}, bf16[272,384]{1,0:T(8,128)(2,1)S(1)}) custom-call(s32[5]{0:T(128)S(1)} %copy-done.5, bf16[128,768]{1,0:T(8,128)(2,1)S(1)} %get-tuple-element.70.refs_9_.refs_0_, bf16[128,768]{1,0:T(8,128)(2,1)S(1)} %collective-permute-done.14.refs_1_, ...), custom_call_target="tpu_custom_call" | custom-call | flops 1 | bytes 1 | tf_op jit(solution)/shard_map/state/pallas_call | solution.py:620
  57.8 1.9 %collective-permute-start.17 = (bf16[272,384]{1,0:T(8,128)(2,1)S(1)}, bf16[272,384]{1,0:T(8,128)(2,1)S(1)}, u32[]{:S(2)}, u32[]{:S(2)}) collective-permute-start(bf16[272,384]{1,0:T(8,128)(2,1)S(1)} %get-tuple-element.84.refs_1_), channel_id=1, source_target_pairs={{0,8},{1,9},{2,10},{3,11},{4,12},{5,13},{6,14},{7,15},{8,16},{9,17... | collective-permute-start | bytes 626696 | tf_op jit(solution)/shard_map/ppermute | solution.py:645
  59.8 1.9 %collective-permute-start.18 = (bf16[272,384]{1,0:T(8,128)(2,1)S(1)}, bf16[272,384]{1,0:T(8,128)(2,1)S(1)}, u32[]{:S(2)}, u32[]{:S(2)}) collective-permute-start(bf16[272,384]{1,0:T(8,128)(2,1)S(1)} %get-tuple-element.85.refs_1_), channel_id=1, source_target_pairs={{0,8},{1,9},{2,10},{3,11},{4,12},{5,13},{6,14},{7,15},{8,16},{9,17... | collective-permute-start | bytes 626696 | tf_op jit(solution)/shard_map/ppermute | solution.py:645
  61.7 3.6 %collective-permute-done.17.refs_0_ = bf16[272,384]{1,0:T(8,128)(2,1)S(1)} collective-permute-done((bf16[272,384]{1,0:T(8,128)(2,1)S(1)}, bf16[272,384]{1,0:T(8,128)(2,1)S(1)}, u32[]{:S(2)}, u32[]{:S(2)}) %collective-permute-start.17) | collective-permute-done | bytes 208928 | tf_op jit(solution)/shard_map/ppermute | solution.py:645
  65.4 2.2 %collective-permute-done.18.refs_0_.refs_1_ = bf16[272,384]{1,0:T(8,128)(2,1)S(1)} collective-permute-done((bf16[272,384]{1,0:T(8,128)(2,1)S(1)}, bf16[272,384]{1,0:T(8,128)(2,1)S(1)}, u32[]{:S(2)}, u32[]{:S(2)}) %collective-permute-start.18) | collective-permute-done | bytes 208928 | tf_op jit(solution)/shard_map/ppermute | solution.py:645
  70.2 1.9 %state.6 = (bf16[512,384]{1,0:T(8,128)(2,1)S(1)}, f32[256,384]{1,0:T(8,128)S(1)}, bf16[272,384]{1,0:T(8,128)(2,1)S(1)}) custom-call(s32[5]{0:T(128)S(1)} %copy-done.5, bf16[128,1024]{1,0:T(8,128)(2,1)S(1)} %get-tuple-element.77.refs_10_.refs_0_, bf16[128,1024]{1,0:T(8,128)(2,1)S(1)} %collective-permute-done.11.refs_1_, ...), custom_call_target="tpu_custom_call" | custom-call | flops 1 | bytes 1 | tf_op jit(solution)/shard_map/state/pallas_call | solution.py:620
  72.1 4.4 %collective-permute-start.20 = (bf16[272,384]{1,0:T(8,128)(2,1)S(1)}, bf16[272,384]{1,0:T(8,128)(2,1)S(1)}, u32[]{:S(2)}, u32[]{:S(2)}) collective-permute-start(bf16[272,384]{1,0:T(8,128)(2,1)S(1)} %get-tuple-element.86.refs_10_.refs_1_), channel_id=1, source_target_pairs={{0,8},{1,9},{2,10},{3,11},{4,12},{5,13},{6,14},{7,15},{8,16},{9,17... | collective-permute-start | bytes 626696 | tf_op jit(solution)/shard_map/ppermute | solution.py:645
  76.6 1.9 %state.7 = (bf16[512,384]{1,0:T(8,128)(2,1)S(1)}, f32[256,384]{1,0:T(8,128)S(1)}, bf16[272,384]{1,0:T(8,128)(2,1)S(1)}) custom-call(s32[5]{0:T(128)S(1)} %copy-done.5, bf16[128,1024]{1,0:T(8,128)(2,1)S(1)} %get-tuple-element.77.refs_10_.refs_0_, bf16[128,1024]{1,0:T(8,128)(2,1)S(1)} %collective-permute-done.11.refs_1_, ...), custom_call_target="tpu_custom_call" | custom-call | flops 1 | bytes 1 | tf_op jit(solution)/shard_map/state/pallas_call | solution.py:620
  78.5 1.9 %collective-permute-start.19 = (bf16[272,384]{1,0:T(8,128)(2,1)S(1)}, bf16[272,384]{1,0:T(8,128)(2,1)S(1)}, u32[]{:S(2)}, u32[]{:S(2)}) collective-permute-start(bf16[272,384]{1,0:T(8,128)(2,1)S(1)} %get-tuple-element.87.refs_8_.refs_1_), channel_id=1, source_target_pairs={{0,8},{1,9},{2,10},{3,11},{4,12},{5,13},{6,14},{7,15},{8,16},{9,17... | collective-permute-start | bytes 626696 | tf_op jit(solution)/shard_map/ppermute | solution.py:645
  80.4 1.5 %collective-permute-start.25 = (bf16[272,512]{1,0:T(8,128)(2,1)S(1)}, bf16[272,512]{1,0:T(8,128)(2,1)S(1)}, u32[]{:S(2)}, u32[]{:S(2)}) collective-permute-start(bf16[272,512]{1,0:T(8,128)(2,1)S(1)} %combine.5.refs_0_), channel_id=1, source_target_pairs={{0,16},{1,17},{2,18},{3,19},{4,20},{5,21},{6,22},{7,23},{8,24},{9,... | collective-permute-start | bytes 835592 | tf_op jit(solution)/shard_map/ppermute | solution.py:645
  84.2 2.6 %final.4 = (bf16[256,768]{1,0:T(8,128)(2,1)S(1)}, bf16[256,768]{1,0:T(8,128)(2,1)S(1)}) custom-call(s32[5]{0:T(128)S(1)} %copy-done.5, bf16[272,384]{1,0:T(8,128)(2,1)S(1)} %collective-permute-done.17.refs_0_, bf16[272,384]{1,0:T(8,128)(2,1)S(1)} %collective-permute-done.18.refs_0_.refs_1_, bf16[272,384]{1,0:T(8,128)(2,1)S(1)} %collective-permute-done.21.refs_9_.refs_2_, ...), custom_call_target="tpu_custom_call" | custom-call | flops 1 | bytes 1 | tf_op jit(solution)/shard_map/final/pallas_call | solution.py:620
  89.6 17.1 %collective-permute-start.28 = (bf16[256,768]{1,0:T(8,128)(2,1)S(1)}, bf16[256,768]{1,0:T(8,128)(2,1)S(1)}, u32[]{:S(2)}, u32[]{:S(2)}) collective-permute-start(bf16[256,768]{1,0:T(8,128)(2,1)S(1)} %get-tuple-element.107), channel_id=1, source_target_pairs={{0,4},{1,5},{2,6},{3,7},{4,0},{5,1},{6,2},{7,3},{8,12},{9,13},{10,... | collective-permute-start | bytes 1179656 | tf_op jit(solution)/shard_map/ppermute | solution.py:645
  108.3 1.9 %final.5 = (bf16[256,512]{1,0:T(8,128)(2,1)S(1)}, bf16[256,512]{1,0:T(8,128)(2,1)S(1)}) custom-call(s32[5]{0:T(128)S(1)} %copy-done.5, bf16[272,256]{1,0:T(8,128)(2,1)S(1)} %collective-permute-done.9.refs_0_, bf16[272,256]{1,0:T(8,128)(2,1)S(1)} %collective-permute-done.10.refs_1_, bf16[272,512]{1,0:T(8,128)(2,1)S(1)} %collective-permute-done.25.refs_2_, ...), custom_call_target="tpu_custom_call" | custom-call | flops 1 | bytes 1 | tf_op jit(solution)/shard_map/final/pallas_call | solution.py:620
  111.4 1.4 %collective-permute-start.27 = (bf16[256,384]{1,0:T(8,128)(2,1)S(1)}, bf16[256,384]{1,0:T(8,128)(2,1)S(1)}, u32[]{:S(2)}, u32[]{:S(2)}) collective-permute-start(bf16[256,384]{1,0:T(8,128)(2,1)S(1)} %get-tuple-element.106), channel_id=1, source_target_pairs={{0,4},{1,5},{2,6},{3,7},{4,0},{5,1},{6,2},{7,3},{8,12},{9,13},{10,... | collective-permute-start | bytes 589832 | tf_op jit(solution)/shard_map/ppermute | solution.py:645
  115.0 1.4 %place.4.refs_0_ = bf16[256,4096]{1,0:T(8,128)(2,1)} custom-call(s32[5]{0:T(128)S(1)} %copy-done.5, bf16[256,512]{1,0:T(8,128)(2,1)S(1)} %get-tuple-element.102.refs_6_.keep, bf16[256,512]{1,0:T(8,128)(2,1)S(1)} %collective-permute-done.29.got), custom_call_target="tpu_custom_call" | custom-call | flops 1 | bytes 1 | tf_op jit(solution)/shard_map/place/pallas_call | solution.py:595
  116.4 1.4 %place.5.refs_0_ = bf16[256,4096]{1,0:T(8,128)(2,1)} custom-call(s32[5]{0:T(128)S(1)} %copy-done.5, bf16[256,768]{1,0:T(8,128)(2,1)S(1)} %get-tuple-element.95.refs_2_.keep, bf16[256,768]{1,0:T(8,128)(2,1)S(1)} %collective-permute-done.28.got, bf16[256,4096]{1,0:T(8,128)(2,1)} %place.4.refs_0_), custom_call_target="tpu_custom_call", output_to_operand_aliasing={{}: (3, {})} | custom-call | flops 1 | bytes 1 | tf_op jit(solution)/shard_map/place/pallas_call | solution.py:595
  117.8 1.3 %place.6.refs_0_ = bf16[256,4096]{1,0:T(8,128)(2,1)} custom-call(s32[5]{0:T(128)S(1)} %copy-done.5, bf16[256,384]{1,0:T(8,128)(2,1)S(1)} %get-tuple-element.103.refs_6_.keep, bf16[256,384]{1,0:T(8,128)(2,1)S(1)} %collective-permute-done.27.got, bf16[256,4096]{1,0:T(8,128)(2,1)} %place.5.refs_0_), custom_call_target="tpu_custom_call", output_to_operand_aliasing={{}: (3, {})} | custom-call | flops 1 | bytes 1 | tf_op jit(solution)/shard_map/place/pallas_call | solution.py:595
  119.2 1.3 %place.7 = bf16[256,4096]{1,0:T(8,128)(2,1)} custom-call(s32[5]{0:T(128)S(1)} %copy-done.5, bf16[256,384]{1,0:T(8,128)(2,1)S(1)} %get-tuple-element.104.keep, bf16[256,384]{1,0:T(8,128)(2,1)S(1)} %collective-permute-done.26.got, bf16[256,4096]{1,0:T(8,128)(2,1)} %place.6.refs_0_), custom_call_target="tpu_custom_call", output_to_operand_aliasing={{}: (3, {})} | custom-call | flops 1 | bytes 1 | tf_op jit(solution)/shard_map/place/pallas_call | solution.py:595
  (76 shorter events, 22.4 us)
Async XLA Ops:
  3.3 7.5 %copy-start = (bf16[64,20480]{1,0:T(8,128)(2,1)S(1)}, bf16[64,20480]{1,0:T(8,128)(2,1)}, u32[]{:S(2)}) copy-start(bf16[64,20480]{1,0:T(8,128)(2,1)} %xbc.11) | copy-start | bytes 7864324
  3.3 7.5 %copy-start.2 = (bf16[64,256]{1,0:T(8,128)(2,1)S(1)}, bf16[64,256]{1,0:T(8,128)(2,1)}, u32[]{:S(2)}) copy-start(bf16[64,256]{1,0:T(8,128)(2,1)} %dt_raw.9) | copy-start | bytes 98308
  7.0 10.4 %collective-permute-start.1 = (bf16[64,8448]{1,0:T(8,128)(2,1)}, bf16[64,8448]{1,0:T(8,128)(2,1)S(1)}, u32[]{:S(2)}, u32[]{:S(2)}) collective-permute-start(bf16[64,8448]{1,0:T(8,128)(2,1)} %get-tuple-element.57), channel_id=1, source_target_pairs={{0,4},{1,5},{2,6},{3,7},{4,0},{5,1},{6,2},{7,3},{8,12},{9,13},{10,... | collective-permute-start | bytes 3244040 | tf_op jit(solution)/shard_map/ppermute | solution.py:645
  7.8 3.1 %collective-permute-start = (bf16[64,4096]{1,0:T(8,128)(2,1)S(1)}, bf16[64,4096]{1,0:T(8,128)(2,1)S(1)}, u32[]{:S(2)}, u32[]{:S(2)}) collective-permute-start(bf16[64,4096]{1,0:T(8,128)(2,1)S(1)} %copy-done.9), channel_id=1, source_target_pairs={{0,4},{1,5},{2,6},{3,7},{4,0},{5,1},{6,2},{7,3},{8,12},{9,13},{10,... | collective-permute-start | bytes 1572872 | tf_op jit(solution)/shard_map/ppermute | solution.py:645
  12.6 4.8 %collective-permute-start.2 = (bf16[128,512]{1,0:T(8,128)(2,1)S(1)}, bf16[128,512]{1,0:T(8,128)(2,1)S(1)}, u32[]{:S(2)}, u32[]{:S(2)}) collective-permute-start(bf16[128,512]{1,0:T(8,128)(2,1)S(1)} %get-tuple-element.60), channel_id=1, source_target_pairs={{0,1},{1,0},{2,3},{3,2},{4,5},{5,4},{6,7},{7,6},{8,9},{9,8},{10,11... | collective-permute-start | bytes 393224 | tf_op jit(solution)/shard_map/ppermute | solution.py:645
  12.9 13.5 %collective-permute-start.3 = (bf16[128,512]{1,0:T(8,128)(2,1)S(1)}, bf16[128,512]{1,0:T(8,128)(2,1)S(1)}, u32[]{:S(2)}, u32[]{:S(2)}) collective-permute-start(bf16[128,512]{1,0:T(8,128)(2,1)S(1)} %get-tuple-element.61), channel_id=1, source_target_pairs={{0,2},{1,3},{2,0},{3,1},{4,6},{5,7},{6,4},{7,5},{8,10},{9,11},{10,... | collective-permute-start | bytes 393224 | tf_op jit(solution)/shard_map/ppermute | solution.py:645
  15.2 11.6 %collective-permute-start.4 = (bf16[128,512]{1,0:T(8,128)(2,1)S(1)}, bf16[128,512]{1,0:T(8,128)(2,1)S(1)}, u32[]{:S(2)}, u32[]{:S(2)}) collective-permute-start(bf16[128,512]{1,0:T(8,128)(2,1)S(1)} %get-tuple-element.62), channel_id=1, source_target_pairs={{0,3},{1,2},{2,1},{3,0},{4,7},{5,6},{6,5},{7,4},{8,11},{9,10},{10,... | collective-permute-start | bytes 393224 | tf_op jit(solution)/shard_map/ppermute | solution.py:645
  15.4 0.7 collective-permute-start.5
  18.5 12.1 %collective-permute-start.6 = (bf16[128,384]{1,0:T(8,128)(2,1)S(1)}, bf16[128,384]{1,0:T(8,128)(2,1)S(1)}, u32[]{:S(2)}, u32[]{:S(2)}) collective-permute-start(bf16[128,384]{1,0:T(8,128)(2,1)S(1)} %get-tuple-element.67), channel_id=1, source_target_pairs={{0,1},{1,0},{2,3},{3,2},{4,5},{5,4},{6,7},{7,6},{8,9},{9,8},{10,11... | collective-permute-start | bytes 294920 | tf_op jit(solution)/shard_map/ppermute | solution.py:645
  18.7 12.1 %collective-permute-start.7 = (bf16[128,384]{1,0:T(8,128)(2,1)S(1)}, bf16[128,384]{1,0:T(8,128)(2,1)S(1)}, u32[]{:S(2)}, u32[]{:S(2)}) collective-permute-start(bf16[128,384]{1,0:T(8,128)(2,1)S(1)} %get-tuple-element.68), channel_id=1, source_target_pairs={{0,2},{1,3},{2,0},{3,1},{4,6},{5,7},{6,4},{7,5},{8,10},{9,11},{10,... | collective-permute-start | bytes 294920 | tf_op jit(solution)/shard_map/ppermute | solution.py:645
  26.1 7.6 %collective-permute-start.8 = (bf16[128,384]{1,0:T(8,128)(2,1)S(1)}, bf16[128,384]{1,0:T(8,128)(2,1)S(1)}, u32[]{:S(2)}, u32[]{:S(2)}) collective-permute-start(bf16[128,384]{1,0:T(8,128)(2,1)S(1)} %get-tuple-element.69), channel_id=1, source_target_pairs={{0,3},{1,2},{2,1},{3,0},{4,7},{5,6},{6,5},{7,4},{8,11},{9,10},{10,... | collective-permute-start | bytes 294920 | tf_op jit(solution)/shard_map/ppermute | solution.py:645
  27.6 27.6 %collective-permute-start.14 = (bf16[128,768]{1,0:T(8,128)(2,1)S(1)}, bf16[128,768]{1,0:T(8,128)(2,1)S(1)}, u32[]{:S(2)}, u32[]{:S(2)}) collective-permute-start(bf16[128,768]{1,0:T(8,128)(2,1)S(1)} %get-tuple-element.81), channel_id=1, source_target_pairs={{0,1},{1,0},{2,3},{3,2},{4,5},{5,4},{6,7},{7,6},{8,9},{9,8},{10,11... | collective-permute-start | bytes 589832 | tf_op jit(solution)/shard_map/ppermute | solution.py:645
  28.4 26.8 %collective-permute-start.15 = (bf16[128,768]{1,0:T(8,128)(2,1)S(1)}, bf16[128,768]{1,0:T(8,128)(2,1)S(1)}, u32[]{:S(2)}, u32[]{:S(2)}) collective-permute-start(bf16[128,768]{1,0:T(8,128)(2,1)S(1)} %get-tuple-element.82), channel_id=1, source_target_pairs={{0,2},{1,3},{2,0},{3,1},{4,6},{5,7},{6,4},{7,5},{8,10},{9,11},{10,... | collective-permute-start | bytes 589832 | tf_op jit(solution)/shard_map/ppermute | solution.py:645
  30.6 24.6 %collective-permute-start.16 = (bf16[128,768]{1,0:T(8,128)(2,1)S(1)}, bf16[128,768]{1,0:T(8,128)(2,1)S(1)}, u32[]{:S(2)}, u32[]{:S(2)}) collective-permute-start(bf16[128,768]{1,0:T(8,128)(2,1)S(1)} %get-tuple-element.83), channel_id=1, source_target_pairs={{0,3},{1,2},{2,1},{3,0},{4,7},{5,6},{6,5},{7,4},{8,11},{9,10},{10,... | collective-permute-start | bytes 589832 | tf_op jit(solution)/shard_map/ppermute | solution.py:645
  37.6 9.2 %collective-permute-start.10 = (bf16[272,256]{1,0:T(8,128)(2,1)S(1)}, bf16[272,256]{1,0:T(8,128)(2,1)S(1)}, u32[]{:S(2)}, u32[]{:S(2)}) collective-permute-start(bf16[272,256]{1,0:T(8,128)(2,1)S(1)} %get-tuple-element.76.refs_3_), channel_id=1, source_target_pairs={{0,8},{1,9},{2,10},{3,11},{4,12},{5,13},{6,14},{7,15},{8,16},{9,17... | collective-permute-start | bytes 417800 | tf_op jit(solution)/shard_map/ppermute | solution.py:645
  44.4 6.7 %collective-permute-start.9 = (bf16[272,256]{1,0:T(8,128)(2,1)S(1)}, bf16[272,256]{1,0:T(8,128)(2,1)S(1)}, u32[]{:S(2)}, u32[]{:S(2)}) collective-permute-start(bf16[272,256]{1,0:T(8,128)(2,1)S(1)} %get-tuple-element.75.refs_2_), channel_id=1, source_target_pairs={{0,8},{1,9},{2,10},{3,11},{4,12},{5,13},{6,14},{7,15},{8,16},{9,17... | collective-permute-start | bytes 417800 | tf_op jit(solution)/shard_map/ppermute | solution.py:645
  52.1 18.1 %collective-permute-start.11 = (bf16[128,1024]{1,0:T(8,128)(2,1)S(1)}, bf16[128,1024]{1,0:T(8,128)(2,1)S(1)}, u32[]{:S(2)}, u32[]{:S(2)}) collective-permute-start(bf16[128,1024]{1,0:T(8,128)(2,1)S(1)} %get-tuple-element.78), channel_id=1, source_target_pairs={{0,1},{1,0},{2,3},{3,2},{4,5},{5,4},{6,7},{7,6},{8,9},{9,8},{10,11... | collective-permute-start | bytes 786440 | tf_op jit(solution)/shard_map/ppermute | solution.py:645
  52.2 18.0 %collective-permute-start.12 = (bf16[128,1024]{1,0:T(8,128)(2,1)S(1)}, bf16[128,1024]{1,0:T(8,128)(2,1)S(1)}, u32[]{:S(2)}, u32[]{:S(2)}) collective-permute-start(bf16[128,1024]{1,0:T(8,128)(2,1)S(1)} %get-tuple-element.79), channel_id=1, source_target_pairs={{0,2},{1,3},{2,0},{3,1},{4,6},{5,7},{6,4},{7,5},{8,10},{9,11},{10,... | collective-permute-start | bytes 786440 | tf_op jit(solution)/shard_map/ppermute | solution.py:645
  55.2 15.0 %collective-permute-start.13 = (bf16[128,1024]{1,0:T(8,128)(2,1)S(1)}, bf16[128,1024]{1,0:T(8,128)(2,1)S(1)}, u32[]{:S(2)}, u32[]{:S(2)}) collective-permute-start(bf16[128,1024]{1,0:T(8,128)(2,1)S(1)} %get-tuple-element.80), channel_id=1, source_target_pairs={{0,3},{1,2},{2,1},{3,0},{4,7},{5,6},{6,5},{7,4},{8,11},{9,10},{10,... | collective-permute-start | bytes 786440 | tf_op jit(solution)/shard_map/ppermute | solution.py:645
  57.8 7.4 %collective-permute-start.17 = (bf16[272,384]{1,0:T(8,128)(2,1)S(1)}, bf16[272,384]{1,0:T(8,128)(2,1)S(1)}, u32[]{:S(2)}, u32[]{:S(2)}) collective-permute-start(bf16[272,384]{1,0:T(8,128)(2,1)S(1)} %get-tuple-element.84.refs_1_), channel_id=1, source_target_pairs={{0,8},{1,9},{2,10},{3,11},{4,12},{5,13},{6,14},{7,15},{8,16},{9,17... | collective-permute-start | bytes 626696 | tf_op jit(solution)/shard_map/ppermute | solution.py:645
  59.8 7.8 %collective-permute-start.18 = (bf16[272,384]{1,0:T(8,128)(2,1)S(1)}, bf16[272,384]{1,0:T(8,128)(2,1)S(1)}, u32[]{:S(2)}, u32[]{:S(2)}) collective-permute-start(bf16[272,384]{1,0:T(8,128)(2,1)S(1)} %get-tuple-element.85.refs_1_), channel_id=1, source_target_pairs={{0,8},{1,9},{2,10},{3,11},{4,12},{5,13},{6,14},{7,15},{8,16},{9,17... | collective-permute-start | bytes 626696 | tf_op jit(solution)/shard_map/ppermute | solution.py:645
  67.6 14.3 %collective-permute-start.22 = (bf16[272,384]{1,0:T(8,128)(2,1)S(1)}, bf16[272,384]{1,0:T(8,128)(2,1)S(1)}, u32[]{:S(2)}, u32[]{:S(2)}) collective-permute-start(bf16[272,384]{1,0:T(8,128)(2,1)S(1)} %combine.7.refs_11_), channel_id=1, source_target_pairs={{0,16},{1,17},{2,18},{3,19},{4,20},{5,21},{6,22},{7,23},{8,24},{9,... | collective-permute-start | bytes 626696 | tf_op jit(solution)/shard_map/ppermute | solution.py:645
  68.9 14.2 %collective-permute-start.21 = (bf16[272,384]{1,0:T(8,128)(2,1)S(1)}, bf16[272,384]{1,0:T(8,128)(2,1)S(1)}, u32[]{:S(2)}, u32[]{:S(2)}) collective-permute-start(bf16[272,384]{1,0:T(8,128)(2,1)S(1)} %combine.6.refs_2_.refs_10_), channel_id=1, source_target_pairs={{0,16},{1,17},{2,18},{3,19},{4,20},{5,21},{6,22},{7,23},{8,24},{9,... | collective-permute-start | bytes 626696 | tf_op jit(solution)/shard_map/ppermute | solution.py:645
  72.1 14.7 %collective-permute-start.20 = (bf16[272,384]{1,0:T(8,128)(2,1)S(1)}, bf16[272,384]{1,0:T(8,128)(2,1)S(1)}, u32[]{:S(2)}, u32[]{:S(2)}) collective-permute-start(bf16[272,384]{1,0:T(8,128)(2,1)S(1)} %get-tuple-element.86.refs_10_.refs_1_), channel_id=1, source_target_pairs={{0,8},{1,9},{2,10},{3,11},{4,12},{5,13},{6,14},{7,15},{8,16},{9,17... | collective-permute-start | bytes 626696 | tf_op jit(solution)/shard_map/ppermute | solution.py:645
  78.5 9.7 %collective-permute-start.19 = (bf16[272,384]{1,0:T(8,128)(2,1)S(1)}, bf16[272,384]{1,0:T(8,128)(2,1)S(1)}, u32[]{:S(2)}, u32[]{:S(2)}) collective-permute-start(bf16[272,384]{1,0:T(8,128)(2,1)S(1)} %get-tuple-element.87.refs_8_.refs_1_), channel_id=1, source_target_pairs={{0,8},{1,9},{2,10},{3,11},{4,12},{5,13},{6,14},{7,15},{8,16},{9,17... | collective-permute-start | bytes 626696 | tf_op jit(solution)/shard_map/ppermute | solution.py:645
  80.4 27.8 %collective-permute-start.25 = (bf16[272,512]{1,0:T(8,128)(2,1)S(1)}, bf16[272,512]{1,0:T(8,128)(2,1)S(1)}, u32[]{:S(2)}, u32[]{:S(2)}) collective-permute-start(bf16[272,512]{1,0:T(8,128)(2,1)S(1)} %combine.5.refs_0_), channel_id=1, source_target_pairs={{0,16},{1,17},{2,18},{3,19},{4,20},{5,21},{6,22},{7,23},{8,24},{9,... | collective-permute-start | bytes 835592 | tf_op jit(solution)/shard_map/ppermute | solution.py:645
  86.9 23.4 %collective-permute-start.24 = (bf16[272,384]{1,0:T(8,128)(2,1)S(1)}, bf16[272,384]{1,0:T(8,128)(2,1)S(1)}, u32[]{:S(2)}, u32[]{:S(2)}) collective-permute-start(bf16[272,384]{1,0:T(8,128)(2,1)S(1)} %combine.8.refs_2_), channel_id=1, source_target_pairs={{0,16},{1,17},{2,18},{3,19},{4,20},{5,21},{6,22},{7,23},{8,24},{9,... | collective-permute-start | bytes 626696 | tf_op jit(solution)/shard_map/ppermute | solution.py:645
  88.3 24.5 %collective-permute-start.23 = (bf16[272,384]{1,0:T(8,128)(2,1)S(1)}, bf16[272,384]{1,0:T(8,128)(2,1)S(1)}, u32[]{:S(2)}, u32[]{:S(2)}) collective-permute-start(bf16[272,384]{1,0:T(8,128)(2,1)S(1)} %combine.9.refs_0_), channel_id=1, source_target_pairs={{0,16},{1,17},{2,18},{3,19},{4,20},{5,21},{6,22},{7,23},{8,24},{9,... | collective-permute-start | bytes 626696 | tf_op jit(solution)/shard_map/ppermute | solution.py:645
  89.6 26.8 %collective-permute-start.28 = (bf16[256,768]{1,0:T(8,128)(2,1)S(1)}, bf16[256,768]{1,0:T(8,128)(2,1)S(1)}, u32[]{:S(2)}, u32[]{:S(2)}) collective-permute-start(bf16[256,768]{1,0:T(8,128)(2,1)S(1)} %get-tuple-element.107), channel_id=1, source_target_pairs={{0,4},{1,5},{2,6},{3,7},{4,0},{5,1},{6,2},{7,3},{8,12},{9,13},{10,... | collective-permute-start | bytes 1179656 | tf_op jit(solution)/shard_map/ppermute | solution.py:645
  110.2 4.8 %collective-permute-start.29 = (bf16[256,512]{1,0:T(8,128)(2,1)S(1)}, bf16[256,512]{1,0:T(8,128)(2,1)S(1)}, u32[]{:S(2)}, u32[]{:S(2)}) collective-permute-start(bf16[256,512]{1,0:T(8,128)(2,1)S(1)} %get-tuple-element.108), channel_id=1, source_target_pairs={{0,4},{1,5},{2,6},{3,7},{4,0},{5,1},{6,2},{7,3},{8,12},{9,13},{10,... | collective-permute-start | bytes 786440 | tf_op jit(solution)/shard_map/ppermute | solution.py:645
  111.4 6.4 %collective-permute-start.27 = (bf16[256,384]{1,0:T(8,128)(2,1)S(1)}, bf16[256,384]{1,0:T(8,128)(2,1)S(1)}, u32[]{:S(2)}, u32[]{:S(2)}) collective-permute-start(bf16[256,384]{1,0:T(8,128)(2,1)S(1)} %get-tuple-element.106), channel_id=1, source_target_pairs={{0,4},{1,5},{2,6},{3,7},{4,0},{5,1},{6,2},{7,3},{8,12},{9,13},{10,... | collective-permute-start | bytes 589832 | tf_op jit(solution)/shard_map/ppermute | solution.py:645
  113.9 5.3 %collective-permute-start.26 = (bf16[256,384]{1,0:T(8,128)(2,1)S(1)}, bf16[256,384]{1,0:T(8,128)(2,1)S(1)}, u32[]{:S(2)}, u32[]{:S(2)}) collective-permute-start(bf16[256,384]{1,0:T(8,128)(2,1)S(1)} %get-tuple-element.105), channel_id=1, source_target_pairs={{0,4},{1,5},{2,6},{3,7},{4,0},{5,1},{6,2},{7,3},{8,12},{9,13},{10,... | collective-permute-start | bytes 589832 | tf_op jit(solution)/shard_map/ppermute | solution.py:645
  (8 other events, 47.8 us)

commit v6 on v5

--- a/solution.py
+++ b/solution.py
@@ -163,11 +163,10 @@
 LANES = 128
 LOG2E = 1.4426950408889634
 F32, BF16 = jnp.float32, jnp.bfloat16
-WIDTHS = (512, 0, 768, 768)
-RESTS = ("", "BD", "", "C")
-GROUPED = ((0, 0, 512), (2, 0, 768), (3, 0, 384), (3, 384, 384))
-FIRST_ROUND = ((256, 256), (384, 384), (384,), (384,))
-SECOND_ROUND = ((512,), (384, 384), (384,), (384,))
+WIDTHS = (768, 1280)
+RESTS = ("BCD", "")
+GROUPED = ((0, 0, 768), (1, 0, 512), (1, 512, 384), (1, 896, 384))
+ROUNDS = ((256, 256, 256), (512,), (384,), (384,))
 
 
 def halves(value, count):
@@ -210,78 +209,60 @@
     return ds(group * PER_GROUP + first, width)
 
 
-def pack_first_kernel(shards, place, xbc, send, sems):
+def runs(group):
+    yield group * PER_GROUP, PER_GROUP
+    yield INNER + group * STATE, STATE
+    yield INNER + (GROUPS + group) * STATE, STATE
+
+
+def pack_kernel(shards, place, xbc, dt_raw, send, near, far, tail, sems):
     core, shard = place[2], place[4]
     count = xbc.shape[0]
-    width = WIDTHS[0]
-    copies = []
+    copies = [(xbc.at[count - 16 :], tail)]
+    to = 0
     for r in range(shards):
-        group = (shard ^ r) * PAIR + 1 - core
-        copies.append((xbc.at[:, channels(group, 0, width)], send.at[:, r * width : (r + 1) * width]))
-        last, rows = xbc.at[count - 16 :], slice(16 * r, 16 * r + 16)
-        to = shards * width
-        copies.append((last.at[:, channels(group, width, PER_GROUP - width)], send.at[rows, to : to + PER_GROUP - width]))
-        to += PER_GROUP - width
-        for i in range(2):
-            at = ds(INNER + (i * GROUPS + group) * STATE, STATE)
-            copies.append((last.at[:, at], send.at[rows, to + i * STATE : to + (i + 1) * STATE]))
+        for start, width in runs((shard ^ r) * PAIR + 1 - core):
+            copies.append((xbc.at[:, ds(start, width)], send.at[:, to : to + width]))
+            to += width
+    copies.append((dt_raw, send.at[:, to:]))
+    started = run(copies, sems)
+    started[0].wait()
+    for edge, side in ((near, 1), (far, 0)):
+        to = 0
+        for r in range(shards):
+            for start, width in runs(((shards - 1) ^ r) * PAIR + side):
+                rows = tail[:, start : start + width].astype(F32)
+                edge[:, to : to + width] = rows[13:16].astype(BF16)
+                to += width
+    for copy in started[1:]:
+        copy.wait()
+
+
+def taps_kernel(place, weight, bias, order, taps, offset, sems):
+    copies, to = [], 0
+    for start, width in runs(place[0]):
+        copies.append((weight.at[:, ds(start, width)], taps.at[:, to : to + width]))
+        copies.append((bias.at[:, ds(start, width)], offset.at[:, to : to + width]))
+        to += width
     for copy in run(copies, sems):
         copy.wait()
 
 
-def pack_kernel(shards, place, xbc, dt_raw, weight, bias, order, send, taps, offset, tail, sems):
+def total_of(piece):
+    return WIDTHS[piece] + sum(LANES if kind == "D" else STATE for kind in RESTS[piece])
+
+
+def view(refs, piece):
+    origin = sum(map(total_of, range(piece)))
+    return [(ref, origin if r < 2 else 0) for r, ref in enumerate(refs)]
+
+
+def merge_kernel(shards, plan, unread, place, xbc, dt_raw, got, near, far, *refs):
+    refs = refs[unread:]
+    outs, sems = refs[: len(plan)], refs[len(plan)]
     core, shard = place[2], place[4]
     count = xbc.shape[0]
-    first = WIDTHS[0]
-    width = PER_GROUP - first
-    rest = width * shards
     size = PER_GROUP + 2 * STATE
-    copies = []
-    for r in range(shards):
-        group = (shard ^ r) * PAIR + 1 - core
-        copies.append((xbc.at[:, channels(group, first, width)], send.at[:, r * width : (r + 1) * width]))
-        for i in range(2):
-            to = rest + (i * shards + r) * STATE
-            copies.append((xbc.at[:, ds(INNER + (i * GROUPS + group) * STATE, STATE)], send.at[:, to : to + STATE]))
-    copies.append((dt_raw, send.at[:, send.shape[1] - HEADS :]))
-    everything = [(weight, taps, place[0], 0), (bias, offset, place[0], 0)]
-    for r in range(shards):
-        everything.append((xbc.at[count - 16 :], tail, (shard ^ r) * PAIR + core, r * size))
-    for source, target, group, to in everything:
-        copies.append((source.at[:, channels(group, 0, PER_GROUP)], target.at[:, to : to + PER_GROUP]))
-        for i in range(2):
-            at = ds(INNER + (i * GROUPS + group) * STATE, STATE)
-            start = to + PER_GROUP + i * STATE
-            copies.append((source.at[:, at], target.at[:, start : start + STATE]))
-    for copy in run(copies, sems):
-        copy.wait()
-
-
-def put_edge(shards, place, got, tail, out):
-    count = got.shape[0]
-    first = WIDTHS[0]
-    size = PER_GROUP + 2 * STATE
-    for r in range(shards):
-        theirs = [got[count - 16 :, r * first : (r + 1) * first]]
-        theirs.append(got[16 * r : 16 * r + 16, shards * first :])
-        to = r * size
-        for part in theirs:
-            at = slice(to, to + part.shape[1])
-            rows = jnp.where(place[2] == 0, part.astype(F32), tail[:, at].astype(F32))
-            out[:, at] = rows[13:16].astype(BF16)
-            to = at.stop
-
-
-def total_of(piece):
-    return WIDTHS[piece] + sum(LANES if kind == "D" else STATE for kind in RESTS[piece])
-
-
-def merge_kernel(shards, plan, unread, place, xbc, dt_raw, got_first, got, edges, *refs):
-    refs = refs[unread:]
-    outs, sems = refs[: len(plan)], refs[-1]
-    core, shard = place[2], place[4]
-    count = xbc.shape[0]
-    stride = PER_GROUP - WIDTHS[0]
     mine = pl.ds(pl.multiple_of(core * count, count), count)
     other = pl.ds(pl.multiple_of((1 - core) * count, count), count)
     copies, steps = [], []
@@ -290,29 +271,19 @@
         to = 0
         for piece in pieces:
             first, width = sum(WIDTHS[:piece]), WIDTHS[piece]
-            if piece == 0:
-                source = got_first.at[:, r * width : (r + 1) * width]
-            else:
-                at = r * stride + first - WIDTHS[0]
-                source = got.at[:, at : at + width]
-            if width:
-                copies.append((xbc.at[:, channels(group, first, width)], out.at[mine, to : to + width]))
-                copies.append((source, out.at[other, to : to + width]))
-            to += width
-            for kind in RESTS[piece]:
-                if kind == "D":
-                    steps.append((out, r, to))
-                    to += LANES
-                    continue
-                i = "BC".index(kind)
-                at = ds(INNER + (i * GROUPS + group) * STATE, STATE)
-                copies.append((xbc.at[:, at], out.at[mine, to : to + STATE]))
-                at = stride * shards + (i * shards + r) * STATE
-                copies.append((got.at[:, at : at + STATE], out.at[other, to : to + STATE]))
-                to += STATE
+            parts = [(group * PER_GROUP + first, r * size + first, width)]
+            for i, kind in enumerate("BC"):
+                if kind in RESTS[piece]:
+                    at = INNER + (i * GROUPS + group) * STATE
+                    parts.append((at, r * size + PER_GROUP + i * STATE, STATE))
+            for own, theirs, width in parts:
+                copies.append((xbc.at[:, ds(own, width)], out.at[mine, to : to + width]))
+                copies.append((got.at[:, theirs : theirs + width], out.at[other, to : to + width]))
+                to += width
+            if "D" in RESTS[piece]:
+                steps.append((out, r, to))
+                to += LANES
     started = run(copies, sems)
-    if len(refs) > len(plan) + 1:
-        put_edge(shards, place, got_first, edges, refs[-2])
     if steps:
         lane = lax.broadcasted_iota(jnp.int32, (count, LANES), 1)
         per_tile = LANES * GROUPS // HEADS
@@ -333,7 +304,8 @@
             out[: count // 2, to : to + LANES] = packed.astype(BF16)
             size = PER_GROUP + 2 * STATE
             at = slice(r * size, (r + 1) * size)
-            edge = jnp.concatenate([edges[:, at].astype(F32), jnp.zeros((1, size), F32)], 0)
+            edge = near[:, at].astype(F32) + far[:, at].astype(F32)
+            edge = jnp.concatenate([edge, jnp.zeros((1, size), F32)], 0)
             edge = jnp.concatenate([edge[:, q * LANES : (q + 1) * LANES] for q in range(size // LANES)], 0)
             fill = jnp.zeros((PAIR * count - count // 2 - edge.shape[0], LANES), F32)
             out[count // 2 :, to : to + LANES] = jnp.concatenate([edge, fill], 0).astype(BF16)
@@ -343,12 +315,12 @@
 
 def convolve_in_order(place, blocks, columns, edge, tap, bias, wide, put):
     width = columns.stop - columns.start
-    count = blocks[0].shape[0] // PAIR
+    count = blocks[0][0].shape[0] // PAIR
     wide[5:8, :width] = edge
-    for r, block in enumerate(blocks):
+    for r, (block, origin) in enumerate(blocks):
         for core in range(PAIR):
             at = pl.multiple_of((core * len(blocks) + (place[4] ^ r)) * count + 8, 8)
-            part = block[core * count : (core + 1) * count, columns]
+            part = block[core * count : (core + 1) * count, origin + columns.start : origin + columns.stop]
             wide[pl.ds(at, count), :width] = part.astype(F32)
     tap, bias = tap * 0.5, bias * 0.5
     for start in range(0, PAIR * len(blocks) * count, count):
@@ -362,12 +334,13 @@
 def prep_kernel(shards, place, *refs):
     blocks, (taps, offset, a_ref, bias_ref, skip_ref, order) = refs[:shards], refs[shards : shards + 6]
     b_ref, edge_ref, cum_ref, row_ref, factor_ref, tail_ref, skip_out, dt_ref, wide = refs[shards + 6 :]
-    start = WIDTHS[1]
-    last = total_of(1) - LANES
+    blocks = view(blocks, 0)
+    start = WIDTHS[0]
+    last = total_of(0) - LANES
     size = edge_ref.shape[1]
-    count = blocks[0].shape[0] // PAIR
+    count = blocks[0][0].shape[0] // PAIR
     half, heads = count // 2, HEADS // GROUPS
-    columns = [block[:, last : last + LANES].astype(F32) for block in blocks]
+    columns = [block[:, last : last + LANES].astype(F32) for block, _ in blocks]
     edge = columns[0][half : half + 4 * size // LANES]
     for column in columns[1:]:
         edge = edge + column[half : half + 4 * size // LANES]
@@ -421,7 +394,8 @@
 def score_kernel(shards, place, *refs):
     blocks, refs = refs[:shards], refs[shards:]
     taps, offset, edge_ref, b_ref, c_ref, score_ref, wide = (*refs[:4], *refs[-3:])
-    start = WIDTHS[3]
+    blocks = view(blocks, 0)
+    start = WIDTHS[0] + STATE
     at = slice(PER_GROUP + STATE, PER_GROUP + 2 * STATE)
 
     def put(start, count, value):
@@ -460,6 +434,7 @@
     def put(row, count, value):
         x_ref[row : row + count] = value
 
+    blocks = view(blocks, piece)
     columns = slice(start, start + width)
     convolve_in_order(place, blocks, columns, edge_ref[0:3, at], taps[:, at], offset[:, at], wide, put)
     expand = spread(first // HEAD_DIM, width, 2)
@@ -577,32 +552,35 @@
     carry(first_head, place[2], last, before, own_ref, c_ref, factor_ref, partial, keep_ref, send_ref)
 
 
-def place_kernel(first, place, keep, got, *refs):
+def place_kernel(firsts, place, *refs):
+    count = len(firsts)
+    keeps, gots = refs[:count], refs[count : 2 * count]
     out, sems = refs[-2:]
     core = place[2]
-    width = keep.shape[1]
     half = out.shape[1] // PAIR
-    copies = [
-        (keep, out.at[:, ds(core * half + first, width)]),
-        (got, out.at[:, ds((1 - core) * half + first, width)]),
-    ]
+    copies = []
+    for first, keep, got in zip(firsts, keeps, gots):
+        width = keep.shape[1]
+        copies.append((keep, out.at[:, ds(core * half + first, width)]))
+        copies.append((got, out.at[:, ds((1 - core) * half + first, width)]))
     for copy in run(copies, sems):
         copy.wait()
 
 
-def put_in_place(first, shape, place, keep, got, before):
+def put_in_place(firsts, shape, place, keeps, gots, before):
     smem, vmem, hbm = (pl.BlockSpec(memory_space=m) for m in (pltpu.SMEM, pltpu.VMEM, pltpu.HBM))
+    count = len(firsts)
     return pl.pallas_call(
-        functools.partial(place_kernel, first),
+        functools.partial(place_kernel, firsts),
         out_shape=jax.ShapeDtypeStruct(shape, BF16),
-        in_specs=[smem, vmem, vmem] + [hbm] * len(before),
+        in_specs=[smem] + [vmem] * (2 * count) + [hbm] * len(before),
         out_specs=hbm,
-        input_output_aliases={3: 0} if before else {},
-        scratch_shapes=[pltpu.SemaphoreType.DMA((2,))],
+        input_output_aliases={2 * count + 1: 0} if before else {},
+        scratch_shapes=[pltpu.SemaphoreType.DMA((2 * count,))],
         compiler_params=pltpu.CompilerParams(vmem_limit_bytes=16 << 20),
         cost_estimate=pl.CostEstimate(flops=1, bytes_accessed=1, transcendentals=0),
         name="place",
-    )(place, keep, got, *before)
+    )(place, *keeps, *gots, *before)
 
 
 class Stay:
@@ -649,63 +627,48 @@
 
     rows = Stay(xbc)
     size = PER_GROUP + 2 * STATE
-    (sent,) = call(
-        functools.partial(pack_first_kernel, shards),
-        [((tok, shards * WIDTHS[0] + size - WIDTHS[0]), BF16)],
-        [place, rows],
-        scratch=[pltpu.SemaphoreType.DMA((4 * shards,))],
-        name="pack_first",
-        limit=None,
-    )
-    got_first = swap(sent)
-    sent, taps, offset, tail = call(
+    sent, near, far = call(
         functools.partial(pack_kernel, shards),
-        [
-            ((tok, shards * (size - WIDTHS[0]) + HEADS), BF16),
-            ((4, size), F32),
-            ((1, size), F32),
-            ((16, shards * size), BF16),
-        ],
-        [place, rows, Stay(dt_raw), Stay(conv_weight), Stay(conv_bias[None]), Stay(sent)],
-        scratch=[pltpu.SemaphoreType.DMA((6 * shards + 7,))],
+        [((tok, shards * size + HEADS), BF16), ((3, shards * size), BF16), ((3, shards * size), BF16)],
+        [place, rows, Stay(dt_raw)],
+        scratch=[pltpu.VMEM((16, xbc.shape[1]), BF16), pltpu.SemaphoreType.DMA((3 * shards + 2,))],
         name="pack",
-        limit=None,
-    )
-    got_rest = swap(sent)
-
-    def send_on(piece, order, edges=None):
-        unused = Stay(got_first)
-        plan = [(r, (piece,)) for r in range(shards)]
-        made = [((3, shards * size), BF16)] if piece == 0 else []
+    )
+    near = over(near, lambda i: i + peers if i % peers == peers - 1 else None)
+    far = over(far, lambda i: i + shards if i % peers == peers - 1 else None)
+    got = swap(sent)
+    taps, offset = call(
+        taps_kernel,
+        [((4, size), F32), ((1, size), F32)],
+        [place, Stay(conv_weight), Stay(conv_bias[None]), Stay(got)],
+        scratch=[pltpu.SemaphoreType.DMA((6,))],
+        name="taps",
+    )
+
+    def merge(plan, order):
+        steps = any("D" in RESTS[p] for _, pieces in plan for p in pieces)
+        parts = [p for _, pieces in plan for p in pieces]
         return call(
             functools.partial(merge_kernel, shards, plan, len(order)),
-            [((PAIR * tok, total_of(piece)), BF16)] * shards + made,
-            [
-                place,
-                rows,
-                dt_raw if piece == 1 else Stay(dt_raw),
-                got_first if piece == 0 else unused,
-                unused if piece == 0 else got_rest,
-                unused if edges is None else edges,
-            ]
+            [((PAIR * tok, sum(map(total_of, pieces))), BF16) for _, pieces in plan],
+            [place, rows] + [o if steps else Stay(o) for o in (dt_raw,)] + [got]
+            + [o if steps else Stay(o) for o in (near, far)]
             + [Stay(o) for o in order],
-            scratch=[pltpu.SemaphoreType.DMA((2 * shards * (1 + len(RESTS[piece])),))],
+            scratch=[pltpu.SemaphoreType.DMA((sum(2 + 4 * ("C" in RESTS[p]) for p in parts),))],
             name="merge",
         )
 
-    def travel(blocks):
-        got = [blocks[0]]
-        for r in range(1, shards):
-            got.append(over(blocks[r], lambda i, r=r: i ^ r))
-        return got
-
-    *first_blocks, edges = send_on(0, [], tail)
-    message = {0: travel(first_blocks)}
-    edges = over(edges, lambda i: i + peers if i % shards == shards - 1 else None)
-    second_blocks = send_on(1, [first_blocks[0], message[0][1]], edges)
-    message[1] = travel(second_blocks)
-    third_blocks = send_on(2, [second_blocks[0], *message[0][2:]])
-    message[2] = travel(third_blocks)
+    def across(block, r):
+        return over(block, lambda i: i ^ r)
+
+    far_apart = list(range(2, shards))
+    first_blocks = merge([(r, (0,)) for r in far_apart] + [(1, (0, 1))], [])
+    *far_blocks, near_block = first_blocks
+    arrived = [across(block, r) for r, block in zip(far_apart, far_blocks)]
+    near_got = across(near_block, 1)
+    *third_blocks, own_block = merge([(r, (1,)) for r in far_apart] + [(0, (0, 1))], [first_blocks[0]])
+    message = [[own_block, near_got, *arrived]]
+    message.append([own_block, near_got] + [across(block, r) for r, block in zip(far_apart, third_blocks)])
 
     tiles = [p.reshape(HEADS // LANES, LANES) for p in (a_log, dt_bias, skip_gain)]
     b, edge, cum, row, factor, tail, skip = call(
@@ -719,7 +682,7 @@
             ((slab, 2 * LANES), BF16),
             ((16, 3 * LANES), BF16),
         ],
-        [place] + message[1] + [taps, offset] + tiles + [Stay(third_blocks[0])],
+        [place] + message[0] + [taps, offset] + tiles + [Stay(third_blocks[0])],
         scratch=[pltpu.VMEM((slab, LANES), F32), pltpu.VMEM((slab + 8, STATE), F32)],
         name="prep",
     )
@@ -732,8 +695,8 @@
     def state_of(i, order):
         piece, _, width = GROUPED[i]
         x[i], own[i], *sent[i] = call(
-            functools.partial(state_kernel, shards, GROUPED[i], FIRST_ROUND[i]),
-            [((slab, width), BF16), ((STATE, width), F32)] + [((STATE + 16, w), BF16) for w in FIRST_ROUND[i]],
+            functools.partial(state_kernel, shards, GROUPED[i], ROUNDS[i]),
+            [((slab, width), BF16), ((STATE, width), F32)] + [((STATE + 16, w), BF16) for w in ROUNDS[i]],
             [place] + message[piece] + [taps, offset, edge, b, factor, tail] + [Stay(o) for o in order],
             scratch=[pltpu.VMEM((slab + 8, width), F32)],
             name="state",
@@ -742,13 +705,11 @@
 
     def combine_of(i, order):
         joined[i], before[i] = [], []
-        step = len(FIRST_ROUND[i]) // len(SECOND_ROUND[i])
-        for j, width in enumerate(SECOND_ROUND[i]):
-            early, late = last[i][j * step : (j + 1) * step], sent[i][j * step : (j + 1) * step]
+        for j, width in enumerate(ROUNDS[i]):
             (total,) = call(
-                functools.partial(combine_kernel, len(early)),
+                functools.partial(combine_kernel, 1),
                 [((STATE + 16, width), BF16)],
-                early + late + [Stay(o) for o in order],
+                [last[i][j], sent[i][j]] + [Stay(o) for o in order],
                 name="combine",
             )
             joined[i].append(total)
@@ -765,17 +726,10 @@
         )
 
     state_of(0, [])
-    combine_of(0, [])
-    fourth_blocks = send_on(3, [joined[0][0]])
-    message[3] = travel(fourth_blocks)
-    state_of(1, [fourth_blocks[0]])
-    combine_of(1, [])
-    state_of(2, joined[1])
-    state_of(3, sent[2])
     c, score = call(
         functools.partial(score_kernel, shards),
         [((slab, STATE), BF16), ((slab, BLOCK), F32)],
-        [place] + message[3] + [taps, offset, edge, b] + [Stay(o) for o in sent[3] + before[1]],
+        [place] + message[0] + [taps, offset, edge, b] + [Stay(o) for o in sent[0]],
         scratch=[pltpu.VMEM((slab + 8, STATE), F32)],
         name="score",
     )
@@ -785,28 +739,29 @@
         wide = [pltpu.VMEM((slab, GROUPED[i][2]), F32)]
         finish_of(finish_kernel, i, [x[i]] + mixes, order, scratch=wide)
 
-    in_full(1, [score])
-    combine_of(2, [keep[1]])
-    combine_of(3, joined[2])
-    order, partial = joined[3][0], {}
-    for i in (2, 3):
+    shape = (BLOCK, PAIR * PER_GROUP)
+    combine_of(0, [score])
+    in_full(0, joined[0])
+    out = put_in_place([0], shape, place, keep[:1], [swap(send[0])], [])
+    order = [out]
+    for i in range(1, count):
+        state_of(i, order)
+        order = sent[i]
+    partial = {}
+    for i in range(1, count):
+        combine_of(i, order)
         (partial[i],) = call(
             functools.partial(local_kernel, first_head(i)),
             [(x[i].shape, F32)],
-            [x[i]] + mixes + [Stay(order)],
+            [x[i]] + mixes + [Stay(o) for o in joined[i]],
             name="local",
         )
-        order = partial[i]
-    in_full(0, [order])
-    order = keep[0]
-    for i in (2, 3):
-        finish_of(final_kernel, i, [partial[i]], [order])
-        order = keep[i]
-    out = []
-    for i in range(count):
-        shape = (BLOCK, PAIR * PER_GROUP)
-        out = [put_in_place(first_head(i) * HEAD_DIM, shape, place, keep[i], swap(send[i]), out)]
-    return out[0]
+        order = [partial[i]]
+    for i in range(1, count):
+        finish_of(final_kernel, i, [partial[i]], order)
+        order = [keep[i]]
+    firsts = [first_head(i) * HEAD_DIM for i in range(1, count)]
+    return put_in_place(firsts, shape, place, keep[1:], [swap(o) for o in send[1:]], [out])
 
 
 def solution(mesh):

time: 122 us -> 153 us (1.25)
  waiting for transfers between devices: 19.5 us -> 82.7 us
  starting transfers between devices: 63.7 us -> 37.7 us
  Pallas kernels: 35.2 us -> 26.9 us
  local copies, waits for them, and re-layouts: 1.61 us -> 4.19 us
    ppermute x30 -> x24, waiting for transfers between devices: 19.5 us -> 82.7 us  [over(): lax.ppermute(block, axes, [(i, j) for i, j in route if j is not None and...]
    ppermute x30 -> x24, starting transfers between devices: 63.7 us -> 37.7 us  [over(): lax.ppermute(block, axes, [(i, j) for i, j in route if j is not None and...]
    pallas_call x23, Pallas kernels: 29.8 us -> 23.8 us  [call(): pl.pallas_call(body, out_shape=shapes, in_specs=specs, out_specs=[vmem] *...]
    unnamed x20 -> x16, local copies, waits for them, and re-layouts: 1.01 us -> 4.11 us
    pallas_call x4 -> x2, Pallas kernels: 5.41 us -> 3.08 us  [put_in_place(): pl.pallas_call(functools.partial(place_kernel, firsts), out_shape=jax.Sha...]
  transfers between devices with their start and end apart: 30 -> 24, of which waited for: 9 -> 18; matrix products, arithmetic and copies ran while one was open for 0% -> 0% of each run, Pallas kernels for 23% -> 9%
where the time goes in v6:
time: 153 us; the launch traced here: 152 us
  waiting for transfers between devices  82.7 us (54%)
  starting transfers between devices  37.7 us (25%)
  Pallas kernels  26.9 us (18%)
  local copies, waits for them, and re-layouts  4.19 us (3%)
    ppermute x24, waiting for transfers between devices, over(): lax.ppermute(block, axes, [(i, j) for i, j in route if j is not None and...  82.7 us
    ppermute x24, starting transfers between devices, over(): lax.ppermute(block, axes, [(i, j) for i, j in route if j is not None and...  37.7 us
    pallas_call x23, Pallas kernels, call(): pl.pallas_call(body, out_shape=shapes, in_specs=specs, out_specs=[vmem] *...  23.8 us
    unnamed x16, local copies, waits for them, and re-layouts  4.11 us
    pallas_call x2, Pallas kernels, put_in_place(): pl.pallas_call(functools.partial(place_kernel, firsts), out_shape=jax.Sha...  3.08 us
  transfers between devices with their start and end apart: 24, of which 18 were waited for; matrix products, arithmetic and copies ran while one was open for 0% of the time, Pallas kernels for 9%

profile of v6, /device:TPU:13, one launch (start us, length us, event | category | flops | bytes accessed | tf_op | source)
XLA Modules:
  0.0 151.9 jit_solution(12283138026480667679)
XLA Ops:
  0.1 1.7 %copy-done = bf16[64,20480]{1,0:T(8,128)(2,1)S(1)} copy-done((bf16[64,20480]{1,0:T(8,128)(2,1)S(1)}, bf16[64,20480]{1,0:T(8,128)(2,1)}, u32[]{:S(2)}) %copy-start) | copy-done | bytes 2621464
  8.6 5.6 %collective-permute-start.6 = (bf16[128,1408]{1,0:T(8,128)(2,1)S(1)}, bf16[128,1408]{1,0:T(8,128)(2,1)S(1)}, u32[]{:S(2)}, u32[]{:S(2)}) collective-permute-start(bf16[128,1408]{1,0:T(8,128)(2,1)S(1)} %get-tuple-element.50.refs_0_), channel_id=1, source_target_pairs={{0,2},{1,3},{2,0},{3,1},{4,6},{5,7},{6,4},{7,5},{8,10},{9,11},{10,... | collective-permute-start | bytes 1081352 | tf_op jit(solution)/shard_map/ppermute | solution.py:623
  16.3 19.4 %collective-permute-done.6.refs_2_ = bf16[128,1408]{1,0:T(8,128)(2,1)S(1)} collective-permute-done((bf16[128,1408]{1,0:T(8,128)(2,1)S(1)}, bf16[128,1408]{1,0:T(8,128)(2,1)S(1)}, u32[]{:S(2)}, u32[]{:S(2)}) %collective-permute-start.6) | collective-permute-done | bytes 360480 | tf_op jit(solution)/shard_map/ppermute | solution.py:623
  35.6 7.5 %collective-permute-done.7.refs_3_ = bf16[128,1408]{1,0:T(8,128)(2,1)S(1)} collective-permute-done((bf16[128,1408]{1,0:T(8,128)(2,1)S(1)}, bf16[128,1408]{1,0:T(8,128)(2,1)S(1)}, u32[]{:S(2)}, u32[]{:S(2)}) %collective-permute-start.7) | collective-permute-done | bytes 360480 | tf_op jit(solution)/shard_map/ppermute | solution.py:623
  43.2 1.7 %prep.1 = (bf16[512,256]{1,0:T(8,128)(2,1)S(1)}, f32[4,2560]{1,0:T(4,128)S(1)}, f32[512,128]{1,0:T(8,128)S(1)}, f32[128,512]{1,0:T(8,128)S(1)}, bf16[512,256]{1,...) custom-call(s32[5]{0:T(128)S(1)} %stack.23.place, ...), custom_call_target="tpu_custom_call" | custom-call | flops 1 | bytes 1 | tf_op jit(solution)/shard_map/prep/pallas_call | solution.py:598
  44.9 2.6 %state.4 = (bf16[512,768]{1,0:T(8,128)(2,1)S(1)}, f32[256,768]{1,0:T(8,128)S(1)}, bf16[272,256]{1,0:T(8,128)(2,1)S(1)}, bf16[272,256]{1,0:T(8,128)(2,1)S(1)}, bf16[272,256]{1,0:T(8,128)(2,1)S(1)}) custom-call(s32[5]{0:T(128)S(1)} %stack.23.place, bf16[128,2688]{1,0:T(8,128)(2,1)S(1)} %get-tuple-element.51.refs_0_, ...), custom_call_target="tpu_custom_call" | custom-call | flops 1 | bytes 1 | tf_op jit(solution)/shard_map/state/pallas_call | solution.py:598
  47.4 2.2 %collective-permute-start.8 = (bf16[272,256]{1,0:T(8,128)(2,1)S(1)}, bf16[272,256]{1,0:T(8,128)(2,1)S(1)}, u32[]{:S(2)}, u32[]{:S(2)}) collective-permute-start(bf16[272,256]{1,0:T(8,128)(2,1)S(1)} %get-tuple-element.62.refs_8_.refs_1_), channel_id=1, source_target_pairs={{0,8},{1,9},{2,10},{3,11},{4,12},{5,13},{6,14},{7,15},{8,16},{9,17... | collective-permute-start | bytes 417800 | tf_op jit(solution)/shard_map/ppermute | solution.py:623
  49.7 1.9 %collective-permute-start.9 = (bf16[272,256]{1,0:T(8,128)(2,1)S(1)}, bf16[272,256]{1,0:T(8,128)(2,1)S(1)}, u32[]{:S(2)}, u32[]{:S(2)}) collective-permute-start(bf16[272,256]{1,0:T(8,128)(2,1)S(1)} %get-tuple-element.63.refs_9_.refs_1_), channel_id=1, source_target_pairs={{0,8},{1,9},{2,10},{3,11},{4,12},{5,13},{6,14},{7,15},{8,16},{9,17... | collective-permute-start | bytes 417800 | tf_op jit(solution)/shard_map/ppermute | solution.py:623
  51.6 1.9 %collective-permute-start.10 = (bf16[272,256]{1,0:T(8,128)(2,1)S(1)}, bf16[272,256]{1,0:T(8,128)(2,1)S(1)}, u32[]{:S(2)}, u32[]{:S(2)}) collective-permute-start(bf16[272,256]{1,0:T(8,128)(2,1)S(1)} %get-tuple-element.64.refs_10_.refs_1_), channel_id=1, source_target_pairs={{0,8},{1,9},{2,10},{3,11},{4,12},{5,13},{6,14},{7,15},{8,16},{9,17... | collective-permute-start | bytes 417800 | tf_op jit(solution)/shard_map/ppermute | solution.py:623
  54.7 1.6 %collective-permute-done.9.refs_0_.refs_1_ = bf16[272,256]{1,0:T(8,128)(2,1)S(1)} collective-permute-done((bf16[272,256]{1,0:T(8,128)(2,1)S(1)}, bf16[272,256]{1,0:T(8,128)(2,1)S(1)}, u32[]{:S(2)}, u32[]{:S(2)}) %collective-permute-start.9) | collective-permute-done | bytes 139296 | tf_op jit(solution)/shard_map/ppermute | solution.py:623
  56.4 3.5 %collective-permute-done.10.refs_0_.refs_2_ = bf16[272,256]{1,0:T(8,128)(2,1)S(1)} collective-permute-done((bf16[272,256]{1,0:T(8,128)(2,1)S(1)}, bf16[272,256]{1,0:T(8,128)(2,1)S(1)}, u32[]{:S(2)}, u32[]{:S(2)}) %collective-permute-start.10) | collective-permute-done | bytes 139296 | tf_op jit(solution)/shard_map/ppermute | solution.py:623
  63.9 1.9 %collective-permute-done.13.refs_5_ = bf16[272,256]{1,0:T(8,128)(2,1)S(1)} collective-permute-done((bf16[272,256]{1,0:T(8,128)(2,1)S(1)}, bf16[272,256]{1,0:T(8,128)(2,1)S(1)}, u32[]{:S(2)}, u32[]{:S(2)}) %collective-permute-start.13) | collective-permute-done | bytes 139296 | tf_op jit(solution)/shard_map/ppermute | solution.py:623
  65.8 1.5 collective-permute-done.12.refs_4_
  67.3 2.2 %collective-permute-done.11.refs_3_ = bf16[272,256]{1,0:T(8,128)(2,1)S(1)} collective-permute-done((bf16[272,256]{1,0:T(8,128)(2,1)S(1)}, bf16[272,256]{1,0:T(8,128)(2,1)S(1)}, u32[]{:S(2)}, u32[]{:S(2)}) %collective-permute-start.11) | collective-permute-done | bytes 139296 | tf_op jit(solution)/shard_map/ppermute | solution.py:623
  69.5 2.4 %final.4 = (bf16[256,768]{1,0:T(8,128)(2,1)S(1)}, bf16[256,768]{1,0:T(8,128)(2,1)S(1)}) custom-call(s32[5]{0:T(128)S(1)} %stack.23.place, bf16[272,256]{1,0:T(8,128)(2,1)S(1)} %collective-permute-done.8.refs_0_, bf16[272,256]{1,0:T(8,128)(2,1)S(1)} %collective-permute-done.9.refs_0_.refs_1_, bf16[272,256]{1,0:T(8,128)(2,1)S(1)} %collective-permute-done.10.refs_0_.refs_2_, ...), custom_call_target="tpu_custom_call" | custom-call | flops 1 | bytes 1 | tf_op jit(solution)/shard_map/final/pallas_call | solution.py:598
  71.8 4.6 %collective-permute-start.14 = (bf16[256,768]{1,0:T(8,128)(2,1)S(1)}, bf16[256,768]{1,0:T(8,128)(2,1)S(1)}, u32[]{:S(2)}, u32[]{:S(2)}) collective-permute-start(bf16[256,768]{1,0:T(8,128)(2,1)S(1)} %get-tuple-element.73), channel_id=1, source_target_pairs={{0,4},{1,5},{2,6},{3,7},{4,0},{5,1},{6,2},{7,3},{8,12},{9,13},{10,... | collective-permute-start | bytes 1179656 | tf_op jit(solution)/shard_map/ppermute | solution.py:623
  76.4 3.9 %collective-permute-start.4 = (bf16[128,1280]{1,0:T(8,128)(2,1)S(1)}, bf16[128,1280]{1,0:T(8,128)(2,1)S(1)}, u32[]{:S(2)}, u32[]{:S(2)}) collective-permute-start(bf16[128,1280]{1,0:T(8,128)(2,1)S(1)} %get-tuple-element.53.refs_9_), channel_id=1, source_target_pairs={{0,2},{1,3},{2,0},{3,1},{4,6},{5,7},{6,4},{7,5},{8,10},{9,11},{10,... | collective-permute-start | bytes 983048 | tf_op jit(solution)/shard_map/ppermute | solution.py:623
  81.7 19.4 %collective-permute-done.4.refs_2_ = bf16[128,1280]{1,0:T(8,128)(2,1)S(1)} collective-permute-done((bf16[128,1280]{1,0:T(8,128)(2,1)S(1)}, bf16[128,1280]{1,0:T(8,128)(2,1)S(1)}, u32[]{:S(2)}, u32[]{:S(2)}) %collective-permute-start.4) | collective-permute-done | bytes 327712 | tf_op jit(solution)/shard_map/ppermute | solution.py:623
  101.1 7.0 %collective-permute-done.5.refs_3_ = bf16[128,1280]{1,0:T(8,128)(2,1)S(1)} collective-permute-done((bf16[128,1280]{1,0:T(8,128)(2,1)S(1)}, bf16[128,1280]{1,0:T(8,128)(2,1)S(1)}, u32[]{:S(2)}, u32[]{:S(2)}) %collective-permute-start.5) | collective-permute-done | bytes 327712 | tf_op jit(solution)/shard_map/ppermute | solution.py:623
  108.2 1.6 %copy-done.1 = bf16[256,4096]{1,0:T(8,128)(2,1)S(1)} copy-done((bf16[256,4096]{1,0:T(8,128)(2,1)S(1)}, bf16[256,4096]{1,0:T(8,128)(2,1)}, u32[]{:S(2)}) %copy-start.1) | copy-done | bytes 2097176
  109.8 2.0 %state.5 = (bf16[512,512]{1,0:T(8,128)(2,1)S(1)}, f32[256,512]{1,0:T(8,128)S(1)}, bf16[272,512]{1,0:T(8,128)(2,1)S(1)}) custom-call(s32[5]{0:T(128)S(1)} %stack.23.place, bf16[128,2688]{1,0:T(8,128)(2,1)S(1)} %get-tuple-element.51.refs_0_, bf16[128,2688]{1,0:T(8,128)(2,1)S(1)} %collective-permute-done.3.refs_1_, ...), custom_call_target="tpu_custom_call" | custom-call | flops 1 | bytes 1 | tf_op jit(solution)/shard_map/state/pallas_call | solution.py:598
  111.8 1.9 %collective-permute-start.15 = (bf16[272,512]{1,0:T(8,128)(2,1)S(1)}, bf16[272,512]{1,0:T(8,128)(2,1)S(1)}, u32[]{:S(2)}, u32[]{:S(2)}) collective-permute-start(bf16[272,512]{1,0:T(8,128)(2,1)S(1)} %get-tuple-element.74.refs_10_.refs_1_), channel_id=1, source_target_pairs={{0,8},{1,9},{2,10},{3,11},{4,12},{5,13},{6,14},{7,15},{8,16},{9,17... | collective-permute-start | bytes 835592 | tf_op jit(solution)/shard_map/ppermute | solution.py:623
  113.7 1.9 %state.6 = (bf16[512,384]{1,0:T(8,128)(2,1)S(1)}, f32[256,384]{1,0:T(8,128)S(1)}, bf16[272,384]{1,0:T(8,128)(2,1)S(1)}) custom-call(s32[5]{0:T(128)S(1)} %stack.23.place, bf16[128,2688]{1,0:T(8,128)(2,1)S(1)} %get-tuple-element.51.refs_0_, bf16[128,2688]{1,0:T(8,128)(2,1)S(1)} %collective-permute-done.3.refs_1_, ...), custom_call_target="tpu_custom_call" | custom-call | flops 1 | bytes 1 | tf_op jit(solution)/shard_map/state/pallas_call | solution.py:598
  115.6 2.1 %collective-permute-start.18 = (bf16[272,384]{1,0:T(8,128)(2,1)S(1)}, bf16[272,384]{1,0:T(8,128)(2,1)S(1)}, u32[]{:S(2)}, u32[]{:S(2)}) collective-permute-start(bf16[272,384]{1,0:T(8,128)(2,1)S(1)} %get-tuple-element.75.refs_10_.refs_1_), channel_id=1, source_target_pairs={{0,8},{1,9},{2,10},{3,11},{4,12},{5,13},{6,14},{7,15},{8,16},{9,17... | collective-permute-start | bytes 626696 | tf_op jit(solution)/shard_map/ppermute | solution.py:623
  117.7 1.9 %state.7 = (bf16[512,384]{1,0:T(8,128)(2,1)S(1)}, f32[256,384]{1,0:T(8,128)S(1)}, bf16[272,384]{1,0:T(8,128)(2,1)S(1)}) custom-call(s32[5]{0:T(128)S(1)} %stack.23.place, bf16[128,2688]{1,0:T(8,128)(2,1)S(1)} %get-tuple-element.51.refs_0_, bf16[128,2688]{1,0:T(8,128)(2,1)S(1)} %collective-permute-done.3.refs_1_, ...), custom_call_target="tpu_custom_call" | custom-call | flops 1 | bytes 1 | tf_op jit(solution)/shard_map/state/pallas_call | solution.py:598
  119.6 1.9 %collective-permute-start.17 = (bf16[272,384]{1,0:T(8,128)(2,1)S(1)}, bf16[272,384]{1,0:T(8,128)(2,1)S(1)}, u32[]{:S(2)}, u32[]{:S(2)}) collective-permute-start(bf16[272,384]{1,0:T(8,128)(2,1)S(1)} %get-tuple-element.76.refs_2_.refs_1_), channel_id=1, source_target_pairs={{0,8},{1,9},{2,10},{3,11},{4,12},{5,13},{6,14},{7,15},{8,16},{9,17... | collective-permute-start | bytes 626696 | tf_op jit(solution)/shard_map/ppermute | solution.py:623
  124.4 2.1 %collective-permute-done.18.refs_0_ = bf16[272,384]{1,0:T(8,128)(2,1)S(1)} collective-permute-done((bf16[272,384]{1,0:T(8,128)(2,1)S(1)}, bf16[272,384]{1,0:T(8,128)(2,1)S(1)}, u32[]{:S(2)}, u32[]{:S(2)}) %collective-permute-start.18) | collective-permute-done | bytes 208928 | tf_op jit(solution)/shard_map/ppermute | solution.py:623
  128.6 2.4 %collective-permute-done.17.refs_0_ = bf16[272,384]{1,0:T(8,128)(2,1)S(1)} collective-permute-done((bf16[272,384]{1,0:T(8,128)(2,1)S(1)}, bf16[272,384]{1,0:T(8,128)(2,1)S(1)}, u32[]{:S(2)}, u32[]{:S(2)}) %collective-permute-start.17) | collective-permute-done | bytes 208928 | tf_op jit(solution)/shard_map/ppermute | solution.py:623
  133.1 5.0 %collective-permute-done.16.refs_1_ = bf16[272,512]{1,0:T(8,128)(2,1)S(1)} collective-permute-done((bf16[272,512]{1,0:T(8,128)(2,1)S(1)}, bf16[272,512]{1,0:T(8,128)(2,1)S(1)}, u32[]{:S(2)}, u32[]{:S(2)}) %collective-permute-start.16) | collective-permute-done | bytes 278560 | tf_op jit(solution)/shard_map/ppermute | solution.py:623
  139.9 2.7 %collective-permute-done.19.refs_1_ = bf16[272,384]{1,0:T(8,128)(2,1)S(1)} collective-permute-done((bf16[272,384]{1,0:T(8,128)(2,1)S(1)}, bf16[272,384]{1,0:T(8,128)(2,1)S(1)}, u32[]{:S(2)}, u32[]{:S(2)}) %collective-permute-start.19) | collective-permute-done | bytes 208928 | tf_op jit(solution)/shard_map/ppermute | solution.py:623
  143.6 3.4 %collective-permute-done.20.refs_1_ = bf16[272,384]{1,0:T(8,128)(2,1)S(1)} collective-permute-done((bf16[272,384]{1,0:T(8,128)(2,1)S(1)}, bf16[272,384]{1,0:T(8,128)(2,1)S(1)}, u32[]{:S(2)}, u32[]{:S(2)}) %collective-permute-start.20) | collective-permute-done | bytes 208928 | tf_op jit(solution)/shard_map/ppermute | solution.py:623
  150.1 1.6 %place.3 = bf16[256,4096]{1,0:T(8,128)(2,1)} custom-call(s32[5]{0:T(128)S(1)} %stack.23.place, bf16[256,512]{1,0:T(8,128)(2,1)S(1)} %get-tuple-element.81.refs_6_.refs_0_, bf16[256,384]{1,0:T(8,128)(2,1)S(1)} %get-tuple-element.83.refs_6_.refs_1_, bf16[256,384]{1,0:T(8,128)(2,1)S(1)} %get-tuple-element.85.refs_2_, ...), custom_call_target="tpu_custom_call", output_to_operand_aliasing={{}: (7, {})} | custom-call | flops 1 | bytes 1 | tf_op jit(solution)/shard_map/place/pallas_call | solution.py:573
  (58 shorter events, 28.4 us)
Async XLA Ops:
  0.1 1.7 %copy-start = (bf16[64,20480]{1,0:T(8,128)(2,1)S(1)}, bf16[64,20480]{1,0:T(8,128)(2,1)}, u32[]{:S(2)}) copy-start(bf16[64,20480]{1,0:T(8,128)(2,1)} %xbc.5) | copy-start | bytes 7864324
  1.8 0.8 copy-start.3
  3.7 3.4 %collective-permute-start = (bf16[64,10496]{1,0:T(8,128)(2,1)S(1)}, bf16[64,10496]{1,0:T(8,128)(2,1)S(1)}, u32[]{:S(2)}, u32[]{:S(2)}) collective-permute-start(bf16[64,10496]{1,0:T(8,128)(2,1)S(1)} %get-tuple-element.47), channel_id=1, source_target_pairs={{0,4},{1,5},{2,6},{3,7},{4,0},{5,1},{6,2},{7,3},{8,12},{9,13},{10,... | collective-permute-start | bytes 4030472 | tf_op jit(solution)/shard_map/ppermute | solution.py:623
  4.4 1.3 collective-permute-start.1
  5.1 0.7 collective-permute-start.2
  8.3 34.8 %collective-permute-start.3 = (bf16[128,2688]{1,0:T(8,128)(2,1)S(1)}, bf16[128,2688]{1,0:T(8,128)(2,1)S(1)}, u32[]{:S(2)}, u32[]{:S(2)}) collective-permute-start(bf16[128,2688]{1,0:T(8,128)(2,1)S(1)} %get-tuple-element.52), channel_id=1, source_target_pairs={{0,1},{1,0},{2,3},{3,2},{4,5},{5,4},{6,7},{7,6},{8,9},{9,8},{10,11... | collective-permute-start | bytes 2064392 | tf_op jit(solution)/shard_map/ppermute | solution.py:623
  8.6 27.0 %collective-permute-start.6 = (bf16[128,1408]{1,0:T(8,128)(2,1)S(1)}, bf16[128,1408]{1,0:T(8,128)(2,1)S(1)}, u32[]{:S(2)}, u32[]{:S(2)}) collective-permute-start(bf16[128,1408]{1,0:T(8,128)(2,1)S(1)} %get-tuple-element.50.refs_0_), channel_id=1, source_target_pairs={{0,2},{1,3},{2,0},{3,1},{4,6},{5,7},{6,4},{7,5},{8,10},{9,11},{10,... | collective-permute-start | bytes 1081352 | tf_op jit(solution)/shard_map/ppermute | solution.py:623
  14.2 1.4 copy-start.2
  14.2 1.4 copy-start.4
  14.2 29.0 %copy-start.5 = (f32[256]{0:T(256)S(1)}, f32[256]{0:T(256)}, u32[]{:S(2)}) copy-start(f32[256]{0:T(256)} %param.11) | copy-start | bytes 3076
  14.2 29.0 %copy-start.6 = (f32[256]{0:T(256)S(1)}, f32[256]{0:T(256)}, u32[]{:S(2)}) copy-start(f32[256]{0:T(256)} %param.12) | copy-start | bytes 3076
  14.2 29.0 %copy-start.7 = (f32[256]{0:T(256)S(1)}, f32[256]{0:T(256)}, u32[]{:S(2)}) copy-start(f32[256]{0:T(256)} %param.13) | copy-start | bytes 3076
  14.2 29.0 %collective-permute-start.7 = (bf16[128,1408]{1,0:T(8,128)(2,1)S(1)}, bf16[128,1408]{1,0:T(8,128)(2,1)S(1)}, u32[]{:S(2)}, u32[]{:S(2)}) collective-permute-start(bf16[128,1408]{1,0:T(8,128)(2,1)S(1)} %get-tuple-element.57), channel_id=1, source_target_pairs={{0,3},{1,2},{2,1},{3,0},{4,7},{5,6},{6,5},{7,4},{8,11},{9,10},{10,... | collective-permute-start | bytes 1081352 | tf_op jit(solution)/shard_map/ppermute | solution.py:623
  47.4 7.2 %collective-permute-start.8 = (bf16[272,256]{1,0:T(8,128)(2,1)S(1)}, bf16[272,256]{1,0:T(8,128)(2,1)S(1)}, u32[]{:S(2)}, u32[]{:S(2)}) collective-permute-start(bf16[272,256]{1,0:T(8,128)(2,1)S(1)} %get-tuple-element.62.refs_8_.refs_1_), channel_id=1, source_target_pairs={{0,8},{1,9},{2,10},{3,11},{4,12},{5,13},{6,14},{7,15},{8,16},{9,17... | collective-permute-start | bytes 417800 | tf_op jit(solution)/shard_map/ppermute | solution.py:623
  49.7 6.7 %collective-permute-start.9 = (bf16[272,256]{1,0:T(8,128)(2,1)S(1)}, bf16[272,256]{1,0:T(8,128)(2,1)S(1)}, u32[]{:S(2)}, u32[]{:S(2)}) collective-permute-start(bf16[272,256]{1,0:T(8,128)(2,1)S(1)} %get-tuple-element.63.refs_9_.refs_1_), channel_id=1, source_target_pairs={{0,8},{1,9},{2,10},{3,11},{4,12},{5,13},{6,14},{7,15},{8,16},{9,17... | collective-permute-start | bytes 417800 | tf_op jit(solution)/shard_map/ppermute | solution.py:623
  51.6 8.4 %collective-permute-start.10 = (bf16[272,256]{1,0:T(8,128)(2,1)S(1)}, bf16[272,256]{1,0:T(8,128)(2,1)S(1)}, u32[]{:S(2)}, u32[]{:S(2)}) collective-permute-start(bf16[272,256]{1,0:T(8,128)(2,1)S(1)} %get-tuple-element.64.refs_10_.refs_1_), channel_id=1, source_target_pairs={{0,8},{1,9},{2,10},{3,11},{4,12},{5,13},{6,14},{7,15},{8,16},{9,17... | collective-permute-start | bytes 417800 | tf_op jit(solution)/shard_map/ppermute | solution.py:623
  60.0 5.8 %collective-permute-start.13 = (bf16[272,256]{1,0:T(8,128)(2,1)S(1)}, bf16[272,256]{1,0:T(8,128)(2,1)S(1)}, u32[]{:S(2)}, u32[]{:S(2)}) collective-permute-start(bf16[272,256]{1,0:T(8,128)(2,1)S(1)} %combine.8.refs_16_), channel_id=1, source_target_pairs={{0,16},{1,17},{2,18},{3,19},{4,20},{5,21},{6,22},{7,23},{8,24},{9,... | collective-permute-start | bytes 417800 | tf_op jit(solution)/shard_map/ppermute | solution.py:623
  61.3 6.0 %collective-permute-start.12 = (bf16[272,256]{1,0:T(8,128)(2,1)S(1)}, bf16[272,256]{1,0:T(8,128)(2,1)S(1)}, u32[]{:S(2)}, u32[]{:S(2)}) collective-permute-start(bf16[272,256]{1,0:T(8,128)(2,1)S(1)} %combine.7.refs_2_.refs_15_), channel_id=1, source_target_pairs={{0,16},{1,17},{2,18},{3,19},{4,20},{5,21},{6,22},{7,23},{8,24},{9,... | collective-permute-start | bytes 417800 | tf_op jit(solution)/shard_map/ppermute | solution.py:623
  62.6 6.9 %collective-permute-start.11 = (bf16[272,256]{1,0:T(8,128)(2,1)S(1)}, bf16[272,256]{1,0:T(8,128)(2,1)S(1)}, u32[]{:S(2)}, u32[]{:S(2)}) collective-permute-start(bf16[272,256]{1,0:T(8,128)(2,1)S(1)} %combine.6.refs_2_.refs_14_), channel_id=1, source_target_pairs={{0,16},{1,17},{2,18},{3,19},{4,20},{5,21},{6,22},{7,23},{8,24},{9,... | collective-permute-start | bytes 417800 | tf_op jit(solution)/shard_map/ppermute | solution.py:623
  71.8 8.5 %collective-permute-start.14 = (bf16[256,768]{1,0:T(8,128)(2,1)S(1)}, bf16[256,768]{1,0:T(8,128)(2,1)S(1)}, u32[]{:S(2)}, u32[]{:S(2)}) collective-permute-start(bf16[256,768]{1,0:T(8,128)(2,1)S(1)} %get-tuple-element.73), channel_id=1, source_target_pairs={{0,4},{1,5},{2,6},{3,7},{4,0},{5,1},{6,2},{7,3},{8,12},{9,13},{10,... | collective-permute-start | bytes 1179656 | tf_op jit(solution)/shard_map/ppermute | solution.py:623
  76.4 24.7 %collective-permute-start.4 = (bf16[128,1280]{1,0:T(8,128)(2,1)S(1)}, bf16[128,1280]{1,0:T(8,128)(2,1)S(1)}, u32[]{:S(2)}, u32[]{:S(2)}) collective-permute-start(bf16[128,1280]{1,0:T(8,128)(2,1)S(1)} %get-tuple-element.53.refs_9_), channel_id=1, source_target_pairs={{0,2},{1,3},{2,0},{3,1},{4,6},{5,7},{6,4},{7,5},{8,10},{9,11},{10,... | collective-permute-start | bytes 983048 | tf_op jit(solution)/shard_map/ppermute | solution.py:623
  80.3 27.9 %collective-permute-start.5 = (bf16[128,1280]{1,0:T(8,128)(2,1)S(1)}, bf16[128,1280]{1,0:T(8,128)(2,1)S(1)}, u32[]{:S(2)}, u32[]{:S(2)}) collective-permute-start(bf16[128,1280]{1,0:T(8,128)(2,1)S(1)} %get-tuple-element.54), channel_id=1, source_target_pairs={{0,3},{1,2},{2,1},{3,0},{4,7},{5,6},{6,5},{7,4},{8,11},{9,10},{10,... | collective-permute-start | bytes 983048 | tf_op jit(solution)/shard_map/ppermute | solution.py:623
  108.2 1.6 %copy-start.1 = (bf16[256,4096]{1,0:T(8,128)(2,1)S(1)}, bf16[256,4096]{1,0:T(8,128)(2,1)}, u32[]{:S(2)}) copy-start(bf16[256,4096]{1,0:T(8,128)(2,1)} %place.2.refs_10_.refs_6_) | copy-start | bytes 6291460
  111.8 10.2 %collective-permute-start.15 = (bf16[272,512]{1,0:T(8,128)(2,1)S(1)}, bf16[272,512]{1,0:T(8,128)(2,1)S(1)}, u32[]{:S(2)}, u32[]{:S(2)}) collective-permute-start(bf16[272,512]{1,0:T(8,128)(2,1)S(1)} %get-tuple-element.74.refs_10_.refs_1_), channel_id=1, source_target_pairs={{0,8},{1,9},{2,10},{3,11},{4,12},{5,13},{6,14},{7,15},{8,16},{9,17... | collective-permute-start | bytes 835592 | tf_op jit(solution)/shard_map/ppermute | solution.py:623
  115.6 10.8 %collective-permute-start.18 = (bf16[272,384]{1,0:T(8,128)(2,1)S(1)}, bf16[272,384]{1,0:T(8,128)(2,1)S(1)}, u32[]{:S(2)}, u32[]{:S(2)}) collective-permute-start(bf16[272,384]{1,0:T(8,128)(2,1)S(1)} %get-tuple-element.75.refs_10_.refs_1_), channel_id=1, source_target_pairs={{0,8},{1,9},{2,10},{3,11},{4,12},{5,13},{6,14},{7,15},{8,16},{9,17... | collective-permute-start | bytes 626696 | tf_op jit(solution)/shard_map/ppermute | solution.py:623
  119.6 11.3 %collective-permute-start.17 = (bf16[272,384]{1,0:T(8,128)(2,1)S(1)}, bf16[272,384]{1,0:T(8,128)(2,1)S(1)}, u32[]{:S(2)}, u32[]{:S(2)}) collective-permute-start(bf16[272,384]{1,0:T(8,128)(2,1)S(1)} %get-tuple-element.76.refs_2_.refs_1_), channel_id=1, source_target_pairs={{0,8},{1,9},{2,10},{3,11},{4,12},{5,13},{6,14},{7,15},{8,16},{9,17... | collective-permute-start | bytes 626696 | tf_op jit(solution)/shard_map/ppermute | solution.py:623
  122.1 16.0 %collective-permute-start.16 = (bf16[272,512]{1,0:T(8,128)(2,1)S(1)}, bf16[272,512]{1,0:T(8,128)(2,1)S(1)}, u32[]{:S(2)}, u32[]{:S(2)}) collective-permute-start(bf16[272,512]{1,0:T(8,128)(2,1)S(1)} %combine.9.refs_0_), channel_id=1, source_target_pairs={{0,16},{1,17},{2,18},{3,19},{4,20},{5,21},{6,22},{7,23},{8,24},{9,... | collective-permute-start | bytes 835592 | tf_op jit(solution)/shard_map/ppermute | solution.py:623
  126.5 16.0 %collective-permute-start.19 = (bf16[272,384]{1,0:T(8,128)(2,1)S(1)}, bf16[272,384]{1,0:T(8,128)(2,1)S(1)}, u32[]{:S(2)}, u32[]{:S(2)}) collective-permute-start(bf16[272,384]{1,0:T(8,128)(2,1)S(1)} %combine.10.refs_0_), channel_id=1, source_target_pairs={{0,16},{1,17},{2,18},{3,19},{4,20},{5,21},{6,22},{7,23},{8,24},{9,... | collective-permute-start | bytes 626696 | tf_op jit(solution)/shard_map/ppermute | solution.py:623
  131.1 16.0 %collective-permute-start.20 = (bf16[272,384]{1,0:T(8,128)(2,1)S(1)}, bf16[272,384]{1,0:T(8,128)(2,1)S(1)}, u32[]{:S(2)}, u32[]{:S(2)}) collective-permute-start(bf16[272,384]{1,0:T(8,128)(2,1)S(1)} %combine.11.refs_0_), channel_id=1, source_target_pairs={{0,16},{1,17},{2,18},{3,19},{4,20},{5,21},{6,22},{7,23},{8,24},{9,... | collective-permute-start | bytes 626696 | tf_op jit(solution)/shard_map/ppermute | solution.py:623
  139.2 10.9 %collective-permute-start.21 = (bf16[256,512]{1,0:T(8,128)(2,1)S(1)}, bf16[256,512]{1,0:T(8,128)(2,1)S(1)}, u32[]{:S(2)}, u32[]{:S(2)}) collective-permute-start(bf16[256,512]{1,0:T(8,128)(2,1)S(1)} %get-tuple-element.86), channel_id=1, source_target_pairs={{0,4},{1,5},{2,6},{3,7},{4,0},{5,1},{6,2},{7,3},{8,12},{9,13},{10,... | collective-permute-start | bytes 786440 | tf_op jit(solution)/shard_map/ppermute | solution.py:623
  148.1 1.6 %collective-permute-start.23 = (bf16[256,384]{1,0:T(8,128)(2,1)S(1)}, bf16[256,384]{1,0:T(8,128)(2,1)S(1)}, u32[]{:S(2)}, u32[]{:S(2)}) collective-permute-start(bf16[256,384]{1,0:T(8,128)(2,1)S(1)} %get-tuple-element.88), channel_id=1, source_target_pairs={{0,4},{1,5},{2,6},{3,7},{4,0},{5,1},{6,2},{7,3},{8,12},{9,13},{10,... | collective-permute-start | bytes 589832 | tf_op jit(solution)/shard_map/ppermute | solution.py:623
  148.7 1.4 collective-permute-start.22

commit v7 on v6

--- a/solution.py
+++ b/solution.py
@@ -163,10 +163,10 @@
 LANES = 128
 LOG2E = 1.4426950408889634
 F32, BF16 = jnp.float32, jnp.bfloat16
-WIDTHS = (768, 1280)
-RESTS = ("BCD", "")
-GROUPED = ((0, 0, 768), (1, 0, 512), (1, 512, 384), (1, 896, 384))
-ROUNDS = ((256, 256, 256), (512,), (384,), (384,))
+WIDTHS = (896, 640, 512)
+RESTS = ("BCD", "", "")
+GROUPED = ((0, 0, 896), (1, 0, 640), (2, 0, 512))
+ROUNDS = ((896,), (640,), (512,))
 
 
 def halves(value, count):
@@ -221,7 +221,7 @@
     copies = [(xbc.at[count - 16 :], tail)]
     to = 0
     for r in range(shards):
-        for start, width in runs((shard ^ r) * PAIR + 1 - core):
+        for start, width in runs(r * PAIR + 1 - core):
             copies.append((xbc.at[:, ds(start, width)], send.at[:, to : to + width]))
             to += width
     copies.append((dt_raw, send.at[:, to:]))
@@ -230,7 +230,7 @@
     for edge, side in ((near, 1), (far, 0)):
         to = 0
         for r in range(shards):
-            for start, width in runs(((shards - 1) ^ r) * PAIR + side):
+            for start, width in runs(r * PAIR + side):
                 rows = tail[:, start : start + width].astype(F32)
                 edge[:, to : to + width] = rows[13:16].astype(BF16)
                 to += width
@@ -252,24 +252,19 @@
     return WIDTHS[piece] + sum(LANES if kind == "D" else STATE for kind in RESTS[piece])
 
 
-def view(refs, piece):
-    origin = sum(map(total_of, range(piece)))
-    return [(ref, origin if r < 2 else 0) for r, ref in enumerate(refs)]
-
-
 def merge_kernel(shards, plan, unread, place, xbc, dt_raw, got, near, far, *refs):
-    refs = refs[unread:]
-    outs, sems = refs[: len(plan)], refs[len(plan)]
+    outs, sems = refs[unread:]
     core, shard = place[2], place[4]
     count = xbc.shape[0]
     size = PER_GROUP + 2 * STATE
     mine = pl.ds(pl.multiple_of(core * count, count), count)
     other = pl.ds(pl.multiple_of((1 - core) * count, count), count)
     copies, steps = [], []
-    for out, (r, pieces) in zip(outs, plan):
-        group = (shard ^ r) * PAIR + core
+    for r in range(shards):
+        out = outs.at[r]
+        group = r * PAIR + core
         to = 0
-        for piece in pieces:
+        for piece in [plan]:
             first, width = sum(WIDTHS[:piece]), WIDTHS[piece]
             parts = [(group * PER_GROUP + first, r * size + first, width)]
             for i, kind in enumerate("BC"):
@@ -289,7 +284,7 @@
         per_tile = LANES * GROUPS // HEADS
         heads = HEADS // GROUPS
         for out, r, to in steps:
-            group = (shard ^ r) * PAIR + core
+            group = r * PAIR + core
             tile, shift = group // per_tile, (LANES - (group % per_tile) * heads) % LANES
             own = dt_raw[:, ds(tile * LANES, LANES)].astype(F32)
             theirs = got[:, ds(got.shape[1] - HEADS + tile * LANES, LANES)].astype(F32)
@@ -313,17 +308,18 @@
         copy.wait()
 
 
-def convolve_in_order(place, blocks, columns, edge, tap, bias, wide, put):
+def convolve_in_order(blocks, columns, edge, tap, bias, wide, put):
     width = columns.stop - columns.start
-    count = blocks[0][0].shape[0] // PAIR
+    shards, rows, _ = blocks.shape
+    count = rows // PAIR
     wide[5:8, :width] = edge
-    for r, (block, origin) in enumerate(blocks):
+    for r in range(shards):
         for core in range(PAIR):
-            at = pl.multiple_of((core * len(blocks) + (place[4] ^ r)) * count + 8, 8)
-            part = block[core * count : (core + 1) * count, origin + columns.start : origin + columns.stop]
-            wide[pl.ds(at, count), :width] = part.astype(F32)
+            at = (core * shards + r) * count + 8
+            part = blocks[r, core * count : (core + 1) * count, columns]
+            wide[at : at + count, :width] = part.astype(F32)
     tap, bias = tap * 0.5, bias * 0.5
-    for start in range(0, PAIR * len(blocks) * count, count):
+    for start in range(0, PAIR * shards * count, count):
         acc = bias + tap[0:1] * wide[start + 5 : start + 5 + count, :width]
         acc = acc + tap[1:2] * wide[start + 6 : start + 6 + count, :width]
         acc = acc + tap[2:3] * wide[start + 7 : start + 7 + count, :width]
@@ -331,16 +327,15 @@
         put(start, count, (acc + acc * jnp.tanh(acc)).astype(BF16))
 
 
-def prep_kernel(shards, place, *refs):
-    blocks, (taps, offset, a_ref, bias_ref, skip_ref, order) = refs[:shards], refs[shards : shards + 6]
-    b_ref, edge_ref, cum_ref, row_ref, factor_ref, tail_ref, skip_out, dt_ref, wide = refs[shards + 6 :]
-    blocks = view(blocks, 0)
+def prep_kernel(shards, place, blocks, *refs):
+    taps, offset, a_ref, bias_ref, skip_ref, order = refs[:6]
+    b_ref, edge_ref, cum_ref, row_ref, factor_ref, tail_ref, skip_out, dt_ref, wide = refs[6:]
     start = WIDTHS[0]
     last = total_of(0) - LANES
     size = edge_ref.shape[1]
-    count = blocks[0][0].shape[0] // PAIR
+    count = blocks.shape[1] // PAIR
     half, heads = count // 2, HEADS // GROUPS
-    columns = [block[:, last : last + LANES].astype(F32) for block, _ in blocks]
+    columns = [blocks[r, :, last : last + LANES].astype(F32) for r in range(shards)]
     edge = columns[0][half : half + 4 * size // LANES]
     for column in columns[1:]:
         edge = edge + column[half : half + 4 * size // LANES]
@@ -349,16 +344,16 @@
     for r, column in enumerate(columns):
         packed = column[:half]
         for j in range(2 * PAIR):
-            at = ((j // 2) * shards + (place[4] ^ r)) * count + (j % 2) * half
+            at = ((j // 2) * shards + r) * count + (j % 2) * half
             rows = packed if j == 0 else pltpu.roll(packed, LANES - j * heads, 1)
-            dt_ref[pl.ds(pl.multiple_of(at, half), half), :] = rows
+            dt_ref[at : at + half] = rows
 
     def put(start, count, value):
         b_ref[start : start + count] = value
 
     at = slice(PER_GROUP, PER_GROUP + STATE)
     convolve_in_order(
-        place, blocks, slice(start, start + STATE), edge_ref[0:3, at], taps[:, at], offset[:, at], wide, put
+        blocks, slice(start, start + STATE), edge_ref[0:3, at], taps[:, at], offset[:, at], wide, put
     )
     per_tile = LANES * GROUPS // HEADS
     group = place[0]
@@ -391,10 +386,8 @@
         tail_ref[at] = jnp.concatenate(halves(tail, 2), 1)
 
 
-def score_kernel(shards, place, *refs):
-    blocks, refs = refs[:shards], refs[shards:]
+def score_kernel(blocks, *refs):
     taps, offset, edge_ref, b_ref, c_ref, score_ref, wide = (*refs[:4], *refs[-3:])
-    blocks = view(blocks, 0)
     start = WIDTHS[0] + STATE
     at = slice(PER_GROUP + STATE, PER_GROUP + 2 * STATE)
 
@@ -402,7 +395,7 @@
         c_ref[start : start + count] = value
 
     convolve_in_order(
-        place, blocks, slice(start, start + STATE), edge_ref[0:3, at], taps[:, at], offset[:, at], wide, put
+        blocks, slice(start, start + STATE), edge_ref[0:3, at], taps[:, at], offset[:, at], wide, put
     )
     for block in range(PAIR):
         at = slice(block * BLOCK, (block + 1) * BLOCK)
@@ -423,8 +416,7 @@
     ref[STATE:] = packed.astype(BF16)
 
 
-def state_kernel(shards, part, sizes, place, *refs):
-    blocks, refs = refs[:shards], refs[shards:]
+def state_kernel(part, sizes, blocks, *refs):
     taps, offset, edge_ref, b_ref, factor_ref, tail_ref = refs[:6]
     x_ref, own_ref, *sends, wide = refs[-3 - len(sizes) :]
     piece, start, width = part
@@ -434,9 +426,8 @@
     def put(row, count, value):
         x_ref[row : row + count] = value
 
-    blocks = view(blocks, piece)
     columns = slice(start, start + width)
-    convolve_in_order(place, blocks, columns, edge_ref[0:3, at], taps[:, at], offset[:, at], wide, put)
+    convolve_in_order(blocks, columns, edge_ref[0:3, at], taps[:, at], offset[:, at], wide, put)
     expand = spread(first // HEAD_DIM, width, 2)
     both = []
     for block in range(PAIR):
@@ -645,30 +636,24 @@
         name="taps",
     )
 
-    def merge(plan, order):
-        steps = any("D" in RESTS[p] for _, pieces in plan for p in pieces)
-        parts = [p for _, pieces in plan for p in pieces]
-        return call(
-            functools.partial(merge_kernel, shards, plan, len(order)),
-            [((PAIR * tok, sum(map(total_of, pieces))), BF16) for _, pieces in plan],
-            [place, rows] + [o if steps else Stay(o) for o in (dt_raw,)] + [got]
+    def travel(piece, order):
+        steps = "D" in RESTS[piece]
+        (blocks,) = call(
+            functools.partial(merge_kernel, shards, piece, len(order)),
+            [((shards, PAIR * tok, total_of(piece)), BF16)],
+            [place, rows, dt_raw if steps else Stay(dt_raw), got]
             + [o if steps else Stay(o) for o in (near, far)]
             + [Stay(o) for o in order],
-            scratch=[pltpu.SemaphoreType.DMA((sum(2 + 4 * ("C" in RESTS[p]) for p in parts),))],
+            scratch=[pltpu.SemaphoreType.DMA((shards * (2 + 4 * ("C" in RESTS[piece])),))],
             name="merge",
         )
-
-    def across(block, r):
-        return over(block, lambda i: i ^ r)
-
-    far_apart = list(range(2, shards))
-    first_blocks = merge([(r, (0,)) for r in far_apart] + [(1, (0, 1))], [])
-    *far_blocks, near_block = first_blocks
-    arrived = [across(block, r) for r, block in zip(far_apart, far_blocks)]
-    near_got = across(near_block, 1)
-    *third_blocks, own_block = merge([(r, (1,)) for r in far_apart] + [(0, (0, 1))], [first_blocks[0]])
-    message = [[own_block, near_got, *arrived]]
-    message.append([own_block, near_got] + [across(block, r) for r, block in zip(far_apart, third_blocks)])
+        return blocks, lax.all_to_all(blocks, "head", 0, 0, tiled=True)
+
+    message, order = [], []
+    for piece in range(len(WIDTHS)):
+        blocks, arrived = travel(piece, order)
+        message.append(arrived)
+        order = [blocks]
 
     tiles = [p.reshape(HEADS // LANES, LANES) for p in (a_log, dt_bias, skip_gain)]
     b, edge, cum, row, factor, tail, skip = call(
@@ -682,7 +667,7 @@
             ((slab, 2 * LANES), BF16),
             ((16, 3 * LANES), BF16),
         ],
-        [place] + message[0] + [taps, offset] + tiles + [Stay(third_blocks[0])],
+        [place, message[0], taps, offset] + tiles + [Stay(blocks)],
         scratch=[pltpu.VMEM((slab, LANES), F32), pltpu.VMEM((slab + 8, STATE), F32)],
         name="prep",
     )
@@ -695,9 +680,9 @@
     def state_of(i, order):
         piece, _, width = GROUPED[i]
         x[i], own[i], *sent[i] = call(
-            functools.partial(state_kernel, shards, GROUPED[i], ROUNDS[i]),
+            functools.partial(state_kernel, GROUPED[i], ROUNDS[i]),
             [((slab, width), BF16), ((STATE, width), F32)] + [((STATE + 16, w), BF16) for w in ROUNDS[i]],
-            [place] + message[piece] + [taps, offset, edge, b, factor, tail] + [Stay(o) for o in order],
+            [message[piece], taps, offset, edge, b, factor, tail] + [Stay(o) for o in order],
             scratch=[pltpu.VMEM((slab + 8, width), F32)],
             name="state",
         )
@@ -727,9 +712,9 @@
 
     state_of(0, [])
     c, score = call(
-        functools.partial(score_kernel, shards),
+        score_kernel,
         [((slab, STATE), BF16), ((slab, BLOCK), F32)],
-        [place] + message[0] + [taps, offset, edge, b] + [Stay(o) for o in sent[0]],
+        [message[0], taps, offset, edge, b] + [Stay(o) for o in sent[0]],
         scratch=[pltpu.VMEM((slab + 8, STATE), F32)],
         name="score",
     )
@@ -743,25 +728,26 @@
     combine_of(0, [score])
     in_full(0, joined[0])
     out = put_in_place([0], shape, place, keep[:1], [swap(send[0])], [])
-    order = [out]
-    for i in range(1, count):
-        state_of(i, order)
-        order = sent[i]
-    partial = {}
-    for i in range(1, count):
-        combine_of(i, order)
-        (partial[i],) = call(
-            functools.partial(local_kernel, first_head(i)),
-            [(x[i].shape, F32)],
-            [x[i]] + mixes + [Stay(o) for o in joined[i]],
-            name="local",
-        )
-        order = [partial[i]]
-    for i in range(1, count):
-        finish_of(final_kernel, i, [partial[i]], order)
-        order = [keep[i]]
-    firsts = [first_head(i) * HEAD_DIM for i in range(1, count)]
-    return put_in_place(firsts, shape, place, keep[1:], [swap(o) for o in send[1:]], [out])
+    state_of(1, [keep[0]])
+    combine_of(1, [])
+    (partial,) = call(
+        functools.partial(local_kernel, first_head(1)),
+        [(x[1].shape, F32)],
+        [x[1]] + mixes + [Stay(o) for o in joined[1]],
+        name="local",
+    )
+    state_of(2, [partial])
+    finish_of(final_kernel, 1, [partial], sent[2])
+    combine_of(2, [keep[1]])
+    (partial,) = call(
+        functools.partial(local_kernel, first_head(2)),
+        [(x[2].shape, F32)],
+        [x[2]] + mixes + [Stay(o) for o in joined[2]],
+        name="local",
+    )
+    out = put_in_place([first_head(1) * HEAD_DIM], shape, place, keep[1:2], [swap(send[1])], [out])
+    finish_of(final_kernel, 2, [partial], [out])
+    return put_in_place([first_head(2) * HEAD_DIM], shape, place, keep[2:], [swap(send[2])], [out])
 
 
 def solution(mesh):

time: 153 us -> 151 us (0.987)
  waiting for transfers between devices: 82.7 us -> 56 us
  local copies, waits for them, and re-layouts: 4.19 us -> 14.6 us
  starting transfers between devices: 37.7 us -> 44.9 us
  Pallas kernels: 26.9 us -> 33 us
    ppermute x24 -> x12, waiting for transfers between devices: 82.7 us -> 28.5 us  [over(): lax.ppermute(block, axes, [(i, j) for i, j in route if j is not None and...]
    all_to_all x0 -> x3, waiting for transfers between devices: none -> 27.4 us  [travel(): return (blocks, lax.all_to_all(blocks, 'head', 0, 0, tiled=True))]
    all_to_all x0 -> x3, starting transfers between devices: none -> 21.2 us  [travel(): return (blocks, lax.all_to_all(blocks, 'head', 0, 0, tiled=True))]
    ppermute x24 -> x12, starting transfers between devices: 37.7 us -> 23.7 us  [over(): lax.ppermute(block, axes, [(i, j) for i, j in route if j is not None and...]
    unnamed x16 -> x78, local copies, waits for them, and re-layouts: 4.11 us -> 14.5 us
    pallas_call x23 -> x18, Pallas kernels: 23.8 us -> 28.8 us  [call(): pl.pallas_call(body, out_shape=shapes, in_specs=specs, out_specs=[vmem] *...]
    pallas_call x2 -> x3, Pallas kernels: 3.08 us -> 4.23 us  [put_in_place(): pl.pallas_call(functools.partial(place_kernel, firsts), out_shape=jax.Sha...]
  transfers between devices with their start and end apart: 24 -> 15, of which waited for: 18 -> 7; matrix products, arithmetic and copies ran while one was open for 0% -> 0% of each run, Pallas kernels for 9% -> 19%
where the time goes in v7:
time: 151 us; the launch traced here: 149 us
  waiting for transfers between devices  56 us (37%)
  starting transfers between devices  44.9 us (30%)
  Pallas kernels  33 us (22%)
  local copies, waits for them, and re-layouts  14.6 us (10%)
    pallas_call x18, Pallas kernels, call(): pl.pallas_call(body, out_shape=shapes, in_specs=specs, out_specs=[vmem] *...  28.8 us
    ppermute x12, waiting for transfers between devices, over(): lax.ppermute(block, axes, [(i, j) for i, j in route if j is not None and...  28.5 us
    all_to_all x3, waiting for transfers between devices, travel(): return (blocks, lax.all_to_all(blocks, 'head', 0, 0, tiled=True))  27.4 us
    ppermute x12, starting transfers between devices, over(): lax.ppermute(block, axes, [(i, j) for i, j in route if j is not None and...  23.7 us
    all_to_all x3, starting transfers between devices, travel(): return (blocks, lax.all_to_all(blocks, 'head', 0, 0, tiled=True))  21.2 us
    unnamed x78, local copies, waits for them, and re-layouts  14.5 us
    pallas_call x3, Pallas kernels, put_in_place(): pl.pallas_call(functools.partial(place_kernel, firsts), out_shape=jax.Sha...  4.23 us
  transfers between devices with their start and end apart: 15, of which 7 were waited for; matrix products, arithmetic and copies ran while one was open for 0% of the time, Pallas kernels for 19%

profile of v7, /device:TPU:13, one launch (start us, length us, event | category | flops | bytes accessed | tf_op | source)
XLA Modules:
  0.0 149.3 jit_solution(16164140876354462477)
XLA Ops:
  0.1 1.7 %copy-done = bf16[64,20480]{1,0:T(8,128)(2,1)S(1)} copy-done((bf16[64,20480]{1,0:T(8,128)(2,1)S(1)}, bf16[64,20480]{1,0:T(8,128)(2,1)}, u32[]{:S(2)}) %copy-start) | copy-done | bytes 2621464
  5.8 1.4 collective-permute-done.got.order
  10.6 8.4 %all-to-all-start.1 = ((bf16[4,128,1536]{2,1,0:T(8,128)(2,1)}), bf16[4,128,1536]{2,1,0:T(8,128)(2,1)}, u32[]{:S(2)}, u32[]{:S(2)}) async-start(bf16[4,128,1536]{2,1,0:T(8,128)(2,1)} %copy-done.6), calls=%async_computation.1 | async-start | bytes 3145728 | tf_op jit(solution)/shard_map/all_to_all | solution.py:650
  20.4 1.4 copy-done.7
  21.8 1.6 %merge.4.refs_0_ = bf16[4,128,640]{2,1,0:T(8,128)(2,1)} custom-call(s32[5]{0:T(128)S(1)} %stack.23.place, bf16[64,20480]{1,0:T(8,128)(2,1)S(1)} %copy-done.1, bf16[64,256]{1,0:T(8,128)(2,1)S(1)} %copy-done.28, bf16[64,10496]{1,0:T(8,128)(2,1)S(1)} %copy-done.4, bf16[3,10240]{1,0:T(4,128)(2,1)S(1)} %collective-permute-done.1.near, ...), custom_call_target="tpu_custom_call" | custom-call | flops 1 | bytes 1 | tf_op jit(solution)/shard_map/merge/pallas_call | solution.py:589
  23.3 27.4 %all-to-all-done.1.blocks = bf16[4,128,1536]{2,1,0:T(8,128)(2,1)} async-done(((bf16[4,128,1536]{2,1,0:T(8,128)(2,1)}), bf16[4,128,1536]{2,1,0:T(8,128)(2,1)}, u32[]{:S(2)}, u32[]{:S(2)}) %all-to-all-start.1) | async-done | bytes 1572896 | tf_op jit(solution)/shard_map/all_to_all | solution.py:650
  50.8 8.3 %all-to-all-start.2 = ((bf16[4,128,640]{2,1,0:T(8,128)(2,1)}), bf16[4,128,640]{2,1,0:T(8,128)(2,1)S(1)}, u32[]{:S(2)}, u32[]{:S(2)}) async-start(bf16[4,128,640]{2,1,0:T(8,128)(2,1)} %merge.4.refs_0_), calls=%async_computation.2 | async-start | bytes 1310720 | tf_op jit(solution)/shard_map/all_to_all | solution.py:650
  60.4 1.5 %merge.5.refs_5_ = bf16[4,128,512]{2,1,0:T(8,128)(2,1)} custom-call(s32[5]{0:T(128)S(1)} %stack.23.place, bf16[64,20480]{1,0:T(8,128)(2,1)S(1)} %copy-done.1, bf16[64,256]{1,0:T(8,128)(2,1)S(1)} %copy-done.28, bf16[64,10496]{1,0:T(8,128)(2,1)S(1)} %copy-done.5, bf16[3,10240]{1,0:T(4,128)(2,1)S(1)} %collective-permute-done.1.near, ...), custom_call_target="tpu_custom_call" | custom-call | flops 1 | bytes 1 | tf_op jit(solution)/shard_map/merge/pallas_call | solution.py:589
  62.7 2.6 %prep.1 = (bf16[512,256]{1,0:T(8,128)(2,1)S(1)}, f32[4,2560]{1,0:T(4,128)S(1)}, f32[512,128]{1,0:T(8,128)S(1)}, f32[128,512]{1,0:T(8,128)S(1)}, bf16[512,256]{1,...) custom-call(s32[5]{0:T(128)S(1)} %stack.23.place, ...), custom_call_target="tpu_custom_call" | custom-call | flops 1 | bytes 1 | tf_op jit(solution)/shard_map/prep/pallas_call | solution.py:589
  65.3 4.2 %state.3 = (bf16[512,896]{1,0:T(8,128)(2,1)S(1)}, f32[256,896]{1,0:T(8,128)S(1)}, bf16[272,896]{1,0:T(8,128)(2,1)S(1)}) custom-call(bf16[4,128,1536]{2,1,0:T(8,128)(2,1)} %all-to-all-done.1.blocks, f32[4,2560]{1,0:T(4,128)S(1)} %get-tuple-element.37.refs_0_, f32[1,2560]{1,0:T(1,128)S(1)} %get-tuple-element.38.refs_1_, ...), custom_call_target="tpu_custom_call" | custom-call | flops 1 | bytes 1 | tf_op jit(solution)/shard_map/state/pallas_call | solution.py:589
  70.4 2.2 %collective-permute-start.3 = (bf16[272,896]{1,0:T(8,128)(2,1)S(1)}, bf16[272,896]{1,0:T(8,128)(2,1)S(1)}, u32[]{:S(2)}, u32[]{:S(2)}) collective-permute-start(bf16[272,896]{1,0:T(8,128)(2,1)S(1)} %get-tuple-element.43.refs_4_.refs_1_), channel_id=1, source_target_pairs={{0,8},{1,9},{2,10},{3,11},{4,12},{5,13},{6,14},{7,15},{8,16},{9,17... | collective-permute-start | bytes 1462280 | tf_op jit(solution)/shard_map/ppermute | solution.py:614
  72.6 2.0 %score.1 = (bf16[512,256]{1,0:T(8,128)(2,1)S(1)}, f32[512,256]{1,0:T(8,128)S(1)}) custom-call(bf16[4,128,1536]{2,1,0:T(8,128)(2,1)} %all-to-all-done.1.blocks, f32[4,2560]{1,0:T(4,128)S(1)} %get-tuple-element.37.refs_0_, f32[1,2560]{1,0:T(1,128)S(1)} %get-tuple-element.38.refs_1_, f32[4,2560]{1,0:T(4,128)S(1)} %get-tuple-element.39.refs_2_, ...), custom_call_target="tpu_custom_call" | custom-call | flops 1 | bytes 1 | tf_op jit(solution)/shard_map/score/pallas_call | solution.py:589
  74.6 9.4 %collective-permute-done.3.refs_0_ = bf16[272,896]{1,0:T(8,128)(2,1)S(1)} collective-permute-done((bf16[272,896]{1,0:T(8,128)(2,1)S(1)}, bf16[272,896]{1,0:T(8,128)(2,1)S(1)}, u32[]{:S(2)}, u32[]{:S(2)}) %collective-permute-start.3) | collective-permute-done | bytes 487456 | tf_op jit(solution)/shard_map/ppermute | solution.py:614
  86.3 4.6 %all-to-all-start = ((bf16[4,128,512]{2,1,0:T(8,128)(2,1)}), bf16[4,128,512]{2,1,0:T(8,128)(2,1)}, u32[]{:S(2)}, u32[]{:S(2)}) async-start(bf16[4,128,512]{2,1,0:T(8,128)(2,1)} %merge.5.refs_5_), calls=%async_computation | async-start | bytes 1048576 | tf_op jit(solution)/shard_map/all_to_all | solution.py:650
  90.9 6.3 %collective-permute-done.4.refs_1_ = bf16[272,896]{1,0:T(8,128)(2,1)} collective-permute-done((bf16[272,896]{1,0:T(8,128)(2,1)}, bf16[272,896]{1,0:T(8,128)(2,1)}, u32[]{:S(2)}, u32[]{:S(2)}) %collective-permute-start.4) | collective-permute-done | bytes 487456 | tf_op jit(solution)/shard_map/ppermute | solution.py:614
  99.6 3.2 %final.3 = (bf16[256,896]{1,0:T(8,128)(2,1)S(1)}, bf16[256,896]{1,0:T(8,128)(2,1)S(1)}) custom-call(s32[5]{0:T(128)S(1)} %stack.23.place, bf16[272,896]{1,0:T(8,128)(2,1)S(1)} %collective-permute-done.3.refs_0_, bf16[272,896]{1,0:T(8,128)(2,1)} %collective-permute-done.4.refs_1_, f32[256,896]{1,0:T(8,128)S(1)} %copy-done.22, ...), custom_call_target="tpu_custom_call" | custom-call | flops 1 | bytes 1 | tf_op jit(solution)/shard_map/final/pallas_call | solution.py:589
  102.9 1.9 %state.4 = (bf16[512,640]{1,0:T(8,128)(2,1)S(1)}, f32[256,640]{1,0:T(8,128)S(1)}, bf16[272,640]{1,0:T(8,128)(2,1)S(1)}) custom-call(bf16[4,128,640]{2,1,0:T(8,128)(2,1)S(1)} %all-to-all-done.2.blocks, f32[4,2560]{1,0:T(4,128)S(1)} %get-tuple-element.37.refs_0_, f32[1,2560]{1,0:T(1,128)S(1)} %get-tuple-element.38.refs_1_, ...), custom_call_target="tpu_custom_call" | custom-call | flops 1 | bytes 1 | tf_op jit(solution)/shard_map/state/pallas_call | solution.py:589
  104.7 1.9 %collective-permute-start.5 = (bf16[272,640]{1,0:T(8,128)(2,1)S(1)}, bf16[272,640]{1,0:T(8,128)(2,1)S(1)}, u32[]{:S(2)}, u32[]{:S(2)}) collective-permute-start(bf16[272,640]{1,0:T(8,128)(2,1)S(1)} %get-tuple-element.53.refs_1_), channel_id=1, source_target_pairs={{0,8},{1,9},{2,10},{3,11},{4,12},{5,13},{6,14},{7,15},{8,16},{9,17... | collective-permute-start | bytes 1044488 | tf_op jit(solution)/shard_map/ppermute | solution.py:614
  106.7 7.0 %collective-permute-done.5.refs_0_ = bf16[272,640]{1,0:T(8,128)(2,1)S(1)} collective-permute-done((bf16[272,640]{1,0:T(8,128)(2,1)S(1)}, bf16[272,640]{1,0:T(8,128)(2,1)S(1)}, u32[]{:S(2)}, u32[]{:S(2)}) %collective-permute-start.5) | collective-permute-done | bytes 348192 | tf_op jit(solution)/shard_map/ppermute | solution.py:614
  113.8 1.5 collective-permute-start.7
  117.4 2.6 %state.5 = (bf16[512,512]{1,0:T(8,128)(2,1)S(1)}, f32[256,512]{1,0:T(8,128)S(1)}, bf16[272,512]{1,0:T(8,128)(2,1)S(1)}) custom-call(bf16[4,128,512]{2,1,0:T(8,128)(2,1)} %all-to-all-done.blocks, f32[4,2560]{1,0:T(4,128)S(1)} %copy-done.18, f32[1,2560]{1,0:T(1,128)S(1)} %get-tuple-element.38.refs_1_, f32[4,2560]{1,0:T(4,128)S(1)} %copy-done.26, ...), custom_call_target="tpu_custom_call" | custom-call | flops 1 | bytes 1 | tf_op jit(solution)/shard_map/state/pallas_call | solution.py:589
  120.1 1.9 %collective-permute-start.6 = (bf16[272,512]{1,0:T(8,128)(2,1)S(1)}, bf16[272,512]{1,0:T(8,128)(2,1)S(1)}, u32[]{:S(2)}, u32[]{:S(2)}) collective-permute-start(bf16[272,512]{1,0:T(8,128)(2,1)S(1)} %get-tuple-element.54.refs_6_.refs_1_), channel_id=1, source_target_pairs={{0,8},{1,9},{2,10},{3,11},{4,12},{5,13},{6,14},{7,15},{8,16},{9,17... | collective-permute-start | bytes 835592 | tf_op jit(solution)/shard_map/ppermute | solution.py:614
  122.0 4.8 %collective-permute-start.10 = (bf16[256,896]{1,0:T(8,128)(2,1)S(1)}, bf16[256,896]{1,0:T(8,128)(2,1)S(1)}, u32[]{:S(2)}, u32[]{:S(2)}) collective-permute-start(bf16[256,896]{1,0:T(8,128)(2,1)S(1)} %copy-done.38), channel_id=1, source_target_pairs={{0,4},{1,5},{2,6},{3,7},{4,0},{5,1},{6,2},{7,3},{8,12},{9,13},{10,... | collective-permute-start | bytes 1376264 | tf_op jit(solution)/shard_map/ppermute | solution.py:614
  126.8 1.7 %final.4 = (bf16[256,640]{1,0:T(8,128)(2,1)S(1)}, bf16[256,640]{1,0:T(8,128)(2,1)S(1)}) custom-call(s32[5]{0:T(128)S(1)} %stack.23.place, bf16[272,640]{1,0:T(8,128)(2,1)S(1)} %copy-done.16, bf16[272,640]{1,0:T(8,128)(2,1)} %collective-permute-done.7.refs_1_, f32[256,640]{1,0:T(8,128)S(1)} %copy-done.24, bf16[512,256]{1,0:T(8,128)(2,1)S(1)} %get-tuple-element.46.refs_3_, ...), custom_call_target="tpu_custom_call" | custom-call | flops 1 | bytes 1 | tf_op jit(solution)/shard_map/final/pallas_call | solution.py:589
  128.5 4.1 %collective-permute-start.9 = (bf16[256,640]{1,0:T(8,128)(2,1)S(1)}, bf16[256,640]{1,0:T(8,128)(2,1)S(1)}, u32[]{:S(2)}, u32[]{:S(2)}) collective-permute-start(bf16[256,640]{1,0:T(8,128)(2,1)S(1)} %get-tuple-element.59), channel_id=1, source_target_pairs={{0,4},{1,5},{2,6},{3,7},{4,0},{5,1},{6,2},{7,3},{8,12},{9,13},{10,... | collective-permute-start | bytes 983048 | tf_op jit(solution)/shard_map/ppermute | solution.py:614
  132.7 1.4 collective-permute-start.8
  134.2 1.5 place.3.refs_2_
  136.7 1.4 place.4.refs_6_.refs_2_
  138.1 3.3 %collective-permute-done.8.refs_1_ = bf16[272,512]{1,0:T(8,128)(2,1)S(1)} collective-permute-done((bf16[272,512]{1,0:T(8,128)(2,1)S(1)}, bf16[272,512]{1,0:T(8,128)(2,1)S(1)}, u32[]{:S(2)}, u32[]{:S(2)}) %collective-permute-start.8) | collective-permute-done | bytes 278560 | tf_op jit(solution)/shard_map/ppermute | solution.py:614
  141.3 1.6 %copy-done.2 = bf16[256,4096]{1,0:T(8,128)(2,1)S(1)} copy-done((bf16[256,4096]{1,0:T(8,128)(2,1)S(1)}, bf16[256,4096]{1,0:T(8,128)(2,1)}, u32[]{:S(2)}) %copy-start.2) | copy-done | bytes 2097176
  144.0 2.5 %collective-permute-start.11 = (bf16[256,512]{1,0:T(8,128)(2,1)S(1)}, bf16[256,512]{1,0:T(8,128)(2,1)S(1)}, u32[]{:S(2)}, u32[]{:S(2)}) collective-permute-start(bf16[256,512]{1,0:T(8,128)(2,1)S(1)} %get-tuple-element.62), channel_id=1, source_target_pairs={{0,4},{1,5},{2,6},{3,7},{4,0},{5,1},{6,2},{7,3},{8,12},{9,13},{10,... | collective-permute-start | bytes 786440 | tf_op jit(solution)/shard_map/ppermute | solution.py:614
  147.7 1.3 place.5
  (98 shorter events, 21.9 us)
Async XLA Ops:
  0.0 7.2 %copy-start.28 = (bf16[64,256]{1,0:T(8,128)(2,1)S(1)}, bf16[64,256]{1,0:T(8,128)(2,1)}, u32[]{:S(2)}) copy-start(bf16[64,256]{1,0:T(8,128)(2,1)} %dt_raw.7) | copy-start | bytes 98308
  3.7 3.4 %collective-permute-start = (bf16[64,10496]{1,0:T(8,128)(2,1)S(1)}, bf16[64,10496]{1,0:T(8,128)(2,1)S(1)}, u32[]{:S(2)}, u32[]{:S(2)}) collective-permute-start(bf16[64,10496]{1,0:T(8,128)(2,1)S(1)} %get-tuple-element.34), channel_id=1, source_target_pairs={{0,4},{1,5},{2,6},{3,7},{4,0},{5,1},{6,2},{7,3},{8,12},{9,13},{10,... | collective-permute-start | bytes 4030472 | tf_op jit(solution)/shard_map/ppermute | solution.py:614
  4.4 1.3 collective-permute-start.1
  5.1 0.7 collective-permute-start.2
  10.6 8.4 %copy-start.1 = (bf16[64,20480]{1,0:T(8,128)(2,1)S(1)}, bf16[64,20480]{1,0:T(8,128)(2,1)}, u32[]{:S(2)}) copy-start(bf16[64,20480]{1,0:T(8,128)(2,1)} %xbc.7) | copy-start | bytes 7864324
  10.6 40.1 %all-to-all-start.1 = ((bf16[4,128,1536]{2,1,0:T(8,128)(2,1)}), bf16[4,128,1536]{2,1,0:T(8,128)(2,1)}, u32[]{:S(2)}, u32[]{:S(2)}) async-start(bf16[4,128,1536]{2,1,0:T(8,128)(2,1)} %copy-done.6), calls=%async_computation.1 | async-start | bytes 3145728 | tf_op jit(solution)/shard_map/all_to_all | solution.py:650
  50.8 35.6 %all-to-all-start.2 = ((bf16[4,128,640]{2,1,0:T(8,128)(2,1)}), bf16[4,128,640]{2,1,0:T(8,128)(2,1)S(1)}, u32[]{:S(2)}, u32[]{:S(2)}) async-start(bf16[4,128,640]{2,1,0:T(8,128)(2,1)} %merge.4.refs_0_), calls=%async_computation.2 | async-start | bytes 1310720 | tf_op jit(solution)/shard_map/all_to_all | solution.py:650
  62.7 40.2 %copy-start.17 = (f32[4,2560]{1,0:T(4,128)}, f32[4,2560]{1,0:T(4,128)S(1)}, u32[]{:S(2)}) copy-start(f32[4,2560]{1,0:T(4,128)S(1)} %get-tuple-element.37.refs_0_) | copy-start | bytes 122884
  65.3 31.9 %copy-start.8 = (f32[128,512]{1,0:T(8,128)}, f32[128,512]{1,0:T(8,128)S(1)}, u32[]{:S(2)}) copy-start(f32[128,512]{1,0:T(8,128)S(1)} %get-tuple-element.49.refs_7_.row_ref) | copy-start | bytes 786436
  65.3 31.9 %copy-start.30 = (bf16[16,384]{1,0:T(8,128)(2,1)}, bf16[16,384]{1,0:T(8,128)(2,1)S(1)}, u32[]{:S(2)}) copy-start(bf16[16,384]{1,0:T(8,128)(2,1)S(1)} %get-tuple-element.50.refs_9_.skip_ref) | copy-start | bytes 36868
  65.3 37.5 %copy-start.11 = (bf16[512,256]{1,0:T(8,128)(2,1)}, bf16[512,256]{1,0:T(8,128)(2,1)S(1)}, u32[]{:S(2)}) copy-start(bf16[512,256]{1,0:T(8,128)(2,1)S(1)} %get-tuple-element.42.refs_5_) | copy-start | bytes 786436
  65.3 37.5 %copy-start.25 = (f32[4,2560]{1,0:T(4,128)}, f32[4,2560]{1,0:T(4,128)S(1)}, u32[]{:S(2)}) copy-start(f32[4,2560]{1,0:T(4,128)S(1)} %get-tuple-element.39.refs_2_) | copy-start | bytes 122884
  70.4 13.7 %copy-start.19 = (bf16[512,896]{1,0:T(8,128)(2,1)}, bf16[512,896]{1,0:T(8,128)(2,1)S(1)}, u32[]{:S(2)}) copy-start(bf16[512,896]{1,0:T(8,128)(2,1)S(1)} %get-tuple-element.47.refs_5_) | copy-start | bytes 2752516
  70.4 13.7 %collective-permute-start.3 = (bf16[272,896]{1,0:T(8,128)(2,1)S(1)}, bf16[272,896]{1,0:T(8,128)(2,1)S(1)}, u32[]{:S(2)}, u32[]{:S(2)}) collective-permute-start(bf16[272,896]{1,0:T(8,128)(2,1)S(1)} %get-tuple-element.43.refs_4_.refs_1_), channel_id=1, source_target_pairs={{0,8},{1,9},{2,10},{3,11},{4,12},{5,13},{6,14},{7,15},{8,16},{9,17... | collective-permute-start | bytes 1462280 | tf_op jit(solution)/shard_map/ppermute | solution.py:614
  85.0 12.2 %collective-permute-start.4 = (bf16[272,896]{1,0:T(8,128)(2,1)}, bf16[272,896]{1,0:T(8,128)(2,1)}, u32[]{:S(2)}, u32[]{:S(2)}) collective-permute-start(bf16[272,896]{1,0:T(8,128)(2,1)} %combine.3.refs_10_), channel_id=1, source_target_pairs={{0,16},{1,17},{2,18},{3,19},{4,20},{5,21},{6,22},{7,23},{8,24},{9,... | collective-permute-start | bytes 1462280 | tf_op jit(solution)/shard_map/ppermute | solution.py:614
  86.3 30.3 %all-to-all-start = ((bf16[4,128,512]{2,1,0:T(8,128)(2,1)}), bf16[4,128,512]{2,1,0:T(8,128)(2,1)}, u32[]{:S(2)}, u32[]{:S(2)}) async-start(bf16[4,128,512]{2,1,0:T(8,128)(2,1)} %merge.5.refs_5_), calls=%async_computation | async-start | bytes 1048576 | tf_op jit(solution)/shard_map/all_to_all | solution.py:650
  102.8 12.5 %copy-start.13 = (bf16[256,896]{1,0:T(8,128)(2,1)}, bf16[256,896]{1,0:T(8,128)(2,1)S(1)}, u32[]{:S(2)}) copy-start(bf16[256,896]{1,0:T(8,128)(2,1)S(1)} %get-tuple-element.51.refs_6_.refs_0_) | copy-start | bytes 1376260
  102.8 12.5 %copy-start.37 = (bf16[256,896]{1,0:T(8,128)(2,1)}, bf16[256,896]{1,0:T(8,128)(2,1)S(1)}, u32[]{:S(2)}) copy-start(bf16[256,896]{1,0:T(8,128)(2,1)S(1)} %get-tuple-element.60) | copy-start | bytes 1376260
  102.8 12.5 %copy-start.9 = (f32[128,512]{1,0:T(8,128)S(1)}, f32[128,512]{1,0:T(8,128)}, u32[]{:S(2)}) copy-start(f32[128,512]{1,0:T(8,128)} %copy-done.8) | copy-start | bytes 786436
  102.8 12.5 %copy-start.31 = (bf16[16,384]{1,0:T(8,128)(2,1)S(1)}, bf16[16,384]{1,0:T(8,128)(2,1)}, u32[]{:S(2)}) copy-start(bf16[16,384]{1,0:T(8,128)(2,1)} %copy-done.30) | copy-start | bytes 36868
  104.7 10.6 %copy-start.23 = (f32[256,640]{1,0:T(8,128)}, f32[256,640]{1,0:T(8,128)S(1)}, u32[]{:S(2)}) copy-start(f32[256,640]{1,0:T(8,128)S(1)} %get-tuple-element.55.refs_2_) | copy-start | bytes 1966084
  104.7 8.9 %collective-permute-start.5 = (bf16[272,640]{1,0:T(8,128)(2,1)S(1)}, bf16[272,640]{1,0:T(8,128)(2,1)S(1)}, u32[]{:S(2)}, u32[]{:S(2)}) collective-permute-start(bf16[272,640]{1,0:T(8,128)(2,1)S(1)} %get-tuple-element.53.refs_1_), channel_id=1, source_target_pairs={{0,8},{1,9},{2,10},{3,11},{4,12},{5,13},{6,14},{7,15},{8,16},{9,17... | collective-permute-start | bytes 1044488 | tf_op jit(solution)/shard_map/ppermute | solution.py:614
  113.8 13.0 %collective-permute-start.7 = (bf16[272,640]{1,0:T(8,128)(2,1)S(1)}, bf16[272,640]{1,0:T(8,128)(2,1)}, u32[]{:S(2)}, u32[]{:S(2)}) collective-permute-start(bf16[272,640]{1,0:T(8,128)(2,1)S(1)} %combine.4.refs_0_), channel_id=1, source_target_pairs={{0,16},{1,17},{2,18},{3,19},{4,20},{5,21},{6,22},{7,23},{8,24},{9,... | collective-permute-start | bytes 1044488 | tf_op jit(solution)/shard_map/ppermute | solution.py:614
  117.4 4.6 %copy-start.38 = (bf16[256,896]{1,0:T(8,128)(2,1)S(1)}, bf16[256,896]{1,0:T(8,128)(2,1)}, u32[]{:S(2)}) copy-start(bf16[256,896]{1,0:T(8,128)(2,1)} %copy-done.37) | copy-start | bytes 1376260
  117.4 9.4 %copy-start.16 = (bf16[272,640]{1,0:T(8,128)(2,1)S(1)}, bf16[272,640]{1,0:T(8,128)(2,1)}, u32[]{:S(2)}) copy-start(bf16[272,640]{1,0:T(8,128)(2,1)} %copy-done.15) | copy-start | bytes 1044484
  117.4 9.4 %copy-start.24 = (f32[256,640]{1,0:T(8,128)S(1)}, f32[256,640]{1,0:T(8,128)}, u32[]{:S(2)}) copy-start(f32[256,640]{1,0:T(8,128)} %copy-done.23) | copy-start | bytes 1966084
  120.1 12.5 %collective-permute-start.6 = (bf16[272,512]{1,0:T(8,128)(2,1)S(1)}, bf16[272,512]{1,0:T(8,128)(2,1)S(1)}, u32[]{:S(2)}, u32[]{:S(2)}) collective-permute-start(bf16[272,512]{1,0:T(8,128)(2,1)S(1)} %get-tuple-element.54.refs_6_.refs_1_), channel_id=1, source_target_pairs={{0,8},{1,9},{2,10},{3,11},{4,12},{5,13},{6,14},{7,15},{8,16},{9,17... | collective-permute-start | bytes 835592 | tf_op jit(solution)/shard_map/ppermute | solution.py:614
  122.0 12.2 %collective-permute-start.10 = (bf16[256,896]{1,0:T(8,128)(2,1)S(1)}, bf16[256,896]{1,0:T(8,128)(2,1)S(1)}, u32[]{:S(2)}, u32[]{:S(2)}) collective-permute-start(bf16[256,896]{1,0:T(8,128)(2,1)S(1)} %copy-done.38), channel_id=1, source_target_pairs={{0,4},{1,5},{2,6},{3,7},{4,0},{5,1},{6,2},{7,3},{8,12},{9,13},{10,... | collective-permute-start | bytes 1376264 | tf_op jit(solution)/shard_map/ppermute | solution.py:614
  126.8 7.3 %copy-start.14 = (bf16[256,896]{1,0:T(8,128)(2,1)S(1)}, bf16[256,896]{1,0:T(8,128)(2,1)}, u32[]{:S(2)}) copy-start(bf16[256,896]{1,0:T(8,128)(2,1)} %copy-done.13) | copy-start | bytes 1376260
  128.5 8.2 %collective-permute-start.9 = (bf16[256,640]{1,0:T(8,128)(2,1)S(1)}, bf16[256,640]{1,0:T(8,128)(2,1)S(1)}, u32[]{:S(2)}, u32[]{:S(2)}) collective-permute-start(bf16[256,640]{1,0:T(8,128)(2,1)S(1)} %get-tuple-element.59), channel_id=1, source_target_pairs={{0,4},{1,5},{2,6},{3,7},{4,0},{5,1},{6,2},{7,3},{8,12},{9,13},{10,... | collective-permute-start | bytes 983048 | tf_op jit(solution)/shard_map/ppermute | solution.py:614
  132.7 8.6 %collective-permute-start.8 = (bf16[272,512]{1,0:T(8,128)(2,1)S(1)}, bf16[272,512]{1,0:T(8,128)(2,1)S(1)}, u32[]{:S(2)}, u32[]{:S(2)}) collective-permute-start(bf16[272,512]{1,0:T(8,128)(2,1)S(1)} %combine.5.refs_0_), channel_id=1, source_target_pairs={{0,16},{1,17},{2,18},{3,19},{4,20},{5,21},{6,22},{7,23},{8,24},{9,... | collective-permute-start | bytes 835592 | tf_op jit(solution)/shard_map/ppermute | solution.py:614
  144.0 3.7 %collective-permute-start.11 = (bf16[256,512]{1,0:T(8,128)(2,1)S(1)}, bf16[256,512]{1,0:T(8,128)(2,1)S(1)}, u32[]{:S(2)}, u32[]{:S(2)}) collective-permute-start(bf16[256,512]{1,0:T(8,128)(2,1)S(1)} %get-tuple-element.62), channel_id=1, source_target_pairs={{0,4},{1,5},{2,6},{3,7},{4,0},{5,1},{6,2},{7,3},{8,12},{9,13},{10,... | collective-permute-start | bytes 786440 | tf_op jit(solution)/shard_map/ppermute | solution.py:614
  (22 other events, 29.9 us)

commit v8 on v6

--- a/solution.py
+++ b/solution.py
@@ -555,7 +555,8 @@
 def place_kernel(firsts, place, *refs):
     count = len(firsts)
     keeps, gots = refs[:count], refs[count : 2 * count]
-    out, sems = refs[-2:]
+    out, token, sems = refs[-3:]
+    token[...] = jnp.zeros_like(token)
     core = place[2]
     half = out.shape[1] // PAIR
     copies = []
@@ -572,9 +573,9 @@
     count = len(firsts)
     return pl.pallas_call(
         functools.partial(place_kernel, firsts),
-        out_shape=jax.ShapeDtypeStruct(shape, BF16),
+        out_shape=[jax.ShapeDtypeStruct(shape, BF16), jax.ShapeDtypeStruct((8, LANES), F32)],
         in_specs=[smem] + [vmem] * (2 * count) + [hbm] * len(before),
-        out_specs=hbm,
+        out_specs=[hbm, vmem],
         input_output_aliases={2 * count + 1: 0} if before else {},
         scratch_shapes=[pltpu.SemaphoreType.DMA((2 * count,))],
         compiler_params=pltpu.CompilerParams(vmem_limit_bytes=16 << 20),
@@ -742,26 +743,30 @@
     shape = (BLOCK, PAIR * PER_GROUP)
     combine_of(0, [score])
     in_full(0, joined[0])
-    out = put_in_place([0], shape, place, keep[:1], [swap(send[0])], [])
-    order = [out]
-    for i in range(1, count):
-        state_of(i, order)
-        order = sent[i]
+    out, token = put_in_place([0], shape, place, keep[:1], [swap(send[0])], [])
     partial = {}
-    for i in range(1, count):
-        combine_of(i, order)
+
+    def local_of(i, order):
         (partial[i],) = call(
             functools.partial(local_kernel, first_head(i)),
             [(x[i].shape, F32)],
-            [x[i]] + mixes + [Stay(o) for o in joined[i]],
+            [x[i]] + mixes + [Stay(o) for o in order],
             name="local",
         )
-        order = [partial[i]]
+
+    state_of(1, [keep[0]])
+    state_of(2, sent[1])
+    state_of(3, sent[2])
+    combine_of(1, sent[3])
+    local_of(1, joined[1] + [token])
+    combine_of(2, [partial[1]])
+    local_of(2, joined[2])
+    local_of(3, [partial[2]])
+    combine_of(3, [partial[3]])
     for i in range(1, count):
-        finish_of(final_kernel, i, [partial[i]], order)
-        order = [keep[i]]
+        finish_of(final_kernel, i, [partial[i]], [keep[i - 1]] if i > 1 else joined[3])
     firsts = [first_head(i) * HEAD_DIM for i in range(1, count)]
-    return put_in_place(firsts, shape, place, keep[1:], [swap(o) for o in send[1:]], [out])
+    return put_in_place(firsts, shape, place, keep[1:], [swap(o) for o in send[1:]], [out])[0]
 
 
 def solution(mesh):

time: 153 us -> 132 us (0.86)
  waiting for transfers between devices: 82.7 us -> 63 us
  local copies, waits for them, and re-layouts: 4.19 us -> 2.6 us
    ppermute x24, waiting for transfers between devices: 82.7 us -> 63 us  [over(): lax.ppermute(block, axes, [(i, j) for i, j in route if j is not None and...]
    unnamed x16 -> x14, local copies, waits for them, and re-layouts: 4.11 us -> 2.52 us
  transfers between devices with their start and end apart: 24 -> 24, of which waited for: 18 -> 14; matrix products, arithmetic and copies ran while one was open for 0% -> 0% of each run, Pallas kernels for 9% -> 16%
where the time goes in v8:
time: 132 us; the launch traced here: 130 us
  waiting for transfers between devices  63 us (48%)
  starting transfers between devices  36.4 us (28%)
  Pallas kernels  27.7 us (21%)
  local copies, waits for them, and re-layouts  2.6 us (2%)
    ppermute x24, waiting for transfers between devices, over(): lax.ppermute(block, axes, [(i, j) for i, j in route if j is not None and...  63 us
    ppermute x24, starting transfers between devices, over(): lax.ppermute(block, axes, [(i, j) for i, j in route if j is not None and...  36.4 us
    pallas_call x23, Pallas kernels, call(): pl.pallas_call(body, out_shape=shapes, in_specs=specs, out_specs=[vmem] *...  24 us
    pallas_call x2, Pallas kernels, put_in_place(): pl.pallas_call(functools.partial(place_kernel, firsts), out_shape=[jax.Sh...  3.67 us
  transfers between devices with their start and end apart: 24, of which 14 were waited for; matrix products, arithmetic and copies ran while one was open for 0% of the time, Pallas kernels for 16%

profile of v8, /device:TPU:13, one launch (start us, length us, event | category | flops | bytes accessed | tf_op | source)
XLA Modules:
  0.0 130.2 jit_solution(586252179976237676)
XLA Ops:
  0.1 1.7 %copy-done = bf16[64,20480]{1,0:T(8,128)(2,1)S(1)} copy-done((bf16[64,20480]{1,0:T(8,128)(2,1)S(1)}, bf16[64,20480]{1,0:T(8,128)(2,1)}, u32[]{:S(2)}) %copy-start) | copy-done | bytes 2621464
  5.8 1.4 %collective-permute-done.got.order = bf16[64,10496]{1,0:T(8,128)(2,1)S(1)} collective-permute-done((bf16[64,10496]{1,0:T(8,128)(2,1)S(1)}, bf16[64,10496]{1,0:T(8,128)(2,1)S(1)}, u32[]{:S(2)}, u32[]{:S(2)}) %collective-permute-start) | collective-permute-done | bytes 1343520 | tf_op jit(solution)/shard_map/ppermute | solution.py:624
  8.6 5.8 %collective-permute-start.7 = (bf16[128,1408]{1,0:T(8,128)(2,1)S(1)}, bf16[128,1408]{1,0:T(8,128)(2,1)S(1)}, u32[]{:S(2)}, u32[]{:S(2)}) collective-permute-start(bf16[128,1408]{1,0:T(8,128)(2,1)S(1)} %get-tuple-element.60), channel_id=1, source_target_pairs={{0,3},{1,2},{2,1},{3,0},{4,7},{5,6},{6,5},{7,4},{8,11},{9,10},{10,... | collective-permute-start | bytes 1081352 | tf_op jit(solution)/shard_map/ppermute | solution.py:624
  15.6 2.2 %collective-permute-start.5 = (bf16[128,1280]{1,0:T(8,128)(2,1)S(1)}, bf16[128,1280]{1,0:T(8,128)(2,1)S(1)}, u32[]{:S(2)}, u32[]{:S(2)}) collective-permute-start(bf16[128,1280]{1,0:T(8,128)(2,1)S(1)} %get-tuple-element.57), channel_id=1, source_target_pairs={{0,3},{1,2},{2,1},{3,0},{4,7},{5,6},{6,5},{7,4},{8,11},{9,10},{10,... | collective-permute-start | bytes 983048 | tf_op jit(solution)/shard_map/ppermute | solution.py:624
  20.8 36.2 %collective-permute-done.6.refs_2_ = bf16[128,1408]{1,0:T(8,128)(2,1)S(1)} collective-permute-done((bf16[128,1408]{1,0:T(8,128)(2,1)S(1)}, bf16[128,1408]{1,0:T(8,128)(2,1)S(1)}, u32[]{:S(2)}, u32[]{:S(2)}) %collective-permute-start.6) | collective-permute-done | bytes 360480 | tf_op jit(solution)/shard_map/ppermute | solution.py:624
  57.0 1.7 %prep.1 = (bf16[512,256]{1,0:T(8,128)(2,1)S(1)}, f32[4,2560]{1,0:T(4,128)S(1)}, f32[512,128]{1,0:T(8,128)S(1)}, f32[128,512]{1,0:T(8,128)S(1)}, bf16[512,256]{1,...) custom-call(s32[5]{0:T(128)S(1)} %stack.23.place, ...), custom_call_target="tpu_custom_call" | custom-call | flops 1 | bytes 1 | tf_op jit(solution)/shard_map/prep/pallas_call | solution.py:599
  58.7 2.6 %state.4 = (bf16[512,768]{1,0:T(8,128)(2,1)S(1)}, f32[256,768]{1,0:T(8,128)S(1)}, bf16[272,256]{1,0:T(8,128)(2,1)S(1)}, bf16[272,256]{1,0:T(8,128)(2,1)S(1)}, bf16[272,256]{1,0:T(8,128)(2,1)S(1)}) custom-call(s32[5]{0:T(128)S(1)} %stack.23.place, bf16[128,2688]{1,0:T(8,128)(2,1)S(1)} %get-tuple-element.54.refs_0_, ...), custom_call_target="tpu_custom_call" | custom-call | flops 1 | bytes 1 | tf_op jit(solution)/shard_map/state/pallas_call | solution.py:599
  61.3 2.2 %collective-permute-start.8 = (bf16[272,256]{1,0:T(8,128)(2,1)S(1)}, bf16[272,256]{1,0:T(8,128)(2,1)S(1)}, u32[]{:S(2)}, u32[]{:S(2)}) collective-permute-start(bf16[272,256]{1,0:T(8,128)(2,1)S(1)} %get-tuple-element.65.refs_8_.refs_1_), channel_id=1, source_target_pairs={{0,8},{1,9},{2,10},{3,11},{4,12},{5,13},{6,14},{7,15},{8,16},{9,17... | collective-permute-start | bytes 417800 | tf_op jit(solution)/shard_map/ppermute | solution.py:624
  63.5 1.9 %collective-permute-start.9 = (bf16[272,256]{1,0:T(8,128)(2,1)S(1)}, bf16[272,256]{1,0:T(8,128)(2,1)S(1)}, u32[]{:S(2)}, u32[]{:S(2)}) collective-permute-start(bf16[272,256]{1,0:T(8,128)(2,1)S(1)} %get-tuple-element.66.refs_9_.refs_1_), channel_id=1, source_target_pairs={{0,8},{1,9},{2,10},{3,11},{4,12},{5,13},{6,14},{7,15},{8,16},{9,17... | collective-permute-start | bytes 417800 | tf_op jit(solution)/shard_map/ppermute | solution.py:624
  65.5 1.9 %collective-permute-start.10 = (bf16[272,256]{1,0:T(8,128)(2,1)S(1)}, bf16[272,256]{1,0:T(8,128)(2,1)S(1)}, u32[]{:S(2)}, u32[]{:S(2)}) collective-permute-start(bf16[272,256]{1,0:T(8,128)(2,1)S(1)} %get-tuple-element.67.refs_10_.refs_1_), channel_id=1, source_target_pairs={{0,8},{1,9},{2,10},{3,11},{4,12},{5,13},{6,14},{7,15},{8,16},{9,17... | collective-permute-start | bytes 417800 | tf_op jit(solution)/shard_map/ppermute | solution.py:624
  68.6 1.3 collective-permute-start.11
  70.3 1.3 collective-permute-start.12
  72.2 1.3 collective-permute-start.13
  73.5 4.5 %collective-permute-done.11.refs_3_ = bf16[272,256]{1,0:T(8,128)(2,1)S(1)} collective-permute-done((bf16[272,256]{1,0:T(8,128)(2,1)S(1)}, bf16[272,256]{1,0:T(8,128)(2,1)S(1)}, u32[]{:S(2)}, u32[]{:S(2)}) %collective-permute-start.11) | collective-permute-done | bytes 139296 | tf_op jit(solution)/shard_map/ppermute | solution.py:624
  78.1 2.3 %collective-permute-done.12.refs_4_ = bf16[272,256]{1,0:T(8,128)(2,1)S(1)} collective-permute-done((bf16[272,256]{1,0:T(8,128)(2,1)S(1)}, bf16[272,256]{1,0:T(8,128)(2,1)S(1)}, u32[]{:S(2)}, u32[]{:S(2)}) %collective-permute-start.12) | collective-permute-done | bytes 139296 | tf_op jit(solution)/shard_map/ppermute | solution.py:624
  80.4 3.2 %collective-permute-done.13.refs_5_ = bf16[272,256]{1,0:T(8,128)(2,1)S(1)} collective-permute-done((bf16[272,256]{1,0:T(8,128)(2,1)S(1)}, bf16[272,256]{1,0:T(8,128)(2,1)S(1)}, u32[]{:S(2)}, u32[]{:S(2)}) %collective-permute-start.13) | collective-permute-done | bytes 139296 | tf_op jit(solution)/shard_map/ppermute | solution.py:624
  83.6 2.5 %final.4 = (bf16[256,768]{1,0:T(8,128)(2,1)S(1)}, bf16[256,768]{1,0:T(8,128)(2,1)S(1)}) custom-call(s32[5]{0:T(128)S(1)} %stack.23.place, bf16[272,256]{1,0:T(8,128)(2,1)S(1)} %collective-permute-done.8.refs_0_, bf16[272,256]{1,0:T(8,128)(2,1)S(1)} %collective-permute-done.9.refs_0_.refs_1_, bf16[272,256]{1,0:T(8,128)(2,1)S(1)} %collective-permute-done.10.refs_0_.refs_2_, ...), custom_call_target="tpu_custom_call" | custom-call | flops 1 | bytes 1 | tf_op jit(solution)/shard_map/final/pallas_call | solution.py:599
  86.1 2.1 %state.5 = (bf16[512,512]{1,0:T(8,128)(2,1)S(1)}, f32[256,512]{1,0:T(8,128)S(1)}, bf16[272,512]{1,0:T(8,128)(2,1)S(1)}) custom-call(s32[5]{0:T(128)S(1)} %stack.23.place, bf16[128,2688]{1,0:T(8,128)(2,1)S(1)} %get-tuple-element.54.refs_0_, bf16[128,2688]{1,0:T(8,128)(2,1)S(1)} %collective-permute-done.3.refs_1_, ...), custom_call_target="tpu_custom_call" | custom-call | flops 1 | bytes 1 | tf_op jit(solution)/shard_map/state/pallas_call | solution.py:599
  88.2 1.9 %collective-permute-start.14 = (bf16[272,512]{1,0:T(8,128)(2,1)S(1)}, bf16[272,512]{1,0:T(8,128)(2,1)S(1)}, u32[]{:S(2)}, u32[]{:S(2)}) collective-permute-start(bf16[272,512]{1,0:T(8,128)(2,1)S(1)} %get-tuple-element.76.refs_10_.refs_1_), channel_id=1, source_target_pairs={{0,8},{1,9},{2,10},{3,11},{4,12},{5,13},{6,14},{7,15},{8,16},{9,17... | collective-permute-start | bytes 835592 | tf_op jit(solution)/shard_map/ppermute | solution.py:624
  90.1 3.6 %collective-permute-start.16 = (bf16[256,768]{1,0:T(8,128)(2,1)S(1)}, bf16[256,768]{1,0:T(8,128)(2,1)S(1)}, u32[]{:S(2)}, u32[]{:S(2)}) collective-permute-start(bf16[256,768]{1,0:T(8,128)(2,1)S(1)} %get-tuple-element.81), channel_id=1, source_target_pairs={{0,4},{1,5},{2,6},{3,7},{4,0},{5,1},{6,2},{7,3},{8,12},{9,13},{10,... | collective-permute-start | bytes 1179656 | tf_op jit(solution)/shard_map/ppermute | solution.py:624
  93.7 1.9 %state.6 = (bf16[512,384]{1,0:T(8,128)(2,1)S(1)}, f32[256,384]{1,0:T(8,128)S(1)}, bf16[272,384]{1,0:T(8,128)(2,1)S(1)}) custom-call(s32[5]{0:T(128)S(1)} %stack.23.place, bf16[128,2688]{1,0:T(8,128)(2,1)S(1)} %get-tuple-element.54.refs_0_, bf16[128,2688]{1,0:T(8,128)(2,1)S(1)} %collective-permute-done.3.refs_1_, ...), custom_call_target="tpu_custom_call" | custom-call | flops 1 | bytes 1 | tf_op jit(solution)/shard_map/state/pallas_call | solution.py:599
  95.6 2.1 %collective-permute-start.18 = (bf16[272,384]{1,0:T(8,128)(2,1)S(1)}, bf16[272,384]{1,0:T(8,128)(2,1)S(1)}, u32[]{:S(2)}, u32[]{:S(2)}) collective-permute-start(bf16[272,384]{1,0:T(8,128)(2,1)S(1)} %get-tuple-element.77.refs_10_.refs_1_), channel_id=1, source_target_pairs={{0,8},{1,9},{2,10},{3,11},{4,12},{5,13},{6,14},{7,15},{8,16},{9,17... | collective-permute-start | bytes 626696 | tf_op jit(solution)/shard_map/ppermute | solution.py:624
  97.7 1.9 %state.7 = (bf16[512,384]{1,0:T(8,128)(2,1)S(1)}, f32[256,384]{1,0:T(8,128)S(1)}, bf16[272,384]{1,0:T(8,128)(2,1)S(1)}) custom-call(s32[5]{0:T(128)S(1)} %stack.23.place, bf16[128,2688]{1,0:T(8,128)(2,1)S(1)} %get-tuple-element.54.refs_0_, bf16[128,2688]{1,0:T(8,128)(2,1)S(1)} %collective-permute-done.3.refs_1_, ...), custom_call_target="tpu_custom_call" | custom-call | flops 1 | bytes 1 | tf_op jit(solution)/shard_map/state/pallas_call | solution.py:599
  99.6 1.9 %collective-permute-start.17 = (bf16[272,384]{1,0:T(8,128)(2,1)S(1)}, bf16[272,384]{1,0:T(8,128)(2,1)S(1)}, u32[]{:S(2)}, u32[]{:S(2)}) collective-permute-start(bf16[272,384]{1,0:T(8,128)(2,1)S(1)} %get-tuple-element.78.refs_2_.refs_1_), channel_id=1, source_target_pairs={{0,8},{1,9},{2,10},{3,11},{4,12},{5,13},{6,14},{7,15},{8,16},{9,17... | collective-permute-start | bytes 626696 | tf_op jit(solution)/shard_map/ppermute | solution.py:624
  103.0 1.4 %place.2 = (bf16[256,4096]{1,0:T(8,128)(2,1)}, f32[8,128]{1,0:T(8,128)S(1)}) custom-call(s32[5]{0:T(128)S(1)} %stack.23.place, bf16[256,768]{1,0:T(8,128)(2,1)S(1)} %get-tuple-element.75.refs_10_.refs_0_, bf16[256,768]{1,0:T(8,128)(2,1)S(1)} %collective-permute-done.16.refs_1_), custom_call_target="tpu_custom_call" | custom-call | flops 1 | bytes 1 | tf_op jit(solution)/shard_map/place/pallas_call | solution.py:574
  105.7 1.3 collective-permute-start.19
  108.6 1.6 %collective-permute-done.17.refs_0_ = bf16[272,384]{1,0:T(8,128)(2,1)S(1)} collective-permute-done((bf16[272,384]{1,0:T(8,128)(2,1)S(1)}, bf16[272,384]{1,0:T(8,128)(2,1)S(1)}, u32[]{:S(2)}, u32[]{:S(2)}) %collective-permute-start.17) | collective-permute-done | bytes 208928 | tf_op jit(solution)/shard_map/ppermute | solution.py:624
  110.3 1.3 collective-permute-start.20
  111.6 4.7 %collective-permute-done.15.refs_1_ = bf16[272,512]{1,0:T(8,128)(2,1)S(1)} collective-permute-done((bf16[272,512]{1,0:T(8,128)(2,1)S(1)}, bf16[272,512]{1,0:T(8,128)(2,1)S(1)}, u32[]{:S(2)}, u32[]{:S(2)}) %collective-permute-start.15) | collective-permute-done | bytes 278560 | tf_op jit(solution)/shard_map/ppermute | solution.py:624
  117.9 2.8 %collective-permute-done.19.refs_1_ = bf16[272,384]{1,0:T(8,128)(2,1)S(1)} collective-permute-done((bf16[272,384]{1,0:T(8,128)(2,1)S(1)}, bf16[272,384]{1,0:T(8,128)(2,1)S(1)}, u32[]{:S(2)}, u32[]{:S(2)}) %collective-permute-start.19) | collective-permute-done | bytes 208928 | tf_op jit(solution)/shard_map/ppermute | solution.py:624
  122.3 2.9 %collective-permute-done.20.refs_1_ = bf16[272,384]{1,0:T(8,128)(2,1)S(1)} collective-permute-done((bf16[272,384]{1,0:T(8,128)(2,1)S(1)}, bf16[272,384]{1,0:T(8,128)(2,1)S(1)}, u32[]{:S(2)}, u32[]{:S(2)}) %collective-permute-start.20) | collective-permute-done | bytes 208928 | tf_op jit(solution)/shard_map/ppermute | solution.py:624
  127.8 2.2 %place.3 = (bf16[256,4096]{1,0:T(8,128)(2,1)}, f32[8,128]{1,0:T(8,128)}) custom-call(s32[5]{0:T(128)S(1)} %stack.23.place, bf16[256,512]{1,0:T(8,128)(2,1)S(1)} %get-tuple-element.85.refs_6_.refs_0_, bf16[256,384]{1,0:T(8,128)(2,1)S(1)} %get-tuple-element.87.refs_6_.refs_1_, ...), custom_call_target="tpu_custom_call", output_to_operand_aliasing={{0}: (7, {})} | custom-call | flops 1 | bytes 1 | tf_op jit(solution)/shard_map/place/pallas_call | solution.py:574
  (56 shorter events, 22.1 us)
Async XLA Ops:
  0.1 1.7 %copy-start = (bf16[64,20480]{1,0:T(8,128)(2,1)S(1)}, bf16[64,20480]{1,0:T(8,128)(2,1)}, u32[]{:S(2)}) copy-start(bf16[64,20480]{1,0:T(8,128)(2,1)} %xbc.5) | copy-start | bytes 7864324
  1.8 0.8 copy-start.2
  3.7 3.4 %collective-permute-start = (bf16[64,10496]{1,0:T(8,128)(2,1)S(1)}, bf16[64,10496]{1,0:T(8,128)(2,1)S(1)}, u32[]{:S(2)}, u32[]{:S(2)}) collective-permute-start(bf16[64,10496]{1,0:T(8,128)(2,1)S(1)} %get-tuple-element.50), channel_id=1, source_target_pairs={{0,4},{1,5},{2,6},{3,7},{4,0},{5,1},{6,2},{7,3},{8,12},{9,13},{10,... | collective-permute-start | bytes 4030472 | tf_op jit(solution)/shard_map/ppermute | solution.py:624
  4.4 1.3 %collective-permute-start.1 = (bf16[3,10240]{1,0:T(4,128)(2,1)S(1)}, bf16[3,10240]{1,0:T(4,128)(2,1)S(1)}, u32[]{:S(2)}, u32[]{:S(2)}) collective-permute-start(bf16[3,10240]{1,0:T(4,128)(2,1)S(1)} %get-tuple-element.51), channel_id=1, source_target_pairs={{7,15},{15,23},{23,31}} | collective-permute-start | bytes 184328 | tf_op jit(solution)/shard_map/ppermute | solution.py:624
  5.1 0.7 collective-permute-start.2
  8.3 48.7 %collective-permute-start.3 = (bf16[128,2688]{1,0:T(8,128)(2,1)S(1)}, bf16[128,2688]{1,0:T(8,128)(2,1)S(1)}, u32[]{:S(2)}, u32[]{:S(2)}) collective-permute-start(bf16[128,2688]{1,0:T(8,128)(2,1)S(1)} %get-tuple-element.55), channel_id=1, source_target_pairs={{0,1},{1,0},{2,3},{3,2},{4,5},{5,4},{6,7},{7,6},{8,9},{9,8},{10,11... | collective-permute-start | bytes 2064392 | tf_op jit(solution)/shard_map/ppermute | solution.py:624
  8.6 12.2 %collective-permute-start.7 = (bf16[128,1408]{1,0:T(8,128)(2,1)S(1)}, bf16[128,1408]{1,0:T(8,128)(2,1)S(1)}, u32[]{:S(2)}, u32[]{:S(2)}) collective-permute-start(bf16[128,1408]{1,0:T(8,128)(2,1)S(1)} %get-tuple-element.60), channel_id=1, source_target_pairs={{0,3},{1,2},{2,1},{3,0},{4,7},{5,6},{6,5},{7,4},{8,11},{9,10},{10,... | collective-permute-start | bytes 1081352 | tf_op jit(solution)/shard_map/ppermute | solution.py:624
  14.4 4.5 %copy-start.1 = (f32[4,20480]{1,0:T(4,128)S(1)}, f32[4,20480]{1,0:T(4,128)}, u32[]{:S(2)}) copy-start(f32[4,20480]{1,0:T(4,128)} %weight.1) | copy-start | bytes 983044
  14.4 4.5 %copy-start.3 = (f32[20480]{0:T(1024)S(1)}, f32[20480]{0:T(1024)}, u32[]{:S(2)}) copy-start(f32[20480]{0:T(1024)} %param.10) | copy-start | bytes 245764
  14.4 42.7 %copy-start.4 = (f32[256]{0:T(256)S(1)}, f32[256]{0:T(256)}, u32[]{:S(2)}) copy-start(f32[256]{0:T(256)} %param.11) | copy-start | bytes 3076
  14.4 42.7 %copy-start.5 = (f32[256]{0:T(256)S(1)}, f32[256]{0:T(256)}, u32[]{:S(2)}) copy-start(f32[256]{0:T(256)} %param.12) | copy-start | bytes 3076
  14.4 42.7 %copy-start.6 = (f32[256]{0:T(256)S(1)}, f32[256]{0:T(256)}, u32[]{:S(2)}) copy-start(f32[256]{0:T(256)} %param.13) | copy-start | bytes 3076
  14.4 42.6 %collective-permute-start.6 = (bf16[128,1408]{1,0:T(8,128)(2,1)S(1)}, bf16[128,1408]{1,0:T(8,128)(2,1)S(1)}, u32[]{:S(2)}, u32[]{:S(2)}) collective-permute-start(bf16[128,1408]{1,0:T(8,128)(2,1)S(1)} %get-tuple-element.53.refs_0_), channel_id=1, source_target_pairs={{0,2},{1,3},{2,0},{3,1},{4,6},{5,7},{6,4},{7,5},{8,10},{9,11},{10,... | collective-permute-start | bytes 1081352 | tf_op jit(solution)/shard_map/ppermute | solution.py:624
  15.6 70.6 %collective-permute-start.5 = (bf16[128,1280]{1,0:T(8,128)(2,1)S(1)}, bf16[128,1280]{1,0:T(8,128)(2,1)S(1)}, u32[]{:S(2)}, u32[]{:S(2)}) collective-permute-start(bf16[128,1280]{1,0:T(8,128)(2,1)S(1)} %get-tuple-element.57), channel_id=1, source_target_pairs={{0,3},{1,2},{2,1},{3,0},{4,7},{5,6},{6,5},{7,4},{8,11},{9,10},{10,... | collective-permute-start | bytes 983048 | tf_op jit(solution)/shard_map/ppermute | solution.py:624
  17.8 68.4 %collective-permute-start.4 = (bf16[128,1280]{1,0:T(8,128)(2,1)S(1)}, bf16[128,1280]{1,0:T(8,128)(2,1)S(1)}, u32[]{:S(2)}, u32[]{:S(2)}) collective-permute-start(bf16[128,1280]{1,0:T(8,128)(2,1)S(1)} %get-tuple-element.56.refs_9_), channel_id=1, source_target_pairs={{0,2},{1,3},{2,0},{3,1},{4,6},{5,7},{6,4},{7,5},{8,10},{9,11},{10,... | collective-permute-start | bytes 983048 | tf_op jit(solution)/shard_map/ppermute | solution.py:624
  61.3 7.2 %collective-permute-start.8 = (bf16[272,256]{1,0:T(8,128)(2,1)S(1)}, bf16[272,256]{1,0:T(8,128)(2,1)S(1)}, u32[]{:S(2)}, u32[]{:S(2)}) collective-permute-start(bf16[272,256]{1,0:T(8,128)(2,1)S(1)} %get-tuple-element.65.refs_8_.refs_1_), channel_id=1, source_target_pairs={{0,8},{1,9},{2,10},{3,11},{4,12},{5,13},{6,14},{7,15},{8,16},{9,17... | collective-permute-start | bytes 417800 | tf_op jit(solution)/shard_map/ppermute | solution.py:624
  63.5 6.7 %collective-permute-start.9 = (bf16[272,256]{1,0:T(8,128)(2,1)S(1)}, bf16[272,256]{1,0:T(8,128)(2,1)S(1)}, u32[]{:S(2)}, u32[]{:S(2)}) collective-permute-start(bf16[272,256]{1,0:T(8,128)(2,1)S(1)} %get-tuple-element.66.refs_9_.refs_1_), channel_id=1, source_target_pairs={{0,8},{1,9},{2,10},{3,11},{4,12},{5,13},{6,14},{7,15},{8,16},{9,17... | collective-permute-start | bytes 417800 | tf_op jit(solution)/shard_map/ppermute | solution.py:624
  65.5 6.7 %collective-permute-start.10 = (bf16[272,256]{1,0:T(8,128)(2,1)S(1)}, bf16[272,256]{1,0:T(8,128)(2,1)S(1)}, u32[]{:S(2)}, u32[]{:S(2)}) collective-permute-start(bf16[272,256]{1,0:T(8,128)(2,1)S(1)} %get-tuple-element.67.refs_10_.refs_1_), channel_id=1, source_target_pairs={{0,8},{1,9},{2,10},{3,11},{4,12},{5,13},{6,14},{7,15},{8,16},{9,17... | collective-permute-start | bytes 417800 | tf_op jit(solution)/shard_map/ppermute | solution.py:624
  68.6 9.5 %collective-permute-start.11 = (bf16[272,256]{1,0:T(8,128)(2,1)S(1)}, bf16[272,256]{1,0:T(8,128)(2,1)S(1)}, u32[]{:S(2)}, u32[]{:S(2)}) collective-permute-start(bf16[272,256]{1,0:T(8,128)(2,1)S(1)} %combine.6.refs_2_.refs_14_), channel_id=1, source_target_pairs={{0,16},{1,17},{2,18},{3,19},{4,20},{5,21},{6,22},{7,23},{8,24},{9,... | collective-permute-start | bytes 417800 | tf_op jit(solution)/shard_map/ppermute | solution.py:624
  70.3 10.1 %collective-permute-start.12 = (bf16[272,256]{1,0:T(8,128)(2,1)S(1)}, bf16[272,256]{1,0:T(8,128)(2,1)S(1)}, u32[]{:S(2)}, u32[]{:S(2)}) collective-permute-start(bf16[272,256]{1,0:T(8,128)(2,1)S(1)} %combine.7.refs_2_.refs_15_), channel_id=1, source_target_pairs={{0,16},{1,17},{2,18},{3,19},{4,20},{5,21},{6,22},{7,23},{8,24},{9,... | collective-permute-start | bytes 417800 | tf_op jit(solution)/shard_map/ppermute | solution.py:624
  72.2 11.4 %collective-permute-start.13 = (bf16[272,256]{1,0:T(8,128)(2,1)S(1)}, bf16[272,256]{1,0:T(8,128)(2,1)S(1)}, u32[]{:S(2)}, u32[]{:S(2)}) collective-permute-start(bf16[272,256]{1,0:T(8,128)(2,1)S(1)} %combine.8.refs_16_), channel_id=1, source_target_pairs={{0,16},{1,17},{2,18},{3,19},{4,20},{5,21},{6,22},{7,23},{8,24},{9,... | collective-permute-start | bytes 417800 | tf_op jit(solution)/shard_map/ppermute | solution.py:624
  88.2 13.3 %collective-permute-start.14 = (bf16[272,512]{1,0:T(8,128)(2,1)S(1)}, bf16[272,512]{1,0:T(8,128)(2,1)S(1)}, u32[]{:S(2)}, u32[]{:S(2)}) collective-permute-start(bf16[272,512]{1,0:T(8,128)(2,1)S(1)} %get-tuple-element.76.refs_10_.refs_1_), channel_id=1, source_target_pairs={{0,8},{1,9},{2,10},{3,11},{4,12},{5,13},{6,14},{7,15},{8,16},{9,17... | collective-permute-start | bytes 835592 | tf_op jit(solution)/shard_map/ppermute | solution.py:624
  90.1 12.8 %collective-permute-start.16 = (bf16[256,768]{1,0:T(8,128)(2,1)S(1)}, bf16[256,768]{1,0:T(8,128)(2,1)S(1)}, u32[]{:S(2)}, u32[]{:S(2)}) collective-permute-start(bf16[256,768]{1,0:T(8,128)(2,1)S(1)} %get-tuple-element.81), channel_id=1, source_target_pairs={{0,4},{1,5},{2,6},{3,7},{4,0},{5,1},{6,2},{7,3},{8,12},{9,13},{10,... | collective-permute-start | bytes 1179656 | tf_op jit(solution)/shard_map/ppermute | solution.py:624
  95.6 10.1 %collective-permute-start.18 = (bf16[272,384]{1,0:T(8,128)(2,1)S(1)}, bf16[272,384]{1,0:T(8,128)(2,1)S(1)}, u32[]{:S(2)}, u32[]{:S(2)}) collective-permute-start(bf16[272,384]{1,0:T(8,128)(2,1)S(1)} %get-tuple-element.77.refs_10_.refs_1_), channel_id=1, source_target_pairs={{0,8},{1,9},{2,10},{3,11},{4,12},{5,13},{6,14},{7,15},{8,16},{9,17... | collective-permute-start | bytes 626696 | tf_op jit(solution)/shard_map/ppermute | solution.py:624
  99.6 10.6 %collective-permute-start.17 = (bf16[272,384]{1,0:T(8,128)(2,1)S(1)}, bf16[272,384]{1,0:T(8,128)(2,1)S(1)}, u32[]{:S(2)}, u32[]{:S(2)}) collective-permute-start(bf16[272,384]{1,0:T(8,128)(2,1)S(1)} %get-tuple-element.78.refs_2_.refs_1_), channel_id=1, source_target_pairs={{0,8},{1,9},{2,10},{3,11},{4,12},{5,13},{6,14},{7,15},{8,16},{9,17... | collective-permute-start | bytes 626696 | tf_op jit(solution)/shard_map/ppermute | solution.py:624
  101.7 14.6 %collective-permute-start.15 = (bf16[272,512]{1,0:T(8,128)(2,1)S(1)}, bf16[272,512]{1,0:T(8,128)(2,1)S(1)}, u32[]{:S(2)}, u32[]{:S(2)}) collective-permute-start(bf16[272,512]{1,0:T(8,128)(2,1)S(1)} %combine.9.refs_0_), channel_id=1, source_target_pairs={{0,16},{1,17},{2,18},{3,19},{4,20},{5,21},{6,22},{7,23},{8,24},{9,... | collective-permute-start | bytes 835592 | tf_op jit(solution)/shard_map/ppermute | solution.py:624
  105.7 15.0 %collective-permute-start.19 = (bf16[272,384]{1,0:T(8,128)(2,1)S(1)}, bf16[272,384]{1,0:T(8,128)(2,1)S(1)}, u32[]{:S(2)}, u32[]{:S(2)}) collective-permute-start(bf16[272,384]{1,0:T(8,128)(2,1)S(1)} %combine.10.refs_0_), channel_id=1, source_target_pairs={{0,16},{1,17},{2,18},{3,19},{4,20},{5,21},{6,22},{7,23},{8,24},{9,... | collective-permute-start | bytes 626696 | tf_op jit(solution)/shard_map/ppermute | solution.py:624
  110.3 14.9 %collective-permute-start.20 = (bf16[272,384]{1,0:T(8,128)(2,1)S(1)}, bf16[272,384]{1,0:T(8,128)(2,1)S(1)}, u32[]{:S(2)}, u32[]{:S(2)}) collective-permute-start(bf16[272,384]{1,0:T(8,128)(2,1)S(1)} %combine.11.refs_6_), channel_id=1, source_target_pairs={{0,16},{1,17},{2,18},{3,19},{4,20},{5,21},{6,22},{7,23},{8,24},{9,... | collective-permute-start | bytes 626696 | tf_op jit(solution)/shard_map/ppermute | solution.py:624
  117.4 10.5 %collective-permute-start.21 = (bf16[256,512]{1,0:T(8,128)(2,1)S(1)}, bf16[256,512]{1,0:T(8,128)(2,1)S(1)}, u32[]{:S(2)}, u32[]{:S(2)}) collective-permute-start(bf16[256,512]{1,0:T(8,128)(2,1)S(1)} %get-tuple-element.90), channel_id=1, source_target_pairs={{0,4},{1,5},{2,6},{3,7},{4,0},{5,1},{6,2},{7,3},{8,12},{9,13},{10,... | collective-permute-start | bytes 786440 | tf_op jit(solution)/shard_map/ppermute | solution.py:624
  121.8 5.0 %collective-permute-start.22 = (bf16[256,384]{1,0:T(8,128)(2,1)S(1)}, bf16[256,384]{1,0:T(8,128)(2,1)S(1)}, u32[]{:S(2)}, u32[]{:S(2)}) collective-permute-start(bf16[256,384]{1,0:T(8,128)(2,1)S(1)} %get-tuple-element.91), channel_id=1, source_target_pairs={{0,4},{1,5},{2,6},{3,7},{4,0},{5,1},{6,2},{7,3},{8,12},{9,13},{10,... | collective-permute-start | bytes 589832 | tf_op jit(solution)/shard_map/ppermute | solution.py:624
  126.3 1.6 %collective-permute-start.23 = (bf16[256,384]{1,0:T(8,128)(2,1)S(1)}, bf16[256,384]{1,0:T(8,128)(2,1)S(1)}, u32[]{:S(2)}, u32[]{:S(2)}) collective-permute-start(bf16[256,384]{1,0:T(8,128)(2,1)S(1)} %get-tuple-element.92), channel_id=1, source_target_pairs={{0,4},{1,5},{2,6},{3,7},{4,0},{5,1},{6,2},{7,3},{8,12},{9,13},{10,... | collective-permute-start | bytes 589832 | tf_op jit(solution)/shard_map/ppermute | solution.py:624

commit v9 on v5

--- a/solution.py
+++ b/solution.py
@@ -168,6 +168,7 @@
 GROUPED = ((0, 0, 512), (2, 0, 768), (3, 0, 384), (3, 384, 384))
 FIRST_ROUND = ((256, 256), (384, 384), (384,), (384,))
 SECOND_ROUND = ((512,), (384, 384), (384,), (384,))
+ALONE = (2, 3)
 
 
 def halves(value, count):
@@ -229,7 +230,7 @@
         copy.wait()
 
 
-def pack_kernel(shards, place, xbc, dt_raw, weight, bias, order, send, taps, offset, tail, sems):
+def pack_kernel(shards, place, xbc, dt_raw, order, send, tail, sems):
     core, shard = place[2], place[4]
     count = xbc.shape[0]
     first = WIDTHS[0]
@@ -244,14 +245,25 @@
             to = rest + (i * shards + r) * STATE
             copies.append((xbc.at[:, ds(INNER + (i * GROUPS + group) * STATE, STATE)], send.at[:, to : to + STATE]))
     copies.append((dt_raw, send.at[:, send.shape[1] - HEADS :]))
-    everything = [(weight, taps, place[0], 0), (bias, offset, place[0], 0)]
     for r in range(shards):
-        everything.append((xbc.at[count - 16 :], tail, (shard ^ r) * PAIR + core, r * size))
-    for source, target, group, to in everything:
-        copies.append((source.at[:, channels(group, 0, PER_GROUP)], target.at[:, to : to + PER_GROUP]))
+        group, to = (shard ^ r) * PAIR + core, r * size
+        last = xbc.at[count - 16 :]
+        copies.append((last.at[:, channels(group, 0, PER_GROUP)], tail.at[:, to : to + PER_GROUP]))
         for i in range(2):
             at = ds(INNER + (i * GROUPS + group) * STATE, STATE)
             start = to + PER_GROUP + i * STATE
+            copies.append((last.at[:, at], tail.at[:, start : start + STATE]))
+    for copy in run(copies, sems):
+        copy.wait()
+
+
+def taps_kernel(place, weight, bias, order, taps, offset, sems):
+    copies = []
+    for source, target in ((weight, taps), (bias, offset)):
+        copies.append((source.at[:, channels(place[0], 0, PER_GROUP)], target.at[:, :PER_GROUP]))
+        for i in range(2):
+            at = ds(INNER + (i * GROUPS + place[0]) * STATE, STATE)
+            start = PER_GROUP + i * STATE
             copies.append((source.at[:, at], target.at[:, start : start + STATE]))
     for copy in run(copies, sems):
         copy.wait()
@@ -341,14 +353,18 @@
         copy.wait()
 
 
+def view(refs, piece):
+    return [(ref, 0) for ref in refs]
+
+
 def convolve_in_order(place, blocks, columns, edge, tap, bias, wide, put):
     width = columns.stop - columns.start
-    count = blocks[0].shape[0] // PAIR
+    count = blocks[0][0].shape[0] // PAIR
     wide[5:8, :width] = edge
-    for r, block in enumerate(blocks):
+    for r, (block, origin) in enumerate(blocks):
         for core in range(PAIR):
             at = pl.multiple_of((core * len(blocks) + (place[4] ^ r)) * count + 8, 8)
-            part = block[core * count : (core + 1) * count, columns]
+            part = block[core * count : (core + 1) * count, origin + columns.start : origin + columns.stop]
             wide[pl.ds(at, count), :width] = part.astype(F32)
     tap, bias = tap * 0.5, bias * 0.5
     for start in range(0, PAIR * len(blocks) * count, count):
@@ -362,12 +378,13 @@
 def prep_kernel(shards, place, *refs):
     blocks, (taps, offset, a_ref, bias_ref, skip_ref, order) = refs[:shards], refs[shards : shards + 6]
     b_ref, edge_ref, cum_ref, row_ref, factor_ref, tail_ref, skip_out, dt_ref, wide = refs[shards + 6 :]
+    blocks = view(blocks, 1)
     start = WIDTHS[1]
     last = total_of(1) - LANES
     size = edge_ref.shape[1]
-    count = blocks[0].shape[0] // PAIR
+    count = blocks[0][0].shape[0] // PAIR
     half, heads = count // 2, HEADS // GROUPS
-    columns = [block[:, last : last + LANES].astype(F32) for block in blocks]
+    columns = [block[:, origin + last : origin + last + LANES].astype(F32) for block, origin in blocks]
     edge = columns[0][half : half + 4 * size // LANES]
     for column in columns[1:]:
         edge = edge + column[half : half + 4 * size // LANES]
@@ -421,6 +438,7 @@
 def score_kernel(shards, place, *refs):
     blocks, refs = refs[:shards], refs[shards:]
     taps, offset, edge_ref, b_ref, c_ref, score_ref, wide = (*refs[:4], *refs[-3:])
+    blocks = view(blocks, 3)
     start = WIDTHS[3]
     at = slice(PER_GROUP + STATE, PER_GROUP + 2 * STATE)
 
@@ -460,6 +478,7 @@
     def put(row, count, value):
         x_ref[row : row + count] = value
 
+    blocks = view(blocks, piece)
     columns = slice(start, start + width)
     convolve_in_order(place, blocks, columns, edge_ref[0:3, at], taps[:, at], offset[:, at], wide, put)
     expand = spread(first // HEAD_DIM, width, 2)
@@ -536,13 +555,15 @@
     mix(first_head, x_ref, cum_ref, row_ref, score_ref, skip_ref, put)
 
 
-def carry(first_head, core, lasts, befores, own_ref, c_ref, factor_ref, add, keep_ref, send_ref):
+def carry(first_head, core, lasts, befores, alones, own_ref, c_ref, factor_ref, add, keep_ref, send_ref):
     expand = spread(first_head, own_ref.shape[1], 2)
     last, before = (
         refs[0][...] if len(refs) == 1 else jnp.concatenate([ref[...] for ref in refs], 1)
         for refs in (lasts, befores)
     )
     held = last[:STATE].astype(F32) + decay_of(last) * before[:STATE].astype(F32)
+    for alone in alones:
+        held = held + alone[:STATE].astype(F32)
     factor = dot(factor_ref[...], expand)
     outs = []
     for block in range(PAIR):
@@ -562,47 +583,53 @@
         send_ref[...] = outs[0]
 
 
-def final_kernel(first_head, lasts, befores, place, *refs):
-    last, refs = refs[:lasts], refs[lasts:]
-    before, refs = refs[:befores], refs[befores:]
-    carry(first_head, place[2], last, before, *refs[:4], *refs[-2:])
-
-
-def finish_kernel(first_head, lasts, befores, place, *refs):
-    last, refs = refs[:lasts], refs[lasts:]
-    before, refs = refs[:befores], refs[befores:]
+def final_kernel(first_head, counts, place, *refs):
+    groups = []
+    for number in counts:
+        groups.append(refs[:number])
+        refs = refs[number:]
+    carry(first_head, place[2], *groups, *refs[:4], *refs[-2:])
+
+
+def finish_kernel(first_head, counts, place, *refs):
+    groups = []
+    for number in counts:
+        groups.append(refs[:number])
+        refs = refs[number:]
     own_ref, c_ref, factor_ref = refs[:3]
     keep_ref, send_ref, partial = refs[-3:]
     local_kernel(first_head, *refs[3:8], partial)
-    carry(first_head, place[2], last, before, own_ref, c_ref, factor_ref, partial, keep_ref, send_ref)
-
-
-def place_kernel(first, place, keep, got, *refs):
+    carry(first_head, place[2], *groups, own_ref, c_ref, factor_ref, partial, keep_ref, send_ref)
+
+
+def place_kernel(firsts, place, *refs):
+    count = len(firsts)
+    keeps, gots = refs[:count], refs[count : 2 * count]
     out, sems = refs[-2:]
     core = place[2]
-    width = keep.shape[1]
     half = out.shape[1] // PAIR
-    copies = [
-        (keep, out.at[:, ds(core * half + first, width)]),
-        (got, out.at[:, ds((1 - core) * half + first, width)]),
-    ]
+    copies = []
+    for first, keep, got in zip(firsts, keeps, gots):
+        width = keep.shape[1]
+        copies.append((keep, out.at[:, ds(core * half + first, width)]))
+        copies.append((got, out.at[:, ds((1 - core) * half + first, width)]))
     for copy in run(copies, sems):
         copy.wait()
 
 
-def put_in_place(first, shape, place, keep, got, before):
+def put_in_place(firsts, shape, place, keeps, gots):
     smem, vmem, hbm = (pl.BlockSpec(memory_space=m) for m in (pltpu.SMEM, pltpu.VMEM, pltpu.HBM))
+    count = len(firsts)
     return pl.pallas_call(
-        functools.partial(place_kernel, first),
+        functools.partial(place_kernel, firsts),
         out_shape=jax.ShapeDtypeStruct(shape, BF16),
-        in_specs=[smem, vmem, vmem] + [hbm] * len(before),
+        in_specs=[smem] + [vmem] * (2 * count),
         out_specs=hbm,
-        input_output_aliases={3: 0} if before else {},
-        scratch_shapes=[pltpu.SemaphoreType.DMA((2,))],
+        scratch_shapes=[pltpu.SemaphoreType.DMA((2 * count,))],
         compiler_params=pltpu.CompilerParams(vmem_limit_bytes=16 << 20),
         cost_estimate=pl.CostEstimate(flops=1, bytes_accessed=1, transcendentals=0),
         name="place",
-    )(place, keep, got, *before)
+    )(place, *keeps, *gots)
 
 
 class Stay:
@@ -655,57 +682,60 @@
         [place, rows],
         scratch=[pltpu.SemaphoreType.DMA((4 * shards,))],
         name="pack_first",
-        limit=None,
     )
     got_first = swap(sent)
-    sent, taps, offset, tail = call(
+    sent, tail = call(
         functools.partial(pack_kernel, shards),
-        [
-            ((tok, shards * (size - WIDTHS[0]) + HEADS), BF16),
-            ((4, size), F32),
-            ((1, size), F32),
-            ((16, shards * size), BF16),
-        ],
-        [place, rows, Stay(dt_raw), Stay(conv_weight), Stay(conv_bias[None]), Stay(sent)],
-        scratch=[pltpu.SemaphoreType.DMA((6 * shards + 7,))],
+        [((tok, shards * (size - WIDTHS[0]) + HEADS), BF16), ((16, shards * size), BF16)],
+        [place, rows, Stay(dt_raw), Stay(sent)],
+        scratch=[pltpu.SemaphoreType.DMA((6 * shards + 1,))],
         name="pack",
-        limit=None,
     )
     got_rest = swap(sent)
-
-    def send_on(piece, order, edges=None):
+    taps, offset = call(
+        taps_kernel,
+        [((4, size), F32), ((1, size), F32)],
+        [place, Stay(conv_weight), Stay(conv_bias[None]), Stay(got_rest)],
+        scratch=[pltpu.SemaphoreType.DMA((6,))],
+        name="taps",
+    )
+
+    def send_on(plan, order, tail=None, edges=None):
         unused = Stay(got_first)
-        plan = [(r, (piece,)) for r in range(shards)]
-        made = [((3, shards * size), BF16)] if piece == 0 else []
+        parts = [p for _, pieces in plan for p in pieces]
+        made = [] if tail is None else [((3, shards * size), BF16)]
         return call(
             functools.partial(merge_kernel, shards, plan, len(order)),
-            [((PAIR * tok, total_of(piece)), BF16)] * shards + made,
+            [((PAIR * tok, sum(map(total_of, pieces))), BF16) for _, pieces in plan] + made,
             [
                 place,
                 rows,
-                dt_raw if piece == 1 else Stay(dt_raw),
-                got_first if piece == 0 else unused,
-                unused if piece == 0 else got_rest,
-                unused if edges is None else edges,
+                Stay(dt_raw) if edges is None else dt_raw,
+                got_first if 0 in parts else unused,
+                got_rest if any(parts) else unused,
+                next((o for o in (tail, edges) if o is not None), unused),
             ]
             + [Stay(o) for o in order],
-            scratch=[pltpu.SemaphoreType.DMA((2 * shards * (1 + len(RESTS[piece])),))],
+            scratch=[pltpu.SemaphoreType.DMA((sum(2 + 2 * len(RESTS[p]) for p in parts),))],
             name="merge",
         )
 
     def travel(blocks):
-        got = [blocks[0]]
-        for r in range(1, shards):
-            got.append(over(blocks[r], lambda i, r=r: i ^ r))
-        return got
-
-    *first_blocks, edges = send_on(0, [], tail)
-    message = {0: travel(first_blocks)}
+        return [blocks[0]] + [over(blocks[r], lambda i, r=r: i ^ r) for r in range(1, shards)]
+
+    def plan(piece):
+        return [(r, (piece,)) for r in range(shards)]
+
+    *first_blocks, edges = send_on(plan(0), [], tail)
+    message = [travel(first_blocks)]
     edges = over(edges, lambda i: i + peers if i % shards == shards - 1 else None)
-    second_blocks = send_on(1, [first_blocks[0], message[0][1]], edges)
-    message[1] = travel(second_blocks)
-    third_blocks = send_on(2, [second_blocks[0], *message[0][2:]])
-    message[2] = travel(third_blocks)
+    second_blocks = send_on(plan(1), [first_blocks[0], message[0][1]], None, edges)
+    message.append(travel(second_blocks))
+    third_blocks = send_on(plan(2), [second_blocks[0], *message[0][2:]])
+    message.append(travel(third_blocks))
+
+    def seen(piece):
+        return message[piece]
 
     tiles = [p.reshape(HEADS // LANES, LANES) for p in (a_log, dt_bias, skip_gain)]
     b, edge, cum, row, factor, tail, skip = call(
@@ -719,12 +749,12 @@
             ((slab, 2 * LANES), BF16),
             ((16, 3 * LANES), BF16),
         ],
-        [place] + message[1] + [taps, offset] + tiles + [Stay(third_blocks[0])],
+        [place] + seen(1) + [taps, offset] + tiles + [Stay(third_blocks[0])],
         scratch=[pltpu.VMEM((slab, LANES), F32), pltpu.VMEM((slab + 8, STATE), F32)],
         name="prep",
     )
     count = len(GROUPED)
-    x, sent, own, last, joined, before, keep, send = ([None] * count for _ in range(8))
+    x, sent, own, last, joined, before, alone, keep, send = ([None] * count for _ in range(9))
 
     def first_head(i):
         return (sum(WIDTHS[: GROUPED[i][0]]) + GROUPED[i][1]) // HEAD_DIM
@@ -734,14 +764,15 @@
         x[i], own[i], *sent[i] = call(
             functools.partial(state_kernel, shards, GROUPED[i], FIRST_ROUND[i]),
             [((slab, width), BF16), ((STATE, width), F32)] + [((STATE + 16, w), BF16) for w in FIRST_ROUND[i]],
-            [place] + message[piece] + [taps, offset, edge, b, factor, tail] + [Stay(o) for o in order],
+            [place] + seen(piece) + [taps, offset, edge, b, factor, tail] + [Stay(o) for o in order],
             scratch=[pltpu.VMEM((slab + 8, width), F32)],
             name="state",
         )
-        last[i] = [over(part, lambda i: i + peers) for part in sent[i]]
+        every = i not in ALONE
+        last[i] = [over(part, lambda i: i + peers if every or i // peers % 2 == 0 else None) for part in sent[i]]
 
     def combine_of(i, order):
-        joined[i], before[i] = [], []
+        joined[i], before[i], alone[i] = [], [], []
         step = len(FIRST_ROUND[i]) // len(SECOND_ROUND[i])
         for j, width in enumerate(SECOND_ROUND[i]):
             early, late = last[i][j * step : (j + 1) * step], sent[i][j * step : (j + 1) * step]
@@ -752,22 +783,26 @@
                 name="combine",
             )
             joined[i].append(total)
-            before[i].append(over(total, lambda i: i + 2 * peers))
+            if i in ALONE:
+                before[i].append(over(total, lambda i: i + 2 * peers if i // peers == 1 else None))
+                alone[i].append(over(total, lambda i: i + peers if i // peers == 1 else None))
+            else:
+                before[i].append(over(total, lambda i: i + 2 * peers))
             order = [total]
 
     def finish_of(body, i, operands, order, **more):
         keep[i], send[i] = call(
-            functools.partial(body, first_head(i), len(last[i]), len(before[i])),
+            functools.partial(body, first_head(i), (len(last[i]), len(before[i]), len(alone[i]))),
             [((BLOCK, GROUPED[i][2]), BF16)] * 2,
-            [place, *last[i], *before[i], own[i], c, factor] + operands + [Stay(o) for o in order],
+            [place, *last[i], *before[i], *alone[i], own[i], c, factor] + operands + [Stay(o) for o in order],
             name="final",
             **more,
         )
 
     state_of(0, [])
     combine_of(0, [])
-    fourth_blocks = send_on(3, [joined[0][0]])
-    message[3] = travel(fourth_blocks)
+    fourth_blocks = send_on(plan(3), [joined[0][0]])
+    message.append(travel(fourth_blocks))
     state_of(1, [fourth_blocks[0]])
     combine_of(1, [])
     state_of(2, joined[1])
@@ -775,7 +810,7 @@
     c, score = call(
         functools.partial(score_kernel, shards),
         [((slab, STATE), BF16), ((slab, BLOCK), F32)],
-        [place] + message[3] + [taps, offset, edge, b] + [Stay(o) for o in sent[3] + before[1]],
+        [place] + seen(3) + [taps, offset, edge, b] + [Stay(o) for o in sent[3] + before[1]],
         scratch=[pltpu.VMEM((slab + 8, STATE), F32)],
         name="score",
     )
@@ -802,11 +837,8 @@
     for i in (2, 3):
         finish_of(final_kernel, i, [partial[i]], [order])
         order = keep[i]
-    out = []
-    for i in range(count):
-        shape = (BLOCK, PAIR * PER_GROUP)
-        out = [put_in_place(first_head(i) * HEAD_DIM, shape, place, keep[i], swap(send[i]), out)]
-    return out[0]
+    firsts = [first_head(i) * HEAD_DIM for i in range(count)]
+    return put_in_place(firsts, (BLOCK, PAIR * PER_GROUP), place, keep, [swap(o) for o in send])
 
 
 def solution(mesh):

time: 122 us -> 110 us (0.902)
  starting transfers between devices: 63.7 us -> 55.2 us
  Pallas kernels: 35.2 us -> 28.3 us
  waiting for transfers between devices: 19.5 us -> 22.1 us
    ppermute x30 -> x32, starting transfers between devices: 63.7 us -> 55.2 us  [over(): lax.ppermute(block, axes, [(i, j) for i, j in route if j is not None and...]
    pallas_call x4 -> x1, Pallas kernels: 5.41 us -> 1.91 us  [put_in_place(): pl.pallas_call(functools.partial(place_kernel, firsts), out_shape=jax.Sha...]
    pallas_call x23 -> x24, Pallas kernels: 29.8 us -> 26.4 us  [call(): pl.pallas_call(body, out_shape=shapes, in_specs=specs, out_specs=[vmem] *...]
    ppermute x30 -> x32, waiting for transfers between devices: 19.5 us -> 22.1 us  [over(): lax.ppermute(block, axes, [(i, j) for i, j in route if j is not None and...]
  transfers between devices with their start and end apart: 30 -> 32, of which waited for: 9 -> 11; matrix products, arithmetic and copies ran while one was open for 0% -> 0% of each run, Pallas kernels for 23% -> 22%
where the time goes in v9:
time: 110 us; the launch traced here: 108 us
  starting transfers between devices  55.2 us (50%)
  Pallas kernels  28.3 us (26%)
  waiting for transfers between devices  22.1 us (20%)
  local copies, waits for them, and re-layouts  1.85 us (2%)
    ppermute x32, starting transfers between devices, over(): lax.ppermute(block, axes, [(i, j) for i, j in route if j is not None and...  55.2 us
    pallas_call x24, Pallas kernels, call(): pl.pallas_call(body, out_shape=shapes, in_specs=specs, out_specs=[vmem] *...  26.4 us
    ppermute x32, waiting for transfers between devices, over(): lax.ppermute(block, axes, [(i, j) for i, j in route if j is not None and...  22.1 us
  transfers between devices with their start and end apart: 32, of which 11 were waited for; matrix products, arithmetic and copies ran while one was open for 0% of the time, Pallas kernels for 22%

profile of v9, /device:TPU:13, one launch (start us, length us, event | category | flops | bytes accessed | tf_op | source)
XLA Modules:
  0.0 108.0 jit_solution(7053004123029023353)
XLA Ops:
  0.1 1.7 %copy-done = bf16[64,20480]{1,0:T(8,128)(2,1)S(1)} copy-done((bf16[64,20480]{1,0:T(8,128)(2,1)S(1)}, bf16[64,20480]{1,0:T(8,128)(2,1)}, u32[]{:S(2)}) %copy-start) | copy-done | bytes 2621464
  2.8 1.3 %pack.1 = (bf16[64,8448]{1,0:T(8,128)(2,1)S(1)}, bf16[16,10240]{1,0:T(8,128)(2,1)S(1)}) custom-call(s32[5]{0:T(128)S(1)} %stack.23.place, bf16[64,20480]{1,0:T(8,128)(2,1)S(1)} %copy-done, bf16[64,256]{1,0:T(8,128)(2,1)S(1)} %copy-done.2, bf16[64,4096]{1,0:T(8,128)(2,1)S(1)} %pack_first.1.order), custom_call_target="tpu_custom_call" | custom-call | flops 1 | bytes 1 | tf_op jit(solution)/shard_map/pack/pallas_call | solution.py:647
  5.0 3.0 %collective-permute-done.got_first.got.edges = bf16[64,4096]{1,0:T(8,128)(2,1)S(1)} collective-permute-done((bf16[64,4096]{1,0:T(8,128)(2,1)S(1)}, bf16[64,4096]{1,0:T(8,128)(2,1)S(1)}, u32[]{:S(2)}, u32[]{:S(2)}) %collective-permute-start) | collective-permute-done | bytes 524320 | tf_op jit(solution)/shard_map/ppermute | solution.py:672
  9.0 2.3 %collective-permute-start.2 = (bf16[128,512]{1,0:T(8,128)(2,1)S(1)}, bf16[128,512]{1,0:T(8,128)(2,1)S(1)}, u32[]{:S(2)}, u32[]{:S(2)}) collective-permute-start(bf16[128,512]{1,0:T(8,128)(2,1)S(1)} %get-tuple-element.60), channel_id=1, source_target_pairs={{0,2},{1,3},{2,0},{3,1},{4,6},{5,7},{6,4},{7,5},{8,10},{9,11},{10,... | collective-permute-start | bytes 393224 | tf_op jit(solution)/shard_map/ppermute | solution.py:672
  12.2 1.4 %collective-permute-done.1.refs_1_ = bf16[128,512]{1,0:T(8,128)(2,1)S(1)} collective-permute-done((bf16[128,512]{1,0:T(8,128)(2,1)S(1)}, bf16[128,512]{1,0:T(8,128)(2,1)S(1)}, u32[]{:S(2)}, u32[]{:S(2)}) %collective-permute-start.1) | collective-permute-done | bytes 131104 | tf_op jit(solution)/shard_map/ppermute | solution.py:672
  14.8 7.4 %collective-permute-start.7 = (bf16[128,384]{1,0:T(8,128)(2,1)S(1)}, bf16[128,384]{1,0:T(8,128)(2,1)S(1)}, u32[]{:S(2)}, u32[]{:S(2)}) collective-permute-start(bf16[128,384]{1,0:T(8,128)(2,1)S(1)} %get-tuple-element.68), channel_id=1, source_target_pairs={{0,2},{1,3},{2,0},{3,1},{4,6},{5,7},{6,4},{7,5},{8,10},{9,11},{10,... | collective-permute-start | bytes 294920 | tf_op jit(solution)/shard_map/ppermute | solution.py:672
  24.6 2.1 %collective-permute-start.16 = (bf16[128,768]{1,0:T(8,128)(2,1)S(1)}, bf16[128,768]{1,0:T(8,128)(2,1)S(1)}, u32[]{:S(2)}, u32[]{:S(2)}) collective-permute-start(bf16[128,768]{1,0:T(8,128)(2,1)S(1)} %get-tuple-element.83), channel_id=1, source_target_pairs={{0,2},{1,3},{2,0},{3,1},{4,6},{5,7},{6,4},{7,5},{8,10},{9,11},{10,... | collective-permute-start | bytes 589832 | tf_op jit(solution)/shard_map/ppermute | solution.py:672
  27.6 2.3 %collective-permute-done.8.refs_3_ = bf16[128,384]{1,0:T(8,128)(2,1)S(1)} collective-permute-done((bf16[128,384]{1,0:T(8,128)(2,1)S(1)}, bf16[128,384]{1,0:T(8,128)(2,1)S(1)}, u32[]{:S(2)}, u32[]{:S(2)}) %collective-permute-start.8) | collective-permute-done | bytes 98336 | tf_op jit(solution)/shard_map/ppermute | solution.py:672
  29.9 1.7 %prep.1 = (bf16[512,256]{1,0:T(8,128)(2,1)S(1)}, f32[4,2560]{1,0:T(4,128)S(1)}, f32[512,128]{1,0:T(8,128)S(1)}, f32[128,512]{1,0:T(8,128)S(1)}, bf16[512,256]{1,...) custom-call(s32[5]{0:T(128)S(1)} %stack.23.place, ...), custom_call_target="tpu_custom_call" | custom-call | flops 1 | bytes 1 | tf_op jit(solution)/shard_map/prep/pallas_call | solution.py:647
  31.6 2.1 %state.4 = (bf16[512,512]{1,0:T(8,128)(2,1)S(1)}, f32[256,512]{1,0:T(8,128)S(1)}, bf16[272,256]{1,0:T(8,128)(2,1)S(1)}, bf16[272,256]{1,0:T(8,128)(2,1)S(1)}) custom-call(s32[5]{0:T(128)S(1)} %stack.23.place, bf16[128,512]{1,0:T(8,128)(2,1)S(1)} %get-tuple-element.58.refs_0_, bf16[128,512]{1,0:T(8,128)(2,1)S(1)} %collective-permute-done.1.refs_1_, ...), custom_call_target="tpu_custom_call" | custom-call | flops 1 | bytes 1 | tf_op jit(solution)/shard_map/state/pallas_call | solution.py:647
  33.7 6.9 %collective-permute-start.10 = (bf16[272,256]{1,0:T(8,128)(2,1)S(1)}, bf16[272,256]{1,0:T(8,128)(2,1)S(1)}, u32[]{:S(2)}, u32[]{:S(2)}) collective-permute-start(bf16[272,256]{1,0:T(8,128)(2,1)S(1)} %get-tuple-element.76.refs_3_), channel_id=1, source_target_pairs={{0,8},{1,9},{2,10},{3,11},{4,12},{5,13},{6,14},{7,15},{8,16},{9,17... | collective-permute-start | bytes 417800 | tf_op jit(solution)/shard_map/ppermute | solution.py:672
  40.5 1.9 %collective-permute-start.9 = (bf16[272,256]{1,0:T(8,128)(2,1)S(1)}, bf16[272,256]{1,0:T(8,128)(2,1)S(1)}, u32[]{:S(2)}, u32[]{:S(2)}) collective-permute-start(bf16[272,256]{1,0:T(8,128)(2,1)S(1)} %get-tuple-element.75.refs_2_), channel_id=1, source_target_pairs={{0,8},{1,9},{2,10},{3,11},{4,12},{5,13},{6,14},{7,15},{8,16},{9,17... | collective-permute-start | bytes 417800 | tf_op jit(solution)/shard_map/ppermute | solution.py:672
  42.9 4.3 %collective-permute-done.9.refs_0_ = bf16[272,256]{1,0:T(8,128)(2,1)S(1)} collective-permute-done((bf16[272,256]{1,0:T(8,128)(2,1)S(1)}, bf16[272,256]{1,0:T(8,128)(2,1)S(1)}, u32[]{:S(2)}, u32[]{:S(2)}) %collective-permute-start.9) | collective-permute-done | bytes 139296 | tf_op jit(solution)/shard_map/ppermute | solution.py:672
  48.3 3.0 %collective-permute-start.13 = (bf16[128,1024]{1,0:T(8,128)(2,1)S(1)}, bf16[128,1024]{1,0:T(8,128)(2,1)S(1)}, u32[]{:S(2)}, u32[]{:S(2)}) collective-permute-start(bf16[128,1024]{1,0:T(8,128)(2,1)S(1)} %get-tuple-element.80), channel_id=1, source_target_pairs={{0,2},{1,3},{2,0},{3,1},{4,6},{5,7},{6,4},{7,5},{8,10},{9,11},{10,... | collective-permute-start | bytes 786440 | tf_op jit(solution)/shard_map/ppermute | solution.py:672
  51.4 2.6 %state.5 = (bf16[512,768]{1,0:T(8,128)(2,1)S(1)}, f32[256,768]{1,0:T(8,128)S(1)}, bf16[272,384]{1,0:T(8,128)(2,1)S(1)}, bf16[272,384]{1,0:T(8,128)(2,1)S(1)}) custom-call(s32[5]{0:T(128)S(1)} %stack.23.place, bf16[128,768]{1,0:T(8,128)(2,1)S(1)} %get-tuple-element.70.refs_9_.refs_0_, bf16[128,768]{1,0:T(8,128)(2,1)S(1)} %collective-permute-done.15.refs_1_, ...), custom_call_target="tpu_custom_call" | custom-call | flops 1 | bytes 1 | tf_op jit(solution)/shard_map/state/pallas_call | solution.py:647
  53.9 1.9 %collective-permute-start.18 = (bf16[272,384]{1,0:T(8,128)(2,1)S(1)}, bf16[272,384]{1,0:T(8,128)(2,1)S(1)}, u32[]{:S(2)}, u32[]{:S(2)}) collective-permute-start(bf16[272,384]{1,0:T(8,128)(2,1)S(1)} %get-tuple-element.85.refs_1_), channel_id=1, source_target_pairs={{0,8},{1,9},{2,10},{3,11},{4,12},{5,13},{6,14},{7,15},{8,16},{9,17... | collective-permute-start | bytes 626696 | tf_op jit(solution)/shard_map/ppermute | solution.py:672
  55.9 1.9 %collective-permute-start.19 = (bf16[272,384]{1,0:T(8,128)(2,1)S(1)}, bf16[272,384]{1,0:T(8,128)(2,1)S(1)}, u32[]{:S(2)}, u32[]{:S(2)}) collective-permute-start(bf16[272,384]{1,0:T(8,128)(2,1)S(1)} %get-tuple-element.86.refs_1_), channel_id=1, source_target_pairs={{0,8},{1,9},{2,10},{3,11},{4,12},{5,13},{6,14},{7,15},{8,16},{9,17... | collective-permute-start | bytes 626696 | tf_op jit(solution)/shard_map/ppermute | solution.py:672
  57.8 3.6 %collective-permute-done.18.refs_0_ = bf16[272,384]{1,0:T(8,128)(2,1)S(1)} collective-permute-done((bf16[272,384]{1,0:T(8,128)(2,1)S(1)}, bf16[272,384]{1,0:T(8,128)(2,1)S(1)}, u32[]{:S(2)}, u32[]{:S(2)}) %collective-permute-start.18) | collective-permute-done | bytes 208928 | tf_op jit(solution)/shard_map/ppermute | solution.py:672
  61.5 2.1 %collective-permute-done.19.refs_0_.refs_1_ = bf16[272,384]{1,0:T(8,128)(2,1)S(1)} collective-permute-done((bf16[272,384]{1,0:T(8,128)(2,1)S(1)}, bf16[272,384]{1,0:T(8,128)(2,1)S(1)}, u32[]{:S(2)}, u32[]{:S(2)}) %collective-permute-start.19) | collective-permute-done | bytes 208928 | tf_op jit(solution)/shard_map/ppermute | solution.py:672
  63.7 1.3 %collective-permute-start.21 = (bf16[272,384]{1,0:T(8,128)(2,1)S(1)}, bf16[272,384]{1,0:T(8,128)(2,1)S(1)}, u32[]{:S(2)}, u32[]{:S(2)}) collective-permute-start(bf16[272,384]{1,0:T(8,128)(2,1)S(1)} %combine.7.refs_11_), channel_id=1, source_target_pairs={{0,16},{1,17},{2,18},{3,19},{4,20},{5,21},{6,22},{7,23},{8,24},{9,... | collective-permute-start | bytes 626696 | tf_op jit(solution)/shard_map/ppermute | solution.py:672
  65.0 1.3 %collective-permute-start.20 = (bf16[272,384]{1,0:T(8,128)(2,1)S(1)}, bf16[272,384]{1,0:T(8,128)(2,1)S(1)}, u32[]{:S(2)}, u32[]{:S(2)}) collective-permute-start(bf16[272,384]{1,0:T(8,128)(2,1)S(1)} %combine.6.refs_2_.refs_10_), channel_id=1, source_target_pairs={{0,16},{1,17},{2,18},{3,19},{4,20},{5,21},{6,22},{7,23},{8,24},{9,... | collective-permute-start | bytes 626696 | tf_op jit(solution)/shard_map/ppermute | solution.py:672
  66.3 3.0 %collective-permute-done.14.refs_3_ = bf16[128,1024]{1,0:T(8,128)(2,1)S(1)} collective-permute-done((bf16[128,1024]{1,0:T(8,128)(2,1)S(1)}, bf16[128,1024]{1,0:T(8,128)(2,1)S(1)}, u32[]{:S(2)}, u32[]{:S(2)}) %collective-permute-start.14) | collective-permute-done | bytes 262176 | tf_op jit(solution)/shard_map/ppermute | solution.py:672
  69.4 1.9 %state.6 = (bf16[512,384]{1,0:T(8,128)(2,1)S(1)}, f32[256,384]{1,0:T(8,128)S(1)}, bf16[272,384]{1,0:T(8,128)(2,1)S(1)}) custom-call(s32[5]{0:T(128)S(1)} %stack.23.place, bf16[128,1024]{1,0:T(8,128)(2,1)S(1)} %get-tuple-element.78.refs_10_.refs_0_, bf16[128,1024]{1,0:T(8,128)(2,1)S(1)} %collective-permute-done.12.refs_1_, ...), custom_call_target="tpu_custom_call" | custom-call | flops 1 | bytes 1 | tf_op jit(solution)/shard_map/state/pallas_call | solution.py:647
  71.3 1.5 %collective-permute-start.23 = (bf16[272,384]{1,0:T(8,128)(2,1)S(1)}, bf16[272,384]{1,0:T(8,128)(2,1)S(1)}, u32[]{:S(2)}, u32[]{:S(2)}) collective-permute-start(bf16[272,384]{1,0:T(8,128)(2,1)S(1)} %get-tuple-element.87.refs_10_.refs_1_), channel_id=1, source_target_pairs={{0,8},{1,9},{2,10},{3,11},{4,12},{5,13},{6,14},{7,15},{16,24},{17,... | collective-permute-start | bytes 626696 | tf_op jit(solution)/shard_map/ppermute | solution.py:672
  72.7 1.3 %collective-permute-start.11 = (bf16[272,512]{1,0:T(8,128)(2,1)S(1)}, bf16[272,512]{1,0:T(8,128)(2,1)S(1)}, u32[]{:S(2)}, u32[]{:S(2)}) collective-permute-start(bf16[272,512]{1,0:T(8,128)(2,1)S(1)} %combine.5.refs_0_), channel_id=1, source_target_pairs={{0,16},{1,17},{2,18},{3,19},{4,20},{5,21},{6,22},{7,23},{8,24},{9,... | collective-permute-start | bytes 835592 | tf_op jit(solution)/shard_map/ppermute | solution.py:672
  74.0 1.9 %state.7 = (bf16[512,384]{1,0:T(8,128)(2,1)S(1)}, f32[256,384]{1,0:T(8,128)S(1)}, bf16[272,384]{1,0:T(8,128)(2,1)S(1)}) custom-call(s32[5]{0:T(128)S(1)} %stack.23.place, bf16[128,1024]{1,0:T(8,128)(2,1)S(1)} %get-tuple-element.78.refs_10_.refs_0_, bf16[128,1024]{1,0:T(8,128)(2,1)S(1)} %collective-permute-done.12.refs_1_, ...), custom_call_target="tpu_custom_call" | custom-call | flops 1 | bytes 1 | tf_op jit(solution)/shard_map/state/pallas_call | solution.py:647
  76.0 1.5 %collective-permute-start.22 = (bf16[272,384]{1,0:T(8,128)(2,1)S(1)}, bf16[272,384]{1,0:T(8,128)(2,1)S(1)}, u32[]{:S(2)}, u32[]{:S(2)}) collective-permute-start(bf16[272,384]{1,0:T(8,128)(2,1)S(1)} %get-tuple-element.88.refs_8_.refs_1_), channel_id=1, source_target_pairs={{0,8},{1,9},{2,10},{3,11},{4,12},{5,13},{6,14},{7,15},{16,24},{17,... | collective-permute-start | bytes 626696 | tf_op jit(solution)/shard_map/ppermute | solution.py:672
  78.6 2.6 %final.4 = (bf16[256,768]{1,0:T(8,128)(2,1)S(1)}, bf16[256,768]{1,0:T(8,128)(2,1)S(1)}) custom-call(s32[5]{0:T(128)S(1)} %stack.23.place, bf16[272,384]{1,0:T(8,128)(2,1)S(1)} %collective-permute-done.18.refs_0_, bf16[272,384]{1,0:T(8,128)(2,1)S(1)} %collective-permute-done.19.refs_0_.refs_1_, bf16[272,384]{1,0:T(8,128)(2,1)S(1)} %collective-permute-done.20.refs_9_.refs_2_, ...), custom_call_target="tpu_custom_call" | custom-call | flops 1 | bytes 1 | tf_op jit(solution)/shard_map/final/pallas_call | solution.py:647
  85.4 10.0 %collective-permute-start.29 = (bf16[256,768]{1,0:T(8,128)(2,1)S(1)}, bf16[256,768]{1,0:T(8,128)(2,1)S(1)}, u32[]{:S(2)}, u32[]{:S(2)}) collective-permute-start(bf16[256,768]{1,0:T(8,128)(2,1)S(1)} %get-tuple-element.106), channel_id=1, source_target_pairs={{0,4},{1,5},{2,6},{3,7},{4,0},{5,1},{6,2},{7,3},{8,12},{9,13},{10,... | collective-permute-start | bytes 1179656 | tf_op jit(solution)/shard_map/ppermute | solution.py:672
  96.9 1.9 %final.5 = (bf16[256,512]{1,0:T(8,128)(2,1)S(1)}, bf16[256,512]{1,0:T(8,128)(2,1)S(1)}) custom-call(s32[5]{0:T(128)S(1)} %stack.23.place, bf16[272,256]{1,0:T(8,128)(2,1)S(1)} %collective-permute-done.9.refs_0_, bf16[272,256]{1,0:T(8,128)(2,1)S(1)} %collective-permute-done.10.refs_1_, bf16[272,512]{1,0:T(8,128)(2,1)S(1)} %collective-permute-done.11.refs_2_, ...), custom_call_target="tpu_custom_call" | custom-call | flops 1 | bytes 1 | tf_op jit(solution)/shard_map/final/pallas_call | solution.py:647
  101.1 3.4 %collective-permute-start.31 = (bf16[256,384]{1,0:T(8,128)(2,1)S(1)}, bf16[256,384]{1,0:T(8,128)(2,1)S(1)}, u32[]{:S(2)}, u32[]{:S(2)}) collective-permute-start(bf16[256,384]{1,0:T(8,128)(2,1)S(1)} %get-tuple-element.108), channel_id=1, source_target_pairs={{0,4},{1,5},{2,6},{3,7},{4,0},{5,1},{6,2},{7,3},{8,12},{9,13},{10,... | collective-permute-start | bytes 589832 | tf_op jit(solution)/shard_map/ppermute | solution.py:672
  105.9 1.9 %place.1 = bf16[256,4096]{1,0:T(8,128)(2,1)} custom-call(s32[5]{0:T(128)S(1)} %stack.23.place, bf16[256,512]{1,0:T(8,128)(2,1)S(1)} %get-tuple-element.100.refs_7_.refs_0_, bf16[256,768]{1,0:T(8,128)(2,1)S(1)} %get-tuple-element.99.refs_2_.refs_1_, bf16[256,384]{1,0:T(8,128)(2,1)S(1)} %get-tuple-element.102.refs_7_.refs_2_, ...), custom_call_target="tpu_custom_call" | custom-call | flops 1 | bytes 1 | tf_op jit(solution)/shard_map/place/pallas_call | solution.py:623
  (74 shorter events, 20.4 us)
Async XLA Ops:
  4.1 9.4 %collective-permute-start.4 = (bf16[64,8448]{1,0:T(8,128)(2,1)S(1)}, bf16[64,8448]{1,0:T(8,128)(2,1)S(1)}, u32[]{:S(2)}, u32[]{:S(2)}) collective-permute-start(bf16[64,8448]{1,0:T(8,128)(2,1)S(1)} %get-tuple-element.62), channel_id=1, source_target_pairs={{0,4},{1,5},{2,6},{3,7},{4,0},{5,1},{6,2},{7,3},{8,12},{9,13},{10,... | collective-permute-start | bytes 3244040 | tf_op jit(solution)/shard_map/ppermute | solution.py:672
  4.9 3.1 %collective-permute-start = (bf16[64,4096]{1,0:T(8,128)(2,1)S(1)}, bf16[64,4096]{1,0:T(8,128)(2,1)S(1)}, u32[]{:S(2)}, u32[]{:S(2)}) collective-permute-start(bf16[64,4096]{1,0:T(8,128)(2,1)S(1)} %pack_first.1.order), channel_id=1, source_target_pairs={{0,4},{1,5},{2,6},{3,7},{4,0},{5,1},{6,2},{7,3},{8,12},{9,13},{10,... | collective-permute-start | bytes 1572872 | tf_op jit(solution)/shard_map/ppermute | solution.py:672
  8.8 4.8 %collective-permute-start.1 = (bf16[128,512]{1,0:T(8,128)(2,1)S(1)}, bf16[128,512]{1,0:T(8,128)(2,1)S(1)}, u32[]{:S(2)}, u32[]{:S(2)}) collective-permute-start(bf16[128,512]{1,0:T(8,128)(2,1)S(1)} %get-tuple-element.59), channel_id=1, source_target_pairs={{0,1},{1,0},{2,3},{3,2},{4,5},{5,4},{6,7},{7,6},{8,9},{9,8},{10,11... | collective-permute-start | bytes 393224 | tf_op jit(solution)/shard_map/ppermute | solution.py:672
  9.0 13.5 %collective-permute-start.2 = (bf16[128,512]{1,0:T(8,128)(2,1)S(1)}, bf16[128,512]{1,0:T(8,128)(2,1)S(1)}, u32[]{:S(2)}, u32[]{:S(2)}) collective-permute-start(bf16[128,512]{1,0:T(8,128)(2,1)S(1)} %get-tuple-element.60), channel_id=1, source_target_pairs={{0,2},{1,3},{2,0},{3,1},{4,6},{5,7},{6,4},{7,5},{8,10},{9,11},{10,... | collective-permute-start | bytes 393224 | tf_op jit(solution)/shard_map/ppermute | solution.py:672
  11.3 11.6 %collective-permute-start.3 = (bf16[128,512]{1,0:T(8,128)(2,1)S(1)}, bf16[128,512]{1,0:T(8,128)(2,1)S(1)}, u32[]{:S(2)}, u32[]{:S(2)}) collective-permute-start(bf16[128,512]{1,0:T(8,128)(2,1)S(1)} %get-tuple-element.61), channel_id=1, source_target_pairs={{0,3},{1,2},{2,1},{3,0},{4,7},{5,6},{6,5},{7,4},{8,11},{9,10},{10,... | collective-permute-start | bytes 393224 | tf_op jit(solution)/shard_map/ppermute | solution.py:672
  11.5 0.7 collective-permute-start.5
  14.6 12.1 %collective-permute-start.6 = (bf16[128,384]{1,0:T(8,128)(2,1)S(1)}, bf16[128,384]{1,0:T(8,128)(2,1)S(1)}, u32[]{:S(2)}, u32[]{:S(2)}) collective-permute-start(bf16[128,384]{1,0:T(8,128)(2,1)S(1)} %get-tuple-element.67), channel_id=1, source_target_pairs={{0,1},{1,0},{2,3},{3,2},{4,5},{5,4},{6,7},{7,6},{8,9},{9,8},{10,11... | collective-permute-start | bytes 294920 | tf_op jit(solution)/shard_map/ppermute | solution.py:672
  14.8 12.8 %collective-permute-start.7 = (bf16[128,384]{1,0:T(8,128)(2,1)S(1)}, bf16[128,384]{1,0:T(8,128)(2,1)S(1)}, u32[]{:S(2)}, u32[]{:S(2)}) collective-permute-start(bf16[128,384]{1,0:T(8,128)(2,1)S(1)} %get-tuple-element.68), channel_id=1, source_target_pairs={{0,2},{1,3},{2,0},{3,1},{4,6},{5,7},{6,4},{7,5},{8,10},{9,11},{10,... | collective-permute-start | bytes 294920 | tf_op jit(solution)/shard_map/ppermute | solution.py:672
  22.3 7.6 %collective-permute-start.8 = (bf16[128,384]{1,0:T(8,128)(2,1)S(1)}, bf16[128,384]{1,0:T(8,128)(2,1)S(1)}, u32[]{:S(2)}, u32[]{:S(2)}) collective-permute-start(bf16[128,384]{1,0:T(8,128)(2,1)S(1)} %get-tuple-element.69), channel_id=1, source_target_pairs={{0,3},{1,2},{2,1},{3,0},{4,7},{5,6},{6,5},{7,4},{8,11},{9,10},{10,... | collective-permute-start | bytes 294920 | tf_op jit(solution)/shard_map/ppermute | solution.py:672
  23.8 27.6 %collective-permute-start.15 = (bf16[128,768]{1,0:T(8,128)(2,1)S(1)}, bf16[128,768]{1,0:T(8,128)(2,1)S(1)}, u32[]{:S(2)}, u32[]{:S(2)}) collective-permute-start(bf16[128,768]{1,0:T(8,128)(2,1)S(1)} %get-tuple-element.82), channel_id=1, source_target_pairs={{0,1},{1,0},{2,3},{3,2},{4,5},{5,4},{6,7},{7,6},{8,9},{9,8},{10,11... | collective-permute-start | bytes 589832 | tf_op jit(solution)/shard_map/ppermute | solution.py:672
  24.6 26.8 %collective-permute-start.16 = (bf16[128,768]{1,0:T(8,128)(2,1)S(1)}, bf16[128,768]{1,0:T(8,128)(2,1)S(1)}, u32[]{:S(2)}, u32[]{:S(2)}) collective-permute-start(bf16[128,768]{1,0:T(8,128)(2,1)S(1)} %get-tuple-element.83), channel_id=1, source_target_pairs={{0,2},{1,3},{2,0},{3,1},{4,6},{5,7},{6,4},{7,5},{8,10},{9,11},{10,... | collective-permute-start | bytes 589832 | tf_op jit(solution)/shard_map/ppermute | solution.py:672
  26.7 24.6 %collective-permute-start.17 = (bf16[128,768]{1,0:T(8,128)(2,1)S(1)}, bf16[128,768]{1,0:T(8,128)(2,1)S(1)}, u32[]{:S(2)}, u32[]{:S(2)}) collective-permute-start(bf16[128,768]{1,0:T(8,128)(2,1)S(1)} %get-tuple-element.84), channel_id=1, source_target_pairs={{0,3},{1,2},{2,1},{3,0},{4,7},{5,6},{6,5},{7,4},{8,11},{9,10},{10,... | collective-permute-start | bytes 589832 | tf_op jit(solution)/shard_map/ppermute | solution.py:672
  33.7 9.2 %collective-permute-start.10 = (bf16[272,256]{1,0:T(8,128)(2,1)S(1)}, bf16[272,256]{1,0:T(8,128)(2,1)S(1)}, u32[]{:S(2)}, u32[]{:S(2)}) collective-permute-start(bf16[272,256]{1,0:T(8,128)(2,1)S(1)} %get-tuple-element.76.refs_3_), channel_id=1, source_target_pairs={{0,8},{1,9},{2,10},{3,11},{4,12},{5,13},{6,14},{7,15},{8,16},{9,17... | collective-permute-start | bytes 417800 | tf_op jit(solution)/shard_map/ppermute | solution.py:672
  40.5 6.7 %collective-permute-start.9 = (bf16[272,256]{1,0:T(8,128)(2,1)S(1)}, bf16[272,256]{1,0:T(8,128)(2,1)S(1)}, u32[]{:S(2)}, u32[]{:S(2)}) collective-permute-start(bf16[272,256]{1,0:T(8,128)(2,1)S(1)} %get-tuple-element.75.refs_2_), channel_id=1, source_target_pairs={{0,8},{1,9},{2,10},{3,11},{4,12},{5,13},{6,14},{7,15},{8,16},{9,17... | collective-permute-start | bytes 417800 | tf_op jit(solution)/shard_map/ppermute | solution.py:672
  48.3 18.1 %collective-permute-start.12 = (bf16[128,1024]{1,0:T(8,128)(2,1)S(1)}, bf16[128,1024]{1,0:T(8,128)(2,1)S(1)}, u32[]{:S(2)}, u32[]{:S(2)}) collective-permute-start(bf16[128,1024]{1,0:T(8,128)(2,1)S(1)} %get-tuple-element.79), channel_id=1, source_target_pairs={{0,1},{1,0},{2,3},{3,2},{4,5},{5,4},{6,7},{7,6},{8,9},{9,8},{10,11... | collective-permute-start | bytes 786440 | tf_op jit(solution)/shard_map/ppermute | solution.py:672
  48.3 18.0 %collective-permute-start.13 = (bf16[128,1024]{1,0:T(8,128)(2,1)S(1)}, bf16[128,1024]{1,0:T(8,128)(2,1)S(1)}, u32[]{:S(2)}, u32[]{:S(2)}) collective-permute-start(bf16[128,1024]{1,0:T(8,128)(2,1)S(1)} %get-tuple-element.80), channel_id=1, source_target_pairs={{0,2},{1,3},{2,0},{3,1},{4,6},{5,7},{6,4},{7,5},{8,10},{9,11},{10,... | collective-permute-start | bytes 786440 | tf_op jit(solution)/shard_map/ppermute | solution.py:672
  51.3 18.0 %collective-permute-start.14 = (bf16[128,1024]{1,0:T(8,128)(2,1)S(1)}, bf16[128,1024]{1,0:T(8,128)(2,1)S(1)}, u32[]{:S(2)}, u32[]{:S(2)}) collective-permute-start(bf16[128,1024]{1,0:T(8,128)(2,1)S(1)} %get-tuple-element.81), channel_id=1, source_target_pairs={{0,3},{1,2},{2,1},{3,0},{4,7},{5,6},{6,5},{7,4},{8,11},{9,10},{10,... | collective-permute-start | bytes 786440 | tf_op jit(solution)/shard_map/ppermute | solution.py:672
  53.9 7.4 %collective-permute-start.18 = (bf16[272,384]{1,0:T(8,128)(2,1)S(1)}, bf16[272,384]{1,0:T(8,128)(2,1)S(1)}, u32[]{:S(2)}, u32[]{:S(2)}) collective-permute-start(bf16[272,384]{1,0:T(8,128)(2,1)S(1)} %get-tuple-element.85.refs_1_), channel_id=1, source_target_pairs={{0,8},{1,9},{2,10},{3,11},{4,12},{5,13},{6,14},{7,15},{8,16},{9,17... | collective-permute-start | bytes 626696 | tf_op jit(solution)/shard_map/ppermute | solution.py:672
  55.9 7.8 %collective-permute-start.19 = (bf16[272,384]{1,0:T(8,128)(2,1)S(1)}, bf16[272,384]{1,0:T(8,128)(2,1)S(1)}, u32[]{:S(2)}, u32[]{:S(2)}) collective-permute-start(bf16[272,384]{1,0:T(8,128)(2,1)S(1)} %get-tuple-element.86.refs_1_), channel_id=1, source_target_pairs={{0,8},{1,9},{2,10},{3,11},{4,12},{5,13},{6,14},{7,15},{8,16},{9,17... | collective-permute-start | bytes 626696 | tf_op jit(solution)/shard_map/ppermute | solution.py:672
  63.7 13.7 %collective-permute-start.21 = (bf16[272,384]{1,0:T(8,128)(2,1)S(1)}, bf16[272,384]{1,0:T(8,128)(2,1)S(1)}, u32[]{:S(2)}, u32[]{:S(2)}) collective-permute-start(bf16[272,384]{1,0:T(8,128)(2,1)S(1)} %combine.7.refs_11_), channel_id=1, source_target_pairs={{0,16},{1,17},{2,18},{3,19},{4,20},{5,21},{6,22},{7,23},{8,24},{9,... | collective-permute-start | bytes 626696 | tf_op jit(solution)/shard_map/ppermute | solution.py:672
  65.0 12.4 %collective-permute-start.20 = (bf16[272,384]{1,0:T(8,128)(2,1)S(1)}, bf16[272,384]{1,0:T(8,128)(2,1)S(1)}, u32[]{:S(2)}, u32[]{:S(2)}) collective-permute-start(bf16[272,384]{1,0:T(8,128)(2,1)S(1)} %combine.6.refs_2_.refs_10_), channel_id=1, source_target_pairs={{0,16},{1,17},{2,18},{3,19},{4,20},{5,21},{6,22},{7,23},{8,24},{9,... | collective-permute-start | bytes 626696 | tf_op jit(solution)/shard_map/ppermute | solution.py:672
  71.3 9.9 %collective-permute-start.23 = (bf16[272,384]{1,0:T(8,128)(2,1)S(1)}, bf16[272,384]{1,0:T(8,128)(2,1)S(1)}, u32[]{:S(2)}, u32[]{:S(2)}) collective-permute-start(bf16[272,384]{1,0:T(8,128)(2,1)S(1)} %get-tuple-element.87.refs_10_.refs_1_), channel_id=1, source_target_pairs={{0,8},{1,9},{2,10},{3,11},{4,12},{5,13},{6,14},{7,15},{16,24},{17,... | collective-permute-start | bytes 626696 | tf_op jit(solution)/shard_map/ppermute | solution.py:672
  72.7 12.6 %collective-permute-start.11 = (bf16[272,512]{1,0:T(8,128)(2,1)S(1)}, bf16[272,512]{1,0:T(8,128)(2,1)S(1)}, u32[]{:S(2)}, u32[]{:S(2)}) collective-permute-start(bf16[272,512]{1,0:T(8,128)(2,1)S(1)} %combine.5.refs_0_), channel_id=1, source_target_pairs={{0,16},{1,17},{2,18},{3,19},{4,20},{5,21},{6,22},{7,23},{8,24},{9,... | collective-permute-start | bytes 835592 | tf_op jit(solution)/shard_map/ppermute | solution.py:672
  76.0 7.3 %collective-permute-start.22 = (bf16[272,384]{1,0:T(8,128)(2,1)S(1)}, bf16[272,384]{1,0:T(8,128)(2,1)S(1)}, u32[]{:S(2)}, u32[]{:S(2)}) collective-permute-start(bf16[272,384]{1,0:T(8,128)(2,1)S(1)} %get-tuple-element.88.refs_8_.refs_1_), channel_id=1, source_target_pairs={{0,8},{1,9},{2,10},{3,11},{4,12},{5,13},{6,14},{7,15},{16,24},{17,... | collective-permute-start | bytes 626696 | tf_op jit(solution)/shard_map/ppermute | solution.py:672
  81.3 17.5 %collective-permute-start.24 = (bf16[272,384]{1,0:T(8,128)(2,1)S(1)}, bf16[272,384]{1,0:T(8,128)(2,1)S(1)}, u32[]{:S(2)}, u32[]{:S(2)}) collective-permute-start(bf16[272,384]{1,0:T(8,128)(2,1)S(1)} %combine.8.refs_2_), channel_id=1, source_target_pairs={{8,24},{9,25},{10,26},{11,27},{12,28},{13,29},{14,30},{15,31}} | collective-permute-start | bytes 626696 | tf_op jit(solution)/shard_map/ppermute | solution.py:672
  82.0 16.9 %collective-permute-start.25 = (bf16[272,384]{1,0:T(8,128)(2,1)S(1)}, bf16[272,384]{1,0:T(8,128)(2,1)S(1)}, u32[]{:S(2)}, u32[]{:S(2)}) collective-permute-start(bf16[272,384]{1,0:T(8,128)(2,1)S(1)} %combine.8.refs_2_), channel_id=1, source_target_pairs={{8,16},{9,17},{10,18},{11,19},{12,20},{13,21},{14,22},{15,23}} | collective-permute-start | bytes 626696 | tf_op jit(solution)/shard_map/ppermute | solution.py:672
  83.4 16.6 %collective-permute-start.26 = (bf16[272,384]{1,0:T(8,128)(2,1)S(1)}, bf16[272,384]{1,0:T(8,128)(2,1)S(1)}, u32[]{:S(2)}, u32[]{:S(2)}) collective-permute-start(bf16[272,384]{1,0:T(8,128)(2,1)S(1)} %combine.9.refs_0_), channel_id=1, source_target_pairs={{8,24},{9,25},{10,26},{11,27},{12,28},{13,29},{14,30},{15,31}} | collective-permute-start | bytes 626696 | tf_op jit(solution)/shard_map/ppermute | solution.py:672
  84.1 15.9 %collective-permute-start.27 = (bf16[272,384]{1,0:T(8,128)(2,1)S(1)}, bf16[272,384]{1,0:T(8,128)(2,1)S(1)}, u32[]{:S(2)}, u32[]{:S(2)}) collective-permute-start(bf16[272,384]{1,0:T(8,128)(2,1)S(1)} %combine.9.refs_0_), channel_id=1, source_target_pairs={{8,16},{9,17},{10,18},{11,19},{12,20},{13,21},{14,22},{15,23}} | collective-permute-start | bytes 626696 | tf_op jit(solution)/shard_map/ppermute | solution.py:672
  85.4 19.2 %collective-permute-start.29 = (bf16[256,768]{1,0:T(8,128)(2,1)S(1)}, bf16[256,768]{1,0:T(8,128)(2,1)S(1)}, u32[]{:S(2)}, u32[]{:S(2)}) collective-permute-start(bf16[256,768]{1,0:T(8,128)(2,1)S(1)} %get-tuple-element.106), channel_id=1, source_target_pairs={{0,4},{1,5},{2,6},{3,7},{4,0},{5,1},{6,2},{7,3},{8,12},{9,13},{10,... | collective-permute-start | bytes 1179656 | tf_op jit(solution)/shard_map/ppermute | solution.py:672
  98.8 5.7 %collective-permute-start.28 = (bf16[256,512]{1,0:T(8,128)(2,1)S(1)}, bf16[256,512]{1,0:T(8,128)(2,1)S(1)}, u32[]{:S(2)}, u32[]{:S(2)}) collective-permute-start(bf16[256,512]{1,0:T(8,128)(2,1)S(1)} %get-tuple-element.105), channel_id=1, source_target_pairs={{0,4},{1,5},{2,6},{3,7},{4,0},{5,1},{6,2},{7,3},{8,12},{9,13},{10,... | collective-permute-start | bytes 786440 | tf_op jit(solution)/shard_map/ppermute | solution.py:672
  101.1 4.5 %collective-permute-start.31 = (bf16[256,384]{1,0:T(8,128)(2,1)S(1)}, bf16[256,384]{1,0:T(8,128)(2,1)S(1)}, u32[]{:S(2)}, u32[]{:S(2)}) collective-permute-start(bf16[256,384]{1,0:T(8,128)(2,1)S(1)} %get-tuple-element.108), channel_id=1, source_target_pairs={{0,4},{1,5},{2,6},{3,7},{4,0},{5,1},{6,2},{7,3},{8,12},{9,13},{10,... | collective-permute-start | bytes 589832 | tf_op jit(solution)/shard_map/ppermute | solution.py:672
  104.5 1.4 %collective-permute-start.30 = (bf16[256,384]{1,0:T(8,128)(2,1)S(1)}, bf16[256,384]{1,0:T(8,128)(2,1)S(1)}, u32[]{:S(2)}, u32[]{:S(2)}) collective-permute-start(bf16[256,384]{1,0:T(8,128)(2,1)S(1)} %get-tuple-element.107), channel_id=1, source_target_pairs={{0,4},{1,5},{2,6},{3,7},{4,0},{5,1},{6,2},{7,3},{8,12},{9,13},{10,... | collective-permute-start | bytes 589832 | tf_op jit(solution)/shard_map/ppermute | solution.py:672
  (8 other events, 53.8 us)

commit v10 on v9

--- a/solution.py
+++ b/solution.py
@@ -729,9 +729,9 @@
     *first_blocks, edges = send_on(plan(0), [], tail)
     message = [travel(first_blocks)]
     edges = over(edges, lambda i: i + peers if i % shards == shards - 1 else None)
-    second_blocks = send_on(plan(1), [first_blocks[0], message[0][1]], None, edges)
+    second_blocks = send_on(plan(1), [first_blocks[0]], None, edges)
     message.append(travel(second_blocks))
-    third_blocks = send_on(plan(2), [second_blocks[0], *message[0][2:]])
+    third_blocks = send_on(plan(2), [*message[0][1:], *message[1][2:]])
     message.append(travel(third_blocks))
 
     def seen(piece):
@@ -820,9 +820,9 @@
         wide = [pltpu.VMEM((slab, GROUPED[i][2]), F32)]
         finish_of(finish_kernel, i, [x[i]] + mixes, order, scratch=wide)
 
-    in_full(1, [score])
-    combine_of(2, [keep[1]])
-    combine_of(3, joined[2])
+    combine_of(2, [score])
+    in_full(1, joined[2])
+    combine_of(3, [keep[1]])
     order, partial = joined[3][0], {}
     for i in (2, 3):
         (partial[i],) = call(

time: 110 us -> 110 us (level); the launches traced: 108 us -> 109 us
  waiting for transfers between devices: 22.1 us -> 34.8 us
  starting transfers between devices: 55.2 us -> 43.9 us
    ppermute x32, waiting for transfers between devices: 22.1 us -> 34.8 us  [over(): lax.ppermute(block, axes, [(i, j) for i, j in route if j is not None and...]
    ppermute x32, starting transfers between devices: 55.2 us -> 43.9 us  [over(): lax.ppermute(block, axes, [(i, j) for i, j in route if j is not None and...]
  transfers between devices with their start and end apart: 32 -> 32, of which waited for: 11 -> 12; matrix products, arithmetic and copies ran while one was open for 0% -> 0% of each run, Pallas kernels for 22% -> 22%
where the time goes in v10:
time: 110 us; the launch traced here: 109 us
  starting transfers between devices  43.9 us (40%)
  waiting for transfers between devices  34.8 us (32%)
  Pallas kernels  28.3 us (26%)
  local copies, waits for them, and re-layouts  1.86 us (2%)
    ppermute x32, starting transfers between devices, over(): lax.ppermute(block, axes, [(i, j) for i, j in route if j is not None and...  43.9 us
    ppermute x32, waiting for transfers between devices, over(): lax.ppermute(block, axes, [(i, j) for i, j in route if j is not None and...  34.8 us
    pallas_call x24, Pallas kernels, call(): pl.pallas_call(body, out_shape=shapes, in_specs=specs, out_specs=[vmem] *...  26.4 us
  transfers between devices with their start and end apart: 32, of which 12 were waited for; matrix products, arithmetic and copies ran while one was open for 0% of the time, Pallas kernels for 22%

profile of v10, /device:TPU:13, one launch (start us, length us, event | category | flops | bytes accessed | tf_op | source)
XLA Modules:
  0.0 109.5 jit_solution(10561543822366658783)
XLA Ops:
  0.1 1.7 %copy-done = bf16[64,20480]{1,0:T(8,128)(2,1)S(1)} copy-done((bf16[64,20480]{1,0:T(8,128)(2,1)S(1)}, bf16[64,20480]{1,0:T(8,128)(2,1)}, u32[]{:S(2)}) %copy-start) | copy-done | bytes 2621464
  5.0 3.0 %collective-permute-done.got_first.got.edges = bf16[64,4096]{1,0:T(8,128)(2,1)S(1)} collective-permute-done((bf16[64,4096]{1,0:T(8,128)(2,1)S(1)}, bf16[64,4096]{1,0:T(8,128)(2,1)S(1)}, u32[]{:S(2)}, u32[]{:S(2)}) %collective-permute-start) | collective-permute-done | bytes 524320 | tf_op jit(solution)/shard_map/ppermute | solution.py:672
  9.7 4.8 %collective-permute-start.2 = (bf16[128,512]{1,0:T(8,128)(2,1)S(1)}, bf16[128,512]{1,0:T(8,128)(2,1)S(1)}, u32[]{:S(2)}, u32[]{:S(2)}) collective-permute-start(bf16[128,512]{1,0:T(8,128)(2,1)S(1)} %get-tuple-element.60), channel_id=1, source_target_pairs={{0,2},{1,3},{2,0},{3,1},{4,6},{5,7},{6,4},{7,5},{8,10},{9,11},{10,... | collective-permute-start | bytes 393224 | tf_op jit(solution)/shard_map/ppermute | solution.py:672
  15.6 2.9 %collective-permute-start.7 = (bf16[128,384]{1,0:T(8,128)(2,1)S(1)}, bf16[128,384]{1,0:T(8,128)(2,1)S(1)}, u32[]{:S(2)}, u32[]{:S(2)}) collective-permute-start(bf16[128,384]{1,0:T(8,128)(2,1)S(1)} %get-tuple-element.68), channel_id=1, source_target_pairs={{0,2},{1,3},{2,0},{3,1},{4,6},{5,7},{6,4},{7,5},{8,10},{9,11},{10,... | collective-permute-start | bytes 294920 | tf_op jit(solution)/shard_map/ppermute | solution.py:672
  19.9 6.2 %collective-permute-done.2.refs_1_.refs_2_ = bf16[128,512]{1,0:T(8,128)(2,1)S(1)} collective-permute-done((bf16[128,512]{1,0:T(8,128)(2,1)S(1)}, bf16[128,512]{1,0:T(8,128)(2,1)S(1)}, u32[]{:S(2)}, u32[]{:S(2)}) %collective-permute-start.2) | collective-permute-done | bytes 131104 | tf_op jit(solution)/shard_map/ppermute | solution.py:672
  26.1 2.8 %collective-permute-done.3.refs_2_.refs_3_ = bf16[128,512]{1,0:T(8,128)(2,1)S(1)} collective-permute-done((bf16[128,512]{1,0:T(8,128)(2,1)S(1)}, bf16[128,512]{1,0:T(8,128)(2,1)S(1)}, u32[]{:S(2)}, u32[]{:S(2)}) %collective-permute-start.3) | collective-permute-done | bytes 131104 | tf_op jit(solution)/shard_map/ppermute | solution.py:672
  28.9 2.1 %collective-permute-done.7.refs_3_.refs_2_ = bf16[128,384]{1,0:T(8,128)(2,1)S(1)} collective-permute-done((bf16[128,384]{1,0:T(8,128)(2,1)S(1)}, bf16[128,384]{1,0:T(8,128)(2,1)S(1)}, u32[]{:S(2)}, u32[]{:S(2)}) %collective-permute-start.7) | collective-permute-done | bytes 98336 | tf_op jit(solution)/shard_map/ppermute | solution.py:672
  31.0 2.1 %collective-permute-done.8.refs_4_.refs_3_ = bf16[128,384]{1,0:T(8,128)(2,1)S(1)} collective-permute-done((bf16[128,384]{1,0:T(8,128)(2,1)S(1)}, bf16[128,384]{1,0:T(8,128)(2,1)S(1)}, u32[]{:S(2)}, u32[]{:S(2)}) %collective-permute-start.8) | collective-permute-done | bytes 98336 | tf_op jit(solution)/shard_map/ppermute | solution.py:672
  34.0 3.4 %collective-permute-start.16 = (bf16[128,768]{1,0:T(8,128)(2,1)S(1)}, bf16[128,768]{1,0:T(8,128)(2,1)S(1)}, u32[]{:S(2)}, u32[]{:S(2)}) collective-permute-start(bf16[128,768]{1,0:T(8,128)(2,1)S(1)} %get-tuple-element.83), channel_id=1, source_target_pairs={{0,2},{1,3},{2,0},{3,1},{4,6},{5,7},{6,4},{7,5},{8,10},{9,11},{10,... | collective-permute-start | bytes 589832 | tf_op jit(solution)/shard_map/ppermute | solution.py:672
  38.1 1.7 %prep.1 = (bf16[512,256]{1,0:T(8,128)(2,1)S(1)}, f32[4,2560]{1,0:T(4,128)S(1)}, f32[512,128]{1,0:T(8,128)S(1)}, f32[128,512]{1,0:T(8,128)S(1)}, bf16[512,256]{1,...) custom-call(s32[5]{0:T(128)S(1)} %stack.23.place, ...), custom_call_target="tpu_custom_call" | custom-call | flops 1 | bytes 1 | tf_op jit(solution)/shard_map/prep/pallas_call | solution.py:647
  39.8 2.1 %state.4 = (bf16[512,512]{1,0:T(8,128)(2,1)S(1)}, f32[256,512]{1,0:T(8,128)S(1)}, bf16[272,256]{1,0:T(8,128)(2,1)S(1)}, bf16[272,256]{1,0:T(8,128)(2,1)S(1)}) custom-call(s32[5]{0:T(128)S(1)} %stack.23.place, bf16[128,512]{1,0:T(8,128)(2,1)S(1)} %get-tuple-element.58.refs_0_, bf16[128,512]{1,0:T(8,128)(2,1)S(1)} %collective-permute-done.1.refs_0_.refs_1_, ...), custom_call_target="tpu_custom_call" | custom-call | flops 1 | bytes 1 | tf_op jit(solution)/shard_map/state/pallas_call | solution.py:647
  41.9 2.3 %collective-permute-start.10 = (bf16[272,256]{1,0:T(8,128)(2,1)S(1)}, bf16[272,256]{1,0:T(8,128)(2,1)S(1)}, u32[]{:S(2)}, u32[]{:S(2)}) collective-permute-start(bf16[272,256]{1,0:T(8,128)(2,1)S(1)} %get-tuple-element.76.refs_3_), channel_id=1, source_target_pairs={{0,8},{1,9},{2,10},{3,11},{4,12},{5,13},{6,14},{7,15},{8,16},{9,17... | collective-permute-start | bytes 417800 | tf_op jit(solution)/shard_map/ppermute | solution.py:672
  44.2 1.9 %collective-permute-start.9 = (bf16[272,256]{1,0:T(8,128)(2,1)S(1)}, bf16[272,256]{1,0:T(8,128)(2,1)S(1)}, u32[]{:S(2)}, u32[]{:S(2)}) collective-permute-start(bf16[272,256]{1,0:T(8,128)(2,1)S(1)} %get-tuple-element.75.refs_2_), channel_id=1, source_target_pairs={{0,8},{1,9},{2,10},{3,11},{4,12},{5,13},{6,14},{7,15},{8,16},{9,17... | collective-permute-start | bytes 417800 | tf_op jit(solution)/shard_map/ppermute | solution.py:672
  46.1 2.4 %collective-permute-done.10.refs_1_ = bf16[272,256]{1,0:T(8,128)(2,1)S(1)} collective-permute-done((bf16[272,256]{1,0:T(8,128)(2,1)S(1)}, bf16[272,256]{1,0:T(8,128)(2,1)S(1)}, u32[]{:S(2)}, u32[]{:S(2)}) %collective-permute-start.10) | collective-permute-done | bytes 139296 | tf_op jit(solution)/shard_map/ppermute | solution.py:672
  48.6 3.0 %collective-permute-done.9.refs_0_ = bf16[272,256]{1,0:T(8,128)(2,1)S(1)} collective-permute-done((bf16[272,256]{1,0:T(8,128)(2,1)S(1)}, bf16[272,256]{1,0:T(8,128)(2,1)S(1)}, u32[]{:S(2)}, u32[]{:S(2)}) %collective-permute-start.9) | collective-permute-done | bytes 139296 | tf_op jit(solution)/shard_map/ppermute | solution.py:672
  52.6 1.4 %collective-permute-start.12 = (bf16[128,1024]{1,0:T(8,128)(2,1)S(1)}, bf16[128,1024]{1,0:T(8,128)(2,1)S(1)}, u32[]{:S(2)}, u32[]{:S(2)}) collective-permute-start(bf16[128,1024]{1,0:T(8,128)(2,1)S(1)} %get-tuple-element.79), channel_id=1, source_target_pairs={{0,1},{1,0},{2,3},{3,2},{4,5},{5,4},{6,7},{7,6},{8,9},{9,8},{10,11... | collective-permute-start | bytes 786440 | tf_op jit(solution)/shard_map/ppermute | solution.py:672
  54.1 1.5 %collective-permute-start.13 = (bf16[128,1024]{1,0:T(8,128)(2,1)S(1)}, bf16[128,1024]{1,0:T(8,128)(2,1)S(1)}, u32[]{:S(2)}, u32[]{:S(2)}) collective-permute-start(bf16[128,1024]{1,0:T(8,128)(2,1)S(1)} %get-tuple-element.80), channel_id=1, source_target_pairs={{0,2},{1,3},{2,0},{3,1},{4,6},{5,7},{6,4},{7,5},{8,10},{9,11},{10,... | collective-permute-start | bytes 786440 | tf_op jit(solution)/shard_map/ppermute | solution.py:672
  55.6 2.6 %state.5 = (bf16[512,768]{1,0:T(8,128)(2,1)S(1)}, f32[256,768]{1,0:T(8,128)S(1)}, bf16[272,384]{1,0:T(8,128)(2,1)S(1)}, bf16[272,384]{1,0:T(8,128)(2,1)S(1)}) custom-call(s32[5]{0:T(128)S(1)} %stack.23.place, bf16[128,768]{1,0:T(8,128)(2,1)S(1)} %get-tuple-element.70.refs_9_.refs_0_, bf16[128,768]{1,0:T(8,128)(2,1)S(1)} %collective-permute-done.15.refs_1_, ...), custom_call_target="tpu_custom_call" | custom-call | flops 1 | bytes 1 | tf_op jit(solution)/shard_map/state/pallas_call | solution.py:647
  58.2 1.9 %collective-permute-start.18 = (bf16[272,384]{1,0:T(8,128)(2,1)S(1)}, bf16[272,384]{1,0:T(8,128)(2,1)S(1)}, u32[]{:S(2)}, u32[]{:S(2)}) collective-permute-start(bf16[272,384]{1,0:T(8,128)(2,1)S(1)} %get-tuple-element.85.refs_1_), channel_id=1, source_target_pairs={{0,8},{1,9},{2,10},{3,11},{4,12},{5,13},{6,14},{7,15},{8,16},{9,17... | collective-permute-start | bytes 626696 | tf_op jit(solution)/shard_map/ppermute | solution.py:672
  60.1 1.9 %collective-permute-start.19 = (bf16[272,384]{1,0:T(8,128)(2,1)S(1)}, bf16[272,384]{1,0:T(8,128)(2,1)S(1)}, u32[]{:S(2)}, u32[]{:S(2)}) collective-permute-start(bf16[272,384]{1,0:T(8,128)(2,1)S(1)} %get-tuple-element.86.refs_1_), channel_id=1, source_target_pairs={{0,8},{1,9},{2,10},{3,11},{4,12},{5,13},{6,14},{7,15},{8,16},{9,17... | collective-permute-start | bytes 626696 | tf_op jit(solution)/shard_map/ppermute | solution.py:672
  62.1 3.9 %collective-permute-done.18.refs_0_ = bf16[272,384]{1,0:T(8,128)(2,1)S(1)} collective-permute-done((bf16[272,384]{1,0:T(8,128)(2,1)S(1)}, bf16[272,384]{1,0:T(8,128)(2,1)S(1)}, u32[]{:S(2)}, u32[]{:S(2)}) %collective-permute-start.18) | collective-permute-done | bytes 208928 | tf_op jit(solution)/shard_map/ppermute | solution.py:672
  67.3 2.0 %collective-permute-done.19.refs_0_.refs_1_ = bf16[272,384]{1,0:T(8,128)(2,1)S(1)} collective-permute-done((bf16[272,384]{1,0:T(8,128)(2,1)S(1)}, bf16[272,384]{1,0:T(8,128)(2,1)S(1)}, u32[]{:S(2)}, u32[]{:S(2)}) %collective-permute-start.19) | collective-permute-done | bytes 208928 | tf_op jit(solution)/shard_map/ppermute | solution.py:672
  70.8 5.8 %collective-permute-done.14.refs_3_ = bf16[128,1024]{1,0:T(8,128)(2,1)S(1)} collective-permute-done((bf16[128,1024]{1,0:T(8,128)(2,1)S(1)}, bf16[128,1024]{1,0:T(8,128)(2,1)S(1)}, u32[]{:S(2)}, u32[]{:S(2)}) %collective-permute-start.14) | collective-permute-done | bytes 262176 | tf_op jit(solution)/shard_map/ppermute | solution.py:672
  76.6 1.9 %state.6 = (bf16[512,384]{1,0:T(8,128)(2,1)S(1)}, f32[256,384]{1,0:T(8,128)S(1)}, bf16[272,384]{1,0:T(8,128)(2,1)S(1)}) custom-call(s32[5]{0:T(128)S(1)} %stack.23.place, bf16[128,1024]{1,0:T(8,128)(2,1)S(1)} %get-tuple-element.78.refs_10_.refs_0_, bf16[128,1024]{1,0:T(8,128)(2,1)S(1)} %collective-permute-done.12.refs_1_, ...), custom_call_target="tpu_custom_call" | custom-call | flops 1 | bytes 1 | tf_op jit(solution)/shard_map/state/pallas_call | solution.py:647
  78.5 2.1 %collective-permute-start.23 = (bf16[272,384]{1,0:T(8,128)(2,1)S(1)}, bf16[272,384]{1,0:T(8,128)(2,1)S(1)}, u32[]{:S(2)}, u32[]{:S(2)}) collective-permute-start(bf16[272,384]{1,0:T(8,128)(2,1)S(1)} %get-tuple-element.87.refs_10_.refs_1_), channel_id=1, source_target_pairs={{0,8},{1,9},{2,10},{3,11},{4,12},{5,13},{6,14},{7,15},{16,24},{17,... | collective-permute-start | bytes 626696 | tf_op jit(solution)/shard_map/ppermute | solution.py:672
  81.8 1.9 %state.7 = (bf16[512,384]{1,0:T(8,128)(2,1)S(1)}, f32[256,384]{1,0:T(8,128)S(1)}, bf16[272,384]{1,0:T(8,128)(2,1)S(1)}) custom-call(s32[5]{0:T(128)S(1)} %stack.23.place, bf16[128,1024]{1,0:T(8,128)(2,1)S(1)} %get-tuple-element.78.refs_10_.refs_0_, bf16[128,1024]{1,0:T(8,128)(2,1)S(1)} %collective-permute-done.12.refs_1_, ...), custom_call_target="tpu_custom_call" | custom-call | flops 1 | bytes 1 | tf_op jit(solution)/shard_map/state/pallas_call | solution.py:647
  87.0 1.5 %collective-permute-start.25 = (bf16[272,384]{1,0:T(8,128)(2,1)S(1)}, bf16[272,384]{1,0:T(8,128)(2,1)S(1)}, u32[]{:S(2)}, u32[]{:S(2)}) collective-permute-start(bf16[272,384]{1,0:T(8,128)(2,1)S(1)} %combine.8.refs_12_), channel_id=1, source_target_pairs={{8,16},{9,17},{10,18},{11,19},{12,20},{13,21},{14,22},{15,23}} | collective-permute-start | bytes 626696 | tf_op jit(solution)/shard_map/ppermute | solution.py:672
  88.5 2.6 %final.4 = (bf16[256,768]{1,0:T(8,128)(2,1)S(1)}, bf16[256,768]{1,0:T(8,128)(2,1)S(1)}) custom-call(s32[5]{0:T(128)S(1)} %stack.23.place, bf16[272,384]{1,0:T(8,128)(2,1)S(1)} %collective-permute-done.18.refs_0_, bf16[272,384]{1,0:T(8,128)(2,1)S(1)} %collective-permute-done.19.refs_0_.refs_1_, bf16[272,384]{1,0:T(8,128)(2,1)S(1)} %collective-permute-done.20.refs_9_.refs_2_, ...), custom_call_target="tpu_custom_call" | custom-call | flops 1 | bytes 1 | tf_op jit(solution)/shard_map/final/pallas_call | solution.py:647
  93.1 3.4 %collective-permute-start.29 = (bf16[256,768]{1,0:T(8,128)(2,1)S(1)}, bf16[256,768]{1,0:T(8,128)(2,1)S(1)}, u32[]{:S(2)}, u32[]{:S(2)}) collective-permute-start(bf16[256,768]{1,0:T(8,128)(2,1)S(1)} %get-tuple-element.106), channel_id=1, source_target_pairs={{0,4},{1,5},{2,6},{3,7},{4,0},{5,1},{6,2},{7,3},{8,12},{9,13},{10,... | collective-permute-start | bytes 1179656 | tf_op jit(solution)/shard_map/ppermute | solution.py:672
  98.1 1.9 %final.5 = (bf16[256,512]{1,0:T(8,128)(2,1)S(1)}, bf16[256,512]{1,0:T(8,128)(2,1)S(1)}) custom-call(s32[5]{0:T(128)S(1)} %stack.23.place, bf16[272,256]{1,0:T(8,128)(2,1)S(1)} %collective-permute-done.9.refs_0_, bf16[272,256]{1,0:T(8,128)(2,1)S(1)} %collective-permute-done.10.refs_1_, bf16[272,512]{1,0:T(8,128)(2,1)S(1)} %collective-permute-done.11.refs_2_, ...), custom_call_target="tpu_custom_call" | custom-call | flops 1 | bytes 1 | tf_op jit(solution)/shard_map/final/pallas_call | solution.py:647
  102.3 3.7 %collective-permute-start.31 = (bf16[256,384]{1,0:T(8,128)(2,1)S(1)}, bf16[256,384]{1,0:T(8,128)(2,1)S(1)}, u32[]{:S(2)}, u32[]{:S(2)}) collective-permute-start(bf16[256,384]{1,0:T(8,128)(2,1)S(1)} %get-tuple-element.108), channel_id=1, source_target_pairs={{0,4},{1,5},{2,6},{3,7},{4,0},{5,1},{6,2},{7,3},{8,12},{9,13},{10,... | collective-permute-start | bytes 589832 | tf_op jit(solution)/shard_map/ppermute | solution.py:672
  107.4 1.9 %place.1 = bf16[256,4096]{1,0:T(8,128)(2,1)} custom-call(s32[5]{0:T(128)S(1)} %stack.23.place, bf16[256,512]{1,0:T(8,128)(2,1)S(1)} %get-tuple-element.100.refs_7_.refs_0_, bf16[256,768]{1,0:T(8,128)(2,1)S(1)} %get-tuple-element.99.refs_2_.refs_1_, bf16[256,384]{1,0:T(8,128)(2,1)S(1)} %get-tuple-element.102.refs_7_.refs_2_, ...), custom_call_target="tpu_custom_call" | custom-call | flops 1 | bytes 1 | tf_op jit(solution)/shard_map/place/pallas_call | solution.py:623
  (74 shorter events, 24.4 us)
Async XLA Ops:
  4.1 10.4 %collective-permute-start.4 = (bf16[64,8448]{1,0:T(8,128)(2,1)S(1)}, bf16[64,8448]{1,0:T(8,128)(2,1)S(1)}, u32[]{:S(2)}, u32[]{:S(2)}) collective-permute-start(bf16[64,8448]{1,0:T(8,128)(2,1)S(1)} %get-tuple-element.62), channel_id=1, source_target_pairs={{0,4},{1,5},{2,6},{3,7},{4,0},{5,1},{6,2},{7,3},{8,12},{9,13},{10,... | collective-permute-start | bytes 3244040 | tf_op jit(solution)/shard_map/ppermute | solution.py:672
  4.9 3.1 %collective-permute-start = (bf16[64,4096]{1,0:T(8,128)(2,1)S(1)}, bf16[64,4096]{1,0:T(8,128)(2,1)S(1)}, u32[]{:S(2)}, u32[]{:S(2)}) collective-permute-start(bf16[64,4096]{1,0:T(8,128)(2,1)S(1)} %pack_first.1.order), channel_id=1, source_target_pairs={{0,4},{1,5},{2,6},{3,7},{4,0},{5,1},{6,2},{7,3},{8,12},{9,13},{10,... | collective-permute-start | bytes 1572872 | tf_op jit(solution)/shard_map/ppermute | solution.py:672
  8.8 9.7 %collective-permute-start.1 = (bf16[128,512]{1,0:T(8,128)(2,1)S(1)}, bf16[128,512]{1,0:T(8,128)(2,1)S(1)}, u32[]{:S(2)}, u32[]{:S(2)}) collective-permute-start(bf16[128,512]{1,0:T(8,128)(2,1)S(1)} %get-tuple-element.59), channel_id=1, source_target_pairs={{0,1},{1,0},{2,3},{3,2},{4,5},{5,4},{6,7},{7,6},{8,9},{9,8},{10,11... | collective-permute-start | bytes 393224 | tf_op jit(solution)/shard_map/ppermute | solution.py:672
  9.0 5.5 %collective-permute-start.5 = (bf16[3,10240]{1,0:T(4,128)(2,1)S(1)}, bf16[3,10240]{1,0:T(4,128)(2,1)S(1)}, u32[]{:S(2)}, u32[]{:S(2)}) collective-permute-start(bf16[3,10240]{1,0:T(4,128)(2,1)S(1)} %get-tuple-element.65), channel_id=1, source_target_pairs={{3,11},{7,15},{11,19},{15,23},{19,27},{23,31}} | collective-permute-start | bytes 184328 | tf_op jit(solution)/shard_map/ppermute | solution.py:672
  9.7 16.4 %collective-permute-start.2 = (bf16[128,512]{1,0:T(8,128)(2,1)S(1)}, bf16[128,512]{1,0:T(8,128)(2,1)S(1)}, u32[]{:S(2)}, u32[]{:S(2)}) collective-permute-start(bf16[128,512]{1,0:T(8,128)(2,1)S(1)} %get-tuple-element.60), channel_id=1, source_target_pairs={{0,2},{1,3},{2,0},{3,1},{4,6},{5,7},{6,4},{7,5},{8,10},{9,11},{10,... | collective-permute-start | bytes 393224 | tf_op jit(solution)/shard_map/ppermute | solution.py:672
  14.5 14.4 %collective-permute-start.3 = (bf16[128,512]{1,0:T(8,128)(2,1)S(1)}, bf16[128,512]{1,0:T(8,128)(2,1)S(1)}, u32[]{:S(2)}, u32[]{:S(2)}) collective-permute-start(bf16[128,512]{1,0:T(8,128)(2,1)S(1)} %get-tuple-element.61), channel_id=1, source_target_pairs={{0,3},{1,2},{2,1},{3,0},{4,7},{5,6},{6,5},{7,4},{8,11},{9,10},{10,... | collective-permute-start | bytes 393224 | tf_op jit(solution)/shard_map/ppermute | solution.py:672
  15.6 15.5 %collective-permute-start.7 = (bf16[128,384]{1,0:T(8,128)(2,1)S(1)}, bf16[128,384]{1,0:T(8,128)(2,1)S(1)}, u32[]{:S(2)}, u32[]{:S(2)}) collective-permute-start(bf16[128,384]{1,0:T(8,128)(2,1)S(1)} %get-tuple-element.68), channel_id=1, source_target_pairs={{0,2},{1,3},{2,0},{3,1},{4,6},{5,7},{6,4},{7,5},{8,10},{9,11},{10,... | collective-permute-start | bytes 294920 | tf_op jit(solution)/shard_map/ppermute | solution.py:672
  18.5 14.6 %collective-permute-start.8 = (bf16[128,384]{1,0:T(8,128)(2,1)S(1)}, bf16[128,384]{1,0:T(8,128)(2,1)S(1)}, u32[]{:S(2)}, u32[]{:S(2)}) collective-permute-start(bf16[128,384]{1,0:T(8,128)(2,1)S(1)} %get-tuple-element.69), channel_id=1, source_target_pairs={{0,3},{1,2},{2,1},{3,0},{4,7},{5,6},{6,5},{7,4},{8,11},{9,10},{10,... | collective-permute-start | bytes 294920 | tf_op jit(solution)/shard_map/ppermute | solution.py:672
  18.6 19.5 %collective-permute-start.6 = (bf16[128,384]{1,0:T(8,128)(2,1)S(1)}, bf16[128,384]{1,0:T(8,128)(2,1)S(1)}, u32[]{:S(2)}, u32[]{:S(2)}) collective-permute-start(bf16[128,384]{1,0:T(8,128)(2,1)S(1)} %get-tuple-element.67), channel_id=1, source_target_pairs={{0,1},{1,0},{2,3},{3,2},{4,5},{5,4},{6,7},{7,6},{8,9},{9,8},{10,11... | collective-permute-start | bytes 294920 | tf_op jit(solution)/shard_map/ppermute | solution.py:672
  33.9 21.7 %collective-permute-start.15 = (bf16[128,768]{1,0:T(8,128)(2,1)S(1)}, bf16[128,768]{1,0:T(8,128)(2,1)S(1)}, u32[]{:S(2)}, u32[]{:S(2)}) collective-permute-start(bf16[128,768]{1,0:T(8,128)(2,1)S(1)} %get-tuple-element.82), channel_id=1, source_target_pairs={{0,1},{1,0},{2,3},{3,2},{4,5},{5,4},{6,7},{7,6},{8,9},{9,8},{10,11... | collective-permute-start | bytes 589832 | tf_op jit(solution)/shard_map/ppermute | solution.py:672
  34.0 21.6 %collective-permute-start.16 = (bf16[128,768]{1,0:T(8,128)(2,1)S(1)}, bf16[128,768]{1,0:T(8,128)(2,1)S(1)}, u32[]{:S(2)}, u32[]{:S(2)}) collective-permute-start(bf16[128,768]{1,0:T(8,128)(2,1)S(1)} %get-tuple-element.83), channel_id=1, source_target_pairs={{0,2},{1,3},{2,0},{3,1},{4,6},{5,7},{6,4},{7,5},{8,10},{9,11},{10,... | collective-permute-start | bytes 589832 | tf_op jit(solution)/shard_map/ppermute | solution.py:672
  37.4 18.2 %collective-permute-start.17 = (bf16[128,768]{1,0:T(8,128)(2,1)S(1)}, bf16[128,768]{1,0:T(8,128)(2,1)S(1)}, u32[]{:S(2)}, u32[]{:S(2)}) collective-permute-start(bf16[128,768]{1,0:T(8,128)(2,1)S(1)} %get-tuple-element.84), channel_id=1, source_target_pairs={{0,3},{1,2},{2,1},{3,0},{4,7},{5,6},{6,5},{7,4},{8,11},{9,10},{10,... | collective-permute-start | bytes 589832 | tf_op jit(solution)/shard_map/ppermute | solution.py:672
  41.9 6.7 %collective-permute-start.10 = (bf16[272,256]{1,0:T(8,128)(2,1)S(1)}, bf16[272,256]{1,0:T(8,128)(2,1)S(1)}, u32[]{:S(2)}, u32[]{:S(2)}) collective-permute-start(bf16[272,256]{1,0:T(8,128)(2,1)S(1)} %get-tuple-element.76.refs_3_), channel_id=1, source_target_pairs={{0,8},{1,9},{2,10},{3,11},{4,12},{5,13},{6,14},{7,15},{8,16},{9,17... | collective-permute-start | bytes 417800 | tf_op jit(solution)/shard_map/ppermute | solution.py:672
  44.2 7.4 %collective-permute-start.9 = (bf16[272,256]{1,0:T(8,128)(2,1)S(1)}, bf16[272,256]{1,0:T(8,128)(2,1)S(1)}, u32[]{:S(2)}, u32[]{:S(2)}) collective-permute-start(bf16[272,256]{1,0:T(8,128)(2,1)S(1)} %get-tuple-element.75.refs_2_), channel_id=1, source_target_pairs={{0,8},{1,9},{2,10},{3,11},{4,12},{5,13},{6,14},{7,15},{8,16},{9,17... | collective-permute-start | bytes 417800 | tf_op jit(solution)/shard_map/ppermute | solution.py:672
  52.6 18.1 %collective-permute-start.12 = (bf16[128,1024]{1,0:T(8,128)(2,1)S(1)}, bf16[128,1024]{1,0:T(8,128)(2,1)S(1)}, u32[]{:S(2)}, u32[]{:S(2)}) collective-permute-start(bf16[128,1024]{1,0:T(8,128)(2,1)S(1)} %get-tuple-element.79), channel_id=1, source_target_pairs={{0,1},{1,0},{2,3},{3,2},{4,5},{5,4},{6,7},{7,6},{8,9},{9,8},{10,11... | collective-permute-start | bytes 786440 | tf_op jit(solution)/shard_map/ppermute | solution.py:672
  54.1 16.7 %collective-permute-start.13 = (bf16[128,1024]{1,0:T(8,128)(2,1)S(1)}, bf16[128,1024]{1,0:T(8,128)(2,1)S(1)}, u32[]{:S(2)}, u32[]{:S(2)}) collective-permute-start(bf16[128,1024]{1,0:T(8,128)(2,1)S(1)} %get-tuple-element.80), channel_id=1, source_target_pairs={{0,2},{1,3},{2,0},{3,1},{4,6},{5,7},{6,4},{7,5},{8,10},{9,11},{10,... | collective-permute-start | bytes 786440 | tf_op jit(solution)/shard_map/ppermute | solution.py:672
  55.6 21.0 %collective-permute-start.14 = (bf16[128,1024]{1,0:T(8,128)(2,1)S(1)}, bf16[128,1024]{1,0:T(8,128)(2,1)S(1)}, u32[]{:S(2)}, u32[]{:S(2)}) collective-permute-start(bf16[128,1024]{1,0:T(8,128)(2,1)S(1)} %get-tuple-element.81), channel_id=1, source_target_pairs={{0,3},{1,2},{2,1},{3,0},{4,7},{5,6},{6,5},{7,4},{8,11},{9,10},{10,... | collective-permute-start | bytes 786440 | tf_op jit(solution)/shard_map/ppermute | solution.py:672
  58.2 7.7 %collective-permute-start.18 = (bf16[272,384]{1,0:T(8,128)(2,1)S(1)}, bf16[272,384]{1,0:T(8,128)(2,1)S(1)}, u32[]{:S(2)}, u32[]{:S(2)}) collective-permute-start(bf16[272,384]{1,0:T(8,128)(2,1)S(1)} %get-tuple-element.85.refs_1_), channel_id=1, source_target_pairs={{0,8},{1,9},{2,10},{3,11},{4,12},{5,13},{6,14},{7,15},{8,16},{9,17... | collective-permute-start | bytes 626696 | tf_op jit(solution)/shard_map/ppermute | solution.py:672
  60.1 9.2 %collective-permute-start.19 = (bf16[272,384]{1,0:T(8,128)(2,1)S(1)}, bf16[272,384]{1,0:T(8,128)(2,1)S(1)}, u32[]{:S(2)}, u32[]{:S(2)}) collective-permute-start(bf16[272,384]{1,0:T(8,128)(2,1)S(1)} %get-tuple-element.86.refs_1_), channel_id=1, source_target_pairs={{0,8},{1,9},{2,10},{3,11},{4,12},{5,13},{6,14},{7,15},{8,16},{9,17... | collective-permute-start | bytes 626696 | tf_op jit(solution)/shard_map/ppermute | solution.py:672
  66.0 19.0 %collective-permute-start.20 = (bf16[272,384]{1,0:T(8,128)(2,1)S(1)}, bf16[272,384]{1,0:T(8,128)(2,1)S(1)}, u32[]{:S(2)}, u32[]{:S(2)}) collective-permute-start(bf16[272,384]{1,0:T(8,128)(2,1)S(1)} %combine.6.refs_2_.refs_10_), channel_id=1, source_target_pairs={{0,16},{1,17},{2,18},{3,19},{4,20},{5,21},{6,22},{7,23},{8,24},{9,... | collective-permute-start | bytes 626696 | tf_op jit(solution)/shard_map/ppermute | solution.py:672
  69.5 15.6 %collective-permute-start.21 = (bf16[272,384]{1,0:T(8,128)(2,1)S(1)}, bf16[272,384]{1,0:T(8,128)(2,1)S(1)}, u32[]{:S(2)}, u32[]{:S(2)}) collective-permute-start(bf16[272,384]{1,0:T(8,128)(2,1)S(1)} %combine.7.refs_11_), channel_id=1, source_target_pairs={{0,16},{1,17},{2,18},{3,19},{4,20},{5,21},{6,22},{7,23},{8,24},{9,... | collective-permute-start | bytes 626696 | tf_op jit(solution)/shard_map/ppermute | solution.py:672
  78.5 7.8 %collective-permute-start.23 = (bf16[272,384]{1,0:T(8,128)(2,1)S(1)}, bf16[272,384]{1,0:T(8,128)(2,1)S(1)}, u32[]{:S(2)}, u32[]{:S(2)}) collective-permute-start(bf16[272,384]{1,0:T(8,128)(2,1)S(1)} %get-tuple-element.87.refs_10_.refs_1_), channel_id=1, source_target_pairs={{0,8},{1,9},{2,10},{3,11},{4,12},{5,13},{6,14},{7,15},{16,24},{17,... | collective-permute-start | bytes 626696 | tf_op jit(solution)/shard_map/ppermute | solution.py:672
  80.5 12.6 %collective-permute-start.11 = (bf16[272,512]{1,0:T(8,128)(2,1)S(1)}, bf16[272,512]{1,0:T(8,128)(2,1)S(1)}, u32[]{:S(2)}, u32[]{:S(2)}) collective-permute-start(bf16[272,512]{1,0:T(8,128)(2,1)S(1)} %combine.5.refs_0_), channel_id=1, source_target_pairs={{0,16},{1,17},{2,18},{3,19},{4,20},{5,21},{6,22},{7,23},{8,24},{9,... | collective-permute-start | bytes 835592 | tf_op jit(solution)/shard_map/ppermute | solution.py:672
  83.7 7.3 %collective-permute-start.22 = (bf16[272,384]{1,0:T(8,128)(2,1)S(1)}, bf16[272,384]{1,0:T(8,128)(2,1)S(1)}, u32[]{:S(2)}, u32[]{:S(2)}) collective-permute-start(bf16[272,384]{1,0:T(8,128)(2,1)S(1)} %get-tuple-element.88.refs_8_.refs_1_), channel_id=1, source_target_pairs={{0,8},{1,9},{2,10},{3,11},{4,12},{5,13},{6,14},{7,15},{16,24},{17,... | collective-permute-start | bytes 626696 | tf_op jit(solution)/shard_map/ppermute | solution.py:672
  86.3 13.7 %collective-permute-start.24 = (bf16[272,384]{1,0:T(8,128)(2,1)S(1)}, bf16[272,384]{1,0:T(8,128)(2,1)S(1)}, u32[]{:S(2)}, u32[]{:S(2)}) collective-permute-start(bf16[272,384]{1,0:T(8,128)(2,1)S(1)} %combine.8.refs_12_), channel_id=1, source_target_pairs={{8,24},{9,25},{10,26},{11,27},{12,28},{13,29},{14,30},{15,31}} | collective-permute-start | bytes 626696 | tf_op jit(solution)/shard_map/ppermute | solution.py:672
  87.0 13.1 %collective-permute-start.25 = (bf16[272,384]{1,0:T(8,128)(2,1)S(1)}, bf16[272,384]{1,0:T(8,128)(2,1)S(1)}, u32[]{:S(2)}, u32[]{:S(2)}) collective-permute-start(bf16[272,384]{1,0:T(8,128)(2,1)S(1)} %combine.8.refs_12_), channel_id=1, source_target_pairs={{8,16},{9,17},{10,18},{11,19},{12,20},{13,21},{14,22},{15,23}} | collective-permute-start | bytes 626696 | tf_op jit(solution)/shard_map/ppermute | solution.py:672
  91.1 10.1 %collective-permute-start.26 = (bf16[272,384]{1,0:T(8,128)(2,1)S(1)}, bf16[272,384]{1,0:T(8,128)(2,1)S(1)}, u32[]{:S(2)}, u32[]{:S(2)}) collective-permute-start(bf16[272,384]{1,0:T(8,128)(2,1)S(1)} %combine.9.refs_0_), channel_id=1, source_target_pairs={{8,24},{9,25},{10,26},{11,27},{12,28},{13,29},{14,30},{15,31}} | collective-permute-start | bytes 626696 | tf_op jit(solution)/shard_map/ppermute | solution.py:672
  91.8 9.4 %collective-permute-start.27 = (bf16[272,384]{1,0:T(8,128)(2,1)S(1)}, bf16[272,384]{1,0:T(8,128)(2,1)S(1)}, u32[]{:S(2)}, u32[]{:S(2)}) collective-permute-start(bf16[272,384]{1,0:T(8,128)(2,1)S(1)} %combine.9.refs_0_), channel_id=1, source_target_pairs={{8,16},{9,17},{10,18},{11,19},{12,20},{13,21},{14,22},{15,23}} | collective-permute-start | bytes 626696 | tf_op jit(solution)/shard_map/ppermute | solution.py:672
  93.1 12.9 %collective-permute-start.29 = (bf16[256,768]{1,0:T(8,128)(2,1)S(1)}, bf16[256,768]{1,0:T(8,128)(2,1)S(1)}, u32[]{:S(2)}, u32[]{:S(2)}) collective-permute-start(bf16[256,768]{1,0:T(8,128)(2,1)S(1)} %get-tuple-element.106), channel_id=1, source_target_pairs={{0,4},{1,5},{2,6},{3,7},{4,0},{5,1},{6,2},{7,3},{8,12},{9,13},{10,... | collective-permute-start | bytes 1179656 | tf_op jit(solution)/shard_map/ppermute | solution.py:672
  100.0 6.0 %collective-permute-start.28 = (bf16[256,512]{1,0:T(8,128)(2,1)S(1)}, bf16[256,512]{1,0:T(8,128)(2,1)S(1)}, u32[]{:S(2)}, u32[]{:S(2)}) collective-permute-start(bf16[256,512]{1,0:T(8,128)(2,1)S(1)} %get-tuple-element.105), channel_id=1, source_target_pairs={{0,4},{1,5},{2,6},{3,7},{4,0},{5,1},{6,2},{7,3},{8,12},{9,13},{10,... | collective-permute-start | bytes 786440 | tf_op jit(solution)/shard_map/ppermute | solution.py:672
  102.3 4.7 %collective-permute-start.31 = (bf16[256,384]{1,0:T(8,128)(2,1)S(1)}, bf16[256,384]{1,0:T(8,128)(2,1)S(1)}, u32[]{:S(2)}, u32[]{:S(2)}) collective-permute-start(bf16[256,384]{1,0:T(8,128)(2,1)S(1)} %get-tuple-element.108), channel_id=1, source_target_pairs={{0,4},{1,5},{2,6},{3,7},{4,0},{5,1},{6,2},{7,3},{8,12},{9,13},{10,... | collective-permute-start | bytes 589832 | tf_op jit(solution)/shard_map/ppermute | solution.py:672
  106.0 1.4 %collective-permute-start.30 = (bf16[256,384]{1,0:T(8,128)(2,1)S(1)}, bf16[256,384]{1,0:T(8,128)(2,1)S(1)}, u32[]{:S(2)}, u32[]{:S(2)}) collective-permute-start(bf16[256,384]{1,0:T(8,128)(2,1)S(1)} %get-tuple-element.107), channel_id=1, source_target_pairs={{0,4},{1,5},{2,6},{3,7},{4,0},{5,1},{6,2},{7,3},{8,12},{9,13},{10,... | collective-permute-start | bytes 589832 | tf_op jit(solution)/shard_map/ppermute | solution.py:672
  (8 other events, 115.3 us)

commit v11 on v10

--- a/solution.py
+++ b/solution.py
@@ -163,11 +163,11 @@
 LANES = 128
 LOG2E = 1.4426950408889634
 F32, BF16 = jnp.float32, jnp.bfloat16
-WIDTHS = (512, 0, 768, 768)
-RESTS = ("", "BD", "", "C")
-GROUPED = ((0, 0, 512), (2, 0, 768), (3, 0, 384), (3, 384, 384))
-FIRST_ROUND = ((256, 256), (384, 384), (384,), (384,))
-SECOND_ROUND = ((512,), (384, 384), (384,), (384,))
+WIDTHS = (512, 0, 640, 896)
+RESTS = ("", "BCD", "", "")
+GROUPED = ((0, 0, 512), (2, 0, 640), (3, 0, 512), (3, 512, 384))
+FIRST_ROUND = ((256, 256), (384, 256), (512,), (384,))
+SECOND_ROUND = ((512,), (384, 256), (512,), (384,))
 ALONE = (2, 3)
 
 
@@ -438,8 +438,8 @@
 def score_kernel(shards, place, *refs):
     blocks, refs = refs[:shards], refs[shards:]
     taps, offset, edge_ref, b_ref, c_ref, score_ref, wide = (*refs[:4], *refs[-3:])
-    blocks = view(blocks, 3)
-    start = WIDTHS[3]
+    blocks = view(blocks, 1)
+    start = WIDTHS[1] + STATE
     at = slice(PER_GROUP + STATE, PER_GROUP + 2 * STATE)
 
     def put(start, count, value):
@@ -637,6 +637,20 @@
         self.array = array
 
 
+def gate(blocks, order):
+    anywhere = pl.BlockSpec(memory_space=pl.ANY)
+    return pl.pallas_call(
+        lambda *refs: None,
+        out_shape=[jax.ShapeDtypeStruct(block.shape, block.dtype) for block in blocks],
+        in_specs=[anywhere] * (len(blocks) + len(order)),
+        out_specs=[anywhere] * len(blocks),
+        input_output_aliases={i: i for i in range(len(blocks))},
+        compiler_params=pltpu.CompilerParams(vmem_limit_bytes=16 << 20),
+        cost_estimate=pl.CostEstimate(flops=1, bytes_accessed=1, transcendentals=0),
+        name="gate",
+    )(*blocks, *order)
+
+
 def call(body, outs, operands, scratch=(), flops=0, transcendentals=0, name=None, limit=16 << 20):
     shapes = [jax.ShapeDtypeStruct(shape, dtype) for shape, dtype in outs]
     smem, vmem, hbm = (pl.BlockSpec(memory_space=m) for m in (pltpu.SMEM, pltpu.VMEM, pltpu.HBM))
@@ -730,9 +744,9 @@
     message = [travel(first_blocks)]
     edges = over(edges, lambda i: i + peers if i % shards == shards - 1 else None)
     second_blocks = send_on(plan(1), [first_blocks[0]], None, edges)
-    message.append(travel(second_blocks))
-    third_blocks = send_on(plan(2), [*message[0][1:], *message[1][2:]])
-    message.append(travel(third_blocks))
+    message.append(travel(second_blocks[:1] + gate(second_blocks[1:], message[0][1:])))
+    third_blocks = send_on(plan(2), [second_blocks[0]])
+    message.append(travel(third_blocks[:1] + gate(third_blocks[1:], message[1][2:])))
 
     def seen(piece):
         return message[piece]
@@ -799,44 +813,41 @@
             **more,
         )
 
+    partial = [None] * count
+
+    def local_of(i, order):
+        (partial[i],) = call(
+            functools.partial(local_kernel, first_head(i)),
+            [(x[i].shape, F32)],
+            [x[i], cum, row, score, skip] + [Stay(o) for o in order],
+            name="local",
+        )
+
     state_of(0, [])
-    combine_of(0, [])
-    fourth_blocks = send_on(plan(3), [joined[0][0]])
+    fourth_blocks = send_on(plan(3), sent[0])
     message.append(travel(fourth_blocks))
-    state_of(1, [fourth_blocks[0]])
-    combine_of(1, [])
-    state_of(2, joined[1])
-    state_of(3, sent[2])
     c, score = call(
         functools.partial(score_kernel, shards),
         [((slab, STATE), BF16), ((slab, BLOCK), F32)],
-        [place] + seen(3) + [taps, offset, edge, b] + [Stay(o) for o in sent[3] + before[1]],
+        [place] + seen(1) + [taps, offset, edge, b] + [Stay(o) for o in sent[0]],
         scratch=[pltpu.VMEM((slab + 8, STATE), F32)],
         name="score",
     )
-    mixes = [cum, row, score, skip]
-
-    def in_full(i, order):
-        wide = [pltpu.VMEM((slab, GROUPED[i][2]), F32)]
-        finish_of(finish_kernel, i, [x[i]] + mixes, order, scratch=wide)
-
-    combine_of(2, [score])
-    in_full(1, joined[2])
+    local_of(0, [])
+    combine_of(0, [partial[0]])
+    state_of(1, joined[0])
+    local_of(1, sent[1])
+    combine_of(1, [partial[1]])
+    state_of(2, joined[1])
+    state_of(3, sent[2])
+    finish_of(final_kernel, 0, [partial[0]], sent[3] + before[1])
+    combine_of(2, [keep[0]])
+    finish_of(final_kernel, 1, [partial[1]], joined[2])
     combine_of(3, [keep[1]])
-    order, partial = joined[3][0], {}
-    for i in (2, 3):
-        (partial[i],) = call(
-            functools.partial(local_kernel, first_head(i)),
-            [(x[i].shape, F32)],
-            [x[i]] + mixes + [Stay(order)],
-            name="local",
-        )
-        order = partial[i]
-    in_full(0, [order])
-    order = keep[0]
-    for i in (2, 3):
-        finish_of(final_kernel, i, [partial[i]], [order])
-        order = keep[i]
+    local_of(2, joined[3])
+    local_of(3, [partial[2]])
+    finish_of(final_kernel, 2, [partial[2]], [partial[3]])
+    finish_of(final_kernel, 3, [partial[3]], [keep[2]])
     firsts = [first_head(i) * HEAD_DIM for i in range(count)]
     return put_in_place(firsts, (BLOCK, PAIR * PER_GROUP), place, keep, [swap(o) for o in send])
 

time: 110 us -> 114 us (1.036)
  waiting for transfers between devices: 34.8 us -> 40.1 us
  starting transfers between devices: 43.9 us -> 41.7 us
    ppermute x32, waiting for transfers between devices: 34.8 us -> 40.1 us  [over(): lax.ppermute(block, axes, [(i, j) for i, j in route if j is not None and...]
    ppermute x32, starting transfers between devices: 43.9 us -> 41.7 us  [over(): lax.ppermute(block, axes, [(i, j) for i, j in route if j is not None and...]
    pallas_call x24 -> x26, Pallas kernels: 26.4 us -> 26.8 us  [call(): pl.pallas_call(body, out_shape=shapes, in_specs=specs, out_specs=[vmem] *...]
  transfers between devices with their start and end apart: 32 -> 32, of which waited for: 12 -> 13; matrix products, arithmetic and copies ran while one was open for 0% -> 0% of each run, Pallas kernels for 22% -> 22%
where the time goes in v11:
time: 114 us; the launch traced here: 113 us
  starting transfers between devices  41.7 us (37%)
  waiting for transfers between devices  40.1 us (35%)
  Pallas kernels  28.7 us (25%)
  local copies, waits for them, and re-layouts  1.86 us (2%)
    ppermute x32, starting transfers between devices, over(): lax.ppermute(block, axes, [(i, j) for i, j in route if j is not None and...  41.7 us
    ppermute x32, waiting for transfers between devices, over(): lax.ppermute(block, axes, [(i, j) for i, j in route if j is not None and...  40.1 us
    pallas_call x26, Pallas kernels, call(): pl.pallas_call(body, out_shape=shapes, in_specs=specs, out_specs=[vmem] *...  26.8 us
  transfers between devices with their start and end apart: 32, of which 13 were waited for; matrix products, arithmetic and copies ran while one was open for 0% of the time, Pallas kernels for 22%

profile of v11, /device:TPU:13, one launch (start us, length us, event | category | flops | bytes accessed | tf_op | source)
XLA Modules:
  0.0 113.0 jit_solution(654592063417581641)
XLA Ops:
  0.1 1.7 %copy-done = bf16[64,20480]{1,0:T(8,128)(2,1)S(1)} copy-done((bf16[64,20480]{1,0:T(8,128)(2,1)S(1)}, bf16[64,20480]{1,0:T(8,128)(2,1)}, u32[]{:S(2)}) %copy-start) | copy-done | bytes 2621464
  2.8 1.3 %pack.1 = (bf16[64,8448]{1,0:T(8,128)(2,1)S(1)}, bf16[16,10240]{1,0:T(8,128)(2,1)S(1)}) custom-call(s32[5]{0:T(128)S(1)} %stack.23.place, bf16[64,20480]{1,0:T(8,128)(2,1)S(1)} %copy-done, bf16[64,256]{1,0:T(8,128)(2,1)S(1)} %copy-done.2, bf16[64,4096]{1,0:T(8,128)(2,1)S(1)} %pack_first.1.order), custom_call_target="tpu_custom_call" | custom-call | flops 1 | bytes 1 | tf_op jit(solution)/shard_map/pack/pallas_call | solution.py:661
  5.0 3.0 %collective-permute-done.got_first.got.edges = bf16[64,4096]{1,0:T(8,128)(2,1)S(1)} collective-permute-done((bf16[64,4096]{1,0:T(8,128)(2,1)S(1)}, bf16[64,4096]{1,0:T(8,128)(2,1)S(1)}, u32[]{:S(2)}, u32[]{:S(2)}) %collective-permute-start) | collective-permute-done | bytes 524320 | tf_op jit(solution)/shard_map/ppermute | solution.py:686
  9.0 2.3 %collective-permute-start.2 = (bf16[128,512]{1,0:T(8,128)(2,1)S(1)}, bf16[128,512]{1,0:T(8,128)(2,1)S(1)}, u32[]{:S(2)}, u32[]{:S(2)}) collective-permute-start(bf16[128,512]{1,0:T(8,128)(2,1)S(1)} %get-tuple-element.66), channel_id=1, source_target_pairs={{0,2},{1,3},{2,0},{3,1},{4,6},{5,7},{6,4},{7,5},{8,10},{9,11},{10,... | collective-permute-start | bytes 393224 | tf_op jit(solution)/shard_map/ppermute | solution.py:686
  13.6 3.9 %collective-permute-done.2.refs_4_.refs_2_ = bf16[128,512]{1,0:T(8,128)(2,1)S(1)} collective-permute-done((bf16[128,512]{1,0:T(8,128)(2,1)S(1)}, bf16[128,512]{1,0:T(8,128)(2,1)S(1)}, u32[]{:S(2)}, u32[]{:S(2)}) %collective-permute-start.2) | collective-permute-done | bytes 131104 | tf_op jit(solution)/shard_map/ppermute | solution.py:686
  17.4 5.5 %collective-permute-done.3.refs_5_.refs_3_ = bf16[128,512]{1,0:T(8,128)(2,1)S(1)} collective-permute-done((bf16[128,512]{1,0:T(8,128)(2,1)S(1)}, bf16[128,512]{1,0:T(8,128)(2,1)S(1)}, u32[]{:S(2)}, u32[]{:S(2)}) %collective-permute-start.3) | collective-permute-done | bytes 131104 | tf_op jit(solution)/shard_map/ppermute | solution.py:686
  22.9 1.3 %collective-permute-start.8 = (bf16[128,640]{1,0:T(8,128)(2,1)S(1)}, bf16[128,640]{1,0:T(8,128)(2,1)S(1)}, u32[]{:S(2)}, u32[]{:S(2)}) collective-permute-start(bf16[128,640]{1,0:T(8,128)(2,1)S(1)} %get-tuple-element.78), channel_id=1, source_target_pairs={{0,3},{1,2},{2,1},{3,0},{4,7},{5,6},{6,5},{7,4},{8,11},{9,10},{10,... | collective-permute-start | bytes 491528 | tf_op jit(solution)/shard_map/ppermute | solution.py:686
  24.3 2.2 %collective-permute-start.6 = (bf16[128,640]{1,0:T(8,128)(2,1)S(1)}, bf16[128,640]{1,0:T(8,128)(2,1)S(1)}, u32[]{:S(2)}, u32[]{:S(2)}) collective-permute-start(bf16[128,640]{1,0:T(8,128)(2,1)S(1)} %get-tuple-element.76), channel_id=1, source_target_pairs={{0,1},{1,0},{2,3},{3,2},{4,5},{5,4},{6,7},{7,6},{8,9},{9,8},{10,11... | collective-permute-start | bytes 491528 | tf_op jit(solution)/shard_map/ppermute | solution.py:686
  28.1 10.2 %collective-permute-done.8.refs_3_.refs_4_ = bf16[128,640]{1,0:T(8,128)(2,1)S(1)} collective-permute-done((bf16[128,640]{1,0:T(8,128)(2,1)S(1)}, bf16[128,640]{1,0:T(8,128)(2,1)S(1)}, u32[]{:S(2)}, u32[]{:S(2)}) %collective-permute-start.8) | collective-permute-done | bytes 163872 | tf_op jit(solution)/shard_map/ppermute | solution.py:686
  38.8 2.2 %collective-permute-start.17 = (bf16[128,640]{1,0:T(8,128)(2,1)S(1)}, bf16[128,640]{1,0:T(8,128)(2,1)S(1)}, u32[]{:S(2)}, u32[]{:S(2)}) collective-permute-start(bf16[128,640]{1,0:T(8,128)(2,1)S(1)} %get-tuple-element.102), channel_id=1, source_target_pairs={{0,3},{1,2},{2,1},{3,0},{4,7},{5,6},{6,5},{7,4},{8,11},{9,10},{10,... | collective-permute-start | bytes 491528 | tf_op jit(solution)/shard_map/ppermute | solution.py:686
  41.7 1.7 %prep.1 = (bf16[512,256]{1,0:T(8,128)(2,1)S(1)}, f32[4,2560]{1,0:T(4,128)S(1)}, f32[512,128]{1,0:T(8,128)S(1)}, f32[128,512]{1,0:T(8,128)S(1)}, bf16[512,256]{1,...) custom-call(s32[5]{0:T(128)S(1)} %stack.23.place, ...), custom_call_target="tpu_custom_call" | custom-call | flops 1 | bytes 1 | tf_op jit(solution)/shard_map/prep/pallas_call | solution.py:661
  43.4 2.1 %state.4 = (bf16[512,512]{1,0:T(8,128)(2,1)S(1)}, f32[256,512]{1,0:T(8,128)S(1)}, bf16[272,256]{1,0:T(8,128)(2,1)S(1)}, bf16[272,256]{1,0:T(8,128)(2,1)S(1)}) custom-call(s32[5]{0:T(128)S(1)} %stack.23.place, bf16[128,512]{1,0:T(8,128)(2,1)S(1)} %get-tuple-element.64.refs_0_, bf16[128,512]{1,0:T(8,128)(2,1)S(1)} %collective-permute-done.1.refs_3_.refs_1_, ...), custom_call_target="tpu_custom_call" | custom-call | flops 1 | bytes 1 | tf_op jit(solution)/shard_map/state/pallas_call | solution.py:661
  45.5 3.1 %collective-permute-start.9 = (bf16[272,256]{1,0:T(8,128)(2,1)S(1)}, bf16[272,256]{1,0:T(8,128)(2,1)S(1)}, u32[]{:S(2)}, u32[]{:S(2)}) collective-permute-start(bf16[272,256]{1,0:T(8,128)(2,1)S(1)} %get-tuple-element.84.refs_8_.refs_2_.refs_0_), channel_id=1, source_target_pairs={{0,8},{1,9},{2,10},{3,11},{4,12},{5,13},{6,14},{7,15},{8,16},{9,17... | collective-permute-start | bytes 417800 | tf_op jit(solution)/shard_map/ppermute | solution.py:686
  48.6 1.9 %collective-permute-start.10 = (bf16[272,256]{1,0:T(8,128)(2,1)S(1)}, bf16[272,256]{1,0:T(8,128)(2,1)S(1)}, u32[]{:S(2)}, u32[]{:S(2)}) collective-permute-start(bf16[272,256]{1,0:T(8,128)(2,1)S(1)} %get-tuple-element.85.refs_9_.refs_3_.refs_1_), channel_id=1, source_target_pairs={{0,8},{1,9},{2,10},{3,11},{4,12},{5,13},{6,14},{7,15},{8,16},{9,17... | collective-permute-start | bytes 417800 | tf_op jit(solution)/shard_map/ppermute | solution.py:686
  53.4 3.3 %collective-permute-done.10.refs_1_ = bf16[272,256]{1,0:T(8,128)(2,1)S(1)} collective-permute-done((bf16[272,256]{1,0:T(8,128)(2,1)S(1)}, bf16[272,256]{1,0:T(8,128)(2,1)S(1)}, u32[]{:S(2)}, u32[]{:S(2)}) %collective-permute-start.10) | collective-permute-done | bytes 139296 | tf_op jit(solution)/shard_map/ppermute | solution.py:686
  60.7 2.4 %state.5 = (bf16[512,640]{1,0:T(8,128)(2,1)S(1)}, f32[256,640]{1,0:T(8,128)S(1)}, bf16[272,384]{1,0:T(8,128)(2,1)S(1)}, bf16[272,256]{1,0:T(8,128)(2,1)S(1)}) custom-call(s32[5]{0:T(128)S(1)} %stack.23.place, bf16[128,640]{1,0:T(8,128)(2,1)S(1)} %get-tuple-element.79.refs_9_.refs_0_, bf16[128,640]{1,0:T(8,128)(2,1)S(1)} %collective-permute-done.15.refs_1_, ...), custom_call_target="tpu_custom_call" | custom-call | flops 1 | bytes 1 | tf_op jit(solution)/shard_map/state/pallas_call | solution.py:661
  63.1 1.9 %collective-permute-start.18 = (bf16[272,384]{1,0:T(8,128)(2,1)S(1)}, bf16[272,384]{1,0:T(8,128)(2,1)S(1)}, u32[]{:S(2)}, u32[]{:S(2)}) collective-permute-start(bf16[272,384]{1,0:T(8,128)(2,1)S(1)} %get-tuple-element.103.refs_0_.refs_1_), channel_id=1, source_target_pairs={{0,8},{1,9},{2,10},{3,11},{4,12},{5,13},{6,14},{7,15},{8,16},{9,17... | collective-permute-start | bytes 626696 | tf_op jit(solution)/shard_map/ppermute | solution.py:686
  65.0 1.9 %collective-permute-start.19 = (bf16[272,256]{1,0:T(8,128)(2,1)S(1)}, bf16[272,256]{1,0:T(8,128)(2,1)S(1)}, u32[]{:S(2)}, u32[]{:S(2)}) collective-permute-start(bf16[272,256]{1,0:T(8,128)(2,1)S(1)} %get-tuple-element.105.refs_1_), channel_id=1, source_target_pairs={{0,8},{1,9},{2,10},{3,11},{4,12},{5,13},{6,14},{7,15},{8,16},{9,17... | collective-permute-start | bytes 417800 | tf_op jit(solution)/shard_map/ppermute | solution.py:686
  68.3 2.3 %collective-permute-done.18.refs_0_ = bf16[272,384]{1,0:T(8,128)(2,1)S(1)} collective-permute-done((bf16[272,384]{1,0:T(8,128)(2,1)S(1)}, bf16[272,384]{1,0:T(8,128)(2,1)S(1)}, u32[]{:S(2)}, u32[]{:S(2)}) %collective-permute-start.18) | collective-permute-done | bytes 208928 | tf_op jit(solution)/shard_map/ppermute | solution.py:686
  72.5 4.9 %collective-permute-done.14.refs_3_ = bf16[128,896]{1,0:T(8,128)(2,1)S(1)} collective-permute-done((bf16[128,896]{1,0:T(8,128)(2,1)S(1)}, bf16[128,896]{1,0:T(8,128)(2,1)S(1)}, u32[]{:S(2)}, u32[]{:S(2)}) %collective-permute-start.14) | collective-permute-done | bytes 229408 | tf_op jit(solution)/shard_map/ppermute | solution.py:686
  77.4 2.0 %state.6 = (bf16[512,512]{1,0:T(8,128)(2,1)S(1)}, f32[256,512]{1,0:T(8,128)S(1)}, bf16[272,512]{1,0:T(8,128)(2,1)S(1)}) custom-call(s32[5]{0:T(128)S(1)} %stack.23.place, bf16[128,896]{1,0:T(8,128)(2,1)S(1)} %get-tuple-element.93.refs_0_, bf16[128,896]{1,0:T(8,128)(2,1)S(1)} %collective-permute-done.12.refs_1_, ...), custom_call_target="tpu_custom_call" | custom-call | flops 1 | bytes 1 | tf_op jit(solution)/shard_map/state/pallas_call | solution.py:661
  79.4 1.8 %collective-permute-start.22 = (bf16[272,512]{1,0:T(8,128)(2,1)S(1)}, bf16[272,512]{1,0:T(8,128)(2,1)S(1)}, u32[]{:S(2)}, u32[]{:S(2)}) collective-permute-start(bf16[272,512]{1,0:T(8,128)(2,1)S(1)} %get-tuple-element.106.refs_10_.refs_1_), channel_id=1, source_target_pairs={{0,8},{1,9},{2,10},{3,11},{4,12},{5,13},{6,14},{7,15},{16,24},{17,... | collective-permute-start | bytes 835592 | tf_op jit(solution)/shard_map/ppermute | solution.py:686
  81.2 1.5 %collective-permute-start.20 = (bf16[272,384]{1,0:T(8,128)(2,1)S(1)}, bf16[272,384]{1,0:T(8,128)(2,1)S(1)}, u32[]{:S(2)}, u32[]{:S(2)}) collective-permute-start(bf16[272,384]{1,0:T(8,128)(2,1)S(1)} %combine.6.refs_2_.refs_10_), channel_id=1, source_target_pairs={{0,16},{1,17},{2,18},{3,19},{4,20},{5,21},{6,22},{7,23},{8,24},{9,... | collective-permute-start | bytes 626696 | tf_op jit(solution)/shard_map/ppermute | solution.py:686
  82.7 1.3 %collective-permute-start.21 = (bf16[272,256]{1,0:T(8,128)(2,1)S(1)}, bf16[272,256]{1,0:T(8,128)(2,1)S(1)}, u32[]{:S(2)}, u32[]{:S(2)}) collective-permute-start(bf16[272,256]{1,0:T(8,128)(2,1)S(1)} %combine.7.refs_11_), channel_id=1, source_target_pairs={{0,16},{1,17},{2,18},{3,19},{4,20},{5,21},{6,22},{7,23},{8,24},{9,... | collective-permute-start | bytes 417800 | tf_op jit(solution)/shard_map/ppermute | solution.py:686
  84.0 1.9 %state.7 = (bf16[512,384]{1,0:T(8,128)(2,1)S(1)}, f32[256,384]{1,0:T(8,128)S(1)}, bf16[272,384]{1,0:T(8,128)(2,1)S(1)}) custom-call(s32[5]{0:T(128)S(1)} %stack.23.place, bf16[128,896]{1,0:T(8,128)(2,1)S(1)} %get-tuple-element.93.refs_0_, bf16[128,896]{1,0:T(8,128)(2,1)S(1)} %collective-permute-done.12.refs_1_, ...), custom_call_target="tpu_custom_call" | custom-call | flops 1 | bytes 1 | tf_op jit(solution)/shard_map/state/pallas_call | solution.py:661
  85.9 1.3 %collective-permute-start.25 = (bf16[272,384]{1,0:T(8,128)(2,1)S(1)}, bf16[272,384]{1,0:T(8,128)(2,1)S(1)}, u32[]{:S(2)}, u32[]{:S(2)}) collective-permute-start(bf16[272,384]{1,0:T(8,128)(2,1)S(1)} %get-tuple-element.107.refs_7_.refs_1_), channel_id=1, source_target_pairs={{0,8},{1,9},{2,10},{3,11},{4,12},{5,13},{6,14},{7,15},{16,24},{17,... | collective-permute-start | bytes 626696 | tf_op jit(solution)/shard_map/ppermute | solution.py:686
  87.2 3.6 %collective-permute-done.21.refs_9_.refs_3_ = bf16[272,256]{1,0:T(8,128)(2,1)S(1)} collective-permute-done((bf16[272,256]{1,0:T(8,128)(2,1)S(1)}, bf16[272,256]{1,0:T(8,128)(2,1)S(1)}, u32[]{:S(2)}, u32[]{:S(2)}) %collective-permute-start.21) | collective-permute-done | bytes 139296 | tf_op jit(solution)/shard_map/ppermute | solution.py:686
  92.0 1.3 %collective-permute-start.24 = (bf16[272,512]{1,0:T(8,128)(2,1)S(1)}, bf16[272,512]{1,0:T(8,128)(2,1)S(1)}, u32[]{:S(2)}, u32[]{:S(2)}) collective-permute-start(bf16[272,512]{1,0:T(8,128)(2,1)S(1)} %combine.8.refs_8_), channel_id=1, source_target_pairs={{8,16},{9,17},{10,18},{11,19},{12,20},{13,21},{14,22},{15,23}} | collective-permute-start | bytes 835592 | tf_op jit(solution)/shard_map/ppermute | solution.py:686
  95.4 1.3 %collective-permute-start.27 = (bf16[272,384]{1,0:T(8,128)(2,1)S(1)}, bf16[272,384]{1,0:T(8,128)(2,1)S(1)}, u32[]{:S(2)}, u32[]{:S(2)}) collective-permute-start(bf16[272,384]{1,0:T(8,128)(2,1)S(1)} %combine.9.refs_0_), channel_id=1, source_target_pairs={{8,16},{9,17},{10,18},{11,19},{12,20},{13,21},{14,22},{15,23}} | collective-permute-start | bytes 626696 | tf_op jit(solution)/shard_map/ppermute | solution.py:686
  97.4 2.9 %collective-permute-start.29 = (bf16[256,640]{1,0:T(8,128)(2,1)S(1)}, bf16[256,640]{1,0:T(8,128)(2,1)S(1)}, u32[]{:S(2)}, u32[]{:S(2)}) collective-permute-start(bf16[256,640]{1,0:T(8,128)(2,1)S(1)} %get-tuple-element.118), channel_id=1, source_target_pairs={{0,4},{1,5},{2,6},{3,7},{4,0},{5,1},{6,2},{7,3},{8,12},{9,13},{10,... | collective-permute-start | bytes 983048 | tf_op jit(solution)/shard_map/ppermute | solution.py:686
  102.1 4.4 %collective-permute-start.28 = (bf16[256,512]{1,0:T(8,128)(2,1)S(1)}, bf16[256,512]{1,0:T(8,128)(2,1)S(1)}, u32[]{:S(2)}, u32[]{:S(2)}) collective-permute-start(bf16[256,512]{1,0:T(8,128)(2,1)S(1)} %get-tuple-element.117), channel_id=1, source_target_pairs={{0,4},{1,5},{2,6},{3,7},{4,0},{5,1},{6,2},{7,3},{8,12},{9,13},{10,... | collective-permute-start | bytes 786440 | tf_op jit(solution)/shard_map/ppermute | solution.py:686
  110.9 1.9 %place.1 = bf16[256,4096]{1,0:T(8,128)(2,1)} custom-call(s32[5]{0:T(128)S(1)} %stack.23.place, bf16[256,512]{1,0:T(8,128)(2,1)S(1)} %get-tuple-element.108.refs_2_.refs_0_, bf16[256,640]{1,0:T(8,128)(2,1)S(1)} %get-tuple-element.110.refs_2_.refs_1_, bf16[256,512]{1,0:T(8,128)(2,1)S(1)} %get-tuple-element.114.refs_7_.refs_2_, ...), custom_call_target="tpu_custom_call" | custom-call | flops 1 | bytes 1 | tf_op jit(solution)/shard_map/place/pallas_call | solution.py:623
  (78 shorter events, 28.0 us)
Async XLA Ops:
  4.1 8.0 %collective-permute-start.4 = (bf16[64,8448]{1,0:T(8,128)(2,1)S(1)}, bf16[64,8448]{1,0:T(8,128)(2,1)S(1)}, u32[]{:S(2)}, u32[]{:S(2)}) collective-permute-start(bf16[64,8448]{1,0:T(8,128)(2,1)S(1)} %get-tuple-element.68), channel_id=1, source_target_pairs={{0,4},{1,5},{2,6},{3,7},{4,0},{5,1},{6,2},{7,3},{8,12},{9,13},{10,... | collective-permute-start | bytes 3244040 | tf_op jit(solution)/shard_map/ppermute | solution.py:686
  4.9 3.1 %collective-permute-start = (bf16[64,4096]{1,0:T(8,128)(2,1)S(1)}, bf16[64,4096]{1,0:T(8,128)(2,1)S(1)}, u32[]{:S(2)}, u32[]{:S(2)}) collective-permute-start(bf16[64,4096]{1,0:T(8,128)(2,1)S(1)} %pack_first.1.order), channel_id=1, source_target_pairs={{0,4},{1,5},{2,6},{3,7},{4,0},{5,1},{6,2},{7,3},{8,12},{9,13},{10,... | collective-permute-start | bytes 1572872 | tf_op jit(solution)/shard_map/ppermute | solution.py:686
  8.8 4.8 %collective-permute-start.1 = (bf16[128,512]{1,0:T(8,128)(2,1)S(1)}, bf16[128,512]{1,0:T(8,128)(2,1)S(1)}, u32[]{:S(2)}, u32[]{:S(2)}) collective-permute-start(bf16[128,512]{1,0:T(8,128)(2,1)S(1)} %get-tuple-element.65), channel_id=1, source_target_pairs={{0,1},{1,0},{2,3},{3,2},{4,5},{5,4},{6,7},{7,6},{8,9},{9,8},{10,11... | collective-permute-start | bytes 393224 | tf_op jit(solution)/shard_map/ppermute | solution.py:686
  9.0 8.4 %collective-permute-start.2 = (bf16[128,512]{1,0:T(8,128)(2,1)S(1)}, bf16[128,512]{1,0:T(8,128)(2,1)S(1)}, u32[]{:S(2)}, u32[]{:S(2)}) collective-permute-start(bf16[128,512]{1,0:T(8,128)(2,1)S(1)} %get-tuple-element.66), channel_id=1, source_target_pairs={{0,2},{1,3},{2,0},{3,1},{4,6},{5,7},{6,4},{7,5},{8,10},{9,11},{10,... | collective-permute-start | bytes 393224 | tf_op jit(solution)/shard_map/ppermute | solution.py:686
  11.3 11.6 %collective-permute-start.3 = (bf16[128,512]{1,0:T(8,128)(2,1)S(1)}, bf16[128,512]{1,0:T(8,128)(2,1)S(1)}, u32[]{:S(2)}, u32[]{:S(2)}) collective-permute-start(bf16[128,512]{1,0:T(8,128)(2,1)S(1)} %get-tuple-element.67), channel_id=1, source_target_pairs={{0,3},{1,2},{2,1},{3,0},{4,7},{5,6},{6,5},{7,4},{8,11},{9,10},{10,... | collective-permute-start | bytes 393224 | tf_op jit(solution)/shard_map/ppermute | solution.py:686
  11.5 0.7 collective-permute-start.5
  22.9 5.2 %collective-permute-start.7 = (bf16[128,640]{1,0:T(8,128)(2,1)S(1)}, bf16[128,640]{1,0:T(8,128)(2,1)S(1)}, u32[]{:S(2)}, u32[]{:S(2)}) collective-permute-start(bf16[128,640]{1,0:T(8,128)(2,1)S(1)} %get-tuple-element.77), channel_id=1, source_target_pairs={{0,2},{1,3},{2,0},{3,1},{4,6},{5,7},{6,4},{7,5},{8,10},{9,11},{10,... | collective-permute-start | bytes 491528 | tf_op jit(solution)/shard_map/ppermute | solution.py:686
  22.9 15.4 %collective-permute-start.8 = (bf16[128,640]{1,0:T(8,128)(2,1)S(1)}, bf16[128,640]{1,0:T(8,128)(2,1)S(1)}, u32[]{:S(2)}, u32[]{:S(2)}) collective-permute-start(bf16[128,640]{1,0:T(8,128)(2,1)S(1)} %get-tuple-element.78), channel_id=1, source_target_pairs={{0,3},{1,2},{2,1},{3,0},{4,7},{5,6},{6,5},{7,4},{8,11},{9,10},{10,... | collective-permute-start | bytes 491528 | tf_op jit(solution)/shard_map/ppermute | solution.py:686
  24.3 17.4 %collective-permute-start.6 = (bf16[128,640]{1,0:T(8,128)(2,1)S(1)}, bf16[128,640]{1,0:T(8,128)(2,1)S(1)}, u32[]{:S(2)}, u32[]{:S(2)}) collective-permute-start(bf16[128,640]{1,0:T(8,128)(2,1)S(1)} %get-tuple-element.76), channel_id=1, source_target_pairs={{0,1},{1,0},{2,3},{3,2},{4,5},{5,4},{6,7},{7,6},{8,9},{9,8},{10,11... | collective-permute-start | bytes 491528 | tf_op jit(solution)/shard_map/ppermute | solution.py:686
  38.3 18.9 %collective-permute-start.15 = (bf16[128,640]{1,0:T(8,128)(2,1)S(1)}, bf16[128,640]{1,0:T(8,128)(2,1)S(1)}, u32[]{:S(2)}, u32[]{:S(2)}) collective-permute-start(bf16[128,640]{1,0:T(8,128)(2,1)S(1)} %get-tuple-element.100), channel_id=1, source_target_pairs={{0,1},{1,0},{2,3},{3,2},{4,5},{5,4},{6,7},{7,6},{8,9},{9,8},{10,11... | collective-permute-start | bytes 491528 | tf_op jit(solution)/shard_map/ppermute | solution.py:686
  38.3 22.3 %collective-permute-start.16 = (bf16[128,640]{1,0:T(8,128)(2,1)S(1)}, bf16[128,640]{1,0:T(8,128)(2,1)S(1)}, u32[]{:S(2)}, u32[]{:S(2)}) collective-permute-start(bf16[128,640]{1,0:T(8,128)(2,1)S(1)} %get-tuple-element.101), channel_id=1, source_target_pairs={{0,2},{1,3},{2,0},{3,1},{4,6},{5,7},{6,4},{7,5},{8,10},{9,11},{10,... | collective-permute-start | bytes 491528 | tf_op jit(solution)/shard_map/ppermute | solution.py:686
  38.8 21.9 %collective-permute-start.17 = (bf16[128,640]{1,0:T(8,128)(2,1)S(1)}, bf16[128,640]{1,0:T(8,128)(2,1)S(1)}, u32[]{:S(2)}, u32[]{:S(2)}) collective-permute-start(bf16[128,640]{1,0:T(8,128)(2,1)S(1)} %get-tuple-element.102), channel_id=1, source_target_pairs={{0,3},{1,2},{2,1},{3,0},{4,7},{5,6},{6,5},{7,4},{8,11},{9,10},{10,... | collective-permute-start | bytes 491528 | tf_op jit(solution)/shard_map/ppermute | solution.py:686
  45.5 6.7 %collective-permute-start.9 = (bf16[272,256]{1,0:T(8,128)(2,1)S(1)}, bf16[272,256]{1,0:T(8,128)(2,1)S(1)}, u32[]{:S(2)}, u32[]{:S(2)}) collective-permute-start(bf16[272,256]{1,0:T(8,128)(2,1)S(1)} %get-tuple-element.84.refs_8_.refs_2_.refs_0_), channel_id=1, source_target_pairs={{0,8},{1,9},{2,10},{3,11},{4,12},{5,13},{6,14},{7,15},{8,16},{9,17... | collective-permute-start | bytes 417800 | tf_op jit(solution)/shard_map/ppermute | solution.py:686
  48.6 8.1 %collective-permute-start.10 = (bf16[272,256]{1,0:T(8,128)(2,1)S(1)}, bf16[272,256]{1,0:T(8,128)(2,1)S(1)}, u32[]{:S(2)}, u32[]{:S(2)}) collective-permute-start(bf16[272,256]{1,0:T(8,128)(2,1)S(1)} %get-tuple-element.85.refs_9_.refs_3_.refs_1_), channel_id=1, source_target_pairs={{0,8},{1,9},{2,10},{3,11},{4,12},{5,13},{6,14},{7,15},{8,16},{9,17... | collective-permute-start | bytes 417800 | tf_op jit(solution)/shard_map/ppermute | solution.py:686
  52.2 20.3 %collective-permute-start.12 = (bf16[128,896]{1,0:T(8,128)(2,1)S(1)}, bf16[128,896]{1,0:T(8,128)(2,1)S(1)}, u32[]{:S(2)}, u32[]{:S(2)}) collective-permute-start(bf16[128,896]{1,0:T(8,128)(2,1)S(1)} %get-tuple-element.94), channel_id=1, source_target_pairs={{0,1},{1,0},{2,3},{3,2},{4,5},{5,4},{6,7},{7,6},{8,9},{9,8},{10,11... | collective-permute-start | bytes 688136 | tf_op jit(solution)/shard_map/ppermute | solution.py:686
  56.6 15.8 %collective-permute-start.13 = (bf16[128,896]{1,0:T(8,128)(2,1)S(1)}, bf16[128,896]{1,0:T(8,128)(2,1)S(1)}, u32[]{:S(2)}, u32[]{:S(2)}) collective-permute-start(bf16[128,896]{1,0:T(8,128)(2,1)S(1)} %get-tuple-element.95), channel_id=1, source_target_pairs={{0,2},{1,3},{2,0},{3,1},{4,6},{5,7},{6,4},{7,5},{8,10},{9,11},{10,... | collective-permute-start | bytes 688136 | tf_op jit(solution)/shard_map/ppermute | solution.py:686
  57.2 20.2 %collective-permute-start.14 = (bf16[128,896]{1,0:T(8,128)(2,1)S(1)}, bf16[128,896]{1,0:T(8,128)(2,1)S(1)}, u32[]{:S(2)}, u32[]{:S(2)}) collective-permute-start(bf16[128,896]{1,0:T(8,128)(2,1)S(1)} %get-tuple-element.96), channel_id=1, source_target_pairs={{0,3},{1,2},{2,1},{3,0},{4,7},{5,6},{6,5},{7,4},{8,11},{9,10},{10,... | collective-permute-start | bytes 688136 | tf_op jit(solution)/shard_map/ppermute | solution.py:686
  63.1 7.4 %collective-permute-start.18 = (bf16[272,384]{1,0:T(8,128)(2,1)S(1)}, bf16[272,384]{1,0:T(8,128)(2,1)S(1)}, u32[]{:S(2)}, u32[]{:S(2)}) collective-permute-start(bf16[272,384]{1,0:T(8,128)(2,1)S(1)} %get-tuple-element.103.refs_0_.refs_1_), channel_id=1, source_target_pairs={{0,8},{1,9},{2,10},{3,11},{4,12},{5,13},{6,14},{7,15},{8,16},{9,17... | collective-permute-start | bytes 626696 | tf_op jit(solution)/shard_map/ppermute | solution.py:686
  65.0 7.3 %collective-permute-start.19 = (bf16[272,256]{1,0:T(8,128)(2,1)S(1)}, bf16[272,256]{1,0:T(8,128)(2,1)S(1)}, u32[]{:S(2)}, u32[]{:S(2)}) collective-permute-start(bf16[272,256]{1,0:T(8,128)(2,1)S(1)} %get-tuple-element.105.refs_1_), channel_id=1, source_target_pairs={{0,8},{1,9},{2,10},{3,11},{4,12},{5,13},{6,14},{7,15},{8,16},{9,17... | collective-permute-start | bytes 417800 | tf_op jit(solution)/shard_map/ppermute | solution.py:686
  70.6 16.7 %collective-permute-start.11 = (bf16[272,512]{1,0:T(8,128)(2,1)S(1)}, bf16[272,512]{1,0:T(8,128)(2,1)S(1)}, u32[]{:S(2)}, u32[]{:S(2)}) collective-permute-start(bf16[272,512]{1,0:T(8,128)(2,1)S(1)} %combine.5.refs_10_), channel_id=1, source_target_pairs={{0,16},{1,17},{2,18},{3,19},{4,20},{5,21},{6,22},{7,23},{8,24},{9,... | collective-permute-start | bytes 835592 | tf_op jit(solution)/shard_map/ppermute | solution.py:686
  79.4 12.5 %collective-permute-start.22 = (bf16[272,512]{1,0:T(8,128)(2,1)S(1)}, bf16[272,512]{1,0:T(8,128)(2,1)S(1)}, u32[]{:S(2)}, u32[]{:S(2)}) collective-permute-start(bf16[272,512]{1,0:T(8,128)(2,1)S(1)} %get-tuple-element.106.refs_10_.refs_1_), channel_id=1, source_target_pairs={{0,8},{1,9},{2,10},{3,11},{4,12},{5,13},{6,14},{7,15},{16,24},{17,... | collective-permute-start | bytes 835592 | tf_op jit(solution)/shard_map/ppermute | solution.py:686
  81.2 9.6 %collective-permute-start.20 = (bf16[272,384]{1,0:T(8,128)(2,1)S(1)}, bf16[272,384]{1,0:T(8,128)(2,1)S(1)}, u32[]{:S(2)}, u32[]{:S(2)}) collective-permute-start(bf16[272,384]{1,0:T(8,128)(2,1)S(1)} %combine.6.refs_2_.refs_10_), channel_id=1, source_target_pairs={{0,16},{1,17},{2,18},{3,19},{4,20},{5,21},{6,22},{7,23},{8,24},{9,... | collective-permute-start | bytes 626696 | tf_op jit(solution)/shard_map/ppermute | solution.py:686
  82.7 8.1 %collective-permute-start.21 = (bf16[272,256]{1,0:T(8,128)(2,1)S(1)}, bf16[272,256]{1,0:T(8,128)(2,1)S(1)}, u32[]{:S(2)}, u32[]{:S(2)}) collective-permute-start(bf16[272,256]{1,0:T(8,128)(2,1)S(1)} %combine.7.refs_11_), channel_id=1, source_target_pairs={{0,16},{1,17},{2,18},{3,19},{4,20},{5,21},{6,22},{7,23},{8,24},{9,... | collective-permute-start | bytes 417800 | tf_op jit(solution)/shard_map/ppermute | solution.py:686
  85.9 9.4 %collective-permute-start.25 = (bf16[272,384]{1,0:T(8,128)(2,1)S(1)}, bf16[272,384]{1,0:T(8,128)(2,1)S(1)}, u32[]{:S(2)}, u32[]{:S(2)}) collective-permute-start(bf16[272,384]{1,0:T(8,128)(2,1)S(1)} %get-tuple-element.107.refs_7_.refs_1_), channel_id=1, source_target_pairs={{0,8},{1,9},{2,10},{3,11},{4,12},{5,13},{6,14},{7,15},{16,24},{17,... | collective-permute-start | bytes 626696 | tf_op jit(solution)/shard_map/ppermute | solution.py:686
  92.0 10.1 %collective-permute-start.24 = (bf16[272,512]{1,0:T(8,128)(2,1)S(1)}, bf16[272,512]{1,0:T(8,128)(2,1)S(1)}, u32[]{:S(2)}, u32[]{:S(2)}) collective-permute-start(bf16[272,512]{1,0:T(8,128)(2,1)S(1)} %combine.8.refs_8_), channel_id=1, source_target_pairs={{8,16},{9,17},{10,18},{11,19},{12,20},{13,21},{14,22},{15,23}} | collective-permute-start | bytes 835592 | tf_op jit(solution)/shard_map/ppermute | solution.py:686
  93.3 13.2 %collective-permute-start.23 = (bf16[272,512]{1,0:T(8,128)(2,1)S(1)}, bf16[272,512]{1,0:T(8,128)(2,1)S(1)}, u32[]{:S(2)}, u32[]{:S(2)}) collective-permute-start(bf16[272,512]{1,0:T(8,128)(2,1)S(1)} %combine.8.refs_8_), channel_id=1, source_target_pairs={{8,24},{9,25},{10,26},{11,27},{12,28},{13,29},{14,30},{15,31}} | collective-permute-start | bytes 835592 | tf_op jit(solution)/shard_map/ppermute | solution.py:686
  95.4 12.3 %collective-permute-start.27 = (bf16[272,384]{1,0:T(8,128)(2,1)S(1)}, bf16[272,384]{1,0:T(8,128)(2,1)S(1)}, u32[]{:S(2)}, u32[]{:S(2)}) collective-permute-start(bf16[272,384]{1,0:T(8,128)(2,1)S(1)} %combine.9.refs_0_), channel_id=1, source_target_pairs={{8,16},{9,17},{10,18},{11,19},{12,20},{13,21},{14,22},{15,23}} | collective-permute-start | bytes 626696 | tf_op jit(solution)/shard_map/ppermute | solution.py:686
  96.7 11.0 %collective-permute-start.26 = (bf16[272,384]{1,0:T(8,128)(2,1)S(1)}, bf16[272,384]{1,0:T(8,128)(2,1)S(1)}, u32[]{:S(2)}, u32[]{:S(2)}) collective-permute-start(bf16[272,384]{1,0:T(8,128)(2,1)S(1)} %combine.9.refs_0_), channel_id=1, source_target_pairs={{8,24},{9,25},{10,26},{11,27},{12,28},{13,29},{14,30},{15,31}} | collective-permute-start | bytes 626696 | tf_op jit(solution)/shard_map/ppermute | solution.py:686
  97.4 12.5 %collective-permute-start.29 = (bf16[256,640]{1,0:T(8,128)(2,1)S(1)}, bf16[256,640]{1,0:T(8,128)(2,1)S(1)}, u32[]{:S(2)}, u32[]{:S(2)}) collective-permute-start(bf16[256,640]{1,0:T(8,128)(2,1)S(1)} %get-tuple-element.118), channel_id=1, source_target_pairs={{0,4},{1,5},{2,6},{3,7},{4,0},{5,1},{6,2},{7,3},{8,12},{9,13},{10,... | collective-permute-start | bytes 983048 | tf_op jit(solution)/shard_map/ppermute | solution.py:686
  102.1 7.7 %collective-permute-start.28 = (bf16[256,512]{1,0:T(8,128)(2,1)S(1)}, bf16[256,512]{1,0:T(8,128)(2,1)S(1)}, u32[]{:S(2)}, u32[]{:S(2)}) collective-permute-start(bf16[256,512]{1,0:T(8,128)(2,1)S(1)} %get-tuple-element.117), channel_id=1, source_target_pairs={{0,4},{1,5},{2,6},{3,7},{4,0},{5,1},{6,2},{7,3},{8,12},{9,13},{10,... | collective-permute-start | bytes 786440 | tf_op jit(solution)/shard_map/ppermute | solution.py:686
  107.6 3.3 %collective-permute-start.30 = (bf16[256,512]{1,0:T(8,128)(2,1)S(1)}, bf16[256,512]{1,0:T(8,128)(2,1)S(1)}, u32[]{:S(2)}, u32[]{:S(2)}) collective-permute-start(bf16[256,512]{1,0:T(8,128)(2,1)S(1)} %get-tuple-element.119), channel_id=1, source_target_pairs={{0,4},{1,5},{2,6},{3,7},{4,0},{5,1},{6,2},{7,3},{8,12},{9,13},{10,... | collective-permute-start | bytes 786440 | tf_op jit(solution)/shard_map/ppermute | solution.py:686
  108.8 2.2 %collective-permute-start.31 = (bf16[256,384]{1,0:T(8,128)(2,1)S(1)}, bf16[256,384]{1,0:T(8,128)(2,1)S(1)}, u32[]{:S(2)}, u32[]{:S(2)}) collective-permute-start(bf16[256,384]{1,0:T(8,128)(2,1)S(1)} %get-tuple-element.120), channel_id=1, source_target_pairs={{0,4},{1,5},{2,6},{3,7},{4,0},{5,1},{6,2},{7,3},{8,12},{9,13},{10,... | collective-permute-start | bytes 589832 | tf_op jit(solution)/shard_map/ppermute | solution.py:686
  (8 other events, 89.3 us)

commit v12 on v10

--- a/solution.py
+++ b/solution.py
@@ -637,6 +637,20 @@
         self.array = array
 
 
+def gate(blocks, order):
+    anywhere = pl.BlockSpec(memory_space=pl.ANY)
+    return pl.pallas_call(
+        lambda *refs: None,
+        out_shape=[jax.ShapeDtypeStruct(block.shape, block.dtype) for block in blocks],
+        in_specs=[anywhere] * (len(blocks) + len(order)),
+        out_specs=[anywhere] * len(blocks),
+        input_output_aliases={i: i for i in range(len(blocks))},
+        compiler_params=pltpu.CompilerParams(vmem_limit_bytes=16 << 20),
+        cost_estimate=pl.CostEstimate(flops=1, bytes_accessed=1, transcendentals=0),
+        name="gate",
+    )(*blocks, *order)
+
+
 def call(body, outs, operands, scratch=(), flops=0, transcendentals=0, name=None, limit=16 << 20):
     shapes = [jax.ShapeDtypeStruct(shape, dtype) for shape, dtype in outs]
     smem, vmem, hbm = (pl.BlockSpec(memory_space=m) for m in (pltpu.SMEM, pltpu.VMEM, pltpu.HBM))
@@ -731,8 +745,8 @@
     edges = over(edges, lambda i: i + peers if i % shards == shards - 1 else None)
     second_blocks = send_on(plan(1), [first_blocks[0]], None, edges)
     message.append(travel(second_blocks))
-    third_blocks = send_on(plan(2), [*message[0][1:], *message[1][2:]])
-    message.append(travel(third_blocks))
+    third_blocks = send_on(plan(2), [second_blocks[0]])
+    message.append(travel(third_blocks[:1] + gate(third_blocks[1:], message[0][1:] + message[1][1:])))
 
     def seen(piece):
         return message[piece]
@@ -801,9 +815,9 @@
 
     state_of(0, [])
     combine_of(0, [])
-    fourth_blocks = send_on(plan(3), [joined[0][0]])
+    fourth_blocks = send_on(plan(3), sent[0])
     message.append(travel(fourth_blocks))
-    state_of(1, [fourth_blocks[0]])
+    state_of(1, [fourth_blocks[0], joined[0][0]])
     combine_of(1, [])
     state_of(2, joined[1])
     state_of(3, sent[2])

time: 110 us -> 112 us (1.018)
  the two profiles are of different devices: /device:TPU:13 before, /device:TPU:19 now
where the time goes in v12:
time: 112 us; the launch traced here: 111 us
  starting transfers between devices  48.5 us (43%)
  waiting for transfers between devices  32 us (29%)
  Pallas kernels  28.3 us (25%)
  local copies, waits for them, and re-layouts  1.86 us (2%)
    ppermute x32, starting transfers between devices, over(): lax.ppermute(block, axes, [(i, j) for i, j in route if j is not None and...  48.5 us
    ppermute x32, waiting for transfers between devices, over(): lax.ppermute(block, axes, [(i, j) for i, j in route if j is not None and...  32 us
    pallas_call x24, Pallas kernels, call(): pl.pallas_call(body, out_shape=shapes, in_specs=specs, out_specs=[vmem] *...  26.4 us
  transfers between devices with their start and end apart: 32, of which 10 were waited for; matrix products, arithmetic and copies ran while one was open for 0% of the time, Pallas kernels for 22%

profile of v12, /device:TPU:19, one launch (start us, length us, event | category | flops | bytes accessed | tf_op | source)
XLA Modules:
  0.0 111.2 jit_solution(5327135211052576293)
XLA Ops:
  0.1 1.7 %copy-done = bf16[64,20480]{1,0:T(8,128)(2,1)S(1)} copy-done((bf16[64,20480]{1,0:T(8,128)(2,1)S(1)}, bf16[64,20480]{1,0:T(8,128)(2,1)}, u32[]{:S(2)}) %copy-start) | copy-done | bytes 2621464
  2.8 1.3 %pack.1 = (bf16[64,8448]{1,0:T(8,128)(2,1)S(1)}, bf16[16,10240]{1,0:T(8,128)(2,1)S(1)}) custom-call(s32[5]{0:T(128)S(1)} %stack.23.place, bf16[64,20480]{1,0:T(8,128)(2,1)S(1)} %copy-done, bf16[64,256]{1,0:T(8,128)(2,1)S(1)} %copy-done.2, bf16[64,4096]{1,0:T(8,128)(2,1)S(1)} %pack_first.1.order), custom_call_target="tpu_custom_call" | custom-call | flops 1 | bytes 1 | tf_op jit(solution)/shard_map/pack/pallas_call | solution.py:661
  5.0 3.0 %collective-permute-done.got_first.got.edges = bf16[64,4096]{1,0:T(8,128)(2,1)S(1)} collective-permute-done((bf16[64,4096]{1,0:T(8,128)(2,1)S(1)}, bf16[64,4096]{1,0:T(8,128)(2,1)S(1)}, u32[]{:S(2)}, u32[]{:S(2)}) %collective-permute-start) | collective-permute-done | bytes 524320 | tf_op jit(solution)/shard_map/ppermute | solution.py:686
  8.8 1.4 %collective-permute-start.1 = (bf16[128,512]{1,0:T(8,128)(2,1)S(1)}, bf16[128,512]{1,0:T(8,128)(2,1)S(1)}, u32[]{:S(2)}, u32[]{:S(2)}) collective-permute-start(bf16[128,512]{1,0:T(8,128)(2,1)S(1)} %get-tuple-element.62), channel_id=1, source_target_pairs={{0,1},{1,0},{2,3},{3,2},{4,5},{5,4},{6,7},{7,6},{8,9},{9,8},{10,11... | collective-permute-start | bytes 393224 | tf_op jit(solution)/shard_map/ppermute | solution.py:686
  10.9 3.7 %collective-permute-start.3 = (bf16[128,512]{1,0:T(8,128)(2,1)S(1)}, bf16[128,512]{1,0:T(8,128)(2,1)S(1)}, u32[]{:S(2)}, u32[]{:S(2)}) collective-permute-start(bf16[128,512]{1,0:T(8,128)(2,1)S(1)} %get-tuple-element.64), channel_id=1, source_target_pairs={{0,3},{1,2},{2,1},{3,0},{4,7},{5,6},{6,5},{7,4},{8,11},{9,10},{10,... | collective-permute-start | bytes 393224 | tf_op jit(solution)/shard_map/ppermute | solution.py:686
  17.0 1.5 %collective-permute-start.8 = (bf16[128,384]{1,0:T(8,128)(2,1)S(1)}, bf16[128,384]{1,0:T(8,128)(2,1)S(1)}, u32[]{:S(2)}, u32[]{:S(2)}) collective-permute-start(bf16[128,384]{1,0:T(8,128)(2,1)S(1)} %get-tuple-element.72), channel_id=1, source_target_pairs={{0,3},{1,2},{2,1},{3,0},{4,7},{5,6},{6,5},{7,4},{8,11},{9,10},{10,... | collective-permute-start | bytes 294920 | tf_op jit(solution)/shard_map/ppermute | solution.py:686
  19.3 10.6 %collective-permute-done.3.refs_3_.refs_5_ = bf16[128,512]{1,0:T(8,128)(2,1)S(1)} collective-permute-done((bf16[128,512]{1,0:T(8,128)(2,1)S(1)}, bf16[128,512]{1,0:T(8,128)(2,1)S(1)}, u32[]{:S(2)}, u32[]{:S(2)}) %collective-permute-start.3) | collective-permute-done | bytes 131104 | tf_op jit(solution)/shard_map/ppermute | solution.py:686
  29.9 4.2 %collective-permute-done.8.refs_3_.refs_8_ = bf16[128,384]{1,0:T(8,128)(2,1)S(1)} collective-permute-done((bf16[128,384]{1,0:T(8,128)(2,1)S(1)}, bf16[128,384]{1,0:T(8,128)(2,1)S(1)}, u32[]{:S(2)}, u32[]{:S(2)}) %collective-permute-start.8) | collective-permute-done | bytes 98336 | tf_op jit(solution)/shard_map/ppermute | solution.py:686
  34.5 2.2 %collective-permute-start.17 = (bf16[128,768]{1,0:T(8,128)(2,1)S(1)}, bf16[128,768]{1,0:T(8,128)(2,1)S(1)}, u32[]{:S(2)}, u32[]{:S(2)}) collective-permute-start(bf16[128,768]{1,0:T(8,128)(2,1)S(1)} %get-tuple-element.90), channel_id=1, source_target_pairs={{0,3},{1,2},{2,1},{3,0},{4,7},{5,6},{6,5},{7,4},{8,11},{9,10},{10,... | collective-permute-start | bytes 589832 | tf_op jit(solution)/shard_map/ppermute | solution.py:686
  37.5 1.7 %prep.1 = (bf16[512,256]{1,0:T(8,128)(2,1)S(1)}, f32[4,2560]{1,0:T(4,128)S(1)}, f32[512,128]{1,0:T(8,128)S(1)}, f32[128,512]{1,0:T(8,128)S(1)}, bf16[512,256]{1,...) custom-call(s32[5]{0:T(128)S(1)} %stack.23.place, ...), custom_call_target="tpu_custom_call" | custom-call | flops 1 | bytes 1 | tf_op jit(solution)/shard_map/prep/pallas_call | solution.py:661
  39.2 2.1 %state.4 = (bf16[512,512]{1,0:T(8,128)(2,1)S(1)}, f32[256,512]{1,0:T(8,128)S(1)}, bf16[272,256]{1,0:T(8,128)(2,1)S(1)}, bf16[272,256]{1,0:T(8,128)(2,1)S(1)}) custom-call(s32[5]{0:T(128)S(1)} %stack.23.place, bf16[128,512]{1,0:T(8,128)(2,1)S(1)} %get-tuple-element.61.refs_0_, bf16[128,512]{1,0:T(8,128)(2,1)S(1)} %collective-permute-done.1.refs_1_.refs_3_, ...), custom_call_target="tpu_custom_call" | custom-call | flops 1 | bytes 1 | tf_op jit(solution)/shard_map/state/pallas_call | solution.py:661
  41.2 3.1 %collective-permute-start.10 = (bf16[272,256]{1,0:T(8,128)(2,1)S(1)}, bf16[272,256]{1,0:T(8,128)(2,1)S(1)}, u32[]{:S(2)}, u32[]{:S(2)}) collective-permute-start(bf16[272,256]{1,0:T(8,128)(2,1)S(1)} %get-tuple-element.79.refs_3_.refs_1_), channel_id=1, source_target_pairs={{0,8},{1,9},{2,10},{3,11},{4,12},{5,13},{6,14},{7,15},{8,16},{9,17... | collective-permute-start | bytes 417800 | tf_op jit(solution)/shard_map/ppermute | solution.py:686
  44.3 2.3 %collective-permute-start.9 = (bf16[272,256]{1,0:T(8,128)(2,1)S(1)}, bf16[272,256]{1,0:T(8,128)(2,1)S(1)}, u32[]{:S(2)}, u32[]{:S(2)}) collective-permute-start(bf16[272,256]{1,0:T(8,128)(2,1)S(1)} %get-tuple-element.78.refs_2_.refs_0_), channel_id=1, source_target_pairs={{0,8},{1,9},{2,10},{3,11},{4,12},{5,13},{6,14},{7,15},{8,16},{9,17... | collective-permute-start | bytes 417800 | tf_op jit(solution)/shard_map/ppermute | solution.py:686
  48.6 1.7 %collective-permute-done.9.refs_0_ = bf16[272,256]{1,0:T(8,128)(2,1)S(1)} collective-permute-done((bf16[272,256]{1,0:T(8,128)(2,1)S(1)}, bf16[272,256]{1,0:T(8,128)(2,1)S(1)}, u32[]{:S(2)}, u32[]{:S(2)}) %collective-permute-start.9) | collective-permute-done | bytes 139296 | tf_op jit(solution)/shard_map/ppermute | solution.py:686
  53.7 2.6 %state.5 = (bf16[512,768]{1,0:T(8,128)(2,1)S(1)}, f32[256,768]{1,0:T(8,128)S(1)}, bf16[272,384]{1,0:T(8,128)(2,1)S(1)}, bf16[272,384]{1,0:T(8,128)(2,1)S(1)}) custom-call(s32[5]{0:T(128)S(1)} %stack.23.place, bf16[128,768]{1,0:T(8,128)(2,1)S(1)} %get-tuple-element.73.refs_9_.refs_0_, bf16[128,768]{1,0:T(8,128)(2,1)S(1)} %collective-permute-done.15.refs_1_, ...), custom_call_target="tpu_custom_call" | custom-call | flops 1 | bytes 1 | tf_op jit(solution)/shard_map/state/pallas_call | solution.py:661
  56.3 3.1 %collective-permute-start.18 = (bf16[272,384]{1,0:T(8,128)(2,1)S(1)}, bf16[272,384]{1,0:T(8,128)(2,1)S(1)}, u32[]{:S(2)}, u32[]{:S(2)}) collective-permute-start(bf16[272,384]{1,0:T(8,128)(2,1)S(1)} %get-tuple-element.91.refs_1_), channel_id=1, source_target_pairs={{0,8},{1,9},{2,10},{3,11},{4,12},{5,13},{6,14},{7,15},{8,16},{9,17... | collective-permute-start | bytes 626696 | tf_op jit(solution)/shard_map/ppermute | solution.py:686
  59.5 2.4 %collective-permute-start.19 = (bf16[272,384]{1,0:T(8,128)(2,1)S(1)}, bf16[272,384]{1,0:T(8,128)(2,1)S(1)}, u32[]{:S(2)}, u32[]{:S(2)}) collective-permute-start(bf16[272,384]{1,0:T(8,128)(2,1)S(1)} %get-tuple-element.92.refs_1_), channel_id=1, source_target_pairs={{0,8},{1,9},{2,10},{3,11},{4,12},{5,13},{6,14},{7,15},{8,16},{9,17... | collective-permute-start | bytes 626696 | tf_op jit(solution)/shard_map/ppermute | solution.py:686
  61.8 1.3 %collective-permute-done.18.refs_0_ = bf16[272,384]{1,0:T(8,128)(2,1)S(1)} collective-permute-done((bf16[272,384]{1,0:T(8,128)(2,1)S(1)}, bf16[272,384]{1,0:T(8,128)(2,1)S(1)}, u32[]{:S(2)}, u32[]{:S(2)}) %collective-permute-start.18) | collective-permute-done | bytes 208928 | tf_op jit(solution)/shard_map/ppermute | solution.py:686
  63.2 2.4 %collective-permute-start.20 = (bf16[272,384]{1,0:T(8,128)(2,1)S(1)}, bf16[272,384]{1,0:T(8,128)(2,1)S(1)}, u32[]{:S(2)}, u32[]{:S(2)}) collective-permute-start(bf16[272,384]{1,0:T(8,128)(2,1)S(1)} %combine.6.refs_2_.refs_10_), channel_id=1, source_target_pairs={{0,16},{1,17},{2,18},{3,19},{4,20},{5,21},{6,22},{7,23},{8,24},{9,... | collective-permute-start | bytes 626696 | tf_op jit(solution)/shard_map/ppermute | solution.py:686
  66.4 1.9 %collective-permute-start.21 = (bf16[272,384]{1,0:T(8,128)(2,1)S(1)}, bf16[272,384]{1,0:T(8,128)(2,1)S(1)}, u32[]{:S(2)}, u32[]{:S(2)}) collective-permute-start(bf16[272,384]{1,0:T(8,128)(2,1)S(1)} %combine.7.refs_11_), channel_id=1, source_target_pairs={{0,16},{1,17},{2,18},{3,19},{4,20},{5,21},{6,22},{7,23},{8,24},{9,... | collective-permute-start | bytes 626696 | tf_op jit(solution)/shard_map/ppermute | solution.py:686
  68.3 8.0 %collective-permute-done.14.refs_3_ = bf16[128,1024]{1,0:T(8,128)(2,1)S(1)} collective-permute-done((bf16[128,1024]{1,0:T(8,128)(2,1)S(1)}, bf16[128,1024]{1,0:T(8,128)(2,1)S(1)}, u32[]{:S(2)}, u32[]{:S(2)}) %collective-permute-start.14) | collective-permute-done | bytes 262176 | tf_op jit(solution)/shard_map/ppermute | solution.py:686
  76.3 1.9 %state.6 = (bf16[512,384]{1,0:T(8,128)(2,1)S(1)}, f32[256,384]{1,0:T(8,128)S(1)}, bf16[272,384]{1,0:T(8,128)(2,1)S(1)}) custom-call(s32[5]{0:T(128)S(1)} %stack.23.place, bf16[128,1024]{1,0:T(8,128)(2,1)S(1)} %get-tuple-element.81.refs_10_.refs_0_, bf16[128,1024]{1,0:T(8,128)(2,1)S(1)} %collective-permute-done.12.refs_1_, ...), custom_call_target="tpu_custom_call" | custom-call | flops 1 | bytes 1 | tf_op jit(solution)/shard_map/state/pallas_call | solution.py:661
  79.5 2.7 %collective-permute-start.11 = (bf16[272,512]{1,0:T(8,128)(2,1)S(1)}, bf16[272,512]{1,0:T(8,128)(2,1)S(1)}, u32[]{:S(2)}, u32[]{:S(2)}) collective-permute-start(bf16[272,512]{1,0:T(8,128)(2,1)S(1)} %combine.5.refs_11_), channel_id=1, source_target_pairs={{0,16},{1,17},{2,18},{3,19},{4,20},{5,21},{6,22},{7,23},{8,24},{9,... | collective-permute-start | bytes 835592 | tf_op jit(solution)/shard_map/ppermute | solution.py:686
  82.2 1.9 %state.7 = (bf16[512,384]{1,0:T(8,128)(2,1)S(1)}, f32[256,384]{1,0:T(8,128)S(1)}, bf16[272,384]{1,0:T(8,128)(2,1)S(1)}) custom-call(s32[5]{0:T(128)S(1)} %stack.23.place, bf16[128,1024]{1,0:T(8,128)(2,1)S(1)} %get-tuple-element.81.refs_10_.refs_0_, bf16[128,1024]{1,0:T(8,128)(2,1)S(1)} %collective-permute-done.12.refs_1_, ...), custom_call_target="tpu_custom_call" | custom-call | flops 1 | bytes 1 | tf_op jit(solution)/shard_map/state/pallas_call | solution.py:661
  86.6 1.3 %collective-permute-start.24 = (bf16[272,384]{1,0:T(8,128)(2,1)S(1)}, bf16[272,384]{1,0:T(8,128)(2,1)S(1)}, u32[]{:S(2)}, u32[]{:S(2)}) collective-permute-start(bf16[272,384]{1,0:T(8,128)(2,1)S(1)} %combine.8.refs_12_), channel_id=1, source_target_pairs={{8,24},{9,25},{10,26},{11,27},{12,28},{13,29},{14,30},{15,31}} | collective-permute-start | bytes 626696 | tf_op jit(solution)/shard_map/ppermute | solution.py:686
  88.0 2.7 %collective-permute-start.25 = (bf16[272,384]{1,0:T(8,128)(2,1)S(1)}, bf16[272,384]{1,0:T(8,128)(2,1)S(1)}, u32[]{:S(2)}, u32[]{:S(2)}) collective-permute-start(bf16[272,384]{1,0:T(8,128)(2,1)S(1)} %combine.8.refs_12_), channel_id=1, source_target_pairs={{8,16},{9,17},{10,18},{11,19},{12,20},{13,21},{14,22},{15,23}} | collective-permute-start | bytes 626696 | tf_op jit(solution)/shard_map/ppermute | solution.py:686
  90.6 2.6 %final.4 = (bf16[256,768]{1,0:T(8,128)(2,1)S(1)}, bf16[256,768]{1,0:T(8,128)(2,1)S(1)}) custom-call(s32[5]{0:T(128)S(1)} %stack.23.place, bf16[272,384]{1,0:T(8,128)(2,1)S(1)} %collective-permute-done.18.refs_0_, bf16[272,384]{1,0:T(8,128)(2,1)S(1)} %collective-permute-done.19.refs_0_.refs_1_, bf16[272,384]{1,0:T(8,128)(2,1)S(1)} %collective-permute-done.20.refs_9_.refs_2_, ...), custom_call_target="tpu_custom_call" | custom-call | flops 1 | bytes 1 | tf_op jit(solution)/shard_map/final/pallas_call | solution.py:661
  93.3 1.3 %collective-permute-start.26 = (bf16[272,384]{1,0:T(8,128)(2,1)S(1)}, bf16[272,384]{1,0:T(8,128)(2,1)S(1)}, u32[]{:S(2)}, u32[]{:S(2)}) collective-permute-start(bf16[272,384]{1,0:T(8,128)(2,1)S(1)} %combine.9.refs_0_), channel_id=1, source_target_pairs={{8,24},{9,25},{10,26},{11,27},{12,28},{13,29},{14,30},{15,31}} | collective-permute-start | bytes 626696 | tf_op jit(solution)/shard_map/ppermute | solution.py:686
  94.6 1.3 %collective-permute-start.27 = (bf16[272,384]{1,0:T(8,128)(2,1)S(1)}, bf16[272,384]{1,0:T(8,128)(2,1)S(1)}, u32[]{:S(2)}, u32[]{:S(2)}) collective-permute-start(bf16[272,384]{1,0:T(8,128)(2,1)S(1)} %combine.9.refs_0_), channel_id=1, source_target_pairs={{8,16},{9,17},{10,18},{11,19},{12,20},{13,21},{14,22},{15,23}} | collective-permute-start | bytes 626696 | tf_op jit(solution)/shard_map/ppermute | solution.py:686
  95.9 5.5 %collective-permute-start.29 = (bf16[256,768]{1,0:T(8,128)(2,1)S(1)}, bf16[256,768]{1,0:T(8,128)(2,1)S(1)}, u32[]{:S(2)}, u32[]{:S(2)}) collective-permute-start(bf16[256,768]{1,0:T(8,128)(2,1)S(1)} %get-tuple-element.112), channel_id=1, source_target_pairs={{0,4},{1,5},{2,6},{3,7},{4,0},{5,1},{6,2},{7,3},{8,12},{9,13},{10,... | collective-permute-start | bytes 1179656 | tf_op jit(solution)/shard_map/ppermute | solution.py:686
  102.9 1.9 %final.5 = (bf16[256,512]{1,0:T(8,128)(2,1)S(1)}, bf16[256,512]{1,0:T(8,128)(2,1)S(1)}) custom-call(s32[5]{0:T(128)S(1)} %stack.23.place, bf16[272,256]{1,0:T(8,128)(2,1)S(1)} %collective-permute-done.9.refs_0_, bf16[272,256]{1,0:T(8,128)(2,1)S(1)} %collective-permute-done.10.refs_1_, bf16[272,512]{1,0:T(8,128)(2,1)S(1)} %collective-permute-done.11.refs_2_, ...), custom_call_target="tpu_custom_call" | custom-call | flops 1 | bytes 1 | tf_op jit(solution)/shard_map/final/pallas_call | solution.py:661
  109.1 1.9 %place.1 = bf16[256,4096]{1,0:T(8,128)(2,1)} custom-call(s32[5]{0:T(128)S(1)} %stack.23.place, bf16[256,512]{1,0:T(8,128)(2,1)S(1)} %get-tuple-element.106.refs_7_.refs_0_, bf16[256,768]{1,0:T(8,128)(2,1)S(1)} %get-tuple-element.105.refs_2_.refs_1_, bf16[256,384]{1,0:T(8,128)(2,1)S(1)} %get-tuple-element.108.refs_7_.refs_2_, ...), custom_call_target="tpu_custom_call" | custom-call | flops 1 | bytes 1 | tf_op jit(solution)/shard_map/place/pallas_call | solution.py:623
  (75 shorter events, 23.5 us)
Async XLA Ops:
  4.1 10.5 %collective-permute-start.4 = (bf16[64,8448]{1,0:T(8,128)(2,1)S(1)}, bf16[64,8448]{1,0:T(8,128)(2,1)S(1)}, u32[]{:S(2)}, u32[]{:S(2)}) collective-permute-start(bf16[64,8448]{1,0:T(8,128)(2,1)S(1)} %get-tuple-element.65), channel_id=1, source_target_pairs={{0,4},{1,5},{2,6},{3,7},{4,0},{5,1},{6,2},{7,3},{8,12},{9,13},{10,... | collective-permute-start | bytes 3244040 | tf_op jit(solution)/shard_map/ppermute | solution.py:686
  4.9 3.1 %collective-permute-start = (bf16[64,4096]{1,0:T(8,128)(2,1)S(1)}, bf16[64,4096]{1,0:T(8,128)(2,1)S(1)}, u32[]{:S(2)}, u32[]{:S(2)}) collective-permute-start(bf16[64,4096]{1,0:T(8,128)(2,1)S(1)} %pack_first.1.order), channel_id=1, source_target_pairs={{0,4},{1,5},{2,6},{3,7},{4,0},{5,1},{6,2},{7,3},{8,12},{9,13},{10,... | collective-permute-start | bytes 1572872 | tf_op jit(solution)/shard_map/ppermute | solution.py:686
  8.8 8.2 %collective-permute-start.1 = (bf16[128,512]{1,0:T(8,128)(2,1)S(1)}, bf16[128,512]{1,0:T(8,128)(2,1)S(1)}, u32[]{:S(2)}, u32[]{:S(2)}) collective-permute-start(bf16[128,512]{1,0:T(8,128)(2,1)S(1)} %get-tuple-element.62), channel_id=1, source_target_pairs={{0,1},{1,0},{2,3},{3,2},{4,5},{5,4},{6,7},{7,6},{8,9},{9,8},{10,11... | collective-permute-start | bytes 393224 | tf_op jit(solution)/shard_map/ppermute | solution.py:686
  10.1 4.5 %collective-permute-start.5 = (bf16[3,10240]{1,0:T(4,128)(2,1)S(1)}, bf16[3,10240]{1,0:T(4,128)(2,1)S(1)}, u32[]{:S(2)}, u32[]{:S(2)}) collective-permute-start(bf16[3,10240]{1,0:T(4,128)(2,1)S(1)} %get-tuple-element.68), channel_id=1, source_target_pairs={{3,11},{7,15},{11,19},{15,23},{19,27},{23,31}} | collective-permute-start | bytes 184328 | tf_op jit(solution)/shard_map/ppermute | solution.py:686
  10.8 8.5 %collective-permute-start.2 = (bf16[128,512]{1,0:T(8,128)(2,1)S(1)}, bf16[128,512]{1,0:T(8,128)(2,1)S(1)}, u32[]{:S(2)}, u32[]{:S(2)}) collective-permute-start(bf16[128,512]{1,0:T(8,128)(2,1)S(1)} %get-tuple-element.63), channel_id=1, source_target_pairs={{0,2},{1,3},{2,0},{3,1},{4,6},{5,7},{6,4},{7,5},{8,10},{9,11},{10,... | collective-permute-start | bytes 393224 | tf_op jit(solution)/shard_map/ppermute | solution.py:686
  10.9 18.9 %collective-permute-start.3 = (bf16[128,512]{1,0:T(8,128)(2,1)S(1)}, bf16[128,512]{1,0:T(8,128)(2,1)S(1)}, u32[]{:S(2)}, u32[]{:S(2)}) collective-permute-start(bf16[128,512]{1,0:T(8,128)(2,1)S(1)} %get-tuple-element.64), channel_id=1, source_target_pairs={{0,3},{1,2},{2,1},{3,0},{4,7},{5,6},{6,5},{7,4},{8,11},{9,10},{10,... | collective-permute-start | bytes 393224 | tf_op jit(solution)/shard_map/ppermute | solution.py:686
  15.7 14.2 %collective-permute-start.6 = (bf16[128,384]{1,0:T(8,128)(2,1)S(1)}, bf16[128,384]{1,0:T(8,128)(2,1)S(1)}, u32[]{:S(2)}, u32[]{:S(2)}) collective-permute-start(bf16[128,384]{1,0:T(8,128)(2,1)S(1)} %get-tuple-element.70), channel_id=1, source_target_pairs={{0,1},{1,0},{2,3},{3,2},{4,5},{5,4},{6,7},{7,6},{8,9},{9,8},{10,11... | collective-permute-start | bytes 294920 | tf_op jit(solution)/shard_map/ppermute | solution.py:686
  16.8 13.1 %collective-permute-start.7 = (bf16[128,384]{1,0:T(8,128)(2,1)S(1)}, bf16[128,384]{1,0:T(8,128)(2,1)S(1)}, u32[]{:S(2)}, u32[]{:S(2)}) collective-permute-start(bf16[128,384]{1,0:T(8,128)(2,1)S(1)} %get-tuple-element.71), channel_id=1, source_target_pairs={{0,2},{1,3},{2,0},{3,1},{4,6},{5,7},{6,4},{7,5},{8,10},{9,11},{10,... | collective-permute-start | bytes 294920 | tf_op jit(solution)/shard_map/ppermute | solution.py:686
  17.0 17.1 %collective-permute-start.8 = (bf16[128,384]{1,0:T(8,128)(2,1)S(1)}, bf16[128,384]{1,0:T(8,128)(2,1)S(1)}, u32[]{:S(2)}, u32[]{:S(2)}) collective-permute-start(bf16[128,384]{1,0:T(8,128)(2,1)S(1)} %get-tuple-element.72), channel_id=1, source_target_pairs={{0,3},{1,2},{2,1},{3,0},{4,7},{5,6},{6,5},{7,4},{8,11},{9,10},{10,... | collective-permute-start | bytes 294920 | tf_op jit(solution)/shard_map/ppermute | solution.py:686
  34.1 17.3 %collective-permute-start.15 = (bf16[128,768]{1,0:T(8,128)(2,1)S(1)}, bf16[128,768]{1,0:T(8,128)(2,1)S(1)}, u32[]{:S(2)}, u32[]{:S(2)}) collective-permute-start(bf16[128,768]{1,0:T(8,128)(2,1)S(1)} %get-tuple-element.88), channel_id=1, source_target_pairs={{0,1},{1,0},{2,3},{3,2},{4,5},{5,4},{6,7},{7,6},{8,9},{9,8},{10,11... | collective-permute-start | bytes 589832 | tf_op jit(solution)/shard_map/ppermute | solution.py:686
  34.1 18.6 %collective-permute-start.16 = (bf16[128,768]{1,0:T(8,128)(2,1)S(1)}, bf16[128,768]{1,0:T(8,128)(2,1)S(1)}, u32[]{:S(2)}, u32[]{:S(2)}) collective-permute-start(bf16[128,768]{1,0:T(8,128)(2,1)S(1)} %get-tuple-element.89), channel_id=1, source_target_pairs={{0,2},{1,3},{2,0},{3,1},{4,6},{5,7},{6,4},{7,5},{8,10},{9,11},{10,... | collective-permute-start | bytes 589832 | tf_op jit(solution)/shard_map/ppermute | solution.py:686
  34.5 19.2 %collective-permute-start.17 = (bf16[128,768]{1,0:T(8,128)(2,1)S(1)}, bf16[128,768]{1,0:T(8,128)(2,1)S(1)}, u32[]{:S(2)}, u32[]{:S(2)}) collective-permute-start(bf16[128,768]{1,0:T(8,128)(2,1)S(1)} %get-tuple-element.90), channel_id=1, source_target_pairs={{0,3},{1,2},{2,1},{3,0},{4,7},{5,6},{6,5},{7,4},{8,11},{9,10},{10,... | collective-permute-start | bytes 589832 | tf_op jit(solution)/shard_map/ppermute | solution.py:686
  41.2 6.4 %collective-permute-start.10 = (bf16[272,256]{1,0:T(8,128)(2,1)S(1)}, bf16[272,256]{1,0:T(8,128)(2,1)S(1)}, u32[]{:S(2)}, u32[]{:S(2)}) collective-permute-start(bf16[272,256]{1,0:T(8,128)(2,1)S(1)} %get-tuple-element.79.refs_3_.refs_1_), channel_id=1, source_target_pairs={{0,8},{1,9},{2,10},{3,11},{4,12},{5,13},{6,14},{7,15},{8,16},{9,17... | collective-permute-start | bytes 417800 | tf_op jit(solution)/shard_map/ppermute | solution.py:686
  44.3 6.0 %collective-permute-start.9 = (bf16[272,256]{1,0:T(8,128)(2,1)S(1)}, bf16[272,256]{1,0:T(8,128)(2,1)S(1)}, u32[]{:S(2)}, u32[]{:S(2)}) collective-permute-start(bf16[272,256]{1,0:T(8,128)(2,1)S(1)} %get-tuple-element.78.refs_2_.refs_0_), channel_id=1, source_target_pairs={{0,8},{1,9},{2,10},{3,11},{4,12},{5,13},{6,14},{7,15},{8,16},{9,17... | collective-permute-start | bytes 417800 | tf_op jit(solution)/shard_map/ppermute | solution.py:686
  47.6 20.6 %collective-permute-start.12 = (bf16[128,1024]{1,0:T(8,128)(2,1)S(1)}, bf16[128,1024]{1,0:T(8,128)(2,1)S(1)}, u32[]{:S(2)}, u32[]{:S(2)}) collective-permute-start(bf16[128,1024]{1,0:T(8,128)(2,1)S(1)} %get-tuple-element.82), channel_id=1, source_target_pairs={{0,1},{1,0},{2,3},{3,2},{4,5},{5,4},{6,7},{7,6},{8,9},{9,8},{10,11... | collective-permute-start | bytes 786440 | tf_op jit(solution)/shard_map/ppermute | solution.py:686
  50.3 18.0 %collective-permute-start.13 = (bf16[128,1024]{1,0:T(8,128)(2,1)S(1)}, bf16[128,1024]{1,0:T(8,128)(2,1)S(1)}, u32[]{:S(2)}, u32[]{:S(2)}) collective-permute-start(bf16[128,1024]{1,0:T(8,128)(2,1)S(1)} %get-tuple-element.83), channel_id=1, source_target_pairs={{0,2},{1,3},{2,0},{3,1},{4,6},{5,7},{6,4},{7,5},{8,10},{9,11},{10,... | collective-permute-start | bytes 786440 | tf_op jit(solution)/shard_map/ppermute | solution.py:686
  51.3 25.0 %collective-permute-start.14 = (bf16[128,1024]{1,0:T(8,128)(2,1)S(1)}, bf16[128,1024]{1,0:T(8,128)(2,1)S(1)}, u32[]{:S(2)}, u32[]{:S(2)}) collective-permute-start(bf16[128,1024]{1,0:T(8,128)(2,1)S(1)} %get-tuple-element.84), channel_id=1, source_target_pairs={{0,3},{1,2},{2,1},{3,0},{4,7},{5,6},{6,5},{7,4},{8,11},{9,10},{10,... | collective-permute-start | bytes 786440 | tf_op jit(solution)/shard_map/ppermute | solution.py:686
  56.3 6.8 %collective-permute-start.18 = (bf16[272,384]{1,0:T(8,128)(2,1)S(1)}, bf16[272,384]{1,0:T(8,128)(2,1)S(1)}, u32[]{:S(2)}, u32[]{:S(2)}) collective-permute-start(bf16[272,384]{1,0:T(8,128)(2,1)S(1)} %get-tuple-element.91.refs_1_), channel_id=1, source_target_pairs={{0,8},{1,9},{2,10},{3,11},{4,12},{5,13},{6,14},{7,15},{8,16},{9,17... | collective-permute-start | bytes 626696 | tf_op jit(solution)/shard_map/ppermute | solution.py:686
  59.5 6.8 %collective-permute-start.19 = (bf16[272,384]{1,0:T(8,128)(2,1)S(1)}, bf16[272,384]{1,0:T(8,128)(2,1)S(1)}, u32[]{:S(2)}, u32[]{:S(2)}) collective-permute-start(bf16[272,384]{1,0:T(8,128)(2,1)S(1)} %get-tuple-element.92.refs_1_), channel_id=1, source_target_pairs={{0,8},{1,9},{2,10},{3,11},{4,12},{5,13},{6,14},{7,15},{8,16},{9,17... | collective-permute-start | bytes 626696 | tf_op jit(solution)/shard_map/ppermute | solution.py:686
  63.2 22.2 %collective-permute-start.20 = (bf16[272,384]{1,0:T(8,128)(2,1)S(1)}, bf16[272,384]{1,0:T(8,128)(2,1)S(1)}, u32[]{:S(2)}, u32[]{:S(2)}) collective-permute-start(bf16[272,384]{1,0:T(8,128)(2,1)S(1)} %combine.6.refs_2_.refs_10_), channel_id=1, source_target_pairs={{0,16},{1,17},{2,18},{3,19},{4,20},{5,21},{6,22},{7,23},{8,24},{9,... | collective-permute-start | bytes 626696 | tf_op jit(solution)/shard_map/ppermute | solution.py:686
  66.4 19.0 %collective-permute-start.21 = (bf16[272,384]{1,0:T(8,128)(2,1)S(1)}, bf16[272,384]{1,0:T(8,128)(2,1)S(1)}, u32[]{:S(2)}, u32[]{:S(2)}) collective-permute-start(bf16[272,384]{1,0:T(8,128)(2,1)S(1)} %combine.7.refs_11_), channel_id=1, source_target_pairs={{0,16},{1,17},{2,18},{3,19},{4,20},{5,21},{6,22},{7,23},{8,24},{9,... | collective-permute-start | bytes 626696 | tf_op jit(solution)/shard_map/ppermute | solution.py:686
  78.2 8.4 %collective-permute-start.23 = (bf16[272,384]{1,0:T(8,128)(2,1)S(1)}, bf16[272,384]{1,0:T(8,128)(2,1)S(1)}, u32[]{:S(2)}, u32[]{:S(2)}) collective-permute-start(bf16[272,384]{1,0:T(8,128)(2,1)S(1)} %get-tuple-element.93.refs_10_.refs_1_), channel_id=1, source_target_pairs={{0,8},{1,9},{2,10},{3,11},{4,12},{5,13},{6,14},{7,15},{16,24},{17,... | collective-permute-start | bytes 626696 | tf_op jit(solution)/shard_map/ppermute | solution.py:686
  79.5 16.4 %collective-permute-start.11 = (bf16[272,512]{1,0:T(8,128)(2,1)S(1)}, bf16[272,512]{1,0:T(8,128)(2,1)S(1)}, u32[]{:S(2)}, u32[]{:S(2)}) collective-permute-start(bf16[272,512]{1,0:T(8,128)(2,1)S(1)} %combine.5.refs_11_), channel_id=1, source_target_pairs={{0,16},{1,17},{2,18},{3,19},{4,20},{5,21},{6,22},{7,23},{8,24},{9,... | collective-permute-start | bytes 835592 | tf_op jit(solution)/shard_map/ppermute | solution.py:686
  84.1 9.1 %collective-permute-start.22 = (bf16[272,384]{1,0:T(8,128)(2,1)S(1)}, bf16[272,384]{1,0:T(8,128)(2,1)S(1)}, u32[]{:S(2)}, u32[]{:S(2)}) collective-permute-start(bf16[272,384]{1,0:T(8,128)(2,1)S(1)} %get-tuple-element.94.refs_8_.refs_1_), channel_id=1, source_target_pairs={{0,8},{1,9},{2,10},{3,11},{4,12},{5,13},{6,14},{7,15},{16,24},{17,... | collective-permute-start | bytes 626696 | tf_op jit(solution)/shard_map/ppermute | solution.py:686
  86.6 18.2 %collective-permute-start.24 = (bf16[272,384]{1,0:T(8,128)(2,1)S(1)}, bf16[272,384]{1,0:T(8,128)(2,1)S(1)}, u32[]{:S(2)}, u32[]{:S(2)}) collective-permute-start(bf16[272,384]{1,0:T(8,128)(2,1)S(1)} %combine.8.refs_12_), channel_id=1, source_target_pairs={{8,24},{9,25},{10,26},{11,27},{12,28},{13,29},{14,30},{15,31}} | collective-permute-start | bytes 626696 | tf_op jit(solution)/shard_map/ppermute | solution.py:686
  88.0 17.0 %collective-permute-start.25 = (bf16[272,384]{1,0:T(8,128)(2,1)S(1)}, bf16[272,384]{1,0:T(8,128)(2,1)S(1)}, u32[]{:S(2)}, u32[]{:S(2)}) collective-permute-start(bf16[272,384]{1,0:T(8,128)(2,1)S(1)} %combine.8.refs_12_), channel_id=1, source_target_pairs={{8,16},{9,17},{10,18},{11,19},{12,20},{13,21},{14,22},{15,23}} | collective-permute-start | bytes 626696 | tf_op jit(solution)/shard_map/ppermute | solution.py:686
  93.3 12.7 %collective-permute-start.26 = (bf16[272,384]{1,0:T(8,128)(2,1)S(1)}, bf16[272,384]{1,0:T(8,128)(2,1)S(1)}, u32[]{:S(2)}, u32[]{:S(2)}) collective-permute-start(bf16[272,384]{1,0:T(8,128)(2,1)S(1)} %combine.9.refs_0_), channel_id=1, source_target_pairs={{8,24},{9,25},{10,26},{11,27},{12,28},{13,29},{14,30},{15,31}} | collective-permute-start | bytes 626696 | tf_op jit(solution)/shard_map/ppermute | solution.py:686
  94.6 11.4 %collective-permute-start.27 = (bf16[272,384]{1,0:T(8,128)(2,1)S(1)}, bf16[272,384]{1,0:T(8,128)(2,1)S(1)}, u32[]{:S(2)}, u32[]{:S(2)}) collective-permute-start(bf16[272,384]{1,0:T(8,128)(2,1)S(1)} %combine.9.refs_0_), channel_id=1, source_target_pairs={{8,16},{9,17},{10,18},{11,19},{12,20},{13,21},{14,22},{15,23}} | collective-permute-start | bytes 626696 | tf_op jit(solution)/shard_map/ppermute | solution.py:686
  95.9 11.9 %collective-permute-start.29 = (bf16[256,768]{1,0:T(8,128)(2,1)S(1)}, bf16[256,768]{1,0:T(8,128)(2,1)S(1)}, u32[]{:S(2)}, u32[]{:S(2)}) collective-permute-start(bf16[256,768]{1,0:T(8,128)(2,1)S(1)} %get-tuple-element.112), channel_id=1, source_target_pairs={{0,4},{1,5},{2,6},{3,7},{4,0},{5,1},{6,2},{7,3},{8,12},{9,13},{10,... | collective-permute-start | bytes 1179656 | tf_op jit(solution)/shard_map/ppermute | solution.py:686
  104.9 2.9 %collective-permute-start.28 = (bf16[256,512]{1,0:T(8,128)(2,1)S(1)}, bf16[256,512]{1,0:T(8,128)(2,1)S(1)}, u32[]{:S(2)}, u32[]{:S(2)}) collective-permute-start(bf16[256,512]{1,0:T(8,128)(2,1)S(1)} %get-tuple-element.111), channel_id=1, source_target_pairs={{0,4},{1,5},{2,6},{3,7},{4,0},{5,1},{6,2},{7,3},{8,12},{9,13},{10,... | collective-permute-start | bytes 786440 | tf_op jit(solution)/shard_map/ppermute | solution.py:686
  107.1 1.6 %collective-permute-start.31 = (bf16[256,384]{1,0:T(8,128)(2,1)S(1)}, bf16[256,384]{1,0:T(8,128)(2,1)S(1)}, u32[]{:S(2)}, u32[]{:S(2)}) collective-permute-start(bf16[256,384]{1,0:T(8,128)(2,1)S(1)} %get-tuple-element.114), channel_id=1, source_target_pairs={{0,4},{1,5},{2,6},{3,7},{4,0},{5,1},{6,2},{7,3},{8,12},{9,13},{10,... | collective-permute-start | bytes 589832 | tf_op jit(solution)/shard_map/ppermute | solution.py:686
  107.7 1.4 %collective-permute-start.30 = (bf16[256,384]{1,0:T(8,128)(2,1)S(1)}, bf16[256,384]{1,0:T(8,128)(2,1)S(1)}, u32[]{:S(2)}, u32[]{:S(2)}) collective-permute-start(bf16[256,384]{1,0:T(8,128)(2,1)S(1)} %get-tuple-element.113), channel_id=1, source_target_pairs={{0,4},{1,5},{2,6},{3,7},{4,0},{5,1},{6,2},{7,3},{8,12},{9,13},{10,... | collective-permute-start | bytes 589832 | tf_op jit(solution)/shard_map/ppermute | solution.py:686
  (8 other events, 108.4 us)

commit v13 on v12

--- a/solution.py
+++ b/solution.py
@@ -168,7 +168,6 @@
 GROUPED = ((0, 0, 512), (2, 0, 768), (3, 0, 384), (3, 384, 384))
 FIRST_ROUND = ((256, 256), (384, 384), (384,), (384,))
 SECOND_ROUND = ((512,), (384, 384), (384,), (384,))
-ALONE = (2, 3)
 
 
 def halves(value, count):
@@ -501,15 +500,17 @@
         start = at.stop
 
 
-def combine_kernel(count, *refs):
-    early, late, out_ref = refs[:count], refs[count : 2 * count], refs[-1]
+def combine_kernel(count, place, *refs):
+    got, own, out_ref = refs[:count], refs[count : 2 * count], refs[-1]
+    odd = place[1] % 2 == 1
     start = 0
-    for early_ref, late_ref in zip(early, late):
-        at = slice(start, start + late_ref.shape[1])
-        decay = decay_of(late_ref)
-        total = decay * early_ref[:STATE].astype(F32) + late_ref[:STATE].astype(F32)
-        out_ref[:STATE, at] = total.astype(BF16)
-        put_decay(out_ref.at[:, at], decay * decay_of(early_ref))
+    for got_ref, own_ref in zip(got, own):
+        at = slice(start, start + own_ref.shape[1])
+        theirs, mine = got_ref[:STATE].astype(F32), own_ref[:STATE].astype(F32)
+        decay, other = decay_of(own_ref), decay_of(got_ref)
+        early, late = jnp.where(odd, theirs, mine), jnp.where(odd, mine, theirs)
+        out_ref[:STATE, at] = (jnp.where(odd, decay, other) * early + late).astype(BF16)
+        put_decay(out_ref.at[:, at], decay * other)
         start = at.stop
 
 
@@ -555,15 +556,15 @@
     mix(first_head, x_ref, cum_ref, row_ref, score_ref, skip_ref, put)
 
 
-def carry(first_head, core, lasts, befores, alones, own_ref, c_ref, factor_ref, add, keep_ref, send_ref):
+def carry(first_head, place, lasts, befores, own_ref, c_ref, factor_ref, add, keep_ref, send_ref):
     expand = spread(first_head, own_ref.shape[1], 2)
     last, before = (
         refs[0][...] if len(refs) == 1 else jnp.concatenate([ref[...] for ref in refs], 1)
         for refs in (lasts, befores)
     )
-    held = last[:STATE].astype(F32) + decay_of(last) * before[:STATE].astype(F32)
-    for alone in alones:
-        held = held + alone[:STATE].astype(F32)
+    odd, core = place[1] % 2 == 1, place[2]
+    near = jnp.where(odd, last[:STATE].astype(F32), 0.0)
+    held = near + jnp.where(odd, decay_of(last), 1.0) * before[:STATE].astype(F32)
     factor = dot(factor_ref[...], expand)
     outs = []
     for block in range(PAIR):
@@ -588,7 +589,7 @@
     for number in counts:
         groups.append(refs[:number])
         refs = refs[number:]
-    carry(first_head, place[2], *groups, *refs[:4], *refs[-2:])
+    carry(first_head, place, *groups, *refs[:4], *refs[-2:])
 
 
 def finish_kernel(first_head, counts, place, *refs):
@@ -599,7 +600,7 @@
     own_ref, c_ref, factor_ref = refs[:3]
     keep_ref, send_ref, partial = refs[-3:]
     local_kernel(first_head, *refs[3:8], partial)
-    carry(first_head, place[2], *groups, own_ref, c_ref, factor_ref, partial, keep_ref, send_ref)
+    carry(first_head, place, *groups, own_ref, c_ref, factor_ref, partial, keep_ref, send_ref)
 
 
 def place_kernel(firsts, place, *refs):
@@ -768,7 +769,7 @@
         name="prep",
     )
     count = len(GROUPED)
-    x, sent, own, last, joined, before, alone, keep, send = ([None] * count for _ in range(9))
+    x, sent, own, last, joined, before, keep, send = ([None] * count for _ in range(8))
 
     def first_head(i):
         return (sum(WIDTHS[: GROUPED[i][0]]) + GROUPED[i][1]) // HEAD_DIM
@@ -782,33 +783,28 @@
             scratch=[pltpu.VMEM((slab + 8, width), F32)],
             name="state",
         )
-        every = i not in ALONE
-        last[i] = [over(part, lambda i: i + peers if every or i // peers % 2 == 0 else None) for part in sent[i]]
+        last[i] = [over(part, lambda i: i ^ peers if i // peers != 3 else None) for part in sent[i]]
 
     def combine_of(i, order):
-        joined[i], before[i], alone[i] = [], [], []
+        joined[i], before[i] = [], []
         step = len(FIRST_ROUND[i]) // len(SECOND_ROUND[i])
         for j, width in enumerate(SECOND_ROUND[i]):
             early, late = last[i][j * step : (j + 1) * step], sent[i][j * step : (j + 1) * step]
             (total,) = call(
                 functools.partial(combine_kernel, len(early)),
                 [((STATE + 16, width), BF16)],
-                early + late + [Stay(o) for o in order],
+                [place] + early + late + [Stay(o) for o in order],
                 name="combine",
             )
             joined[i].append(total)
-            if i in ALONE:
-                before[i].append(over(total, lambda i: i + 2 * peers if i // peers == 1 else None))
-                alone[i].append(over(total, lambda i: i + peers if i // peers == 1 else None))
-            else:
-                before[i].append(over(total, lambda i: i + 2 * peers))
+            before[i].append(over(total, lambda i: i + 2 * peers))
             order = [total]
 
     def finish_of(body, i, operands, order, **more):
         keep[i], send[i] = call(
-            functools.partial(body, first_head(i), (len(last[i]), len(before[i]), len(alone[i]))),
+            functools.partial(body, first_head(i), (len(last[i]), len(before[i]))),
             [((BLOCK, GROUPED[i][2]), BF16)] * 2,
-            [place, *last[i], *before[i], *alone[i], own[i], c, factor] + operands + [Stay(o) for o in order],
+            [place, *last[i], *before[i], own[i], c, factor] + operands + [Stay(o) for o in order],
             name="final",
             **more,
         )

time: 112 us -> 111 us (level)
  Pallas kernels: 28.3 us -> 31.2 us
  waiting for transfers between devices: 32 us -> 29.9 us
    pallas_call x24, Pallas kernels: 26.4 us -> 29.3 us  [call(): pl.pallas_call(body, out_shape=shapes, in_specs=specs, out_specs=[vmem] *...]
    ppermute x32 -> x30, waiting for transfers between devices: 32 us -> 29.9 us  [over(): lax.ppermute(block, axes, [(i, j) for i, j in route if j is not None and...]
    ppermute x32 -> x30, starting transfers between devices: 48.5 us -> 47.6 us  [over(): lax.ppermute(block, axes, [(i, j) for i, j in route if j is not None and...]
  transfers between devices with their start and end apart: 32 -> 30, of which waited for: 10 -> 9; matrix products, arithmetic and copies ran while one was open for 0% -> 0% of each run, Pallas kernels for 22% -> 24%
where the time goes in v13:
time: 111 us
  starting transfers between devices  47.6 us (43%)
  Pallas kernels  31.2 us (28%)
  waiting for transfers between devices  29.9 us (27%)
  local copies, waits for them, and re-layouts  1.86 us (2%)
    ppermute x30, starting transfers between devices, over(): lax.ppermute(block, axes, [(i, j) for i, j in route if j is not None and...  47.6 us
    ppermute x30, waiting for transfers between devices, over(): lax.ppermute(block, axes, [(i, j) for i, j in route if j is not None and...  29.9 us
    pallas_call x24, Pallas kernels, call(): pl.pallas_call(body, out_shape=shapes, in_specs=specs, out_specs=[vmem] *...  29.3 us
  transfers between devices with their start and end apart: 30, of which 9 were waited for; matrix products, arithmetic and copies ran while one was open for 0% of the time, Pallas kernels for 24%

profile of v13, /device:TPU:19, one launch (start us, length us, event | category | flops | bytes accessed | tf_op | source)
XLA Modules:
  0.0 111.1 jit_solution(5995196615702315954)
XLA Ops:
  0.1 1.7 %copy-done = bf16[64,20480]{1,0:T(8,128)(2,1)S(1)} copy-done((bf16[64,20480]{1,0:T(8,128)(2,1)S(1)}, bf16[64,20480]{1,0:T(8,128)(2,1)}, u32[]{:S(2)}) %copy-start) | copy-done | bytes 2621464
  2.8 1.3 %pack.1 = (bf16[64,8448]{1,0:T(8,128)(2,1)S(1)}, bf16[16,10240]{1,0:T(8,128)(2,1)S(1)}) custom-call(s32[5]{0:T(128)S(1)} %stack.23.place, bf16[64,20480]{1,0:T(8,128)(2,1)S(1)} %copy-done, bf16[64,256]{1,0:T(8,128)(2,1)S(1)} %copy-done.2, bf16[64,4096]{1,0:T(8,128)(2,1)S(1)} %pack_first.1.order), custom_call_target="tpu_custom_call" | custom-call | flops 1 | bytes 1 | tf_op jit(solution)/shard_map/pack/pallas_call | solution.py:662
  5.0 3.0 %collective-permute-done.got_first.got.edges = bf16[64,4096]{1,0:T(8,128)(2,1)S(1)} collective-permute-done((bf16[64,4096]{1,0:T(8,128)(2,1)S(1)}, bf16[64,4096]{1,0:T(8,128)(2,1)S(1)}, u32[]{:S(2)}, u32[]{:S(2)}) %collective-permute-start) | collective-permute-done | bytes 524320 | tf_op jit(solution)/shard_map/ppermute | solution.py:687
  8.8 1.4 %collective-permute-start.1 = (bf16[128,512]{1,0:T(8,128)(2,1)S(1)}, bf16[128,512]{1,0:T(8,128)(2,1)S(1)}, u32[]{:S(2)}, u32[]{:S(2)}) collective-permute-start(bf16[128,512]{1,0:T(8,128)(2,1)S(1)} %get-tuple-element.62), channel_id=1, source_target_pairs={{0,1},{1,0},{2,3},{3,2},{4,5},{5,4},{6,7},{7,6},{8,9},{9,8},{10,11... | collective-permute-start | bytes 393224 | tf_op jit(solution)/shard_map/ppermute | solution.py:687
  10.9 3.7 %collective-permute-start.3 = (bf16[128,512]{1,0:T(8,128)(2,1)S(1)}, bf16[128,512]{1,0:T(8,128)(2,1)S(1)}, u32[]{:S(2)}, u32[]{:S(2)}) collective-permute-start(bf16[128,512]{1,0:T(8,128)(2,1)S(1)} %get-tuple-element.64), channel_id=1, source_target_pairs={{0,3},{1,2},{2,1},{3,0},{4,7},{5,6},{6,5},{7,4},{8,11},{9,10},{10,... | collective-permute-start | bytes 393224 | tf_op jit(solution)/shard_map/ppermute | solution.py:687
  17.0 1.5 %collective-permute-start.8 = (bf16[128,384]{1,0:T(8,128)(2,1)S(1)}, bf16[128,384]{1,0:T(8,128)(2,1)S(1)}, u32[]{:S(2)}, u32[]{:S(2)}) collective-permute-start(bf16[128,384]{1,0:T(8,128)(2,1)S(1)} %get-tuple-element.72), channel_id=1, source_target_pairs={{0,3},{1,2},{2,1},{3,0},{4,7},{5,6},{6,5},{7,4},{8,11},{9,10},{10,... | collective-permute-start | bytes 294920 | tf_op jit(solution)/shard_map/ppermute | solution.py:687
  19.3 10.6 %collective-permute-done.3.refs_3_.refs_5_ = bf16[128,512]{1,0:T(8,128)(2,1)S(1)} collective-permute-done((bf16[128,512]{1,0:T(8,128)(2,1)S(1)}, bf16[128,512]{1,0:T(8,128)(2,1)S(1)}, u32[]{:S(2)}, u32[]{:S(2)}) %collective-permute-start.3) | collective-permute-done | bytes 131104 | tf_op jit(solution)/shard_map/ppermute | solution.py:687
  29.9 4.2 %collective-permute-done.8.refs_3_.refs_8_ = bf16[128,384]{1,0:T(8,128)(2,1)S(1)} collective-permute-done((bf16[128,384]{1,0:T(8,128)(2,1)S(1)}, bf16[128,384]{1,0:T(8,128)(2,1)S(1)}, u32[]{:S(2)}, u32[]{:S(2)}) %collective-permute-start.8) | collective-permute-done | bytes 98336 | tf_op jit(solution)/shard_map/ppermute | solution.py:687
  34.5 2.2 %collective-permute-start.17 = (bf16[128,768]{1,0:T(8,128)(2,1)S(1)}, bf16[128,768]{1,0:T(8,128)(2,1)S(1)}, u32[]{:S(2)}, u32[]{:S(2)}) collective-permute-start(bf16[128,768]{1,0:T(8,128)(2,1)S(1)} %get-tuple-element.90), channel_id=1, source_target_pairs={{0,3},{1,2},{2,1},{3,0},{4,7},{5,6},{6,5},{7,4},{8,11},{9,10},{10,... | collective-permute-start | bytes 589832 | tf_op jit(solution)/shard_map/ppermute | solution.py:687
  37.5 1.7 %prep.1 = (bf16[512,256]{1,0:T(8,128)(2,1)S(1)}, f32[4,2560]{1,0:T(4,128)S(1)}, f32[512,128]{1,0:T(8,128)S(1)}, f32[128,512]{1,0:T(8,128)S(1)}, bf16[512,256]{1,...) custom-call(s32[5]{0:T(128)S(1)} %stack.23.place, ...), custom_call_target="tpu_custom_call" | custom-call | flops 1 | bytes 1 | tf_op jit(solution)/shard_map/prep/pallas_call | solution.py:662
  39.2 2.1 %state.4 = (bf16[512,512]{1,0:T(8,128)(2,1)S(1)}, f32[256,512]{1,0:T(8,128)S(1)}, bf16[272,256]{1,0:T(8,128)(2,1)S(1)}, bf16[272,256]{1,0:T(8,128)(2,1)S(1)}) custom-call(s32[5]{0:T(128)S(1)} %stack.23.place, bf16[128,512]{1,0:T(8,128)(2,1)S(1)} %get-tuple-element.61.refs_0_, bf16[128,512]{1,0:T(8,128)(2,1)S(1)} %collective-permute-done.1.refs_1_.refs_3_, ...), custom_call_target="tpu_custom_call" | custom-call | flops 1 | bytes 1 | tf_op jit(solution)/shard_map/state/pallas_call | solution.py:662
  41.2 2.2 %collective-permute-start.10 = (bf16[272,256]{1,0:T(8,128)(2,1)S(1)}, bf16[272,256]{1,0:T(8,128)(2,1)S(1)}, u32[]{:S(2)}, u32[]{:S(2)}) collective-permute-start(bf16[272,256]{1,0:T(8,128)(2,1)S(1)} %get-tuple-element.79.refs_3_.refs_1_), channel_id=1, source_target_pairs={{0,8},{1,9},{2,10},{3,11},{4,12},{5,13},{6,14},{7,15},{8,0},{9,1},... | collective-permute-start | bytes 417800 | tf_op jit(solution)/shard_map/ppermute | solution.py:687
  43.4 3.1 %collective-permute-start.9 = (bf16[272,256]{1,0:T(8,128)(2,1)S(1)}, bf16[272,256]{1,0:T(8,128)(2,1)S(1)}, u32[]{:S(2)}, u32[]{:S(2)}) collective-permute-start(bf16[272,256]{1,0:T(8,128)(2,1)S(1)} %get-tuple-element.78.refs_2_.refs_0_), channel_id=1, source_target_pairs={{0,8},{1,9},{2,10},{3,11},{4,12},{5,13},{6,14},{7,15},{8,0},{9,1},... | collective-permute-start | bytes 417800 | tf_op jit(solution)/shard_map/ppermute | solution.py:687
  48.4 2.5 %collective-permute-done.9.refs_0_ = bf16[272,256]{1,0:T(8,128)(2,1)S(1)} collective-permute-done((bf16[272,256]{1,0:T(8,128)(2,1)S(1)}, bf16[272,256]{1,0:T(8,128)(2,1)S(1)}, u32[]{:S(2)}, u32[]{:S(2)}) %collective-permute-start.9) | collective-permute-done | bytes 139296 | tf_op jit(solution)/shard_map/ppermute | solution.py:687
  53.7 2.6 %state.5 = (bf16[512,768]{1,0:T(8,128)(2,1)S(1)}, f32[256,768]{1,0:T(8,128)S(1)}, bf16[272,384]{1,0:T(8,128)(2,1)S(1)}, bf16[272,384]{1,0:T(8,128)(2,1)S(1)}) custom-call(s32[5]{0:T(128)S(1)} %stack.23.place, bf16[128,768]{1,0:T(8,128)(2,1)S(1)} %get-tuple-element.73.refs_9_.refs_0_, bf16[128,768]{1,0:T(8,128)(2,1)S(1)} %collective-permute-done.15.refs_1_, ...), custom_call_target="tpu_custom_call" | custom-call | flops 1 | bytes 1 | tf_op jit(solution)/shard_map/state/pallas_call | solution.py:662
  56.3 2.2 %collective-permute-start.18 = (bf16[272,384]{1,0:T(8,128)(2,1)S(1)}, bf16[272,384]{1,0:T(8,128)(2,1)S(1)}, u32[]{:S(2)}, u32[]{:S(2)}) collective-permute-start(bf16[272,384]{1,0:T(8,128)(2,1)S(1)} %get-tuple-element.91.refs_1_), channel_id=1, source_target_pairs={{0,8},{1,9},{2,10},{3,11},{4,12},{5,13},{6,14},{7,15},{8,0},{9,1},... | collective-permute-start | bytes 626696 | tf_op jit(solution)/shard_map/ppermute | solution.py:687
  58.5 3.1 %collective-permute-start.19 = (bf16[272,384]{1,0:T(8,128)(2,1)S(1)}, bf16[272,384]{1,0:T(8,128)(2,1)S(1)}, u32[]{:S(2)}, u32[]{:S(2)}) collective-permute-start(bf16[272,384]{1,0:T(8,128)(2,1)S(1)} %get-tuple-element.92.refs_1_), channel_id=1, source_target_pairs={{0,8},{1,9},{2,10},{3,11},{4,12},{5,13},{6,14},{7,15},{8,0},{9,1},... | collective-permute-start | bytes 626696 | tf_op jit(solution)/shard_map/ppermute | solution.py:687
  61.6 1.2 %collective-permute-done.18.refs_0_ = bf16[272,384]{1,0:T(8,128)(2,1)S(1)} collective-permute-done((bf16[272,384]{1,0:T(8,128)(2,1)S(1)}, bf16[272,384]{1,0:T(8,128)(2,1)S(1)}, u32[]{:S(2)}, u32[]{:S(2)}) %collective-permute-start.18) | collective-permute-done | bytes 208928 | tf_op jit(solution)/shard_map/ppermute | solution.py:687
  63.5 4.1 %collective-permute-start.20 = (bf16[272,384]{1,0:T(8,128)(2,1)S(1)}, bf16[272,384]{1,0:T(8,128)(2,1)S(1)}, u32[]{:S(2)}, u32[]{:S(2)}) collective-permute-start(bf16[272,384]{1,0:T(8,128)(2,1)S(1)} %combine.6.refs_2_.refs_10_), channel_id=1, source_target_pairs={{0,16},{1,17},{2,18},{3,19},{4,20},{5,21},{6,22},{7,23},{8,24},{9,... | collective-permute-start | bytes 626696 | tf_op jit(solution)/shard_map/ppermute | solution.py:687
  68.3 1.6 %collective-permute-start.21 = (bf16[272,384]{1,0:T(8,128)(2,1)S(1)}, bf16[272,384]{1,0:T(8,128)(2,1)S(1)}, u32[]{:S(2)}, u32[]{:S(2)}) collective-permute-start(bf16[272,384]{1,0:T(8,128)(2,1)S(1)} %combine.7.refs_11_), channel_id=1, source_target_pairs={{0,16},{1,17},{2,18},{3,19},{4,20},{5,21},{6,22},{7,23},{8,24},{9,... | collective-permute-start | bytes 626696 | tf_op jit(solution)/shard_map/ppermute | solution.py:687
  69.9 6.8 %collective-permute-done.14.refs_3_ = bf16[128,1024]{1,0:T(8,128)(2,1)S(1)} collective-permute-done((bf16[128,1024]{1,0:T(8,128)(2,1)S(1)}, bf16[128,1024]{1,0:T(8,128)(2,1)S(1)}, u32[]{:S(2)}, u32[]{:S(2)}) %collective-permute-start.14) | collective-permute-done | bytes 262176 | tf_op jit(solution)/shard_map/ppermute | solution.py:687
  76.6 1.9 %state.6 = (bf16[512,384]{1,0:T(8,128)(2,1)S(1)}, f32[256,384]{1,0:T(8,128)S(1)}, bf16[272,384]{1,0:T(8,128)(2,1)S(1)}) custom-call(s32[5]{0:T(128)S(1)} %stack.23.place, bf16[128,1024]{1,0:T(8,128)(2,1)S(1)} %get-tuple-element.81.refs_10_.refs_0_, bf16[128,1024]{1,0:T(8,128)(2,1)S(1)} %collective-permute-done.12.refs_1_, ...), custom_call_target="tpu_custom_call" | custom-call | flops 1 | bytes 1 | tf_op jit(solution)/shard_map/state/pallas_call | solution.py:662
  78.5 1.9 %collective-permute-start.23 = (bf16[272,384]{1,0:T(8,128)(2,1)S(1)}, bf16[272,384]{1,0:T(8,128)(2,1)S(1)}, u32[]{:S(2)}, u32[]{:S(2)}) collective-permute-start(bf16[272,384]{1,0:T(8,128)(2,1)S(1)} %get-tuple-element.93.refs_10_.refs_1_), channel_id=1, source_target_pairs={{0,8},{1,9},{2,10},{3,11},{4,12},{5,13},{6,14},{7,15},{8,0},{9,1},... | collective-permute-start | bytes 626696 | tf_op jit(solution)/shard_map/ppermute | solution.py:687
  80.5 1.9 %state.7 = (bf16[512,384]{1,0:T(8,128)(2,1)S(1)}, f32[256,384]{1,0:T(8,128)S(1)}, bf16[272,384]{1,0:T(8,128)(2,1)S(1)}) custom-call(s32[5]{0:T(128)S(1)} %stack.23.place, bf16[128,1024]{1,0:T(8,128)(2,1)S(1)} %get-tuple-element.81.refs_10_.refs_0_, bf16[128,1024]{1,0:T(8,128)(2,1)S(1)} %collective-permute-done.12.refs_1_, ...), custom_call_target="tpu_custom_call" | custom-call | flops 1 | bytes 1 | tf_op jit(solution)/shard_map/state/pallas_call | solution.py:662
  82.4 3.4 %collective-permute-start.22 = (bf16[272,384]{1,0:T(8,128)(2,1)S(1)}, bf16[272,384]{1,0:T(8,128)(2,1)S(1)}, u32[]{:S(2)}, u32[]{:S(2)}) collective-permute-start(bf16[272,384]{1,0:T(8,128)(2,1)S(1)} %get-tuple-element.94.refs_8_.refs_1_), channel_id=1, source_target_pairs={{0,8},{1,9},{2,10},{3,11},{4,12},{5,13},{6,14},{7,15},{8,0},{9,1},... | collective-permute-start | bytes 626696 | tf_op jit(solution)/shard_map/ppermute | solution.py:687
  85.8 1.3 %collective-permute-start.11 = (bf16[272,512]{1,0:T(8,128)(2,1)S(1)}, bf16[272,512]{1,0:T(8,128)(2,1)S(1)}, u32[]{:S(2)}, u32[]{:S(2)}) collective-permute-start(bf16[272,512]{1,0:T(8,128)(2,1)S(1)} %combine.5.refs_11_), channel_id=1, source_target_pairs={{0,16},{1,17},{2,18},{3,19},{4,20},{5,21},{6,22},{7,23},{8,24},{9,... | collective-permute-start | bytes 835592 | tf_op jit(solution)/shard_map/ppermute | solution.py:687
  88.9 1.5 %collective-permute-start.24 = (bf16[272,384]{1,0:T(8,128)(2,1)S(1)}, bf16[272,384]{1,0:T(8,128)(2,1)S(1)}, u32[]{:S(2)}, u32[]{:S(2)}) collective-permute-start(bf16[272,384]{1,0:T(8,128)(2,1)S(1)} %combine.8.refs_12_), channel_id=1, source_target_pairs={{0,16},{1,17},{2,18},{3,19},{4,20},{5,21},{6,22},{7,23},{8,24},{9,... | collective-permute-start | bytes 626696 | tf_op jit(solution)/shard_map/ppermute | solution.py:687
  90.4 2.6 %final.4 = (bf16[256,768]{1,0:T(8,128)(2,1)S(1)}, bf16[256,768]{1,0:T(8,128)(2,1)S(1)}) custom-call(s32[5]{0:T(128)S(1)} %stack.23.place, bf16[272,384]{1,0:T(8,128)(2,1)S(1)} %collective-permute-done.18.refs_0_, bf16[272,384]{1,0:T(8,128)(2,1)S(1)} %collective-permute-done.19.refs_0_.refs_1_, bf16[272,384]{1,0:T(8,128)(2,1)S(1)} %collective-permute-done.20.refs_9_.refs_2_, ...), custom_call_target="tpu_custom_call" | custom-call | flops 1 | bytes 1 | tf_op jit(solution)/shard_map/final/pallas_call | solution.py:662
  93.7 1.3 %collective-permute-start.25 = (bf16[272,384]{1,0:T(8,128)(2,1)S(1)}, bf16[272,384]{1,0:T(8,128)(2,1)S(1)}, u32[]{:S(2)}, u32[]{:S(2)}) collective-permute-start(bf16[272,384]{1,0:T(8,128)(2,1)S(1)} %combine.9.refs_0_), channel_id=1, source_target_pairs={{0,16},{1,17},{2,18},{3,19},{4,20},{5,21},{6,22},{7,23},{8,24},{9,... | collective-permute-start | bytes 626696 | tf_op jit(solution)/shard_map/ppermute | solution.py:687
  95.0 6.3 %collective-permute-start.27 = (bf16[256,768]{1,0:T(8,128)(2,1)S(1)}, bf16[256,768]{1,0:T(8,128)(2,1)S(1)}, u32[]{:S(2)}, u32[]{:S(2)}) collective-permute-start(bf16[256,768]{1,0:T(8,128)(2,1)S(1)} %get-tuple-element.112), channel_id=1, source_target_pairs={{0,4},{1,5},{2,6},{3,7},{4,0},{5,1},{6,2},{7,3},{8,12},{9,13},{10,... | collective-permute-start | bytes 1179656 | tf_op jit(solution)/shard_map/ppermute | solution.py:687
  102.8 1.9 %final.5 = (bf16[256,512]{1,0:T(8,128)(2,1)S(1)}, bf16[256,512]{1,0:T(8,128)(2,1)S(1)}) custom-call(s32[5]{0:T(128)S(1)} %stack.23.place, bf16[272,256]{1,0:T(8,128)(2,1)S(1)} %collective-permute-done.9.refs_0_, bf16[272,256]{1,0:T(8,128)(2,1)S(1)} %collective-permute-done.10.refs_1_, bf16[272,512]{1,0:T(8,128)(2,1)S(1)} %collective-permute-done.11.refs_2_, ...), custom_call_target="tpu_custom_call" | custom-call | flops 1 | bytes 1 | tf_op jit(solution)/shard_map/final/pallas_call | solution.py:662
  109.0 1.9 %place.1 = bf16[256,4096]{1,0:T(8,128)(2,1)} custom-call(s32[5]{0:T(128)S(1)} %stack.23.place, bf16[256,512]{1,0:T(8,128)(2,1)S(1)} %get-tuple-element.106.refs_6_.refs_0_, bf16[256,768]{1,0:T(8,128)(2,1)S(1)} %get-tuple-element.105.refs_2_.refs_1_, bf16[256,384]{1,0:T(8,128)(2,1)S(1)} %get-tuple-element.108.refs_6_.refs_2_, ...), custom_call_target="tpu_custom_call" | custom-call | flops 1 | bytes 1 | tf_op jit(solution)/shard_map/place/pallas_call | solution.py:624
  (71 shorter events, 22.0 us)
Async XLA Ops:
  4.1 10.5 %collective-permute-start.4 = (bf16[64,8448]{1,0:T(8,128)(2,1)S(1)}, bf16[64,8448]{1,0:T(8,128)(2,1)S(1)}, u32[]{:S(2)}, u32[]{:S(2)}) collective-permute-start(bf16[64,8448]{1,0:T(8,128)(2,1)S(1)} %get-tuple-element.65), channel_id=1, source_target_pairs={{0,4},{1,5},{2,6},{3,7},{4,0},{5,1},{6,2},{7,3},{8,12},{9,13},{10,... | collective-permute-start | bytes 3244040 | tf_op jit(solution)/shard_map/ppermute | solution.py:687
  4.9 3.1 %collective-permute-start = (bf16[64,4096]{1,0:T(8,128)(2,1)S(1)}, bf16[64,4096]{1,0:T(8,128)(2,1)S(1)}, u32[]{:S(2)}, u32[]{:S(2)}) collective-permute-start(bf16[64,4096]{1,0:T(8,128)(2,1)S(1)} %pack_first.1.order), channel_id=1, source_target_pairs={{0,4},{1,5},{2,6},{3,7},{4,0},{5,1},{6,2},{7,3},{8,12},{9,13},{10,... | collective-permute-start | bytes 1572872 | tf_op jit(solution)/shard_map/ppermute | solution.py:687
  8.8 8.2 %collective-permute-start.1 = (bf16[128,512]{1,0:T(8,128)(2,1)S(1)}, bf16[128,512]{1,0:T(8,128)(2,1)S(1)}, u32[]{:S(2)}, u32[]{:S(2)}) collective-permute-start(bf16[128,512]{1,0:T(8,128)(2,1)S(1)} %get-tuple-element.62), channel_id=1, source_target_pairs={{0,1},{1,0},{2,3},{3,2},{4,5},{5,4},{6,7},{7,6},{8,9},{9,8},{10,11... | collective-permute-start | bytes 393224 | tf_op jit(solution)/shard_map/ppermute | solution.py:687
  10.1 4.5 %collective-permute-start.5 = (bf16[3,10240]{1,0:T(4,128)(2,1)S(1)}, bf16[3,10240]{1,0:T(4,128)(2,1)S(1)}, u32[]{:S(2)}, u32[]{:S(2)}) collective-permute-start(bf16[3,10240]{1,0:T(4,128)(2,1)S(1)} %get-tuple-element.68), channel_id=1, source_target_pairs={{3,11},{7,15},{11,19},{15,23},{19,27},{23,31}} | collective-permute-start | bytes 184328 | tf_op jit(solution)/shard_map/ppermute | solution.py:687
  10.8 8.5 %collective-permute-start.2 = (bf16[128,512]{1,0:T(8,128)(2,1)S(1)}, bf16[128,512]{1,0:T(8,128)(2,1)S(1)}, u32[]{:S(2)}, u32[]{:S(2)}) collective-permute-start(bf16[128,512]{1,0:T(8,128)(2,1)S(1)} %get-tuple-element.63), channel_id=1, source_target_pairs={{0,2},{1,3},{2,0},{3,1},{4,6},{5,7},{6,4},{7,5},{8,10},{9,11},{10,... | collective-permute-start | bytes 393224 | tf_op jit(solution)/shard_map/ppermute | solution.py:687
  10.9 18.9 %collective-permute-start.3 = (bf16[128,512]{1,0:T(8,128)(2,1)S(1)}, bf16[128,512]{1,0:T(8,128)(2,1)S(1)}, u32[]{:S(2)}, u32[]{:S(2)}) collective-permute-start(bf16[128,512]{1,0:T(8,128)(2,1)S(1)} %get-tuple-element.64), channel_id=1, source_target_pairs={{0,3},{1,2},{2,1},{3,0},{4,7},{5,6},{6,5},{7,4},{8,11},{9,10},{10,... | collective-permute-start | bytes 393224 | tf_op jit(solution)/shard_map/ppermute | solution.py:687
  15.7 14.2 %collective-permute-start.6 = (bf16[128,384]{1,0:T(8,128)(2,1)S(1)}, bf16[128,384]{1,0:T(8,128)(2,1)S(1)}, u32[]{:S(2)}, u32[]{:S(2)}) collective-permute-start(bf16[128,384]{1,0:T(8,128)(2,1)S(1)} %get-tuple-element.70), channel_id=1, source_target_pairs={{0,1},{1,0},{2,3},{3,2},{4,5},{5,4},{6,7},{7,6},{8,9},{9,8},{10,11... | collective-permute-start | bytes 294920 | tf_op jit(solution)/shard_map/ppermute | solution.py:687
  16.8 13.1 %collective-permute-start.7 = (bf16[128,384]{1,0:T(8,128)(2,1)S(1)}, bf16[128,384]{1,0:T(8,128)(2,1)S(1)}, u32[]{:S(2)}, u32[]{:S(2)}) collective-permute-start(bf16[128,384]{1,0:T(8,128)(2,1)S(1)} %get-tuple-element.71), channel_id=1, source_target_pairs={{0,2},{1,3},{2,0},{3,1},{4,6},{5,7},{6,4},{7,5},{8,10},{9,11},{10,... | collective-permute-start | bytes 294920 | tf_op jit(solution)/shard_map/ppermute | solution.py:687
  17.0 17.1 %collective-permute-start.8 = (bf16[128,384]{1,0:T(8,128)(2,1)S(1)}, bf16[128,384]{1,0:T(8,128)(2,1)S(1)}, u32[]{:S(2)}, u32[]{:S(2)}) collective-permute-start(bf16[128,384]{1,0:T(8,128)(2,1)S(1)} %get-tuple-element.72), channel_id=1, source_target_pairs={{0,3},{1,2},{2,1},{3,0},{4,7},{5,6},{6,5},{7,4},{8,11},{9,10},{10,... | collective-permute-start | bytes 294920 | tf_op jit(solution)/shard_map/ppermute | solution.py:687
  18.4 18.3 %copy-start.3 = (f32[4,20480]{1,0:T(4,128)S(1)}, f32[4,20480]{1,0:T(4,128)}, u32[]{:S(2)}) copy-start(f32[4,20480]{1,0:T(4,128)} %weight.1) | copy-start | bytes 983044
  18.4 18.3 %copy-start.4 = (f32[20480]{0:T(1024)S(1)}, f32[20480]{0:T(1024)}, u32[]{:S(2)}) copy-start(f32[20480]{0:T(1024)} %param.10) | copy-start | bytes 245764
  34.1 17.6 %collective-permute-start.15 = (bf16[128,768]{1,0:T(8,128)(2,1)S(1)}, bf16[128,768]{1,0:T(8,128)(2,1)S(1)}, u32[]{:S(2)}, u32[]{:S(2)}) collective-permute-start(bf16[128,768]{1,0:T(8,128)(2,1)S(1)} %get-tuple-element.88), channel_id=1, source_target_pairs={{0,1},{1,0},{2,3},{3,2},{4,5},{5,4},{6,7},{7,6},{8,9},{9,8},{10,11... | collective-permute-start | bytes 589832 | tf_op jit(solution)/shard_map/ppermute | solution.py:687
  34.1 19.5 %collective-permute-start.16 = (bf16[128,768]{1,0:T(8,128)(2,1)S(1)}, bf16[128,768]{1,0:T(8,128)(2,1)S(1)}, u32[]{:S(2)}, u32[]{:S(2)}) collective-permute-start(bf16[128,768]{1,0:T(8,128)(2,1)S(1)} %get-tuple-element.89), channel_id=1, source_target_pairs={{0,2},{1,3},{2,0},{3,1},{4,6},{5,7},{6,4},{7,5},{8,10},{9,11},{10,... | collective-permute-start | bytes 589832 | tf_op jit(solution)/shard_map/ppermute | solution.py:687
  34.5 19.2 %collective-permute-start.17 = (bf16[128,768]{1,0:T(8,128)(2,1)S(1)}, bf16[128,768]{1,0:T(8,128)(2,1)S(1)}, u32[]{:S(2)}, u32[]{:S(2)}) collective-permute-start(bf16[128,768]{1,0:T(8,128)(2,1)S(1)} %get-tuple-element.90), channel_id=1, source_target_pairs={{0,3},{1,2},{2,1},{3,0},{4,7},{5,6},{6,5},{7,4},{8,11},{9,10},{10,... | collective-permute-start | bytes 589832 | tf_op jit(solution)/shard_map/ppermute | solution.py:687
  41.2 6.2 %collective-permute-start.10 = (bf16[272,256]{1,0:T(8,128)(2,1)S(1)}, bf16[272,256]{1,0:T(8,128)(2,1)S(1)}, u32[]{:S(2)}, u32[]{:S(2)}) collective-permute-start(bf16[272,256]{1,0:T(8,128)(2,1)S(1)} %get-tuple-element.79.refs_3_.refs_1_), channel_id=1, source_target_pairs={{0,8},{1,9},{2,10},{3,11},{4,12},{5,13},{6,14},{7,15},{8,0},{9,1},... | collective-permute-start | bytes 417800 | tf_op jit(solution)/shard_map/ppermute | solution.py:687
  43.4 7.5 %collective-permute-start.9 = (bf16[272,256]{1,0:T(8,128)(2,1)S(1)}, bf16[272,256]{1,0:T(8,128)(2,1)S(1)}, u32[]{:S(2)}, u32[]{:S(2)}) collective-permute-start(bf16[272,256]{1,0:T(8,128)(2,1)S(1)} %get-tuple-element.78.refs_2_.refs_0_), channel_id=1, source_target_pairs={{0,8},{1,9},{2,10},{3,11},{4,12},{5,13},{6,14},{7,15},{8,0},{9,1},... | collective-permute-start | bytes 417800 | tf_op jit(solution)/shard_map/ppermute | solution.py:687
  47.5 22.4 %collective-permute-start.12 = (bf16[128,1024]{1,0:T(8,128)(2,1)S(1)}, bf16[128,1024]{1,0:T(8,128)(2,1)S(1)}, u32[]{:S(2)}, u32[]{:S(2)}) collective-permute-start(bf16[128,1024]{1,0:T(8,128)(2,1)S(1)} %get-tuple-element.82), channel_id=1, source_target_pairs={{0,1},{1,0},{2,3},{3,2},{4,5},{5,4},{6,7},{7,6},{8,9},{9,8},{10,11... | collective-permute-start | bytes 786440 | tf_op jit(solution)/shard_map/ppermute | solution.py:687
  50.9 19.0 %collective-permute-start.13 = (bf16[128,1024]{1,0:T(8,128)(2,1)S(1)}, bf16[128,1024]{1,0:T(8,128)(2,1)S(1)}, u32[]{:S(2)}, u32[]{:S(2)}) collective-permute-start(bf16[128,1024]{1,0:T(8,128)(2,1)S(1)} %get-tuple-element.83), channel_id=1, source_target_pairs={{0,2},{1,3},{2,0},{3,1},{4,6},{5,7},{6,4},{7,5},{8,10},{9,11},{10,... | collective-permute-start | bytes 786440 | tf_op jit(solution)/shard_map/ppermute | solution.py:687
  51.7 25.0 %collective-permute-start.14 = (bf16[128,1024]{1,0:T(8,128)(2,1)S(1)}, bf16[128,1024]{1,0:T(8,128)(2,1)S(1)}, u32[]{:S(2)}, u32[]{:S(2)}) collective-permute-start(bf16[128,1024]{1,0:T(8,128)(2,1)S(1)} %get-tuple-element.84), channel_id=1, source_target_pairs={{0,3},{1,2},{2,1},{3,0},{4,7},{5,6},{6,5},{7,4},{8,11},{9,10},{10,... | collective-permute-start | bytes 786440 | tf_op jit(solution)/shard_map/ppermute | solution.py:687
  56.3 6.5 %collective-permute-start.18 = (bf16[272,384]{1,0:T(8,128)(2,1)S(1)}, bf16[272,384]{1,0:T(8,128)(2,1)S(1)}, u32[]{:S(2)}, u32[]{:S(2)}) collective-permute-start(bf16[272,384]{1,0:T(8,128)(2,1)S(1)} %get-tuple-element.91.refs_1_), channel_id=1, source_target_pairs={{0,8},{1,9},{2,10},{3,11},{4,12},{5,13},{6,14},{7,15},{8,0},{9,1},... | collective-permute-start | bytes 626696 | tf_op jit(solution)/shard_map/ppermute | solution.py:687
  58.5 9.1 %collective-permute-start.19 = (bf16[272,384]{1,0:T(8,128)(2,1)S(1)}, bf16[272,384]{1,0:T(8,128)(2,1)S(1)}, u32[]{:S(2)}, u32[]{:S(2)}) collective-permute-start(bf16[272,384]{1,0:T(8,128)(2,1)S(1)} %get-tuple-element.92.refs_1_), channel_id=1, source_target_pairs={{0,8},{1,9},{2,10},{3,11},{4,12},{5,13},{6,14},{7,15},{8,0},{9,1},... | collective-permute-start | bytes 626696 | tf_op jit(solution)/shard_map/ppermute | solution.py:687
  63.5 23.6 %collective-permute-start.20 = (bf16[272,384]{1,0:T(8,128)(2,1)S(1)}, bf16[272,384]{1,0:T(8,128)(2,1)S(1)}, u32[]{:S(2)}, u32[]{:S(2)}) collective-permute-start(bf16[272,384]{1,0:T(8,128)(2,1)S(1)} %combine.6.refs_2_.refs_10_), channel_id=1, source_target_pairs={{0,16},{1,17},{2,18},{3,19},{4,20},{5,21},{6,22},{7,23},{8,24},{9,... | collective-permute-start | bytes 626696 | tf_op jit(solution)/shard_map/ppermute | solution.py:687
  68.3 18.8 %collective-permute-start.21 = (bf16[272,384]{1,0:T(8,128)(2,1)S(1)}, bf16[272,384]{1,0:T(8,128)(2,1)S(1)}, u32[]{:S(2)}, u32[]{:S(2)}) collective-permute-start(bf16[272,384]{1,0:T(8,128)(2,1)S(1)} %combine.7.refs_11_), channel_id=1, source_target_pairs={{0,16},{1,17},{2,18},{3,19},{4,20},{5,21},{6,22},{7,23},{8,24},{9,... | collective-permute-start | bytes 626696 | tf_op jit(solution)/shard_map/ppermute | solution.py:687
  78.5 9.7 %collective-permute-start.23 = (bf16[272,384]{1,0:T(8,128)(2,1)S(1)}, bf16[272,384]{1,0:T(8,128)(2,1)S(1)}, u32[]{:S(2)}, u32[]{:S(2)}) collective-permute-start(bf16[272,384]{1,0:T(8,128)(2,1)S(1)} %get-tuple-element.93.refs_10_.refs_1_), channel_id=1, source_target_pairs={{0,8},{1,9},{2,10},{3,11},{4,12},{5,13},{6,14},{7,15},{8,0},{9,1},... | collective-permute-start | bytes 626696 | tf_op jit(solution)/shard_map/ppermute | solution.py:687
  82.4 10.6 %collective-permute-start.22 = (bf16[272,384]{1,0:T(8,128)(2,1)S(1)}, bf16[272,384]{1,0:T(8,128)(2,1)S(1)}, u32[]{:S(2)}, u32[]{:S(2)}) collective-permute-start(bf16[272,384]{1,0:T(8,128)(2,1)S(1)} %get-tuple-element.94.refs_8_.refs_1_), channel_id=1, source_target_pairs={{0,8},{1,9},{2,10},{3,11},{4,12},{5,13},{6,14},{7,15},{8,0},{9,1},... | collective-permute-start | bytes 626696 | tf_op jit(solution)/shard_map/ppermute | solution.py:687
  85.8 17.1 %collective-permute-start.11 = (bf16[272,512]{1,0:T(8,128)(2,1)S(1)}, bf16[272,512]{1,0:T(8,128)(2,1)S(1)}, u32[]{:S(2)}, u32[]{:S(2)}) collective-permute-start(bf16[272,512]{1,0:T(8,128)(2,1)S(1)} %combine.5.refs_11_), channel_id=1, source_target_pairs={{0,16},{1,17},{2,18},{3,19},{4,20},{5,21},{6,22},{7,23},{8,24},{9,... | collective-permute-start | bytes 835592 | tf_op jit(solution)/shard_map/ppermute | solution.py:687
  88.9 15.9 %collective-permute-start.24 = (bf16[272,384]{1,0:T(8,128)(2,1)S(1)}, bf16[272,384]{1,0:T(8,128)(2,1)S(1)}, u32[]{:S(2)}, u32[]{:S(2)}) collective-permute-start(bf16[272,384]{1,0:T(8,128)(2,1)S(1)} %combine.8.refs_12_), channel_id=1, source_target_pairs={{0,16},{1,17},{2,18},{3,19},{4,20},{5,21},{6,22},{7,23},{8,24},{9,... | collective-permute-start | bytes 626696 | tf_op jit(solution)/shard_map/ppermute | solution.py:687
  93.7 12.2 %collective-permute-start.25 = (bf16[272,384]{1,0:T(8,128)(2,1)S(1)}, bf16[272,384]{1,0:T(8,128)(2,1)S(1)}, u32[]{:S(2)}, u32[]{:S(2)}) collective-permute-start(bf16[272,384]{1,0:T(8,128)(2,1)S(1)} %combine.9.refs_0_), channel_id=1, source_target_pairs={{0,16},{1,17},{2,18},{3,19},{4,20},{5,21},{6,22},{7,23},{8,24},{9,... | collective-permute-start | bytes 626696 | tf_op jit(solution)/shard_map/ppermute | solution.py:687
  95.0 12.7 %collective-permute-start.27 = (bf16[256,768]{1,0:T(8,128)(2,1)S(1)}, bf16[256,768]{1,0:T(8,128)(2,1)S(1)}, u32[]{:S(2)}, u32[]{:S(2)}) collective-permute-start(bf16[256,768]{1,0:T(8,128)(2,1)S(1)} %get-tuple-element.112), channel_id=1, source_target_pairs={{0,4},{1,5},{2,6},{3,7},{4,0},{5,1},{6,2},{7,3},{8,12},{9,13},{10,... | collective-permute-start | bytes 1179656 | tf_op jit(solution)/shard_map/ppermute | solution.py:687
  104.8 2.9 %collective-permute-start.26 = (bf16[256,512]{1,0:T(8,128)(2,1)S(1)}, bf16[256,512]{1,0:T(8,128)(2,1)S(1)}, u32[]{:S(2)}, u32[]{:S(2)}) collective-permute-start(bf16[256,512]{1,0:T(8,128)(2,1)S(1)} %get-tuple-element.111), channel_id=1, source_target_pairs={{0,4},{1,5},{2,6},{3,7},{4,0},{5,1},{6,2},{7,3},{8,12},{9,13},{10,... | collective-permute-start | bytes 786440 | tf_op jit(solution)/shard_map/ppermute | solution.py:687
  107.0 1.6 %collective-permute-start.29 = (bf16[256,384]{1,0:T(8,128)(2,1)S(1)}, bf16[256,384]{1,0:T(8,128)(2,1)S(1)}, u32[]{:S(2)}, u32[]{:S(2)}) collective-permute-start(bf16[256,384]{1,0:T(8,128)(2,1)S(1)} %get-tuple-element.114), channel_id=1, source_target_pairs={{0,4},{1,5},{2,6},{3,7},{4,0},{5,1},{6,2},{7,3},{8,12},{9,13},{10,... | collective-permute-start | bytes 589832 | tf_op jit(solution)/shard_map/ppermute | solution.py:687
  107.6 1.4 %collective-permute-start.28 = (bf16[256,384]{1,0:T(8,128)(2,1)S(1)}, bf16[256,384]{1,0:T(8,128)(2,1)S(1)}, u32[]{:S(2)}, u32[]{:S(2)}) collective-permute-start(bf16[256,384]{1,0:T(8,128)(2,1)S(1)} %get-tuple-element.113), channel_id=1, source_target_pairs={{0,4},{1,5},{2,6},{3,7},{4,0},{5,1},{6,2},{7,3},{8,12},{9,13},{10,... | collective-permute-start | bytes 589832 | tf_op jit(solution)/shard_map/ppermute | solution.py:687
  (6 other events, 71.6 us)

commit v14 on v13

--- a/solution.py
+++ b/solution.py
@@ -812,8 +812,8 @@
     state_of(0, [])
     combine_of(0, [])
     fourth_blocks = send_on(plan(3), sent[0])
-    message.append(travel(fourth_blocks))
-    state_of(1, [fourth_blocks[0], joined[0][0]])
+    message.append(travel(fourth_blocks[:1] + gate(fourth_blocks[1:], message[2][1:])))
+    state_of(1, joined[0])
     combine_of(1, [])
     state_of(2, joined[1])
     state_of(3, sent[2])

time: 111 us -> 111 us (level)
  the two profiles are of different devices: /device:TPU:19 before, /device:TPU:13 now
where the time goes in v14:
time: 111 us; the launch traced here: 110 us
  starting transfers between devices  40 us (36%)
  waiting for transfers between devices  36 us (32%)
  Pallas kernels  31.2 us (28%)
  local copies, waits for them, and re-layouts  1.86 us (2%)
    ppermute x30, starting transfers between devices, over(): lax.ppermute(block, axes, [(i, j) for i, j in route if j is not None and...  40 us
    ppermute x30, waiting for transfers between devices, over(): lax.ppermute(block, axes, [(i, j) for i, j in route if j is not None and...  36 us
    pallas_call x24, Pallas kernels, call(): pl.pallas_call(body, out_shape=shapes, in_specs=specs, out_specs=[vmem] *...  29.3 us
  transfers between devices with their start and end apart: 30, of which 13 were waited for; matrix products, arithmetic and copies ran while one was open for 0% of the time, Pallas kernels for 25%

profile of v14, /device:TPU:13, one launch (start us, length us, event | category | flops | bytes accessed | tf_op | source)
XLA Modules:
  0.0 109.6 jit_solution(6731333395684180779)
XLA Ops:
  0.1 1.7 %copy-done = bf16[64,20480]{1,0:T(8,128)(2,1)S(1)} copy-done((bf16[64,20480]{1,0:T(8,128)(2,1)S(1)}, bf16[64,20480]{1,0:T(8,128)(2,1)}, u32[]{:S(2)}) %copy-start) | copy-done | bytes 2621464
  2.8 1.3 %pack.1 = (bf16[64,8448]{1,0:T(8,128)(2,1)S(1)}, bf16[16,10240]{1,0:T(8,128)(2,1)S(1)}) custom-call(s32[5]{0:T(128)S(1)} %stack.23.place, bf16[64,20480]{1,0:T(8,128)(2,1)S(1)} %copy-done, bf16[64,256]{1,0:T(8,128)(2,1)S(1)} %copy-done.2, bf16[64,4096]{1,0:T(8,128)(2,1)S(1)} %pack_first.1.order), custom_call_target="tpu_custom_call" | custom-call | flops 1 | bytes 1 | tf_op jit(solution)/shard_map/pack/pallas_call | solution.py:662
  5.0 3.0 %collective-permute-done.got_first.got.edges = bf16[64,4096]{1,0:T(8,128)(2,1)S(1)} collective-permute-done((bf16[64,4096]{1,0:T(8,128)(2,1)S(1)}, bf16[64,4096]{1,0:T(8,128)(2,1)S(1)}, u32[]{:S(2)}, u32[]{:S(2)}) %collective-permute-start) | collective-permute-done | bytes 524320 | tf_op jit(solution)/shard_map/ppermute | solution.py:687
  9.7 4.8 %collective-permute-start.2 = (bf16[128,512]{1,0:T(8,128)(2,1)S(1)}, bf16[128,512]{1,0:T(8,128)(2,1)S(1)}, u32[]{:S(2)}, u32[]{:S(2)}) collective-permute-start(bf16[128,512]{1,0:T(8,128)(2,1)S(1)} %get-tuple-element.66), channel_id=1, source_target_pairs={{0,2},{1,3},{2,0},{3,1},{4,6},{5,7},{6,4},{7,5},{8,10},{9,11},{10,... | collective-permute-start | bytes 393224 | tf_op jit(solution)/shard_map/ppermute | solution.py:687
  15.6 1.3 %collective-permute-start.6 = (bf16[128,384]{1,0:T(8,128)(2,1)S(1)}, bf16[128,384]{1,0:T(8,128)(2,1)S(1)}, u32[]{:S(2)}, u32[]{:S(2)}) collective-permute-start(bf16[128,384]{1,0:T(8,128)(2,1)S(1)} %get-tuple-element.73), channel_id=1, source_target_pairs={{0,1},{1,0},{2,3},{3,2},{4,5},{5,4},{6,7},{7,6},{8,9},{9,8},{10,11... | collective-permute-start | bytes 294920 | tf_op jit(solution)/shard_map/ppermute | solution.py:687
  16.9 1.7 %collective-permute-start.7 = (bf16[128,384]{1,0:T(8,128)(2,1)S(1)}, bf16[128,384]{1,0:T(8,128)(2,1)S(1)}, u32[]{:S(2)}, u32[]{:S(2)}) collective-permute-start(bf16[128,384]{1,0:T(8,128)(2,1)S(1)} %get-tuple-element.74), channel_id=1, source_target_pairs={{0,2},{1,3},{2,0},{3,1},{4,6},{5,7},{6,4},{7,5},{8,10},{9,11},{10,... | collective-permute-start | bytes 294920 | tf_op jit(solution)/shard_map/ppermute | solution.py:687
  19.6 6.4 %collective-permute-done.2.refs_2_.refs_4_ = bf16[128,512]{1,0:T(8,128)(2,1)S(1)} collective-permute-done((bf16[128,512]{1,0:T(8,128)(2,1)S(1)}, bf16[128,512]{1,0:T(8,128)(2,1)S(1)}, u32[]{:S(2)}, u32[]{:S(2)}) %collective-permute-start.2) | collective-permute-done | bytes 131104 | tf_op jit(solution)/shard_map/ppermute | solution.py:687
  26.0 3.0 %collective-permute-done.3.refs_3_.refs_5_ = bf16[128,512]{1,0:T(8,128)(2,1)S(1)} collective-permute-done((bf16[128,512]{1,0:T(8,128)(2,1)S(1)}, bf16[128,512]{1,0:T(8,128)(2,1)S(1)}, u32[]{:S(2)}, u32[]{:S(2)}) %collective-permute-start.3) | collective-permute-done | bytes 131104 | tf_op jit(solution)/shard_map/ppermute | solution.py:687
  29.0 2.1 %collective-permute-done.7.refs_2_.refs_7_ = bf16[128,384]{1,0:T(8,128)(2,1)S(1)} collective-permute-done((bf16[128,384]{1,0:T(8,128)(2,1)S(1)}, bf16[128,384]{1,0:T(8,128)(2,1)S(1)}, u32[]{:S(2)}, u32[]{:S(2)}) %collective-permute-start.7) | collective-permute-done | bytes 98336 | tf_op jit(solution)/shard_map/ppermute | solution.py:687
  31.1 2.1 %collective-permute-done.8.refs_3_.refs_8_ = bf16[128,384]{1,0:T(8,128)(2,1)S(1)} collective-permute-done((bf16[128,384]{1,0:T(8,128)(2,1)S(1)}, bf16[128,384]{1,0:T(8,128)(2,1)S(1)}, u32[]{:S(2)}, u32[]{:S(2)}) %collective-permute-start.8) | collective-permute-done | bytes 98336 | tf_op jit(solution)/shard_map/ppermute | solution.py:687
  33.2 3.4 %collective-permute-start.13 = (bf16[128,768]{1,0:T(8,128)(2,1)S(1)}, bf16[128,768]{1,0:T(8,128)(2,1)S(1)}, u32[]{:S(2)}, u32[]{:S(2)}) collective-permute-start(bf16[128,768]{1,0:T(8,128)(2,1)S(1)} %get-tuple-element.92), channel_id=1, source_target_pairs={{0,2},{1,3},{2,0},{3,1},{4,6},{5,7},{6,4},{7,5},{8,10},{9,11},{10,... | collective-permute-start | bytes 589832 | tf_op jit(solution)/shard_map/ppermute | solution.py:687
  37.3 1.7 %prep.1 = (bf16[512,256]{1,0:T(8,128)(2,1)S(1)}, f32[4,2560]{1,0:T(4,128)S(1)}, f32[512,128]{1,0:T(8,128)S(1)}, f32[128,512]{1,0:T(8,128)S(1)}, bf16[512,256]{1,...) custom-call(s32[5]{0:T(128)S(1)} %stack.23.place, ...), custom_call_target="tpu_custom_call" | custom-call | flops 1 | bytes 1 | tf_op jit(solution)/shard_map/prep/pallas_call | solution.py:662
  39.0 2.1 %state.4 = (bf16[512,512]{1,0:T(8,128)(2,1)S(1)}, f32[256,512]{1,0:T(8,128)S(1)}, bf16[272,256]{1,0:T(8,128)(2,1)S(1)}, bf16[272,256]{1,0:T(8,128)(2,1)S(1)}) custom-call(s32[5]{0:T(128)S(1)} %stack.23.place, bf16[128,512]{1,0:T(8,128)(2,1)S(1)} %get-tuple-element.64.refs_0_, bf16[128,512]{1,0:T(8,128)(2,1)S(1)} %collective-permute-done.1.refs_1_.refs_3_, ...), custom_call_target="tpu_custom_call" | custom-call | flops 1 | bytes 1 | tf_op jit(solution)/shard_map/state/pallas_call | solution.py:662
  41.1 2.3 %collective-permute-start.10 = (bf16[272,256]{1,0:T(8,128)(2,1)S(1)}, bf16[272,256]{1,0:T(8,128)(2,1)S(1)}, u32[]{:S(2)}, u32[]{:S(2)}) collective-permute-start(bf16[272,256]{1,0:T(8,128)(2,1)S(1)} %get-tuple-element.82.refs_3_.refs_1_), channel_id=1, source_target_pairs={{0,8},{1,9},{2,10},{3,11},{4,12},{5,13},{6,14},{7,15},{8,0},{9,1},... | collective-permute-start | bytes 417800 | tf_op jit(solution)/shard_map/ppermute | solution.py:687
  45.6 3.0 %collective-permute-done.13.refs_4_.refs_2_ = bf16[128,768]{1,0:T(8,128)(2,1)S(1)} collective-permute-done((bf16[128,768]{1,0:T(8,128)(2,1)S(1)}, bf16[128,768]{1,0:T(8,128)(2,1)S(1)}, u32[]{:S(2)}, u32[]{:S(2)}) %collective-permute-start.13) | collective-permute-done | bytes 196640 | tf_op jit(solution)/shard_map/ppermute | solution.py:687
  48.6 4.2 %collective-permute-done.14.refs_5_.refs_3_ = bf16[128,768]{1,0:T(8,128)(2,1)S(1)} collective-permute-done((bf16[128,768]{1,0:T(8,128)(2,1)S(1)}, bf16[128,768]{1,0:T(8,128)(2,1)S(1)}, u32[]{:S(2)}, u32[]{:S(2)}) %collective-permute-start.14) | collective-permute-done | bytes 196640 | tf_op jit(solution)/shard_map/ppermute | solution.py:687
  52.8 3.4 %collective-permute-start.16 = (bf16[128,1024]{1,0:T(8,128)(2,1)S(1)}, bf16[128,1024]{1,0:T(8,128)(2,1)S(1)}, u32[]{:S(2)}, u32[]{:S(2)}) collective-permute-start(bf16[128,1024]{1,0:T(8,128)(2,1)S(1)} %get-tuple-element.95), channel_id=1, source_target_pairs={{0,2},{1,3},{2,0},{3,1},{4,6},{5,7},{6,4},{7,5},{8,10},{9,11},{10,... | collective-permute-start | bytes 786440 | tf_op jit(solution)/shard_map/ppermute | solution.py:687
  56.9 2.6 %state.5 = (bf16[512,768]{1,0:T(8,128)(2,1)S(1)}, f32[256,768]{1,0:T(8,128)S(1)}, bf16[272,384]{1,0:T(8,128)(2,1)S(1)}, bf16[272,384]{1,0:T(8,128)(2,1)S(1)}) custom-call(s32[5]{0:T(128)S(1)} %stack.23.place, bf16[128,768]{1,0:T(8,128)(2,1)S(1)} %get-tuple-element.76.refs_9_.refs_0_, bf16[128,768]{1,0:T(8,128)(2,1)S(1)} %collective-permute-done.12.refs_3_.refs_1_, ...), custom_call_target="tpu_custom_call" | custom-call | flops 1 | bytes 1 | tf_op jit(solution)/shard_map/state/pallas_call | solution.py:662
  59.5 2.4 %collective-permute-start.18 = (bf16[272,384]{1,0:T(8,128)(2,1)S(1)}, bf16[272,384]{1,0:T(8,128)(2,1)S(1)}, u32[]{:S(2)}, u32[]{:S(2)}) collective-permute-start(bf16[272,384]{1,0:T(8,128)(2,1)S(1)} %get-tuple-element.97.refs_1_), channel_id=1, source_target_pairs={{0,8},{1,9},{2,10},{3,11},{4,12},{5,13},{6,14},{7,15},{8,0},{9,1},... | collective-permute-start | bytes 626696 | tf_op jit(solution)/shard_map/ppermute | solution.py:687
  61.9 1.3 %collective-permute-start.19 = (bf16[272,384]{1,0:T(8,128)(2,1)S(1)}, bf16[272,384]{1,0:T(8,128)(2,1)S(1)}, u32[]{:S(2)}, u32[]{:S(2)}) collective-permute-start(bf16[272,384]{1,0:T(8,128)(2,1)S(1)} %get-tuple-element.98.refs_1_), channel_id=1, source_target_pairs={{0,8},{1,9},{2,10},{3,11},{4,12},{5,13},{6,14},{7,15},{8,0},{9,1},... | collective-permute-start | bytes 626696 | tf_op jit(solution)/shard_map/ppermute | solution.py:687
  63.2 1.4 %collective-permute-done.18.refs_0_ = bf16[272,384]{1,0:T(8,128)(2,1)S(1)} collective-permute-done((bf16[272,384]{1,0:T(8,128)(2,1)S(1)}, bf16[272,384]{1,0:T(8,128)(2,1)S(1)}, u32[]{:S(2)}, u32[]{:S(2)}) %collective-permute-start.18) | collective-permute-done | bytes 208928 | tf_op jit(solution)/shard_map/ppermute | solution.py:687
  66.6 2.2 %collective-permute-done.19.refs_0_.refs_1_ = bf16[272,384]{1,0:T(8,128)(2,1)S(1)} collective-permute-done((bf16[272,384]{1,0:T(8,128)(2,1)S(1)}, bf16[272,384]{1,0:T(8,128)(2,1)S(1)}, u32[]{:S(2)}, u32[]{:S(2)}) %collective-permute-start.19) | collective-permute-done | bytes 208928 | tf_op jit(solution)/shard_map/ppermute | solution.py:687
  70.8 6.6 %collective-permute-done.17.refs_3_ = bf16[128,1024]{1,0:T(8,128)(2,1)S(1)} collective-permute-done((bf16[128,1024]{1,0:T(8,128)(2,1)S(1)}, bf16[128,1024]{1,0:T(8,128)(2,1)S(1)}, u32[]{:S(2)}, u32[]{:S(2)}) %collective-permute-start.17) | collective-permute-done | bytes 262176 | tf_op jit(solution)/shard_map/ppermute | solution.py:687
  77.4 1.9 %state.6 = (bf16[512,384]{1,0:T(8,128)(2,1)S(1)}, f32[256,384]{1,0:T(8,128)S(1)}, bf16[272,384]{1,0:T(8,128)(2,1)S(1)}) custom-call(s32[5]{0:T(128)S(1)} %stack.23.place, bf16[128,1024]{1,0:T(8,128)(2,1)S(1)} %get-tuple-element.84.refs_0_, bf16[128,1024]{1,0:T(8,128)(2,1)S(1)} %collective-permute-done.15.refs_1_, ...), custom_call_target="tpu_custom_call" | custom-call | flops 1 | bytes 1 | tf_op jit(solution)/shard_map/state/pallas_call | solution.py:662
  79.3 2.4 %collective-permute-start.23 = (bf16[272,384]{1,0:T(8,128)(2,1)S(1)}, bf16[272,384]{1,0:T(8,128)(2,1)S(1)}, u32[]{:S(2)}, u32[]{:S(2)}) collective-permute-start(bf16[272,384]{1,0:T(8,128)(2,1)S(1)} %get-tuple-element.99.refs_10_.refs_1_), channel_id=1, source_target_pairs={{0,8},{1,9},{2,10},{3,11},{4,12},{5,13},{6,14},{7,15},{8,0},{9,1},... | collective-permute-start | bytes 626696 | tf_op jit(solution)/shard_map/ppermute | solution.py:687
  81.7 1.9 %state.7 = (bf16[512,384]{1,0:T(8,128)(2,1)S(1)}, f32[256,384]{1,0:T(8,128)S(1)}, bf16[272,384]{1,0:T(8,128)(2,1)S(1)}) custom-call(s32[5]{0:T(128)S(1)} %stack.23.place, bf16[128,1024]{1,0:T(8,128)(2,1)S(1)} %get-tuple-element.84.refs_0_, bf16[128,1024]{1,0:T(8,128)(2,1)S(1)} %collective-permute-done.15.refs_1_, ...), custom_call_target="tpu_custom_call" | custom-call | flops 1 | bytes 1 | tf_op jit(solution)/shard_map/state/pallas_call | solution.py:662
  88.1 1.5 %collective-permute-start.24 = (bf16[272,384]{1,0:T(8,128)(2,1)S(1)}, bf16[272,384]{1,0:T(8,128)(2,1)S(1)}, u32[]{:S(2)}, u32[]{:S(2)}) collective-permute-start(bf16[272,384]{1,0:T(8,128)(2,1)S(1)} %combine.8.refs_12_), channel_id=1, source_target_pairs={{0,16},{1,17},{2,18},{3,19},{4,20},{5,21},{6,22},{7,23},{8,24},{9,... | collective-permute-start | bytes 626696 | tf_op jit(solution)/shard_map/ppermute | solution.py:687
  89.6 2.6 %final.4 = (bf16[256,768]{1,0:T(8,128)(2,1)S(1)}, bf16[256,768]{1,0:T(8,128)(2,1)S(1)}) custom-call(s32[5]{0:T(128)S(1)} %stack.23.place, bf16[272,384]{1,0:T(8,128)(2,1)S(1)} %collective-permute-done.18.refs_0_, bf16[272,384]{1,0:T(8,128)(2,1)S(1)} %collective-permute-done.19.refs_0_.refs_1_, bf16[272,384]{1,0:T(8,128)(2,1)S(1)} %collective-permute-done.20.refs_9_.refs_2_, ...), custom_call_target="tpu_custom_call" | custom-call | flops 1 | bytes 1 | tf_op jit(solution)/shard_map/final/pallas_call | solution.py:662
  94.1 2.6 %collective-permute-start.27 = (bf16[256,768]{1,0:T(8,128)(2,1)S(1)}, bf16[256,768]{1,0:T(8,128)(2,1)S(1)}, u32[]{:S(2)}, u32[]{:S(2)}) collective-permute-start(bf16[256,768]{1,0:T(8,128)(2,1)S(1)} %get-tuple-element.118), channel_id=1, source_target_pairs={{0,4},{1,5},{2,6},{3,7},{4,0},{5,1},{6,2},{7,3},{8,12},{9,13},{10,... | collective-permute-start | bytes 1179656 | tf_op jit(solution)/shard_map/ppermute | solution.py:687
  98.3 1.9 %final.5 = (bf16[256,512]{1,0:T(8,128)(2,1)S(1)}, bf16[256,512]{1,0:T(8,128)(2,1)S(1)}) custom-call(s32[5]{0:T(128)S(1)} %stack.23.place, bf16[272,256]{1,0:T(8,128)(2,1)S(1)} %collective-permute-done.9.refs_0_, bf16[272,256]{1,0:T(8,128)(2,1)S(1)} %collective-permute-done.10.refs_1_, bf16[272,512]{1,0:T(8,128)(2,1)S(1)} %collective-permute-done.11.refs_2_, ...), custom_call_target="tpu_custom_call" | custom-call | flops 1 | bytes 1 | tf_op jit(solution)/shard_map/final/pallas_call | solution.py:662
  103.1 2.9 %collective-permute-start.29 = (bf16[256,384]{1,0:T(8,128)(2,1)S(1)}, bf16[256,384]{1,0:T(8,128)(2,1)S(1)}, u32[]{:S(2)}, u32[]{:S(2)}) collective-permute-start(bf16[256,384]{1,0:T(8,128)(2,1)S(1)} %get-tuple-element.120), channel_id=1, source_target_pairs={{0,4},{1,5},{2,6},{3,7},{4,0},{5,1},{6,2},{7,3},{8,12},{9,13},{10,... | collective-permute-start | bytes 589832 | tf_op jit(solution)/shard_map/ppermute | solution.py:687
  107.5 1.9 %place.1 = bf16[256,4096]{1,0:T(8,128)(2,1)} custom-call(s32[5]{0:T(128)S(1)} %stack.23.place, bf16[256,512]{1,0:T(8,128)(2,1)S(1)} %get-tuple-element.112.refs_6_.refs_0_, bf16[256,768]{1,0:T(8,128)(2,1)S(1)} %get-tuple-element.111.refs_2_.refs_1_, bf16[256,384]{1,0:T(8,128)(2,1)S(1)} %get-tuple-element.114.refs_6_.refs_2_, ...), custom_call_target="tpu_custom_call" | custom-call | flops 1 | bytes 1 | tf_op jit(solution)/shard_map/place/pallas_call | solution.py:624
  (72 shorter events, 25.4 us)
Async XLA Ops:
  4.1 10.4 %collective-permute-start.4 = (bf16[64,8448]{1,0:T(8,128)(2,1)S(1)}, bf16[64,8448]{1,0:T(8,128)(2,1)S(1)}, u32[]{:S(2)}, u32[]{:S(2)}) collective-permute-start(bf16[64,8448]{1,0:T(8,128)(2,1)S(1)} %get-tuple-element.68), channel_id=1, source_target_pairs={{0,4},{1,5},{2,6},{3,7},{4,0},{5,1},{6,2},{7,3},{8,12},{9,13},{10,... | collective-permute-start | bytes 3244040 | tf_op jit(solution)/shard_map/ppermute | solution.py:687
  4.9 3.1 %collective-permute-start = (bf16[64,4096]{1,0:T(8,128)(2,1)S(1)}, bf16[64,4096]{1,0:T(8,128)(2,1)S(1)}, u32[]{:S(2)}, u32[]{:S(2)}) collective-permute-start(bf16[64,4096]{1,0:T(8,128)(2,1)S(1)} %pack_first.1.order), channel_id=1, source_target_pairs={{0,4},{1,5},{2,6},{3,7},{4,0},{5,1},{6,2},{7,3},{8,12},{9,13},{10,... | collective-permute-start | bytes 1572872 | tf_op jit(solution)/shard_map/ppermute | solution.py:687
  8.8 9.8 %collective-permute-start.1 = (bf16[128,512]{1,0:T(8,128)(2,1)S(1)}, bf16[128,512]{1,0:T(8,128)(2,1)S(1)}, u32[]{:S(2)}, u32[]{:S(2)}) collective-permute-start(bf16[128,512]{1,0:T(8,128)(2,1)S(1)} %get-tuple-element.65), channel_id=1, source_target_pairs={{0,1},{1,0},{2,3},{3,2},{4,5},{5,4},{6,7},{7,6},{8,9},{9,8},{10,11... | collective-permute-start | bytes 393224 | tf_op jit(solution)/shard_map/ppermute | solution.py:687
  9.0 5.5 %collective-permute-start.5 = (bf16[3,10240]{1,0:T(4,128)(2,1)S(1)}, bf16[3,10240]{1,0:T(4,128)(2,1)S(1)}, u32[]{:S(2)}, u32[]{:S(2)}) collective-permute-start(bf16[3,10240]{1,0:T(4,128)(2,1)S(1)} %get-tuple-element.71), channel_id=1, source_target_pairs={{3,11},{7,15},{11,19},{15,23},{19,27},{23,31}} | collective-permute-start | bytes 184328 | tf_op jit(solution)/shard_map/ppermute | solution.py:687
  9.7 16.3 %collective-permute-start.2 = (bf16[128,512]{1,0:T(8,128)(2,1)S(1)}, bf16[128,512]{1,0:T(8,128)(2,1)S(1)}, u32[]{:S(2)}, u32[]{:S(2)}) collective-permute-start(bf16[128,512]{1,0:T(8,128)(2,1)S(1)} %get-tuple-element.66), channel_id=1, source_target_pairs={{0,2},{1,3},{2,0},{3,1},{4,6},{5,7},{6,4},{7,5},{8,10},{9,11},{10,... | collective-permute-start | bytes 393224 | tf_op jit(solution)/shard_map/ppermute | solution.py:687
  14.5 14.5 %collective-permute-start.3 = (bf16[128,512]{1,0:T(8,128)(2,1)S(1)}, bf16[128,512]{1,0:T(8,128)(2,1)S(1)}, u32[]{:S(2)}, u32[]{:S(2)}) collective-permute-start(bf16[128,512]{1,0:T(8,128)(2,1)S(1)} %get-tuple-element.67), channel_id=1, source_target_pairs={{0,3},{1,2},{2,1},{3,0},{4,7},{5,6},{6,5},{7,4},{8,11},{9,10},{10,... | collective-permute-start | bytes 393224 | tf_op jit(solution)/shard_map/ppermute | solution.py:687
  15.6 13.4 %collective-permute-start.6 = (bf16[128,384]{1,0:T(8,128)(2,1)S(1)}, bf16[128,384]{1,0:T(8,128)(2,1)S(1)}, u32[]{:S(2)}, u32[]{:S(2)}) collective-permute-start(bf16[128,384]{1,0:T(8,128)(2,1)S(1)} %get-tuple-element.73), channel_id=1, source_target_pairs={{0,1},{1,0},{2,3},{3,2},{4,5},{5,4},{6,7},{7,6},{8,9},{9,8},{10,11... | collective-permute-start | bytes 294920 | tf_op jit(solution)/shard_map/ppermute | solution.py:687
  16.9 14.2 %collective-permute-start.7 = (bf16[128,384]{1,0:T(8,128)(2,1)S(1)}, bf16[128,384]{1,0:T(8,128)(2,1)S(1)}, u32[]{:S(2)}, u32[]{:S(2)}) collective-permute-start(bf16[128,384]{1,0:T(8,128)(2,1)S(1)} %get-tuple-element.74), channel_id=1, source_target_pairs={{0,2},{1,3},{2,0},{3,1},{4,6},{5,7},{6,4},{7,5},{8,10},{9,11},{10,... | collective-permute-start | bytes 294920 | tf_op jit(solution)/shard_map/ppermute | solution.py:687
  18.6 14.6 %collective-permute-start.8 = (bf16[128,384]{1,0:T(8,128)(2,1)S(1)}, bf16[128,384]{1,0:T(8,128)(2,1)S(1)}, u32[]{:S(2)}, u32[]{:S(2)}) collective-permute-start(bf16[128,384]{1,0:T(8,128)(2,1)S(1)} %get-tuple-element.75), channel_id=1, source_target_pairs={{0,3},{1,2},{2,1},{3,0},{4,7},{5,6},{6,5},{7,4},{8,11},{9,10},{10,... | collective-permute-start | bytes 294920 | tf_op jit(solution)/shard_map/ppermute | solution.py:687
  18.8 17.8 %copy-start.3 = (f32[4,20480]{1,0:T(4,128)S(1)}, f32[4,20480]{1,0:T(4,128)}, u32[]{:S(2)}) copy-start(f32[4,20480]{1,0:T(4,128)} %weight.1) | copy-start | bytes 983044
  18.8 17.8 %copy-start.4 = (f32[20480]{0:T(1024)S(1)}, f32[20480]{0:T(1024)}, u32[]{:S(2)}) copy-start(f32[20480]{0:T(1024)} %param.10) | copy-start | bytes 245764
  33.2 12.4 %collective-permute-start.12 = (bf16[128,768]{1,0:T(8,128)(2,1)S(1)}, bf16[128,768]{1,0:T(8,128)(2,1)S(1)}, u32[]{:S(2)}, u32[]{:S(2)}) collective-permute-start(bf16[128,768]{1,0:T(8,128)(2,1)S(1)} %get-tuple-element.91), channel_id=1, source_target_pairs={{0,1},{1,0},{2,3},{3,2},{4,5},{5,4},{6,7},{7,6},{8,9},{9,8},{10,11... | collective-permute-start | bytes 589832 | tf_op jit(solution)/shard_map/ppermute | solution.py:687
  33.2 15.4 %collective-permute-start.13 = (bf16[128,768]{1,0:T(8,128)(2,1)S(1)}, bf16[128,768]{1,0:T(8,128)(2,1)S(1)}, u32[]{:S(2)}, u32[]{:S(2)}) collective-permute-start(bf16[128,768]{1,0:T(8,128)(2,1)S(1)} %get-tuple-element.92), channel_id=1, source_target_pairs={{0,2},{1,3},{2,0},{3,1},{4,6},{5,7},{6,4},{7,5},{8,10},{9,11},{10,... | collective-permute-start | bytes 589832 | tf_op jit(solution)/shard_map/ppermute | solution.py:687
  36.6 16.3 %collective-permute-start.14 = (bf16[128,768]{1,0:T(8,128)(2,1)S(1)}, bf16[128,768]{1,0:T(8,128)(2,1)S(1)}, u32[]{:S(2)}, u32[]{:S(2)}) collective-permute-start(bf16[128,768]{1,0:T(8,128)(2,1)S(1)} %get-tuple-element.93), channel_id=1, source_target_pairs={{0,3},{1,2},{2,1},{3,0},{4,7},{5,6},{6,5},{7,4},{8,11},{9,10},{10,... | collective-permute-start | bytes 589832 | tf_op jit(solution)/shard_map/ppermute | solution.py:687
  41.1 15.2 %collective-permute-start.10 = (bf16[272,256]{1,0:T(8,128)(2,1)S(1)}, bf16[272,256]{1,0:T(8,128)(2,1)S(1)}, u32[]{:S(2)}, u32[]{:S(2)}) collective-permute-start(bf16[272,256]{1,0:T(8,128)(2,1)S(1)} %get-tuple-element.82.refs_3_.refs_1_), channel_id=1, source_target_pairs={{0,8},{1,9},{2,10},{3,11},{4,12},{5,13},{6,14},{7,15},{8,0},{9,1},... | collective-permute-start | bytes 417800 | tf_op jit(solution)/shard_map/ppermute | solution.py:687
  43.4 12.8 %collective-permute-start.9 = (bf16[272,256]{1,0:T(8,128)(2,1)S(1)}, bf16[272,256]{1,0:T(8,128)(2,1)S(1)}, u32[]{:S(2)}, u32[]{:S(2)}) collective-permute-start(bf16[272,256]{1,0:T(8,128)(2,1)S(1)} %get-tuple-element.81.refs_2_.refs_0_), channel_id=1, source_target_pairs={{0,8},{1,9},{2,10},{3,11},{4,12},{5,13},{6,14},{7,15},{8,0},{9,1},... | collective-permute-start | bytes 417800 | tf_op jit(solution)/shard_map/ppermute | solution.py:687
  52.8 17.9 %collective-permute-start.15 = (bf16[128,1024]{1,0:T(8,128)(2,1)S(1)}, bf16[128,1024]{1,0:T(8,128)(2,1)S(1)}, u32[]{:S(2)}, u32[]{:S(2)}) collective-permute-start(bf16[128,1024]{1,0:T(8,128)(2,1)S(1)} %get-tuple-element.94), channel_id=1, source_target_pairs={{0,1},{1,0},{2,3},{3,2},{4,5},{5,4},{6,7},{7,6},{8,9},{9,8},{10,11... | collective-permute-start | bytes 786440 | tf_op jit(solution)/shard_map/ppermute | solution.py:687
  52.8 18.0 %collective-permute-start.16 = (bf16[128,1024]{1,0:T(8,128)(2,1)S(1)}, bf16[128,1024]{1,0:T(8,128)(2,1)S(1)}, u32[]{:S(2)}, u32[]{:S(2)}) collective-permute-start(bf16[128,1024]{1,0:T(8,128)(2,1)S(1)} %get-tuple-element.95), channel_id=1, source_target_pairs={{0,2},{1,3},{2,0},{3,1},{4,6},{5,7},{6,4},{7,5},{8,10},{9,11},{10,... | collective-permute-start | bytes 786440 | tf_op jit(solution)/shard_map/ppermute | solution.py:687
  56.2 21.2 %collective-permute-start.17 = (bf16[128,1024]{1,0:T(8,128)(2,1)S(1)}, bf16[128,1024]{1,0:T(8,128)(2,1)S(1)}, u32[]{:S(2)}, u32[]{:S(2)}) collective-permute-start(bf16[128,1024]{1,0:T(8,128)(2,1)S(1)} %get-tuple-element.96), channel_id=1, source_target_pairs={{0,3},{1,2},{2,1},{3,0},{4,7},{5,6},{6,5},{7,4},{8,11},{9,10},{10,... | collective-permute-start | bytes 786440 | tf_op jit(solution)/shard_map/ppermute | solution.py:687
  59.5 5.1 %collective-permute-start.18 = (bf16[272,384]{1,0:T(8,128)(2,1)S(1)}, bf16[272,384]{1,0:T(8,128)(2,1)S(1)}, u32[]{:S(2)}, u32[]{:S(2)}) collective-permute-start(bf16[272,384]{1,0:T(8,128)(2,1)S(1)} %get-tuple-element.97.refs_1_), channel_id=1, source_target_pairs={{0,8},{1,9},{2,10},{3,11},{4,12},{5,13},{6,14},{7,15},{8,0},{9,1},... | collective-permute-start | bytes 626696 | tf_op jit(solution)/shard_map/ppermute | solution.py:687
  61.9 6.9 %collective-permute-start.19 = (bf16[272,384]{1,0:T(8,128)(2,1)S(1)}, bf16[272,384]{1,0:T(8,128)(2,1)S(1)}, u32[]{:S(2)}, u32[]{:S(2)}) collective-permute-start(bf16[272,384]{1,0:T(8,128)(2,1)S(1)} %get-tuple-element.98.refs_1_), channel_id=1, source_target_pairs={{0,8},{1,9},{2,10},{3,11},{4,12},{5,13},{6,14},{7,15},{8,0},{9,1},... | collective-permute-start | bytes 626696 | tf_op jit(solution)/shard_map/ppermute | solution.py:687
  65.3 21.0 %collective-permute-start.20 = (bf16[272,384]{1,0:T(8,128)(2,1)S(1)}, bf16[272,384]{1,0:T(8,128)(2,1)S(1)}, u32[]{:S(2)}, u32[]{:S(2)}) collective-permute-start(bf16[272,384]{1,0:T(8,128)(2,1)S(1)} %combine.6.refs_2_.refs_10_), channel_id=1, source_target_pairs={{0,16},{1,17},{2,18},{3,19},{4,20},{5,21},{6,22},{7,23},{8,24},{9,... | collective-permute-start | bytes 626696 | tf_op jit(solution)/shard_map/ppermute | solution.py:687
  69.5 16.8 %collective-permute-start.21 = (bf16[272,384]{1,0:T(8,128)(2,1)S(1)}, bf16[272,384]{1,0:T(8,128)(2,1)S(1)}, u32[]{:S(2)}, u32[]{:S(2)}) collective-permute-start(bf16[272,384]{1,0:T(8,128)(2,1)S(1)} %combine.7.refs_11_), channel_id=1, source_target_pairs={{0,16},{1,17},{2,18},{3,19},{4,20},{5,21},{6,22},{7,23},{8,24},{9,... | collective-permute-start | bytes 626696 | tf_op jit(solution)/shard_map/ppermute | solution.py:687
  79.3 8.1 %collective-permute-start.23 = (bf16[272,384]{1,0:T(8,128)(2,1)S(1)}, bf16[272,384]{1,0:T(8,128)(2,1)S(1)}, u32[]{:S(2)}, u32[]{:S(2)}) collective-permute-start(bf16[272,384]{1,0:T(8,128)(2,1)S(1)} %get-tuple-element.99.refs_10_.refs_1_), channel_id=1, source_target_pairs={{0,8},{1,9},{2,10},{3,11},{4,12},{5,13},{6,14},{7,15},{8,0},{9,1},... | collective-permute-start | bytes 626696 | tf_op jit(solution)/shard_map/ppermute | solution.py:687
  83.6 8.5 %collective-permute-start.22 = (bf16[272,384]{1,0:T(8,128)(2,1)S(1)}, bf16[272,384]{1,0:T(8,128)(2,1)S(1)}, u32[]{:S(2)}, u32[]{:S(2)}) collective-permute-start(bf16[272,384]{1,0:T(8,128)(2,1)S(1)} %get-tuple-element.100.refs_8_.refs_1_), channel_id=1, source_target_pairs={{0,8},{1,9},{2,10},{3,11},{4,12},{5,13},{6,14},{7,15},{8,0},{9,1},... | collective-permute-start | bytes 626696 | tf_op jit(solution)/shard_map/ppermute | solution.py:687
  85.0 13.3 %collective-permute-start.11 = (bf16[272,512]{1,0:T(8,128)(2,1)S(1)}, bf16[272,512]{1,0:T(8,128)(2,1)S(1)}, u32[]{:S(2)}, u32[]{:S(2)}) collective-permute-start(bf16[272,512]{1,0:T(8,128)(2,1)S(1)} %combine.5.refs_10_), channel_id=1, source_target_pairs={{0,16},{1,17},{2,18},{3,19},{4,20},{5,21},{6,22},{7,23},{8,24},{9,... | collective-permute-start | bytes 835592 | tf_op jit(solution)/shard_map/ppermute | solution.py:687
  88.1 12.3 %collective-permute-start.24 = (bf16[272,384]{1,0:T(8,128)(2,1)S(1)}, bf16[272,384]{1,0:T(8,128)(2,1)S(1)}, u32[]{:S(2)}, u32[]{:S(2)}) collective-permute-start(bf16[272,384]{1,0:T(8,128)(2,1)S(1)} %combine.8.refs_12_), channel_id=1, source_target_pairs={{0,16},{1,17},{2,18},{3,19},{4,20},{5,21},{6,22},{7,23},{8,24},{9,... | collective-permute-start | bytes 626696 | tf_op jit(solution)/shard_map/ppermute | solution.py:687
  92.8 9.2 %collective-permute-start.25 = (bf16[272,384]{1,0:T(8,128)(2,1)S(1)}, bf16[272,384]{1,0:T(8,128)(2,1)S(1)}, u32[]{:S(2)}, u32[]{:S(2)}) collective-permute-start(bf16[272,384]{1,0:T(8,128)(2,1)S(1)} %combine.9.refs_0_), channel_id=1, source_target_pairs={{0,16},{1,17},{2,18},{3,19},{4,20},{5,21},{6,22},{7,23},{8,24},{9,... | collective-permute-start | bytes 626696 | tf_op jit(solution)/shard_map/ppermute | solution.py:687
  94.1 12.0 %collective-permute-start.27 = (bf16[256,768]{1,0:T(8,128)(2,1)S(1)}, bf16[256,768]{1,0:T(8,128)(2,1)S(1)}, u32[]{:S(2)}, u32[]{:S(2)}) collective-permute-start(bf16[256,768]{1,0:T(8,128)(2,1)S(1)} %get-tuple-element.118), channel_id=1, source_target_pairs={{0,4},{1,5},{2,6},{3,7},{4,0},{5,1},{6,2},{7,3},{8,12},{9,13},{10,... | collective-permute-start | bytes 1179656 | tf_op jit(solution)/shard_map/ppermute | solution.py:687
  100.2 5.9 %collective-permute-start.26 = (bf16[256,512]{1,0:T(8,128)(2,1)S(1)}, bf16[256,512]{1,0:T(8,128)(2,1)S(1)}, u32[]{:S(2)}, u32[]{:S(2)}) collective-permute-start(bf16[256,512]{1,0:T(8,128)(2,1)S(1)} %get-tuple-element.117), channel_id=1, source_target_pairs={{0,4},{1,5},{2,6},{3,7},{4,0},{5,1},{6,2},{7,3},{8,12},{9,13},{10,... | collective-permute-start | bytes 786440 | tf_op jit(solution)/shard_map/ppermute | solution.py:687
  103.1 4.0 %collective-permute-start.29 = (bf16[256,384]{1,0:T(8,128)(2,1)S(1)}, bf16[256,384]{1,0:T(8,128)(2,1)S(1)}, u32[]{:S(2)}, u32[]{:S(2)}) collective-permute-start(bf16[256,384]{1,0:T(8,128)(2,1)S(1)} %get-tuple-element.120), channel_id=1, source_target_pairs={{0,4},{1,5},{2,6},{3,7},{4,0},{5,1},{6,2},{7,3},{8,12},{9,13},{10,... | collective-permute-start | bytes 589832 | tf_op jit(solution)/shard_map/ppermute | solution.py:687
  106.0 1.4 %collective-permute-start.28 = (bf16[256,384]{1,0:T(8,128)(2,1)S(1)}, bf16[256,384]{1,0:T(8,128)(2,1)S(1)}, u32[]{:S(2)}, u32[]{:S(2)}) collective-permute-start(bf16[256,384]{1,0:T(8,128)(2,1)S(1)} %get-tuple-element.119), channel_id=1, source_target_pairs={{0,4},{1,5},{2,6},{3,7},{4,0},{5,1},{6,2},{7,3},{8,12},{9,13},{10,... | collective-permute-start | bytes 589832 | tf_op jit(solution)/shard_map/ppermute | solution.py:687
  (6 other events, 69.1 us)

commit v15 on v14

--- a/solution.py
+++ b/solution.py
@@ -164,9 +164,9 @@
 LOG2E = 1.4426950408889634
 F32, BF16 = jnp.float32, jnp.bfloat16
 WIDTHS = (512, 0, 768, 768)
-RESTS = ("", "BD", "", "C")
+RESTS = ("", "BD", "C", "")
 GROUPED = ((0, 0, 512), (2, 0, 768), (3, 0, 384), (3, 384, 384))
-FIRST_ROUND = ((256, 256), (384, 384), (384,), (384,))
+FIRST_ROUND = ((256, 256), (256, 256, 256), (384,), (384,))
 SECOND_ROUND = ((512,), (384, 384), (384,), (384,))
 
 
@@ -353,7 +353,7 @@
 
 
 def view(refs, piece):
-    return [(ref, 0) for ref in refs]
+    return [(ref, total_of(2) if piece == 3 and r == 1 else 0) for r, ref in enumerate(refs)]
 
 
 def convolve_in_order(place, blocks, columns, edge, tap, bias, wide, put):
@@ -437,8 +437,8 @@
 def score_kernel(shards, place, *refs):
     blocks, refs = refs[:shards], refs[shards:]
     taps, offset, edge_ref, b_ref, c_ref, score_ref, wide = (*refs[:4], *refs[-3:])
-    blocks = view(blocks, 3)
-    start = WIDTHS[3]
+    blocks = view(blocks, 2)
+    start = WIDTHS[2]
     at = slice(PER_GROUP + STATE, PER_GROUP + 2 * STATE)
 
     def put(start, count, value):
@@ -500,14 +500,15 @@
         start = at.stop
 
 
-def combine_kernel(count, place, *refs):
+def combine_kernel(spans, place, *refs):
+    count = len(spans)
     got, own, out_ref = refs[:count], refs[count : 2 * count], refs[-1]
     odd = place[1] % 2 == 1
     start = 0
-    for got_ref, own_ref in zip(got, own):
-        at = slice(start, start + own_ref.shape[1])
-        theirs, mine = got_ref[:STATE].astype(F32), own_ref[:STATE].astype(F32)
-        decay, other = decay_of(own_ref), decay_of(got_ref)
+    for got_ref, own_ref, span in zip(got, own, spans):
+        at = slice(start, start + span.stop - span.start)
+        theirs, mine = got_ref[:STATE, span].astype(F32), own_ref[:STATE, span].astype(F32)
+        decay, other = decay_of(own_ref.at[:, span]), decay_of(got_ref.at[:, span])
         early, late = jnp.where(odd, theirs, mine), jnp.where(odd, mine, theirs)
         out_ref[:STATE, at] = (jnp.where(odd, decay, other) * early + late).astype(BF16)
         put_decay(out_ref.at[:, at], decay * other)
@@ -746,7 +747,8 @@
     edges = over(edges, lambda i: i + peers if i % shards == shards - 1 else None)
     second_blocks = send_on(plan(1), [first_blocks[0]], None, edges)
     message.append(travel(second_blocks))
-    third_blocks = send_on(plan(2), [second_blocks[0]])
+    third_plan = [(r, (2, 3) if r == 1 else (2,)) for r in range(shards)]
+    third_blocks = send_on(third_plan, [second_blocks[0]])
     message.append(travel(third_blocks[:1] + gate(third_blocks[1:], message[0][1:] + message[1][1:])))
 
     def seen(piece):
@@ -787,11 +789,19 @@
 
     def combine_of(i, order):
         joined[i], before[i] = [], []
-        step = len(FIRST_ROUND[i]) // len(SECOND_ROUND[i])
-        for j, width in enumerate(SECOND_ROUND[i]):
-            early, late = last[i][j * step : (j + 1) * step], sent[i][j * step : (j + 1) * step]
+        end = 0
+        for width in SECOND_ROUND[i]:
+            begin, end = end, end + width
+            early, late, spans, first = [], [], [], 0
+            for got, mine, size_of in zip(last[i], sent[i], FIRST_ROUND[i]):
+                low, high = max(begin - first, 0), min(end - first, size_of)
+                first += size_of
+                if low < high:
+                    early.append(got)
+                    late.append(mine)
+                    spans.append(slice(low, high))
             (total,) = call(
-                functools.partial(combine_kernel, len(early)),
+                functools.partial(combine_kernel, spans),
                 [((STATE + 16, width), BF16)],
                 [place] + early + late + [Stay(o) for o in order],
                 name="combine",
@@ -809,44 +819,43 @@
             **more,
         )
 
+    partial = [None] * count
+
+    def local_of(i, order):
+        (partial[i],) = call(
+            functools.partial(local_kernel, first_head(i)),
+            [(x[i].shape, F32)],
+            [x[i], cum, row, score, skip] + [Stay(o) for o in order],
+            name="local",
+        )
+
     state_of(0, [])
+    own_block, *fourth_blocks = send_on([(r, (3,)) for r in range(shards) if r != 1], sent[0])
+    fourth_blocks = gate(fourth_blocks, message[2][1:])
+    fourth_blocks = [over(block, lambda i, r=r: i ^ r) for r, block in enumerate(fourth_blocks, 2)]
+    message.append([own_block, message[2][1], *fourth_blocks])
     combine_of(0, [])
-    fourth_blocks = send_on(plan(3), sent[0])
-    message.append(travel(fourth_blocks[:1] + gate(fourth_blocks[1:], message[2][1:])))
     state_of(1, joined[0])
-    combine_of(1, [])
-    state_of(2, joined[1])
-    state_of(3, sent[2])
     c, score = call(
         functools.partial(score_kernel, shards),
         [((slab, STATE), BF16), ((slab, BLOCK), F32)],
-        [place] + seen(3) + [taps, offset, edge, b] + [Stay(o) for o in sent[3] + before[1]],
+        [place] + seen(2) + [taps, offset, edge, b] + [Stay(o) for o in sent[1]],
         scratch=[pltpu.VMEM((slab + 8, STATE), F32)],
         name="score",
     )
-    mixes = [cum, row, score, skip]
-
-    def in_full(i, order):
-        wide = [pltpu.VMEM((slab, GROUPED[i][2]), F32)]
-        finish_of(finish_kernel, i, [x[i]] + mixes, order, scratch=wide)
-
-    combine_of(2, [score])
-    in_full(1, joined[2])
-    combine_of(3, [keep[1]])
-    order, partial = joined[3][0], {}
-    for i in (2, 3):
-        (partial[i],) = call(
-            functools.partial(local_kernel, first_head(i)),
-            [(x[i].shape, F32)],
-            [x[i]] + mixes + [Stay(order)],
-            name="local",
-        )
-        order = partial[i]
-    in_full(0, [order])
-    order = keep[0]
-    for i in (2, 3):
-        finish_of(final_kernel, i, [partial[i]], [order])
-        order = keep[i]
+    local_of(0, [])
+    combine_of(1, [partial[0]])
+    local_of(1, joined[1])
+    state_of(2, [partial[1]])
+    state_of(3, sent[2])
+    finish_of(final_kernel, 1, [partial[1]], sent[3])
+    combine_of(2, [keep[1]])
+    combine_of(3, joined[2])
+    local_of(2, joined[3])
+    local_of(3, [partial[2]])
+    finish_of(final_kernel, 0, [partial[0]], [partial[3]])
+    finish_of(final_kernel, 2, [partial[2]], [keep[0]])
+    finish_of(final_kernel, 3, [partial[3]], [keep[2]])
     firsts = [first_head(i) * HEAD_DIM for i in range(count)]
     return put_in_place(firsts, (BLOCK, PAIR * PER_GROUP), place, keep, [swap(o) for o in send])
 

time: 111 us -> 114 us (1.027)
  starting transfers between devices: 40 us -> 46.2 us
  waiting for transfers between devices: 36 us -> 32.8 us
    ppermute x30, starting transfers between devices: 40 us -> 46.2 us  [over(): lax.ppermute(block, axes, [(i, j) for i, j in route if j is not None and...]
    ppermute x30, waiting for transfers between devices: 36 us -> 32.8 us  [over(): lax.ppermute(block, axes, [(i, j) for i, j in route if j is not None and...]
    pallas_call x24 -> x26, Pallas kernels: 29.3 us -> 29.5 us  [call(): pl.pallas_call(body, out_shape=shapes, in_specs=specs, out_specs=[vmem] *...]
  transfers between devices with their start and end apart: 30 -> 30, of which waited for: 13 -> 10; matrix products, arithmetic and copies ran while one was open for 0% -> 0% of each run, Pallas kernels for 25% -> 24%
where the time goes in v15:
time: 114 us; the launch traced here: 113 us
  starting transfers between devices  46.2 us (41%)
  waiting for transfers between devices  32.8 us (29%)
  Pallas kernels  31.4 us (28%)
  local copies, waits for them, and re-layouts  1.86 us (2%)
    ppermute x30, starting transfers between devices, over(): lax.ppermute(block, axes, [(i, j) for i, j in route if j is not None and...  46.2 us
    ppermute x30, waiting for transfers between devices, over(): lax.ppermute(block, axes, [(i, j) for i, j in route if j is not None and...  32.8 us
    pallas_call x26, Pallas kernels, call(): pl.pallas_call(body, out_shape=shapes, in_specs=specs, out_specs=[vmem] *...  29.5 us
  transfers between devices with their start and end apart: 30, of which 10 were waited for; matrix products, arithmetic and copies ran while one was open for 0% of the time, Pallas kernels for 24%

profile of v15, /device:TPU:13, one launch (start us, length us, event | category | flops | bytes accessed | tf_op | source)
XLA Modules:
  0.0 112.8 jit_solution(7581892382817014203)
XLA Ops:
  0.1 1.7 %copy-done = bf16[64,20480]{1,0:T(8,128)(2,1)S(1)} copy-done((bf16[64,20480]{1,0:T(8,128)(2,1)S(1)}, bf16[64,20480]{1,0:T(8,128)(2,1)}, u32[]{:S(2)}) %copy-start) | copy-done | bytes 2621464
  2.8 1.3 %pack.1 = (bf16[64,8448]{1,0:T(8,128)(2,1)S(1)}, bf16[16,10240]{1,0:T(8,128)(2,1)S(1)}) custom-call(s32[5]{0:T(128)S(1)} %stack.23.place, bf16[64,20480]{1,0:T(8,128)(2,1)S(1)} %copy-done, bf16[64,256]{1,0:T(8,128)(2,1)S(1)} %copy-done.2, bf16[64,4096]{1,0:T(8,128)(2,1)S(1)} %pack_first.1.order), custom_call_target="tpu_custom_call" | custom-call | flops 1 | bytes 1 | tf_op jit(solution)/shard_map/pack/pallas_call | solution.py:663
  5.0 3.0 %collective-permute-done.got_first.got.edges = bf16[64,4096]{1,0:T(8,128)(2,1)S(1)} collective-permute-done((bf16[64,4096]{1,0:T(8,128)(2,1)S(1)}, bf16[64,4096]{1,0:T(8,128)(2,1)S(1)}, u32[]{:S(2)}, u32[]{:S(2)}) %collective-permute-start) | collective-permute-done | bytes 524320 | tf_op jit(solution)/shard_map/ppermute | solution.py:688
  9.7 4.8 %collective-permute-start.2 = (bf16[128,512]{1,0:T(8,128)(2,1)S(1)}, bf16[128,512]{1,0:T(8,128)(2,1)S(1)}, u32[]{:S(2)}, u32[]{:S(2)}) collective-permute-start(bf16[128,512]{1,0:T(8,128)(2,1)S(1)} %get-tuple-element.65), channel_id=1, source_target_pairs={{0,2},{1,3},{2,0},{3,1},{4,6},{5,7},{6,4},{7,5},{8,10},{9,11},{10,... | collective-permute-start | bytes 393224 | tf_op jit(solution)/shard_map/ppermute | solution.py:688
  15.6 1.3 %collective-permute-start.6 = (bf16[128,384]{1,0:T(8,128)(2,1)S(1)}, bf16[128,384]{1,0:T(8,128)(2,1)S(1)}, u32[]{:S(2)}, u32[]{:S(2)}) collective-permute-start(bf16[128,384]{1,0:T(8,128)(2,1)S(1)} %get-tuple-element.72), channel_id=1, source_target_pairs={{0,1},{1,0},{2,3},{3,2},{4,5},{5,4},{6,7},{7,6},{8,9},{9,8},{10,11... | collective-permute-start | bytes 294920 | tf_op jit(solution)/shard_map/ppermute | solution.py:688
  16.9 1.7 %collective-permute-start.7 = (bf16[128,384]{1,0:T(8,128)(2,1)S(1)}, bf16[128,384]{1,0:T(8,128)(2,1)S(1)}, u32[]{:S(2)}, u32[]{:S(2)}) collective-permute-start(bf16[128,384]{1,0:T(8,128)(2,1)S(1)} %get-tuple-element.73), channel_id=1, source_target_pairs={{0,2},{1,3},{2,0},{3,1},{4,6},{5,7},{6,4},{7,5},{8,10},{9,11},{10,... | collective-permute-start | bytes 294920 | tf_op jit(solution)/shard_map/ppermute | solution.py:688
  19.8 6.2 %collective-permute-done.2.refs_2_.refs_4_ = bf16[128,512]{1,0:T(8,128)(2,1)S(1)} collective-permute-done((bf16[128,512]{1,0:T(8,128)(2,1)S(1)}, bf16[128,512]{1,0:T(8,128)(2,1)S(1)}, u32[]{:S(2)}, u32[]{:S(2)}) %collective-permute-start.2) | collective-permute-done | bytes 131104 | tf_op jit(solution)/shard_map/ppermute | solution.py:688
  26.0 3.0 %collective-permute-done.3.refs_3_.refs_5_ = bf16[128,512]{1,0:T(8,128)(2,1)S(1)} collective-permute-done((bf16[128,512]{1,0:T(8,128)(2,1)S(1)}, bf16[128,512]{1,0:T(8,128)(2,1)S(1)}, u32[]{:S(2)}, u32[]{:S(2)}) %collective-permute-start.3) | collective-permute-done | bytes 131104 | tf_op jit(solution)/shard_map/ppermute | solution.py:688
  29.0 2.1 %collective-permute-done.7.refs_2_.refs_7_ = bf16[128,384]{1,0:T(8,128)(2,1)S(1)} collective-permute-done((bf16[128,384]{1,0:T(8,128)(2,1)S(1)}, bf16[128,384]{1,0:T(8,128)(2,1)S(1)}, u32[]{:S(2)}, u32[]{:S(2)}) %collective-permute-start.7) | collective-permute-done | bytes 98336 | tf_op jit(solution)/shard_map/ppermute | solution.py:688
  31.1 2.1 %collective-permute-done.8.refs_3_.refs_8_ = bf16[128,384]{1,0:T(8,128)(2,1)S(1)} collective-permute-done((bf16[128,384]{1,0:T(8,128)(2,1)S(1)}, bf16[128,384]{1,0:T(8,128)(2,1)S(1)}, u32[]{:S(2)}, u32[]{:S(2)}) %collective-permute-start.8) | collective-permute-done | bytes 98336 | tf_op jit(solution)/shard_map/ppermute | solution.py:688
  33.2 3.4 %collective-permute-start.13 = (bf16[128,1024]{1,0:T(8,128)(2,1)S(1)}, bf16[128,1024]{1,0:T(8,128)(2,1)S(1)}, u32[]{:S(2)}, u32[]{:S(2)}) collective-permute-start(bf16[128,1024]{1,0:T(8,128)(2,1)S(1)} %get-tuple-element.87), channel_id=1, source_target_pairs={{0,2},{1,3},{2,0},{3,1},{4,6},{5,7},{6,4},{7,5},{8,10},{9,11},{10,... | collective-permute-start | bytes 786440 | tf_op jit(solution)/shard_map/ppermute | solution.py:688
  37.4 1.7 %prep.1 = (bf16[512,256]{1,0:T(8,128)(2,1)S(1)}, f32[4,2560]{1,0:T(4,128)S(1)}, f32[512,128]{1,0:T(8,128)S(1)}, f32[128,512]{1,0:T(8,128)S(1)}, bf16[512,256]{1,...) custom-call(s32[5]{0:T(128)S(1)} %stack.23.place, ...), custom_call_target="tpu_custom_call" | custom-call | flops 1 | bytes 1 | tf_op jit(solution)/shard_map/prep/pallas_call | solution.py:663
  39.1 2.1 %state.4 = (bf16[512,512]{1,0:T(8,128)(2,1)S(1)}, f32[256,512]{1,0:T(8,128)S(1)}, bf16[272,256]{1,0:T(8,128)(2,1)S(1)}, bf16[272,256]{1,0:T(8,128)(2,1)S(1)}) custom-call(s32[5]{0:T(128)S(1)} %stack.23.place, bf16[128,512]{1,0:T(8,128)(2,1)S(1)} %get-tuple-element.63.refs_0_, bf16[128,512]{1,0:T(8,128)(2,1)S(1)} %collective-permute-done.1.refs_1_.refs_3_, ...), custom_call_target="tpu_custom_call" | custom-call | flops 1 | bytes 1 | tf_op jit(solution)/shard_map/state/pallas_call | solution.py:663
  41.1 2.3 %collective-permute-start.9 = (bf16[272,256]{1,0:T(8,128)(2,1)S(1)}, bf16[272,256]{1,0:T(8,128)(2,1)S(1)}, u32[]{:S(2)}, u32[]{:S(2)}) collective-permute-start(bf16[272,256]{1,0:T(8,128)(2,1)S(1)} %get-tuple-element.80.refs_2_.refs_0_), channel_id=1, source_target_pairs={{0,8},{1,9},{2,10},{3,11},{4,12},{5,13},{6,14},{7,15},{8,0},{9,1},... | collective-permute-start | bytes 417800 | tf_op jit(solution)/shard_map/ppermute | solution.py:688
  43.5 1.3 %collective-permute-start.10 = (bf16[272,256]{1,0:T(8,128)(2,1)S(1)}, bf16[272,256]{1,0:T(8,128)(2,1)S(1)}, u32[]{:S(2)}, u32[]{:S(2)}) collective-permute-start(bf16[272,256]{1,0:T(8,128)(2,1)S(1)} %get-tuple-element.81.refs_3_.refs_1_), channel_id=1, source_target_pairs={{0,8},{1,9},{2,10},{3,11},{4,12},{5,13},{6,14},{7,15},{8,0},{9,1},... | collective-permute-start | bytes 417800 | tf_op jit(solution)/shard_map/ppermute | solution.py:688
  45.5 6.9 %collective-permute-done.13.refs_2_.refs_3_ = bf16[128,1024]{1,0:T(8,128)(2,1)S(1)} collective-permute-done((bf16[128,1024]{1,0:T(8,128)(2,1)S(1)}, bf16[128,1024]{1,0:T(8,128)(2,1)S(1)}, u32[]{:S(2)}, u32[]{:S(2)}) %collective-permute-start.13) | collective-permute-done | bytes 262176 | tf_op jit(solution)/shard_map/ppermute | solution.py:688
  52.4 6.0 %collective-permute-done.14.refs_3_.refs_4_ = bf16[128,1024]{1,0:T(8,128)(2,1)S(1)} collective-permute-done((bf16[128,1024]{1,0:T(8,128)(2,1)S(1)}, bf16[128,1024]{1,0:T(8,128)(2,1)S(1)}, u32[]{:S(2)}, u32[]{:S(2)}) %collective-permute-start.14) | collective-permute-done | bytes 262176 | tf_op jit(solution)/shard_map/ppermute | solution.py:688
  58.4 2.3 %collective-permute-start.16 = (bf16[128,768]{1,0:T(8,128)(2,1)S(1)}, bf16[128,768]{1,0:T(8,128)(2,1)S(1)}, u32[]{:S(2)}, u32[]{:S(2)}) collective-permute-start(bf16[128,768]{1,0:T(8,128)(2,1)S(1)} %get-tuple-element.102), channel_id=1, source_target_pairs={{0,3},{1,2},{2,1},{3,0},{4,7},{5,6},{6,5},{7,4},{8,11},{9,10},{10,... | collective-permute-start | bytes 589832 | tf_op jit(solution)/shard_map/ppermute | solution.py:688
  61.4 2.6 %state.5 = (bf16[512,768]{1,0:T(8,128)(2,1)S(1)}, f32[256,768]{1,0:T(8,128)S(1)}, bf16[272,256]{1,0:T(8,128)(2,1)S(1)}, bf16[272,256]{1,0:T(8,128)(2,1)S(1)}, bf16[272,256]{1,0:T(8,128)(2,1)S(1)}) custom-call(s32[5]{0:T(128)S(1)} %stack.23.place, bf16[128,1024]{1,0:T(8,128)(2,1)S(1)} %get-tuple-element.75.refs_9_.refs_0_, ...), custom_call_target="tpu_custom_call" | custom-call | flops 1 | bytes 1 | tf_op jit(solution)/shard_map/state/pallas_call | solution.py:663
  64.0 1.9 %collective-permute-start.17 = (bf16[272,256]{1,0:T(8,128)(2,1)S(1)}, bf16[272,256]{1,0:T(8,128)(2,1)S(1)}, u32[]{:S(2)}, u32[]{:S(2)}) collective-permute-start(bf16[272,256]{1,0:T(8,128)(2,1)S(1)} %get-tuple-element.89.refs_8_.refs_2_), channel_id=1, source_target_pairs={{0,8},{1,9},{2,10},{3,11},{4,12},{5,13},{6,14},{7,15},{8,0},{9,1},... | collective-permute-start | bytes 417800 | tf_op jit(solution)/shard_map/ppermute | solution.py:688
  65.9 1.3 %collective-permute-start.18 = (bf16[272,256]{1,0:T(8,128)(2,1)S(1)}, bf16[272,256]{1,0:T(8,128)(2,1)S(1)}, u32[]{:S(2)}, u32[]{:S(2)}) collective-permute-start(bf16[272,256]{1,0:T(8,128)(2,1)S(1)} %get-tuple-element.90.refs_9_.refs_3_.refs_2_), channel_id=1, source_target_pairs={{0,8},{1,9},{2,10},{3,11},{4,12},{5,13},{6,14},{7,15},{8,0},{9,1},... | collective-permute-start | bytes 417800 | tf_op jit(solution)/shard_map/ppermute | solution.py:688
  73.3 1.5 %collective-permute-start.23 = (bf16[272,384]{1,0:T(8,128)(2,1)S(1)}, bf16[272,384]{1,0:T(8,128)(2,1)S(1)}, u32[]{:S(2)}, u32[]{:S(2)}) collective-permute-start(bf16[272,384]{1,0:T(8,128)(2,1)S(1)} %combine.7.refs_1_), channel_id=1, source_target_pairs={{0,16},{1,17},{2,18},{3,19},{4,20},{5,21},{6,22},{7,23},{8,24},{9,... | collective-permute-start | bytes 626696 | tf_op jit(solution)/shard_map/ppermute | solution.py:688
  74.8 1.5 %local.5.refs_10_.refs_8_ = f32[512,768]{1,0:T(8,128)S(1)} custom-call(bf16[512,768]{1,0:T(8,128)(2,1)S(1)} %get-tuple-element.103.x_ref, f32[512,128]{1,0:T(8,128)S(1)} %get-tuple-element.94.cum_ref, f32[128,512]{1,0:T(8,128)S(1)} %get-tuple-element.95.row_ref, f32[512,256]{1,0:T(8,128)S(1)} %get-tuple-element.96.score_ref, ...), custom_call_target="tpu_custom_call" | custom-call | flops 1 | bytes 1 | tf_op jit(solution)/shard_map/local/pallas_call | solution.py:663
  76.3 2.1 %collective-permute-done.16.refs_3_ = bf16[128,768]{1,0:T(8,128)(2,1)S(1)} collective-permute-done((bf16[128,768]{1,0:T(8,128)(2,1)S(1)}, bf16[128,768]{1,0:T(8,128)(2,1)S(1)}, u32[]{:S(2)}, u32[]{:S(2)}) %collective-permute-start.16) | collective-permute-done | bytes 196640 | tf_op jit(solution)/shard_map/ppermute | solution.py:688
  78.4 1.9 %state.6 = (bf16[512,384]{1,0:T(8,128)(2,1)S(1)}, f32[256,384]{1,0:T(8,128)S(1)}, bf16[272,384]{1,0:T(8,128)(2,1)S(1)}) custom-call(s32[5]{0:T(128)S(1)} %stack.23.place, bf16[128,768]{1,0:T(8,128)(2,1)S(1)} %get-tuple-element.98.refs_0_, bf16[128,1792]{1,0:T(8,128)(2,1)S(1)} %collective-permute-done.12.refs_1_.refs_2_, ...), custom_call_target="tpu_custom_call" | custom-call | flops 1 | bytes 1 | tf_op jit(solution)/shard_map/state/pallas_call | solution.py:663
  80.3 1.3 %collective-permute-start.21 = (bf16[272,384]{1,0:T(8,128)(2,1)S(1)}, bf16[272,384]{1,0:T(8,128)(2,1)S(1)}, u32[]{:S(2)}, u32[]{:S(2)}) collective-permute-start(bf16[272,384]{1,0:T(8,128)(2,1)S(1)} %get-tuple-element.104.refs_10_.refs_1_), channel_id=1, source_target_pairs={{0,8},{1,9},{2,10},{3,11},{4,12},{5,13},{6,14},{7,15},{8,0},{9,1},... | collective-permute-start | bytes 626696 | tf_op jit(solution)/shard_map/ppermute | solution.py:688
  81.6 1.9 %state.7 = (bf16[512,384]{1,0:T(8,128)(2,1)S(1)}, f32[256,384]{1,0:T(8,128)S(1)}, bf16[272,384]{1,0:T(8,128)(2,1)S(1)}) custom-call(s32[5]{0:T(128)S(1)} %stack.23.place, bf16[128,768]{1,0:T(8,128)(2,1)S(1)} %get-tuple-element.98.refs_0_, bf16[128,1792]{1,0:T(8,128)(2,1)S(1)} %collective-permute-done.12.refs_1_.refs_2_, ...), custom_call_target="tpu_custom_call" | custom-call | flops 1 | bytes 1 | tf_op jit(solution)/shard_map/state/pallas_call | solution.py:663
  83.5 1.3 %collective-permute-start.20 = (bf16[272,384]{1,0:T(8,128)(2,1)S(1)}, bf16[272,384]{1,0:T(8,128)(2,1)S(1)}, u32[]{:S(2)}, u32[]{:S(2)}) collective-permute-start(bf16[272,384]{1,0:T(8,128)(2,1)S(1)} %get-tuple-element.107.refs_9_.refs_1_), channel_id=1, source_target_pairs={{0,8},{1,9},{2,10},{3,11},{4,12},{5,13},{6,14},{7,15},{8,0},{9,1},... | collective-permute-start | bytes 626696 | tf_op jit(solution)/shard_map/ppermute | solution.py:688
  91.3 4.7 %collective-permute-start.27 = (bf16[256,768]{1,0:T(8,128)(2,1)S(1)}, bf16[256,768]{1,0:T(8,128)(2,1)S(1)}, u32[]{:S(2)}, u32[]{:S(2)}) collective-permute-start(bf16[256,768]{1,0:T(8,128)(2,1)S(1)} %get-tuple-element.116), channel_id=1, source_target_pairs={{0,4},{1,5},{2,6},{3,7},{4,0},{5,1},{6,2},{7,3},{8,12},{9,13},{10,... | collective-permute-start | bytes 1179656 | tf_op jit(solution)/shard_map/ppermute | solution.py:688
  98.6 5.0 %collective-permute-start.26 = (bf16[256,512]{1,0:T(8,128)(2,1)S(1)}, bf16[256,512]{1,0:T(8,128)(2,1)S(1)}, u32[]{:S(2)}, u32[]{:S(2)}) collective-permute-start(bf16[256,512]{1,0:T(8,128)(2,1)S(1)} %get-tuple-element.115), channel_id=1, source_target_pairs={{0,4},{1,5},{2,6},{3,7},{4,0},{5,1},{6,2},{7,3},{8,12},{9,13},{10,... | collective-permute-start | bytes 786440 | tf_op jit(solution)/shard_map/ppermute | solution.py:688
  105.8 3.5 %collective-permute-start.29 = (bf16[256,384]{1,0:T(8,128)(2,1)S(1)}, bf16[256,384]{1,0:T(8,128)(2,1)S(1)}, u32[]{:S(2)}, u32[]{:S(2)}) collective-permute-start(bf16[256,384]{1,0:T(8,128)(2,1)S(1)} %get-tuple-element.118), channel_id=1, source_target_pairs={{0,4},{1,5},{2,6},{3,7},{4,0},{5,1},{6,2},{7,3},{8,12},{9,13},{10,... | collective-permute-start | bytes 589832 | tf_op jit(solution)/shard_map/ppermute | solution.py:688
  110.8 1.9 %place.1 = bf16[256,4096]{1,0:T(8,128)(2,1)} custom-call(s32[5]{0:T(128)S(1)} %stack.23.place, bf16[256,512]{1,0:T(8,128)(2,1)S(1)} %get-tuple-element.110.refs_6_.refs_0_, bf16[256,768]{1,0:T(8,128)(2,1)S(1)} %get-tuple-element.109.refs_2_.refs_1_, bf16[256,384]{1,0:T(8,128)(2,1)S(1)} %get-tuple-element.112.refs_6_.refs_2_, ...), custom_call_target="tpu_custom_call" | custom-call | flops 1 | bytes 1 | tf_op jit(solution)/shard_map/place/pallas_call | solution.py:625
  (74 shorter events, 26.6 us)
Async XLA Ops:
  4.1 10.4 %collective-permute-start.4 = (bf16[64,8448]{1,0:T(8,128)(2,1)S(1)}, bf16[64,8448]{1,0:T(8,128)(2,1)S(1)}, u32[]{:S(2)}, u32[]{:S(2)}) collective-permute-start(bf16[64,8448]{1,0:T(8,128)(2,1)S(1)} %get-tuple-element.67), channel_id=1, source_target_pairs={{0,4},{1,5},{2,6},{3,7},{4,0},{5,1},{6,2},{7,3},{8,12},{9,13},{10,... | collective-permute-start | bytes 3244040 | tf_op jit(solution)/shard_map/ppermute | solution.py:688
  4.9 3.1 %collective-permute-start = (bf16[64,4096]{1,0:T(8,128)(2,1)S(1)}, bf16[64,4096]{1,0:T(8,128)(2,1)S(1)}, u32[]{:S(2)}, u32[]{:S(2)}) collective-permute-start(bf16[64,4096]{1,0:T(8,128)(2,1)S(1)} %pack_first.1.order), channel_id=1, source_target_pairs={{0,4},{1,5},{2,6},{3,7},{4,0},{5,1},{6,2},{7,3},{8,12},{9,13},{10,... | collective-permute-start | bytes 1572872 | tf_op jit(solution)/shard_map/ppermute | solution.py:688
  8.8 9.8 %collective-permute-start.1 = (bf16[128,512]{1,0:T(8,128)(2,1)S(1)}, bf16[128,512]{1,0:T(8,128)(2,1)S(1)}, u32[]{:S(2)}, u32[]{:S(2)}) collective-permute-start(bf16[128,512]{1,0:T(8,128)(2,1)S(1)} %get-tuple-element.64), channel_id=1, source_target_pairs={{0,1},{1,0},{2,3},{3,2},{4,5},{5,4},{6,7},{7,6},{8,9},{9,8},{10,11... | collective-permute-start | bytes 393224 | tf_op jit(solution)/shard_map/ppermute | solution.py:688
  9.0 5.5 %collective-permute-start.5 = (bf16[3,10240]{1,0:T(4,128)(2,1)S(1)}, bf16[3,10240]{1,0:T(4,128)(2,1)S(1)}, u32[]{:S(2)}, u32[]{:S(2)}) collective-permute-start(bf16[3,10240]{1,0:T(4,128)(2,1)S(1)} %get-tuple-element.70), channel_id=1, source_target_pairs={{3,11},{7,15},{11,19},{15,23},{19,27},{23,31}} | collective-permute-start | bytes 184328 | tf_op jit(solution)/shard_map/ppermute | solution.py:688
  9.7 16.3 %collective-permute-start.2 = (bf16[128,512]{1,0:T(8,128)(2,1)S(1)}, bf16[128,512]{1,0:T(8,128)(2,1)S(1)}, u32[]{:S(2)}, u32[]{:S(2)}) collective-permute-start(bf16[128,512]{1,0:T(8,128)(2,1)S(1)} %get-tuple-element.65), channel_id=1, source_target_pairs={{0,2},{1,3},{2,0},{3,1},{4,6},{5,7},{6,4},{7,5},{8,10},{9,11},{10,... | collective-permute-start | bytes 393224 | tf_op jit(solution)/shard_map/ppermute | solution.py:688
  14.5 14.5 %collective-permute-start.3 = (bf16[128,512]{1,0:T(8,128)(2,1)S(1)}, bf16[128,512]{1,0:T(8,128)(2,1)S(1)}, u32[]{:S(2)}, u32[]{:S(2)}) collective-permute-start(bf16[128,512]{1,0:T(8,128)(2,1)S(1)} %get-tuple-element.66), channel_id=1, source_target_pairs={{0,3},{1,2},{2,1},{3,0},{4,7},{5,6},{6,5},{7,4},{8,11},{9,10},{10,... | collective-permute-start | bytes 393224 | tf_op jit(solution)/shard_map/ppermute | solution.py:688
  15.6 13.4 %collective-permute-start.6 = (bf16[128,384]{1,0:T(8,128)(2,1)S(1)}, bf16[128,384]{1,0:T(8,128)(2,1)S(1)}, u32[]{:S(2)}, u32[]{:S(2)}) collective-permute-start(bf16[128,384]{1,0:T(8,128)(2,1)S(1)} %get-tuple-element.72), channel_id=1, source_target_pairs={{0,1},{1,0},{2,3},{3,2},{4,5},{5,4},{6,7},{7,6},{8,9},{9,8},{10,11... | collective-permute-start | bytes 294920 | tf_op jit(solution)/shard_map/ppermute | solution.py:688
  16.9 14.2 %collective-permute-start.7 = (bf16[128,384]{1,0:T(8,128)(2,1)S(1)}, bf16[128,384]{1,0:T(8,128)(2,1)S(1)}, u32[]{:S(2)}, u32[]{:S(2)}) collective-permute-start(bf16[128,384]{1,0:T(8,128)(2,1)S(1)} %get-tuple-element.73), channel_id=1, source_target_pairs={{0,2},{1,3},{2,0},{3,1},{4,6},{5,7},{6,4},{7,5},{8,10},{9,11},{10,... | collective-permute-start | bytes 294920 | tf_op jit(solution)/shard_map/ppermute | solution.py:688
  18.6 14.6 %collective-permute-start.8 = (bf16[128,384]{1,0:T(8,128)(2,1)S(1)}, bf16[128,384]{1,0:T(8,128)(2,1)S(1)}, u32[]{:S(2)}, u32[]{:S(2)}) collective-permute-start(bf16[128,384]{1,0:T(8,128)(2,1)S(1)} %get-tuple-element.74), channel_id=1, source_target_pairs={{0,3},{1,2},{2,1},{3,0},{4,7},{5,6},{6,5},{7,4},{8,11},{9,10},{10,... | collective-permute-start | bytes 294920 | tf_op jit(solution)/shard_map/ppermute | solution.py:688
  19.8 16.9 %copy-start.3 = (f32[4,20480]{1,0:T(4,128)S(1)}, f32[4,20480]{1,0:T(4,128)}, u32[]{:S(2)}) copy-start(f32[4,20480]{1,0:T(4,128)} %weight.1) | copy-start | bytes 983044
  19.8 16.9 %copy-start.4 = (f32[20480]{0:T(1024)S(1)}, f32[20480]{0:T(1024)}, u32[]{:S(2)}) copy-start(f32[20480]{0:T(1024)} %param.10) | copy-start | bytes 245764
  33.2 25.3 %collective-permute-start.12 = (bf16[128,1792]{1,0:T(8,128)(2,1)S(1)}, bf16[128,1792]{1,0:T(8,128)(2,1)S(1)}, u32[]{:S(2)}, u32[]{:S(2)}) collective-permute-start(bf16[128,1792]{1,0:T(8,128)(2,1)S(1)} %get-tuple-element.86), channel_id=1, source_target_pairs={{0,1},{1,0},{2,3},{3,2},{4,5},{5,4},{6,7},{7,6},{8,9},{9,8},{10,11... | collective-permute-start | bytes 1376264 | tf_op jit(solution)/shard_map/ppermute | solution.py:688
  33.2 19.2 %collective-permute-start.13 = (bf16[128,1024]{1,0:T(8,128)(2,1)S(1)}, bf16[128,1024]{1,0:T(8,128)(2,1)S(1)}, u32[]{:S(2)}, u32[]{:S(2)}) collective-permute-start(bf16[128,1024]{1,0:T(8,128)(2,1)S(1)} %get-tuple-element.87), channel_id=1, source_target_pairs={{0,2},{1,3},{2,0},{3,1},{4,6},{5,7},{6,4},{7,5},{8,10},{9,11},{10,... | collective-permute-start | bytes 786440 | tf_op jit(solution)/shard_map/ppermute | solution.py:688
  36.6 21.8 %collective-permute-start.14 = (bf16[128,1024]{1,0:T(8,128)(2,1)S(1)}, bf16[128,1024]{1,0:T(8,128)(2,1)S(1)}, u32[]{:S(2)}, u32[]{:S(2)}) collective-permute-start(bf16[128,1024]{1,0:T(8,128)(2,1)S(1)} %get-tuple-element.88), channel_id=1, source_target_pairs={{0,3},{1,2},{2,1},{3,0},{4,7},{5,6},{6,5},{7,4},{8,11},{9,10},{10,... | collective-permute-start | bytes 786440 | tf_op jit(solution)/shard_map/ppermute | solution.py:688
  41.1 19.6 %collective-permute-start.9 = (bf16[272,256]{1,0:T(8,128)(2,1)S(1)}, bf16[272,256]{1,0:T(8,128)(2,1)S(1)}, u32[]{:S(2)}, u32[]{:S(2)}) collective-permute-start(bf16[272,256]{1,0:T(8,128)(2,1)S(1)} %get-tuple-element.80.refs_2_.refs_0_), channel_id=1, source_target_pairs={{0,8},{1,9},{2,10},{3,11},{4,12},{5,13},{6,14},{7,15},{8,0},{9,1},... | collective-permute-start | bytes 417800 | tf_op jit(solution)/shard_map/ppermute | solution.py:688
  43.5 17.2 %collective-permute-start.10 = (bf16[272,256]{1,0:T(8,128)(2,1)S(1)}, bf16[272,256]{1,0:T(8,128)(2,1)S(1)}, u32[]{:S(2)}, u32[]{:S(2)}) collective-permute-start(bf16[272,256]{1,0:T(8,128)(2,1)S(1)} %get-tuple-element.81.refs_3_.refs_1_), channel_id=1, source_target_pairs={{0,8},{1,9},{2,10},{3,11},{4,12},{5,13},{6,14},{7,15},{8,0},{9,1},... | collective-permute-start | bytes 417800 | tf_op jit(solution)/shard_map/ppermute | solution.py:688
  58.4 17.9 %collective-permute-start.15 = (bf16[128,768]{1,0:T(8,128)(2,1)S(1)}, bf16[128,768]{1,0:T(8,128)(2,1)S(1)}, u32[]{:S(2)}, u32[]{:S(2)}) collective-permute-start(bf16[128,768]{1,0:T(8,128)(2,1)S(1)} %get-tuple-element.101), channel_id=1, source_target_pairs={{0,2},{1,3},{2,0},{3,1},{4,6},{5,7},{6,4},{7,5},{8,10},{9,11},{10,... | collective-permute-start | bytes 589832 | tf_op jit(solution)/shard_map/ppermute | solution.py:688
  58.4 20.0 %collective-permute-start.16 = (bf16[128,768]{1,0:T(8,128)(2,1)S(1)}, bf16[128,768]{1,0:T(8,128)(2,1)S(1)}, u32[]{:S(2)}, u32[]{:S(2)}) collective-permute-start(bf16[128,768]{1,0:T(8,128)(2,1)S(1)} %get-tuple-element.102), channel_id=1, source_target_pairs={{0,3},{1,2},{2,1},{3,0},{4,7},{5,6},{6,5},{7,4},{8,11},{9,10},{10,... | collective-permute-start | bytes 589832 | tf_op jit(solution)/shard_map/ppermute | solution.py:688
  64.0 6.7 %collective-permute-start.17 = (bf16[272,256]{1,0:T(8,128)(2,1)S(1)}, bf16[272,256]{1,0:T(8,128)(2,1)S(1)}, u32[]{:S(2)}, u32[]{:S(2)}) collective-permute-start(bf16[272,256]{1,0:T(8,128)(2,1)S(1)} %get-tuple-element.89.refs_8_.refs_2_), channel_id=1, source_target_pairs={{0,8},{1,9},{2,10},{3,11},{4,12},{5,13},{6,14},{7,15},{8,0},{9,1},... | collective-permute-start | bytes 417800 | tf_op jit(solution)/shard_map/ppermute | solution.py:688
  65.9 4.8 %collective-permute-start.18 = (bf16[272,256]{1,0:T(8,128)(2,1)S(1)}, bf16[272,256]{1,0:T(8,128)(2,1)S(1)}, u32[]{:S(2)}, u32[]{:S(2)}) collective-permute-start(bf16[272,256]{1,0:T(8,128)(2,1)S(1)} %get-tuple-element.90.refs_9_.refs_3_.refs_2_), channel_id=1, source_target_pairs={{0,8},{1,9},{2,10},{3,11},{4,12},{5,13},{6,14},{7,15},{8,0},{9,1},... | collective-permute-start | bytes 417800 | tf_op jit(solution)/shard_map/ppermute | solution.py:688
  67.2 5.4 %collective-permute-start.19 = (bf16[272,256]{1,0:T(8,128)(2,1)S(1)}, bf16[272,256]{1,0:T(8,128)(2,1)S(1)}, u32[]{:S(2)}, u32[]{:S(2)}) collective-permute-start(bf16[272,256]{1,0:T(8,128)(2,1)S(1)} %get-tuple-element.91.refs_10_.refs_3_), channel_id=1, source_target_pairs={{0,8},{1,9},{2,10},{3,11},{4,12},{5,13},{6,14},{7,15},{8,0},{9,1},... | collective-permute-start | bytes 417800 | tf_op jit(solution)/shard_map/ppermute | solution.py:688
  71.4 14.8 %collective-permute-start.22 = (bf16[272,384]{1,0:T(8,128)(2,1)S(1)}, bf16[272,384]{1,0:T(8,128)(2,1)S(1)}, u32[]{:S(2)}, u32[]{:S(2)}) collective-permute-start(bf16[272,384]{1,0:T(8,128)(2,1)S(1)} %combine.6.refs_4_.refs_0_), channel_id=1, source_target_pairs={{0,16},{1,17},{2,18},{3,19},{4,20},{5,21},{6,22},{7,23},{8,24},{9,... | collective-permute-start | bytes 626696 | tf_op jit(solution)/shard_map/ppermute | solution.py:688
  73.3 12.8 %collective-permute-start.23 = (bf16[272,384]{1,0:T(8,128)(2,1)S(1)}, bf16[272,384]{1,0:T(8,128)(2,1)S(1)}, u32[]{:S(2)}, u32[]{:S(2)}) collective-permute-start(bf16[272,384]{1,0:T(8,128)(2,1)S(1)} %combine.7.refs_1_), channel_id=1, source_target_pairs={{0,16},{1,17},{2,18},{3,19},{4,20},{5,21},{6,22},{7,23},{8,24},{9,... | collective-permute-start | bytes 626696 | tf_op jit(solution)/shard_map/ppermute | solution.py:688
  80.3 7.1 %collective-permute-start.21 = (bf16[272,384]{1,0:T(8,128)(2,1)S(1)}, bf16[272,384]{1,0:T(8,128)(2,1)S(1)}, u32[]{:S(2)}, u32[]{:S(2)}) collective-permute-start(bf16[272,384]{1,0:T(8,128)(2,1)S(1)} %get-tuple-element.104.refs_10_.refs_1_), channel_id=1, source_target_pairs={{0,8},{1,9},{2,10},{3,11},{4,12},{5,13},{6,14},{7,15},{8,0},{9,1},... | collective-permute-start | bytes 626696 | tf_op jit(solution)/shard_map/ppermute | solution.py:688
  83.5 5.9 %collective-permute-start.20 = (bf16[272,384]{1,0:T(8,128)(2,1)S(1)}, bf16[272,384]{1,0:T(8,128)(2,1)S(1)}, u32[]{:S(2)}, u32[]{:S(2)}) collective-permute-start(bf16[272,384]{1,0:T(8,128)(2,1)S(1)} %get-tuple-element.107.refs_9_.refs_1_), channel_id=1, source_target_pairs={{0,8},{1,9},{2,10},{3,11},{4,12},{5,13},{6,14},{7,15},{8,0},{9,1},... | collective-permute-start | bytes 626696 | tf_op jit(solution)/shard_map/ppermute | solution.py:688
  84.8 12.7 %collective-permute-start.11 = (bf16[272,512]{1,0:T(8,128)(2,1)S(1)}, bf16[272,512]{1,0:T(8,128)(2,1)S(1)}, u32[]{:S(2)}, u32[]{:S(2)}) collective-permute-start(bf16[272,512]{1,0:T(8,128)(2,1)S(1)} %combine.5.refs_10_), channel_id=1, source_target_pairs={{0,16},{1,17},{2,18},{3,19},{4,20},{5,21},{6,22},{7,23},{8,24},{9,... | collective-permute-start | bytes 835592 | tf_op jit(solution)/shard_map/ppermute | solution.py:688
  88.1 15.6 %collective-permute-start.24 = (bf16[272,384]{1,0:T(8,128)(2,1)S(1)}, bf16[272,384]{1,0:T(8,128)(2,1)S(1)}, u32[]{:S(2)}, u32[]{:S(2)}) collective-permute-start(bf16[272,384]{1,0:T(8,128)(2,1)S(1)} %combine.8.refs_2_), channel_id=1, source_target_pairs={{0,16},{1,17},{2,18},{3,19},{4,20},{5,21},{6,22},{7,23},{8,24},{9,... | collective-permute-start | bytes 626696 | tf_op jit(solution)/shard_map/ppermute | solution.py:688
  90.0 14.7 %collective-permute-start.25 = (bf16[272,384]{1,0:T(8,128)(2,1)S(1)}, bf16[272,384]{1,0:T(8,128)(2,1)S(1)}, u32[]{:S(2)}, u32[]{:S(2)}) collective-permute-start(bf16[272,384]{1,0:T(8,128)(2,1)S(1)} %combine.9.refs_0_), channel_id=1, source_target_pairs={{0,16},{1,17},{2,18},{3,19},{4,20},{5,21},{6,22},{7,23},{8,24},{9,... | collective-permute-start | bytes 626696 | tf_op jit(solution)/shard_map/ppermute | solution.py:688
  91.3 18.1 %collective-permute-start.27 = (bf16[256,768]{1,0:T(8,128)(2,1)S(1)}, bf16[256,768]{1,0:T(8,128)(2,1)S(1)}, u32[]{:S(2)}, u32[]{:S(2)}) collective-permute-start(bf16[256,768]{1,0:T(8,128)(2,1)S(1)} %get-tuple-element.116), channel_id=1, source_target_pairs={{0,4},{1,5},{2,6},{3,7},{4,0},{5,1},{6,2},{7,3},{8,12},{9,13},{10,... | collective-permute-start | bytes 1179656 | tf_op jit(solution)/shard_map/ppermute | solution.py:688
  98.6 10.8 %collective-permute-start.26 = (bf16[256,512]{1,0:T(8,128)(2,1)S(1)}, bf16[256,512]{1,0:T(8,128)(2,1)S(1)}, u32[]{:S(2)}, u32[]{:S(2)}) collective-permute-start(bf16[256,512]{1,0:T(8,128)(2,1)S(1)} %get-tuple-element.115), channel_id=1, source_target_pairs={{0,4},{1,5},{2,6},{3,7},{4,0},{5,1},{6,2},{7,3},{8,12},{9,13},{10,... | collective-permute-start | bytes 786440 | tf_op jit(solution)/shard_map/ppermute | solution.py:688
  105.8 4.6 %collective-permute-start.29 = (bf16[256,384]{1,0:T(8,128)(2,1)S(1)}, bf16[256,384]{1,0:T(8,128)(2,1)S(1)}, u32[]{:S(2)}, u32[]{:S(2)}) collective-permute-start(bf16[256,384]{1,0:T(8,128)(2,1)S(1)} %get-tuple-element.118), channel_id=1, source_target_pairs={{0,4},{1,5},{2,6},{3,7},{4,0},{5,1},{6,2},{7,3},{8,12},{9,13},{10,... | collective-permute-start | bytes 589832 | tf_op jit(solution)/shard_map/ppermute | solution.py:688
  109.3 1.4 %collective-permute-start.28 = (bf16[256,384]{1,0:T(8,128)(2,1)S(1)}, bf16[256,384]{1,0:T(8,128)(2,1)S(1)}, u32[]{:S(2)}, u32[]{:S(2)}) collective-permute-start(bf16[256,384]{1,0:T(8,128)(2,1)S(1)} %get-tuple-element.117), channel_id=1, source_target_pairs={{0,4},{1,5},{2,6},{3,7},{4,0},{5,1},{6,2},{7,3},{8,12},{9,13},{10,... | collective-permute-start | bytes 589832 | tf_op jit(solution)/shard_map/ppermute | solution.py:688
  (6 other events, 23.4 us)

commit v16 on v15

--- a/solution.py
+++ b/solution.py
@@ -164,9 +164,9 @@
 LOG2E = 1.4426950408889634
 F32, BF16 = jnp.float32, jnp.bfloat16
 WIDTHS = (512, 0, 768, 768)
-RESTS = ("", "BD", "C", "")
+RESTS = ("", "BD", "", "C")
 GROUPED = ((0, 0, 512), (2, 0, 768), (3, 0, 384), (3, 384, 384))
-FIRST_ROUND = ((256, 256), (256, 256, 256), (384,), (384,))
+FIRST_ROUND = ((256, 256), (384, 384), (384,), (384,))
 SECOND_ROUND = ((512,), (384, 384), (384,), (384,))
 
 
@@ -437,8 +437,8 @@
 def score_kernel(shards, place, *refs):
     blocks, refs = refs[:shards], refs[shards:]
     taps, offset, edge_ref, b_ref, c_ref, score_ref, wide = (*refs[:4], *refs[-3:])
-    blocks = view(blocks, 2)
-    start = WIDTHS[2]
+    blocks = view(blocks, 3)
+    start = WIDTHS[3]
     at = slice(PER_GROUP + STATE, PER_GROUP + 2 * STATE)
 
     def put(start, count, value):
@@ -836,25 +836,28 @@
     message.append([own_block, message[2][1], *fourth_blocks])
     combine_of(0, [])
     state_of(1, joined[0])
+    combine_of(1, [])
+    state_of(2, joined[1] + before[0])
+    state_of(3, sent[2])
     c, score = call(
         functools.partial(score_kernel, shards),
         [((slab, STATE), BF16), ((slab, BLOCK), F32)],
-        [place] + seen(2) + [taps, offset, edge, b] + [Stay(o) for o in sent[1]],
+        [place] + seen(3) + [taps, offset, edge, b] + [Stay(o) for o in sent[3] + before[1]],
         scratch=[pltpu.VMEM((slab + 8, STATE), F32)],
         name="score",
     )
-    local_of(0, [])
-    combine_of(1, [partial[0]])
-    local_of(1, joined[1])
-    state_of(2, [partial[1]])
-    state_of(3, sent[2])
-    finish_of(final_kernel, 1, [partial[1]], sent[3])
-    combine_of(2, [keep[1]])
-    combine_of(3, joined[2])
-    local_of(2, joined[3])
+
+    def in_full(i, order):
+        wide = [pltpu.VMEM((slab, GROUPED[i][2]), F32)]
+        finish_of(finish_kernel, i, [x[i], cum, row, score, skip], order, scratch=wide)
+
+    combine_of(2, [score])
+    in_full(1, joined[2])
+    combine_of(3, [keep[1]])
+    in_full(0, joined[3])
+    local_of(2, [keep[0]])
     local_of(3, [partial[2]])
-    finish_of(final_kernel, 0, [partial[0]], [partial[3]])
-    finish_of(final_kernel, 2, [partial[2]], [keep[0]])
+    finish_of(final_kernel, 2, [partial[2]], [partial[3]])
     finish_of(final_kernel, 3, [partial[3]], [keep[2]])
     firsts = [first_head(i) * HEAD_DIM for i in range(count)]
     return put_in_place(firsts, (BLOCK, PAIR * PER_GROUP), place, keep, [swap(o) for o in send])

time: 114 us -> 109 us (0.956)
  starting transfers between devices: 46.2 us -> 40.8 us
    ppermute x30 -> x29, starting transfers between devices: 46.2 us -> 40.8 us  [over(): lax.ppermute(block, axes, [(i, j) for i, j in route if j is not None and...]
    pallas_call x26 -> x24, Pallas kernels: 29.5 us -> 29.2 us  [call(): pl.pallas_call(body, out_shape=shapes, in_specs=specs, out_specs=[vmem] *...]
    ppermute x30 -> x29, waiting for transfers between devices: 32.8 us -> 33 us  [over(): lax.ppermute(block, axes, [(i, j) for i, j in route if j is not None and...]
  transfers between devices with their start and end apart: 30 -> 29, of which waited for: 10 -> 14; matrix products, arithmetic and copies ran while one was open for 0% -> 0% of each run, Pallas kernels for 24% -> 25%
where the time goes in v16:
time: 109 us; the launch traced here: 107 us
  starting transfers between devices  40.8 us (37%)
  waiting for transfers between devices  33 us (30%)
  Pallas kernels  31.1 us (29%)
  local copies, waits for them, and re-layouts  1.86 us (2%)
    ppermute x29, starting transfers between devices, over(): lax.ppermute(block, axes, [(i, j) for i, j in route if j is not None and...  40.8 us
    ppermute x29, waiting for transfers between devices, over(): lax.ppermute(block, axes, [(i, j) for i, j in route if j is not None and...  33 us
    pallas_call x24, Pallas kernels, call(): pl.pallas_call(body, out_shape=shapes, in_specs=specs, out_specs=[vmem] *...  29.2 us
  transfers between devices with their start and end apart: 29, of which 14 were waited for; matrix products, arithmetic and copies ran while one was open for 0% of the time, Pallas kernels for 25%

profile of v16, /device:TPU:13, one launch (start us, length us, event | category | flops | bytes accessed | tf_op | source)
XLA Modules:
  0.0 107.3 jit_solution(2432009574988878544)
XLA Ops:
  0.1 1.7 %copy-done = bf16[64,20480]{1,0:T(8,128)(2,1)S(1)} copy-done((bf16[64,20480]{1,0:T(8,128)(2,1)S(1)}, bf16[64,20480]{1,0:T(8,128)(2,1)}, u32[]{:S(2)}) %copy-start) | copy-done | bytes 2621464
  2.8 1.3 %pack.1 = (bf16[64,8448]{1,0:T(8,128)(2,1)S(1)}, bf16[16,10240]{1,0:T(8,128)(2,1)S(1)}) custom-call(s32[5]{0:T(128)S(1)} %stack.23.place, bf16[64,20480]{1,0:T(8,128)(2,1)S(1)} %copy-done, bf16[64,256]{1,0:T(8,128)(2,1)S(1)} %copy-done.2, bf16[64,4096]{1,0:T(8,128)(2,1)S(1)} %pack_first.1.order), custom_call_target="tpu_custom_call" | custom-call | flops 1 | bytes 1 | tf_op jit(solution)/shard_map/pack/pallas_call | solution.py:663
  5.0 3.0 %collective-permute-done.got_first.got.edges = bf16[64,4096]{1,0:T(8,128)(2,1)S(1)} collective-permute-done((bf16[64,4096]{1,0:T(8,128)(2,1)S(1)}, bf16[64,4096]{1,0:T(8,128)(2,1)S(1)}, u32[]{:S(2)}, u32[]{:S(2)}) %collective-permute-start) | collective-permute-done | bytes 524320 | tf_op jit(solution)/shard_map/ppermute | solution.py:688
  9.7 4.8 %collective-permute-start.2 = (bf16[128,512]{1,0:T(8,128)(2,1)S(1)}, bf16[128,512]{1,0:T(8,128)(2,1)S(1)}, u32[]{:S(2)}, u32[]{:S(2)}) collective-permute-start(bf16[128,512]{1,0:T(8,128)(2,1)S(1)} %get-tuple-element.64), channel_id=1, source_target_pairs={{0,2},{1,3},{2,0},{3,1},{4,6},{5,7},{6,4},{7,5},{8,10},{9,11},{10,... | collective-permute-start | bytes 393224 | tf_op jit(solution)/shard_map/ppermute | solution.py:688
  15.6 1.3 %collective-permute-start.6 = (bf16[128,384]{1,0:T(8,128)(2,1)S(1)}, bf16[128,384]{1,0:T(8,128)(2,1)S(1)}, u32[]{:S(2)}, u32[]{:S(2)}) collective-permute-start(bf16[128,384]{1,0:T(8,128)(2,1)S(1)} %get-tuple-element.71), channel_id=1, source_target_pairs={{0,1},{1,0},{2,3},{3,2},{4,5},{5,4},{6,7},{7,6},{8,9},{9,8},{10,11... | collective-permute-start | bytes 294920 | tf_op jit(solution)/shard_map/ppermute | solution.py:688
  16.9 1.7 %collective-permute-start.7 = (bf16[128,384]{1,0:T(8,128)(2,1)S(1)}, bf16[128,384]{1,0:T(8,128)(2,1)S(1)}, u32[]{:S(2)}, u32[]{:S(2)}) collective-permute-start(bf16[128,384]{1,0:T(8,128)(2,1)S(1)} %get-tuple-element.72), channel_id=1, source_target_pairs={{0,2},{1,3},{2,0},{3,1},{4,6},{5,7},{6,4},{7,5},{8,10},{9,11},{10,... | collective-permute-start | bytes 294920 | tf_op jit(solution)/shard_map/ppermute | solution.py:688
  19.7 6.3 %collective-permute-done.2.refs_2_.refs_4_ = bf16[128,512]{1,0:T(8,128)(2,1)S(1)} collective-permute-done((bf16[128,512]{1,0:T(8,128)(2,1)S(1)}, bf16[128,512]{1,0:T(8,128)(2,1)S(1)}, u32[]{:S(2)}, u32[]{:S(2)}) %collective-permute-start.2) | collective-permute-done | bytes 131104 | tf_op jit(solution)/shard_map/ppermute | solution.py:688
  26.0 3.0 %collective-permute-done.3.refs_3_.refs_5_ = bf16[128,512]{1,0:T(8,128)(2,1)S(1)} collective-permute-done((bf16[128,512]{1,0:T(8,128)(2,1)S(1)}, bf16[128,512]{1,0:T(8,128)(2,1)S(1)}, u32[]{:S(2)}, u32[]{:S(2)}) %collective-permute-start.3) | collective-permute-done | bytes 131104 | tf_op jit(solution)/shard_map/ppermute | solution.py:688
  29.0 2.1 %collective-permute-done.7.refs_2_.refs_7_ = bf16[128,384]{1,0:T(8,128)(2,1)S(1)} collective-permute-done((bf16[128,384]{1,0:T(8,128)(2,1)S(1)}, bf16[128,384]{1,0:T(8,128)(2,1)S(1)}, u32[]{:S(2)}, u32[]{:S(2)}) %collective-permute-start.7) | collective-permute-done | bytes 98336 | tf_op jit(solution)/shard_map/ppermute | solution.py:688
  31.1 2.1 %collective-permute-done.8.refs_3_.refs_8_ = bf16[128,384]{1,0:T(8,128)(2,1)S(1)} collective-permute-done((bf16[128,384]{1,0:T(8,128)(2,1)S(1)}, bf16[128,384]{1,0:T(8,128)(2,1)S(1)}, u32[]{:S(2)}, u32[]{:S(2)}) %collective-permute-start.8) | collective-permute-done | bytes 98336 | tf_op jit(solution)/shard_map/ppermute | solution.py:688
  33.2 3.4 %collective-permute-start.13 = (bf16[128,768]{1,0:T(8,128)(2,1)S(1)}, bf16[128,768]{1,0:T(8,128)(2,1)S(1)}, u32[]{:S(2)}, u32[]{:S(2)}) collective-permute-start(bf16[128,768]{1,0:T(8,128)(2,1)S(1)} %get-tuple-element.89), channel_id=1, source_target_pairs={{0,2},{1,3},{2,0},{3,1},{4,6},{5,7},{6,4},{7,5},{8,10},{9,11},{10,... | collective-permute-start | bytes 589832 | tf_op jit(solution)/shard_map/ppermute | solution.py:688
  37.3 1.7 %prep.1 = (bf16[512,256]{1,0:T(8,128)(2,1)S(1)}, f32[4,2560]{1,0:T(4,128)S(1)}, f32[512,128]{1,0:T(8,128)S(1)}, f32[128,512]{1,0:T(8,128)S(1)}, bf16[512,256]{1,...) custom-call(s32[5]{0:T(128)S(1)} %stack.23.place, ...), custom_call_target="tpu_custom_call" | custom-call | flops 1 | bytes 1 | tf_op jit(solution)/shard_map/prep/pallas_call | solution.py:663
  39.0 2.1 %state.4 = (bf16[512,512]{1,0:T(8,128)(2,1)S(1)}, f32[256,512]{1,0:T(8,128)S(1)}, bf16[272,256]{1,0:T(8,128)(2,1)S(1)}, bf16[272,256]{1,0:T(8,128)(2,1)S(1)}) custom-call(s32[5]{0:T(128)S(1)} %stack.23.place, bf16[128,512]{1,0:T(8,128)(2,1)S(1)} %get-tuple-element.62.refs_0_, bf16[128,512]{1,0:T(8,128)(2,1)S(1)} %collective-permute-done.1.refs_1_.refs_3_, ...), custom_call_target="tpu_custom_call" | custom-call | flops 1 | bytes 1 | tf_op jit(solution)/shard_map/state/pallas_call | solution.py:663
  41.1 2.3 %collective-permute-start.10 = (bf16[272,256]{1,0:T(8,128)(2,1)S(1)}, bf16[272,256]{1,0:T(8,128)(2,1)S(1)}, u32[]{:S(2)}, u32[]{:S(2)}) collective-permute-start(bf16[272,256]{1,0:T(8,128)(2,1)S(1)} %get-tuple-element.80.refs_3_.refs_1_), channel_id=1, source_target_pairs={{0,8},{1,9},{2,10},{3,11},{4,12},{5,13},{6,14},{7,15},{8,0},{9,1},... | collective-permute-start | bytes 417800 | tf_op jit(solution)/shard_map/ppermute | solution.py:688
  45.4 2.5 %collective-permute-done.9.refs_0_ = bf16[272,256]{1,0:T(8,128)(2,1)S(1)} collective-permute-done((bf16[272,256]{1,0:T(8,128)(2,1)S(1)}, bf16[272,256]{1,0:T(8,128)(2,1)S(1)}, u32[]{:S(2)}, u32[]{:S(2)}) %collective-permute-start.9) | collective-permute-done | bytes 139296 | tf_op jit(solution)/shard_map/ppermute | solution.py:688
  50.9 4.4 %collective-permute-start.15 = (bf16[128,1024]{1,0:T(8,128)(2,1)S(1)}, bf16[128,1024]{1,0:T(8,128)(2,1)S(1)}, u32[]{:S(2)}, u32[]{:S(2)}) collective-permute-start(bf16[128,1024]{1,0:T(8,128)(2,1)S(1)} %get-tuple-element.91), channel_id=1, source_target_pairs={{0,2},{1,3},{2,0},{3,1},{4,6},{5,7},{6,4},{7,5},{8,10},{9,11},{10,... | collective-permute-start | bytes 786440 | tf_op jit(solution)/shard_map/ppermute | solution.py:688
  55.3 2.2 %collective-permute-start.16 = (bf16[128,1024]{1,0:T(8,128)(2,1)S(1)}, bf16[128,1024]{1,0:T(8,128)(2,1)S(1)}, u32[]{:S(2)}, u32[]{:S(2)}) collective-permute-start(bf16[128,1024]{1,0:T(8,128)(2,1)S(1)} %get-tuple-element.92), channel_id=1, source_target_pairs={{0,3},{1,2},{2,1},{3,0},{4,7},{5,6},{6,5},{7,4},{8,11},{9,10},{10,... | collective-permute-start | bytes 786440 | tf_op jit(solution)/shard_map/ppermute | solution.py:688
  57.5 2.6 %state.5 = (bf16[512,768]{1,0:T(8,128)(2,1)S(1)}, f32[256,768]{1,0:T(8,128)S(1)}, bf16[272,384]{1,0:T(8,128)(2,1)S(1)}, bf16[272,384]{1,0:T(8,128)(2,1)S(1)}) custom-call(s32[5]{0:T(128)S(1)} %stack.23.place, bf16[128,768]{1,0:T(8,128)(2,1)S(1)} %get-tuple-element.74.refs_9_.refs_0_, bf16[128,1792]{1,0:T(8,128)(2,1)S(1)} %collective-permute-done.12.refs_2_.refs_1_, ...), custom_call_target="tpu_custom_call" | custom-call | flops 1 | bytes 1 | tf_op jit(solution)/shard_map/state/pallas_call | solution.py:663
  60.1 1.9 %collective-permute-start.17 = (bf16[272,384]{1,0:T(8,128)(2,1)S(1)}, bf16[272,384]{1,0:T(8,128)(2,1)S(1)}, u32[]{:S(2)}, u32[]{:S(2)}) collective-permute-start(bf16[272,384]{1,0:T(8,128)(2,1)S(1)} %get-tuple-element.93.refs_1_), channel_id=1, source_target_pairs={{0,8},{1,9},{2,10},{3,11},{4,12},{5,13},{6,14},{7,15},{8,0},{9,1},... | collective-permute-start | bytes 626696 | tf_op jit(solution)/shard_map/ppermute | solution.py:688
  63.3 1.4 %collective-permute-done.17.refs_0_ = bf16[272,384]{1,0:T(8,128)(2,1)S(1)} collective-permute-done((bf16[272,384]{1,0:T(8,128)(2,1)S(1)}, bf16[272,384]{1,0:T(8,128)(2,1)S(1)}, u32[]{:S(2)}, u32[]{:S(2)}) %collective-permute-start.17) | collective-permute-done | bytes 208928 | tf_op jit(solution)/shard_map/ppermute | solution.py:688
  66.6 1.9 %collective-permute-done.18.refs_0_.refs_1_ = bf16[272,384]{1,0:T(8,128)(2,1)S(1)} collective-permute-done((bf16[272,384]{1,0:T(8,128)(2,1)S(1)}, bf16[272,384]{1,0:T(8,128)(2,1)S(1)}, u32[]{:S(2)}, u32[]{:S(2)}) %collective-permute-start.18) | collective-permute-done | bytes 208928 | tf_op jit(solution)/shard_map/ppermute | solution.py:688
  70.5 1.4 %collective-permute-done.15.refs_2_ = bf16[128,1024]{1,0:T(8,128)(2,1)S(1)} collective-permute-done((bf16[128,1024]{1,0:T(8,128)(2,1)S(1)}, bf16[128,1024]{1,0:T(8,128)(2,1)S(1)}, u32[]{:S(2)}, u32[]{:S(2)}) %collective-permute-start.15) | collective-permute-done | bytes 262176 | tf_op jit(solution)/shard_map/ppermute | solution.py:688
  71.8 7.1 %collective-permute-done.16.refs_3_ = bf16[128,1024]{1,0:T(8,128)(2,1)S(1)} collective-permute-done((bf16[128,1024]{1,0:T(8,128)(2,1)S(1)}, bf16[128,1024]{1,0:T(8,128)(2,1)S(1)}, u32[]{:S(2)}, u32[]{:S(2)}) %collective-permute-start.16) | collective-permute-done | bytes 262176 | tf_op jit(solution)/shard_map/ppermute | solution.py:688
  79.0 1.9 %state.6 = (bf16[512,384]{1,0:T(8,128)(2,1)S(1)}, f32[256,384]{1,0:T(8,128)S(1)}, bf16[272,384]{1,0:T(8,128)(2,1)S(1)}) custom-call(s32[5]{0:T(128)S(1)} %stack.23.place, bf16[128,1024]{1,0:T(8,128)(2,1)S(1)} %get-tuple-element.82.refs_0_, bf16[128,1792]{1,0:T(8,128)(2,1)S(1)} %collective-permute-done.12.refs_2_.refs_1_, ...), custom_call_target="tpu_custom_call" | custom-call | flops 1 | bytes 1 | tf_op jit(solution)/shard_map/state/pallas_call | solution.py:663
  80.9 1.9 %collective-permute-start.22 = (bf16[272,384]{1,0:T(8,128)(2,1)S(1)}, bf16[272,384]{1,0:T(8,128)(2,1)S(1)}, u32[]{:S(2)}, u32[]{:S(2)}) collective-permute-start(bf16[272,384]{1,0:T(8,128)(2,1)S(1)} %get-tuple-element.95.refs_10_.refs_1_), channel_id=1, source_target_pairs={{0,8},{1,9},{2,10},{3,11},{4,12},{5,13},{6,14},{7,15},{8,0},{9,1},... | collective-permute-start | bytes 626696 | tf_op jit(solution)/shard_map/ppermute | solution.py:688
  82.8 1.9 %state.7 = (bf16[512,384]{1,0:T(8,128)(2,1)S(1)}, f32[256,384]{1,0:T(8,128)S(1)}, bf16[272,384]{1,0:T(8,128)(2,1)S(1)}) custom-call(s32[5]{0:T(128)S(1)} %stack.23.place, bf16[128,1024]{1,0:T(8,128)(2,1)S(1)} %get-tuple-element.82.refs_0_, bf16[128,1792]{1,0:T(8,128)(2,1)S(1)} %collective-permute-done.12.refs_2_.refs_1_, ...), custom_call_target="tpu_custom_call" | custom-call | flops 1 | bytes 1 | tf_op jit(solution)/shard_map/state/pallas_call | solution.py:663
  87.9 1.5 %collective-permute-start.23 = (bf16[272,384]{1,0:T(8,128)(2,1)S(1)}, bf16[272,384]{1,0:T(8,128)(2,1)S(1)}, u32[]{:S(2)}, u32[]{:S(2)}) collective-permute-start(bf16[272,384]{1,0:T(8,128)(2,1)S(1)} %combine.8.refs_12_), channel_id=1, source_target_pairs={{0,16},{1,17},{2,18},{3,19},{4,20},{5,21},{6,22},{7,23},{8,24},{9,... | collective-permute-start | bytes 626696 | tf_op jit(solution)/shard_map/ppermute | solution.py:688
  89.3 2.6 %final.4 = (bf16[256,768]{1,0:T(8,128)(2,1)S(1)}, bf16[256,768]{1,0:T(8,128)(2,1)S(1)}) custom-call(s32[5]{0:T(128)S(1)} %stack.23.place, bf16[272,384]{1,0:T(8,128)(2,1)S(1)} %collective-permute-done.17.refs_0_, bf16[272,384]{1,0:T(8,128)(2,1)S(1)} %collective-permute-done.18.refs_0_.refs_1_, bf16[272,384]{1,0:T(8,128)(2,1)S(1)} %collective-permute-done.19.refs_9_.refs_2_, ...), custom_call_target="tpu_custom_call" | custom-call | flops 1 | bytes 1 | tf_op jit(solution)/shard_map/final/pallas_call | solution.py:663
  93.9 2.0 %collective-permute-start.26 = (bf16[256,768]{1,0:T(8,128)(2,1)S(1)}, bf16[256,768]{1,0:T(8,128)(2,1)S(1)}, u32[]{:S(2)}, u32[]{:S(2)}) collective-permute-start(bf16[256,768]{1,0:T(8,128)(2,1)S(1)} %get-tuple-element.114), channel_id=1, source_target_pairs={{0,4},{1,5},{2,6},{3,7},{4,0},{5,1},{6,2},{7,3},{8,12},{9,13},{10,... | collective-permute-start | bytes 1179656 | tf_op jit(solution)/shard_map/ppermute | solution.py:688
  95.9 1.9 %final.5 = (bf16[256,512]{1,0:T(8,128)(2,1)S(1)}, bf16[256,512]{1,0:T(8,128)(2,1)S(1)}) custom-call(s32[5]{0:T(128)S(1)} %stack.23.place, bf16[272,256]{1,0:T(8,128)(2,1)S(1)} %collective-permute-done.9.refs_0_, bf16[272,256]{1,0:T(8,128)(2,1)S(1)} %collective-permute-done.10.refs_1_, bf16[272,512]{1,0:T(8,128)(2,1)S(1)} %collective-permute-done.11.refs_12_.refs_2_, ...), custom_call_target="tpu_custom_call" | custom-call | flops 1 | bytes 1 | tf_op jit(solution)/shard_map/final/pallas_call | solution.py:663
  101.6 2.2 %collective-permute-start.28 = (bf16[256,384]{1,0:T(8,128)(2,1)S(1)}, bf16[256,384]{1,0:T(8,128)(2,1)S(1)}, u32[]{:S(2)}, u32[]{:S(2)}) collective-permute-start(bf16[256,384]{1,0:T(8,128)(2,1)S(1)} %get-tuple-element.116), channel_id=1, source_target_pairs={{0,4},{1,5},{2,6},{3,7},{4,0},{5,1},{6,2},{7,3},{8,12},{9,13},{10,... | collective-permute-start | bytes 589832 | tf_op jit(solution)/shard_map/ppermute | solution.py:688
  105.3 1.9 %place.1 = bf16[256,4096]{1,0:T(8,128)(2,1)} custom-call(s32[5]{0:T(128)S(1)} %stack.23.place, bf16[256,512]{1,0:T(8,128)(2,1)S(1)} %get-tuple-element.106.refs_0_, bf16[256,768]{1,0:T(8,128)(2,1)S(1)} %get-tuple-element.105.refs_2_.refs_1_, bf16[256,384]{1,0:T(8,128)(2,1)S(1)} %get-tuple-element.110.refs_6_.refs_2_, ...), custom_call_target="tpu_custom_call" | custom-call | flops 1 | bytes 1 | tf_op jit(solution)/shard_map/place/pallas_call | solution.py:625
  (70 shorter events, 26.9 us)
Async XLA Ops:
  4.1 10.4 %collective-permute-start.4 = (bf16[64,8448]{1,0:T(8,128)(2,1)S(1)}, bf16[64,8448]{1,0:T(8,128)(2,1)S(1)}, u32[]{:S(2)}, u32[]{:S(2)}) collective-permute-start(bf16[64,8448]{1,0:T(8,128)(2,1)S(1)} %get-tuple-element.66), channel_id=1, source_target_pairs={{0,4},{1,5},{2,6},{3,7},{4,0},{5,1},{6,2},{7,3},{8,12},{9,13},{10,... | collective-permute-start | bytes 3244040 | tf_op jit(solution)/shard_map/ppermute | solution.py:688
  4.9 3.1 %collective-permute-start = (bf16[64,4096]{1,0:T(8,128)(2,1)S(1)}, bf16[64,4096]{1,0:T(8,128)(2,1)S(1)}, u32[]{:S(2)}, u32[]{:S(2)}) collective-permute-start(bf16[64,4096]{1,0:T(8,128)(2,1)S(1)} %pack_first.1.order), channel_id=1, source_target_pairs={{0,4},{1,5},{2,6},{3,7},{4,0},{5,1},{6,2},{7,3},{8,12},{9,13},{10,... | collective-permute-start | bytes 1572872 | tf_op jit(solution)/shard_map/ppermute | solution.py:688
  8.8 9.8 %collective-permute-start.1 = (bf16[128,512]{1,0:T(8,128)(2,1)S(1)}, bf16[128,512]{1,0:T(8,128)(2,1)S(1)}, u32[]{:S(2)}, u32[]{:S(2)}) collective-permute-start(bf16[128,512]{1,0:T(8,128)(2,1)S(1)} %get-tuple-element.63), channel_id=1, source_target_pairs={{0,1},{1,0},{2,3},{3,2},{4,5},{5,4},{6,7},{7,6},{8,9},{9,8},{10,11... | collective-permute-start | bytes 393224 | tf_op jit(solution)/shard_map/ppermute | solution.py:688
  9.0 5.5 %collective-permute-start.5 = (bf16[3,10240]{1,0:T(4,128)(2,1)S(1)}, bf16[3,10240]{1,0:T(4,128)(2,1)S(1)}, u32[]{:S(2)}, u32[]{:S(2)}) collective-permute-start(bf16[3,10240]{1,0:T(4,128)(2,1)S(1)} %get-tuple-element.69), channel_id=1, source_target_pairs={{3,11},{7,15},{11,19},{15,23},{19,27},{23,31}} | collective-permute-start | bytes 184328 | tf_op jit(solution)/shard_map/ppermute | solution.py:688
  9.7 16.3 %collective-permute-start.2 = (bf16[128,512]{1,0:T(8,128)(2,1)S(1)}, bf16[128,512]{1,0:T(8,128)(2,1)S(1)}, u32[]{:S(2)}, u32[]{:S(2)}) collective-permute-start(bf16[128,512]{1,0:T(8,128)(2,1)S(1)} %get-tuple-element.64), channel_id=1, source_target_pairs={{0,2},{1,3},{2,0},{3,1},{4,6},{5,7},{6,4},{7,5},{8,10},{9,11},{10,... | collective-permute-start | bytes 393224 | tf_op jit(solution)/shard_map/ppermute | solution.py:688
  14.5 14.5 %collective-permute-start.3 = (bf16[128,512]{1,0:T(8,128)(2,1)S(1)}, bf16[128,512]{1,0:T(8,128)(2,1)S(1)}, u32[]{:S(2)}, u32[]{:S(2)}) collective-permute-start(bf16[128,512]{1,0:T(8,128)(2,1)S(1)} %get-tuple-element.65), channel_id=1, source_target_pairs={{0,3},{1,2},{2,1},{3,0},{4,7},{5,6},{6,5},{7,4},{8,11},{9,10},{10,... | collective-permute-start | bytes 393224 | tf_op jit(solution)/shard_map/ppermute | solution.py:688
  15.6 13.4 %collective-permute-start.6 = (bf16[128,384]{1,0:T(8,128)(2,1)S(1)}, bf16[128,384]{1,0:T(8,128)(2,1)S(1)}, u32[]{:S(2)}, u32[]{:S(2)}) collective-permute-start(bf16[128,384]{1,0:T(8,128)(2,1)S(1)} %get-tuple-element.71), channel_id=1, source_target_pairs={{0,1},{1,0},{2,3},{3,2},{4,5},{5,4},{6,7},{7,6},{8,9},{9,8},{10,11... | collective-permute-start | bytes 294920 | tf_op jit(solution)/shard_map/ppermute | solution.py:688
  16.9 14.2 %collective-permute-start.7 = (bf16[128,384]{1,0:T(8,128)(2,1)S(1)}, bf16[128,384]{1,0:T(8,128)(2,1)S(1)}, u32[]{:S(2)}, u32[]{:S(2)}) collective-permute-start(bf16[128,384]{1,0:T(8,128)(2,1)S(1)} %get-tuple-element.72), channel_id=1, source_target_pairs={{0,2},{1,3},{2,0},{3,1},{4,6},{5,7},{6,4},{7,5},{8,10},{9,11},{10,... | collective-permute-start | bytes 294920 | tf_op jit(solution)/shard_map/ppermute | solution.py:688
  18.6 14.6 %collective-permute-start.8 = (bf16[128,384]{1,0:T(8,128)(2,1)S(1)}, bf16[128,384]{1,0:T(8,128)(2,1)S(1)}, u32[]{:S(2)}, u32[]{:S(2)}) collective-permute-start(bf16[128,384]{1,0:T(8,128)(2,1)S(1)} %get-tuple-element.73), channel_id=1, source_target_pairs={{0,3},{1,2},{2,1},{3,0},{4,7},{5,6},{6,5},{7,4},{8,11},{9,10},{10,... | collective-permute-start | bytes 294920 | tf_op jit(solution)/shard_map/ppermute | solution.py:688
  18.8 17.8 %copy-start.3 = (f32[4,20480]{1,0:T(4,128)S(1)}, f32[4,20480]{1,0:T(4,128)}, u32[]{:S(2)}) copy-start(f32[4,20480]{1,0:T(4,128)} %weight.1) | copy-start | bytes 983044
  18.8 17.8 %copy-start.4 = (f32[20480]{0:T(1024)S(1)}, f32[20480]{0:T(1024)}, u32[]{:S(2)}) copy-start(f32[20480]{0:T(1024)} %param.10) | copy-start | bytes 245764
  19.7 17.6 %copy-start.5 = (f32[256]{0:T(256)S(1)}, f32[256]{0:T(256)}, u32[]{:S(2)}) copy-start(f32[256]{0:T(256)} %param.11) | copy-start | bytes 3076
  33.2 17.7 %collective-permute-start.12 = (bf16[128,1792]{1,0:T(8,128)(2,1)S(1)}, bf16[128,1792]{1,0:T(8,128)(2,1)S(1)}, u32[]{:S(2)}, u32[]{:S(2)}) collective-permute-start(bf16[128,1792]{1,0:T(8,128)(2,1)S(1)} %get-tuple-element.86), channel_id=1, source_target_pairs={{0,1},{1,0},{2,3},{3,2},{4,5},{5,4},{6,7},{7,6},{8,9},{9,8},{10,11... | collective-permute-start | bytes 1376264 | tf_op jit(solution)/shard_map/ppermute | solution.py:688
  33.2 17.7 %collective-permute-start.13 = (bf16[128,768]{1,0:T(8,128)(2,1)S(1)}, bf16[128,768]{1,0:T(8,128)(2,1)S(1)}, u32[]{:S(2)}, u32[]{:S(2)}) collective-permute-start(bf16[128,768]{1,0:T(8,128)(2,1)S(1)} %get-tuple-element.89), channel_id=1, source_target_pairs={{0,2},{1,3},{2,0},{3,1},{4,6},{5,7},{6,4},{7,5},{8,10},{9,11},{10,... | collective-permute-start | bytes 589832 | tf_op jit(solution)/shard_map/ppermute | solution.py:688
  36.6 14.3 %collective-permute-start.14 = (bf16[128,768]{1,0:T(8,128)(2,1)S(1)}, bf16[128,768]{1,0:T(8,128)(2,1)S(1)}, u32[]{:S(2)}, u32[]{:S(2)}) collective-permute-start(bf16[128,768]{1,0:T(8,128)(2,1)S(1)} %get-tuple-element.90), channel_id=1, source_target_pairs={{0,3},{1,2},{2,1},{3,0},{4,7},{5,6},{6,5},{7,4},{8,11},{9,10},{10,... | collective-permute-start | bytes 589832 | tf_op jit(solution)/shard_map/ppermute | solution.py:688
  41.1 4.3 %collective-permute-start.10 = (bf16[272,256]{1,0:T(8,128)(2,1)S(1)}, bf16[272,256]{1,0:T(8,128)(2,1)S(1)}, u32[]{:S(2)}, u32[]{:S(2)}) collective-permute-start(bf16[272,256]{1,0:T(8,128)(2,1)S(1)} %get-tuple-element.80.refs_3_.refs_1_), channel_id=1, source_target_pairs={{0,8},{1,9},{2,10},{3,11},{4,12},{5,13},{6,14},{7,15},{8,0},{9,1},... | collective-permute-start | bytes 417800 | tf_op jit(solution)/shard_map/ppermute | solution.py:688
  43.4 4.5 %collective-permute-start.9 = (bf16[272,256]{1,0:T(8,128)(2,1)S(1)}, bf16[272,256]{1,0:T(8,128)(2,1)S(1)}, u32[]{:S(2)}, u32[]{:S(2)}) collective-permute-start(bf16[272,256]{1,0:T(8,128)(2,1)S(1)} %get-tuple-element.79.refs_2_.refs_0_), channel_id=1, source_target_pairs={{0,8},{1,9},{2,10},{3,11},{4,12},{5,13},{6,14},{7,15},{8,0},{9,1},... | collective-permute-start | bytes 417800 | tf_op jit(solution)/shard_map/ppermute | solution.py:688
  48.6 21.9 %collective-permute-start.11 = (bf16[272,512]{1,0:T(8,128)(2,1)S(1)}, bf16[272,512]{1,0:T(8,128)(2,1)S(1)}, u32[]{:S(2)}, u32[]{:S(2)}) collective-permute-start(bf16[272,512]{1,0:T(8,128)(2,1)S(1)} %combine.5.refs_10_), channel_id=1, source_target_pairs={{0,16},{1,17},{2,18},{3,19},{4,20},{5,21},{6,22},{7,23},{8,24},{9,... | collective-permute-start | bytes 835592 | tf_op jit(solution)/shard_map/ppermute | solution.py:688
  50.9 20.9 %collective-permute-start.15 = (bf16[128,1024]{1,0:T(8,128)(2,1)S(1)}, bf16[128,1024]{1,0:T(8,128)(2,1)S(1)}, u32[]{:S(2)}, u32[]{:S(2)}) collective-permute-start(bf16[128,1024]{1,0:T(8,128)(2,1)S(1)} %get-tuple-element.91), channel_id=1, source_target_pairs={{0,2},{1,3},{2,0},{3,1},{4,6},{5,7},{6,4},{7,5},{8,10},{9,11},{10,... | collective-permute-start | bytes 786440 | tf_op jit(solution)/shard_map/ppermute | solution.py:688
  55.3 23.6 %collective-permute-start.16 = (bf16[128,1024]{1,0:T(8,128)(2,1)S(1)}, bf16[128,1024]{1,0:T(8,128)(2,1)S(1)}, u32[]{:S(2)}, u32[]{:S(2)}) collective-permute-start(bf16[128,1024]{1,0:T(8,128)(2,1)S(1)} %get-tuple-element.92), channel_id=1, source_target_pairs={{0,3},{1,2},{2,1},{3,0},{4,7},{5,6},{6,5},{7,4},{8,11},{9,10},{10,... | collective-permute-start | bytes 786440 | tf_op jit(solution)/shard_map/ppermute | solution.py:688
  60.1 4.6 %collective-permute-start.17 = (bf16[272,384]{1,0:T(8,128)(2,1)S(1)}, bf16[272,384]{1,0:T(8,128)(2,1)S(1)}, u32[]{:S(2)}, u32[]{:S(2)}) collective-permute-start(bf16[272,384]{1,0:T(8,128)(2,1)S(1)} %get-tuple-element.93.refs_1_), channel_id=1, source_target_pairs={{0,8},{1,9},{2,10},{3,11},{4,12},{5,13},{6,14},{7,15},{8,0},{9,1},... | collective-permute-start | bytes 626696 | tf_op jit(solution)/shard_map/ppermute | solution.py:688
  62.0 6.5 %collective-permute-start.18 = (bf16[272,384]{1,0:T(8,128)(2,1)S(1)}, bf16[272,384]{1,0:T(8,128)(2,1)S(1)}, u32[]{:S(2)}, u32[]{:S(2)}) collective-permute-start(bf16[272,384]{1,0:T(8,128)(2,1)S(1)} %get-tuple-element.94.refs_1_), channel_id=1, source_target_pairs={{0,8},{1,9},{2,10},{3,11},{4,12},{5,13},{6,14},{7,15},{8,0},{9,1},... | collective-permute-start | bytes 626696 | tf_op jit(solution)/shard_map/ppermute | solution.py:688
  65.3 20.7 %collective-permute-start.19 = (bf16[272,384]{1,0:T(8,128)(2,1)S(1)}, bf16[272,384]{1,0:T(8,128)(2,1)S(1)}, u32[]{:S(2)}, u32[]{:S(2)}) collective-permute-start(bf16[272,384]{1,0:T(8,128)(2,1)S(1)} %combine.6.refs_2_.refs_10_), channel_id=1, source_target_pairs={{0,16},{1,17},{2,18},{3,19},{4,20},{5,21},{6,22},{7,23},{8,24},{9,... | collective-permute-start | bytes 626696 | tf_op jit(solution)/shard_map/ppermute | solution.py:688
  69.2 16.9 %collective-permute-start.20 = (bf16[272,384]{1,0:T(8,128)(2,1)S(1)}, bf16[272,384]{1,0:T(8,128)(2,1)S(1)}, u32[]{:S(2)}, u32[]{:S(2)}) collective-permute-start(bf16[272,384]{1,0:T(8,128)(2,1)S(1)} %combine.7.refs_11_), channel_id=1, source_target_pairs={{0,16},{1,17},{2,18},{3,19},{4,20},{5,21},{6,22},{7,23},{8,24},{9,... | collective-permute-start | bytes 626696 | tf_op jit(solution)/shard_map/ppermute | solution.py:688
  80.9 6.3 %collective-permute-start.22 = (bf16[272,384]{1,0:T(8,128)(2,1)S(1)}, bf16[272,384]{1,0:T(8,128)(2,1)S(1)}, u32[]{:S(2)}, u32[]{:S(2)}) collective-permute-start(bf16[272,384]{1,0:T(8,128)(2,1)S(1)} %get-tuple-element.95.refs_10_.refs_1_), channel_id=1, source_target_pairs={{0,8},{1,9},{2,10},{3,11},{4,12},{5,13},{6,14},{7,15},{8,0},{9,1},... | collective-permute-start | bytes 626696 | tf_op jit(solution)/shard_map/ppermute | solution.py:688
  84.7 7.2 %collective-permute-start.21 = (bf16[272,384]{1,0:T(8,128)(2,1)S(1)}, bf16[272,384]{1,0:T(8,128)(2,1)S(1)}, u32[]{:S(2)}, u32[]{:S(2)}) collective-permute-start(bf16[272,384]{1,0:T(8,128)(2,1)S(1)} %get-tuple-element.96.refs_8_.refs_1_), channel_id=1, source_target_pairs={{0,8},{1,9},{2,10},{3,11},{4,12},{5,13},{6,14},{7,15},{8,0},{9,1},... | collective-permute-start | bytes 626696 | tf_op jit(solution)/shard_map/ppermute | solution.py:688
  87.9 11.6 %collective-permute-start.23 = (bf16[272,384]{1,0:T(8,128)(2,1)S(1)}, bf16[272,384]{1,0:T(8,128)(2,1)S(1)}, u32[]{:S(2)}, u32[]{:S(2)}) collective-permute-start(bf16[272,384]{1,0:T(8,128)(2,1)S(1)} %combine.8.refs_12_), channel_id=1, source_target_pairs={{0,16},{1,17},{2,18},{3,19},{4,20},{5,21},{6,22},{7,23},{8,24},{9,... | collective-permute-start | bytes 626696 | tf_op jit(solution)/shard_map/ppermute | solution.py:688
  92.6 7.9 %collective-permute-start.24 = (bf16[272,384]{1,0:T(8,128)(2,1)S(1)}, bf16[272,384]{1,0:T(8,128)(2,1)S(1)}, u32[]{:S(2)}, u32[]{:S(2)}) collective-permute-start(bf16[272,384]{1,0:T(8,128)(2,1)S(1)} %combine.9.refs_11_), channel_id=1, source_target_pairs={{0,16},{1,17},{2,18},{3,19},{4,20},{5,21},{6,22},{7,23},{8,24},{9,... | collective-permute-start | bytes 626696 | tf_op jit(solution)/shard_map/ppermute | solution.py:688
  93.9 10.0 %collective-permute-start.26 = (bf16[256,768]{1,0:T(8,128)(2,1)S(1)}, bf16[256,768]{1,0:T(8,128)(2,1)S(1)}, u32[]{:S(2)}, u32[]{:S(2)}) collective-permute-start(bf16[256,768]{1,0:T(8,128)(2,1)S(1)} %get-tuple-element.114), channel_id=1, source_target_pairs={{0,4},{1,5},{2,6},{3,7},{4,0},{5,1},{6,2},{7,3},{8,12},{9,13},{10,... | collective-permute-start | bytes 1179656 | tf_op jit(solution)/shard_map/ppermute | solution.py:688
  97.8 6.1 %collective-permute-start.25 = (bf16[256,512]{1,0:T(8,128)(2,1)S(1)}, bf16[256,512]{1,0:T(8,128)(2,1)S(1)}, u32[]{:S(2)}, u32[]{:S(2)}) collective-permute-start(bf16[256,512]{1,0:T(8,128)(2,1)S(1)} %get-tuple-element.113), channel_id=1, source_target_pairs={{0,4},{1,5},{2,6},{3,7},{4,0},{5,1},{6,2},{7,3},{8,12},{9,13},{10,... | collective-permute-start | bytes 786440 | tf_op jit(solution)/shard_map/ppermute | solution.py:688
  101.6 3.3 %collective-permute-start.28 = (bf16[256,384]{1,0:T(8,128)(2,1)S(1)}, bf16[256,384]{1,0:T(8,128)(2,1)S(1)}, u32[]{:S(2)}, u32[]{:S(2)}) collective-permute-start(bf16[256,384]{1,0:T(8,128)(2,1)S(1)} %get-tuple-element.116), channel_id=1, source_target_pairs={{0,4},{1,5},{2,6},{3,7},{4,0},{5,1},{6,2},{7,3},{8,12},{9,13},{10,... | collective-permute-start | bytes 589832 | tf_op jit(solution)/shard_map/ppermute | solution.py:688
  103.8 1.4 %collective-permute-start.27 = (bf16[256,384]{1,0:T(8,128)(2,1)S(1)}, bf16[256,384]{1,0:T(8,128)(2,1)S(1)}, u32[]{:S(2)}, u32[]{:S(2)}) collective-permute-start(bf16[256,384]{1,0:T(8,128)(2,1)S(1)} %get-tuple-element.115), channel_id=1, source_target_pairs={{0,4},{1,5},{2,6},{3,7},{4,0},{5,1},{6,2},{7,3},{8,12},{9,13},{10,... | collective-permute-start | bytes 589832 | tf_op jit(solution)/shard_map/ppermute | solution.py:688
  (5 other events, 53.0 us)

commit v17 on v16

--- a/solution.py
+++ b/solution.py
@@ -170,6 +170,10 @@
 SECOND_ROUND = ((512,), (384, 384), (384,), (384,))
 
 
+FLIP = (0, 2, 3, 1)
+NEAR = 3
+
+
 def halves(value, count):
     parts = []
     for _ in range(count):
@@ -216,7 +220,7 @@
     width = WIDTHS[0]
     copies = []
     for r in range(shards):
-        group = (shard ^ r) * PAIR + 1 - core
+        group = (shard ^ FLIP[r]) * PAIR + 1 - core
         copies.append((xbc.at[:, channels(group, 0, width)], send.at[:, r * width : (r + 1) * width]))
         last, rows = xbc.at[count - 16 :], slice(16 * r, 16 * r + 16)
         to = shards * width
@@ -238,14 +242,14 @@
     size = PER_GROUP + 2 * STATE
     copies = []
     for r in range(shards):
-        group = (shard ^ r) * PAIR + 1 - core
+        group = (shard ^ FLIP[r]) * PAIR + 1 - core
         copies.append((xbc.at[:, channels(group, first, width)], send.at[:, r * width : (r + 1) * width]))
         for i in range(2):
             to = rest + (i * shards + r) * STATE
             copies.append((xbc.at[:, ds(INNER + (i * GROUPS + group) * STATE, STATE)], send.at[:, to : to + STATE]))
     copies.append((dt_raw, send.at[:, send.shape[1] - HEADS :]))
     for r in range(shards):
-        group, to = (shard ^ r) * PAIR + core, r * size
+        group, to = (shard ^ FLIP[r]) * PAIR + core, r * size
         last = xbc.at[count - 16 :]
         copies.append((last.at[:, channels(group, 0, PER_GROUP)], tail.at[:, to : to + PER_GROUP]))
         for i in range(2):
@@ -297,7 +301,7 @@
     other = pl.ds(pl.multiple_of((1 - core) * count, count), count)
     copies, steps = [], []
     for out, (r, pieces) in zip(outs, plan):
-        group = (shard ^ r) * PAIR + core
+        group = (shard ^ FLIP[r]) * PAIR + core
         to = 0
         for piece in pieces:
             first, width = sum(WIDTHS[:piece]), WIDTHS[piece]
@@ -329,7 +333,7 @@
         per_tile = LANES * GROUPS // HEADS
         heads = HEADS // GROUPS
         for out, r, to in steps:
-            group = (shard ^ r) * PAIR + core
+            group = (shard ^ FLIP[r]) * PAIR + core
             tile, shift = group // per_tile, (LANES - (group % per_tile) * heads) % LANES
             own = dt_raw[:, ds(tile * LANES, LANES)].astype(F32)
             theirs = got[:, ds(got.shape[1] - HEADS + tile * LANES, LANES)].astype(F32)
@@ -353,7 +357,7 @@
 
 
 def view(refs, piece):
-    return [(ref, total_of(2) if piece == 3 and r == 1 else 0) for r, ref in enumerate(refs)]
+    return [(ref, total_of(2) if piece == 3 and r == NEAR else 0) for r, ref in enumerate(refs)]
 
 
 def convolve_in_order(place, blocks, columns, edge, tap, bias, wide, put):
@@ -362,7 +366,7 @@
     wide[5:8, :width] = edge
     for r, (block, origin) in enumerate(blocks):
         for core in range(PAIR):
-            at = pl.multiple_of((core * len(blocks) + (place[4] ^ r)) * count + 8, 8)
+            at = pl.multiple_of((core * len(blocks) + (place[4] ^ FLIP[r])) * count + 8, 8)
             part = block[core * count : (core + 1) * count, origin + columns.start : origin + columns.stop]
             wide[pl.ds(at, count), :width] = part.astype(F32)
     tap, bias = tap * 0.5, bias * 0.5
@@ -392,7 +396,7 @@
     for r, column in enumerate(columns):
         packed = column[:half]
         for j in range(2 * PAIR):
-            at = ((j // 2) * shards + (place[4] ^ r)) * count + (j % 2) * half
+            at = ((j // 2) * shards + (place[4] ^ FLIP[r])) * count + (j % 2) * half
             rows = packed if j == 0 else pltpu.roll(packed, LANES - j * heads, 1)
             dt_ref[pl.ds(pl.multiple_of(at, half), half), :] = rows
 
@@ -737,7 +741,7 @@
         )
 
     def travel(blocks):
-        return [blocks[0]] + [over(blocks[r], lambda i, r=r: i ^ r) for r in range(1, shards)]
+        return [blocks[0]] + [over(blocks[r], lambda i, r=r: i ^ FLIP[r]) for r in range(1, shards)]
 
     def plan(piece):
         return [(r, (piece,)) for r in range(shards)]
@@ -747,7 +751,7 @@
     edges = over(edges, lambda i: i + peers if i % shards == shards - 1 else None)
     second_blocks = send_on(plan(1), [first_blocks[0]], None, edges)
     message.append(travel(second_blocks))
-    third_plan = [(r, (2, 3) if r == 1 else (2,)) for r in range(shards)]
+    third_plan = [(r, (2, 3) if r == NEAR else (2,)) for r in range(shards)]
     third_blocks = send_on(third_plan, [second_blocks[0]])
     message.append(travel(third_blocks[:1] + gate(third_blocks[1:], message[0][1:] + message[1][1:])))
 
@@ -830,10 +834,10 @@
         )
 
     state_of(0, [])
-    own_block, *fourth_blocks = send_on([(r, (3,)) for r in range(shards) if r != 1], sent[0])
+    own_block, *fourth_blocks = send_on([(r, (3,)) for r in range(shards) if r != NEAR], sent[0])
     fourth_blocks = gate(fourth_blocks, message[2][1:])
-    fourth_blocks = [over(block, lambda i, r=r: i ^ r) for r, block in enumerate(fourth_blocks, 2)]
-    message.append([own_block, message[2][1], *fourth_blocks])
+    fourth_blocks = [over(block, lambda i, r=r: i ^ FLIP[r]) for r, block in enumerate(fourth_blocks, 1)]
+    message.append([own_block, *fourth_blocks, message[2][NEAR]])
     combine_of(0, [])
     state_of(1, joined[0])
     combine_of(1, [])

time: 109 us -> 108 us (level)
  waiting for transfers between devices: 33 us -> 29.2 us
  starting transfers between devices: 40.8 us -> 43.9 us
    ppermute x29, waiting for transfers between devices: 33 us -> 29.2 us  [over(): lax.ppermute(block, axes, [(i, j) for i, j in route if j is not None and...]
    ppermute x29, starting transfers between devices: 40.8 us -> 43.9 us  [over(): lax.ppermute(block, axes, [(i, j) for i, j in route if j is not None and...]
  transfers between devices with their start and end apart: 29 -> 29, of which waited for: 14 -> 13; matrix products, arithmetic and copies ran while one was open for 0% -> 0% of each run, Pallas kernels for 25% -> 25%
where the time goes in v17:
time: 108 us; the launch traced here: 107 us
  starting transfers between devices  43.9 us (41%)
  Pallas kernels  31.1 us (29%)
  waiting for transfers between devices  29.2 us (27%)
  local copies, waits for them, and re-layouts  1.86 us (2%)
    ppermute x29, starting transfers between devices, over(): lax.ppermute(block, axes, [(i, j) for i, j in route if j is not None and...  43.9 us
    pallas_call x24, Pallas kernels, call(): pl.pallas_call(body, out_shape=shapes, in_specs=specs, out_specs=[vmem] *...  29.2 us
    ppermute x29, waiting for transfers between devices, over(): lax.ppermute(block, axes, [(i, j) for i, j in route if j is not None and...  29.2 us
  transfers between devices with their start and end apart: 29, of which 13 were waited for; matrix products, arithmetic and copies ran while one was open for 0% of the time, Pallas kernels for 25%

profile of v17, /device:TPU:13, one launch (start us, length us, event | category | flops | bytes accessed | tf_op | source)
XLA Modules:
  0.0 106.6 jit_solution(10238464178605307034)
XLA Ops:
  0.1 1.7 %copy-done = bf16[64,20480]{1,0:T(8,128)(2,1)S(1)} copy-done((bf16[64,20480]{1,0:T(8,128)(2,1)S(1)}, bf16[64,20480]{1,0:T(8,128)(2,1)}, u32[]{:S(2)}) %copy-start) | copy-done | bytes 2621464
  2.8 1.3 %pack.1 = (bf16[64,8448]{1,0:T(8,128)(2,1)S(1)}, bf16[16,10240]{1,0:T(8,128)(2,1)S(1)}) custom-call(s32[5]{0:T(128)S(1)} %stack.23.place, bf16[64,20480]{1,0:T(8,128)(2,1)S(1)} %copy-done, bf16[64,256]{1,0:T(8,128)(2,1)S(1)} %copy-done.2, bf16[64,4096]{1,0:T(8,128)(2,1)S(1)} %pack_first.1.order), custom_call_target="tpu_custom_call" | custom-call | flops 1 | bytes 1 | tf_op jit(solution)/shard_map/pack/pallas_call | solution.py:667
  5.0 3.0 %collective-permute-done.got_first.got.edges = bf16[64,4096]{1,0:T(8,128)(2,1)S(1)} collective-permute-done((bf16[64,4096]{1,0:T(8,128)(2,1)S(1)}, bf16[64,4096]{1,0:T(8,128)(2,1)S(1)}, u32[]{:S(2)}, u32[]{:S(2)}) %collective-permute-start) | collective-permute-done | bytes 524320 | tf_op jit(solution)/shard_map/ppermute | solution.py:692
  8.8 2.4 %collective-permute-start.1 = (bf16[128,512]{1,0:T(8,128)(2,1)S(1)}, bf16[128,512]{1,0:T(8,128)(2,1)S(1)}, u32[]{:S(2)}, u32[]{:S(2)}) collective-permute-start(bf16[128,512]{1,0:T(8,128)(2,1)S(1)} %get-tuple-element.63), channel_id=1, source_target_pairs={{0,2},{1,3},{2,0},{3,1},{4,6},{5,7},{6,4},{7,5},{8,10},{9,11},{10,... | collective-permute-start | bytes 393224 | tf_op jit(solution)/shard_map/ppermute | solution.py:692
  11.9 3.7 %collective-permute-start.3 = (bf16[128,512]{1,0:T(8,128)(2,1)S(1)}, bf16[128,512]{1,0:T(8,128)(2,1)S(1)}, u32[]{:S(2)}, u32[]{:S(2)}) collective-permute-start(bf16[128,512]{1,0:T(8,128)(2,1)S(1)} %get-tuple-element.65), channel_id=1, source_target_pairs={{0,1},{1,0},{2,3},{3,2},{4,5},{5,4},{6,7},{7,6},{8,9},{9,8},{10,11... | collective-permute-start | bytes 393224 | tf_op jit(solution)/shard_map/ppermute | solution.py:692
  16.6 2.1 %collective-permute-start.6 = (bf16[128,384]{1,0:T(8,128)(2,1)S(1)}, bf16[128,384]{1,0:T(8,128)(2,1)S(1)}, u32[]{:S(2)}, u32[]{:S(2)}) collective-permute-start(bf16[128,384]{1,0:T(8,128)(2,1)S(1)} %get-tuple-element.71), channel_id=1, source_target_pairs={{0,2},{1,3},{2,0},{3,1},{4,6},{5,7},{6,4},{7,5},{8,10},{9,11},{10,... | collective-permute-start | bytes 294920 | tf_op jit(solution)/shard_map/ppermute | solution.py:692
  21.2 5.2 %collective-permute-done.2.refs_2_.refs_4_ = bf16[128,512]{1,0:T(8,128)(2,1)S(1)} collective-permute-done((bf16[128,512]{1,0:T(8,128)(2,1)S(1)}, bf16[128,512]{1,0:T(8,128)(2,1)S(1)}, u32[]{:S(2)}, u32[]{:S(2)}) %collective-permute-start.2) | collective-permute-done | bytes 131104 | tf_op jit(solution)/shard_map/ppermute | solution.py:692
  26.4 2.7 %collective-permute-done.6.refs_1_.refs_6_ = bf16[128,384]{1,0:T(8,128)(2,1)S(1)} collective-permute-done((bf16[128,384]{1,0:T(8,128)(2,1)S(1)}, bf16[128,384]{1,0:T(8,128)(2,1)S(1)}, u32[]{:S(2)}, u32[]{:S(2)}) %collective-permute-start.6) | collective-permute-done | bytes 98336 | tf_op jit(solution)/shard_map/ppermute | solution.py:692
  29.1 2.1 %collective-permute-done.7.refs_2_.refs_7_ = bf16[128,384]{1,0:T(8,128)(2,1)S(1)} collective-permute-done((bf16[128,384]{1,0:T(8,128)(2,1)S(1)}, bf16[128,384]{1,0:T(8,128)(2,1)S(1)}, u32[]{:S(2)}, u32[]{:S(2)}) %collective-permute-start.7) | collective-permute-done | bytes 98336 | tf_op jit(solution)/shard_map/ppermute | solution.py:692
  31.2 3.4 %collective-permute-start.12 = (bf16[128,768]{1,0:T(8,128)(2,1)S(1)}, bf16[128,768]{1,0:T(8,128)(2,1)S(1)}, u32[]{:S(2)}, u32[]{:S(2)}) collective-permute-start(bf16[128,768]{1,0:T(8,128)(2,1)S(1)} %get-tuple-element.88), channel_id=1, source_target_pairs={{0,2},{1,3},{2,0},{3,1},{4,6},{5,7},{6,4},{7,5},{8,10},{9,11},{10,... | collective-permute-start | bytes 589832 | tf_op jit(solution)/shard_map/ppermute | solution.py:692
  35.3 1.7 %prep.1 = (bf16[512,256]{1,0:T(8,128)(2,1)S(1)}, f32[4,2560]{1,0:T(4,128)S(1)}, f32[512,128]{1,0:T(8,128)S(1)}, f32[128,512]{1,0:T(8,128)S(1)}, bf16[512,256]{1,...) custom-call(s32[5]{0:T(128)S(1)} %stack.23.place, ...), custom_call_target="tpu_custom_call" | custom-call | flops 1 | bytes 1 | tf_op jit(solution)/shard_map/prep/pallas_call | solution.py:667
  37.0 2.1 %state.4 = (bf16[512,512]{1,0:T(8,128)(2,1)S(1)}, f32[256,512]{1,0:T(8,128)S(1)}, bf16[272,256]{1,0:T(8,128)(2,1)S(1)}, bf16[272,256]{1,0:T(8,128)(2,1)S(1)}) custom-call(s32[5]{0:T(128)S(1)} %stack.23.place, bf16[128,512]{1,0:T(8,128)(2,1)S(1)} %get-tuple-element.62.refs_0_, bf16[128,512]{1,0:T(8,128)(2,1)S(1)} %collective-permute-done.1.refs_1_.refs_3_, ...), custom_call_target="tpu_custom_call" | custom-call | flops 1 | bytes 1 | tf_op jit(solution)/shard_map/state/pallas_call | solution.py:667
  39.1 3.1 %collective-permute-start.10 = (bf16[272,256]{1,0:T(8,128)(2,1)S(1)}, bf16[272,256]{1,0:T(8,128)(2,1)S(1)}, u32[]{:S(2)}, u32[]{:S(2)}) collective-permute-start(bf16[272,256]{1,0:T(8,128)(2,1)S(1)} %get-tuple-element.80.refs_3_.refs_1_), channel_id=1, source_target_pairs={{0,8},{1,9},{2,10},{3,11},{4,12},{5,13},{6,14},{7,15},{8,0},{9,1},... | collective-permute-start | bytes 417800 | tf_op jit(solution)/shard_map/ppermute | solution.py:692
  44.2 2.9 %collective-permute-done.9.refs_0_ = bf16[272,256]{1,0:T(8,128)(2,1)S(1)} collective-permute-done((bf16[272,256]{1,0:T(8,128)(2,1)S(1)}, bf16[272,256]{1,0:T(8,128)(2,1)S(1)}, u32[]{:S(2)}, u32[]{:S(2)}) %collective-permute-start.9) | collective-permute-done | bytes 139296 | tf_op jit(solution)/shard_map/ppermute | solution.py:692
  50.0 3.4 %collective-permute-start.15 = (bf16[128,1024]{1,0:T(8,128)(2,1)S(1)}, bf16[128,1024]{1,0:T(8,128)(2,1)S(1)}, u32[]{:S(2)}, u32[]{:S(2)}) collective-permute-start(bf16[128,1024]{1,0:T(8,128)(2,1)S(1)} %get-tuple-element.91), channel_id=1, source_target_pairs={{0,2},{1,3},{2,0},{3,1},{4,6},{5,7},{6,4},{7,5},{8,10},{9,11},{10,... | collective-permute-start | bytes 786440 | tf_op jit(solution)/shard_map/ppermute | solution.py:692
  53.4 2.2 %collective-permute-start.16 = (bf16[128,1024]{1,0:T(8,128)(2,1)S(1)}, bf16[128,1024]{1,0:T(8,128)(2,1)S(1)}, u32[]{:S(2)}, u32[]{:S(2)}) collective-permute-start(bf16[128,1024]{1,0:T(8,128)(2,1)S(1)} %get-tuple-element.92), channel_id=1, source_target_pairs={{0,3},{1,2},{2,1},{3,0},{4,7},{5,6},{6,5},{7,4},{8,11},{9,10},{10,... | collective-permute-start | bytes 786440 | tf_op jit(solution)/shard_map/ppermute | solution.py:692
  55.5 2.6 %state.5 = (bf16[512,768]{1,0:T(8,128)(2,1)S(1)}, f32[256,768]{1,0:T(8,128)S(1)}, bf16[272,384]{1,0:T(8,128)(2,1)S(1)}, bf16[272,384]{1,0:T(8,128)(2,1)S(1)}) custom-call(s32[5]{0:T(128)S(1)} %stack.23.place, bf16[128,768]{1,0:T(8,128)(2,1)S(1)} %get-tuple-element.74.refs_9_.refs_0_, bf16[128,768]{1,0:T(8,128)(2,1)S(1)} %collective-permute-done.12.refs_2_.refs_1_, ...), custom_call_target="tpu_custom_call" | custom-call | flops 1 | bytes 1 | tf_op jit(solution)/shard_map/state/pallas_call | solution.py:667
  58.1 3.1 %collective-permute-start.17 = (bf16[272,384]{1,0:T(8,128)(2,1)S(1)}, bf16[272,384]{1,0:T(8,128)(2,1)S(1)}, u32[]{:S(2)}, u32[]{:S(2)}) collective-permute-start(bf16[272,384]{1,0:T(8,128)(2,1)S(1)} %get-tuple-element.93.refs_1_), channel_id=1, source_target_pairs={{0,8},{1,9},{2,10},{3,11},{4,12},{5,13},{6,14},{7,15},{8,0},{9,1},... | collective-permute-start | bytes 626696 | tf_op jit(solution)/shard_map/ppermute | solution.py:692
  61.2 1.3 %collective-permute-start.18 = (bf16[272,384]{1,0:T(8,128)(2,1)S(1)}, bf16[272,384]{1,0:T(8,128)(2,1)S(1)}, u32[]{:S(2)}, u32[]{:S(2)}) collective-permute-start(bf16[272,384]{1,0:T(8,128)(2,1)S(1)} %get-tuple-element.94.refs_1_), channel_id=1, source_target_pairs={{0,8},{1,9},{2,10},{3,11},{4,12},{5,13},{6,14},{7,15},{8,0},{9,1},... | collective-permute-start | bytes 626696 | tf_op jit(solution)/shard_map/ppermute | solution.py:692
  62.5 1.4 %collective-permute-done.17.refs_0_ = bf16[272,384]{1,0:T(8,128)(2,1)S(1)} collective-permute-done((bf16[272,384]{1,0:T(8,128)(2,1)S(1)}, bf16[272,384]{1,0:T(8,128)(2,1)S(1)}, u32[]{:S(2)}, u32[]{:S(2)}) %collective-permute-start.17) | collective-permute-done | bytes 208928 | tf_op jit(solution)/shard_map/ppermute | solution.py:692
  65.9 2.4 %collective-permute-done.18.refs_0_.refs_1_ = bf16[272,384]{1,0:T(8,128)(2,1)S(1)} collective-permute-done((bf16[272,384]{1,0:T(8,128)(2,1)S(1)}, bf16[272,384]{1,0:T(8,128)(2,1)S(1)}, u32[]{:S(2)}, u32[]{:S(2)}) %collective-permute-start.18) | collective-permute-done | bytes 208928 | tf_op jit(solution)/shard_map/ppermute | solution.py:692
  70.2 6.7 %collective-permute-done.16.refs_2_ = bf16[128,1024]{1,0:T(8,128)(2,1)S(1)} collective-permute-done((bf16[128,1024]{1,0:T(8,128)(2,1)S(1)}, bf16[128,1024]{1,0:T(8,128)(2,1)S(1)}, u32[]{:S(2)}, u32[]{:S(2)}) %collective-permute-start.16) | collective-permute-done | bytes 262176 | tf_op jit(solution)/shard_map/ppermute | solution.py:692
  77.0 1.9 %state.6 = (bf16[512,384]{1,0:T(8,128)(2,1)S(1)}, f32[256,384]{1,0:T(8,128)S(1)}, bf16[272,384]{1,0:T(8,128)(2,1)S(1)}) custom-call(s32[5]{0:T(128)S(1)} %stack.23.place, bf16[128,1024]{1,0:T(8,128)(2,1)S(1)} %get-tuple-element.82.refs_0_, bf16[128,1024]{1,0:T(8,128)(2,1)S(1)} %collective-permute-done.15.refs_1_, ...), custom_call_target="tpu_custom_call" | custom-call | flops 1 | bytes 1 | tf_op jit(solution)/shard_map/state/pallas_call | solution.py:667
  78.9 3.1 %collective-permute-start.22 = (bf16[272,384]{1,0:T(8,128)(2,1)S(1)}, bf16[272,384]{1,0:T(8,128)(2,1)S(1)}, u32[]{:S(2)}, u32[]{:S(2)}) collective-permute-start(bf16[272,384]{1,0:T(8,128)(2,1)S(1)} %get-tuple-element.95.refs_10_.refs_1_), channel_id=1, source_target_pairs={{0,8},{1,9},{2,10},{3,11},{4,12},{5,13},{6,14},{7,15},{8,0},{9,1},... | collective-permute-start | bytes 626696 | tf_op jit(solution)/shard_map/ppermute | solution.py:692
  82.0 1.9 %state.7 = (bf16[512,384]{1,0:T(8,128)(2,1)S(1)}, f32[256,384]{1,0:T(8,128)S(1)}, bf16[272,384]{1,0:T(8,128)(2,1)S(1)}) custom-call(s32[5]{0:T(128)S(1)} %stack.23.place, bf16[128,1024]{1,0:T(8,128)(2,1)S(1)} %get-tuple-element.82.refs_0_, bf16[128,1024]{1,0:T(8,128)(2,1)S(1)} %collective-permute-done.15.refs_1_, ...), custom_call_target="tpu_custom_call" | custom-call | flops 1 | bytes 1 | tf_op jit(solution)/shard_map/state/pallas_call | solution.py:667
  83.9 1.3 %collective-permute-start.21 = (bf16[272,384]{1,0:T(8,128)(2,1)S(1)}, bf16[272,384]{1,0:T(8,128)(2,1)S(1)}, u32[]{:S(2)}, u32[]{:S(2)}) collective-permute-start(bf16[272,384]{1,0:T(8,128)(2,1)S(1)} %get-tuple-element.96.refs_8_.refs_1_), channel_id=1, source_target_pairs={{0,8},{1,9},{2,10},{3,11},{4,12},{5,13},{6,14},{7,15},{8,0},{9,1},... | collective-permute-start | bytes 626696 | tf_op jit(solution)/shard_map/ppermute | solution.py:692
  87.1 1.5 %collective-permute-start.23 = (bf16[272,384]{1,0:T(8,128)(2,1)S(1)}, bf16[272,384]{1,0:T(8,128)(2,1)S(1)}, u32[]{:S(2)}, u32[]{:S(2)}) collective-permute-start(bf16[272,384]{1,0:T(8,128)(2,1)S(1)} %combine.8.refs_12_), channel_id=1, source_target_pairs={{0,16},{1,17},{2,18},{3,19},{4,20},{5,21},{6,22},{7,23},{8,24},{9,... | collective-permute-start | bytes 626696 | tf_op jit(solution)/shard_map/ppermute | solution.py:692
  88.6 2.6 %final.4 = (bf16[256,768]{1,0:T(8,128)(2,1)S(1)}, bf16[256,768]{1,0:T(8,128)(2,1)S(1)}) custom-call(s32[5]{0:T(128)S(1)} %stack.23.place, bf16[272,384]{1,0:T(8,128)(2,1)S(1)} %collective-permute-done.17.refs_0_, bf16[272,384]{1,0:T(8,128)(2,1)S(1)} %collective-permute-done.18.refs_0_.refs_1_, bf16[272,384]{1,0:T(8,128)(2,1)S(1)} %collective-permute-done.19.refs_9_.refs_2_, ...), custom_call_target="tpu_custom_call" | custom-call | flops 1 | bytes 1 | tf_op jit(solution)/shard_map/final/pallas_call | solution.py:667
  93.1 2.0 %collective-permute-start.26 = (bf16[256,768]{1,0:T(8,128)(2,1)S(1)}, bf16[256,768]{1,0:T(8,128)(2,1)S(1)}, u32[]{:S(2)}, u32[]{:S(2)}) collective-permute-start(bf16[256,768]{1,0:T(8,128)(2,1)S(1)} %get-tuple-element.114), channel_id=1, source_target_pairs={{0,4},{1,5},{2,6},{3,7},{4,0},{5,1},{6,2},{7,3},{8,12},{9,13},{10,... | collective-permute-start | bytes 1179656 | tf_op jit(solution)/shard_map/ppermute | solution.py:692
  95.1 1.9 %final.5 = (bf16[256,512]{1,0:T(8,128)(2,1)S(1)}, bf16[256,512]{1,0:T(8,128)(2,1)S(1)}) custom-call(s32[5]{0:T(128)S(1)} %stack.23.place, bf16[272,256]{1,0:T(8,128)(2,1)S(1)} %collective-permute-done.9.refs_0_, bf16[272,256]{1,0:T(8,128)(2,1)S(1)} %collective-permute-done.10.refs_1_, bf16[272,512]{1,0:T(8,128)(2,1)S(1)} %collective-permute-done.11.refs_12_.refs_2_, ...), custom_call_target="tpu_custom_call" | custom-call | flops 1 | bytes 1 | tf_op jit(solution)/shard_map/final/pallas_call | solution.py:667
  100.9 2.3 %collective-permute-start.28 = (bf16[256,384]{1,0:T(8,128)(2,1)S(1)}, bf16[256,384]{1,0:T(8,128)(2,1)S(1)}, u32[]{:S(2)}, u32[]{:S(2)}) collective-permute-start(bf16[256,384]{1,0:T(8,128)(2,1)S(1)} %get-tuple-element.116), channel_id=1, source_target_pairs={{0,4},{1,5},{2,6},{3,7},{4,0},{5,1},{6,2},{7,3},{8,12},{9,13},{10,... | collective-permute-start | bytes 589832 | tf_op jit(solution)/shard_map/ppermute | solution.py:692
  104.6 1.9 %place.1 = bf16[256,4096]{1,0:T(8,128)(2,1)} custom-call(s32[5]{0:T(128)S(1)} %stack.23.place, bf16[256,512]{1,0:T(8,128)(2,1)S(1)} %get-tuple-element.106.refs_0_, bf16[256,768]{1,0:T(8,128)(2,1)S(1)} %get-tuple-element.105.refs_2_.refs_1_, bf16[256,384]{1,0:T(8,128)(2,1)S(1)} %get-tuple-element.110.refs_6_.refs_2_, ...), custom_call_target="tpu_custom_call" | custom-call | flops 1 | bytes 1 | tf_op jit(solution)/shard_map/place/pallas_call | solution.py:629
  (70 shorter events, 25.3 us)
Async XLA Ops:
  4.1 11.4 %collective-permute-start.4 = (bf16[64,8448]{1,0:T(8,128)(2,1)S(1)}, bf16[64,8448]{1,0:T(8,128)(2,1)S(1)}, u32[]{:S(2)}, u32[]{:S(2)}) collective-permute-start(bf16[64,8448]{1,0:T(8,128)(2,1)S(1)} %get-tuple-element.66), channel_id=1, source_target_pairs={{0,4},{1,5},{2,6},{3,7},{4,0},{5,1},{6,2},{7,3},{8,12},{9,13},{10,... | collective-permute-start | bytes 3244040 | tf_op jit(solution)/shard_map/ppermute | solution.py:692
  4.9 3.1 %collective-permute-start = (bf16[64,4096]{1,0:T(8,128)(2,1)S(1)}, bf16[64,4096]{1,0:T(8,128)(2,1)S(1)}, u32[]{:S(2)}, u32[]{:S(2)}) collective-permute-start(bf16[64,4096]{1,0:T(8,128)(2,1)S(1)} %pack_first.1.order), channel_id=1, source_target_pairs={{0,4},{1,5},{2,6},{3,7},{4,0},{5,1},{6,2},{7,3},{8,12},{9,13},{10,... | collective-permute-start | bytes 1572872 | tf_op jit(solution)/shard_map/ppermute | solution.py:692
  8.8 10.5 %collective-permute-start.1 = (bf16[128,512]{1,0:T(8,128)(2,1)S(1)}, bf16[128,512]{1,0:T(8,128)(2,1)S(1)}, u32[]{:S(2)}, u32[]{:S(2)}) collective-permute-start(bf16[128,512]{1,0:T(8,128)(2,1)S(1)} %get-tuple-element.63), channel_id=1, source_target_pairs={{0,2},{1,3},{2,0},{3,1},{4,6},{5,7},{6,4},{7,5},{8,10},{9,11},{10,... | collective-permute-start | bytes 393224 | tf_op jit(solution)/shard_map/ppermute | solution.py:692
  11.2 4.4 %collective-permute-start.5 = (bf16[3,10240]{1,0:T(4,128)(2,1)S(1)}, bf16[3,10240]{1,0:T(4,128)(2,1)S(1)}, u32[]{:S(2)}, u32[]{:S(2)}) collective-permute-start(bf16[3,10240]{1,0:T(4,128)(2,1)S(1)} %get-tuple-element.69), channel_id=1, source_target_pairs={{3,11},{7,15},{11,19},{15,23},{19,27},{23,31}} | collective-permute-start | bytes 184328 | tf_op jit(solution)/shard_map/ppermute | solution.py:692
  11.8 14.5 %collective-permute-start.2 = (bf16[128,512]{1,0:T(8,128)(2,1)S(1)}, bf16[128,512]{1,0:T(8,128)(2,1)S(1)}, u32[]{:S(2)}, u32[]{:S(2)}) collective-permute-start(bf16[128,512]{1,0:T(8,128)(2,1)S(1)} %get-tuple-element.64), channel_id=1, source_target_pairs={{0,3},{1,2},{2,1},{3,0},{4,7},{5,6},{6,5},{7,4},{8,11},{9,10},{10,... | collective-permute-start | bytes 393224 | tf_op jit(solution)/shard_map/ppermute | solution.py:692
  11.9 14.5 %collective-permute-start.3 = (bf16[128,512]{1,0:T(8,128)(2,1)S(1)}, bf16[128,512]{1,0:T(8,128)(2,1)S(1)}, u32[]{:S(2)}, u32[]{:S(2)}) collective-permute-start(bf16[128,512]{1,0:T(8,128)(2,1)S(1)} %get-tuple-element.65), channel_id=1, source_target_pairs={{0,1},{1,0},{2,3},{3,2},{4,5},{5,4},{6,7},{7,6},{8,9},{9,8},{10,11... | collective-permute-start | bytes 393224 | tf_op jit(solution)/shard_map/ppermute | solution.py:692
  16.6 12.4 %collective-permute-start.6 = (bf16[128,384]{1,0:T(8,128)(2,1)S(1)}, bf16[128,384]{1,0:T(8,128)(2,1)S(1)}, u32[]{:S(2)}, u32[]{:S(2)}) collective-permute-start(bf16[128,384]{1,0:T(8,128)(2,1)S(1)} %get-tuple-element.71), channel_id=1, source_target_pairs={{0,2},{1,3},{2,0},{3,1},{4,6},{5,7},{6,4},{7,5},{8,10},{9,11},{10,... | collective-permute-start | bytes 294920 | tf_op jit(solution)/shard_map/ppermute | solution.py:692
  18.7 12.5 %collective-permute-start.7 = (bf16[128,384]{1,0:T(8,128)(2,1)S(1)}, bf16[128,384]{1,0:T(8,128)(2,1)S(1)}, u32[]{:S(2)}, u32[]{:S(2)}) collective-permute-start(bf16[128,384]{1,0:T(8,128)(2,1)S(1)} %get-tuple-element.72), channel_id=1, source_target_pairs={{0,3},{1,2},{2,1},{3,0},{4,7},{5,6},{6,5},{7,4},{8,11},{9,10},{10,... | collective-permute-start | bytes 294920 | tf_op jit(solution)/shard_map/ppermute | solution.py:692
  19.3 11.9 %collective-permute-start.8 = (bf16[128,384]{1,0:T(8,128)(2,1)S(1)}, bf16[128,384]{1,0:T(8,128)(2,1)S(1)}, u32[]{:S(2)}, u32[]{:S(2)}) collective-permute-start(bf16[128,384]{1,0:T(8,128)(2,1)S(1)} %get-tuple-element.73), channel_id=1, source_target_pairs={{0,1},{1,0},{2,3},{3,2},{4,5},{5,4},{6,7},{7,6},{8,9},{9,8},{10,11... | collective-permute-start | bytes 294920 | tf_op jit(solution)/shard_map/ppermute | solution.py:692
  20.2 14.3 %copy-start.3 = (f32[4,20480]{1,0:T(4,128)S(1)}, f32[4,20480]{1,0:T(4,128)}, u32[]{:S(2)}) copy-start(f32[4,20480]{1,0:T(4,128)} %weight.1) | copy-start | bytes 983044
  20.2 14.3 %copy-start.4 = (f32[20480]{0:T(1024)S(1)}, f32[20480]{0:T(1024)}, u32[]{:S(2)}) copy-start(f32[20480]{0:T(1024)} %param.10) | copy-start | bytes 245764
  31.2 18.8 %collective-permute-start.14 = (bf16[128,1792]{1,0:T(8,128)(2,1)S(1)}, bf16[128,1792]{1,0:T(8,128)(2,1)S(1)}, u32[]{:S(2)}, u32[]{:S(2)}) collective-permute-start(bf16[128,1792]{1,0:T(8,128)(2,1)S(1)} %get-tuple-element.90), channel_id=1, source_target_pairs={{0,1},{1,0},{2,3},{3,2},{4,5},{5,4},{6,7},{7,6},{8,9},{9,8},{10,11... | collective-permute-start | bytes 1376264 | tf_op jit(solution)/shard_map/ppermute | solution.py:692
  31.2 18.7 %collective-permute-start.12 = (bf16[128,768]{1,0:T(8,128)(2,1)S(1)}, bf16[128,768]{1,0:T(8,128)(2,1)S(1)}, u32[]{:S(2)}, u32[]{:S(2)}) collective-permute-start(bf16[128,768]{1,0:T(8,128)(2,1)S(1)} %get-tuple-element.88), channel_id=1, source_target_pairs={{0,2},{1,3},{2,0},{3,1},{4,6},{5,7},{6,4},{7,5},{8,10},{9,11},{10,... | collective-permute-start | bytes 589832 | tf_op jit(solution)/shard_map/ppermute | solution.py:692
  34.6 15.4 %collective-permute-start.13 = (bf16[128,768]{1,0:T(8,128)(2,1)S(1)}, bf16[128,768]{1,0:T(8,128)(2,1)S(1)}, u32[]{:S(2)}, u32[]{:S(2)}) collective-permute-start(bf16[128,768]{1,0:T(8,128)(2,1)S(1)} %get-tuple-element.89), channel_id=1, source_target_pairs={{0,3},{1,2},{2,1},{3,0},{4,7},{5,6},{6,5},{7,4},{8,11},{9,10},{10,... | collective-permute-start | bytes 589832 | tf_op jit(solution)/shard_map/ppermute | solution.py:692
  34.6 14.5 %copy-start.1 = (bf16[64,20480]{1,0:T(8,128)(2,1)S(1)}, bf16[64,20480]{1,0:T(8,128)(2,1)}, u32[]{:S(2)}) copy-start(bf16[64,20480]{1,0:T(8,128)(2,1)} %xbc.11) | copy-start | bytes 7864324
  39.1 5.1 %collective-permute-start.10 = (bf16[272,256]{1,0:T(8,128)(2,1)S(1)}, bf16[272,256]{1,0:T(8,128)(2,1)S(1)}, u32[]{:S(2)}, u32[]{:S(2)}) collective-permute-start(bf16[272,256]{1,0:T(8,128)(2,1)S(1)} %get-tuple-element.80.refs_3_.refs_1_), channel_id=1, source_target_pairs={{0,8},{1,9},{2,10},{3,11},{4,12},{5,13},{6,14},{7,15},{8,0},{9,1},... | collective-permute-start | bytes 417800 | tf_op jit(solution)/shard_map/ppermute | solution.py:692
  42.2 4.9 %collective-permute-start.9 = (bf16[272,256]{1,0:T(8,128)(2,1)S(1)}, bf16[272,256]{1,0:T(8,128)(2,1)S(1)}, u32[]{:S(2)}, u32[]{:S(2)}) collective-permute-start(bf16[272,256]{1,0:T(8,128)(2,1)S(1)} %get-tuple-element.79.refs_2_.refs_0_), channel_id=1, source_target_pairs={{0,8},{1,9},{2,10},{3,11},{4,12},{5,13},{6,14},{7,15},{8,0},{9,1},... | collective-permute-start | bytes 417800 | tf_op jit(solution)/shard_map/ppermute | solution.py:692
  47.8 22.4 %collective-permute-start.11 = (bf16[272,512]{1,0:T(8,128)(2,1)S(1)}, bf16[272,512]{1,0:T(8,128)(2,1)S(1)}, u32[]{:S(2)}, u32[]{:S(2)}) collective-permute-start(bf16[272,512]{1,0:T(8,128)(2,1)S(1)} %combine.5.refs_10_), channel_id=1, source_target_pairs={{0,16},{1,17},{2,18},{3,19},{4,20},{5,21},{6,22},{7,23},{8,24},{9,... | collective-permute-start | bytes 835592 | tf_op jit(solution)/shard_map/ppermute | solution.py:692
  50.0 20.3 %collective-permute-start.15 = (bf16[128,1024]{1,0:T(8,128)(2,1)S(1)}, bf16[128,1024]{1,0:T(8,128)(2,1)S(1)}, u32[]{:S(2)}, u32[]{:S(2)}) collective-permute-start(bf16[128,1024]{1,0:T(8,128)(2,1)S(1)} %get-tuple-element.91), channel_id=1, source_target_pairs={{0,2},{1,3},{2,0},{3,1},{4,6},{5,7},{6,4},{7,5},{8,10},{9,11},{10,... | collective-permute-start | bytes 786440 | tf_op jit(solution)/shard_map/ppermute | solution.py:692
  53.4 23.6 %collective-permute-start.16 = (bf16[128,1024]{1,0:T(8,128)(2,1)S(1)}, bf16[128,1024]{1,0:T(8,128)(2,1)S(1)}, u32[]{:S(2)}, u32[]{:S(2)}) collective-permute-start(bf16[128,1024]{1,0:T(8,128)(2,1)S(1)} %get-tuple-element.92), channel_id=1, source_target_pairs={{0,3},{1,2},{2,1},{3,0},{4,7},{5,6},{6,5},{7,4},{8,11},{9,10},{10,... | collective-permute-start | bytes 786440 | tf_op jit(solution)/shard_map/ppermute | solution.py:692
  58.1 5.9 %collective-permute-start.17 = (bf16[272,384]{1,0:T(8,128)(2,1)S(1)}, bf16[272,384]{1,0:T(8,128)(2,1)S(1)}, u32[]{:S(2)}, u32[]{:S(2)}) collective-permute-start(bf16[272,384]{1,0:T(8,128)(2,1)S(1)} %get-tuple-element.93.refs_1_), channel_id=1, source_target_pairs={{0,8},{1,9},{2,10},{3,11},{4,12},{5,13},{6,14},{7,15},{8,0},{9,1},... | collective-permute-start | bytes 626696 | tf_op jit(solution)/shard_map/ppermute | solution.py:692
  61.2 7.0 %collective-permute-start.18 = (bf16[272,384]{1,0:T(8,128)(2,1)S(1)}, bf16[272,384]{1,0:T(8,128)(2,1)S(1)}, u32[]{:S(2)}, u32[]{:S(2)}) collective-permute-start(bf16[272,384]{1,0:T(8,128)(2,1)S(1)} %get-tuple-element.94.refs_1_), channel_id=1, source_target_pairs={{0,8},{1,9},{2,10},{3,11},{4,12},{5,13},{6,14},{7,15},{8,0},{9,1},... | collective-permute-start | bytes 626696 | tf_op jit(solution)/shard_map/ppermute | solution.py:692
  64.6 20.7 %collective-permute-start.19 = (bf16[272,384]{1,0:T(8,128)(2,1)S(1)}, bf16[272,384]{1,0:T(8,128)(2,1)S(1)}, u32[]{:S(2)}, u32[]{:S(2)}) collective-permute-start(bf16[272,384]{1,0:T(8,128)(2,1)S(1)} %combine.6.refs_2_.refs_10_), channel_id=1, source_target_pairs={{0,16},{1,17},{2,18},{3,19},{4,20},{5,21},{6,22},{7,23},{8,24},{9,... | collective-permute-start | bytes 626696 | tf_op jit(solution)/shard_map/ppermute | solution.py:692
  68.9 16.3 %collective-permute-start.20 = (bf16[272,384]{1,0:T(8,128)(2,1)S(1)}, bf16[272,384]{1,0:T(8,128)(2,1)S(1)}, u32[]{:S(2)}, u32[]{:S(2)}) collective-permute-start(bf16[272,384]{1,0:T(8,128)(2,1)S(1)} %combine.7.refs_11_), channel_id=1, source_target_pairs={{0,16},{1,17},{2,18},{3,19},{4,20},{5,21},{6,22},{7,23},{8,24},{9,... | collective-permute-start | bytes 626696 | tf_op jit(solution)/shard_map/ppermute | solution.py:692
  78.9 7.5 %collective-permute-start.22 = (bf16[272,384]{1,0:T(8,128)(2,1)S(1)}, bf16[272,384]{1,0:T(8,128)(2,1)S(1)}, u32[]{:S(2)}, u32[]{:S(2)}) collective-permute-start(bf16[272,384]{1,0:T(8,128)(2,1)S(1)} %get-tuple-element.95.refs_10_.refs_1_), channel_id=1, source_target_pairs={{0,8},{1,9},{2,10},{3,11},{4,12},{5,13},{6,14},{7,15},{8,0},{9,1},... | collective-permute-start | bytes 626696 | tf_op jit(solution)/shard_map/ppermute | solution.py:692
  83.9 7.2 %collective-permute-start.21 = (bf16[272,384]{1,0:T(8,128)(2,1)S(1)}, bf16[272,384]{1,0:T(8,128)(2,1)S(1)}, u32[]{:S(2)}, u32[]{:S(2)}) collective-permute-start(bf16[272,384]{1,0:T(8,128)(2,1)S(1)} %get-tuple-element.96.refs_8_.refs_1_), channel_id=1, source_target_pairs={{0,8},{1,9},{2,10},{3,11},{4,12},{5,13},{6,14},{7,15},{8,0},{9,1},... | collective-permute-start | bytes 626696 | tf_op jit(solution)/shard_map/ppermute | solution.py:692
  87.1 11.6 %collective-permute-start.23 = (bf16[272,384]{1,0:T(8,128)(2,1)S(1)}, bf16[272,384]{1,0:T(8,128)(2,1)S(1)}, u32[]{:S(2)}, u32[]{:S(2)}) collective-permute-start(bf16[272,384]{1,0:T(8,128)(2,1)S(1)} %combine.8.refs_12_), channel_id=1, source_target_pairs={{0,16},{1,17},{2,18},{3,19},{4,20},{5,21},{6,22},{7,23},{8,24},{9,... | collective-permute-start | bytes 626696 | tf_op jit(solution)/shard_map/ppermute | solution.py:692
  91.8 8.0 %collective-permute-start.24 = (bf16[272,384]{1,0:T(8,128)(2,1)S(1)}, bf16[272,384]{1,0:T(8,128)(2,1)S(1)}, u32[]{:S(2)}, u32[]{:S(2)}) collective-permute-start(bf16[272,384]{1,0:T(8,128)(2,1)S(1)} %combine.9.refs_11_), channel_id=1, source_target_pairs={{0,16},{1,17},{2,18},{3,19},{4,20},{5,21},{6,22},{7,23},{8,24},{9,... | collective-permute-start | bytes 626696 | tf_op jit(solution)/shard_map/ppermute | solution.py:692
  93.1 10.1 %collective-permute-start.26 = (bf16[256,768]{1,0:T(8,128)(2,1)S(1)}, bf16[256,768]{1,0:T(8,128)(2,1)S(1)}, u32[]{:S(2)}, u32[]{:S(2)}) collective-permute-start(bf16[256,768]{1,0:T(8,128)(2,1)S(1)} %get-tuple-element.114), channel_id=1, source_target_pairs={{0,4},{1,5},{2,6},{3,7},{4,0},{5,1},{6,2},{7,3},{8,12},{9,13},{10,... | collective-permute-start | bytes 1179656 | tf_op jit(solution)/shard_map/ppermute | solution.py:692
  97.0 6.2 %collective-permute-start.25 = (bf16[256,512]{1,0:T(8,128)(2,1)S(1)}, bf16[256,512]{1,0:T(8,128)(2,1)S(1)}, u32[]{:S(2)}, u32[]{:S(2)}) collective-permute-start(bf16[256,512]{1,0:T(8,128)(2,1)S(1)} %get-tuple-element.113), channel_id=1, source_target_pairs={{0,4},{1,5},{2,6},{3,7},{4,0},{5,1},{6,2},{7,3},{8,12},{9,13},{10,... | collective-permute-start | bytes 786440 | tf_op jit(solution)/shard_map/ppermute | solution.py:692
  100.9 3.3 %collective-permute-start.28 = (bf16[256,384]{1,0:T(8,128)(2,1)S(1)}, bf16[256,384]{1,0:T(8,128)(2,1)S(1)}, u32[]{:S(2)}, u32[]{:S(2)}) collective-permute-start(bf16[256,384]{1,0:T(8,128)(2,1)S(1)} %get-tuple-element.116), channel_id=1, source_target_pairs={{0,4},{1,5},{2,6},{3,7},{4,0},{5,1},{6,2},{7,3},{8,12},{9,13},{10,... | collective-permute-start | bytes 589832 | tf_op jit(solution)/shard_map/ppermute | solution.py:692
  103.1 1.4 %collective-permute-start.27 = (bf16[256,384]{1,0:T(8,128)(2,1)S(1)}, bf16[256,384]{1,0:T(8,128)(2,1)S(1)}, u32[]{:S(2)}, u32[]{:S(2)}) collective-permute-start(bf16[256,384]{1,0:T(8,128)(2,1)S(1)} %get-tuple-element.115), channel_id=1, source_target_pairs={{0,4},{1,5},{2,6},{3,7},{4,0},{5,1},{6,2},{7,3},{8,12},{9,13},{10,... | collective-permute-start | bytes 589832 | tf_op jit(solution)/shard_map/ppermute | solution.py:692
  (5 other events, 47.0 us)

commit v18 on v17

--- a/solution.py
+++ b/solution.py
@@ -753,7 +753,7 @@
     message.append(travel(second_blocks))
     third_plan = [(r, (2, 3) if r == NEAR else (2,)) for r in range(shards)]
     third_blocks = send_on(third_plan, [second_blocks[0]])
-    message.append(travel(third_blocks[:1] + gate(third_blocks[1:], message[0][1:] + message[1][1:])))
+    message.append(travel(third_blocks[:1] + gate(third_blocks[1:], message[0][1:] + message[1][1:] + [taps])))
 
     def seen(piece):
         return message[piece]
@@ -838,30 +838,31 @@
     fourth_blocks = gate(fourth_blocks, message[2][1:])
     fourth_blocks = [over(block, lambda i, r=r: i ^ FLIP[r]) for r, block in enumerate(fourth_blocks, 1)]
     message.append([own_block, *fourth_blocks, message[2][NEAR]])
-    combine_of(0, [])
+    combine_of(0, [own_block])
     state_of(1, joined[0])
     combine_of(1, [])
     state_of(2, joined[1] + before[0])
-    state_of(3, sent[2])
     c, score = call(
         functools.partial(score_kernel, shards),
         [((slab, STATE), BF16), ((slab, BLOCK), F32)],
-        [place] + seen(3) + [taps, offset, edge, b] + [Stay(o) for o in sent[3] + before[1]],
+        [place] + seen(3) + [taps, offset, edge, b] + [Stay(o) for o in sent[2]],
         scratch=[pltpu.VMEM((slab + 8, STATE), F32)],
         name="score",
     )
+    local_of(0, [])
+    state_of(3, [partial[0]])
 
     def in_full(i, order):
         wide = [pltpu.VMEM((slab, GROUPED[i][2]), F32)]
         finish_of(finish_kernel, i, [x[i], cum, row, score, skip], order, scratch=wide)
 
-    combine_of(2, [score])
+    combine_of(2, sent[3] + before[1])
     in_full(1, joined[2])
     combine_of(3, [keep[1]])
-    in_full(0, joined[3])
-    local_of(2, [keep[0]])
+    local_of(2, joined[3])
     local_of(3, [partial[2]])
-    finish_of(final_kernel, 2, [partial[2]], [partial[3]])
+    finish_of(final_kernel, 0, [partial[0]], [partial[3]])
+    finish_of(final_kernel, 2, [partial[2]], [keep[0]])
     finish_of(final_kernel, 3, [partial[3]], [keep[2]])
     firsts = [first_head(i) * HEAD_DIM for i in range(count)]
     return put_in_place(firsts, (BLOCK, PAIR * PER_GROUP), place, keep, [swap(o) for o in send])

time: 108 us -> 108 us (level)
    pallas_call x24 -> x25, Pallas kernels: 29.2 us -> 29.5 us  [call(): pl.pallas_call(body, out_shape=shapes, in_specs=specs, out_specs=[vmem] *...]
  transfers between devices with their start and end apart: 29 -> 29, of which waited for: 13 -> 12; matrix products, arithmetic and copies ran while one was open for 0% -> 0% of each run, Pallas kernels for 25% -> 25%
where the time goes in v18:
time: 108 us; the launch traced here: 107 us
  starting transfers between devices  44.3 us (41%)
  Pallas kernels  31.4 us (29%)
  waiting for transfers between devices  28.8 us (27%)
  local copies, waits for them, and re-layouts  1.93 us (2%)
    ppermute x29, starting transfers between devices, over(): lax.ppermute(block, axes, [(i, j) for i, j in route if j is not None and...  44.3 us
    pallas_call x25, Pallas kernels, call(): pl.pallas_call(body, out_shape=shapes, in_specs=specs, out_specs=[vmem] *...  29.5 us
    ppermute x29, waiting for transfers between devices, over(): lax.ppermute(block, axes, [(i, j) for i, j in route if j is not None and...  28.8 us
  transfers between devices with their start and end apart: 29, of which 12 were waited for; matrix products, arithmetic and copies ran while one was open for 0% of the time, Pallas kernels for 25%

profile of v18, /device:TPU:13, one launch (start us, length us, event | category | flops | bytes accessed | tf_op | source)
XLA Modules:
  0.0 107.0 jit_solution(1487123798982080471)
XLA Ops:
  0.1 1.7 %copy-done = bf16[64,20480]{1,0:T(8,128)(2,1)S(1)} copy-done((bf16[64,20480]{1,0:T(8,128)(2,1)S(1)}, bf16[64,20480]{1,0:T(8,128)(2,1)}, u32[]{:S(2)}) %copy-start) | copy-done | bytes 2621464
  2.8 1.3 %pack.1 = (bf16[64,8448]{1,0:T(8,128)(2,1)S(1)}, bf16[16,10240]{1,0:T(8,128)(2,1)S(1)}) custom-call(s32[5]{0:T(128)S(1)} %stack.23.place, bf16[64,20480]{1,0:T(8,128)(2,1)S(1)} %copy-done, bf16[64,256]{1,0:T(8,128)(2,1)S(1)} %copy-done.2, bf16[64,4096]{1,0:T(8,128)(2,1)S(1)} %pack_first.1.order), custom_call_target="tpu_custom_call" | custom-call | flops 1 | bytes 1 | tf_op jit(solution)/shard_map/pack/pallas_call | solution.py:667
  5.0 3.0 %collective-permute-done.got_first.got.edges = bf16[64,4096]{1,0:T(8,128)(2,1)S(1)} collective-permute-done((bf16[64,4096]{1,0:T(8,128)(2,1)S(1)}, bf16[64,4096]{1,0:T(8,128)(2,1)S(1)}, u32[]{:S(2)}, u32[]{:S(2)}) %collective-permute-start) | collective-permute-done | bytes 524320 | tf_op jit(solution)/shard_map/ppermute | solution.py:692
  8.8 2.4 %collective-permute-start.1 = (bf16[128,512]{1,0:T(8,128)(2,1)S(1)}, bf16[128,512]{1,0:T(8,128)(2,1)S(1)}, u32[]{:S(2)}, u32[]{:S(2)}) collective-permute-start(bf16[128,512]{1,0:T(8,128)(2,1)S(1)} %get-tuple-element.63), channel_id=1, source_target_pairs={{0,2},{1,3},{2,0},{3,1},{4,6},{5,7},{6,4},{7,5},{8,10},{9,11},{10,... | collective-permute-start | bytes 393224 | tf_op jit(solution)/shard_map/ppermute | solution.py:692
  11.9 3.7 %collective-permute-start.3 = (bf16[128,512]{1,0:T(8,128)(2,1)S(1)}, bf16[128,512]{1,0:T(8,128)(2,1)S(1)}, u32[]{:S(2)}, u32[]{:S(2)}) collective-permute-start(bf16[128,512]{1,0:T(8,128)(2,1)S(1)} %get-tuple-element.65), channel_id=1, source_target_pairs={{0,1},{1,0},{2,3},{3,2},{4,5},{5,4},{6,7},{7,6},{8,9},{9,8},{10,11... | collective-permute-start | bytes 393224 | tf_op jit(solution)/shard_map/ppermute | solution.py:692
  16.6 2.1 %collective-permute-start.6 = (bf16[128,384]{1,0:T(8,128)(2,1)S(1)}, bf16[128,384]{1,0:T(8,128)(2,1)S(1)}, u32[]{:S(2)}, u32[]{:S(2)}) collective-permute-start(bf16[128,384]{1,0:T(8,128)(2,1)S(1)} %get-tuple-element.71), channel_id=1, source_target_pairs={{0,2},{1,3},{2,0},{3,1},{4,6},{5,7},{6,4},{7,5},{8,10},{9,11},{10,... | collective-permute-start | bytes 294920 | tf_op jit(solution)/shard_map/ppermute | solution.py:692
  21.9 4.4 %collective-permute-done.2.refs_2_.refs_4_ = bf16[128,512]{1,0:T(8,128)(2,1)S(1)} collective-permute-done((bf16[128,512]{1,0:T(8,128)(2,1)S(1)}, bf16[128,512]{1,0:T(8,128)(2,1)S(1)}, u32[]{:S(2)}, u32[]{:S(2)}) %collective-permute-start.2) | collective-permute-done | bytes 131104 | tf_op jit(solution)/shard_map/ppermute | solution.py:692
  26.4 2.7 %collective-permute-done.6.refs_1_.refs_6_ = bf16[128,384]{1,0:T(8,128)(2,1)S(1)} collective-permute-done((bf16[128,384]{1,0:T(8,128)(2,1)S(1)}, bf16[128,384]{1,0:T(8,128)(2,1)S(1)}, u32[]{:S(2)}, u32[]{:S(2)}) %collective-permute-start.6) | collective-permute-done | bytes 98336 | tf_op jit(solution)/shard_map/ppermute | solution.py:692
  29.1 2.1 %collective-permute-done.7.refs_2_.refs_7_ = bf16[128,384]{1,0:T(8,128)(2,1)S(1)} collective-permute-done((bf16[128,384]{1,0:T(8,128)(2,1)S(1)}, bf16[128,384]{1,0:T(8,128)(2,1)S(1)}, u32[]{:S(2)}, u32[]{:S(2)}) %collective-permute-start.7) | collective-permute-done | bytes 98336 | tf_op jit(solution)/shard_map/ppermute | solution.py:692
  31.2 3.4 %collective-permute-start.12 = (bf16[128,768]{1,0:T(8,128)(2,1)S(1)}, bf16[128,768]{1,0:T(8,128)(2,1)S(1)}, u32[]{:S(2)}, u32[]{:S(2)}) collective-permute-start(bf16[128,768]{1,0:T(8,128)(2,1)S(1)} %get-tuple-element.88), channel_id=1, source_target_pairs={{0,2},{1,3},{2,0},{3,1},{4,6},{5,7},{6,4},{7,5},{8,10},{9,11},{10,... | collective-permute-start | bytes 589832 | tf_op jit(solution)/shard_map/ppermute | solution.py:692
  34.6 1.7 %prep.1 = (bf16[512,256]{1,0:T(8,128)(2,1)S(1)}, f32[4,2560]{1,0:T(4,128)S(1)}, f32[512,128]{1,0:T(8,128)S(1)}, f32[128,512]{1,0:T(8,128)S(1)}, bf16[512,256]{1,...) custom-call(s32[5]{0:T(128)S(1)} %stack.23.place, ...), custom_call_target="tpu_custom_call" | custom-call | flops 1 | bytes 1 | tf_op jit(solution)/shard_map/prep/pallas_call | solution.py:667
  36.3 2.1 %state.4 = (bf16[512,512]{1,0:T(8,128)(2,1)S(1)}, f32[256,512]{1,0:T(8,128)S(1)}, bf16[272,256]{1,0:T(8,128)(2,1)S(1)}, bf16[272,256]{1,0:T(8,128)(2,1)S(1)}) custom-call(s32[5]{0:T(128)S(1)} %stack.23.place, bf16[128,512]{1,0:T(8,128)(2,1)S(1)} %get-tuple-element.62.refs_0_, bf16[128,512]{1,0:T(8,128)(2,1)S(1)} %collective-permute-done.1.refs_1_.refs_3_, ...), custom_call_target="tpu_custom_call" | custom-call | flops 1 | bytes 1 | tf_op jit(solution)/shard_map/state/pallas_call | solution.py:667
  38.3 3.1 %collective-permute-start.9 = (bf16[272,256]{1,0:T(8,128)(2,1)S(1)}, bf16[272,256]{1,0:T(8,128)(2,1)S(1)}, u32[]{:S(2)}, u32[]{:S(2)}) collective-permute-start(bf16[272,256]{1,0:T(8,128)(2,1)S(1)} %get-tuple-element.79.refs_0_.refs_2_), channel_id=1, source_target_pairs={{0,8},{1,9},{2,10},{3,11},{4,12},{5,13},{6,14},{7,15},{8,0},{9,1},... | collective-permute-start | bytes 417800 | tf_op jit(solution)/shard_map/ppermute | solution.py:692
  41.5 1.3 %collective-permute-start.10 = (bf16[272,256]{1,0:T(8,128)(2,1)S(1)}, bf16[272,256]{1,0:T(8,128)(2,1)S(1)}, u32[]{:S(2)}, u32[]{:S(2)}) collective-permute-start(bf16[272,256]{1,0:T(8,128)(2,1)S(1)} %get-tuple-element.80.refs_1_.refs_3_), channel_id=1, source_target_pairs={{0,8},{1,9},{2,10},{3,11},{4,12},{5,13},{6,14},{7,15},{8,0},{9,1},... | collective-permute-start | bytes 417800 | tf_op jit(solution)/shard_map/ppermute | solution.py:692
  43.6 2.7 %collective-permute-done.10.refs_1_ = bf16[272,256]{1,0:T(8,128)(2,1)S(1)} collective-permute-done((bf16[272,256]{1,0:T(8,128)(2,1)S(1)}, bf16[272,256]{1,0:T(8,128)(2,1)S(1)}, u32[]{:S(2)}, u32[]{:S(2)}) %collective-permute-start.10) | collective-permute-done | bytes 139296 | tf_op jit(solution)/shard_map/ppermute | solution.py:692
  47.1 1.3 %collective-permute-start.11 = (bf16[272,512]{1,0:T(8,128)(2,1)S(1)}, bf16[272,512]{1,0:T(8,128)(2,1)S(1)}, u32[]{:S(2)}, u32[]{:S(2)}) collective-permute-start(bf16[272,512]{1,0:T(8,128)(2,1)S(1)} %combine.5.refs_10_), channel_id=1, source_target_pairs={{0,16},{1,17},{2,18},{3,19},{4,20},{5,21},{6,22},{7,23},{8,24},{9,... | collective-permute-start | bytes 835592 | tf_op jit(solution)/shard_map/ppermute | solution.py:692
  48.9 4.4 %collective-permute-start.15 = (bf16[128,1024]{1,0:T(8,128)(2,1)S(1)}, bf16[128,1024]{1,0:T(8,128)(2,1)S(1)}, u32[]{:S(2)}, u32[]{:S(2)}) collective-permute-start(bf16[128,1024]{1,0:T(8,128)(2,1)S(1)} %get-tuple-element.91), channel_id=1, source_target_pairs={{0,2},{1,3},{2,0},{3,1},{4,6},{5,7},{6,4},{7,5},{8,10},{9,11},{10,... | collective-permute-start | bytes 786440 | tf_op jit(solution)/shard_map/ppermute | solution.py:692
  53.4 2.2 %collective-permute-start.16 = (bf16[128,1024]{1,0:T(8,128)(2,1)S(1)}, bf16[128,1024]{1,0:T(8,128)(2,1)S(1)}, u32[]{:S(2)}, u32[]{:S(2)}) collective-permute-start(bf16[128,1024]{1,0:T(8,128)(2,1)S(1)} %get-tuple-element.92), channel_id=1, source_target_pairs={{0,3},{1,2},{2,1},{3,0},{4,7},{5,6},{6,5},{7,4},{8,11},{9,10},{10,... | collective-permute-start | bytes 786440 | tf_op jit(solution)/shard_map/ppermute | solution.py:692
  55.5 2.6 %state.5 = (bf16[512,768]{1,0:T(8,128)(2,1)S(1)}, f32[256,768]{1,0:T(8,128)S(1)}, bf16[272,384]{1,0:T(8,128)(2,1)S(1)}, bf16[272,384]{1,0:T(8,128)(2,1)S(1)}) custom-call(s32[5]{0:T(128)S(1)} %stack.23.place, bf16[128,768]{1,0:T(8,128)(2,1)S(1)} %get-tuple-element.74.refs_9_.refs_0_, bf16[128,768]{1,0:T(8,128)(2,1)S(1)} %collective-permute-done.12.refs_2_.refs_1_, ...), custom_call_target="tpu_custom_call" | custom-call | flops 1 | bytes 1 | tf_op jit(solution)/shard_map/state/pallas_call | solution.py:667
  58.1 3.1 %collective-permute-start.17 = (bf16[272,384]{1,0:T(8,128)(2,1)S(1)}, bf16[272,384]{1,0:T(8,128)(2,1)S(1)}, u32[]{:S(2)}, u32[]{:S(2)}) collective-permute-start(bf16[272,384]{1,0:T(8,128)(2,1)S(1)} %get-tuple-element.93.refs_1_), channel_id=1, source_target_pairs={{0,8},{1,9},{2,10},{3,11},{4,12},{5,13},{6,14},{7,15},{8,0},{9,1},... | collective-permute-start | bytes 626696 | tf_op jit(solution)/shard_map/ppermute | solution.py:692
  61.2 1.3 %collective-permute-start.18 = (bf16[272,384]{1,0:T(8,128)(2,1)S(1)}, bf16[272,384]{1,0:T(8,128)(2,1)S(1)}, u32[]{:S(2)}, u32[]{:S(2)}) collective-permute-start(bf16[272,384]{1,0:T(8,128)(2,1)S(1)} %get-tuple-element.94.refs_1_), channel_id=1, source_target_pairs={{0,8},{1,9},{2,10},{3,11},{4,12},{5,13},{6,14},{7,15},{8,0},{9,1},... | collective-permute-start | bytes 626696 | tf_op jit(solution)/shard_map/ppermute | solution.py:692
  62.5 1.4 %collective-permute-done.17.refs_0_ = bf16[272,384]{1,0:T(8,128)(2,1)S(1)} collective-permute-done((bf16[272,384]{1,0:T(8,128)(2,1)S(1)}, bf16[272,384]{1,0:T(8,128)(2,1)S(1)}, u32[]{:S(2)}, u32[]{:S(2)}) %collective-permute-start.17) | collective-permute-done | bytes 208928 | tf_op jit(solution)/shard_map/ppermute | solution.py:692
  65.9 2.4 %collective-permute-done.18.refs_0_.refs_1_ = bf16[272,384]{1,0:T(8,128)(2,1)S(1)} collective-permute-done((bf16[272,384]{1,0:T(8,128)(2,1)S(1)}, bf16[272,384]{1,0:T(8,128)(2,1)S(1)}, u32[]{:S(2)}, u32[]{:S(2)}) %collective-permute-start.18) | collective-permute-done | bytes 208928 | tf_op jit(solution)/shard_map/ppermute | solution.py:692
  68.9 1.3 %collective-permute-start.21 = (bf16[272,384]{1,0:T(8,128)(2,1)S(1)}, bf16[272,384]{1,0:T(8,128)(2,1)S(1)}, u32[]{:S(2)}, u32[]{:S(2)}) collective-permute-start(bf16[272,384]{1,0:T(8,128)(2,1)S(1)} %combine.7.refs_11_), channel_id=1, source_target_pairs={{0,16},{1,17},{2,18},{3,19},{4,20},{5,21},{6,22},{7,23},{8,24},{9,... | collective-permute-start | bytes 626696 | tf_op jit(solution)/shard_map/ppermute | solution.py:692
  70.2 6.7 %collective-permute-done.16.refs_2_ = bf16[128,1024]{1,0:T(8,128)(2,1)S(1)} collective-permute-done((bf16[128,1024]{1,0:T(8,128)(2,1)S(1)}, bf16[128,1024]{1,0:T(8,128)(2,1)S(1)}, u32[]{:S(2)}, u32[]{:S(2)}) %collective-permute-start.16) | collective-permute-done | bytes 262176 | tf_op jit(solution)/shard_map/ppermute | solution.py:692
  77.0 1.9 %state.6 = (bf16[512,384]{1,0:T(8,128)(2,1)S(1)}, f32[256,384]{1,0:T(8,128)S(1)}, bf16[272,384]{1,0:T(8,128)(2,1)S(1)}) custom-call(s32[5]{0:T(128)S(1)} %stack.23.place, bf16[128,1024]{1,0:T(8,128)(2,1)S(1)} %get-tuple-element.81.refs_4_.refs_0_, bf16[128,1024]{1,0:T(8,128)(2,1)S(1)} %collective-permute-done.15.refs_1_, ...), custom_call_target="tpu_custom_call" | custom-call | flops 1 | bytes 1 | tf_op jit(solution)/shard_map/state/pallas_call | solution.py:667
  78.9 3.3 %collective-permute-start.22 = (bf16[272,384]{1,0:T(8,128)(2,1)S(1)}, bf16[272,384]{1,0:T(8,128)(2,1)S(1)}, u32[]{:S(2)}, u32[]{:S(2)}) collective-permute-start(bf16[272,384]{1,0:T(8,128)(2,1)S(1)} %get-tuple-element.95.refs_8_.refs_1_), channel_id=1, source_target_pairs={{0,8},{1,9},{2,10},{3,11},{4,12},{5,13},{6,14},{7,15},{8,0},{9,1},... | collective-permute-start | bytes 626696 | tf_op jit(solution)/shard_map/ppermute | solution.py:692
  84.4 1.9 %state.7 = (bf16[512,384]{1,0:T(8,128)(2,1)S(1)}, f32[256,384]{1,0:T(8,128)S(1)}, bf16[272,384]{1,0:T(8,128)(2,1)S(1)}) custom-call(s32[5]{0:T(128)S(1)} %stack.23.place, bf16[128,1024]{1,0:T(8,128)(2,1)S(1)} %get-tuple-element.81.refs_4_.refs_0_, bf16[128,1024]{1,0:T(8,128)(2,1)S(1)} %collective-permute-done.15.refs_1_, ...), custom_call_target="tpu_custom_call" | custom-call | flops 1 | bytes 1 | tf_op jit(solution)/shard_map/state/pallas_call | solution.py:667
  86.3 1.3 %collective-permute-start.19 = (bf16[272,384]{1,0:T(8,128)(2,1)S(1)}, bf16[272,384]{1,0:T(8,128)(2,1)S(1)}, u32[]{:S(2)}, u32[]{:S(2)}) collective-permute-start(bf16[272,384]{1,0:T(8,128)(2,1)S(1)} %get-tuple-element.104.refs_2_.refs_1_), channel_id=1, source_target_pairs={{0,8},{1,9},{2,10},{3,11},{4,12},{5,13},{6,14},{7,15},{8,0},{9,1},... | collective-permute-start | bytes 626696 | tf_op jit(solution)/shard_map/ppermute | solution.py:692
  89.6 2.6 %final.4 = (bf16[256,768]{1,0:T(8,128)(2,1)S(1)}, bf16[256,768]{1,0:T(8,128)(2,1)S(1)}) custom-call(s32[5]{0:T(128)S(1)} %stack.23.place, bf16[272,384]{1,0:T(8,128)(2,1)S(1)} %collective-permute-done.17.refs_0_, bf16[272,384]{1,0:T(8,128)(2,1)S(1)} %collective-permute-done.18.refs_0_.refs_1_, bf16[272,384]{1,0:T(8,128)(2,1)S(1)} %collective-permute-done.20.refs_3_.refs_2_, ...), custom_call_target="tpu_custom_call" | custom-call | flops 1 | bytes 1 | tf_op jit(solution)/shard_map/final/pallas_call | solution.py:667
  101.5 2.4 %collective-permute-start.28 = (bf16[256,384]{1,0:T(8,128)(2,1)S(1)}, bf16[256,384]{1,0:T(8,128)(2,1)S(1)}, u32[]{:S(2)}, u32[]{:S(2)}) collective-permute-start(bf16[256,384]{1,0:T(8,128)(2,1)S(1)} %get-tuple-element.116), channel_id=1, source_target_pairs={{0,4},{1,5},{2,6},{3,7},{4,0},{5,1},{6,2},{7,3},{8,12},{9,13},{10,... | collective-permute-start | bytes 589832 | tf_op jit(solution)/shard_map/ppermute | solution.py:692
  104.9 1.9 %place.1 = bf16[256,4096]{1,0:T(8,128)(2,1)} custom-call(s32[5]{0:T(128)S(1)} %stack.23.place, bf16[256,512]{1,0:T(8,128)(2,1)S(1)} %get-tuple-element.108.refs_6_.refs_0_, bf16[256,768]{1,0:T(8,128)(2,1)S(1)} %get-tuple-element.107.refs_2_.refs_1_, bf16[256,384]{1,0:T(8,128)(2,1)S(1)} %get-tuple-element.110.refs_6_.refs_2_, ...), custom_call_target="tpu_custom_call" | custom-call | flops 1 | bytes 1 | tf_op jit(solution)/shard_map/place/pallas_call | solution.py:629
  (71 shorter events, 26.7 us)
Async XLA Ops:
  4.1 11.4 %collective-permute-start.4 = (bf16[64,8448]{1,0:T(8,128)(2,1)S(1)}, bf16[64,8448]{1,0:T(8,128)(2,1)S(1)}, u32[]{:S(2)}, u32[]{:S(2)}) collective-permute-start(bf16[64,8448]{1,0:T(8,128)(2,1)S(1)} %get-tuple-element.66), channel_id=1, source_target_pairs={{0,4},{1,5},{2,6},{3,7},{4,0},{5,1},{6,2},{7,3},{8,12},{9,13},{10,... | collective-permute-start | bytes 3244040 | tf_op jit(solution)/shard_map/ppermute | solution.py:692
  4.9 3.1 %collective-permute-start = (bf16[64,4096]{1,0:T(8,128)(2,1)S(1)}, bf16[64,4096]{1,0:T(8,128)(2,1)S(1)}, u32[]{:S(2)}, u32[]{:S(2)}) collective-permute-start(bf16[64,4096]{1,0:T(8,128)(2,1)S(1)} %pack_first.1.order), channel_id=1, source_target_pairs={{0,4},{1,5},{2,6},{3,7},{4,0},{5,1},{6,2},{7,3},{8,12},{9,13},{10,... | collective-permute-start | bytes 1572872 | tf_op jit(solution)/shard_map/ppermute | solution.py:692
  8.8 10.5 %collective-permute-start.1 = (bf16[128,512]{1,0:T(8,128)(2,1)S(1)}, bf16[128,512]{1,0:T(8,128)(2,1)S(1)}, u32[]{:S(2)}, u32[]{:S(2)}) collective-permute-start(bf16[128,512]{1,0:T(8,128)(2,1)S(1)} %get-tuple-element.63), channel_id=1, source_target_pairs={{0,2},{1,3},{2,0},{3,1},{4,6},{5,7},{6,4},{7,5},{8,10},{9,11},{10,... | collective-permute-start | bytes 393224 | tf_op jit(solution)/shard_map/ppermute | solution.py:692
  11.2 4.4 %collective-permute-start.5 = (bf16[3,10240]{1,0:T(4,128)(2,1)S(1)}, bf16[3,10240]{1,0:T(4,128)(2,1)S(1)}, u32[]{:S(2)}, u32[]{:S(2)}) collective-permute-start(bf16[3,10240]{1,0:T(4,128)(2,1)S(1)} %get-tuple-element.69), channel_id=1, source_target_pairs={{3,11},{7,15},{11,19},{15,23},{19,27},{23,31}} | collective-permute-start | bytes 184328 | tf_op jit(solution)/shard_map/ppermute | solution.py:692
  11.8 14.5 %collective-permute-start.2 = (bf16[128,512]{1,0:T(8,128)(2,1)S(1)}, bf16[128,512]{1,0:T(8,128)(2,1)S(1)}, u32[]{:S(2)}, u32[]{:S(2)}) collective-permute-start(bf16[128,512]{1,0:T(8,128)(2,1)S(1)} %get-tuple-element.64), channel_id=1, source_target_pairs={{0,3},{1,2},{2,1},{3,0},{4,7},{5,6},{6,5},{7,4},{8,11},{9,10},{10,... | collective-permute-start | bytes 393224 | tf_op jit(solution)/shard_map/ppermute | solution.py:692
  11.9 14.5 %collective-permute-start.3 = (bf16[128,512]{1,0:T(8,128)(2,1)S(1)}, bf16[128,512]{1,0:T(8,128)(2,1)S(1)}, u32[]{:S(2)}, u32[]{:S(2)}) collective-permute-start(bf16[128,512]{1,0:T(8,128)(2,1)S(1)} %get-tuple-element.65), channel_id=1, source_target_pairs={{0,1},{1,0},{2,3},{3,2},{4,5},{5,4},{6,7},{7,6},{8,9},{9,8},{10,11... | collective-permute-start | bytes 393224 | tf_op jit(solution)/shard_map/ppermute | solution.py:692
  16.6 12.4 %collective-permute-start.6 = (bf16[128,384]{1,0:T(8,128)(2,1)S(1)}, bf16[128,384]{1,0:T(8,128)(2,1)S(1)}, u32[]{:S(2)}, u32[]{:S(2)}) collective-permute-start(bf16[128,384]{1,0:T(8,128)(2,1)S(1)} %get-tuple-element.71), channel_id=1, source_target_pairs={{0,2},{1,3},{2,0},{3,1},{4,6},{5,7},{6,4},{7,5},{8,10},{9,11},{10,... | collective-permute-start | bytes 294920 | tf_op jit(solution)/shard_map/ppermute | solution.py:692
  18.7 12.5 %collective-permute-start.7 = (bf16[128,384]{1,0:T(8,128)(2,1)S(1)}, bf16[128,384]{1,0:T(8,128)(2,1)S(1)}, u32[]{:S(2)}, u32[]{:S(2)}) collective-permute-start(bf16[128,384]{1,0:T(8,128)(2,1)S(1)} %get-tuple-element.72), channel_id=1, source_target_pairs={{0,3},{1,2},{2,1},{3,0},{4,7},{5,6},{6,5},{7,4},{8,11},{9,10},{10,... | collective-permute-start | bytes 294920 | tf_op jit(solution)/shard_map/ppermute | solution.py:692
  19.3 11.9 %collective-permute-start.8 = (bf16[128,384]{1,0:T(8,128)(2,1)S(1)}, bf16[128,384]{1,0:T(8,128)(2,1)S(1)}, u32[]{:S(2)}, u32[]{:S(2)}) collective-permute-start(bf16[128,384]{1,0:T(8,128)(2,1)S(1)} %get-tuple-element.73), channel_id=1, source_target_pairs={{0,1},{1,0},{2,3},{3,2},{4,5},{5,4},{6,7},{7,6},{8,9},{9,8},{10,11... | collective-permute-start | bytes 294920 | tf_op jit(solution)/shard_map/ppermute | solution.py:692
  21.1 13.5 %copy-start.5 = (f32[256]{0:T(256)S(1)}, f32[256]{0:T(256)}, u32[]{:S(2)}) copy-start(f32[256]{0:T(256)} %param.11) | copy-start | bytes 3076
  21.1 13.4 %copy-start.6 = (f32[256]{0:T(256)S(1)}, f32[256]{0:T(256)}, u32[]{:S(2)}) copy-start(f32[256]{0:T(256)} %param.12) | copy-start | bytes 3076
  21.9 20.9 %copy-start.1 = (bf16[64,20480]{1,0:T(8,128)(2,1)S(1)}, bf16[64,20480]{1,0:T(8,128)(2,1)}, u32[]{:S(2)}) copy-start(bf16[64,20480]{1,0:T(8,128)(2,1)} %xbc.11) | copy-start | bytes 7864324
  31.2 17.7 %collective-permute-start.14 = (bf16[128,1792]{1,0:T(8,128)(2,1)S(1)}, bf16[128,1792]{1,0:T(8,128)(2,1)S(1)}, u32[]{:S(2)}, u32[]{:S(2)}) collective-permute-start(bf16[128,1792]{1,0:T(8,128)(2,1)S(1)} %get-tuple-element.90), channel_id=1, source_target_pairs={{0,1},{1,0},{2,3},{3,2},{4,5},{5,4},{6,7},{7,6},{8,9},{9,8},{10,11... | collective-permute-start | bytes 1376264 | tf_op jit(solution)/shard_map/ppermute | solution.py:692
  31.2 17.7 %collective-permute-start.12 = (bf16[128,768]{1,0:T(8,128)(2,1)S(1)}, bf16[128,768]{1,0:T(8,128)(2,1)S(1)}, u32[]{:S(2)}, u32[]{:S(2)}) collective-permute-start(bf16[128,768]{1,0:T(8,128)(2,1)S(1)} %get-tuple-element.88), channel_id=1, source_target_pairs={{0,2},{1,3},{2,0},{3,1},{4,6},{5,7},{6,4},{7,5},{8,10},{9,11},{10,... | collective-permute-start | bytes 589832 | tf_op jit(solution)/shard_map/ppermute | solution.py:692
  34.6 14.4 %collective-permute-start.13 = (bf16[128,768]{1,0:T(8,128)(2,1)S(1)}, bf16[128,768]{1,0:T(8,128)(2,1)S(1)}, u32[]{:S(2)}, u32[]{:S(2)}) collective-permute-start(bf16[128,768]{1,0:T(8,128)(2,1)S(1)} %get-tuple-element.89), channel_id=1, source_target_pairs={{0,3},{1,2},{2,1},{3,0},{4,7},{5,6},{6,5},{7,4},{8,11},{9,10},{10,... | collective-permute-start | bytes 589832 | tf_op jit(solution)/shard_map/ppermute | solution.py:692
  38.3 5.3 %collective-permute-start.9 = (bf16[272,256]{1,0:T(8,128)(2,1)S(1)}, bf16[272,256]{1,0:T(8,128)(2,1)S(1)}, u32[]{:S(2)}, u32[]{:S(2)}) collective-permute-start(bf16[272,256]{1,0:T(8,128)(2,1)S(1)} %get-tuple-element.79.refs_0_.refs_2_), channel_id=1, source_target_pairs={{0,8},{1,9},{2,10},{3,11},{4,12},{5,13},{6,14},{7,15},{8,0},{9,1},... | collective-permute-start | bytes 417800 | tf_op jit(solution)/shard_map/ppermute | solution.py:692
  41.5 4.9 %collective-permute-start.10 = (bf16[272,256]{1,0:T(8,128)(2,1)S(1)}, bf16[272,256]{1,0:T(8,128)(2,1)S(1)}, u32[]{:S(2)}, u32[]{:S(2)}) collective-permute-start(bf16[272,256]{1,0:T(8,128)(2,1)S(1)} %get-tuple-element.80.refs_1_.refs_3_), channel_id=1, source_target_pairs={{0,8},{1,9},{2,10},{3,11},{4,12},{5,13},{6,14},{7,15},{8,0},{9,1},... | collective-permute-start | bytes 417800 | tf_op jit(solution)/shard_map/ppermute | solution.py:692
  47.1 23.2 %collective-permute-start.11 = (bf16[272,512]{1,0:T(8,128)(2,1)S(1)}, bf16[272,512]{1,0:T(8,128)(2,1)S(1)}, u32[]{:S(2)}, u32[]{:S(2)}) collective-permute-start(bf16[272,512]{1,0:T(8,128)(2,1)S(1)} %combine.5.refs_10_), channel_id=1, source_target_pairs={{0,16},{1,17},{2,18},{3,19},{4,20},{5,21},{6,22},{7,23},{8,24},{9,... | collective-permute-start | bytes 835592 | tf_op jit(solution)/shard_map/ppermute | solution.py:692
  48.9 21.3 %collective-permute-start.15 = (bf16[128,1024]{1,0:T(8,128)(2,1)S(1)}, bf16[128,1024]{1,0:T(8,128)(2,1)S(1)}, u32[]{:S(2)}, u32[]{:S(2)}) collective-permute-start(bf16[128,1024]{1,0:T(8,128)(2,1)S(1)} %get-tuple-element.91), channel_id=1, source_target_pairs={{0,2},{1,3},{2,0},{3,1},{4,6},{5,7},{6,4},{7,5},{8,10},{9,11},{10,... | collective-permute-start | bytes 786440 | tf_op jit(solution)/shard_map/ppermute | solution.py:692
  53.4 23.6 %collective-permute-start.16 = (bf16[128,1024]{1,0:T(8,128)(2,1)S(1)}, bf16[128,1024]{1,0:T(8,128)(2,1)S(1)}, u32[]{:S(2)}, u32[]{:S(2)}) collective-permute-start(bf16[128,1024]{1,0:T(8,128)(2,1)S(1)} %get-tuple-element.92), channel_id=1, source_target_pairs={{0,3},{1,2},{2,1},{3,0},{4,7},{5,6},{6,5},{7,4},{8,11},{9,10},{10,... | collective-permute-start | bytes 786440 | tf_op jit(solution)/shard_map/ppermute | solution.py:692
  58.1 5.9 %collective-permute-start.17 = (bf16[272,384]{1,0:T(8,128)(2,1)S(1)}, bf16[272,384]{1,0:T(8,128)(2,1)S(1)}, u32[]{:S(2)}, u32[]{:S(2)}) collective-permute-start(bf16[272,384]{1,0:T(8,128)(2,1)S(1)} %get-tuple-element.93.refs_1_), channel_id=1, source_target_pairs={{0,8},{1,9},{2,10},{3,11},{4,12},{5,13},{6,14},{7,15},{8,0},{9,1},... | collective-permute-start | bytes 626696 | tf_op jit(solution)/shard_map/ppermute | solution.py:692
  61.2 7.0 %collective-permute-start.18 = (bf16[272,384]{1,0:T(8,128)(2,1)S(1)}, bf16[272,384]{1,0:T(8,128)(2,1)S(1)}, u32[]{:S(2)}, u32[]{:S(2)}) collective-permute-start(bf16[272,384]{1,0:T(8,128)(2,1)S(1)} %get-tuple-element.94.refs_1_), channel_id=1, source_target_pairs={{0,8},{1,9},{2,10},{3,11},{4,12},{5,13},{6,14},{7,15},{8,0},{9,1},... | collective-permute-start | bytes 626696 | tf_op jit(solution)/shard_map/ppermute | solution.py:692
  64.6 23.0 %collective-permute-start.20 = (bf16[272,384]{1,0:T(8,128)(2,1)S(1)}, bf16[272,384]{1,0:T(8,128)(2,1)S(1)}, u32[]{:S(2)}, u32[]{:S(2)}) collective-permute-start(bf16[272,384]{1,0:T(8,128)(2,1)S(1)} %combine.6.refs_2_.refs_10_), channel_id=1, source_target_pairs={{0,16},{1,17},{2,18},{3,19},{4,20},{5,21},{6,22},{7,23},{8,24},{9,... | collective-permute-start | bytes 626696 | tf_op jit(solution)/shard_map/ppermute | solution.py:692
  68.9 18.7 %collective-permute-start.21 = (bf16[272,384]{1,0:T(8,128)(2,1)S(1)}, bf16[272,384]{1,0:T(8,128)(2,1)S(1)}, u32[]{:S(2)}, u32[]{:S(2)}) collective-permute-start(bf16[272,384]{1,0:T(8,128)(2,1)S(1)} %combine.7.refs_11_), channel_id=1, source_target_pairs={{0,16},{1,17},{2,18},{3,19},{4,20},{5,21},{6,22},{7,23},{8,24},{9,... | collective-permute-start | bytes 626696 | tf_op jit(solution)/shard_map/ppermute | solution.py:692
  78.9 8.7 %collective-permute-start.22 = (bf16[272,384]{1,0:T(8,128)(2,1)S(1)}, bf16[272,384]{1,0:T(8,128)(2,1)S(1)}, u32[]{:S(2)}, u32[]{:S(2)}) collective-permute-start(bf16[272,384]{1,0:T(8,128)(2,1)S(1)} %get-tuple-element.95.refs_8_.refs_1_), channel_id=1, source_target_pairs={{0,8},{1,9},{2,10},{3,11},{4,12},{5,13},{6,14},{7,15},{8,0},{9,1},... | collective-permute-start | bytes 626696 | tf_op jit(solution)/shard_map/ppermute | solution.py:692
  86.3 5.9 %collective-permute-start.19 = (bf16[272,384]{1,0:T(8,128)(2,1)S(1)}, bf16[272,384]{1,0:T(8,128)(2,1)S(1)}, u32[]{:S(2)}, u32[]{:S(2)}) collective-permute-start(bf16[272,384]{1,0:T(8,128)(2,1)S(1)} %get-tuple-element.104.refs_2_.refs_1_), channel_id=1, source_target_pairs={{0,8},{1,9},{2,10},{3,11},{4,12},{5,13},{6,14},{7,15},{8,0},{9,1},... | collective-permute-start | bytes 626696 | tf_op jit(solution)/shard_map/ppermute | solution.py:692
  88.3 9.5 %collective-permute-start.23 = (bf16[272,384]{1,0:T(8,128)(2,1)S(1)}, bf16[272,384]{1,0:T(8,128)(2,1)S(1)}, u32[]{:S(2)}, u32[]{:S(2)}) collective-permute-start(bf16[272,384]{1,0:T(8,128)(2,1)S(1)} %combine.8.refs_12_), channel_id=1, source_target_pairs={{0,16},{1,17},{2,18},{3,19},{4,20},{5,21},{6,22},{7,23},{8,24},{9,... | collective-permute-start | bytes 626696 | tf_op jit(solution)/shard_map/ppermute | solution.py:692
  92.9 7.5 %collective-permute-start.24 = (bf16[272,384]{1,0:T(8,128)(2,1)S(1)}, bf16[272,384]{1,0:T(8,128)(2,1)S(1)}, u32[]{:S(2)}, u32[]{:S(2)}) collective-permute-start(bf16[272,384]{1,0:T(8,128)(2,1)S(1)} %combine.9.refs_0_), channel_id=1, source_target_pairs={{0,16},{1,17},{2,18},{3,19},{4,20},{5,21},{6,22},{7,23},{8,24},{9,... | collective-permute-start | bytes 626696 | tf_op jit(solution)/shard_map/ppermute | solution.py:692
  94.2 9.7 %collective-permute-start.26 = (bf16[256,768]{1,0:T(8,128)(2,1)S(1)}, bf16[256,768]{1,0:T(8,128)(2,1)S(1)}, u32[]{:S(2)}, u32[]{:S(2)}) collective-permute-start(bf16[256,768]{1,0:T(8,128)(2,1)S(1)} %get-tuple-element.114), channel_id=1, source_target_pairs={{0,4},{1,5},{2,6},{3,7},{4,0},{5,1},{6,2},{7,3},{8,12},{9,13},{10,... | collective-permute-start | bytes 1179656 | tf_op jit(solution)/shard_map/ppermute | solution.py:692
  97.7 6.2 %collective-permute-start.25 = (bf16[256,512]{1,0:T(8,128)(2,1)S(1)}, bf16[256,512]{1,0:T(8,128)(2,1)S(1)}, u32[]{:S(2)}, u32[]{:S(2)}) collective-permute-start(bf16[256,512]{1,0:T(8,128)(2,1)S(1)} %get-tuple-element.113), channel_id=1, source_target_pairs={{0,4},{1,5},{2,6},{3,7},{4,0},{5,1},{6,2},{7,3},{8,12},{9,13},{10,... | collective-permute-start | bytes 786440 | tf_op jit(solution)/shard_map/ppermute | solution.py:692
  98.8 5.0 %collective-permute-start.27 = (bf16[256,384]{1,0:T(8,128)(2,1)S(1)}, bf16[256,384]{1,0:T(8,128)(2,1)S(1)}, u32[]{:S(2)}, u32[]{:S(2)}) collective-permute-start(bf16[256,384]{1,0:T(8,128)(2,1)S(1)} %get-tuple-element.115), channel_id=1, source_target_pairs={{0,4},{1,5},{2,6},{3,7},{4,0},{5,1},{6,2},{7,3},{8,12},{9,13},{10,... | collective-permute-start | bytes 589832 | tf_op jit(solution)/shard_map/ppermute | solution.py:692
  101.5 3.4 %collective-permute-start.28 = (bf16[256,384]{1,0:T(8,128)(2,1)S(1)}, bf16[256,384]{1,0:T(8,128)(2,1)S(1)}, u32[]{:S(2)}, u32[]{:S(2)}) collective-permute-start(bf16[256,384]{1,0:T(8,128)(2,1)S(1)} %get-tuple-element.116), channel_id=1, source_target_pairs={{0,4},{1,5},{2,6},{3,7},{4,0},{5,1},{6,2},{7,3},{8,12},{9,13},{10,... | collective-permute-start | bytes 589832 | tf_op jit(solution)/shard_map/ppermute | solution.py:692
  (5 other events, 19.9 us)

commit v19 on v18

--- a/solution.py
+++ b/solution.py
@@ -216,19 +216,11 @@
 
 def pack_first_kernel(shards, place, xbc, send, sems):
     core, shard = place[2], place[4]
-    count = xbc.shape[0]
     width = WIDTHS[0]
     copies = []
     for r in range(shards):
         group = (shard ^ FLIP[r]) * PAIR + 1 - core
         copies.append((xbc.at[:, channels(group, 0, width)], send.at[:, r * width : (r + 1) * width]))
-        last, rows = xbc.at[count - 16 :], slice(16 * r, 16 * r + 16)
-        to = shards * width
-        copies.append((last.at[:, channels(group, width, PER_GROUP - width)], send.at[rows, to : to + PER_GROUP - width]))
-        to += PER_GROUP - width
-        for i in range(2):
-            at = ds(INNER + (i * GROUPS + group) * STATE, STATE)
-            copies.append((last.at[:, at], send.at[rows, to + i * STATE : to + (i + 1) * STATE]))
     for copy in run(copies, sems):
         copy.wait()
 
@@ -272,19 +264,20 @@
         copy.wait()
 
 
-def put_edge(shards, place, got, tail, out):
+def edge_kernel(shards, place, got_first, got, tail, out):
     count = got.shape[0]
     first = WIDTHS[0]
+    width = PER_GROUP - first
     size = PER_GROUP + 2 * STATE
     for r in range(shards):
-        theirs = [got[count - 16 :, r * first : (r + 1) * first]]
-        theirs.append(got[16 * r : 16 * r + 16, shards * first :])
+        theirs = [(got_first, r * first, first), (got, r * width, width)]
+        theirs += [(got, width * shards + (i * shards + r) * STATE, STATE) for i in range(2)]
         to = r * size
-        for part in theirs:
-            at = slice(to, to + part.shape[1])
-            rows = jnp.where(place[2] == 0, part.astype(F32), tail[:, at].astype(F32))
-            out[:, at] = rows[13:16].astype(BF16)
-            to = at.stop
+        for ref, start, size_of in theirs:
+            a = ref[count - 16 :, start : start + size_of].astype(F32)
+            b = tail[:, to : to + size_of].astype(F32)
+            out[:, to : to + size_of] = jnp.where(place[2] == 0, a, b)[13:16].astype(BF16)
+            to += size_of
 
 
 def total_of(piece):
@@ -326,8 +319,6 @@
                 copies.append((got.at[:, at : at + STATE], out.at[other, to : to + STATE]))
                 to += STATE
     started = run(copies, sems)
-    if len(refs) > len(plan) + 1:
-        put_edge(shards, place, got_first, edges, refs[-2])
     if steps:
         lane = lax.broadcasted_iota(jnp.int32, (count, LANES), 1)
         per_tile = LANES * GROUPS // HEADS
@@ -698,9 +689,9 @@
     size = PER_GROUP + 2 * STATE
     (sent,) = call(
         functools.partial(pack_first_kernel, shards),
-        [((tok, shards * WIDTHS[0] + size - WIDTHS[0]), BF16)],
+        [((tok, shards * WIDTHS[0]), BF16)],
         [place, rows],
-        scratch=[pltpu.SemaphoreType.DMA((4 * shards,))],
+        scratch=[pltpu.SemaphoreType.DMA((shards,))],
         name="pack_first",
     )
     got_first = swap(sent)
@@ -720,20 +711,19 @@
         name="taps",
     )
 
-    def send_on(plan, order, tail=None, edges=None):
+    def send_on(plan, order, edges=None):
         unused = Stay(got_first)
         parts = [p for _, pieces in plan for p in pieces]
-        made = [] if tail is None else [((3, shards * size), BF16)]
         return call(
             functools.partial(merge_kernel, shards, plan, len(order)),
-            [((PAIR * tok, sum(map(total_of, pieces))), BF16) for _, pieces in plan] + made,
+            [((PAIR * tok, sum(map(total_of, pieces))), BF16) for _, pieces in plan],
             [
                 place,
                 rows,
                 Stay(dt_raw) if edges is None else dt_raw,
                 got_first if 0 in parts else unused,
                 got_rest if any(parts) else unused,
-                next((o for o in (tail, edges) if o is not None), unused),
+                unused if edges is None else edges,
             ]
             + [Stay(o) for o in order],
             scratch=[pltpu.SemaphoreType.DMA((sum(2 + 2 * len(RESTS[p]) for p in parts),))],
@@ -746,10 +736,16 @@
     def plan(piece):
         return [(r, (piece,)) for r in range(shards)]
 
-    *first_blocks, edges = send_on(plan(0), [], tail)
+    first_blocks = send_on(plan(0), [])
     message = [travel(first_blocks)]
+    (edges,) = call(
+        functools.partial(edge_kernel, shards),
+        [((3, shards * size), BF16)],
+        [place, got_first, got_rest, tail],
+        name="edge",
+    )
     edges = over(edges, lambda i: i + peers if i % shards == shards - 1 else None)
-    second_blocks = send_on(plan(1), [first_blocks[0]], None, edges)
+    second_blocks = send_on(plan(1), [first_blocks[0]], edges)
     message.append(travel(second_blocks))
     third_plan = [(r, (2, 3) if r == NEAR else (2,)) for r in range(shards)]
     third_blocks = send_on(third_plan, [second_blocks[0]])

time: 108 us -> 107 us (level)
  waiting for transfers between devices: 28.8 us -> 27.2 us
    ppermute x29, waiting for transfers between devices: 28.8 us -> 27.2 us  [over(): lax.ppermute(block, axes, [(i, j) for i, j in route if j is not None and...]
    pallas_call x25 -> x26, Pallas kernels: 29.5 us -> 29.7 us  [call(): pl.pallas_call(body, out_shape=shapes, in_specs=specs, out_specs=[vmem] *...]
  transfers between devices with their start and end apart: 29 -> 29, of which waited for: 12 -> 11; matrix products, arithmetic and copies ran while one was open for 0% -> 0% of each run, Pallas kernels for 25% -> 26%
where the time goes in v19:
time: 107 us; the launch traced here: 106 us
  starting transfers between devices  45 us (42%)
  Pallas kernels  31.6 us (30%)
  waiting for transfers between devices  27.2 us (25%)
  local copies, waits for them, and re-layouts  1.86 us (2%)
    ppermute x29, starting transfers between devices, over(): lax.ppermute(block, axes, [(i, j) for i, j in route if j is not None and...  45 us
    pallas_call x26, Pallas kernels, call(): pl.pallas_call(body, out_shape=shapes, in_specs=specs, out_specs=[vmem] *...  29.7 us
    ppermute x29, waiting for transfers between devices, over(): lax.ppermute(block, axes, [(i, j) for i, j in route if j is not None and...  27.2 us
  transfers between devices with their start and end apart: 29, of which 11 were waited for; matrix products, arithmetic and copies ran while one was open for 0% of the time, Pallas kernels for 26%

profile of v19, /device:TPU:13, one launch (start us, length us, event | category | flops | bytes accessed | tf_op | source)
XLA Modules:
  0.0 106.2 jit_solution(14767637860349463088)
XLA Ops:
  0.1 1.7 %copy-done = bf16[64,20480]{1,0:T(8,128)(2,1)S(1)} copy-done((bf16[64,20480]{1,0:T(8,128)(2,1)S(1)}, bf16[64,20480]{1,0:T(8,128)(2,1)}, u32[]{:S(2)}) %copy-start) | copy-done | bytes 2621464
  2.5 1.3 %pack.1 = (bf16[64,8448]{1,0:T(8,128)(2,1)S(1)}, bf16[16,10240]{1,0:T(8,128)(2,1)S(1)}) custom-call(s32[5]{0:T(128)S(1)} %stack.23.place, bf16[64,20480]{1,0:T(8,128)(2,1)S(1)} %copy-done, bf16[64,256]{1,0:T(8,128)(2,1)S(1)} %copy-done.2, bf16[64,2048]{1,0:T(8,128)(2,1)S(1)} %pack_first.1.order), custom_call_target="tpu_custom_call" | custom-call | flops 1 | bytes 1 | tf_op jit(solution)/shard_map/pack/pallas_call | solution.py:658
  4.7 2.6 %collective-permute-done.got_first.got.edges = bf16[64,2048]{1,0:T(8,128)(2,1)S(1)} collective-permute-done((bf16[64,2048]{1,0:T(8,128)(2,1)S(1)}, bf16[64,2048]{1,0:T(8,128)(2,1)S(1)}, u32[]{:S(2)}, u32[]{:S(2)}) %collective-permute-start) | collective-permute-done | bytes 262176 | tf_op jit(solution)/shard_map/ppermute | solution.py:683
  8.0 2.4 %collective-permute-start.1 = (bf16[128,512]{1,0:T(8,128)(2,1)S(1)}, bf16[128,512]{1,0:T(8,128)(2,1)S(1)}, u32[]{:S(2)}, u32[]{:S(2)}) collective-permute-start(bf16[128,512]{1,0:T(8,128)(2,1)S(1)} %get-tuple-element.61), channel_id=1, source_target_pairs={{0,2},{1,3},{2,0},{3,1},{4,6},{5,7},{6,4},{7,5},{8,10},{9,11},{10,... | collective-permute-start | bytes 393224 | tf_op jit(solution)/shard_map/ppermute | solution.py:683
  11.8 3.7 %collective-permute-start.3 = (bf16[128,512]{1,0:T(8,128)(2,1)S(1)}, bf16[128,512]{1,0:T(8,128)(2,1)S(1)}, u32[]{:S(2)}, u32[]{:S(2)}) collective-permute-start(bf16[128,512]{1,0:T(8,128)(2,1)S(1)} %get-tuple-element.63), channel_id=1, source_target_pairs={{0,1},{1,0},{2,3},{3,2},{4,5},{5,4},{6,7},{7,6},{8,9},{9,8},{10,11... | collective-permute-start | bytes 393224 | tf_op jit(solution)/shard_map/ppermute | solution.py:683
  16.5 2.1 %collective-permute-start.6 = (bf16[128,384]{1,0:T(8,128)(2,1)S(1)}, bf16[128,384]{1,0:T(8,128)(2,1)S(1)}, u32[]{:S(2)}, u32[]{:S(2)}) collective-permute-start(bf16[128,384]{1,0:T(8,128)(2,1)S(1)} %get-tuple-element.69), channel_id=1, source_target_pairs={{0,2},{1,3},{2,0},{3,1},{4,6},{5,7},{6,4},{7,5},{8,10},{9,11},{10,... | collective-permute-start | bytes 294920 | tf_op jit(solution)/shard_map/ppermute | solution.py:683
  18.6 1.6 %collective-permute-start.8 = (bf16[128,384]{1,0:T(8,128)(2,1)S(1)}, bf16[128,384]{1,0:T(8,128)(2,1)S(1)}, u32[]{:S(2)}, u32[]{:S(2)}) collective-permute-start(bf16[128,384]{1,0:T(8,128)(2,1)S(1)} %get-tuple-element.71), channel_id=1, source_target_pairs={{0,1},{1,0},{2,3},{3,2},{4,5},{5,4},{6,7},{7,6},{8,9},{9,8},{10,11... | collective-permute-start | bytes 294920 | tf_op jit(solution)/shard_map/ppermute | solution.py:683
  21.7 3.2 %collective-permute-done.2.refs_2_.refs_4_ = bf16[128,512]{1,0:T(8,128)(2,1)S(1)} collective-permute-done((bf16[128,512]{1,0:T(8,128)(2,1)S(1)}, bf16[128,512]{1,0:T(8,128)(2,1)S(1)}, u32[]{:S(2)}, u32[]{:S(2)}) %collective-permute-start.2) | collective-permute-done | bytes 131104 | tf_op jit(solution)/shard_map/ppermute | solution.py:683
  24.9 3.4 %collective-permute-done.6.refs_1_.refs_6_ = bf16[128,384]{1,0:T(8,128)(2,1)S(1)} collective-permute-done((bf16[128,384]{1,0:T(8,128)(2,1)S(1)}, bf16[128,384]{1,0:T(8,128)(2,1)S(1)}, u32[]{:S(2)}, u32[]{:S(2)}) %collective-permute-start.6) | collective-permute-done | bytes 98336 | tf_op jit(solution)/shard_map/ppermute | solution.py:683
  28.3 2.1 %collective-permute-done.7.refs_2_.refs_7_ = bf16[128,384]{1,0:T(8,128)(2,1)S(1)} collective-permute-done((bf16[128,384]{1,0:T(8,128)(2,1)S(1)}, bf16[128,384]{1,0:T(8,128)(2,1)S(1)}, u32[]{:S(2)}, u32[]{:S(2)}) %collective-permute-start.7) | collective-permute-done | bytes 98336 | tf_op jit(solution)/shard_map/ppermute | solution.py:683
  30.4 3.4 %collective-permute-start.12 = (bf16[128,768]{1,0:T(8,128)(2,1)S(1)}, bf16[128,768]{1,0:T(8,128)(2,1)S(1)}, u32[]{:S(2)}, u32[]{:S(2)}) collective-permute-start(bf16[128,768]{1,0:T(8,128)(2,1)S(1)} %get-tuple-element.86), channel_id=1, source_target_pairs={{0,2},{1,3},{2,0},{3,1},{4,6},{5,7},{6,4},{7,5},{8,10},{9,11},{10,... | collective-permute-start | bytes 589832 | tf_op jit(solution)/shard_map/ppermute | solution.py:683
  33.8 1.7 %prep.1 = (bf16[512,256]{1,0:T(8,128)(2,1)S(1)}, f32[4,2560]{1,0:T(4,128)S(1)}, f32[512,128]{1,0:T(8,128)S(1)}, f32[128,512]{1,0:T(8,128)S(1)}, bf16[512,256]{1,...) custom-call(s32[5]{0:T(128)S(1)} %stack.23.place, ...), custom_call_target="tpu_custom_call" | custom-call | flops 1 | bytes 1 | tf_op jit(solution)/shard_map/prep/pallas_call | solution.py:658
  35.5 2.1 %state.4 = (bf16[512,512]{1,0:T(8,128)(2,1)S(1)}, f32[256,512]{1,0:T(8,128)S(1)}, bf16[272,256]{1,0:T(8,128)(2,1)S(1)}, bf16[272,256]{1,0:T(8,128)(2,1)S(1)}) custom-call(s32[5]{0:T(128)S(1)} %stack.23.place, bf16[128,512]{1,0:T(8,128)(2,1)S(1)} %get-tuple-element.60.refs_0_, bf16[128,512]{1,0:T(8,128)(2,1)S(1)} %collective-permute-done.1.refs_1_.refs_3_, ...), custom_call_target="tpu_custom_call" | custom-call | flops 1 | bytes 1 | tf_op jit(solution)/shard_map/state/pallas_call | solution.py:658
  37.6 3.1 %collective-permute-start.9 = (bf16[272,256]{1,0:T(8,128)(2,1)S(1)}, bf16[272,256]{1,0:T(8,128)(2,1)S(1)}, u32[]{:S(2)}, u32[]{:S(2)}) collective-permute-start(bf16[272,256]{1,0:T(8,128)(2,1)S(1)} %get-tuple-element.77.refs_0_.refs_2_), channel_id=1, source_target_pairs={{0,8},{1,9},{2,10},{3,11},{4,12},{5,13},{6,14},{7,15},{8,0},{9,1},... | collective-permute-start | bytes 417800 | tf_op jit(solution)/shard_map/ppermute | solution.py:683
  40.7 1.3 %collective-permute-start.10 = (bf16[272,256]{1,0:T(8,128)(2,1)S(1)}, bf16[272,256]{1,0:T(8,128)(2,1)S(1)}, u32[]{:S(2)}, u32[]{:S(2)}) collective-permute-start(bf16[272,256]{1,0:T(8,128)(2,1)S(1)} %get-tuple-element.78.refs_1_.refs_3_), channel_id=1, source_target_pairs={{0,8},{1,9},{2,10},{3,11},{4,12},{5,13},{6,14},{7,15},{8,0},{9,1},... | collective-permute-start | bytes 417800 | tf_op jit(solution)/shard_map/ppermute | solution.py:683
  42.9 2.7 %collective-permute-done.10.refs_1_ = bf16[272,256]{1,0:T(8,128)(2,1)S(1)} collective-permute-done((bf16[272,256]{1,0:T(8,128)(2,1)S(1)}, bf16[272,256]{1,0:T(8,128)(2,1)S(1)}, u32[]{:S(2)}, u32[]{:S(2)}) %collective-permute-start.10) | collective-permute-done | bytes 139296 | tf_op jit(solution)/shard_map/ppermute | solution.py:683
  48.2 4.4 %collective-permute-start.15 = (bf16[128,1024]{1,0:T(8,128)(2,1)S(1)}, bf16[128,1024]{1,0:T(8,128)(2,1)S(1)}, u32[]{:S(2)}, u32[]{:S(2)}) collective-permute-start(bf16[128,1024]{1,0:T(8,128)(2,1)S(1)} %get-tuple-element.89), channel_id=1, source_target_pairs={{0,2},{1,3},{2,0},{3,1},{4,6},{5,7},{6,4},{7,5},{8,10},{9,11},{10,... | collective-permute-start | bytes 786440 | tf_op jit(solution)/shard_map/ppermute | solution.py:683
  52.6 2.2 %collective-permute-start.16 = (bf16[128,1024]{1,0:T(8,128)(2,1)S(1)}, bf16[128,1024]{1,0:T(8,128)(2,1)S(1)}, u32[]{:S(2)}, u32[]{:S(2)}) collective-permute-start(bf16[128,1024]{1,0:T(8,128)(2,1)S(1)} %get-tuple-element.90), channel_id=1, source_target_pairs={{0,3},{1,2},{2,1},{3,0},{4,7},{5,6},{6,5},{7,4},{8,11},{9,10},{10,... | collective-permute-start | bytes 786440 | tf_op jit(solution)/shard_map/ppermute | solution.py:683
  54.7 2.6 %state.5 = (bf16[512,768]{1,0:T(8,128)(2,1)S(1)}, f32[256,768]{1,0:T(8,128)S(1)}, bf16[272,384]{1,0:T(8,128)(2,1)S(1)}, bf16[272,384]{1,0:T(8,128)(2,1)S(1)}) custom-call(s32[5]{0:T(128)S(1)} %stack.23.place, bf16[128,768]{1,0:T(8,128)(2,1)S(1)} %get-tuple-element.72.refs_9_.refs_0_, bf16[128,768]{1,0:T(8,128)(2,1)S(1)} %collective-permute-done.12.refs_2_.refs_1_, ...), custom_call_target="tpu_custom_call" | custom-call | flops 1 | bytes 1 | tf_op jit(solution)/shard_map/state/pallas_call | solution.py:658
  57.3 3.1 %collective-permute-start.17 = (bf16[272,384]{1,0:T(8,128)(2,1)S(1)}, bf16[272,384]{1,0:T(8,128)(2,1)S(1)}, u32[]{:S(2)}, u32[]{:S(2)}) collective-permute-start(bf16[272,384]{1,0:T(8,128)(2,1)S(1)} %get-tuple-element.91.refs_1_), channel_id=1, source_target_pairs={{0,8},{1,9},{2,10},{3,11},{4,12},{5,13},{6,14},{7,15},{8,0},{9,1},... | collective-permute-start | bytes 626696 | tf_op jit(solution)/shard_map/ppermute | solution.py:683
  60.5 1.3 %collective-permute-start.18 = (bf16[272,384]{1,0:T(8,128)(2,1)S(1)}, bf16[272,384]{1,0:T(8,128)(2,1)S(1)}, u32[]{:S(2)}, u32[]{:S(2)}) collective-permute-start(bf16[272,384]{1,0:T(8,128)(2,1)S(1)} %get-tuple-element.92.refs_1_), channel_id=1, source_target_pairs={{0,8},{1,9},{2,10},{3,11},{4,12},{5,13},{6,14},{7,15},{8,0},{9,1},... | collective-permute-start | bytes 626696 | tf_op jit(solution)/shard_map/ppermute | solution.py:683
  61.8 1.4 %collective-permute-done.17.refs_0_ = bf16[272,384]{1,0:T(8,128)(2,1)S(1)} collective-permute-done((bf16[272,384]{1,0:T(8,128)(2,1)S(1)}, bf16[272,384]{1,0:T(8,128)(2,1)S(1)}, u32[]{:S(2)}, u32[]{:S(2)}) %collective-permute-start.17) | collective-permute-done | bytes 208928 | tf_op jit(solution)/shard_map/ppermute | solution.py:683
  63.8 1.3 %collective-permute-start.20 = (bf16[272,384]{1,0:T(8,128)(2,1)S(1)}, bf16[272,384]{1,0:T(8,128)(2,1)S(1)}, u32[]{:S(2)}, u32[]{:S(2)}) collective-permute-start(bf16[272,384]{1,0:T(8,128)(2,1)S(1)} %combine.6.refs_2_.refs_10_), channel_id=1, source_target_pairs={{0,16},{1,17},{2,18},{3,19},{4,20},{5,21},{6,22},{7,23},{8,24},{9,... | collective-permute-start | bytes 626696 | tf_op jit(solution)/shard_map/ppermute | solution.py:683
  65.1 2.4 %collective-permute-done.18.refs_0_.refs_1_ = bf16[272,384]{1,0:T(8,128)(2,1)S(1)} collective-permute-done((bf16[272,384]{1,0:T(8,128)(2,1)S(1)}, bf16[272,384]{1,0:T(8,128)(2,1)S(1)}, u32[]{:S(2)}, u32[]{:S(2)}) %collective-permute-start.18) | collective-permute-done | bytes 208928 | tf_op jit(solution)/shard_map/ppermute | solution.py:683
  69.5 6.7 %collective-permute-done.16.refs_2_ = bf16[128,1024]{1,0:T(8,128)(2,1)S(1)} collective-permute-done((bf16[128,1024]{1,0:T(8,128)(2,1)S(1)}, bf16[128,1024]{1,0:T(8,128)(2,1)S(1)}, u32[]{:S(2)}, u32[]{:S(2)}) %collective-permute-start.16) | collective-permute-done | bytes 262176 | tf_op jit(solution)/shard_map/ppermute | solution.py:683
  76.2 1.9 %state.6 = (bf16[512,384]{1,0:T(8,128)(2,1)S(1)}, f32[256,384]{1,0:T(8,128)S(1)}, bf16[272,384]{1,0:T(8,128)(2,1)S(1)}) custom-call(s32[5]{0:T(128)S(1)} %stack.23.place, bf16[128,1024]{1,0:T(8,128)(2,1)S(1)} %get-tuple-element.79.refs_4_.refs_0_, bf16[128,1024]{1,0:T(8,128)(2,1)S(1)} %collective-permute-done.15.refs_1_, ...), custom_call_target="tpu_custom_call" | custom-call | flops 1 | bytes 1 | tf_op jit(solution)/shard_map/state/pallas_call | solution.py:658
  78.1 3.3 %collective-permute-start.22 = (bf16[272,384]{1,0:T(8,128)(2,1)S(1)}, bf16[272,384]{1,0:T(8,128)(2,1)S(1)}, u32[]{:S(2)}, u32[]{:S(2)}) collective-permute-start(bf16[272,384]{1,0:T(8,128)(2,1)S(1)} %get-tuple-element.93.refs_8_.refs_1_), channel_id=1, source_target_pairs={{0,8},{1,9},{2,10},{3,11},{4,12},{5,13},{6,14},{7,15},{8,0},{9,1},... | collective-permute-start | bytes 626696 | tf_op jit(solution)/shard_map/ppermute | solution.py:683
  83.6 1.9 %state.7 = (bf16[512,384]{1,0:T(8,128)(2,1)S(1)}, f32[256,384]{1,0:T(8,128)S(1)}, bf16[272,384]{1,0:T(8,128)(2,1)S(1)}) custom-call(s32[5]{0:T(128)S(1)} %stack.23.place, bf16[128,1024]{1,0:T(8,128)(2,1)S(1)} %get-tuple-element.79.refs_4_.refs_0_, bf16[128,1024]{1,0:T(8,128)(2,1)S(1)} %collective-permute-done.15.refs_1_, ...), custom_call_target="tpu_custom_call" | custom-call | flops 1 | bytes 1 | tf_op jit(solution)/shard_map/state/pallas_call | solution.py:658
  85.5 1.3 %collective-permute-start.19 = (bf16[272,384]{1,0:T(8,128)(2,1)S(1)}, bf16[272,384]{1,0:T(8,128)(2,1)S(1)}, u32[]{:S(2)}, u32[]{:S(2)}) collective-permute-start(bf16[272,384]{1,0:T(8,128)(2,1)S(1)} %get-tuple-element.102.refs_2_.refs_1_), channel_id=1, source_target_pairs={{0,8},{1,9},{2,10},{3,11},{4,12},{5,13},{6,14},{7,15},{8,0},{9,1},... | collective-permute-start | bytes 626696 | tf_op jit(solution)/shard_map/ppermute | solution.py:683
  88.8 2.6 %final.4 = (bf16[256,768]{1,0:T(8,128)(2,1)S(1)}, bf16[256,768]{1,0:T(8,128)(2,1)S(1)}) custom-call(s32[5]{0:T(128)S(1)} %stack.23.place, bf16[272,384]{1,0:T(8,128)(2,1)S(1)} %collective-permute-done.17.refs_0_, bf16[272,384]{1,0:T(8,128)(2,1)S(1)} %collective-permute-done.18.refs_0_.refs_1_, bf16[272,384]{1,0:T(8,128)(2,1)S(1)} %collective-permute-done.20.refs_3_.refs_2_, ...), custom_call_target="tpu_custom_call" | custom-call | flops 1 | bytes 1 | tf_op jit(solution)/shard_map/final/pallas_call | solution.py:658
  100.7 2.4 %collective-permute-start.28 = (bf16[256,384]{1,0:T(8,128)(2,1)S(1)}, bf16[256,384]{1,0:T(8,128)(2,1)S(1)}, u32[]{:S(2)}, u32[]{:S(2)}) collective-permute-start(bf16[256,384]{1,0:T(8,128)(2,1)S(1)} %get-tuple-element.114), channel_id=1, source_target_pairs={{0,4},{1,5},{2,6},{3,7},{4,0},{5,1},{6,2},{7,3},{8,12},{9,13},{10,... | collective-permute-start | bytes 589832 | tf_op jit(solution)/shard_map/ppermute | solution.py:683
  104.1 1.9 %place.1 = bf16[256,4096]{1,0:T(8,128)(2,1)} custom-call(s32[5]{0:T(128)S(1)} %stack.23.place, bf16[256,512]{1,0:T(8,128)(2,1)S(1)} %get-tuple-element.106.refs_6_.refs_0_, bf16[256,768]{1,0:T(8,128)(2,1)S(1)} %get-tuple-element.105.refs_2_.refs_1_, bf16[256,384]{1,0:T(8,128)(2,1)S(1)} %get-tuple-element.108.refs_6_.refs_2_, ...), custom_call_target="tpu_custom_call" | custom-call | flops 1 | bytes 1 | tf_op jit(solution)/shard_map/place/pallas_call | solution.py:620
  (72 shorter events, 26.7 us)
Async XLA Ops:
  3.8 6.6 %collective-permute-start.4 = (bf16[64,8448]{1,0:T(8,128)(2,1)S(1)}, bf16[64,8448]{1,0:T(8,128)(2,1)S(1)}, u32[]{:S(2)}, u32[]{:S(2)}) collective-permute-start(bf16[64,8448]{1,0:T(8,128)(2,1)S(1)} %get-tuple-element.64), channel_id=1, source_target_pairs={{0,4},{1,5},{2,6},{3,7},{4,0},{5,1},{6,2},{7,3},{8,12},{9,13},{10,... | collective-permute-start | bytes 3244040 | tf_op jit(solution)/shard_map/ppermute | solution.py:683
  4.6 2.7 %collective-permute-start = (bf16[64,2048]{1,0:T(8,128)(2,1)S(1)}, bf16[64,2048]{1,0:T(8,128)(2,1)S(1)}, u32[]{:S(2)}, u32[]{:S(2)}) collective-permute-start(bf16[64,2048]{1,0:T(8,128)(2,1)S(1)} %pack_first.1.order), channel_id=1, source_target_pairs={{0,4},{1,5},{2,6},{3,7},{4,0},{5,1},{6,2},{7,3},{8,12},{9,13},{10,... | collective-permute-start | bytes 786440 | tf_op jit(solution)/shard_map/ppermute | solution.py:683
  8.0 10.6 %collective-permute-start.1 = (bf16[128,512]{1,0:T(8,128)(2,1)S(1)}, bf16[128,512]{1,0:T(8,128)(2,1)S(1)}, u32[]{:S(2)}, u32[]{:S(2)}) collective-permute-start(bf16[128,512]{1,0:T(8,128)(2,1)S(1)} %get-tuple-element.61), channel_id=1, source_target_pairs={{0,2},{1,3},{2,0},{3,1},{4,6},{5,7},{6,4},{7,5},{8,10},{9,11},{10,... | collective-permute-start | bytes 393224 | tf_op jit(solution)/shard_map/ppermute | solution.py:683
  11.0 4.4 %collective-permute-start.5 = (bf16[3,10240]{1,0:T(4,128)(2,1)S(1)}, bf16[3,10240]{1,0:T(4,128)(2,1)S(1)}, u32[]{:S(2)}, u32[]{:S(2)}) collective-permute-start(bf16[3,10240]{1,0:T(4,128)(2,1)S(1)} %edge.1), channel_id=1, source_target_pairs={{3,11},{7,15},{11,19},{15,23},{19,27},{23,31}} | collective-permute-start | bytes 184328 | tf_op jit(solution)/shard_map/ppermute | solution.py:683
  11.7 13.2 %collective-permute-start.2 = (bf16[128,512]{1,0:T(8,128)(2,1)S(1)}, bf16[128,512]{1,0:T(8,128)(2,1)S(1)}, u32[]{:S(2)}, u32[]{:S(2)}) collective-permute-start(bf16[128,512]{1,0:T(8,128)(2,1)S(1)} %get-tuple-element.62), channel_id=1, source_target_pairs={{0,3},{1,2},{2,1},{3,0},{4,7},{5,6},{6,5},{7,4},{8,11},{9,10},{10,... | collective-permute-start | bytes 393224 | tf_op jit(solution)/shard_map/ppermute | solution.py:683
  11.8 13.2 %collective-permute-start.3 = (bf16[128,512]{1,0:T(8,128)(2,1)S(1)}, bf16[128,512]{1,0:T(8,128)(2,1)S(1)}, u32[]{:S(2)}, u32[]{:S(2)}) collective-permute-start(bf16[128,512]{1,0:T(8,128)(2,1)S(1)} %get-tuple-element.63), channel_id=1, source_target_pairs={{0,1},{1,0},{2,3},{3,2},{4,5},{5,4},{6,7},{7,6},{8,9},{9,8},{10,11... | collective-permute-start | bytes 393224 | tf_op jit(solution)/shard_map/ppermute | solution.py:683
  16.5 11.8 %collective-permute-start.6 = (bf16[128,384]{1,0:T(8,128)(2,1)S(1)}, bf16[128,384]{1,0:T(8,128)(2,1)S(1)}, u32[]{:S(2)}, u32[]{:S(2)}) collective-permute-start(bf16[128,384]{1,0:T(8,128)(2,1)S(1)} %get-tuple-element.69), channel_id=1, source_target_pairs={{0,2},{1,3},{2,0},{3,1},{4,6},{5,7},{6,4},{7,5},{8,10},{9,11},{10,... | collective-permute-start | bytes 294920 | tf_op jit(solution)/shard_map/ppermute | solution.py:683
  18.6 11.8 %collective-permute-start.7 = (bf16[128,384]{1,0:T(8,128)(2,1)S(1)}, bf16[128,384]{1,0:T(8,128)(2,1)S(1)}, u32[]{:S(2)}, u32[]{:S(2)}) collective-permute-start(bf16[128,384]{1,0:T(8,128)(2,1)S(1)} %get-tuple-element.70), channel_id=1, source_target_pairs={{0,3},{1,2},{2,1},{3,0},{4,7},{5,6},{6,5},{7,4},{8,11},{9,10},{10,... | collective-permute-start | bytes 294920 | tf_op jit(solution)/shard_map/ppermute | solution.py:683
  18.6 11.8 %collective-permute-start.8 = (bf16[128,384]{1,0:T(8,128)(2,1)S(1)}, bf16[128,384]{1,0:T(8,128)(2,1)S(1)}, u32[]{:S(2)}, u32[]{:S(2)}) collective-permute-start(bf16[128,384]{1,0:T(8,128)(2,1)S(1)} %get-tuple-element.71), channel_id=1, source_target_pairs={{0,1},{1,0},{2,3},{3,2},{4,5},{5,4},{6,7},{7,6},{8,9},{9,8},{10,11... | collective-permute-start | bytes 294920 | tf_op jit(solution)/shard_map/ppermute | solution.py:683
  20.8 13.0 %copy-start.5 = (f32[256]{0:T(256)S(1)}, f32[256]{0:T(256)}, u32[]{:S(2)}) copy-start(f32[256]{0:T(256)} %param.11) | copy-start | bytes 3076
  20.8 13.0 %copy-start.6 = (f32[256]{0:T(256)S(1)}, f32[256]{0:T(256)}, u32[]{:S(2)}) copy-start(f32[256]{0:T(256)} %param.12) | copy-start | bytes 3076
  20.8 13.0 %copy-start.7 = (f32[256]{0:T(256)S(1)}, f32[256]{0:T(256)}, u32[]{:S(2)}) copy-start(f32[256]{0:T(256)} %param.13) | copy-start | bytes 3076
  30.4 17.7 %collective-permute-start.14 = (bf16[128,1792]{1,0:T(8,128)(2,1)S(1)}, bf16[128,1792]{1,0:T(8,128)(2,1)S(1)}, u32[]{:S(2)}, u32[]{:S(2)}) collective-permute-start(bf16[128,1792]{1,0:T(8,128)(2,1)S(1)} %get-tuple-element.88), channel_id=1, source_target_pairs={{0,1},{1,0},{2,3},{3,2},{4,5},{5,4},{6,7},{7,6},{8,9},{9,8},{10,11... | collective-permute-start | bytes 1376264 | tf_op jit(solution)/shard_map/ppermute | solution.py:683
  30.4 17.7 %collective-permute-start.12 = (bf16[128,768]{1,0:T(8,128)(2,1)S(1)}, bf16[128,768]{1,0:T(8,128)(2,1)S(1)}, u32[]{:S(2)}, u32[]{:S(2)}) collective-permute-start(bf16[128,768]{1,0:T(8,128)(2,1)S(1)} %get-tuple-element.86), channel_id=1, source_target_pairs={{0,2},{1,3},{2,0},{3,1},{4,6},{5,7},{6,4},{7,5},{8,10},{9,11},{10,... | collective-permute-start | bytes 589832 | tf_op jit(solution)/shard_map/ppermute | solution.py:683
  33.8 14.4 %collective-permute-start.13 = (bf16[128,768]{1,0:T(8,128)(2,1)S(1)}, bf16[128,768]{1,0:T(8,128)(2,1)S(1)}, u32[]{:S(2)}, u32[]{:S(2)}) collective-permute-start(bf16[128,768]{1,0:T(8,128)(2,1)S(1)} %get-tuple-element.87), channel_id=1, source_target_pairs={{0,3},{1,2},{2,1},{3,0},{4,7},{5,6},{6,5},{7,4},{8,11},{9,10},{10,... | collective-permute-start | bytes 589832 | tf_op jit(solution)/shard_map/ppermute | solution.py:683
  37.6 5.3 %collective-permute-start.9 = (bf16[272,256]{1,0:T(8,128)(2,1)S(1)}, bf16[272,256]{1,0:T(8,128)(2,1)S(1)}, u32[]{:S(2)}, u32[]{:S(2)}) collective-permute-start(bf16[272,256]{1,0:T(8,128)(2,1)S(1)} %get-tuple-element.77.refs_0_.refs_2_), channel_id=1, source_target_pairs={{0,8},{1,9},{2,10},{3,11},{4,12},{5,13},{6,14},{7,15},{8,0},{9,1},... | collective-permute-start | bytes 417800 | tf_op jit(solution)/shard_map/ppermute | solution.py:683
  40.7 4.9 %collective-permute-start.10 = (bf16[272,256]{1,0:T(8,128)(2,1)S(1)}, bf16[272,256]{1,0:T(8,128)(2,1)S(1)}, u32[]{:S(2)}, u32[]{:S(2)}) collective-permute-start(bf16[272,256]{1,0:T(8,128)(2,1)S(1)} %get-tuple-element.78.refs_1_.refs_3_), channel_id=1, source_target_pairs={{0,8},{1,9},{2,10},{3,11},{4,12},{5,13},{6,14},{7,15},{8,0},{9,1},... | collective-permute-start | bytes 417800 | tf_op jit(solution)/shard_map/ppermute | solution.py:683
  46.3 23.2 %collective-permute-start.11 = (bf16[272,512]{1,0:T(8,128)(2,1)S(1)}, bf16[272,512]{1,0:T(8,128)(2,1)S(1)}, u32[]{:S(2)}, u32[]{:S(2)}) collective-permute-start(bf16[272,512]{1,0:T(8,128)(2,1)S(1)} %combine.5.refs_10_), channel_id=1, source_target_pairs={{0,16},{1,17},{2,18},{3,19},{4,20},{5,21},{6,22},{7,23},{8,24},{9,... | collective-permute-start | bytes 835592 | tf_op jit(solution)/shard_map/ppermute | solution.py:683
  48.2 21.3 %collective-permute-start.15 = (bf16[128,1024]{1,0:T(8,128)(2,1)S(1)}, bf16[128,1024]{1,0:T(8,128)(2,1)S(1)}, u32[]{:S(2)}, u32[]{:S(2)}) collective-permute-start(bf16[128,1024]{1,0:T(8,128)(2,1)S(1)} %get-tuple-element.89), channel_id=1, source_target_pairs={{0,2},{1,3},{2,0},{3,1},{4,6},{5,7},{6,4},{7,5},{8,10},{9,11},{10,... | collective-permute-start | bytes 786440 | tf_op jit(solution)/shard_map/ppermute | solution.py:683
  52.6 23.6 %collective-permute-start.16 = (bf16[128,1024]{1,0:T(8,128)(2,1)S(1)}, bf16[128,1024]{1,0:T(8,128)(2,1)S(1)}, u32[]{:S(2)}, u32[]{:S(2)}) collective-permute-start(bf16[128,1024]{1,0:T(8,128)(2,1)S(1)} %get-tuple-element.90), channel_id=1, source_target_pairs={{0,3},{1,2},{2,1},{3,0},{4,7},{5,6},{6,5},{7,4},{8,11},{9,10},{10,... | collective-permute-start | bytes 786440 | tf_op jit(solution)/shard_map/ppermute | solution.py:683
  57.3 5.9 %collective-permute-start.17 = (bf16[272,384]{1,0:T(8,128)(2,1)S(1)}, bf16[272,384]{1,0:T(8,128)(2,1)S(1)}, u32[]{:S(2)}, u32[]{:S(2)}) collective-permute-start(bf16[272,384]{1,0:T(8,128)(2,1)S(1)} %get-tuple-element.91.refs_1_), channel_id=1, source_target_pairs={{0,8},{1,9},{2,10},{3,11},{4,12},{5,13},{6,14},{7,15},{8,0},{9,1},... | collective-permute-start | bytes 626696 | tf_op jit(solution)/shard_map/ppermute | solution.py:683
  60.5 7.0 %collective-permute-start.18 = (bf16[272,384]{1,0:T(8,128)(2,1)S(1)}, bf16[272,384]{1,0:T(8,128)(2,1)S(1)}, u32[]{:S(2)}, u32[]{:S(2)}) collective-permute-start(bf16[272,384]{1,0:T(8,128)(2,1)S(1)} %get-tuple-element.92.refs_1_), channel_id=1, source_target_pairs={{0,8},{1,9},{2,10},{3,11},{4,12},{5,13},{6,14},{7,15},{8,0},{9,1},... | collective-permute-start | bytes 626696 | tf_op jit(solution)/shard_map/ppermute | solution.py:683
  63.8 23.0 %collective-permute-start.20 = (bf16[272,384]{1,0:T(8,128)(2,1)S(1)}, bf16[272,384]{1,0:T(8,128)(2,1)S(1)}, u32[]{:S(2)}, u32[]{:S(2)}) collective-permute-start(bf16[272,384]{1,0:T(8,128)(2,1)S(1)} %combine.6.refs_2_.refs_10_), channel_id=1, source_target_pairs={{0,16},{1,17},{2,18},{3,19},{4,20},{5,21},{6,22},{7,23},{8,24},{9,... | collective-permute-start | bytes 626696 | tf_op jit(solution)/shard_map/ppermute | solution.py:683
  68.1 18.7 %collective-permute-start.21 = (bf16[272,384]{1,0:T(8,128)(2,1)S(1)}, bf16[272,384]{1,0:T(8,128)(2,1)S(1)}, u32[]{:S(2)}, u32[]{:S(2)}) collective-permute-start(bf16[272,384]{1,0:T(8,128)(2,1)S(1)} %combine.7.refs_11_), channel_id=1, source_target_pairs={{0,16},{1,17},{2,18},{3,19},{4,20},{5,21},{6,22},{7,23},{8,24},{9,... | collective-permute-start | bytes 626696 | tf_op jit(solution)/shard_map/ppermute | solution.py:683
  78.1 8.7 %collective-permute-start.22 = (bf16[272,384]{1,0:T(8,128)(2,1)S(1)}, bf16[272,384]{1,0:T(8,128)(2,1)S(1)}, u32[]{:S(2)}, u32[]{:S(2)}) collective-permute-start(bf16[272,384]{1,0:T(8,128)(2,1)S(1)} %get-tuple-element.93.refs_8_.refs_1_), channel_id=1, source_target_pairs={{0,8},{1,9},{2,10},{3,11},{4,12},{5,13},{6,14},{7,15},{8,0},{9,1},... | collective-permute-start | bytes 626696 | tf_op jit(solution)/shard_map/ppermute | solution.py:683
  85.5 5.9 %collective-permute-start.19 = (bf16[272,384]{1,0:T(8,128)(2,1)S(1)}, bf16[272,384]{1,0:T(8,128)(2,1)S(1)}, u32[]{:S(2)}, u32[]{:S(2)}) collective-permute-start(bf16[272,384]{1,0:T(8,128)(2,1)S(1)} %get-tuple-element.102.refs_2_.refs_1_), channel_id=1, source_target_pairs={{0,8},{1,9},{2,10},{3,11},{4,12},{5,13},{6,14},{7,15},{8,0},{9,1},... | collective-permute-start | bytes 626696 | tf_op jit(solution)/shard_map/ppermute | solution.py:683
  87.5 9.5 %collective-permute-start.23 = (bf16[272,384]{1,0:T(8,128)(2,1)S(1)}, bf16[272,384]{1,0:T(8,128)(2,1)S(1)}, u32[]{:S(2)}, u32[]{:S(2)}) collective-permute-start(bf16[272,384]{1,0:T(8,128)(2,1)S(1)} %combine.8.refs_12_), channel_id=1, source_target_pairs={{0,16},{1,17},{2,18},{3,19},{4,20},{5,21},{6,22},{7,23},{8,24},{9,... | collective-permute-start | bytes 626696 | tf_op jit(solution)/shard_map/ppermute | solution.py:683
  92.1 7.5 %collective-permute-start.24 = (bf16[272,384]{1,0:T(8,128)(2,1)S(1)}, bf16[272,384]{1,0:T(8,128)(2,1)S(1)}, u32[]{:S(2)}, u32[]{:S(2)}) collective-permute-start(bf16[272,384]{1,0:T(8,128)(2,1)S(1)} %combine.9.refs_0_), channel_id=1, source_target_pairs={{0,16},{1,17},{2,18},{3,19},{4,20},{5,21},{6,22},{7,23},{8,24},{9,... | collective-permute-start | bytes 626696 | tf_op jit(solution)/shard_map/ppermute | solution.py:683
  93.4 9.7 %collective-permute-start.26 = (bf16[256,768]{1,0:T(8,128)(2,1)S(1)}, bf16[256,768]{1,0:T(8,128)(2,1)S(1)}, u32[]{:S(2)}, u32[]{:S(2)}) collective-permute-start(bf16[256,768]{1,0:T(8,128)(2,1)S(1)} %get-tuple-element.112), channel_id=1, source_target_pairs={{0,4},{1,5},{2,6},{3,7},{4,0},{5,1},{6,2},{7,3},{8,12},{9,13},{10,... | collective-permute-start | bytes 1179656 | tf_op jit(solution)/shard_map/ppermute | solution.py:683
  96.9 6.2 %collective-permute-start.25 = (bf16[256,512]{1,0:T(8,128)(2,1)S(1)}, bf16[256,512]{1,0:T(8,128)(2,1)S(1)}, u32[]{:S(2)}, u32[]{:S(2)}) collective-permute-start(bf16[256,512]{1,0:T(8,128)(2,1)S(1)} %get-tuple-element.111), channel_id=1, source_target_pairs={{0,4},{1,5},{2,6},{3,7},{4,0},{5,1},{6,2},{7,3},{8,12},{9,13},{10,... | collective-permute-start | bytes 786440 | tf_op jit(solution)/shard_map/ppermute | solution.py:683
  98.1 5.0 %collective-permute-start.27 = (bf16[256,384]{1,0:T(8,128)(2,1)S(1)}, bf16[256,384]{1,0:T(8,128)(2,1)S(1)}, u32[]{:S(2)}, u32[]{:S(2)}) collective-permute-start(bf16[256,384]{1,0:T(8,128)(2,1)S(1)} %get-tuple-element.113), channel_id=1, source_target_pairs={{0,4},{1,5},{2,6},{3,7},{4,0},{5,1},{6,2},{7,3},{8,12},{9,13},{10,... | collective-permute-start | bytes 589832 | tf_op jit(solution)/shard_map/ppermute | solution.py:683
  100.7 3.4 %collective-permute-start.28 = (bf16[256,384]{1,0:T(8,128)(2,1)S(1)}, bf16[256,384]{1,0:T(8,128)(2,1)S(1)}, u32[]{:S(2)}, u32[]{:S(2)}) collective-permute-start(bf16[256,384]{1,0:T(8,128)(2,1)S(1)} %get-tuple-element.114), channel_id=1, source_target_pairs={{0,4},{1,5},{2,6},{3,7},{4,0},{5,1},{6,2},{7,3},{8,12},{9,13},{10,... | collective-permute-start | bytes 589832 | tf_op jit(solution)/shard_map/ppermute | solution.py:683
  (5 other events, 25.2 us)

commit v20 on v19

--- a/solution.py
+++ b/solution.py
@@ -702,7 +702,7 @@
         scratch=[pltpu.SemaphoreType.DMA((6 * shards + 1,))],
         name="pack",
     )
-    got_rest = swap(sent)
+    got_rest = swap(gate([sent], [got_first])[0])
     taps, offset = call(
         taps_kernel,
         [((4, size), F32), ((1, size), F32)],

time: 107 us -> 105 us (0.981)
  waiting for transfers between devices: 27.2 us -> 22.2 us
  starting transfers between devices: 45 us -> 47.4 us
    ppermute x29, waiting for transfers between devices: 27.2 us -> 22.2 us  [over(): lax.ppermute(block, axes, [(i, j) for i, j in route if j is not None and...]
    ppermute x29, starting transfers between devices: 45 us -> 47.4 us  [over(): lax.ppermute(block, axes, [(i, j) for i, j in route if j is not None and...]
  transfers between devices with their start and end apart: 29 -> 29, of which waited for: 11 -> 9; matrix products, arithmetic and copies ran while one was open for 0% -> 0% of each run, Pallas kernels for 26% -> 28%
where the time goes in v20:
time: 105 us; the launch traced here: 104 us
  starting transfers between devices  47.4 us (45%)
  Pallas kernels  31.6 us (30%)
  waiting for transfers between devices  22.2 us (21%)
  local copies, waits for them, and re-layouts  2.06 us (2%)
    ppermute x29, starting transfers between devices, over(): lax.ppermute(block, axes, [(i, j) for i, j in route if j is not None and...  47.4 us
    pallas_call x26, Pallas kernels, call(): pl.pallas_call(body, out_shape=shapes, in_specs=specs, out_specs=[vmem] *...  29.7 us
    ppermute x29, waiting for transfers between devices, over(): lax.ppermute(block, axes, [(i, j) for i, j in route if j is not None and...  22.2 us
  transfers between devices with their start and end apart: 29, of which 9 were waited for; matrix products, arithmetic and copies ran while one was open for 0% of the time, Pallas kernels for 28%

profile of v20, /device:TPU:13, one launch (start us, length us, event | category | flops | bytes accessed | tf_op | source)
XLA Modules:
  0.0 103.9 jit_solution(14604214539192241052)
XLA Ops:
  0.1 1.7 %copy-done = bf16[64,20480]{1,0:T(8,128)(2,1)S(1)} copy-done((bf16[64,20480]{1,0:T(8,128)(2,1)S(1)}, bf16[64,20480]{1,0:T(8,128)(2,1)}, u32[]{:S(2)}) %copy-start) | copy-done | bytes 2621464
  3.2 1.3 %pack.1 = (bf16[64,8448]{1,0:T(8,128)(2,1)S(1)}, bf16[16,10240]{1,0:T(8,128)(2,1)S(1)}) custom-call(s32[5]{0:T(128)S(1)} %stack.23.place, bf16[64,20480]{1,0:T(8,128)(2,1)S(1)} %copy-done, bf16[64,256]{1,0:T(8,128)(2,1)S(1)} %copy-done.2, bf16[64,2048]{1,0:T(8,128)(2,1)S(1)} %pack_first.1.order), custom_call_target="tpu_custom_call" | custom-call | flops 1 | bytes 1 | tf_op jit(solution)/shard_map/pack/pallas_call | solution.py:658
  5.7 2.4 %collective-permute-start.1 = (bf16[128,512]{1,0:T(8,128)(2,1)S(1)}, bf16[128,512]{1,0:T(8,128)(2,1)S(1)}, u32[]{:S(2)}, u32[]{:S(2)}) collective-permute-start(bf16[128,512]{1,0:T(8,128)(2,1)S(1)} %get-tuple-element.61), channel_id=1, source_target_pairs={{0,2},{1,3},{2,0},{3,1},{4,6},{5,7},{6,4},{7,5},{8,10},{9,11},{10,... | collective-permute-start | bytes 393224 | tf_op jit(solution)/shard_map/ppermute | solution.py:683
  10.0 4.6 %collective-permute-start.3 = (bf16[128,512]{1,0:T(8,128)(2,1)S(1)}, bf16[128,512]{1,0:T(8,128)(2,1)S(1)}, u32[]{:S(2)}, u32[]{:S(2)}) collective-permute-start(bf16[128,512]{1,0:T(8,128)(2,1)S(1)} %get-tuple-element.63), channel_id=1, source_target_pairs={{0,1},{1,0},{2,3},{3,2},{4,5},{5,4},{6,7},{7,6},{8,9},{9,8},{10,11... | collective-permute-start | bytes 393224 | tf_op jit(solution)/shard_map/ppermute | solution.py:683
  15.7 2.4 %collective-permute-start.6 = (bf16[128,384]{1,0:T(8,128)(2,1)S(1)}, bf16[128,384]{1,0:T(8,128)(2,1)S(1)}, u32[]{:S(2)}, u32[]{:S(2)}) collective-permute-start(bf16[128,384]{1,0:T(8,128)(2,1)S(1)} %get-tuple-element.69), channel_id=1, source_target_pairs={{0,2},{1,3},{2,0},{3,1},{4,6},{5,7},{6,4},{7,5},{8,10},{9,11},{10,... | collective-permute-start | bytes 294920 | tf_op jit(solution)/shard_map/ppermute | solution.py:683
  21.0 4.5 %collective-permute-done.6.refs_1_.refs_6_ = bf16[128,384]{1,0:T(8,128)(2,1)S(1)} collective-permute-done((bf16[128,384]{1,0:T(8,128)(2,1)S(1)}, bf16[128,384]{1,0:T(8,128)(2,1)S(1)}, u32[]{:S(2)}, u32[]{:S(2)}) %collective-permute-start.6) | collective-permute-done | bytes 98336 | tf_op jit(solution)/shard_map/ppermute | solution.py:683
  25.5 2.5 %collective-permute-done.7.refs_2_.refs_7_ = bf16[128,384]{1,0:T(8,128)(2,1)S(1)} collective-permute-done((bf16[128,384]{1,0:T(8,128)(2,1)S(1)}, bf16[128,384]{1,0:T(8,128)(2,1)S(1)}, u32[]{:S(2)}, u32[]{:S(2)}) %collective-permute-start.7) | collective-permute-done | bytes 98336 | tf_op jit(solution)/shard_map/ppermute | solution.py:683
  27.9 3.4 %collective-permute-start.12 = (bf16[128,768]{1,0:T(8,128)(2,1)S(1)}, bf16[128,768]{1,0:T(8,128)(2,1)S(1)}, u32[]{:S(2)}, u32[]{:S(2)}) collective-permute-start(bf16[128,768]{1,0:T(8,128)(2,1)S(1)} %get-tuple-element.86), channel_id=1, source_target_pairs={{0,2},{1,3},{2,0},{3,1},{4,6},{5,7},{6,4},{7,5},{8,10},{9,11},{10,... | collective-permute-start | bytes 589832 | tf_op jit(solution)/shard_map/ppermute | solution.py:683
  31.3 1.7 %prep.1 = (bf16[512,256]{1,0:T(8,128)(2,1)S(1)}, f32[4,2560]{1,0:T(4,128)S(1)}, f32[512,128]{1,0:T(8,128)S(1)}, f32[128,512]{1,0:T(8,128)S(1)}, bf16[512,256]{1,...) custom-call(s32[5]{0:T(128)S(1)} %stack.23.place, ...), custom_call_target="tpu_custom_call" | custom-call | flops 1 | bytes 1 | tf_op jit(solution)/shard_map/prep/pallas_call | solution.py:658
  33.0 2.1 %state.4 = (bf16[512,512]{1,0:T(8,128)(2,1)S(1)}, f32[256,512]{1,0:T(8,128)S(1)}, bf16[272,256]{1,0:T(8,128)(2,1)S(1)}, bf16[272,256]{1,0:T(8,128)(2,1)S(1)}) custom-call(s32[5]{0:T(128)S(1)} %stack.23.place, bf16[128,512]{1,0:T(8,128)(2,1)S(1)} %get-tuple-element.60.refs_0_, bf16[128,512]{1,0:T(8,128)(2,1)S(1)} %collective-permute-done.1.refs_1_.refs_3_, ...), custom_call_target="tpu_custom_call" | custom-call | flops 1 | bytes 1 | tf_op jit(solution)/shard_map/state/pallas_call | solution.py:658
  35.1 3.3 %collective-permute-start.9 = (bf16[272,256]{1,0:T(8,128)(2,1)S(1)}, bf16[272,256]{1,0:T(8,128)(2,1)S(1)}, u32[]{:S(2)}, u32[]{:S(2)}) collective-permute-start(bf16[272,256]{1,0:T(8,128)(2,1)S(1)} %get-tuple-element.77.refs_0_.refs_2_), channel_id=1, source_target_pairs={{0,8},{1,9},{2,10},{3,11},{4,12},{5,13},{6,14},{7,15},{8,0},{9,1},... | collective-permute-start | bytes 417800 | tf_op jit(solution)/shard_map/ppermute | solution.py:683
  38.4 1.3 %collective-permute-start.10 = (bf16[272,256]{1,0:T(8,128)(2,1)S(1)}, bf16[272,256]{1,0:T(8,128)(2,1)S(1)}, u32[]{:S(2)}, u32[]{:S(2)}) collective-permute-start(bf16[272,256]{1,0:T(8,128)(2,1)S(1)} %get-tuple-element.78.refs_1_.refs_3_), channel_id=1, source_target_pairs={{0,8},{1,9},{2,10},{3,11},{4,12},{5,13},{6,14},{7,15},{8,0},{9,1},... | collective-permute-start | bytes 417800 | tf_op jit(solution)/shard_map/ppermute | solution.py:683
  40.6 2.8 %collective-permute-done.10.refs_1_ = bf16[272,256]{1,0:T(8,128)(2,1)S(1)} collective-permute-done((bf16[272,256]{1,0:T(8,128)(2,1)S(1)}, bf16[272,256]{1,0:T(8,128)(2,1)S(1)}, u32[]{:S(2)}, u32[]{:S(2)}) %collective-permute-start.10) | collective-permute-done | bytes 139296 | tf_op jit(solution)/shard_map/ppermute | solution.py:683
  44.0 1.3 %collective-permute-start.11 = (bf16[272,512]{1,0:T(8,128)(2,1)S(1)}, bf16[272,512]{1,0:T(8,128)(2,1)S(1)}, u32[]{:S(2)}, u32[]{:S(2)}) collective-permute-start(bf16[272,512]{1,0:T(8,128)(2,1)S(1)} %combine.5.refs_10_), channel_id=1, source_target_pairs={{0,16},{1,17},{2,18},{3,19},{4,20},{5,21},{6,22},{7,23},{8,24},{9,... | collective-permute-start | bytes 835592 | tf_op jit(solution)/shard_map/ppermute | solution.py:683
  45.6 4.4 %collective-permute-start.15 = (bf16[128,1024]{1,0:T(8,128)(2,1)S(1)}, bf16[128,1024]{1,0:T(8,128)(2,1)S(1)}, u32[]{:S(2)}, u32[]{:S(2)}) collective-permute-start(bf16[128,1024]{1,0:T(8,128)(2,1)S(1)} %get-tuple-element.89), channel_id=1, source_target_pairs={{0,2},{1,3},{2,0},{3,1},{4,6},{5,7},{6,4},{7,5},{8,10},{9,11},{10,... | collective-permute-start | bytes 786440 | tf_op jit(solution)/shard_map/ppermute | solution.py:683
  50.0 2.2 %collective-permute-start.16 = (bf16[128,1024]{1,0:T(8,128)(2,1)S(1)}, bf16[128,1024]{1,0:T(8,128)(2,1)S(1)}, u32[]{:S(2)}, u32[]{:S(2)}) collective-permute-start(bf16[128,1024]{1,0:T(8,128)(2,1)S(1)} %get-tuple-element.90), channel_id=1, source_target_pairs={{0,3},{1,2},{2,1},{3,0},{4,7},{5,6},{6,5},{7,4},{8,11},{9,10},{10,... | collective-permute-start | bytes 786440 | tf_op jit(solution)/shard_map/ppermute | solution.py:683
  52.1 2.6 %state.5 = (bf16[512,768]{1,0:T(8,128)(2,1)S(1)}, f32[256,768]{1,0:T(8,128)S(1)}, bf16[272,384]{1,0:T(8,128)(2,1)S(1)}, bf16[272,384]{1,0:T(8,128)(2,1)S(1)}) custom-call(s32[5]{0:T(128)S(1)} %stack.23.place, bf16[128,768]{1,0:T(8,128)(2,1)S(1)} %get-tuple-element.72.refs_9_.refs_0_, bf16[128,768]{1,0:T(8,128)(2,1)S(1)} %collective-permute-done.12.refs_2_.refs_1_, ...), custom_call_target="tpu_custom_call" | custom-call | flops 1 | bytes 1 | tf_op jit(solution)/shard_map/state/pallas_call | solution.py:658
  54.7 3.5 %collective-permute-start.17 = (bf16[272,384]{1,0:T(8,128)(2,1)S(1)}, bf16[272,384]{1,0:T(8,128)(2,1)S(1)}, u32[]{:S(2)}, u32[]{:S(2)}) collective-permute-start(bf16[272,384]{1,0:T(8,128)(2,1)S(1)} %get-tuple-element.91.refs_1_), channel_id=1, source_target_pairs={{0,8},{1,9},{2,10},{3,11},{4,12},{5,13},{6,14},{7,15},{8,0},{9,1},... | collective-permute-start | bytes 626696 | tf_op jit(solution)/shard_map/ppermute | solution.py:683
  58.2 1.3 %collective-permute-start.18 = (bf16[272,384]{1,0:T(8,128)(2,1)S(1)}, bf16[272,384]{1,0:T(8,128)(2,1)S(1)}, u32[]{:S(2)}, u32[]{:S(2)}) collective-permute-start(bf16[272,384]{1,0:T(8,128)(2,1)S(1)} %get-tuple-element.92.refs_1_), channel_id=1, source_target_pairs={{0,8},{1,9},{2,10},{3,11},{4,12},{5,13},{6,14},{7,15},{8,0},{9,1},... | collective-permute-start | bytes 626696 | tf_op jit(solution)/shard_map/ppermute | solution.py:683
  59.5 1.4 %collective-permute-done.17.refs_0_ = bf16[272,384]{1,0:T(8,128)(2,1)S(1)} collective-permute-done((bf16[272,384]{1,0:T(8,128)(2,1)S(1)}, bf16[272,384]{1,0:T(8,128)(2,1)S(1)}, u32[]{:S(2)}, u32[]{:S(2)}) %collective-permute-start.17) | collective-permute-done | bytes 208928 | tf_op jit(solution)/shard_map/ppermute | solution.py:683
  61.6 1.3 %collective-permute-start.20 = (bf16[272,384]{1,0:T(8,128)(2,1)S(1)}, bf16[272,384]{1,0:T(8,128)(2,1)S(1)}, u32[]{:S(2)}, u32[]{:S(2)}) collective-permute-start(bf16[272,384]{1,0:T(8,128)(2,1)S(1)} %combine.6.refs_2_.refs_10_), channel_id=1, source_target_pairs={{0,16},{1,17},{2,18},{3,19},{4,20},{5,21},{6,22},{7,23},{8,24},{9,... | collective-permute-start | bytes 626696 | tf_op jit(solution)/shard_map/ppermute | solution.py:683
  62.9 2.4 %collective-permute-done.18.refs_0_.refs_1_ = bf16[272,384]{1,0:T(8,128)(2,1)S(1)} collective-permute-done((bf16[272,384]{1,0:T(8,128)(2,1)S(1)}, bf16[272,384]{1,0:T(8,128)(2,1)S(1)}, u32[]{:S(2)}, u32[]{:S(2)}) %collective-permute-start.18) | collective-permute-done | bytes 208928 | tf_op jit(solution)/shard_map/ppermute | solution.py:683
  65.9 1.3 %collective-permute-start.21 = (bf16[272,384]{1,0:T(8,128)(2,1)S(1)}, bf16[272,384]{1,0:T(8,128)(2,1)S(1)}, u32[]{:S(2)}, u32[]{:S(2)}) collective-permute-start(bf16[272,384]{1,0:T(8,128)(2,1)S(1)} %combine.7.refs_11_), channel_id=1, source_target_pairs={{0,16},{1,17},{2,18},{3,19},{4,20},{5,21},{6,22},{7,23},{8,24},{9,... | collective-permute-start | bytes 626696 | tf_op jit(solution)/shard_map/ppermute | solution.py:683
  67.2 6.4 %collective-permute-done.16.refs_2_ = bf16[128,1024]{1,0:T(8,128)(2,1)S(1)} collective-permute-done((bf16[128,1024]{1,0:T(8,128)(2,1)S(1)}, bf16[128,1024]{1,0:T(8,128)(2,1)S(1)}, u32[]{:S(2)}, u32[]{:S(2)}) %collective-permute-start.16) | collective-permute-done | bytes 262176 | tf_op jit(solution)/shard_map/ppermute | solution.py:683
  73.6 1.9 %state.6 = (bf16[512,384]{1,0:T(8,128)(2,1)S(1)}, f32[256,384]{1,0:T(8,128)S(1)}, bf16[272,384]{1,0:T(8,128)(2,1)S(1)}) custom-call(s32[5]{0:T(128)S(1)} %stack.23.place, bf16[128,1024]{1,0:T(8,128)(2,1)S(1)} %get-tuple-element.79.refs_4_.refs_0_, bf16[128,1024]{1,0:T(8,128)(2,1)S(1)} %collective-permute-done.15.refs_1_, ...), custom_call_target="tpu_custom_call" | custom-call | flops 1 | bytes 1 | tf_op jit(solution)/shard_map/state/pallas_call | solution.py:658
  75.5 3.6 %collective-permute-start.22 = (bf16[272,384]{1,0:T(8,128)(2,1)S(1)}, bf16[272,384]{1,0:T(8,128)(2,1)S(1)}, u32[]{:S(2)}, u32[]{:S(2)}) collective-permute-start(bf16[272,384]{1,0:T(8,128)(2,1)S(1)} %get-tuple-element.93.refs_8_.refs_1_), channel_id=1, source_target_pairs={{0,8},{1,9},{2,10},{3,11},{4,12},{5,13},{6,14},{7,15},{8,0},{9,1},... | collective-permute-start | bytes 626696 | tf_op jit(solution)/shard_map/ppermute | solution.py:683
  81.3 1.9 %state.7 = (bf16[512,384]{1,0:T(8,128)(2,1)S(1)}, f32[256,384]{1,0:T(8,128)S(1)}, bf16[272,384]{1,0:T(8,128)(2,1)S(1)}) custom-call(s32[5]{0:T(128)S(1)} %stack.23.place, bf16[128,1024]{1,0:T(8,128)(2,1)S(1)} %get-tuple-element.79.refs_4_.refs_0_, bf16[128,1024]{1,0:T(8,128)(2,1)S(1)} %collective-permute-done.15.refs_1_, ...), custom_call_target="tpu_custom_call" | custom-call | flops 1 | bytes 1 | tf_op jit(solution)/shard_map/state/pallas_call | solution.py:658
  83.2 1.3 %collective-permute-start.19 = (bf16[272,384]{1,0:T(8,128)(2,1)S(1)}, bf16[272,384]{1,0:T(8,128)(2,1)S(1)}, u32[]{:S(2)}, u32[]{:S(2)}) collective-permute-start(bf16[272,384]{1,0:T(8,128)(2,1)S(1)} %get-tuple-element.102.refs_2_.refs_1_), channel_id=1, source_target_pairs={{0,8},{1,9},{2,10},{3,11},{4,12},{5,13},{6,14},{7,15},{8,0},{9,1},... | collective-permute-start | bytes 626696 | tf_op jit(solution)/shard_map/ppermute | solution.py:683
  85.2 1.3 %collective-permute-start.23 = (bf16[272,384]{1,0:T(8,128)(2,1)S(1)}, bf16[272,384]{1,0:T(8,128)(2,1)S(1)}, u32[]{:S(2)}, u32[]{:S(2)}) collective-permute-start(bf16[272,384]{1,0:T(8,128)(2,1)S(1)} %combine.8.refs_12_), channel_id=1, source_target_pairs={{0,16},{1,17},{2,18},{3,19},{4,20},{5,21},{6,22},{7,23},{8,24},{9,... | collective-permute-start | bytes 626696 | tf_op jit(solution)/shard_map/ppermute | solution.py:683
  86.5 2.6 %final.4 = (bf16[256,768]{1,0:T(8,128)(2,1)S(1)}, bf16[256,768]{1,0:T(8,128)(2,1)S(1)}) custom-call(s32[5]{0:T(128)S(1)} %stack.23.place, bf16[272,384]{1,0:T(8,128)(2,1)S(1)} %collective-permute-done.17.refs_0_, bf16[272,384]{1,0:T(8,128)(2,1)S(1)} %collective-permute-done.18.refs_0_.refs_1_, bf16[272,384]{1,0:T(8,128)(2,1)S(1)} %collective-permute-done.20.refs_3_.refs_2_, ...), custom_call_target="tpu_custom_call" | custom-call | flops 1 | bytes 1 | tf_op jit(solution)/shard_map/final/pallas_call | solution.py:658
  98.4 2.4 %collective-permute-start.28 = (bf16[256,384]{1,0:T(8,128)(2,1)S(1)}, bf16[256,384]{1,0:T(8,128)(2,1)S(1)}, u32[]{:S(2)}, u32[]{:S(2)}) collective-permute-start(bf16[256,384]{1,0:T(8,128)(2,1)S(1)} %get-tuple-element.114), channel_id=1, source_target_pairs={{0,4},{1,5},{2,6},{3,7},{4,0},{5,1},{6,2},{7,3},{8,12},{9,13},{10,... | collective-permute-start | bytes 589832 | tf_op jit(solution)/shard_map/ppermute | solution.py:683
  101.9 1.9 %place.1 = bf16[256,4096]{1,0:T(8,128)(2,1)} custom-call(s32[5]{0:T(128)S(1)} %stack.23.place, bf16[256,512]{1,0:T(8,128)(2,1)S(1)} %get-tuple-element.106.refs_6_.refs_0_, bf16[256,768]{1,0:T(8,128)(2,1)S(1)} %get-tuple-element.105.refs_2_.refs_1_, bf16[256,384]{1,0:T(8,128)(2,1)S(1)} %get-tuple-element.108.refs_6_.refs_2_, ...), custom_call_target="tpu_custom_call" | custom-call | flops 1 | bytes 1 | tf_op jit(solution)/shard_map/place/pallas_call | solution.py:620
  (73 shorter events, 24.6 us)
Async XLA Ops:
  2.5 2.1 %collective-permute-start = (bf16[64,2048]{1,0:T(8,128)(2,1)S(1)}, bf16[64,2048]{1,0:T(8,128)(2,1)S(1)}, u32[]{:S(2)}, u32[]{:S(2)}) collective-permute-start(bf16[64,2048]{1,0:T(8,128)(2,1)S(1)} %pack_first.1.order), channel_id=1, source_target_pairs={{0,4},{1,5},{2,6},{3,7},{4,0},{5,1},{6,2},{7,3},{8,12},{9,13},{10,... | collective-permute-start | bytes 786440 | tf_op jit(solution)/shard_map/ppermute | solution.py:683
  4.6 3.5 %collective-permute-start.4 = (bf16[64,8448]{1,0:T(8,128)(2,1)S(1)}, bf16[64,8448]{1,0:T(8,128)(2,1)S(1)}, u32[]{:S(2)}, u32[]{:S(2)}) collective-permute-start(bf16[64,8448]{1,0:T(8,128)(2,1)S(1)} %gate.3), channel_id=1, source_target_pairs={{0,4},{1,5},{2,6},{3,7},{4,0},{5,1},{6,2},{7,3},{8,12},{9,13},{10,... | collective-permute-start | bytes 3244040 | tf_op jit(solution)/shard_map/ppermute | solution.py:683
  5.7 12.4 %collective-permute-start.1 = (bf16[128,512]{1,0:T(8,128)(2,1)S(1)}, bf16[128,512]{1,0:T(8,128)(2,1)S(1)}, u32[]{:S(2)}, u32[]{:S(2)}) collective-permute-start(bf16[128,512]{1,0:T(8,128)(2,1)S(1)} %get-tuple-element.61), channel_id=1, source_target_pairs={{0,2},{1,3},{2,0},{3,1},{4,6},{5,7},{6,4},{7,5},{8,10},{9,11},{10,... | collective-permute-start | bytes 393224 | tf_op jit(solution)/shard_map/ppermute | solution.py:683
  8.7 6.0 %collective-permute-start.5 = (bf16[3,10240]{1,0:T(4,128)(2,1)S(1)}, bf16[3,10240]{1,0:T(4,128)(2,1)S(1)}, u32[]{:S(2)}, u32[]{:S(2)}) collective-permute-start(bf16[3,10240]{1,0:T(4,128)(2,1)S(1)} %edge.1), channel_id=1, source_target_pairs={{3,11},{7,15},{11,19},{15,23},{19,27},{23,31}} | collective-permute-start | bytes 184328 | tf_op jit(solution)/shard_map/ppermute | solution.py:683
  9.4 11.6 %collective-permute-start.2 = (bf16[128,512]{1,0:T(8,128)(2,1)S(1)}, bf16[128,512]{1,0:T(8,128)(2,1)S(1)}, u32[]{:S(2)}, u32[]{:S(2)}) collective-permute-start(bf16[128,512]{1,0:T(8,128)(2,1)S(1)} %get-tuple-element.62), channel_id=1, source_target_pairs={{0,3},{1,2},{2,1},{3,0},{4,7},{5,6},{6,5},{7,4},{8,11},{9,10},{10,... | collective-permute-start | bytes 393224 | tf_op jit(solution)/shard_map/ppermute | solution.py:683
  10.0 11.0 %collective-permute-start.3 = (bf16[128,512]{1,0:T(8,128)(2,1)S(1)}, bf16[128,512]{1,0:T(8,128)(2,1)S(1)}, u32[]{:S(2)}, u32[]{:S(2)}) collective-permute-start(bf16[128,512]{1,0:T(8,128)(2,1)S(1)} %get-tuple-element.63), channel_id=1, source_target_pairs={{0,1},{1,0},{2,3},{3,2},{4,5},{5,4},{6,7},{7,6},{8,9},{9,8},{10,11... | collective-permute-start | bytes 393224 | tf_op jit(solution)/shard_map/ppermute | solution.py:683
  15.7 9.8 %collective-permute-start.6 = (bf16[128,384]{1,0:T(8,128)(2,1)S(1)}, bf16[128,384]{1,0:T(8,128)(2,1)S(1)}, u32[]{:S(2)}, u32[]{:S(2)}) collective-permute-start(bf16[128,384]{1,0:T(8,128)(2,1)S(1)} %get-tuple-element.69), channel_id=1, source_target_pairs={{0,2},{1,3},{2,0},{3,1},{4,6},{5,7},{6,4},{7,5},{8,10},{9,11},{10,... | collective-permute-start | bytes 294920 | tf_op jit(solution)/shard_map/ppermute | solution.py:683
  18.1 9.9 %collective-permute-start.7 = (bf16[128,384]{1,0:T(8,128)(2,1)S(1)}, bf16[128,384]{1,0:T(8,128)(2,1)S(1)}, u32[]{:S(2)}, u32[]{:S(2)}) collective-permute-start(bf16[128,384]{1,0:T(8,128)(2,1)S(1)} %get-tuple-element.70), channel_id=1, source_target_pairs={{0,3},{1,2},{2,1},{3,0},{4,7},{5,6},{6,5},{7,4},{8,11},{9,10},{10,... | collective-permute-start | bytes 294920 | tf_op jit(solution)/shard_map/ppermute | solution.py:683
  18.1 9.8 %collective-permute-start.8 = (bf16[128,384]{1,0:T(8,128)(2,1)S(1)}, bf16[128,384]{1,0:T(8,128)(2,1)S(1)}, u32[]{:S(2)}, u32[]{:S(2)}) collective-permute-start(bf16[128,384]{1,0:T(8,128)(2,1)S(1)} %get-tuple-element.71), channel_id=1, source_target_pairs={{0,1},{1,0},{2,3},{3,2},{4,5},{5,4},{6,7},{7,6},{8,9},{9,8},{10,11... | collective-permute-start | bytes 294920 | tf_op jit(solution)/shard_map/ppermute | solution.py:683
  20.9 10.4 %copy-start.5 = (f32[256]{0:T(256)S(1)}, f32[256]{0:T(256)}, u32[]{:S(2)}) copy-start(f32[256]{0:T(256)} %param.11) | copy-start | bytes 3076
  20.9 10.4 %copy-start.6 = (f32[256]{0:T(256)S(1)}, f32[256]{0:T(256)}, u32[]{:S(2)}) copy-start(f32[256]{0:T(256)} %param.12) | copy-start | bytes 3076
  20.9 10.4 %copy-start.7 = (f32[256]{0:T(256)S(1)}, f32[256]{0:T(256)}, u32[]{:S(2)}) copy-start(f32[256]{0:T(256)} %param.13) | copy-start | bytes 3076
  27.9 17.6 %collective-permute-start.14 = (bf16[128,1792]{1,0:T(8,128)(2,1)S(1)}, bf16[128,1792]{1,0:T(8,128)(2,1)S(1)}, u32[]{:S(2)}, u32[]{:S(2)}) collective-permute-start(bf16[128,1792]{1,0:T(8,128)(2,1)S(1)} %get-tuple-element.88), channel_id=1, source_target_pairs={{0,1},{1,0},{2,3},{3,2},{4,5},{5,4},{6,7},{7,6},{8,9},{9,8},{10,11... | collective-permute-start | bytes 1376264 | tf_op jit(solution)/shard_map/ppermute | solution.py:683
  27.9 17.6 %collective-permute-start.12 = (bf16[128,768]{1,0:T(8,128)(2,1)S(1)}, bf16[128,768]{1,0:T(8,128)(2,1)S(1)}, u32[]{:S(2)}, u32[]{:S(2)}) collective-permute-start(bf16[128,768]{1,0:T(8,128)(2,1)S(1)} %get-tuple-element.86), channel_id=1, source_target_pairs={{0,2},{1,3},{2,0},{3,1},{4,6},{5,7},{6,4},{7,5},{8,10},{9,11},{10,... | collective-permute-start | bytes 589832 | tf_op jit(solution)/shard_map/ppermute | solution.py:683
  31.3 14.2 %collective-permute-start.13 = (bf16[128,768]{1,0:T(8,128)(2,1)S(1)}, bf16[128,768]{1,0:T(8,128)(2,1)S(1)}, u32[]{:S(2)}, u32[]{:S(2)}) collective-permute-start(bf16[128,768]{1,0:T(8,128)(2,1)S(1)} %get-tuple-element.87), channel_id=1, source_target_pairs={{0,3},{1,2},{2,1},{3,0},{4,7},{5,6},{6,5},{7,4},{8,11},{9,10},{10,... | collective-permute-start | bytes 589832 | tf_op jit(solution)/shard_map/ppermute | solution.py:683
  35.1 5.5 %collective-permute-start.9 = (bf16[272,256]{1,0:T(8,128)(2,1)S(1)}, bf16[272,256]{1,0:T(8,128)(2,1)S(1)}, u32[]{:S(2)}, u32[]{:S(2)}) collective-permute-start(bf16[272,256]{1,0:T(8,128)(2,1)S(1)} %get-tuple-element.77.refs_0_.refs_2_), channel_id=1, source_target_pairs={{0,8},{1,9},{2,10},{3,11},{4,12},{5,13},{6,14},{7,15},{8,0},{9,1},... | collective-permute-start | bytes 417800 | tf_op jit(solution)/shard_map/ppermute | solution.py:683
  38.4 4.9 %collective-permute-start.10 = (bf16[272,256]{1,0:T(8,128)(2,1)S(1)}, bf16[272,256]{1,0:T(8,128)(2,1)S(1)}, u32[]{:S(2)}, u32[]{:S(2)}) collective-permute-start(bf16[272,256]{1,0:T(8,128)(2,1)S(1)} %get-tuple-element.78.refs_1_.refs_3_), channel_id=1, source_target_pairs={{0,8},{1,9},{2,10},{3,11},{4,12},{5,13},{6,14},{7,15},{8,0},{9,1},... | collective-permute-start | bytes 417800 | tf_op jit(solution)/shard_map/ppermute | solution.py:683
  44.0 23.2 %collective-permute-start.11 = (bf16[272,512]{1,0:T(8,128)(2,1)S(1)}, bf16[272,512]{1,0:T(8,128)(2,1)S(1)}, u32[]{:S(2)}, u32[]{:S(2)}) collective-permute-start(bf16[272,512]{1,0:T(8,128)(2,1)S(1)} %combine.5.refs_10_), channel_id=1, source_target_pairs={{0,16},{1,17},{2,18},{3,19},{4,20},{5,21},{6,22},{7,23},{8,24},{9,... | collective-permute-start | bytes 835592 | tf_op jit(solution)/shard_map/ppermute | solution.py:683
  45.6 21.6 %collective-permute-start.15 = (bf16[128,1024]{1,0:T(8,128)(2,1)S(1)}, bf16[128,1024]{1,0:T(8,128)(2,1)S(1)}, u32[]{:S(2)}, u32[]{:S(2)}) collective-permute-start(bf16[128,1024]{1,0:T(8,128)(2,1)S(1)} %get-tuple-element.89), channel_id=1, source_target_pairs={{0,2},{1,3},{2,0},{3,1},{4,6},{5,7},{6,4},{7,5},{8,10},{9,11},{10,... | collective-permute-start | bytes 786440 | tf_op jit(solution)/shard_map/ppermute | solution.py:683
  50.0 23.6 %collective-permute-start.16 = (bf16[128,1024]{1,0:T(8,128)(2,1)S(1)}, bf16[128,1024]{1,0:T(8,128)(2,1)S(1)}, u32[]{:S(2)}, u32[]{:S(2)}) collective-permute-start(bf16[128,1024]{1,0:T(8,128)(2,1)S(1)} %get-tuple-element.90), channel_id=1, source_target_pairs={{0,3},{1,2},{2,1},{3,0},{4,7},{5,6},{6,5},{7,4},{8,11},{9,10},{10,... | collective-permute-start | bytes 786440 | tf_op jit(solution)/shard_map/ppermute | solution.py:683
  54.7 6.2 %collective-permute-start.17 = (bf16[272,384]{1,0:T(8,128)(2,1)S(1)}, bf16[272,384]{1,0:T(8,128)(2,1)S(1)}, u32[]{:S(2)}, u32[]{:S(2)}) collective-permute-start(bf16[272,384]{1,0:T(8,128)(2,1)S(1)} %get-tuple-element.91.refs_1_), channel_id=1, source_target_pairs={{0,8},{1,9},{2,10},{3,11},{4,12},{5,13},{6,14},{7,15},{8,0},{9,1},... | collective-permute-start | bytes 626696 | tf_op jit(solution)/shard_map/ppermute | solution.py:683
  58.2 7.0 %collective-permute-start.18 = (bf16[272,384]{1,0:T(8,128)(2,1)S(1)}, bf16[272,384]{1,0:T(8,128)(2,1)S(1)}, u32[]{:S(2)}, u32[]{:S(2)}) collective-permute-start(bf16[272,384]{1,0:T(8,128)(2,1)S(1)} %get-tuple-element.92.refs_1_), channel_id=1, source_target_pairs={{0,8},{1,9},{2,10},{3,11},{4,12},{5,13},{6,14},{7,15},{8,0},{9,1},... | collective-permute-start | bytes 626696 | tf_op jit(solution)/shard_map/ppermute | solution.py:683
  61.6 23.0 %collective-permute-start.20 = (bf16[272,384]{1,0:T(8,128)(2,1)S(1)}, bf16[272,384]{1,0:T(8,128)(2,1)S(1)}, u32[]{:S(2)}, u32[]{:S(2)}) collective-permute-start(bf16[272,384]{1,0:T(8,128)(2,1)S(1)} %combine.6.refs_2_.refs_10_), channel_id=1, source_target_pairs={{0,16},{1,17},{2,18},{3,19},{4,20},{5,21},{6,22},{7,23},{8,24},{9,... | collective-permute-start | bytes 626696 | tf_op jit(solution)/shard_map/ppermute | solution.py:683
  65.9 18.7 %collective-permute-start.21 = (bf16[272,384]{1,0:T(8,128)(2,1)S(1)}, bf16[272,384]{1,0:T(8,128)(2,1)S(1)}, u32[]{:S(2)}, u32[]{:S(2)}) collective-permute-start(bf16[272,384]{1,0:T(8,128)(2,1)S(1)} %combine.7.refs_11_), channel_id=1, source_target_pairs={{0,16},{1,17},{2,18},{3,19},{4,20},{5,21},{6,22},{7,23},{8,24},{9,... | collective-permute-start | bytes 626696 | tf_op jit(solution)/shard_map/ppermute | solution.py:683
  75.5 9.1 %collective-permute-start.22 = (bf16[272,384]{1,0:T(8,128)(2,1)S(1)}, bf16[272,384]{1,0:T(8,128)(2,1)S(1)}, u32[]{:S(2)}, u32[]{:S(2)}) collective-permute-start(bf16[272,384]{1,0:T(8,128)(2,1)S(1)} %get-tuple-element.93.refs_8_.refs_1_), channel_id=1, source_target_pairs={{0,8},{1,9},{2,10},{3,11},{4,12},{5,13},{6,14},{7,15},{8,0},{9,1},... | collective-permute-start | bytes 626696 | tf_op jit(solution)/shard_map/ppermute | solution.py:683
  83.2 5.9 %collective-permute-start.19 = (bf16[272,384]{1,0:T(8,128)(2,1)S(1)}, bf16[272,384]{1,0:T(8,128)(2,1)S(1)}, u32[]{:S(2)}, u32[]{:S(2)}) collective-permute-start(bf16[272,384]{1,0:T(8,128)(2,1)S(1)} %get-tuple-element.102.refs_2_.refs_1_), channel_id=1, source_target_pairs={{0,8},{1,9},{2,10},{3,11},{4,12},{5,13},{6,14},{7,15},{8,0},{9,1},... | collective-permute-start | bytes 626696 | tf_op jit(solution)/shard_map/ppermute | solution.py:683
  85.2 9.5 %collective-permute-start.23 = (bf16[272,384]{1,0:T(8,128)(2,1)S(1)}, bf16[272,384]{1,0:T(8,128)(2,1)S(1)}, u32[]{:S(2)}, u32[]{:S(2)}) collective-permute-start(bf16[272,384]{1,0:T(8,128)(2,1)S(1)} %combine.8.refs_12_), channel_id=1, source_target_pairs={{0,16},{1,17},{2,18},{3,19},{4,20},{5,21},{6,22},{7,23},{8,24},{9,... | collective-permute-start | bytes 626696 | tf_op jit(solution)/shard_map/ppermute | solution.py:683
  89.8 7.6 %collective-permute-start.24 = (bf16[272,384]{1,0:T(8,128)(2,1)S(1)}, bf16[272,384]{1,0:T(8,128)(2,1)S(1)}, u32[]{:S(2)}, u32[]{:S(2)}) collective-permute-start(bf16[272,384]{1,0:T(8,128)(2,1)S(1)} %combine.9.refs_0_), channel_id=1, source_target_pairs={{0,16},{1,17},{2,18},{3,19},{4,20},{5,21},{6,22},{7,23},{8,24},{9,... | collective-permute-start | bytes 626696 | tf_op jit(solution)/shard_map/ppermute | solution.py:683
  91.1 9.7 %collective-permute-start.26 = (bf16[256,768]{1,0:T(8,128)(2,1)S(1)}, bf16[256,768]{1,0:T(8,128)(2,1)S(1)}, u32[]{:S(2)}, u32[]{:S(2)}) collective-permute-start(bf16[256,768]{1,0:T(8,128)(2,1)S(1)} %get-tuple-element.112), channel_id=1, source_target_pairs={{0,4},{1,5},{2,6},{3,7},{4,0},{5,1},{6,2},{7,3},{8,12},{9,13},{10,... | collective-permute-start | bytes 1179656 | tf_op jit(solution)/shard_map/ppermute | solution.py:683
  94.6 6.2 %collective-permute-start.25 = (bf16[256,512]{1,0:T(8,128)(2,1)S(1)}, bf16[256,512]{1,0:T(8,128)(2,1)S(1)}, u32[]{:S(2)}, u32[]{:S(2)}) collective-permute-start(bf16[256,512]{1,0:T(8,128)(2,1)S(1)} %get-tuple-element.111), channel_id=1, source_target_pairs={{0,4},{1,5},{2,6},{3,7},{4,0},{5,1},{6,2},{7,3},{8,12},{9,13},{10,... | collective-permute-start | bytes 786440 | tf_op jit(solution)/shard_map/ppermute | solution.py:683
  95.8 5.0 %collective-permute-start.27 = (bf16[256,384]{1,0:T(8,128)(2,1)S(1)}, bf16[256,384]{1,0:T(8,128)(2,1)S(1)}, u32[]{:S(2)}, u32[]{:S(2)}) collective-permute-start(bf16[256,384]{1,0:T(8,128)(2,1)S(1)} %get-tuple-element.113), channel_id=1, source_target_pairs={{0,4},{1,5},{2,6},{3,7},{4,0},{5,1},{6,2},{7,3},{8,12},{9,13},{10,... | collective-permute-start | bytes 589832 | tf_op jit(solution)/shard_map/ppermute | solution.py:683
  98.4 3.4 %collective-permute-start.28 = (bf16[256,384]{1,0:T(8,128)(2,1)S(1)}, bf16[256,384]{1,0:T(8,128)(2,1)S(1)}, u32[]{:S(2)}, u32[]{:S(2)}) collective-permute-start(bf16[256,384]{1,0:T(8,128)(2,1)S(1)} %get-tuple-element.114), channel_id=1, source_target_pairs={{0,4},{1,5},{2,6},{3,7},{4,0},{5,1},{6,2},{7,3},{8,12},{9,13},{10,... | collective-permute-start | bytes 589832 | tf_op jit(solution)/shard_map/ppermute | solution.py:683
  (5 other events, 14.3 us)

commit v21 on v20

--- a/solution.py
+++ b/solution.py
@@ -837,7 +837,7 @@
     combine_of(0, [own_block])
     state_of(1, joined[0])
     combine_of(1, [])
-    state_of(2, joined[1] + before[0])
+    state_of(2, joined[1])
     c, score = call(
         functools.partial(score_kernel, shards),
         [((slab, STATE), BF16), ((slab, BLOCK), F32)],
@@ -852,7 +852,7 @@
         wide = [pltpu.VMEM((slab, GROUPED[i][2]), F32)]
         finish_of(finish_kernel, i, [x[i], cum, row, score, skip], order, scratch=wide)
 
-    combine_of(2, sent[3] + before[1])
+    combine_of(2, sent[3] + before[1] + before[0])
     in_full(1, joined[2])
     combine_of(3, [keep[1]])
     local_of(2, joined[3])

time: 105 us -> 105 us (level)
  transfers between devices with their start and end apart: 29 -> 29, of which waited for: 9 -> 8; matrix products, arithmetic and copies ran while one was open for 0% -> 0% of each run, Pallas kernels for 28% -> 28%
where the time goes in v21:
time: 105 us; the launch traced here: 104 us
  starting transfers between devices  47.4 us (45%)
  Pallas kernels  31.6 us (30%)
  waiting for transfers between devices  21.9 us (21%)
  local copies, waits for them, and re-layouts  2.06 us (2%)
    ppermute x29, starting transfers between devices, over(): lax.ppermute(block, axes, [(i, j) for i, j in route if j is not None and...  47.4 us
    pallas_call x26, Pallas kernels, call(): pl.pallas_call(body, out_shape=shapes, in_specs=specs, out_specs=[vmem] *...  29.7 us
    ppermute x29, waiting for transfers between devices, over(): lax.ppermute(block, axes, [(i, j) for i, j in route if j is not None and...  21.9 us
  transfers between devices with their start and end apart: 29, of which 8 were waited for; matrix products, arithmetic and copies ran while one was open for 0% of the time, Pallas kernels for 28%

profile of v21, /device:TPU:13, one launch (start us, length us, event | category | flops | bytes accessed | tf_op | source)
XLA Modules:
  0.0 103.6 jit_solution(167163918489957749)
XLA Ops:
  0.1 1.7 %copy-done = bf16[64,20480]{1,0:T(8,128)(2,1)S(1)} copy-done((bf16[64,20480]{1,0:T(8,128)(2,1)S(1)}, bf16[64,20480]{1,0:T(8,128)(2,1)}, u32[]{:S(2)}) %copy-start) | copy-done | bytes 2621464
  3.2 1.3 %pack.1 = (bf16[64,8448]{1,0:T(8,128)(2,1)S(1)}, bf16[16,10240]{1,0:T(8,128)(2,1)S(1)}) custom-call(s32[5]{0:T(128)S(1)} %stack.23.place, bf16[64,20480]{1,0:T(8,128)(2,1)S(1)} %copy-done, bf16[64,256]{1,0:T(8,128)(2,1)S(1)} %copy-done.2, bf16[64,2048]{1,0:T(8,128)(2,1)S(1)} %pack_first.1.order), custom_call_target="tpu_custom_call" | custom-call | flops 1 | bytes 1 | tf_op jit(solution)/shard_map/pack/pallas_call | solution.py:658
  5.7 2.4 %collective-permute-start.1 = (bf16[128,512]{1,0:T(8,128)(2,1)S(1)}, bf16[128,512]{1,0:T(8,128)(2,1)S(1)}, u32[]{:S(2)}, u32[]{:S(2)}) collective-permute-start(bf16[128,512]{1,0:T(8,128)(2,1)S(1)} %get-tuple-element.61), channel_id=1, source_target_pairs={{0,2},{1,3},{2,0},{3,1},{4,6},{5,7},{6,4},{7,5},{8,10},{9,11},{10,... | collective-permute-start | bytes 393224 | tf_op jit(solution)/shard_map/ppermute | solution.py:683
  10.0 4.6 %collective-permute-start.3 = (bf16[128,512]{1,0:T(8,128)(2,1)S(1)}, bf16[128,512]{1,0:T(8,128)(2,1)S(1)}, u32[]{:S(2)}, u32[]{:S(2)}) collective-permute-start(bf16[128,512]{1,0:T(8,128)(2,1)S(1)} %get-tuple-element.63), channel_id=1, source_target_pairs={{0,1},{1,0},{2,3},{3,2},{4,5},{5,4},{6,7},{7,6},{8,9},{9,8},{10,11... | collective-permute-start | bytes 393224 | tf_op jit(solution)/shard_map/ppermute | solution.py:683
  15.7 2.4 %collective-permute-start.6 = (bf16[128,384]{1,0:T(8,128)(2,1)S(1)}, bf16[128,384]{1,0:T(8,128)(2,1)S(1)}, u32[]{:S(2)}, u32[]{:S(2)}) collective-permute-start(bf16[128,384]{1,0:T(8,128)(2,1)S(1)} %get-tuple-element.69), channel_id=1, source_target_pairs={{0,2},{1,3},{2,0},{3,1},{4,6},{5,7},{6,4},{7,5},{8,10},{9,11},{10,... | collective-permute-start | bytes 294920 | tf_op jit(solution)/shard_map/ppermute | solution.py:683
  21.0 4.5 %collective-permute-done.6.refs_1_.refs_6_ = bf16[128,384]{1,0:T(8,128)(2,1)S(1)} collective-permute-done((bf16[128,384]{1,0:T(8,128)(2,1)S(1)}, bf16[128,384]{1,0:T(8,128)(2,1)S(1)}, u32[]{:S(2)}, u32[]{:S(2)}) %collective-permute-start.6) | collective-permute-done | bytes 98336 | tf_op jit(solution)/shard_map/ppermute | solution.py:683
  25.5 2.5 %collective-permute-done.7.refs_2_.refs_7_ = bf16[128,384]{1,0:T(8,128)(2,1)S(1)} collective-permute-done((bf16[128,384]{1,0:T(8,128)(2,1)S(1)}, bf16[128,384]{1,0:T(8,128)(2,1)S(1)}, u32[]{:S(2)}, u32[]{:S(2)}) %collective-permute-start.7) | collective-permute-done | bytes 98336 | tf_op jit(solution)/shard_map/ppermute | solution.py:683
  27.9 3.4 %collective-permute-start.12 = (bf16[128,768]{1,0:T(8,128)(2,1)S(1)}, bf16[128,768]{1,0:T(8,128)(2,1)S(1)}, u32[]{:S(2)}, u32[]{:S(2)}) collective-permute-start(bf16[128,768]{1,0:T(8,128)(2,1)S(1)} %get-tuple-element.86), channel_id=1, source_target_pairs={{0,2},{1,3},{2,0},{3,1},{4,6},{5,7},{6,4},{7,5},{8,10},{9,11},{10,... | collective-permute-start | bytes 589832 | tf_op jit(solution)/shard_map/ppermute | solution.py:683
  31.3 1.7 %prep.1 = (bf16[512,256]{1,0:T(8,128)(2,1)S(1)}, f32[4,2560]{1,0:T(4,128)S(1)}, f32[512,128]{1,0:T(8,128)S(1)}, f32[128,512]{1,0:T(8,128)S(1)}, bf16[512,256]{1,...) custom-call(s32[5]{0:T(128)S(1)} %stack.23.place, ...), custom_call_target="tpu_custom_call" | custom-call | flops 1 | bytes 1 | tf_op jit(solution)/shard_map/prep/pallas_call | solution.py:658
  33.0 2.1 %state.4 = (bf16[512,512]{1,0:T(8,128)(2,1)S(1)}, f32[256,512]{1,0:T(8,128)S(1)}, bf16[272,256]{1,0:T(8,128)(2,1)S(1)}, bf16[272,256]{1,0:T(8,128)(2,1)S(1)}) custom-call(s32[5]{0:T(128)S(1)} %stack.23.place, bf16[128,512]{1,0:T(8,128)(2,1)S(1)} %get-tuple-element.60.refs_0_, bf16[128,512]{1,0:T(8,128)(2,1)S(1)} %collective-permute-done.1.refs_1_.refs_3_, ...), custom_call_target="tpu_custom_call" | custom-call | flops 1 | bytes 1 | tf_op jit(solution)/shard_map/state/pallas_call | solution.py:658
  35.1 3.3 %collective-permute-start.9 = (bf16[272,256]{1,0:T(8,128)(2,1)S(1)}, bf16[272,256]{1,0:T(8,128)(2,1)S(1)}, u32[]{:S(2)}, u32[]{:S(2)}) collective-permute-start(bf16[272,256]{1,0:T(8,128)(2,1)S(1)} %get-tuple-element.77.refs_0_.refs_2_), channel_id=1, source_target_pairs={{0,8},{1,9},{2,10},{3,11},{4,12},{5,13},{6,14},{7,15},{8,0},{9,1},... | collective-permute-start | bytes 417800 | tf_op jit(solution)/shard_map/ppermute | solution.py:683
  38.4 1.3 %collective-permute-start.10 = (bf16[272,256]{1,0:T(8,128)(2,1)S(1)}, bf16[272,256]{1,0:T(8,128)(2,1)S(1)}, u32[]{:S(2)}, u32[]{:S(2)}) collective-permute-start(bf16[272,256]{1,0:T(8,128)(2,1)S(1)} %get-tuple-element.78.refs_1_.refs_3_), channel_id=1, source_target_pairs={{0,8},{1,9},{2,10},{3,11},{4,12},{5,13},{6,14},{7,15},{8,0},{9,1},... | collective-permute-start | bytes 417800 | tf_op jit(solution)/shard_map/ppermute | solution.py:683
  40.6 5.0 %collective-permute-done.12.refs_2_.refs_1_ = bf16[128,768]{1,0:T(8,128)(2,1)S(1)} collective-permute-done((bf16[128,768]{1,0:T(8,128)(2,1)S(1)}, bf16[128,768]{1,0:T(8,128)(2,1)S(1)}, u32[]{:S(2)}, u32[]{:S(2)}) %collective-permute-start.12) | collective-permute-done | bytes 196640 | tf_op jit(solution)/shard_map/ppermute | solution.py:683
  45.6 4.4 %collective-permute-start.15 = (bf16[128,1024]{1,0:T(8,128)(2,1)S(1)}, bf16[128,1024]{1,0:T(8,128)(2,1)S(1)}, u32[]{:S(2)}, u32[]{:S(2)}) collective-permute-start(bf16[128,1024]{1,0:T(8,128)(2,1)S(1)} %get-tuple-element.89), channel_id=1, source_target_pairs={{0,2},{1,3},{2,0},{3,1},{4,6},{5,7},{6,4},{7,5},{8,10},{9,11},{10,... | collective-permute-start | bytes 786440 | tf_op jit(solution)/shard_map/ppermute | solution.py:683
  50.0 2.2 %collective-permute-start.16 = (bf16[128,1024]{1,0:T(8,128)(2,1)S(1)}, bf16[128,1024]{1,0:T(8,128)(2,1)S(1)}, u32[]{:S(2)}, u32[]{:S(2)}) collective-permute-start(bf16[128,1024]{1,0:T(8,128)(2,1)S(1)} %get-tuple-element.90), channel_id=1, source_target_pairs={{0,3},{1,2},{2,1},{3,0},{4,7},{5,6},{6,5},{7,4},{8,11},{9,10},{10,... | collective-permute-start | bytes 786440 | tf_op jit(solution)/shard_map/ppermute | solution.py:683
  52.8 2.6 %state.5 = (bf16[512,768]{1,0:T(8,128)(2,1)S(1)}, f32[256,768]{1,0:T(8,128)S(1)}, bf16[272,384]{1,0:T(8,128)(2,1)S(1)}, bf16[272,384]{1,0:T(8,128)(2,1)S(1)}) custom-call(s32[5]{0:T(128)S(1)} %stack.23.place, bf16[128,768]{1,0:T(8,128)(2,1)S(1)} %get-tuple-element.72.refs_9_.refs_0_, bf16[128,768]{1,0:T(8,128)(2,1)S(1)} %collective-permute-done.12.refs_2_.refs_1_, ...), custom_call_target="tpu_custom_call" | custom-call | flops 1 | bytes 1 | tf_op jit(solution)/shard_map/state/pallas_call | solution.py:658
  55.4 3.5 %collective-permute-start.17 = (bf16[272,384]{1,0:T(8,128)(2,1)S(1)}, bf16[272,384]{1,0:T(8,128)(2,1)S(1)}, u32[]{:S(2)}, u32[]{:S(2)}) collective-permute-start(bf16[272,384]{1,0:T(8,128)(2,1)S(1)} %get-tuple-element.91.refs_1_), channel_id=1, source_target_pairs={{0,8},{1,9},{2,10},{3,11},{4,12},{5,13},{6,14},{7,15},{8,0},{9,1},... | collective-permute-start | bytes 626696 | tf_op jit(solution)/shard_map/ppermute | solution.py:683
  58.9 1.3 %collective-permute-start.18 = (bf16[272,384]{1,0:T(8,128)(2,1)S(1)}, bf16[272,384]{1,0:T(8,128)(2,1)S(1)}, u32[]{:S(2)}, u32[]{:S(2)}) collective-permute-start(bf16[272,384]{1,0:T(8,128)(2,1)S(1)} %get-tuple-element.92.refs_1_), channel_id=1, source_target_pairs={{0,8},{1,9},{2,10},{3,11},{4,12},{5,13},{6,14},{7,15},{8,0},{9,1},... | collective-permute-start | bytes 626696 | tf_op jit(solution)/shard_map/ppermute | solution.py:683
  60.2 1.3 %collective-permute-start.11 = (bf16[272,512]{1,0:T(8,128)(2,1)S(1)}, bf16[272,512]{1,0:T(8,128)(2,1)S(1)}, u32[]{:S(2)}, u32[]{:S(2)}) collective-permute-start(bf16[272,512]{1,0:T(8,128)(2,1)S(1)} %combine.5.refs_10_), channel_id=1, source_target_pairs={{0,16},{1,17},{2,18},{3,19},{4,20},{5,21},{6,22},{7,23},{8,24},{9,... | collective-permute-start | bytes 835592 | tf_op jit(solution)/shard_map/ppermute | solution.py:683
  62.3 1.3 %collective-permute-start.20 = (bf16[272,384]{1,0:T(8,128)(2,1)S(1)}, bf16[272,384]{1,0:T(8,128)(2,1)S(1)}, u32[]{:S(2)}, u32[]{:S(2)}) collective-permute-start(bf16[272,384]{1,0:T(8,128)(2,1)S(1)} %combine.6.refs_2_.refs_10_), channel_id=1, source_target_pairs={{0,16},{1,17},{2,18},{3,19},{4,20},{5,21},{6,22},{7,23},{8,24},{9,... | collective-permute-start | bytes 626696 | tf_op jit(solution)/shard_map/ppermute | solution.py:683
  63.6 2.4 %collective-permute-done.18.refs_0_.refs_1_ = bf16[272,384]{1,0:T(8,128)(2,1)S(1)} collective-permute-done((bf16[272,384]{1,0:T(8,128)(2,1)S(1)}, bf16[272,384]{1,0:T(8,128)(2,1)S(1)}, u32[]{:S(2)}, u32[]{:S(2)}) %collective-permute-start.18) | collective-permute-done | bytes 208928 | tf_op jit(solution)/shard_map/ppermute | solution.py:683
  66.6 1.3 %collective-permute-start.21 = (bf16[272,384]{1,0:T(8,128)(2,1)S(1)}, bf16[272,384]{1,0:T(8,128)(2,1)S(1)}, u32[]{:S(2)}, u32[]{:S(2)}) collective-permute-start(bf16[272,384]{1,0:T(8,128)(2,1)S(1)} %combine.7.refs_11_), channel_id=1, source_target_pairs={{0,16},{1,17},{2,18},{3,19},{4,20},{5,21},{6,22},{7,23},{8,24},{9,... | collective-permute-start | bytes 626696 | tf_op jit(solution)/shard_map/ppermute | solution.py:683
  67.9 5.7 %collective-permute-done.16.refs_2_ = bf16[128,1024]{1,0:T(8,128)(2,1)S(1)} collective-permute-done((bf16[128,1024]{1,0:T(8,128)(2,1)S(1)}, bf16[128,1024]{1,0:T(8,128)(2,1)S(1)}, u32[]{:S(2)}, u32[]{:S(2)}) %collective-permute-start.16) | collective-permute-done | bytes 262176 | tf_op jit(solution)/shard_map/ppermute | solution.py:683
  73.6 1.9 %state.6 = (bf16[512,384]{1,0:T(8,128)(2,1)S(1)}, f32[256,384]{1,0:T(8,128)S(1)}, bf16[272,384]{1,0:T(8,128)(2,1)S(1)}) custom-call(s32[5]{0:T(128)S(1)} %stack.23.place, bf16[128,1024]{1,0:T(8,128)(2,1)S(1)} %get-tuple-element.79.refs_4_.refs_0_, bf16[128,1024]{1,0:T(8,128)(2,1)S(1)} %collective-permute-done.15.refs_1_, ...), custom_call_target="tpu_custom_call" | custom-call | flops 1 | bytes 1 | tf_op jit(solution)/shard_map/state/pallas_call | solution.py:658
  75.5 3.6 %collective-permute-start.22 = (bf16[272,384]{1,0:T(8,128)(2,1)S(1)}, bf16[272,384]{1,0:T(8,128)(2,1)S(1)}, u32[]{:S(2)}, u32[]{:S(2)}) collective-permute-start(bf16[272,384]{1,0:T(8,128)(2,1)S(1)} %get-tuple-element.93.refs_8_.refs_1_), channel_id=1, source_target_pairs={{0,8},{1,9},{2,10},{3,11},{4,12},{5,13},{6,14},{7,15},{8,0},{9,1},... | collective-permute-start | bytes 626696 | tf_op jit(solution)/shard_map/ppermute | solution.py:683
  81.3 1.9 %state.7 = (bf16[512,384]{1,0:T(8,128)(2,1)S(1)}, f32[256,384]{1,0:T(8,128)S(1)}, bf16[272,384]{1,0:T(8,128)(2,1)S(1)}) custom-call(s32[5]{0:T(128)S(1)} %stack.23.place, bf16[128,1024]{1,0:T(8,128)(2,1)S(1)} %get-tuple-element.79.refs_4_.refs_0_, bf16[128,1024]{1,0:T(8,128)(2,1)S(1)} %collective-permute-done.15.refs_1_, ...), custom_call_target="tpu_custom_call" | custom-call | flops 1 | bytes 1 | tf_op jit(solution)/shard_map/state/pallas_call | solution.py:658
  83.2 1.3 %collective-permute-start.19 = (bf16[272,384]{1,0:T(8,128)(2,1)S(1)}, bf16[272,384]{1,0:T(8,128)(2,1)S(1)}, u32[]{:S(2)}, u32[]{:S(2)}) collective-permute-start(bf16[272,384]{1,0:T(8,128)(2,1)S(1)} %get-tuple-element.102.refs_2_.refs_1_), channel_id=1, source_target_pairs={{0,8},{1,9},{2,10},{3,11},{4,12},{5,13},{6,14},{7,15},{8,0},{9,1},... | collective-permute-start | bytes 626696 | tf_op jit(solution)/shard_map/ppermute | solution.py:683
  85.2 1.3 %collective-permute-start.23 = (bf16[272,384]{1,0:T(8,128)(2,1)S(1)}, bf16[272,384]{1,0:T(8,128)(2,1)S(1)}, u32[]{:S(2)}, u32[]{:S(2)}) collective-permute-start(bf16[272,384]{1,0:T(8,128)(2,1)S(1)} %combine.8.refs_12_), channel_id=1, source_target_pairs={{0,16},{1,17},{2,18},{3,19},{4,20},{5,21},{6,22},{7,23},{8,24},{9,... | collective-permute-start | bytes 626696 | tf_op jit(solution)/shard_map/ppermute | solution.py:683
  86.5 2.6 %final.4 = (bf16[256,768]{1,0:T(8,128)(2,1)S(1)}, bf16[256,768]{1,0:T(8,128)(2,1)S(1)}) custom-call(s32[5]{0:T(128)S(1)} %stack.23.place, bf16[272,384]{1,0:T(8,128)(2,1)S(1)} %collective-permute-done.17.refs_0_, bf16[272,384]{1,0:T(8,128)(2,1)S(1)} %collective-permute-done.18.refs_0_.refs_1_, bf16[272,384]{1,0:T(8,128)(2,1)S(1)} %collective-permute-done.20.refs_3_.refs_2_, ...), custom_call_target="tpu_custom_call" | custom-call | flops 1 | bytes 1 | tf_op jit(solution)/shard_map/final/pallas_call | solution.py:658
  89.8 1.3 %collective-permute-start.24 = (bf16[272,384]{1,0:T(8,128)(2,1)S(1)}, bf16[272,384]{1,0:T(8,128)(2,1)S(1)}, u32[]{:S(2)}, u32[]{:S(2)}) collective-permute-start(bf16[272,384]{1,0:T(8,128)(2,1)S(1)} %combine.9.refs_0_), channel_id=1, source_target_pairs={{0,16},{1,17},{2,18},{3,19},{4,20},{5,21},{6,22},{7,23},{8,24},{9,... | collective-permute-start | bytes 626696 | tf_op jit(solution)/shard_map/ppermute | solution.py:683
  98.1 2.3 %collective-permute-start.28 = (bf16[256,384]{1,0:T(8,128)(2,1)S(1)}, bf16[256,384]{1,0:T(8,128)(2,1)S(1)}, u32[]{:S(2)}, u32[]{:S(2)}) collective-permute-start(bf16[256,384]{1,0:T(8,128)(2,1)S(1)} %get-tuple-element.114), channel_id=1, source_target_pairs={{0,4},{1,5},{2,6},{3,7},{4,0},{5,1},{6,2},{7,3},{8,12},{9,13},{10,... | collective-permute-start | bytes 589832 | tf_op jit(solution)/shard_map/ppermute | solution.py:683
  101.5 1.9 %place.1 = bf16[256,4096]{1,0:T(8,128)(2,1)} custom-call(s32[5]{0:T(128)S(1)} %stack.23.place, bf16[256,512]{1,0:T(8,128)(2,1)S(1)} %get-tuple-element.106.refs_6_.refs_0_, bf16[256,768]{1,0:T(8,128)(2,1)S(1)} %get-tuple-element.105.refs_2_.refs_1_, bf16[256,384]{1,0:T(8,128)(2,1)S(1)} %get-tuple-element.108.refs_6_.refs_2_, ...), custom_call_target="tpu_custom_call" | custom-call | flops 1 | bytes 1 | tf_op jit(solution)/shard_map/place/pallas_call | solution.py:620
  (73 shorter events, 22.8 us)
Async XLA Ops:
  2.5 2.1 %collective-permute-start = (bf16[64,2048]{1,0:T(8,128)(2,1)S(1)}, bf16[64,2048]{1,0:T(8,128)(2,1)S(1)}, u32[]{:S(2)}, u32[]{:S(2)}) collective-permute-start(bf16[64,2048]{1,0:T(8,128)(2,1)S(1)} %pack_first.1.order), channel_id=1, source_target_pairs={{0,4},{1,5},{2,6},{3,7},{4,0},{5,1},{6,2},{7,3},{8,12},{9,13},{10,... | collective-permute-start | bytes 786440 | tf_op jit(solution)/shard_map/ppermute | solution.py:683
  4.6 3.5 %collective-permute-start.4 = (bf16[64,8448]{1,0:T(8,128)(2,1)S(1)}, bf16[64,8448]{1,0:T(8,128)(2,1)S(1)}, u32[]{:S(2)}, u32[]{:S(2)}) collective-permute-start(bf16[64,8448]{1,0:T(8,128)(2,1)S(1)} %gate.3), channel_id=1, source_target_pairs={{0,4},{1,5},{2,6},{3,7},{4,0},{5,1},{6,2},{7,3},{8,12},{9,13},{10,... | collective-permute-start | bytes 3244040 | tf_op jit(solution)/shard_map/ppermute | solution.py:683
  5.7 12.4 %collective-permute-start.1 = (bf16[128,512]{1,0:T(8,128)(2,1)S(1)}, bf16[128,512]{1,0:T(8,128)(2,1)S(1)}, u32[]{:S(2)}, u32[]{:S(2)}) collective-permute-start(bf16[128,512]{1,0:T(8,128)(2,1)S(1)} %get-tuple-element.61), channel_id=1, source_target_pairs={{0,2},{1,3},{2,0},{3,1},{4,6},{5,7},{6,4},{7,5},{8,10},{9,11},{10,... | collective-permute-start | bytes 393224 | tf_op jit(solution)/shard_map/ppermute | solution.py:683
  8.7 6.0 %collective-permute-start.5 = (bf16[3,10240]{1,0:T(4,128)(2,1)S(1)}, bf16[3,10240]{1,0:T(4,128)(2,1)S(1)}, u32[]{:S(2)}, u32[]{:S(2)}) collective-permute-start(bf16[3,10240]{1,0:T(4,128)(2,1)S(1)} %edge.1), channel_id=1, source_target_pairs={{3,11},{7,15},{11,19},{15,23},{19,27},{23,31}} | collective-permute-start | bytes 184328 | tf_op jit(solution)/shard_map/ppermute | solution.py:683
  9.4 11.6 %collective-permute-start.2 = (bf16[128,512]{1,0:T(8,128)(2,1)S(1)}, bf16[128,512]{1,0:T(8,128)(2,1)S(1)}, u32[]{:S(2)}, u32[]{:S(2)}) collective-permute-start(bf16[128,512]{1,0:T(8,128)(2,1)S(1)} %get-tuple-element.62), channel_id=1, source_target_pairs={{0,3},{1,2},{2,1},{3,0},{4,7},{5,6},{6,5},{7,4},{8,11},{9,10},{10,... | collective-permute-start | bytes 393224 | tf_op jit(solution)/shard_map/ppermute | solution.py:683
  10.0 11.0 %collective-permute-start.3 = (bf16[128,512]{1,0:T(8,128)(2,1)S(1)}, bf16[128,512]{1,0:T(8,128)(2,1)S(1)}, u32[]{:S(2)}, u32[]{:S(2)}) collective-permute-start(bf16[128,512]{1,0:T(8,128)(2,1)S(1)} %get-tuple-element.63), channel_id=1, source_target_pairs={{0,1},{1,0},{2,3},{3,2},{4,5},{5,4},{6,7},{7,6},{8,9},{9,8},{10,11... | collective-permute-start | bytes 393224 | tf_op jit(solution)/shard_map/ppermute | solution.py:683
  15.7 9.8 %collective-permute-start.6 = (bf16[128,384]{1,0:T(8,128)(2,1)S(1)}, bf16[128,384]{1,0:T(8,128)(2,1)S(1)}, u32[]{:S(2)}, u32[]{:S(2)}) collective-permute-start(bf16[128,384]{1,0:T(8,128)(2,1)S(1)} %get-tuple-element.69), channel_id=1, source_target_pairs={{0,2},{1,3},{2,0},{3,1},{4,6},{5,7},{6,4},{7,5},{8,10},{9,11},{10,... | collective-permute-start | bytes 294920 | tf_op jit(solution)/shard_map/ppermute | solution.py:683
  18.1 9.9 %collective-permute-start.7 = (bf16[128,384]{1,0:T(8,128)(2,1)S(1)}, bf16[128,384]{1,0:T(8,128)(2,1)S(1)}, u32[]{:S(2)}, u32[]{:S(2)}) collective-permute-start(bf16[128,384]{1,0:T(8,128)(2,1)S(1)} %get-tuple-element.70), channel_id=1, source_target_pairs={{0,3},{1,2},{2,1},{3,0},{4,7},{5,6},{6,5},{7,4},{8,11},{9,10},{10,... | collective-permute-start | bytes 294920 | tf_op jit(solution)/shard_map/ppermute | solution.py:683
  18.1 9.8 %collective-permute-start.8 = (bf16[128,384]{1,0:T(8,128)(2,1)S(1)}, bf16[128,384]{1,0:T(8,128)(2,1)S(1)}, u32[]{:S(2)}, u32[]{:S(2)}) collective-permute-start(bf16[128,384]{1,0:T(8,128)(2,1)S(1)} %get-tuple-element.71), channel_id=1, source_target_pairs={{0,1},{1,0},{2,3},{3,2},{4,5},{5,4},{6,7},{7,6},{8,9},{9,8},{10,11... | collective-permute-start | bytes 294920 | tf_op jit(solution)/shard_map/ppermute | solution.py:683
  20.9 10.4 %copy-start.5 = (f32[256]{0:T(256)S(1)}, f32[256]{0:T(256)}, u32[]{:S(2)}) copy-start(f32[256]{0:T(256)} %param.11) | copy-start | bytes 3076
  20.9 10.4 %copy-start.6 = (f32[256]{0:T(256)S(1)}, f32[256]{0:T(256)}, u32[]{:S(2)}) copy-start(f32[256]{0:T(256)} %param.12) | copy-start | bytes 3076
  20.9 10.4 %copy-start.7 = (f32[256]{0:T(256)S(1)}, f32[256]{0:T(256)}, u32[]{:S(2)}) copy-start(f32[256]{0:T(256)} %param.13) | copy-start | bytes 3076
  27.9 17.6 %collective-permute-start.14 = (bf16[128,1792]{1,0:T(8,128)(2,1)S(1)}, bf16[128,1792]{1,0:T(8,128)(2,1)S(1)}, u32[]{:S(2)}, u32[]{:S(2)}) collective-permute-start(bf16[128,1792]{1,0:T(8,128)(2,1)S(1)} %get-tuple-element.88), channel_id=1, source_target_pairs={{0,1},{1,0},{2,3},{3,2},{4,5},{5,4},{6,7},{7,6},{8,9},{9,8},{10,11... | collective-permute-start | bytes 1376264 | tf_op jit(solution)/shard_map/ppermute | solution.py:683
  27.9 17.6 %collective-permute-start.12 = (bf16[128,768]{1,0:T(8,128)(2,1)S(1)}, bf16[128,768]{1,0:T(8,128)(2,1)S(1)}, u32[]{:S(2)}, u32[]{:S(2)}) collective-permute-start(bf16[128,768]{1,0:T(8,128)(2,1)S(1)} %get-tuple-element.86), channel_id=1, source_target_pairs={{0,2},{1,3},{2,0},{3,1},{4,6},{5,7},{6,4},{7,5},{8,10},{9,11},{10,... | collective-permute-start | bytes 589832 | tf_op jit(solution)/shard_map/ppermute | solution.py:683
  31.3 14.2 %collective-permute-start.13 = (bf16[128,768]{1,0:T(8,128)(2,1)S(1)}, bf16[128,768]{1,0:T(8,128)(2,1)S(1)}, u32[]{:S(2)}, u32[]{:S(2)}) collective-permute-start(bf16[128,768]{1,0:T(8,128)(2,1)S(1)} %get-tuple-element.87), channel_id=1, source_target_pairs={{0,3},{1,2},{2,1},{3,0},{4,7},{5,6},{6,5},{7,4},{8,11},{9,10},{10,... | collective-permute-start | bytes 589832 | tf_op jit(solution)/shard_map/ppermute | solution.py:683
  35.1 17.0 %collective-permute-start.9 = (bf16[272,256]{1,0:T(8,128)(2,1)S(1)}, bf16[272,256]{1,0:T(8,128)(2,1)S(1)}, u32[]{:S(2)}, u32[]{:S(2)}) collective-permute-start(bf16[272,256]{1,0:T(8,128)(2,1)S(1)} %get-tuple-element.77.refs_0_.refs_2_), channel_id=1, source_target_pairs={{0,8},{1,9},{2,10},{3,11},{4,12},{5,13},{6,14},{7,15},{8,0},{9,1},... | collective-permute-start | bytes 417800 | tf_op jit(solution)/shard_map/ppermute | solution.py:683
  38.4 13.7 %collective-permute-start.10 = (bf16[272,256]{1,0:T(8,128)(2,1)S(1)}, bf16[272,256]{1,0:T(8,128)(2,1)S(1)}, u32[]{:S(2)}, u32[]{:S(2)}) collective-permute-start(bf16[272,256]{1,0:T(8,128)(2,1)S(1)} %get-tuple-element.78.refs_1_.refs_3_), channel_id=1, source_target_pairs={{0,8},{1,9},{2,10},{3,11},{4,12},{5,13},{6,14},{7,15},{8,0},{9,1},... | collective-permute-start | bytes 417800 | tf_op jit(solution)/shard_map/ppermute | solution.py:683
  45.6 22.4 %collective-permute-start.15 = (bf16[128,1024]{1,0:T(8,128)(2,1)S(1)}, bf16[128,1024]{1,0:T(8,128)(2,1)S(1)}, u32[]{:S(2)}, u32[]{:S(2)}) collective-permute-start(bf16[128,1024]{1,0:T(8,128)(2,1)S(1)} %get-tuple-element.89), channel_id=1, source_target_pairs={{0,2},{1,3},{2,0},{3,1},{4,6},{5,7},{6,4},{7,5},{8,10},{9,11},{10,... | collective-permute-start | bytes 786440 | tf_op jit(solution)/shard_map/ppermute | solution.py:683
  50.0 23.6 %collective-permute-start.16 = (bf16[128,1024]{1,0:T(8,128)(2,1)S(1)}, bf16[128,1024]{1,0:T(8,128)(2,1)S(1)}, u32[]{:S(2)}, u32[]{:S(2)}) collective-permute-start(bf16[128,1024]{1,0:T(8,128)(2,1)S(1)} %get-tuple-element.90), channel_id=1, source_target_pairs={{0,3},{1,2},{2,1},{3,0},{4,7},{5,6},{6,5},{7,4},{8,11},{9,10},{10,... | collective-permute-start | bytes 786440 | tf_op jit(solution)/shard_map/ppermute | solution.py:683
  55.4 6.2 %collective-permute-start.17 = (bf16[272,384]{1,0:T(8,128)(2,1)S(1)}, bf16[272,384]{1,0:T(8,128)(2,1)S(1)}, u32[]{:S(2)}, u32[]{:S(2)}) collective-permute-start(bf16[272,384]{1,0:T(8,128)(2,1)S(1)} %get-tuple-element.91.refs_1_), channel_id=1, source_target_pairs={{0,8},{1,9},{2,10},{3,11},{4,12},{5,13},{6,14},{7,15},{8,0},{9,1},... | collective-permute-start | bytes 626696 | tf_op jit(solution)/shard_map/ppermute | solution.py:683
  58.9 7.0 %collective-permute-start.18 = (bf16[272,384]{1,0:T(8,128)(2,1)S(1)}, bf16[272,384]{1,0:T(8,128)(2,1)S(1)}, u32[]{:S(2)}, u32[]{:S(2)}) collective-permute-start(bf16[272,384]{1,0:T(8,128)(2,1)S(1)} %get-tuple-element.92.refs_1_), channel_id=1, source_target_pairs={{0,8},{1,9},{2,10},{3,11},{4,12},{5,13},{6,14},{7,15},{8,0},{9,1},... | collective-permute-start | bytes 626696 | tf_op jit(solution)/shard_map/ppermute | solution.py:683
  60.2 24.3 %collective-permute-start.11 = (bf16[272,512]{1,0:T(8,128)(2,1)S(1)}, bf16[272,512]{1,0:T(8,128)(2,1)S(1)}, u32[]{:S(2)}, u32[]{:S(2)}) collective-permute-start(bf16[272,512]{1,0:T(8,128)(2,1)S(1)} %combine.5.refs_10_), channel_id=1, source_target_pairs={{0,16},{1,17},{2,18},{3,19},{4,20},{5,21},{6,22},{7,23},{8,24},{9,... | collective-permute-start | bytes 835592 | tf_op jit(solution)/shard_map/ppermute | solution.py:683
  62.3 22.3 %collective-permute-start.20 = (bf16[272,384]{1,0:T(8,128)(2,1)S(1)}, bf16[272,384]{1,0:T(8,128)(2,1)S(1)}, u32[]{:S(2)}, u32[]{:S(2)}) collective-permute-start(bf16[272,384]{1,0:T(8,128)(2,1)S(1)} %combine.6.refs_2_.refs_10_), channel_id=1, source_target_pairs={{0,16},{1,17},{2,18},{3,19},{4,20},{5,21},{6,22},{7,23},{8,24},{9,... | collective-permute-start | bytes 626696 | tf_op jit(solution)/shard_map/ppermute | solution.py:683
  66.6 18.0 %collective-permute-start.21 = (bf16[272,384]{1,0:T(8,128)(2,1)S(1)}, bf16[272,384]{1,0:T(8,128)(2,1)S(1)}, u32[]{:S(2)}, u32[]{:S(2)}) collective-permute-start(bf16[272,384]{1,0:T(8,128)(2,1)S(1)} %combine.7.refs_11_), channel_id=1, source_target_pairs={{0,16},{1,17},{2,18},{3,19},{4,20},{5,21},{6,22},{7,23},{8,24},{9,... | collective-permute-start | bytes 626696 | tf_op jit(solution)/shard_map/ppermute | solution.py:683
  75.5 9.1 %collective-permute-start.22 = (bf16[272,384]{1,0:T(8,128)(2,1)S(1)}, bf16[272,384]{1,0:T(8,128)(2,1)S(1)}, u32[]{:S(2)}, u32[]{:S(2)}) collective-permute-start(bf16[272,384]{1,0:T(8,128)(2,1)S(1)} %get-tuple-element.93.refs_8_.refs_1_), channel_id=1, source_target_pairs={{0,8},{1,9},{2,10},{3,11},{4,12},{5,13},{6,14},{7,15},{8,0},{9,1},... | collective-permute-start | bytes 626696 | tf_op jit(solution)/shard_map/ppermute | solution.py:683
  83.2 5.9 %collective-permute-start.19 = (bf16[272,384]{1,0:T(8,128)(2,1)S(1)}, bf16[272,384]{1,0:T(8,128)(2,1)S(1)}, u32[]{:S(2)}, u32[]{:S(2)}) collective-permute-start(bf16[272,384]{1,0:T(8,128)(2,1)S(1)} %get-tuple-element.102.refs_2_.refs_1_), channel_id=1, source_target_pairs={{0,8},{1,9},{2,10},{3,11},{4,12},{5,13},{6,14},{7,15},{8,0},{9,1},... | collective-permute-start | bytes 626696 | tf_op jit(solution)/shard_map/ppermute | solution.py:683
  85.2 9.5 %collective-permute-start.23 = (bf16[272,384]{1,0:T(8,128)(2,1)S(1)}, bf16[272,384]{1,0:T(8,128)(2,1)S(1)}, u32[]{:S(2)}, u32[]{:S(2)}) collective-permute-start(bf16[272,384]{1,0:T(8,128)(2,1)S(1)} %combine.8.refs_12_), channel_id=1, source_target_pairs={{0,16},{1,17},{2,18},{3,19},{4,20},{5,21},{6,22},{7,23},{8,24},{9,... | collective-permute-start | bytes 626696 | tf_op jit(solution)/shard_map/ppermute | solution.py:683
  89.8 7.2 %collective-permute-start.24 = (bf16[272,384]{1,0:T(8,128)(2,1)S(1)}, bf16[272,384]{1,0:T(8,128)(2,1)S(1)}, u32[]{:S(2)}, u32[]{:S(2)}) collective-permute-start(bf16[272,384]{1,0:T(8,128)(2,1)S(1)} %combine.9.refs_0_), channel_id=1, source_target_pairs={{0,16},{1,17},{2,18},{3,19},{4,20},{5,21},{6,22},{7,23},{8,24},{9,... | collective-permute-start | bytes 626696 | tf_op jit(solution)/shard_map/ppermute | solution.py:683
  91.1 9.3 %collective-permute-start.26 = (bf16[256,768]{1,0:T(8,128)(2,1)S(1)}, bf16[256,768]{1,0:T(8,128)(2,1)S(1)}, u32[]{:S(2)}, u32[]{:S(2)}) collective-permute-start(bf16[256,768]{1,0:T(8,128)(2,1)S(1)} %get-tuple-element.112), channel_id=1, source_target_pairs={{0,4},{1,5},{2,6},{3,7},{4,0},{5,1},{6,2},{7,3},{8,12},{9,13},{10,... | collective-permute-start | bytes 1179656 | tf_op jit(solution)/shard_map/ppermute | solution.py:683
  94.6 5.8 %collective-permute-start.25 = (bf16[256,512]{1,0:T(8,128)(2,1)S(1)}, bf16[256,512]{1,0:T(8,128)(2,1)S(1)}, u32[]{:S(2)}, u32[]{:S(2)}) collective-permute-start(bf16[256,512]{1,0:T(8,128)(2,1)S(1)} %get-tuple-element.111), channel_id=1, source_target_pairs={{0,4},{1,5},{2,6},{3,7},{4,0},{5,1},{6,2},{7,3},{8,12},{9,13},{10,... | collective-permute-start | bytes 786440 | tf_op jit(solution)/shard_map/ppermute | solution.py:683
  95.8 4.6 %collective-permute-start.27 = (bf16[256,384]{1,0:T(8,128)(2,1)S(1)}, bf16[256,384]{1,0:T(8,128)(2,1)S(1)}, u32[]{:S(2)}, u32[]{:S(2)}) collective-permute-start(bf16[256,384]{1,0:T(8,128)(2,1)S(1)} %get-tuple-element.113), channel_id=1, source_target_pairs={{0,4},{1,5},{2,6},{3,7},{4,0},{5,1},{6,2},{7,3},{8,12},{9,13},{10,... | collective-permute-start | bytes 589832 | tf_op jit(solution)/shard_map/ppermute | solution.py:683
  98.1 3.4 %collective-permute-start.28 = (bf16[256,384]{1,0:T(8,128)(2,1)S(1)}, bf16[256,384]{1,0:T(8,128)(2,1)S(1)}, u32[]{:S(2)}, u32[]{:S(2)}) collective-permute-start(bf16[256,384]{1,0:T(8,128)(2,1)S(1)} %get-tuple-element.114), channel_id=1, source_target_pairs={{0,4},{1,5},{2,6},{3,7},{4,0},{5,1},{6,2},{7,3},{8,12},{9,13},{10,... | collective-permute-start | bytes 589832 | tf_op jit(solution)/shard_map/ppermute | solution.py:683
  (5 other events, 14.3 us)

commit v22 on v21

--- a/solution.py
+++ b/solution.py
@@ -504,8 +504,8 @@
         at = slice(start, start + span.stop - span.start)
         theirs, mine = got_ref[:STATE, span].astype(F32), own_ref[:STATE, span].astype(F32)
         decay, other = decay_of(own_ref.at[:, span]), decay_of(got_ref.at[:, span])
-        early, late = jnp.where(odd, theirs, mine), jnp.where(odd, mine, theirs)
-        out_ref[:STATE, at] = (jnp.where(odd, decay, other) * early + late).astype(BF16)
+        total = jnp.where(odd, decay, 1.0) * theirs + jnp.where(odd, 1.0, other) * mine
+        out_ref[:STATE, at] = total.astype(BF16)
         put_decay(out_ref.at[:, at], decay * other)
         start = at.stop
 
@@ -608,8 +608,10 @@
     copies = []
     for first, keep, got in zip(firsts, keeps, gots):
         width = keep.shape[1]
-        copies.append((keep, out.at[:, ds(core * half + first, width)]))
-        copies.append((got, out.at[:, ds((1 - core) * half + first, width)]))
+        for top in range(0, keep.shape[0], 64):
+            rows = slice(top, top + 64)
+            copies.append((keep.at[rows], out.at[rows, ds(core * half + first, width)]))
+            copies.append((got.at[rows], out.at[rows, ds((1 - core) * half + first, width)]))
     for copy in run(copies, sems):
         copy.wait()
 
@@ -622,7 +624,7 @@
         out_shape=jax.ShapeDtypeStruct(shape, BF16),
         in_specs=[smem] + [vmem] * (2 * count),
         out_specs=hbm,
-        scratch_shapes=[pltpu.SemaphoreType.DMA((2 * count,))],
+        scratch_shapes=[pltpu.SemaphoreType.DMA((2 * count * (shape[0] // 64),))],
         compiler_params=pltpu.CompilerParams(vmem_limit_bytes=16 << 20),
         cost_estimate=pl.CostEstimate(flops=1, bytes_accessed=1, transcendentals=0),
         name="place",
@@ -846,14 +848,11 @@
         name="score",
     )
     local_of(0, [])
-    state_of(3, [partial[0]])
-
-    def in_full(i, order):
-        wide = [pltpu.VMEM((slab, GROUPED[i][2]), F32)]
-        finish_of(finish_kernel, i, [x[i], cum, row, score, skip], order, scratch=wide)
+    local_of(1, [partial[0]])
+    state_of(3, [partial[1]])
 
     combine_of(2, sent[3] + before[1] + before[0])
-    in_full(1, joined[2])
+    finish_of(final_kernel, 1, [partial[1]], joined[2])
     combine_of(3, [keep[1]])
     local_of(2, joined[3])
     local_of(3, [partial[2]])

time: 105 us -> 106 us (level)
    pallas_call x26 -> x27, Pallas kernels: 29.7 us -> 29.6 us  [call(): pl.pallas_call(body, out_shape=shapes, in_specs=specs, out_specs=[vmem] *...]
  transfers between devices with their start and end apart: 29 -> 29, of which waited for: 8 -> 9; matrix products, arithmetic and copies ran while one was open for 0% -> 0% of each run, Pallas kernels for 28% -> 28%
where the time goes in v22:
time: 106 us; the launch traced here: 105 us
  starting transfers between devices  48 us (45%)
  Pallas kernels  31.7 us (30%)
  waiting for transfers between devices  22.8 us (22%)
  local copies, waits for them, and re-layouts  2.06 us (2%)
    ppermute x29, starting transfers between devices, over(): lax.ppermute(block, axes, [(i, j) for i, j in route if j is not None and...  48 us
    pallas_call x27, Pallas kernels, call(): pl.pallas_call(body, out_shape=shapes, in_specs=specs, out_specs=[vmem] *...  29.6 us
    ppermute x29, waiting for transfers between devices, over(): lax.ppermute(block, axes, [(i, j) for i, j in route if j is not None and...  22.8 us
  transfers between devices with their start and end apart: 29, of which 9 were waited for; matrix products, arithmetic and copies ran while one was open for 0% of the time, Pallas kernels for 28%

profile of v22, /device:TPU:13, one launch (start us, length us, event | category | flops | bytes accessed | tf_op | source)
XLA Modules:
  0.0 105.1 jit_solution(17230470068576650194)
XLA Ops:
  0.1 1.7 %copy-done = bf16[64,20480]{1,0:T(8,128)(2,1)S(1)} copy-done((bf16[64,20480]{1,0:T(8,128)(2,1)S(1)}, bf16[64,20480]{1,0:T(8,128)(2,1)}, u32[]{:S(2)}) %copy-start) | copy-done | bytes 2621464
  3.2 1.3 %pack.1 = (bf16[64,8448]{1,0:T(8,128)(2,1)S(1)}, bf16[16,10240]{1,0:T(8,128)(2,1)S(1)}) custom-call(s32[5]{0:T(128)S(1)} %stack.23.place, bf16[64,20480]{1,0:T(8,128)(2,1)S(1)} %copy-done, bf16[64,256]{1,0:T(8,128)(2,1)S(1)} %copy-done.2, bf16[64,2048]{1,0:T(8,128)(2,1)S(1)} %pack_first.1.order), custom_call_target="tpu_custom_call" | custom-call | flops 1 | bytes 1 | tf_op jit(solution)/shard_map/pack/pallas_call | solution.py:660
  5.7 2.4 %collective-permute-start.1 = (bf16[128,512]{1,0:T(8,128)(2,1)S(1)}, bf16[128,512]{1,0:T(8,128)(2,1)S(1)}, u32[]{:S(2)}, u32[]{:S(2)}) collective-permute-start(bf16[128,512]{1,0:T(8,128)(2,1)S(1)} %get-tuple-element.61), channel_id=1, source_target_pairs={{0,2},{1,3},{2,0},{3,1},{4,6},{5,7},{6,4},{7,5},{8,10},{9,11},{10,... | collective-permute-start | bytes 393224 | tf_op jit(solution)/shard_map/ppermute | solution.py:685
  10.0 4.6 %collective-permute-start.3 = (bf16[128,512]{1,0:T(8,128)(2,1)S(1)}, bf16[128,512]{1,0:T(8,128)(2,1)S(1)}, u32[]{:S(2)}, u32[]{:S(2)}) collective-permute-start(bf16[128,512]{1,0:T(8,128)(2,1)S(1)} %get-tuple-element.63), channel_id=1, source_target_pairs={{0,1},{1,0},{2,3},{3,2},{4,5},{5,4},{6,7},{7,6},{8,9},{9,8},{10,11... | collective-permute-start | bytes 393224 | tf_op jit(solution)/shard_map/ppermute | solution.py:685
  15.7 2.4 %collective-permute-start.6 = (bf16[128,384]{1,0:T(8,128)(2,1)S(1)}, bf16[128,384]{1,0:T(8,128)(2,1)S(1)}, u32[]{:S(2)}, u32[]{:S(2)}) collective-permute-start(bf16[128,384]{1,0:T(8,128)(2,1)S(1)} %get-tuple-element.69), channel_id=1, source_target_pairs={{0,2},{1,3},{2,0},{3,1},{4,6},{5,7},{6,4},{7,5},{8,10},{9,11},{10,... | collective-permute-start | bytes 294920 | tf_op jit(solution)/shard_map/ppermute | solution.py:685
  21.0 4.5 %collective-permute-done.6.refs_1_.refs_6_ = bf16[128,384]{1,0:T(8,128)(2,1)S(1)} collective-permute-done((bf16[128,384]{1,0:T(8,128)(2,1)S(1)}, bf16[128,384]{1,0:T(8,128)(2,1)S(1)}, u32[]{:S(2)}, u32[]{:S(2)}) %collective-permute-start.6) | collective-permute-done | bytes 98336 | tf_op jit(solution)/shard_map/ppermute | solution.py:685
  25.5 2.5 %collective-permute-done.7.refs_2_.refs_7_ = bf16[128,384]{1,0:T(8,128)(2,1)S(1)} collective-permute-done((bf16[128,384]{1,0:T(8,128)(2,1)S(1)}, bf16[128,384]{1,0:T(8,128)(2,1)S(1)}, u32[]{:S(2)}, u32[]{:S(2)}) %collective-permute-start.7) | collective-permute-done | bytes 98336 | tf_op jit(solution)/shard_map/ppermute | solution.py:685
  27.9 3.4 %collective-permute-start.12 = (bf16[128,768]{1,0:T(8,128)(2,1)S(1)}, bf16[128,768]{1,0:T(8,128)(2,1)S(1)}, u32[]{:S(2)}, u32[]{:S(2)}) collective-permute-start(bf16[128,768]{1,0:T(8,128)(2,1)S(1)} %get-tuple-element.86), channel_id=1, source_target_pairs={{0,2},{1,3},{2,0},{3,1},{4,6},{5,7},{6,4},{7,5},{8,10},{9,11},{10,... | collective-permute-start | bytes 589832 | tf_op jit(solution)/shard_map/ppermute | solution.py:685
  31.3 1.7 %prep.1 = (bf16[512,256]{1,0:T(8,128)(2,1)S(1)}, f32[4,2560]{1,0:T(4,128)S(1)}, f32[512,128]{1,0:T(8,128)S(1)}, f32[128,512]{1,0:T(8,128)S(1)}, bf16[512,256]{1,...) custom-call(s32[5]{0:T(128)S(1)} %stack.23.place, ...), custom_call_target="tpu_custom_call" | custom-call | flops 1 | bytes 1 | tf_op jit(solution)/shard_map/prep/pallas_call | solution.py:660
  33.0 2.0 %state.4 = (bf16[512,512]{1,0:T(8,128)(2,1)S(1)}, f32[256,512]{1,0:T(8,128)S(1)}, bf16[272,256]{1,0:T(8,128)(2,1)S(1)}, bf16[272,256]{1,0:T(8,128)(2,1)S(1)}) custom-call(s32[5]{0:T(128)S(1)} %stack.23.place, bf16[128,512]{1,0:T(8,128)(2,1)S(1)} %get-tuple-element.60.refs_0_, bf16[128,512]{1,0:T(8,128)(2,1)S(1)} %collective-permute-done.1.refs_1_.refs_3_, ...), custom_call_target="tpu_custom_call" | custom-call | flops 1 | bytes 1 | tf_op jit(solution)/shard_map/state/pallas_call | solution.py:660
  35.1 3.3 %collective-permute-start.9 = (bf16[272,256]{1,0:T(8,128)(2,1)S(1)}, bf16[272,256]{1,0:T(8,128)(2,1)S(1)}, u32[]{:S(2)}, u32[]{:S(2)}) collective-permute-start(bf16[272,256]{1,0:T(8,128)(2,1)S(1)} %get-tuple-element.77.refs_0_.refs_2_), channel_id=1, source_target_pairs={{0,8},{1,9},{2,10},{3,11},{4,12},{5,13},{6,14},{7,15},{8,0},{9,1},... | collective-permute-start | bytes 417800 | tf_op jit(solution)/shard_map/ppermute | solution.py:685
  38.4 1.3 %collective-permute-start.10 = (bf16[272,256]{1,0:T(8,128)(2,1)S(1)}, bf16[272,256]{1,0:T(8,128)(2,1)S(1)}, u32[]{:S(2)}, u32[]{:S(2)}) collective-permute-start(bf16[272,256]{1,0:T(8,128)(2,1)S(1)} %get-tuple-element.78.refs_1_.refs_3_), channel_id=1, source_target_pairs={{0,8},{1,9},{2,10},{3,11},{4,12},{5,13},{6,14},{7,15},{8,0},{9,1},... | collective-permute-start | bytes 417800 | tf_op jit(solution)/shard_map/ppermute | solution.py:685
  40.5 5.0 %collective-permute-done.12.refs_2_.refs_1_ = bf16[128,768]{1,0:T(8,128)(2,1)S(1)} collective-permute-done((bf16[128,768]{1,0:T(8,128)(2,1)S(1)}, bf16[128,768]{1,0:T(8,128)(2,1)S(1)}, u32[]{:S(2)}, u32[]{:S(2)}) %collective-permute-start.12) | collective-permute-done | bytes 196640 | tf_op jit(solution)/shard_map/ppermute | solution.py:685
  45.6 4.4 %collective-permute-start.15 = (bf16[128,1024]{1,0:T(8,128)(2,1)S(1)}, bf16[128,1024]{1,0:T(8,128)(2,1)S(1)}, u32[]{:S(2)}, u32[]{:S(2)}) collective-permute-start(bf16[128,1024]{1,0:T(8,128)(2,1)S(1)} %get-tuple-element.89), channel_id=1, source_target_pairs={{0,2},{1,3},{2,0},{3,1},{4,6},{5,7},{6,4},{7,5},{8,10},{9,11},{10,... | collective-permute-start | bytes 786440 | tf_op jit(solution)/shard_map/ppermute | solution.py:685
  50.0 2.2 %collective-permute-start.16 = (bf16[128,1024]{1,0:T(8,128)(2,1)S(1)}, bf16[128,1024]{1,0:T(8,128)(2,1)S(1)}, u32[]{:S(2)}, u32[]{:S(2)}) collective-permute-start(bf16[128,1024]{1,0:T(8,128)(2,1)S(1)} %get-tuple-element.90), channel_id=1, source_target_pairs={{0,3},{1,2},{2,1},{3,0},{4,7},{5,6},{6,5},{7,4},{8,11},{9,10},{10,... | collective-permute-start | bytes 786440 | tf_op jit(solution)/shard_map/ppermute | solution.py:685
  52.8 2.6 %state.5 = (bf16[512,768]{1,0:T(8,128)(2,1)S(1)}, f32[256,768]{1,0:T(8,128)S(1)}, bf16[272,384]{1,0:T(8,128)(2,1)S(1)}, bf16[272,384]{1,0:T(8,128)(2,1)S(1)}) custom-call(s32[5]{0:T(128)S(1)} %stack.23.place, bf16[128,768]{1,0:T(8,128)(2,1)S(1)} %get-tuple-element.72.refs_9_.refs_0_, bf16[128,768]{1,0:T(8,128)(2,1)S(1)} %collective-permute-done.12.refs_2_.refs_1_, ...), custom_call_target="tpu_custom_call" | custom-call | flops 1 | bytes 1 | tf_op jit(solution)/shard_map/state/pallas_call | solution.py:660
  55.4 3.5 %collective-permute-start.17 = (bf16[272,384]{1,0:T(8,128)(2,1)S(1)}, bf16[272,384]{1,0:T(8,128)(2,1)S(1)}, u32[]{:S(2)}, u32[]{:S(2)}) collective-permute-start(bf16[272,384]{1,0:T(8,128)(2,1)S(1)} %get-tuple-element.91.refs_1_), channel_id=1, source_target_pairs={{0,8},{1,9},{2,10},{3,11},{4,12},{5,13},{6,14},{7,15},{8,0},{9,1},... | collective-permute-start | bytes 626696 | tf_op jit(solution)/shard_map/ppermute | solution.py:685
  58.9 1.3 %collective-permute-start.18 = (bf16[272,384]{1,0:T(8,128)(2,1)S(1)}, bf16[272,384]{1,0:T(8,128)(2,1)S(1)}, u32[]{:S(2)}, u32[]{:S(2)}) collective-permute-start(bf16[272,384]{1,0:T(8,128)(2,1)S(1)} %get-tuple-element.92.refs_1_), channel_id=1, source_target_pairs={{0,8},{1,9},{2,10},{3,11},{4,12},{5,13},{6,14},{7,15},{8,0},{9,1},... | collective-permute-start | bytes 626696 | tf_op jit(solution)/shard_map/ppermute | solution.py:685
  60.2 1.3 %collective-permute-start.11 = (bf16[272,512]{1,0:T(8,128)(2,1)S(1)}, bf16[272,512]{1,0:T(8,128)(2,1)S(1)}, u32[]{:S(2)}, u32[]{:S(2)}) collective-permute-start(bf16[272,512]{1,0:T(8,128)(2,1)S(1)} %combine.5.refs_10_), channel_id=1, source_target_pairs={{0,16},{1,17},{2,18},{3,19},{4,20},{5,21},{6,22},{7,23},{8,24},{9,... | collective-permute-start | bytes 835592 | tf_op jit(solution)/shard_map/ppermute | solution.py:685
  62.2 1.3 %collective-permute-start.20 = (bf16[272,384]{1,0:T(8,128)(2,1)S(1)}, bf16[272,384]{1,0:T(8,128)(2,1)S(1)}, u32[]{:S(2)}, u32[]{:S(2)}) collective-permute-start(bf16[272,384]{1,0:T(8,128)(2,1)S(1)} %combine.6.refs_2_.refs_10_), channel_id=1, source_target_pairs={{0,16},{1,17},{2,18},{3,19},{4,20},{5,21},{6,22},{7,23},{8,24},{9,... | collective-permute-start | bytes 626696 | tf_op jit(solution)/shard_map/ppermute | solution.py:685
  63.5 2.4 %collective-permute-done.18.refs_0_.refs_1_ = bf16[272,384]{1,0:T(8,128)(2,1)S(1)} collective-permute-done((bf16[272,384]{1,0:T(8,128)(2,1)S(1)}, bf16[272,384]{1,0:T(8,128)(2,1)S(1)}, u32[]{:S(2)}, u32[]{:S(2)}) %collective-permute-start.18) | collective-permute-done | bytes 208928 | tf_op jit(solution)/shard_map/ppermute | solution.py:685
  66.6 1.3 %collective-permute-start.21 = (bf16[272,384]{1,0:T(8,128)(2,1)S(1)}, bf16[272,384]{1,0:T(8,128)(2,1)S(1)}, u32[]{:S(2)}, u32[]{:S(2)}) collective-permute-start(bf16[272,384]{1,0:T(8,128)(2,1)S(1)} %combine.7.refs_11_), channel_id=1, source_target_pairs={{0,16},{1,17},{2,18},{3,19},{4,20},{5,21},{6,22},{7,23},{8,24},{9,... | collective-permute-start | bytes 626696 | tf_op jit(solution)/shard_map/ppermute | solution.py:685
  67.9 5.7 %collective-permute-done.16.refs_2_ = bf16[128,1024]{1,0:T(8,128)(2,1)S(1)} collective-permute-done((bf16[128,1024]{1,0:T(8,128)(2,1)S(1)}, bf16[128,1024]{1,0:T(8,128)(2,1)S(1)}, u32[]{:S(2)}, u32[]{:S(2)}) %collective-permute-start.16) | collective-permute-done | bytes 262176 | tf_op jit(solution)/shard_map/ppermute | solution.py:685
  73.6 1.9 %state.6 = (bf16[512,384]{1,0:T(8,128)(2,1)S(1)}, f32[256,384]{1,0:T(8,128)S(1)}, bf16[272,384]{1,0:T(8,128)(2,1)S(1)}) custom-call(s32[5]{0:T(128)S(1)} %stack.23.place, bf16[128,1024]{1,0:T(8,128)(2,1)S(1)} %get-tuple-element.79.refs_4_.refs_0_, bf16[128,1024]{1,0:T(8,128)(2,1)S(1)} %collective-permute-done.15.refs_1_, ...), custom_call_target="tpu_custom_call" | custom-call | flops 1 | bytes 1 | tf_op jit(solution)/shard_map/state/pallas_call | solution.py:660
  75.5 3.6 %collective-permute-start.22 = (bf16[272,384]{1,0:T(8,128)(2,1)S(1)}, bf16[272,384]{1,0:T(8,128)(2,1)S(1)}, u32[]{:S(2)}, u32[]{:S(2)}) collective-permute-start(bf16[272,384]{1,0:T(8,128)(2,1)S(1)} %get-tuple-element.93.refs_8_.refs_1_), channel_id=1, source_target_pairs={{0,8},{1,9},{2,10},{3,11},{4,12},{5,13},{6,14},{7,15},{8,0},{9,1},... | collective-permute-start | bytes 626696 | tf_op jit(solution)/shard_map/ppermute | solution.py:685
  81.2 1.5 %local.5.refs_10_.refs_7_ = f32[512,768]{1,0:T(8,128)S(1)} custom-call(bf16[512,768]{1,0:T(8,128)(2,1)S(1)} %get-tuple-element.100.x_ref, f32[512,128]{1,0:T(8,128)S(1)} %get-tuple-element.96.cum_ref, f32[128,512]{1,0:T(8,128)S(1)} %get-tuple-element.97.row_ref, f32[512,256]{1,0:T(8,128)S(1)} %get-tuple-element.98.score_ref, ...), custom_call_target="tpu_custom_call" | custom-call | flops 1 | bytes 1 | tf_op jit(solution)/shard_map/local/pallas_call | solution.py:660
  82.7 1.9 %state.7 = (bf16[512,384]{1,0:T(8,128)(2,1)S(1)}, f32[256,384]{1,0:T(8,128)S(1)}, bf16[272,384]{1,0:T(8,128)(2,1)S(1)}) custom-call(s32[5]{0:T(128)S(1)} %stack.23.place, bf16[128,1024]{1,0:T(8,128)(2,1)S(1)} %get-tuple-element.79.refs_4_.refs_0_, bf16[128,1024]{1,0:T(8,128)(2,1)S(1)} %collective-permute-done.15.refs_1_, ...), custom_call_target="tpu_custom_call" | custom-call | flops 1 | bytes 1 | tf_op jit(solution)/shard_map/state/pallas_call | solution.py:660
  84.7 1.3 %collective-permute-start.19 = (bf16[272,384]{1,0:T(8,128)(2,1)S(1)}, bf16[272,384]{1,0:T(8,128)(2,1)S(1)}, u32[]{:S(2)}, u32[]{:S(2)}) collective-permute-start(bf16[272,384]{1,0:T(8,128)(2,1)S(1)} %get-tuple-element.103.refs_2_.refs_1_), channel_id=1, source_target_pairs={{0,8},{1,9},{2,10},{3,11},{4,12},{5,13},{6,14},{7,15},{8,0},{9,1},... | collective-permute-start | bytes 626696 | tf_op jit(solution)/shard_map/ppermute | solution.py:685
  86.7 1.3 %collective-permute-start.23 = (bf16[272,384]{1,0:T(8,128)(2,1)S(1)}, bf16[272,384]{1,0:T(8,128)(2,1)S(1)}, u32[]{:S(2)}, u32[]{:S(2)}) collective-permute-start(bf16[272,384]{1,0:T(8,128)(2,1)S(1)} %combine.8.refs_8_), channel_id=1, source_target_pairs={{0,16},{1,17},{2,18},{3,19},{4,20},{5,21},{6,22},{7,23},{8,24},{9,... | collective-permute-start | bytes 626696 | tf_op jit(solution)/shard_map/ppermute | solution.py:685
  91.9 1.4 %collective-permute-start.26 = (bf16[256,768]{1,0:T(8,128)(2,1)S(1)}, bf16[256,768]{1,0:T(8,128)(2,1)S(1)}, u32[]{:S(2)}, u32[]{:S(2)}) collective-permute-start(bf16[256,768]{1,0:T(8,128)(2,1)S(1)} %get-tuple-element.112), channel_id=1, source_target_pairs={{0,4},{1,5},{2,6},{3,7},{4,0},{5,1},{6,2},{7,3},{8,12},{9,13},{10,... | collective-permute-start | bytes 1179656 | tf_op jit(solution)/shard_map/ppermute | solution.py:685
  99.4 2.4 %collective-permute-start.28 = (bf16[256,384]{1,0:T(8,128)(2,1)S(1)}, bf16[256,384]{1,0:T(8,128)(2,1)S(1)}, u32[]{:S(2)}, u32[]{:S(2)}) collective-permute-start(bf16[256,384]{1,0:T(8,128)(2,1)S(1)} %get-tuple-element.114), channel_id=1, source_target_pairs={{0,4},{1,5},{2,6},{3,7},{4,0},{5,1},{6,2},{7,3},{8,12},{9,13},{10,... | collective-permute-start | bytes 589832 | tf_op jit(solution)/shard_map/ppermute | solution.py:685
  102.9 2.1 %place.1 = bf16[256,4096]{1,0:T(8,128)(2,1)} custom-call(s32[5]{0:T(128)S(1)} %stack.23.place, bf16[256,512]{1,0:T(8,128)(2,1)S(1)} %get-tuple-element.106.refs_6_.refs_0_, bf16[256,768]{1,0:T(8,128)(2,1)S(1)} %get-tuple-element.105.refs_2_.refs_1_, bf16[256,384]{1,0:T(8,128)(2,1)S(1)} %get-tuple-element.108.refs_6_.refs_2_, ...), custom_call_target="tpu_custom_call" | custom-call | flops 1 | bytes 1 | tf_op jit(solution)/shard_map/place/pallas_call | solution.py:622
  (74 shorter events, 25.1 us)
Async XLA Ops:
  2.5 2.1 %collective-permute-start = (bf16[64,2048]{1,0:T(8,128)(2,1)S(1)}, bf16[64,2048]{1,0:T(8,128)(2,1)S(1)}, u32[]{:S(2)}, u32[]{:S(2)}) collective-permute-start(bf16[64,2048]{1,0:T(8,128)(2,1)S(1)} %pack_first.1.order), channel_id=1, source_target_pairs={{0,4},{1,5},{2,6},{3,7},{4,0},{5,1},{6,2},{7,3},{8,12},{9,13},{10,... | collective-permute-start | bytes 786440 | tf_op jit(solution)/shard_map/ppermute | solution.py:685
  4.6 3.5 %collective-permute-start.4 = (bf16[64,8448]{1,0:T(8,128)(2,1)S(1)}, bf16[64,8448]{1,0:T(8,128)(2,1)S(1)}, u32[]{:S(2)}, u32[]{:S(2)}) collective-permute-start(bf16[64,8448]{1,0:T(8,128)(2,1)S(1)} %gate.3), channel_id=1, source_target_pairs={{0,4},{1,5},{2,6},{3,7},{4,0},{5,1},{6,2},{7,3},{8,12},{9,13},{10,... | collective-permute-start | bytes 3244040 | tf_op jit(solution)/shard_map/ppermute | solution.py:685
  5.7 12.4 %collective-permute-start.1 = (bf16[128,512]{1,0:T(8,128)(2,1)S(1)}, bf16[128,512]{1,0:T(8,128)(2,1)S(1)}, u32[]{:S(2)}, u32[]{:S(2)}) collective-permute-start(bf16[128,512]{1,0:T(8,128)(2,1)S(1)} %get-tuple-element.61), channel_id=1, source_target_pairs={{0,2},{1,3},{2,0},{3,1},{4,6},{5,7},{6,4},{7,5},{8,10},{9,11},{10,... | collective-permute-start | bytes 393224 | tf_op jit(solution)/shard_map/ppermute | solution.py:685
  8.7 6.0 %collective-permute-start.5 = (bf16[3,10240]{1,0:T(4,128)(2,1)S(1)}, bf16[3,10240]{1,0:T(4,128)(2,1)S(1)}, u32[]{:S(2)}, u32[]{:S(2)}) collective-permute-start(bf16[3,10240]{1,0:T(4,128)(2,1)S(1)} %edge.1), channel_id=1, source_target_pairs={{3,11},{7,15},{11,19},{15,23},{19,27},{23,31}} | collective-permute-start | bytes 184328 | tf_op jit(solution)/shard_map/ppermute | solution.py:685
  9.4 11.6 %collective-permute-start.2 = (bf16[128,512]{1,0:T(8,128)(2,1)S(1)}, bf16[128,512]{1,0:T(8,128)(2,1)S(1)}, u32[]{:S(2)}, u32[]{:S(2)}) collective-permute-start(bf16[128,512]{1,0:T(8,128)(2,1)S(1)} %get-tuple-element.62), channel_id=1, source_target_pairs={{0,3},{1,2},{2,1},{3,0},{4,7},{5,6},{6,5},{7,4},{8,11},{9,10},{10,... | collective-permute-start | bytes 393224 | tf_op jit(solution)/shard_map/ppermute | solution.py:685
  10.0 11.0 %collective-permute-start.3 = (bf16[128,512]{1,0:T(8,128)(2,1)S(1)}, bf16[128,512]{1,0:T(8,128)(2,1)S(1)}, u32[]{:S(2)}, u32[]{:S(2)}) collective-permute-start(bf16[128,512]{1,0:T(8,128)(2,1)S(1)} %get-tuple-element.63), channel_id=1, source_target_pairs={{0,1},{1,0},{2,3},{3,2},{4,5},{5,4},{6,7},{7,6},{8,9},{9,8},{10,11... | collective-permute-start | bytes 393224 | tf_op jit(solution)/shard_map/ppermute | solution.py:685
  15.7 9.8 %collective-permute-start.6 = (bf16[128,384]{1,0:T(8,128)(2,1)S(1)}, bf16[128,384]{1,0:T(8,128)(2,1)S(1)}, u32[]{:S(2)}, u32[]{:S(2)}) collective-permute-start(bf16[128,384]{1,0:T(8,128)(2,1)S(1)} %get-tuple-element.69), channel_id=1, source_target_pairs={{0,2},{1,3},{2,0},{3,1},{4,6},{5,7},{6,4},{7,5},{8,10},{9,11},{10,... | collective-permute-start | bytes 294920 | tf_op jit(solution)/shard_map/ppermute | solution.py:685
  18.1 9.9 %collective-permute-start.7 = (bf16[128,384]{1,0:T(8,128)(2,1)S(1)}, bf16[128,384]{1,0:T(8,128)(2,1)S(1)}, u32[]{:S(2)}, u32[]{:S(2)}) collective-permute-start(bf16[128,384]{1,0:T(8,128)(2,1)S(1)} %get-tuple-element.70), channel_id=1, source_target_pairs={{0,3},{1,2},{2,1},{3,0},{4,7},{5,6},{6,5},{7,4},{8,11},{9,10},{10,... | collective-permute-start | bytes 294920 | tf_op jit(solution)/shard_map/ppermute | solution.py:685
  18.1 9.8 %collective-permute-start.8 = (bf16[128,384]{1,0:T(8,128)(2,1)S(1)}, bf16[128,384]{1,0:T(8,128)(2,1)S(1)}, u32[]{:S(2)}, u32[]{:S(2)}) collective-permute-start(bf16[128,384]{1,0:T(8,128)(2,1)S(1)} %get-tuple-element.71), channel_id=1, source_target_pairs={{0,1},{1,0},{2,3},{3,2},{4,5},{5,4},{6,7},{7,6},{8,9},{9,8},{10,11... | collective-permute-start | bytes 294920 | tf_op jit(solution)/shard_map/ppermute | solution.py:685
  20.9 10.4 %copy-start.5 = (f32[256]{0:T(256)S(1)}, f32[256]{0:T(256)}, u32[]{:S(2)}) copy-start(f32[256]{0:T(256)} %param.11) | copy-start | bytes 3076
  20.9 10.4 %copy-start.6 = (f32[256]{0:T(256)S(1)}, f32[256]{0:T(256)}, u32[]{:S(2)}) copy-start(f32[256]{0:T(256)} %param.12) | copy-start | bytes 3076
  20.9 10.4 %copy-start.7 = (f32[256]{0:T(256)S(1)}, f32[256]{0:T(256)}, u32[]{:S(2)}) copy-start(f32[256]{0:T(256)} %param.13) | copy-start | bytes 3076
  27.9 17.6 %collective-permute-start.14 = (bf16[128,1792]{1,0:T(8,128)(2,1)S(1)}, bf16[128,1792]{1,0:T(8,128)(2,1)S(1)}, u32[]{:S(2)}, u32[]{:S(2)}) collective-permute-start(bf16[128,1792]{1,0:T(8,128)(2,1)S(1)} %get-tuple-element.88), channel_id=1, source_target_pairs={{0,1},{1,0},{2,3},{3,2},{4,5},{5,4},{6,7},{7,6},{8,9},{9,8},{10,11... | collective-permute-start | bytes 1376264 | tf_op jit(solution)/shard_map/ppermute | solution.py:685
  27.9 17.6 %collective-permute-start.12 = (bf16[128,768]{1,0:T(8,128)(2,1)S(1)}, bf16[128,768]{1,0:T(8,128)(2,1)S(1)}, u32[]{:S(2)}, u32[]{:S(2)}) collective-permute-start(bf16[128,768]{1,0:T(8,128)(2,1)S(1)} %get-tuple-element.86), channel_id=1, source_target_pairs={{0,2},{1,3},{2,0},{3,1},{4,6},{5,7},{6,4},{7,5},{8,10},{9,11},{10,... | collective-permute-start | bytes 589832 | tf_op jit(solution)/shard_map/ppermute | solution.py:685
  31.3 14.2 %collective-permute-start.13 = (bf16[128,768]{1,0:T(8,128)(2,1)S(1)}, bf16[128,768]{1,0:T(8,128)(2,1)S(1)}, u32[]{:S(2)}, u32[]{:S(2)}) collective-permute-start(bf16[128,768]{1,0:T(8,128)(2,1)S(1)} %get-tuple-element.87), channel_id=1, source_target_pairs={{0,3},{1,2},{2,1},{3,0},{4,7},{5,6},{6,5},{7,4},{8,11},{9,10},{10,... | collective-permute-start | bytes 589832 | tf_op jit(solution)/shard_map/ppermute | solution.py:685
  35.1 17.0 %collective-permute-start.9 = (bf16[272,256]{1,0:T(8,128)(2,1)S(1)}, bf16[272,256]{1,0:T(8,128)(2,1)S(1)}, u32[]{:S(2)}, u32[]{:S(2)}) collective-permute-start(bf16[272,256]{1,0:T(8,128)(2,1)S(1)} %get-tuple-element.77.refs_0_.refs_2_), channel_id=1, source_target_pairs={{0,8},{1,9},{2,10},{3,11},{4,12},{5,13},{6,14},{7,15},{8,0},{9,1},... | collective-permute-start | bytes 417800 | tf_op jit(solution)/shard_map/ppermute | solution.py:685
  38.4 13.7 %collective-permute-start.10 = (bf16[272,256]{1,0:T(8,128)(2,1)S(1)}, bf16[272,256]{1,0:T(8,128)(2,1)S(1)}, u32[]{:S(2)}, u32[]{:S(2)}) collective-permute-start(bf16[272,256]{1,0:T(8,128)(2,1)S(1)} %get-tuple-element.78.refs_1_.refs_3_), channel_id=1, source_target_pairs={{0,8},{1,9},{2,10},{3,11},{4,12},{5,13},{6,14},{7,15},{8,0},{9,1},... | collective-permute-start | bytes 417800 | tf_op jit(solution)/shard_map/ppermute | solution.py:685
  45.6 22.3 %collective-permute-start.15 = (bf16[128,1024]{1,0:T(8,128)(2,1)S(1)}, bf16[128,1024]{1,0:T(8,128)(2,1)S(1)}, u32[]{:S(2)}, u32[]{:S(2)}) collective-permute-start(bf16[128,1024]{1,0:T(8,128)(2,1)S(1)} %get-tuple-element.89), channel_id=1, source_target_pairs={{0,2},{1,3},{2,0},{3,1},{4,6},{5,7},{6,4},{7,5},{8,10},{9,11},{10,... | collective-permute-start | bytes 786440 | tf_op jit(solution)/shard_map/ppermute | solution.py:685
  50.0 23.6 %collective-permute-start.16 = (bf16[128,1024]{1,0:T(8,128)(2,1)S(1)}, bf16[128,1024]{1,0:T(8,128)(2,1)S(1)}, u32[]{:S(2)}, u32[]{:S(2)}) collective-permute-start(bf16[128,1024]{1,0:T(8,128)(2,1)S(1)} %get-tuple-element.90), channel_id=1, source_target_pairs={{0,3},{1,2},{2,1},{3,0},{4,7},{5,6},{6,5},{7,4},{8,11},{9,10},{10,... | collective-permute-start | bytes 786440 | tf_op jit(solution)/shard_map/ppermute | solution.py:685
  55.4 6.2 %collective-permute-start.17 = (bf16[272,384]{1,0:T(8,128)(2,1)S(1)}, bf16[272,384]{1,0:T(8,128)(2,1)S(1)}, u32[]{:S(2)}, u32[]{:S(2)}) collective-permute-start(bf16[272,384]{1,0:T(8,128)(2,1)S(1)} %get-tuple-element.91.refs_1_), channel_id=1, source_target_pairs={{0,8},{1,9},{2,10},{3,11},{4,12},{5,13},{6,14},{7,15},{8,0},{9,1},... | collective-permute-start | bytes 626696 | tf_op jit(solution)/shard_map/ppermute | solution.py:685
  58.9 7.0 %collective-permute-start.18 = (bf16[272,384]{1,0:T(8,128)(2,1)S(1)}, bf16[272,384]{1,0:T(8,128)(2,1)S(1)}, u32[]{:S(2)}, u32[]{:S(2)}) collective-permute-start(bf16[272,384]{1,0:T(8,128)(2,1)S(1)} %get-tuple-element.92.refs_1_), channel_id=1, source_target_pairs={{0,8},{1,9},{2,10},{3,11},{4,12},{5,13},{6,14},{7,15},{8,0},{9,1},... | collective-permute-start | bytes 626696 | tf_op jit(solution)/shard_map/ppermute | solution.py:685
  60.2 25.8 %collective-permute-start.11 = (bf16[272,512]{1,0:T(8,128)(2,1)S(1)}, bf16[272,512]{1,0:T(8,128)(2,1)S(1)}, u32[]{:S(2)}, u32[]{:S(2)}) collective-permute-start(bf16[272,512]{1,0:T(8,128)(2,1)S(1)} %combine.5.refs_10_), channel_id=1, source_target_pairs={{0,16},{1,17},{2,18},{3,19},{4,20},{5,21},{6,22},{7,23},{8,24},{9,... | collective-permute-start | bytes 835592 | tf_op jit(solution)/shard_map/ppermute | solution.py:685
  62.2 23.8 %collective-permute-start.20 = (bf16[272,384]{1,0:T(8,128)(2,1)S(1)}, bf16[272,384]{1,0:T(8,128)(2,1)S(1)}, u32[]{:S(2)}, u32[]{:S(2)}) collective-permute-start(bf16[272,384]{1,0:T(8,128)(2,1)S(1)} %combine.6.refs_2_.refs_10_), channel_id=1, source_target_pairs={{0,16},{1,17},{2,18},{3,19},{4,20},{5,21},{6,22},{7,23},{8,24},{9,... | collective-permute-start | bytes 626696 | tf_op jit(solution)/shard_map/ppermute | solution.py:685
  66.6 19.4 %collective-permute-start.21 = (bf16[272,384]{1,0:T(8,128)(2,1)S(1)}, bf16[272,384]{1,0:T(8,128)(2,1)S(1)}, u32[]{:S(2)}, u32[]{:S(2)}) collective-permute-start(bf16[272,384]{1,0:T(8,128)(2,1)S(1)} %combine.7.refs_11_), channel_id=1, source_target_pairs={{0,16},{1,17},{2,18},{3,19},{4,20},{5,21},{6,22},{7,23},{8,24},{9,... | collective-permute-start | bytes 626696 | tf_op jit(solution)/shard_map/ppermute | solution.py:685
  75.5 10.5 %collective-permute-start.22 = (bf16[272,384]{1,0:T(8,128)(2,1)S(1)}, bf16[272,384]{1,0:T(8,128)(2,1)S(1)}, u32[]{:S(2)}, u32[]{:S(2)}) collective-permute-start(bf16[272,384]{1,0:T(8,128)(2,1)S(1)} %get-tuple-element.93.refs_8_.refs_1_), channel_id=1, source_target_pairs={{0,8},{1,9},{2,10},{3,11},{4,12},{5,13},{6,14},{7,15},{8,0},{9,1},... | collective-permute-start | bytes 626696 | tf_op jit(solution)/shard_map/ppermute | solution.py:685
  84.7 5.3 %collective-permute-start.19 = (bf16[272,384]{1,0:T(8,128)(2,1)S(1)}, bf16[272,384]{1,0:T(8,128)(2,1)S(1)}, u32[]{:S(2)}, u32[]{:S(2)}) collective-permute-start(bf16[272,384]{1,0:T(8,128)(2,1)S(1)} %get-tuple-element.103.refs_2_.refs_1_), channel_id=1, source_target_pairs={{0,8},{1,9},{2,10},{3,11},{4,12},{5,13},{6,14},{7,15},{8,0},{9,1},... | collective-permute-start | bytes 626696 | tf_op jit(solution)/shard_map/ppermute | solution.py:685
  86.7 9.4 %collective-permute-start.23 = (bf16[272,384]{1,0:T(8,128)(2,1)S(1)}, bf16[272,384]{1,0:T(8,128)(2,1)S(1)}, u32[]{:S(2)}, u32[]{:S(2)}) collective-permute-start(bf16[272,384]{1,0:T(8,128)(2,1)S(1)} %combine.8.refs_8_), channel_id=1, source_target_pairs={{0,16},{1,17},{2,18},{3,19},{4,20},{5,21},{6,22},{7,23},{8,24},{9,... | collective-permute-start | bytes 626696 | tf_op jit(solution)/shard_map/ppermute | solution.py:685
  90.6 7.7 %collective-permute-start.24 = (bf16[272,384]{1,0:T(8,128)(2,1)S(1)}, bf16[272,384]{1,0:T(8,128)(2,1)S(1)}, u32[]{:S(2)}, u32[]{:S(2)}) collective-permute-start(bf16[272,384]{1,0:T(8,128)(2,1)S(1)} %combine.9.refs_0_), channel_id=1, source_target_pairs={{0,16},{1,17},{2,18},{3,19},{4,20},{5,21},{6,22},{7,23},{8,24},{9,... | collective-permute-start | bytes 626696 | tf_op jit(solution)/shard_map/ppermute | solution.py:685
  91.9 9.9 %collective-permute-start.26 = (bf16[256,768]{1,0:T(8,128)(2,1)S(1)}, bf16[256,768]{1,0:T(8,128)(2,1)S(1)}, u32[]{:S(2)}, u32[]{:S(2)}) collective-permute-start(bf16[256,768]{1,0:T(8,128)(2,1)S(1)} %get-tuple-element.112), channel_id=1, source_target_pairs={{0,4},{1,5},{2,6},{3,7},{4,0},{5,1},{6,2},{7,3},{8,12},{9,13},{10,... | collective-permute-start | bytes 1179656 | tf_op jit(solution)/shard_map/ppermute | solution.py:685
  96.0 5.8 %collective-permute-start.25 = (bf16[256,512]{1,0:T(8,128)(2,1)S(1)}, bf16[256,512]{1,0:T(8,128)(2,1)S(1)}, u32[]{:S(2)}, u32[]{:S(2)}) collective-permute-start(bf16[256,512]{1,0:T(8,128)(2,1)S(1)} %get-tuple-element.111), channel_id=1, source_target_pairs={{0,4},{1,5},{2,6},{3,7},{4,0},{5,1},{6,2},{7,3},{8,12},{9,13},{10,... | collective-permute-start | bytes 786440 | tf_op jit(solution)/shard_map/ppermute | solution.py:685
  97.1 4.7 %collective-permute-start.27 = (bf16[256,384]{1,0:T(8,128)(2,1)S(1)}, bf16[256,384]{1,0:T(8,128)(2,1)S(1)}, u32[]{:S(2)}, u32[]{:S(2)}) collective-permute-start(bf16[256,384]{1,0:T(8,128)(2,1)S(1)} %get-tuple-element.113), channel_id=1, source_target_pairs={{0,4},{1,5},{2,6},{3,7},{4,0},{5,1},{6,2},{7,3},{8,12},{9,13},{10,... | collective-permute-start | bytes 589832 | tf_op jit(solution)/shard_map/ppermute | solution.py:685
  99.4 3.4 %collective-permute-start.28 = (bf16[256,384]{1,0:T(8,128)(2,1)S(1)}, bf16[256,384]{1,0:T(8,128)(2,1)S(1)}, u32[]{:S(2)}, u32[]{:S(2)}) collective-permute-start(bf16[256,384]{1,0:T(8,128)(2,1)S(1)} %get-tuple-element.114), channel_id=1, source_target_pairs={{0,4},{1,5},{2,6},{3,7},{4,0},{5,1},{6,2},{7,3},{8,12},{9,13},{10,... | collective-permute-start | bytes 589832 | tf_op jit(solution)/shard_map/ppermute | solution.py:685
  (5 other events, 16.1 us)

commit v23 on v21

--- a/solution.py
+++ b/solution.py
@@ -504,8 +504,8 @@
         at = slice(start, start + span.stop - span.start)
         theirs, mine = got_ref[:STATE, span].astype(F32), own_ref[:STATE, span].astype(F32)
         decay, other = decay_of(own_ref.at[:, span]), decay_of(got_ref.at[:, span])
-        early, late = jnp.where(odd, theirs, mine), jnp.where(odd, mine, theirs)
-        out_ref[:STATE, at] = (jnp.where(odd, decay, other) * early + late).astype(BF16)
+        total = jnp.where(odd, decay, 1.0) * theirs + jnp.where(odd, 1.0, other) * mine
+        out_ref[:STATE, at] = total.astype(BF16)
         put_decay(out_ref.at[:, at], decay * other)
         start = at.stop
 
@@ -845,14 +845,14 @@
         scratch=[pltpu.VMEM((slab + 8, STATE), F32)],
         name="score",
     )
-    local_of(0, [])
-    state_of(3, [partial[0]])
+    state_of(3, [score])
+    local_of(0, sent[3])
 
     def in_full(i, order):
         wide = [pltpu.VMEM((slab, GROUPED[i][2]), F32)]
         finish_of(finish_kernel, i, [x[i], cum, row, score, skip], order, scratch=wide)
 
-    combine_of(2, sent[3] + before[1] + before[0])
+    combine_of(2, [partial[0]] + before[1] + before[0])
     in_full(1, joined[2])
     combine_of(3, [keep[1]])
     local_of(2, joined[3])

time: 105 us -> 104 us (level)
  no operation moved by 1% of the time
where the time goes in v23:
time: 104 us
  starting transfers between devices  46.8 us (45%)
  Pallas kernels  31.5 us (30%)
  waiting for transfers between devices  22.6 us (22%)
  local copies, waits for them, and re-layouts  2.06 us (2%)
    ppermute x29, starting transfers between devices, over(): lax.ppermute(block, axes, [(i, j) for i, j in route if j is not None and...  46.8 us
    pallas_call x26, Pallas kernels, call(): pl.pallas_call(body, out_shape=shapes, in_specs=specs, out_specs=[vmem] *...  29.6 us
    ppermute x29, waiting for transfers between devices, over(): lax.ppermute(block, axes, [(i, j) for i, j in route if j is not None and...  22.6 us
  transfers between devices with their start and end apart: 29, of which 8 were waited for; matrix products, arithmetic and copies ran while one was open for 0% of the time, Pallas kernels for 28%

profile of v23, /device:TPU:13, one launch (start us, length us, event | category | flops | bytes accessed | tf_op | source)
XLA Modules:
  0.0 103.5 jit_solution(13874199378468331047)
XLA Ops:
  0.1 1.7 %copy-done = bf16[64,20480]{1,0:T(8,128)(2,1)S(1)} copy-done((bf16[64,20480]{1,0:T(8,128)(2,1)S(1)}, bf16[64,20480]{1,0:T(8,128)(2,1)}, u32[]{:S(2)}) %copy-start) | copy-done | bytes 2621464
  3.2 1.3 %pack.1 = (bf16[64,8448]{1,0:T(8,128)(2,1)S(1)}, bf16[16,10240]{1,0:T(8,128)(2,1)S(1)}) custom-call(s32[5]{0:T(128)S(1)} %stack.23.place, bf16[64,20480]{1,0:T(8,128)(2,1)S(1)} %copy-done, bf16[64,256]{1,0:T(8,128)(2,1)S(1)} %copy-done.2, bf16[64,2048]{1,0:T(8,128)(2,1)S(1)} %pack_first.1.order), custom_call_target="tpu_custom_call" | custom-call | flops 1 | bytes 1 | tf_op jit(solution)/shard_map/pack/pallas_call | solution.py:658
  5.7 2.4 %collective-permute-start.1 = (bf16[128,512]{1,0:T(8,128)(2,1)S(1)}, bf16[128,512]{1,0:T(8,128)(2,1)S(1)}, u32[]{:S(2)}, u32[]{:S(2)}) collective-permute-start(bf16[128,512]{1,0:T(8,128)(2,1)S(1)} %get-tuple-element.61), channel_id=1, source_target_pairs={{0,2},{1,3},{2,0},{3,1},{4,6},{5,7},{6,4},{7,5},{8,10},{9,11},{10,... | collective-permute-start | bytes 393224 | tf_op jit(solution)/shard_map/ppermute | solution.py:683
  10.0 4.6 %collective-permute-start.3 = (bf16[128,512]{1,0:T(8,128)(2,1)S(1)}, bf16[128,512]{1,0:T(8,128)(2,1)S(1)}, u32[]{:S(2)}, u32[]{:S(2)}) collective-permute-start(bf16[128,512]{1,0:T(8,128)(2,1)S(1)} %get-tuple-element.63), channel_id=1, source_target_pairs={{0,1},{1,0},{2,3},{3,2},{4,5},{5,4},{6,7},{7,6},{8,9},{9,8},{10,11... | collective-permute-start | bytes 393224 | tf_op jit(solution)/shard_map/ppermute | solution.py:683
  15.7 2.4 %collective-permute-start.6 = (bf16[128,384]{1,0:T(8,128)(2,1)S(1)}, bf16[128,384]{1,0:T(8,128)(2,1)S(1)}, u32[]{:S(2)}, u32[]{:S(2)}) collective-permute-start(bf16[128,384]{1,0:T(8,128)(2,1)S(1)} %get-tuple-element.69), channel_id=1, source_target_pairs={{0,2},{1,3},{2,0},{3,1},{4,6},{5,7},{6,4},{7,5},{8,10},{9,11},{10,... | collective-permute-start | bytes 294920 | tf_op jit(solution)/shard_map/ppermute | solution.py:683
  21.0 4.5 %collective-permute-done.6.refs_1_.refs_6_ = bf16[128,384]{1,0:T(8,128)(2,1)S(1)} collective-permute-done((bf16[128,384]{1,0:T(8,128)(2,1)S(1)}, bf16[128,384]{1,0:T(8,128)(2,1)S(1)}, u32[]{:S(2)}, u32[]{:S(2)}) %collective-permute-start.6) | collective-permute-done | bytes 98336 | tf_op jit(solution)/shard_map/ppermute | solution.py:683
  25.5 2.5 %collective-permute-done.7.refs_2_.refs_7_ = bf16[128,384]{1,0:T(8,128)(2,1)S(1)} collective-permute-done((bf16[128,384]{1,0:T(8,128)(2,1)S(1)}, bf16[128,384]{1,0:T(8,128)(2,1)S(1)}, u32[]{:S(2)}, u32[]{:S(2)}) %collective-permute-start.7) | collective-permute-done | bytes 98336 | tf_op jit(solution)/shard_map/ppermute | solution.py:683
  27.9 3.4 %collective-permute-start.12 = (bf16[128,768]{1,0:T(8,128)(2,1)S(1)}, bf16[128,768]{1,0:T(8,128)(2,1)S(1)}, u32[]{:S(2)}, u32[]{:S(2)}) collective-permute-start(bf16[128,768]{1,0:T(8,128)(2,1)S(1)} %get-tuple-element.86), channel_id=1, source_target_pairs={{0,2},{1,3},{2,0},{3,1},{4,6},{5,7},{6,4},{7,5},{8,10},{9,11},{10,... | collective-permute-start | bytes 589832 | tf_op jit(solution)/shard_map/ppermute | solution.py:683
  31.3 1.7 %prep.1 = (bf16[512,256]{1,0:T(8,128)(2,1)S(1)}, f32[4,2560]{1,0:T(4,128)S(1)}, f32[512,128]{1,0:T(8,128)S(1)}, f32[128,512]{1,0:T(8,128)S(1)}, bf16[512,256]{1,...) custom-call(s32[5]{0:T(128)S(1)} %stack.23.place, ...), custom_call_target="tpu_custom_call" | custom-call | flops 1 | bytes 1 | tf_op jit(solution)/shard_map/prep/pallas_call | solution.py:658
  33.0 2.1 %state.4 = (bf16[512,512]{1,0:T(8,128)(2,1)S(1)}, f32[256,512]{1,0:T(8,128)S(1)}, bf16[272,256]{1,0:T(8,128)(2,1)S(1)}, bf16[272,256]{1,0:T(8,128)(2,1)S(1)}) custom-call(s32[5]{0:T(128)S(1)} %stack.23.place, bf16[128,512]{1,0:T(8,128)(2,1)S(1)} %get-tuple-element.60.refs_0_, bf16[128,512]{1,0:T(8,128)(2,1)S(1)} %collective-permute-done.1.refs_1_.refs_3_, ...), custom_call_target="tpu_custom_call" | custom-call | flops 1 | bytes 1 | tf_op jit(solution)/shard_map/state/pallas_call | solution.py:658
  35.1 3.3 %collective-permute-start.9 = (bf16[272,256]{1,0:T(8,128)(2,1)S(1)}, bf16[272,256]{1,0:T(8,128)(2,1)S(1)}, u32[]{:S(2)}, u32[]{:S(2)}) collective-permute-start(bf16[272,256]{1,0:T(8,128)(2,1)S(1)} %get-tuple-element.77.refs_0_.refs_2_), channel_id=1, source_target_pairs={{0,8},{1,9},{2,10},{3,11},{4,12},{5,13},{6,14},{7,15},{8,0},{9,1},... | collective-permute-start | bytes 417800 | tf_op jit(solution)/shard_map/ppermute | solution.py:683
  38.4 1.3 %collective-permute-start.10 = (bf16[272,256]{1,0:T(8,128)(2,1)S(1)}, bf16[272,256]{1,0:T(8,128)(2,1)S(1)}, u32[]{:S(2)}, u32[]{:S(2)}) collective-permute-start(bf16[272,256]{1,0:T(8,128)(2,1)S(1)} %get-tuple-element.78.refs_1_.refs_3_), channel_id=1, source_target_pairs={{0,8},{1,9},{2,10},{3,11},{4,12},{5,13},{6,14},{7,15},{8,0},{9,1},... | collective-permute-start | bytes 417800 | tf_op jit(solution)/shard_map/ppermute | solution.py:683
  40.5 5.0 %collective-permute-done.12.refs_2_.refs_1_ = bf16[128,768]{1,0:T(8,128)(2,1)S(1)} collective-permute-done((bf16[128,768]{1,0:T(8,128)(2,1)S(1)}, bf16[128,768]{1,0:T(8,128)(2,1)S(1)}, u32[]{:S(2)}, u32[]{:S(2)}) %collective-permute-start.12) | collective-permute-done | bytes 196640 | tf_op jit(solution)/shard_map/ppermute | solution.py:683
  45.6 4.4 %collective-permute-start.15 = (bf16[128,1024]{1,0:T(8,128)(2,1)S(1)}, bf16[128,1024]{1,0:T(8,128)(2,1)S(1)}, u32[]{:S(2)}, u32[]{:S(2)}) collective-permute-start(bf16[128,1024]{1,0:T(8,128)(2,1)S(1)} %get-tuple-element.89), channel_id=1, source_target_pairs={{0,2},{1,3},{2,0},{3,1},{4,6},{5,7},{6,4},{7,5},{8,10},{9,11},{10,... | collective-permute-start | bytes 786440 | tf_op jit(solution)/shard_map/ppermute | solution.py:683
  50.0 2.2 %collective-permute-start.16 = (bf16[128,1024]{1,0:T(8,128)(2,1)S(1)}, bf16[128,1024]{1,0:T(8,128)(2,1)S(1)}, u32[]{:S(2)}, u32[]{:S(2)}) collective-permute-start(bf16[128,1024]{1,0:T(8,128)(2,1)S(1)} %get-tuple-element.90), channel_id=1, source_target_pairs={{0,3},{1,2},{2,1},{3,0},{4,7},{5,6},{6,5},{7,4},{8,11},{9,10},{10,... | collective-permute-start | bytes 786440 | tf_op jit(solution)/shard_map/ppermute | solution.py:683
  52.8 2.6 %state.5 = (bf16[512,768]{1,0:T(8,128)(2,1)S(1)}, f32[256,768]{1,0:T(8,128)S(1)}, bf16[272,384]{1,0:T(8,128)(2,1)S(1)}, bf16[272,384]{1,0:T(8,128)(2,1)S(1)}) custom-call(s32[5]{0:T(128)S(1)} %stack.23.place, bf16[128,768]{1,0:T(8,128)(2,1)S(1)} %get-tuple-element.72.refs_9_.refs_0_, bf16[128,768]{1,0:T(8,128)(2,1)S(1)} %collective-permute-done.12.refs_2_.refs_1_, ...), custom_call_target="tpu_custom_call" | custom-call | flops 1 | bytes 1 | tf_op jit(solution)/shard_map/state/pallas_call | solution.py:658
  55.4 3.5 %collective-permute-start.17 = (bf16[272,384]{1,0:T(8,128)(2,1)S(1)}, bf16[272,384]{1,0:T(8,128)(2,1)S(1)}, u32[]{:S(2)}, u32[]{:S(2)}) collective-permute-start(bf16[272,384]{1,0:T(8,128)(2,1)S(1)} %get-tuple-element.91.refs_1_), channel_id=1, source_target_pairs={{0,8},{1,9},{2,10},{3,11},{4,12},{5,13},{6,14},{7,15},{8,0},{9,1},... | collective-permute-start | bytes 626696 | tf_op jit(solution)/shard_map/ppermute | solution.py:683
  58.9 1.3 %collective-permute-start.18 = (bf16[272,384]{1,0:T(8,128)(2,1)S(1)}, bf16[272,384]{1,0:T(8,128)(2,1)S(1)}, u32[]{:S(2)}, u32[]{:S(2)}) collective-permute-start(bf16[272,384]{1,0:T(8,128)(2,1)S(1)} %get-tuple-element.92.refs_1_), channel_id=1, source_target_pairs={{0,8},{1,9},{2,10},{3,11},{4,12},{5,13},{6,14},{7,15},{8,0},{9,1},... | collective-permute-start | bytes 626696 | tf_op jit(solution)/shard_map/ppermute | solution.py:683
  60.2 1.3 %collective-permute-start.11 = (bf16[272,512]{1,0:T(8,128)(2,1)S(1)}, bf16[272,512]{1,0:T(8,128)(2,1)S(1)}, u32[]{:S(2)}, u32[]{:S(2)}) collective-permute-start(bf16[272,512]{1,0:T(8,128)(2,1)S(1)} %combine.5.refs_10_), channel_id=1, source_target_pairs={{0,16},{1,17},{2,18},{3,19},{4,20},{5,21},{6,22},{7,23},{8,24},{9,... | collective-permute-start | bytes 835592 | tf_op jit(solution)/shard_map/ppermute | solution.py:683
  62.2 1.3 %collective-permute-start.20 = (bf16[272,384]{1,0:T(8,128)(2,1)S(1)}, bf16[272,384]{1,0:T(8,128)(2,1)S(1)}, u32[]{:S(2)}, u32[]{:S(2)}) collective-permute-start(bf16[272,384]{1,0:T(8,128)(2,1)S(1)} %combine.6.refs_2_.refs_10_), channel_id=1, source_target_pairs={{0,16},{1,17},{2,18},{3,19},{4,20},{5,21},{6,22},{7,23},{8,24},{9,... | collective-permute-start | bytes 626696 | tf_op jit(solution)/shard_map/ppermute | solution.py:683
  63.5 2.4 %collective-permute-done.18.refs_0_.refs_1_ = bf16[272,384]{1,0:T(8,128)(2,1)S(1)} collective-permute-done((bf16[272,384]{1,0:T(8,128)(2,1)S(1)}, bf16[272,384]{1,0:T(8,128)(2,1)S(1)}, u32[]{:S(2)}, u32[]{:S(2)}) %collective-permute-start.18) | collective-permute-done | bytes 208928 | tf_op jit(solution)/shard_map/ppermute | solution.py:683
  66.6 1.3 %collective-permute-start.21 = (bf16[272,384]{1,0:T(8,128)(2,1)S(1)}, bf16[272,384]{1,0:T(8,128)(2,1)S(1)}, u32[]{:S(2)}, u32[]{:S(2)}) collective-permute-start(bf16[272,384]{1,0:T(8,128)(2,1)S(1)} %combine.7.refs_11_), channel_id=1, source_target_pairs={{0,16},{1,17},{2,18},{3,19},{4,20},{5,21},{6,22},{7,23},{8,24},{9,... | collective-permute-start | bytes 626696 | tf_op jit(solution)/shard_map/ppermute | solution.py:683
  67.9 5.7 %collective-permute-done.16.refs_2_ = bf16[128,1024]{1,0:T(8,128)(2,1)S(1)} collective-permute-done((bf16[128,1024]{1,0:T(8,128)(2,1)S(1)}, bf16[128,1024]{1,0:T(8,128)(2,1)S(1)}, u32[]{:S(2)}, u32[]{:S(2)}) %collective-permute-start.16) | collective-permute-done | bytes 262176 | tf_op jit(solution)/shard_map/ppermute | solution.py:683
  73.6 1.9 %state.6 = (bf16[512,384]{1,0:T(8,128)(2,1)S(1)}, f32[256,384]{1,0:T(8,128)S(1)}, bf16[272,384]{1,0:T(8,128)(2,1)S(1)}) custom-call(s32[5]{0:T(128)S(1)} %stack.23.place, bf16[128,1024]{1,0:T(8,128)(2,1)S(1)} %get-tuple-element.79.refs_4_.refs_0_, bf16[128,1024]{1,0:T(8,128)(2,1)S(1)} %collective-permute-done.15.refs_1_, ...), custom_call_target="tpu_custom_call" | custom-call | flops 1 | bytes 1 | tf_op jit(solution)/shard_map/state/pallas_call | solution.py:658
  75.5 3.4 %collective-permute-start.22 = (bf16[272,384]{1,0:T(8,128)(2,1)S(1)}, bf16[272,384]{1,0:T(8,128)(2,1)S(1)}, u32[]{:S(2)}, u32[]{:S(2)}) collective-permute-start(bf16[272,384]{1,0:T(8,128)(2,1)S(1)} %get-tuple-element.93.refs_8_.refs_1_), channel_id=1, source_target_pairs={{0,8},{1,9},{2,10},{3,11},{4,12},{5,13},{6,14},{7,15},{8,0},{9,1},... | collective-permute-start | bytes 626696 | tf_op jit(solution)/shard_map/ppermute | solution.py:683
  80.1 1.9 %state.7 = (bf16[512,384]{1,0:T(8,128)(2,1)S(1)}, f32[256,384]{1,0:T(8,128)S(1)}, bf16[272,384]{1,0:T(8,128)(2,1)S(1)}) custom-call(s32[5]{0:T(128)S(1)} %stack.23.place, bf16[128,1024]{1,0:T(8,128)(2,1)S(1)} %get-tuple-element.79.refs_4_.refs_0_, bf16[128,1024]{1,0:T(8,128)(2,1)S(1)} %collective-permute-done.15.refs_1_, ...), custom_call_target="tpu_custom_call" | custom-call | flops 1 | bytes 1 | tf_op jit(solution)/shard_map/state/pallas_call | solution.py:658
  82.0 1.5 %collective-permute-start.19 = (bf16[272,384]{1,0:T(8,128)(2,1)S(1)}, bf16[272,384]{1,0:T(8,128)(2,1)S(1)}, u32[]{:S(2)}, u32[]{:S(2)}) collective-permute-start(bf16[272,384]{1,0:T(8,128)(2,1)S(1)} %get-tuple-element.100.refs_0_.refs_1_), channel_id=1, source_target_pairs={{0,8},{1,9},{2,10},{3,11},{4,12},{5,13},{6,14},{7,15},{8,0},{9,1},... | collective-permute-start | bytes 626696 | tf_op jit(solution)/shard_map/ppermute | solution.py:683
  85.2 1.3 %collective-permute-start.23 = (bf16[272,384]{1,0:T(8,128)(2,1)S(1)}, bf16[272,384]{1,0:T(8,128)(2,1)S(1)}, u32[]{:S(2)}, u32[]{:S(2)}) collective-permute-start(bf16[272,384]{1,0:T(8,128)(2,1)S(1)} %combine.8.refs_12_), channel_id=1, source_target_pairs={{0,16},{1,17},{2,18},{3,19},{4,20},{5,21},{6,22},{7,23},{8,24},{9,... | collective-permute-start | bytes 626696 | tf_op jit(solution)/shard_map/ppermute | solution.py:683
  86.5 2.6 %final.4 = (bf16[256,768]{1,0:T(8,128)(2,1)S(1)}, bf16[256,768]{1,0:T(8,128)(2,1)S(1)}) custom-call(s32[5]{0:T(128)S(1)} %stack.23.place, bf16[272,384]{1,0:T(8,128)(2,1)S(1)} %collective-permute-done.17.refs_0_, bf16[272,384]{1,0:T(8,128)(2,1)S(1)} %collective-permute-done.18.refs_0_.refs_1_, bf16[272,384]{1,0:T(8,128)(2,1)S(1)} %collective-permute-done.20.refs_3_.refs_2_, ...), custom_call_target="tpu_custom_call" | custom-call | flops 1 | bytes 1 | tf_op jit(solution)/shard_map/final/pallas_call | solution.py:658
  89.8 1.3 %collective-permute-start.24 = (bf16[272,384]{1,0:T(8,128)(2,1)S(1)}, bf16[272,384]{1,0:T(8,128)(2,1)S(1)}, u32[]{:S(2)}, u32[]{:S(2)}) collective-permute-start(bf16[272,384]{1,0:T(8,128)(2,1)S(1)} %combine.9.refs_0_), channel_id=1, source_target_pairs={{0,16},{1,17},{2,18},{3,19},{4,20},{5,21},{6,22},{7,23},{8,24},{9,... | collective-permute-start | bytes 626696 | tf_op jit(solution)/shard_map/ppermute | solution.py:683
  98.7 1.7 %collective-permute-start.28 = (bf16[256,384]{1,0:T(8,128)(2,1)S(1)}, bf16[256,384]{1,0:T(8,128)(2,1)S(1)}, u32[]{:S(2)}, u32[]{:S(2)}) collective-permute-start(bf16[256,384]{1,0:T(8,128)(2,1)S(1)} %get-tuple-element.114), channel_id=1, source_target_pairs={{0,4},{1,5},{2,6},{3,7},{4,0},{5,1},{6,2},{7,3},{8,12},{9,13},{10,... | collective-permute-start | bytes 589832 | tf_op jit(solution)/shard_map/ppermute | solution.py:683
  101.5 1.9 %place.1 = bf16[256,4096]{1,0:T(8,128)(2,1)} custom-call(s32[5]{0:T(128)S(1)} %stack.23.place, bf16[256,512]{1,0:T(8,128)(2,1)S(1)} %get-tuple-element.106.refs_6_.refs_0_, bf16[256,768]{1,0:T(8,128)(2,1)S(1)} %get-tuple-element.105.refs_2_.refs_1_, bf16[256,384]{1,0:T(8,128)(2,1)S(1)} %get-tuple-element.108.refs_6_.refs_2_, ...), custom_call_target="tpu_custom_call" | custom-call | flops 1 | bytes 1 | tf_op jit(solution)/shard_map/place/pallas_call | solution.py:620
  (73 shorter events, 23.4 us)
Async XLA Ops:
  2.5 2.1 %collective-permute-start = (bf16[64,2048]{1,0:T(8,128)(2,1)S(1)}, bf16[64,2048]{1,0:T(8,128)(2,1)S(1)}, u32[]{:S(2)}, u32[]{:S(2)}) collective-permute-start(bf16[64,2048]{1,0:T(8,128)(2,1)S(1)} %pack_first.1.order), channel_id=1, source_target_pairs={{0,4},{1,5},{2,6},{3,7},{4,0},{5,1},{6,2},{7,3},{8,12},{9,13},{10,... | collective-permute-start | bytes 786440 | tf_op jit(solution)/shard_map/ppermute | solution.py:683
  4.6 3.5 %collective-permute-start.4 = (bf16[64,8448]{1,0:T(8,128)(2,1)S(1)}, bf16[64,8448]{1,0:T(8,128)(2,1)S(1)}, u32[]{:S(2)}, u32[]{:S(2)}) collective-permute-start(bf16[64,8448]{1,0:T(8,128)(2,1)S(1)} %gate.3), channel_id=1, source_target_pairs={{0,4},{1,5},{2,6},{3,7},{4,0},{5,1},{6,2},{7,3},{8,12},{9,13},{10,... | collective-permute-start | bytes 3244040 | tf_op jit(solution)/shard_map/ppermute | solution.py:683
  5.7 12.4 %collective-permute-start.1 = (bf16[128,512]{1,0:T(8,128)(2,1)S(1)}, bf16[128,512]{1,0:T(8,128)(2,1)S(1)}, u32[]{:S(2)}, u32[]{:S(2)}) collective-permute-start(bf16[128,512]{1,0:T(8,128)(2,1)S(1)} %get-tuple-element.61), channel_id=1, source_target_pairs={{0,2},{1,3},{2,0},{3,1},{4,6},{5,7},{6,4},{7,5},{8,10},{9,11},{10,... | collective-permute-start | bytes 393224 | tf_op jit(solution)/shard_map/ppermute | solution.py:683
  8.7 6.0 %collective-permute-start.5 = (bf16[3,10240]{1,0:T(4,128)(2,1)S(1)}, bf16[3,10240]{1,0:T(4,128)(2,1)S(1)}, u32[]{:S(2)}, u32[]{:S(2)}) collective-permute-start(bf16[3,10240]{1,0:T(4,128)(2,1)S(1)} %edge.1), channel_id=1, source_target_pairs={{3,11},{7,15},{11,19},{15,23},{19,27},{23,31}} | collective-permute-start | bytes 184328 | tf_op jit(solution)/shard_map/ppermute | solution.py:683
  9.4 11.6 %collective-permute-start.2 = (bf16[128,512]{1,0:T(8,128)(2,1)S(1)}, bf16[128,512]{1,0:T(8,128)(2,1)S(1)}, u32[]{:S(2)}, u32[]{:S(2)}) collective-permute-start(bf16[128,512]{1,0:T(8,128)(2,1)S(1)} %get-tuple-element.62), channel_id=1, source_target_pairs={{0,3},{1,2},{2,1},{3,0},{4,7},{5,6},{6,5},{7,4},{8,11},{9,10},{10,... | collective-permute-start | bytes 393224 | tf_op jit(solution)/shard_map/ppermute | solution.py:683
  10.0 11.0 %collective-permute-start.3 = (bf16[128,512]{1,0:T(8,128)(2,1)S(1)}, bf16[128,512]{1,0:T(8,128)(2,1)S(1)}, u32[]{:S(2)}, u32[]{:S(2)}) collective-permute-start(bf16[128,512]{1,0:T(8,128)(2,1)S(1)} %get-tuple-element.63), channel_id=1, source_target_pairs={{0,1},{1,0},{2,3},{3,2},{4,5},{5,4},{6,7},{7,6},{8,9},{9,8},{10,11... | collective-permute-start | bytes 393224 | tf_op jit(solution)/shard_map/ppermute | solution.py:683
  15.7 9.8 %collective-permute-start.6 = (bf16[128,384]{1,0:T(8,128)(2,1)S(1)}, bf16[128,384]{1,0:T(8,128)(2,1)S(1)}, u32[]{:S(2)}, u32[]{:S(2)}) collective-permute-start(bf16[128,384]{1,0:T(8,128)(2,1)S(1)} %get-tuple-element.69), channel_id=1, source_target_pairs={{0,2},{1,3},{2,0},{3,1},{4,6},{5,7},{6,4},{7,5},{8,10},{9,11},{10,... | collective-permute-start | bytes 294920 | tf_op jit(solution)/shard_map/ppermute | solution.py:683
  18.1 9.9 %collective-permute-start.7 = (bf16[128,384]{1,0:T(8,128)(2,1)S(1)}, bf16[128,384]{1,0:T(8,128)(2,1)S(1)}, u32[]{:S(2)}, u32[]{:S(2)}) collective-permute-start(bf16[128,384]{1,0:T(8,128)(2,1)S(1)} %get-tuple-element.70), channel_id=1, source_target_pairs={{0,3},{1,2},{2,1},{3,0},{4,7},{5,6},{6,5},{7,4},{8,11},{9,10},{10,... | collective-permute-start | bytes 294920 | tf_op jit(solution)/shard_map/ppermute | solution.py:683
  18.1 9.8 %collective-permute-start.8 = (bf16[128,384]{1,0:T(8,128)(2,1)S(1)}, bf16[128,384]{1,0:T(8,128)(2,1)S(1)}, u32[]{:S(2)}, u32[]{:S(2)}) collective-permute-start(bf16[128,384]{1,0:T(8,128)(2,1)S(1)} %get-tuple-element.71), channel_id=1, source_target_pairs={{0,1},{1,0},{2,3},{3,2},{4,5},{5,4},{6,7},{7,6},{8,9},{9,8},{10,11... | collective-permute-start | bytes 294920 | tf_op jit(solution)/shard_map/ppermute | solution.py:683
  20.9 10.4 %copy-start.5 = (f32[256]{0:T(256)S(1)}, f32[256]{0:T(256)}, u32[]{:S(2)}) copy-start(f32[256]{0:T(256)} %param.11) | copy-start | bytes 3076
  20.9 10.4 %copy-start.6 = (f32[256]{0:T(256)S(1)}, f32[256]{0:T(256)}, u32[]{:S(2)}) copy-start(f32[256]{0:T(256)} %param.12) | copy-start | bytes 3076
  20.9 10.4 %copy-start.7 = (f32[256]{0:T(256)S(1)}, f32[256]{0:T(256)}, u32[]{:S(2)}) copy-start(f32[256]{0:T(256)} %param.13) | copy-start | bytes 3076
  27.9 17.6 %collective-permute-start.14 = (bf16[128,1792]{1,0:T(8,128)(2,1)S(1)}, bf16[128,1792]{1,0:T(8,128)(2,1)S(1)}, u32[]{:S(2)}, u32[]{:S(2)}) collective-permute-start(bf16[128,1792]{1,0:T(8,128)(2,1)S(1)} %get-tuple-element.88), channel_id=1, source_target_pairs={{0,1},{1,0},{2,3},{3,2},{4,5},{5,4},{6,7},{7,6},{8,9},{9,8},{10,11... | collective-permute-start | bytes 1376264 | tf_op jit(solution)/shard_map/ppermute | solution.py:683
  27.9 17.6 %collective-permute-start.12 = (bf16[128,768]{1,0:T(8,128)(2,1)S(1)}, bf16[128,768]{1,0:T(8,128)(2,1)S(1)}, u32[]{:S(2)}, u32[]{:S(2)}) collective-permute-start(bf16[128,768]{1,0:T(8,128)(2,1)S(1)} %get-tuple-element.86), channel_id=1, source_target_pairs={{0,2},{1,3},{2,0},{3,1},{4,6},{5,7},{6,4},{7,5},{8,10},{9,11},{10,... | collective-permute-start | bytes 589832 | tf_op jit(solution)/shard_map/ppermute | solution.py:683
  31.3 14.2 %collective-permute-start.13 = (bf16[128,768]{1,0:T(8,128)(2,1)S(1)}, bf16[128,768]{1,0:T(8,128)(2,1)S(1)}, u32[]{:S(2)}, u32[]{:S(2)}) collective-permute-start(bf16[128,768]{1,0:T(8,128)(2,1)S(1)} %get-tuple-element.87), channel_id=1, source_target_pairs={{0,3},{1,2},{2,1},{3,0},{4,7},{5,6},{6,5},{7,4},{8,11},{9,10},{10,... | collective-permute-start | bytes 589832 | tf_op jit(solution)/shard_map/ppermute | solution.py:683
  35.1 17.0 %collective-permute-start.9 = (bf16[272,256]{1,0:T(8,128)(2,1)S(1)}, bf16[272,256]{1,0:T(8,128)(2,1)S(1)}, u32[]{:S(2)}, u32[]{:S(2)}) collective-permute-start(bf16[272,256]{1,0:T(8,128)(2,1)S(1)} %get-tuple-element.77.refs_0_.refs_2_), channel_id=1, source_target_pairs={{0,8},{1,9},{2,10},{3,11},{4,12},{5,13},{6,14},{7,15},{8,0},{9,1},... | collective-permute-start | bytes 417800 | tf_op jit(solution)/shard_map/ppermute | solution.py:683
  38.4 13.7 %collective-permute-start.10 = (bf16[272,256]{1,0:T(8,128)(2,1)S(1)}, bf16[272,256]{1,0:T(8,128)(2,1)S(1)}, u32[]{:S(2)}, u32[]{:S(2)}) collective-permute-start(bf16[272,256]{1,0:T(8,128)(2,1)S(1)} %get-tuple-element.78.refs_1_.refs_3_), channel_id=1, source_target_pairs={{0,8},{1,9},{2,10},{3,11},{4,12},{5,13},{6,14},{7,15},{8,0},{9,1},... | collective-permute-start | bytes 417800 | tf_op jit(solution)/shard_map/ppermute | solution.py:683
  45.6 22.3 %collective-permute-start.15 = (bf16[128,1024]{1,0:T(8,128)(2,1)S(1)}, bf16[128,1024]{1,0:T(8,128)(2,1)S(1)}, u32[]{:S(2)}, u32[]{:S(2)}) collective-permute-start(bf16[128,1024]{1,0:T(8,128)(2,1)S(1)} %get-tuple-element.89), channel_id=1, source_target_pairs={{0,2},{1,3},{2,0},{3,1},{4,6},{5,7},{6,4},{7,5},{8,10},{9,11},{10,... | collective-permute-start | bytes 786440 | tf_op jit(solution)/shard_map/ppermute | solution.py:683
  50.0 23.6 %collective-permute-start.16 = (bf16[128,1024]{1,0:T(8,128)(2,1)S(1)}, bf16[128,1024]{1,0:T(8,128)(2,1)S(1)}, u32[]{:S(2)}, u32[]{:S(2)}) collective-permute-start(bf16[128,1024]{1,0:T(8,128)(2,1)S(1)} %get-tuple-element.90), channel_id=1, source_target_pairs={{0,3},{1,2},{2,1},{3,0},{4,7},{5,6},{6,5},{7,4},{8,11},{9,10},{10,... | collective-permute-start | bytes 786440 | tf_op jit(solution)/shard_map/ppermute | solution.py:683
  55.4 6.2 %collective-permute-start.17 = (bf16[272,384]{1,0:T(8,128)(2,1)S(1)}, bf16[272,384]{1,0:T(8,128)(2,1)S(1)}, u32[]{:S(2)}, u32[]{:S(2)}) collective-permute-start(bf16[272,384]{1,0:T(8,128)(2,1)S(1)} %get-tuple-element.91.refs_1_), channel_id=1, source_target_pairs={{0,8},{1,9},{2,10},{3,11},{4,12},{5,13},{6,14},{7,15},{8,0},{9,1},... | collective-permute-start | bytes 626696 | tf_op jit(solution)/shard_map/ppermute | solution.py:683
  58.9 7.0 %collective-permute-start.18 = (bf16[272,384]{1,0:T(8,128)(2,1)S(1)}, bf16[272,384]{1,0:T(8,128)(2,1)S(1)}, u32[]{:S(2)}, u32[]{:S(2)}) collective-permute-start(bf16[272,384]{1,0:T(8,128)(2,1)S(1)} %get-tuple-element.92.refs_1_), channel_id=1, source_target_pairs={{0,8},{1,9},{2,10},{3,11},{4,12},{5,13},{6,14},{7,15},{8,0},{9,1},... | collective-permute-start | bytes 626696 | tf_op jit(solution)/shard_map/ppermute | solution.py:683
  60.2 24.4 %collective-permute-start.11 = (bf16[272,512]{1,0:T(8,128)(2,1)S(1)}, bf16[272,512]{1,0:T(8,128)(2,1)S(1)}, u32[]{:S(2)}, u32[]{:S(2)}) collective-permute-start(bf16[272,512]{1,0:T(8,128)(2,1)S(1)} %combine.5.refs_10_), channel_id=1, source_target_pairs={{0,16},{1,17},{2,18},{3,19},{4,20},{5,21},{6,22},{7,23},{8,24},{9,... | collective-permute-start | bytes 835592 | tf_op jit(solution)/shard_map/ppermute | solution.py:683
  62.2 22.3 %collective-permute-start.20 = (bf16[272,384]{1,0:T(8,128)(2,1)S(1)}, bf16[272,384]{1,0:T(8,128)(2,1)S(1)}, u32[]{:S(2)}, u32[]{:S(2)}) collective-permute-start(bf16[272,384]{1,0:T(8,128)(2,1)S(1)} %combine.6.refs_2_.refs_10_), channel_id=1, source_target_pairs={{0,16},{1,17},{2,18},{3,19},{4,20},{5,21},{6,22},{7,23},{8,24},{9,... | collective-permute-start | bytes 626696 | tf_op jit(solution)/shard_map/ppermute | solution.py:683
  66.6 18.0 %collective-permute-start.21 = (bf16[272,384]{1,0:T(8,128)(2,1)S(1)}, bf16[272,384]{1,0:T(8,128)(2,1)S(1)}, u32[]{:S(2)}, u32[]{:S(2)}) collective-permute-start(bf16[272,384]{1,0:T(8,128)(2,1)S(1)} %combine.7.refs_11_), channel_id=1, source_target_pairs={{0,16},{1,17},{2,18},{3,19},{4,20},{5,21},{6,22},{7,23},{8,24},{9,... | collective-permute-start | bytes 626696 | tf_op jit(solution)/shard_map/ppermute | solution.py:683
  75.5 9.1 %collective-permute-start.22 = (bf16[272,384]{1,0:T(8,128)(2,1)S(1)}, bf16[272,384]{1,0:T(8,128)(2,1)S(1)}, u32[]{:S(2)}, u32[]{:S(2)}) collective-permute-start(bf16[272,384]{1,0:T(8,128)(2,1)S(1)} %get-tuple-element.93.refs_8_.refs_1_), channel_id=1, source_target_pairs={{0,8},{1,9},{2,10},{3,11},{4,12},{5,13},{6,14},{7,15},{8,0},{9,1},... | collective-permute-start | bytes 626696 | tf_op jit(solution)/shard_map/ppermute | solution.py:683
  82.0 7.1 %collective-permute-start.19 = (bf16[272,384]{1,0:T(8,128)(2,1)S(1)}, bf16[272,384]{1,0:T(8,128)(2,1)S(1)}, u32[]{:S(2)}, u32[]{:S(2)}) collective-permute-start(bf16[272,384]{1,0:T(8,128)(2,1)S(1)} %get-tuple-element.100.refs_0_.refs_1_), channel_id=1, source_target_pairs={{0,8},{1,9},{2,10},{3,11},{4,12},{5,13},{6,14},{7,15},{8,0},{9,1},... | collective-permute-start | bytes 626696 | tf_op jit(solution)/shard_map/ppermute | solution.py:683
  85.2 9.4 %collective-permute-start.23 = (bf16[272,384]{1,0:T(8,128)(2,1)S(1)}, bf16[272,384]{1,0:T(8,128)(2,1)S(1)}, u32[]{:S(2)}, u32[]{:S(2)}) collective-permute-start(bf16[272,384]{1,0:T(8,128)(2,1)S(1)} %combine.8.refs_12_), channel_id=1, source_target_pairs={{0,16},{1,17},{2,18},{3,19},{4,20},{5,21},{6,22},{7,23},{8,24},{9,... | collective-permute-start | bytes 626696 | tf_op jit(solution)/shard_map/ppermute | solution.py:683
  89.8 7.8 %collective-permute-start.24 = (bf16[272,384]{1,0:T(8,128)(2,1)S(1)}, bf16[272,384]{1,0:T(8,128)(2,1)S(1)}, u32[]{:S(2)}, u32[]{:S(2)}) collective-permute-start(bf16[272,384]{1,0:T(8,128)(2,1)S(1)} %combine.9.refs_0_), channel_id=1, source_target_pairs={{0,16},{1,17},{2,18},{3,19},{4,20},{5,21},{6,22},{7,23},{8,24},{9,... | collective-permute-start | bytes 626696 | tf_op jit(solution)/shard_map/ppermute | solution.py:683
  91.1 9.3 %collective-permute-start.26 = (bf16[256,768]{1,0:T(8,128)(2,1)S(1)}, bf16[256,768]{1,0:T(8,128)(2,1)S(1)}, u32[]{:S(2)}, u32[]{:S(2)}) collective-permute-start(bf16[256,768]{1,0:T(8,128)(2,1)S(1)} %get-tuple-element.112), channel_id=1, source_target_pairs={{0,4},{1,5},{2,6},{3,7},{4,0},{5,1},{6,2},{7,3},{8,12},{9,13},{10,... | collective-permute-start | bytes 1179656 | tf_op jit(solution)/shard_map/ppermute | solution.py:683
  94.6 5.8 %collective-permute-start.25 = (bf16[256,512]{1,0:T(8,128)(2,1)S(1)}, bf16[256,512]{1,0:T(8,128)(2,1)S(1)}, u32[]{:S(2)}, u32[]{:S(2)}) collective-permute-start(bf16[256,512]{1,0:T(8,128)(2,1)S(1)} %get-tuple-element.111), channel_id=1, source_target_pairs={{0,4},{1,5},{2,6},{3,7},{4,0},{5,1},{6,2},{7,3},{8,12},{9,13},{10,... | collective-permute-start | bytes 786440 | tf_op jit(solution)/shard_map/ppermute | solution.py:683
  95.8 4.6 %collective-permute-start.27 = (bf16[256,384]{1,0:T(8,128)(2,1)S(1)}, bf16[256,384]{1,0:T(8,128)(2,1)S(1)}, u32[]{:S(2)}, u32[]{:S(2)}) collective-permute-start(bf16[256,384]{1,0:T(8,128)(2,1)S(1)} %get-tuple-element.113), channel_id=1, source_target_pairs={{0,4},{1,5},{2,6},{3,7},{4,0},{5,1},{6,2},{7,3},{8,12},{9,13},{10,... | collective-permute-start | bytes 589832 | tf_op jit(solution)/shard_map/ppermute | solution.py:683
  98.7 2.8 %collective-permute-start.28 = (bf16[256,384]{1,0:T(8,128)(2,1)S(1)}, bf16[256,384]{1,0:T(8,128)(2,1)S(1)}, u32[]{:S(2)}, u32[]{:S(2)}) collective-permute-start(bf16[256,384]{1,0:T(8,128)(2,1)S(1)} %get-tuple-element.114), channel_id=1, source_target_pairs={{0,4},{1,5},{2,6},{3,7},{4,0},{5,1},{6,2},{7,3},{8,12},{9,13},{10,... | collective-permute-start | bytes 589832 | tf_op jit(solution)/shard_map/ppermute | solution.py:683
  (5 other events, 14.3 us)

commit v24 on v23

--- a/solution.py
+++ b/solution.py
@@ -171,7 +171,6 @@
 
 
 FLIP = (0, 2, 3, 1)
-NEAR = 3
 
 
 def halves(value, count):
@@ -348,7 +347,7 @@
 
 
 def view(refs, piece):
-    return [(ref, total_of(2) if piece == 3 and r == NEAR else 0) for r, ref in enumerate(refs)]
+    return [(ref, 0) for ref in refs]
 
 
 def convolve_in_order(place, blocks, columns, edge, tap, bias, wide, put):
@@ -747,8 +746,7 @@
     edges = over(edges, lambda i: i + peers if i % shards == shards - 1 else None)
     second_blocks = send_on(plan(1), [first_blocks[0]], edges)
     message.append(travel(second_blocks))
-    third_plan = [(r, (2, 3) if r == NEAR else (2,)) for r in range(shards)]
-    third_blocks = send_on(third_plan, [second_blocks[0]])
+    third_blocks = send_on(plan(2), [second_blocks[0]])
     message.append(travel(third_blocks[:1] + gate(third_blocks[1:], message[0][1:] + message[1][1:] + [taps])))
 
     def seen(piece):
@@ -830,10 +828,8 @@
         )
 
     state_of(0, [])
-    own_block, *fourth_blocks = send_on([(r, (3,)) for r in range(shards) if r != NEAR], sent[0])
-    fourth_blocks = gate(fourth_blocks, message[2][1:])
-    fourth_blocks = [over(block, lambda i, r=r: i ^ FLIP[r]) for r, block in enumerate(fourth_blocks, 1)]
-    message.append([own_block, *fourth_blocks, message[2][NEAR]])
+    own_block, *fourth_blocks = send_on(plan(3), sent[0])
+    message.append(travel([own_block, *gate(fourth_blocks, message[2][1:])]))
     combine_of(0, [own_block])
     state_of(1, joined[0])
     combine_of(1, [])
@@ -852,7 +848,7 @@
         wide = [pltpu.VMEM((slab, GROUPED[i][2]), F32)]
         finish_of(finish_kernel, i, [x[i], cum, row, score, skip], order, scratch=wide)
 
-    combine_of(2, [partial[0]] + before[1] + before[0])
+    combine_of(2, [partial[0]] + before[1])
     in_full(1, joined[2])
     combine_of(3, [keep[1]])
     local_of(2, joined[3])

time: 104 us -> 106 us (1.019)
  waiting for transfers between devices: 22.6 us -> 25.1 us
  starting transfers between devices: 46.8 us -> 45.4 us
    ppermute x29 -> x30, waiting for transfers between devices: 22.6 us -> 25.1 us  [over(): lax.ppermute(block, axes, [(i, j) for i, j in route if j is not None and...]
    ppermute x29 -> x30, starting transfers between devices: 46.8 us -> 45.4 us  [over(): lax.ppermute(block, axes, [(i, j) for i, j in route if j is not None and...]
  transfers between devices with their start and end apart: 29 -> 30, of which waited for: 8 -> 9; matrix products, arithmetic and copies ran while one was open for 0% -> 0% of each run, Pallas kernels for 28% -> 28%
where the time goes in v24:
time: 106 us; the launch traced here: 105 us
  starting transfers between devices  45.4 us (43%)
  Pallas kernels  31.6 us (30%)
  waiting for transfers between devices  25.1 us (24%)
  local copies, waits for them, and re-layouts  2.06 us (2%)
    ppermute x30, starting transfers between devices, over(): lax.ppermute(block, axes, [(i, j) for i, j in route if j is not None and...  45.4 us
    pallas_call x26, Pallas kernels, call(): pl.pallas_call(body, out_shape=shapes, in_specs=specs, out_specs=[vmem] *...  29.6 us
    ppermute x30, waiting for transfers between devices, over(): lax.ppermute(block, axes, [(i, j) for i, j in route if j is not None and...  25.1 us
  transfers between devices with their start and end apart: 30, of which 9 were waited for; matrix products, arithmetic and copies ran while one was open for 0% of the time, Pallas kernels for 28%

profile of v24, /device:TPU:13, one launch (start us, length us, event | category | flops | bytes accessed | tf_op | source)
XLA Modules:
  0.0 104.6 jit_solution(13915208803688945388)
XLA Ops:
  0.1 1.7 %copy-done = bf16[64,20480]{1,0:T(8,128)(2,1)S(1)} copy-done((bf16[64,20480]{1,0:T(8,128)(2,1)S(1)}, bf16[64,20480]{1,0:T(8,128)(2,1)}, u32[]{:S(2)}) %copy-start) | copy-done | bytes 2621464
  3.2 1.3 %pack.1 = (bf16[64,8448]{1,0:T(8,128)(2,1)S(1)}, bf16[16,10240]{1,0:T(8,128)(2,1)S(1)}) custom-call(s32[5]{0:T(128)S(1)} %stack.23.place, bf16[64,20480]{1,0:T(8,128)(2,1)S(1)} %copy-done, bf16[64,256]{1,0:T(8,128)(2,1)S(1)} %copy-done.2, bf16[64,2048]{1,0:T(8,128)(2,1)S(1)} %pack_first.1.order), custom_call_target="tpu_custom_call" | custom-call | flops 1 | bytes 1 | tf_op jit(solution)/shard_map/pack/pallas_call | solution.py:657
  5.7 2.4 %collective-permute-start.1 = (bf16[128,512]{1,0:T(8,128)(2,1)S(1)}, bf16[128,512]{1,0:T(8,128)(2,1)S(1)}, u32[]{:S(2)}, u32[]{:S(2)}) collective-permute-start(bf16[128,512]{1,0:T(8,128)(2,1)S(1)} %get-tuple-element.63), channel_id=1, source_target_pairs={{0,2},{1,3},{2,0},{3,1},{4,6},{5,7},{6,4},{7,5},{8,10},{9,11},{10,... | collective-permute-start | bytes 393224 | tf_op jit(solution)/shard_map/ppermute | solution.py:682
  10.0 4.6 %collective-permute-start.3 = (bf16[128,512]{1,0:T(8,128)(2,1)S(1)}, bf16[128,512]{1,0:T(8,128)(2,1)S(1)}, u32[]{:S(2)}, u32[]{:S(2)}) collective-permute-start(bf16[128,512]{1,0:T(8,128)(2,1)S(1)} %get-tuple-element.65), channel_id=1, source_target_pairs={{0,1},{1,0},{2,3},{3,2},{4,5},{5,4},{6,7},{7,6},{8,9},{9,8},{10,11... | collective-permute-start | bytes 393224 | tf_op jit(solution)/shard_map/ppermute | solution.py:682
  15.7 2.4 %collective-permute-start.6 = (bf16[128,384]{1,0:T(8,128)(2,1)S(1)}, bf16[128,384]{1,0:T(8,128)(2,1)S(1)}, u32[]{:S(2)}, u32[]{:S(2)}) collective-permute-start(bf16[128,384]{1,0:T(8,128)(2,1)S(1)} %get-tuple-element.71), channel_id=1, source_target_pairs={{0,2},{1,3},{2,0},{3,1},{4,6},{5,7},{6,4},{7,5},{8,10},{9,11},{10,... | collective-permute-start | bytes 294920 | tf_op jit(solution)/shard_map/ppermute | solution.py:682
  20.9 4.6 %collective-permute-done.6.refs_1_.refs_6_ = bf16[128,384]{1,0:T(8,128)(2,1)S(1)} collective-permute-done((bf16[128,384]{1,0:T(8,128)(2,1)S(1)}, bf16[128,384]{1,0:T(8,128)(2,1)S(1)}, u32[]{:S(2)}, u32[]{:S(2)}) %collective-permute-start.6) | collective-permute-done | bytes 98336 | tf_op jit(solution)/shard_map/ppermute | solution.py:682
  25.5 2.5 %collective-permute-done.7.refs_2_.refs_7_ = bf16[128,384]{1,0:T(8,128)(2,1)S(1)} collective-permute-done((bf16[128,384]{1,0:T(8,128)(2,1)S(1)}, bf16[128,384]{1,0:T(8,128)(2,1)S(1)}, u32[]{:S(2)}, u32[]{:S(2)}) %collective-permute-start.7) | collective-permute-done | bytes 98336 | tf_op jit(solution)/shard_map/ppermute | solution.py:682
  31.5 1.7 %prep.1 = (bf16[512,256]{1,0:T(8,128)(2,1)S(1)}, f32[4,2560]{1,0:T(4,128)S(1)}, f32[512,128]{1,0:T(8,128)S(1)}, f32[128,512]{1,0:T(8,128)S(1)}, bf16[512,256]{1,...) custom-call(s32[5]{0:T(128)S(1)} %stack.23.place, ...), custom_call_target="tpu_custom_call" | custom-call | flops 1 | bytes 1 | tf_op jit(solution)/shard_map/prep/pallas_call | solution.py:657
  33.2 2.1 %state.4 = (bf16[512,512]{1,0:T(8,128)(2,1)S(1)}, f32[256,512]{1,0:T(8,128)S(1)}, bf16[272,256]{1,0:T(8,128)(2,1)S(1)}, bf16[272,256]{1,0:T(8,128)(2,1)S(1)}) custom-call(s32[5]{0:T(128)S(1)} %stack.23.place, bf16[128,512]{1,0:T(8,128)(2,1)S(1)} %get-tuple-element.62.refs_0_, bf16[128,512]{1,0:T(8,128)(2,1)S(1)} %collective-permute-done.1.refs_1_.refs_3_, ...), custom_call_target="tpu_custom_call" | custom-call | flops 1 | bytes 1 | tf_op jit(solution)/shard_map/state/pallas_call | solution.py:657
  35.2 3.3 %collective-permute-start.10 = (bf16[272,256]{1,0:T(8,128)(2,1)S(1)}, bf16[272,256]{1,0:T(8,128)(2,1)S(1)}, u32[]{:S(2)}, u32[]{:S(2)}) collective-permute-start(bf16[272,256]{1,0:T(8,128)(2,1)S(1)} %get-tuple-element.80.refs_1_.refs_3_), channel_id=1, source_target_pairs={{0,8},{1,9},{2,10},{3,11},{4,12},{5,13},{6,14},{7,15},{8,0},{9,1},... | collective-permute-start | bytes 417800 | tf_op jit(solution)/shard_map/ppermute | solution.py:682
  38.6 1.3 %collective-permute-start.9 = (bf16[272,256]{1,0:T(8,128)(2,1)S(1)}, bf16[272,256]{1,0:T(8,128)(2,1)S(1)}, u32[]{:S(2)}, u32[]{:S(2)}) collective-permute-start(bf16[272,256]{1,0:T(8,128)(2,1)S(1)} %get-tuple-element.79.refs_0_.refs_2_), channel_id=1, source_target_pairs={{0,8},{1,9},{2,10},{3,11},{4,12},{5,13},{6,14},{7,15},{8,0},{9,1},... | collective-permute-start | bytes 417800 | tf_op jit(solution)/shard_map/ppermute | solution.py:682
  40.8 7.2 %collective-permute-done.13.refs_4_.refs_2_ = bf16[128,768]{1,0:T(8,128)(2,1)S(1)} collective-permute-done((bf16[128,768]{1,0:T(8,128)(2,1)S(1)}, bf16[128,768]{1,0:T(8,128)(2,1)S(1)}, u32[]{:S(2)}, u32[]{:S(2)}) %collective-permute-start.13) | collective-permute-done | bytes 196640 | tf_op jit(solution)/shard_map/ppermute | solution.py:682
  48.1 3.5 %collective-permute-start.17 = (bf16[128,1024]{1,0:T(8,128)(2,1)S(1)}, bf16[128,1024]{1,0:T(8,128)(2,1)S(1)}, u32[]{:S(2)}, u32[]{:S(2)}) collective-permute-start(bf16[128,1024]{1,0:T(8,128)(2,1)S(1)} %get-tuple-element.94), channel_id=1, source_target_pairs={{0,1},{1,0},{2,3},{3,2},{4,5},{5,4},{6,7},{7,6},{8,9},{9,8},{10,11... | collective-permute-start | bytes 786440 | tf_op jit(solution)/shard_map/ppermute | solution.py:682
  52.3 2.6 %state.5 = (bf16[512,768]{1,0:T(8,128)(2,1)S(1)}, f32[256,768]{1,0:T(8,128)S(1)}, bf16[272,384]{1,0:T(8,128)(2,1)S(1)}, bf16[272,384]{1,0:T(8,128)(2,1)S(1)}) custom-call(s32[5]{0:T(128)S(1)} %stack.23.place, bf16[128,768]{1,0:T(8,128)(2,1)S(1)} %get-tuple-element.74.refs_9_.refs_0_, bf16[128,768]{1,0:T(8,128)(2,1)S(1)} %collective-permute-done.12.refs_3_.refs_1_, ...), custom_call_target="tpu_custom_call" | custom-call | flops 1 | bytes 1 | tf_op jit(solution)/shard_map/state/pallas_call | solution.py:657
  54.8 3.3 %collective-permute-start.18 = (bf16[272,384]{1,0:T(8,128)(2,1)S(1)}, bf16[272,384]{1,0:T(8,128)(2,1)S(1)}, u32[]{:S(2)}, u32[]{:S(2)}) collective-permute-start(bf16[272,384]{1,0:T(8,128)(2,1)S(1)} %get-tuple-element.95.refs_1_), channel_id=1, source_target_pairs={{0,8},{1,9},{2,10},{3,11},{4,12},{5,13},{6,14},{7,15},{8,0},{9,1},... | collective-permute-start | bytes 626696 | tf_op jit(solution)/shard_map/ppermute | solution.py:682
  58.2 1.3 %collective-permute-start.19 = (bf16[272,384]{1,0:T(8,128)(2,1)S(1)}, bf16[272,384]{1,0:T(8,128)(2,1)S(1)}, u32[]{:S(2)}, u32[]{:S(2)}) collective-permute-start(bf16[272,384]{1,0:T(8,128)(2,1)S(1)} %get-tuple-element.96.refs_1_), channel_id=1, source_target_pairs={{0,8},{1,9},{2,10},{3,11},{4,12},{5,13},{6,14},{7,15},{8,0},{9,1},... | collective-permute-start | bytes 626696 | tf_op jit(solution)/shard_map/ppermute | solution.py:682
  59.5 1.6 %collective-permute-done.18.refs_0_ = bf16[272,384]{1,0:T(8,128)(2,1)S(1)} collective-permute-done((bf16[272,384]{1,0:T(8,128)(2,1)S(1)}, bf16[272,384]{1,0:T(8,128)(2,1)S(1)}, u32[]{:S(2)}, u32[]{:S(2)}) %collective-permute-start.18) | collective-permute-done | bytes 208928 | tf_op jit(solution)/shard_map/ppermute | solution.py:682
  61.7 1.3 %collective-permute-start.21 = (bf16[272,384]{1,0:T(8,128)(2,1)S(1)}, bf16[272,384]{1,0:T(8,128)(2,1)S(1)}, u32[]{:S(2)}, u32[]{:S(2)}) collective-permute-start(bf16[272,384]{1,0:T(8,128)(2,1)S(1)} %combine.6.refs_2_.refs_10_), channel_id=1, source_target_pairs={{0,16},{1,17},{2,18},{3,19},{4,20},{5,21},{6,22},{7,23},{8,24},{9,... | collective-permute-start | bytes 626696 | tf_op jit(solution)/shard_map/ppermute | solution.py:682
  63.0 2.5 %collective-permute-done.19.refs_0_.refs_1_ = bf16[272,384]{1,0:T(8,128)(2,1)S(1)} collective-permute-done((bf16[272,384]{1,0:T(8,128)(2,1)S(1)}, bf16[272,384]{1,0:T(8,128)(2,1)S(1)}, u32[]{:S(2)}, u32[]{:S(2)}) %collective-permute-start.19) | collective-permute-done | bytes 208928 | tf_op jit(solution)/shard_map/ppermute | solution.py:682
  66.2 1.3 %collective-permute-start.22 = (bf16[272,384]{1,0:T(8,128)(2,1)S(1)}, bf16[272,384]{1,0:T(8,128)(2,1)S(1)}, u32[]{:S(2)}, u32[]{:S(2)}) collective-permute-start(bf16[272,384]{1,0:T(8,128)(2,1)S(1)} %combine.7.refs_11_), channel_id=1, source_target_pairs={{0,16},{1,17},{2,18},{3,19},{4,20},{5,21},{6,22},{7,23},{8,24},{9,... | collective-permute-start | bytes 626696 | tf_op jit(solution)/shard_map/ppermute | solution.py:682
  67.5 3.2 %collective-permute-done.16.refs_2_ = bf16[128,1024]{1,0:T(8,128)(2,1)S(1)} collective-permute-done((bf16[128,1024]{1,0:T(8,128)(2,1)S(1)}, bf16[128,1024]{1,0:T(8,128)(2,1)S(1)}, u32[]{:S(2)}, u32[]{:S(2)}) %collective-permute-start.16) | collective-permute-done | bytes 262176 | tf_op jit(solution)/shard_map/ppermute | solution.py:682
  70.8 1.9 %state.6 = (bf16[512,384]{1,0:T(8,128)(2,1)S(1)}, f32[256,384]{1,0:T(8,128)S(1)}, bf16[272,384]{1,0:T(8,128)(2,1)S(1)}) custom-call(s32[5]{0:T(128)S(1)} %stack.23.place, bf16[128,1024]{1,0:T(8,128)(2,1)S(1)} %get-tuple-element.81.refs_4_.refs_0_, bf16[128,1024]{1,0:T(8,128)(2,1)S(1)} %collective-permute-done.15.refs_1_, ...), custom_call_target="tpu_custom_call" | custom-call | flops 1 | bytes 1 | tf_op jit(solution)/shard_map/state/pallas_call | solution.py:657
  72.7 3.0 %collective-permute-start.23 = (bf16[272,384]{1,0:T(8,128)(2,1)S(1)}, bf16[272,384]{1,0:T(8,128)(2,1)S(1)}, u32[]{:S(2)}, u32[]{:S(2)}) collective-permute-start(bf16[272,384]{1,0:T(8,128)(2,1)S(1)} %get-tuple-element.97.refs_8_.refs_1_), channel_id=1, source_target_pairs={{0,8},{1,9},{2,10},{3,11},{4,12},{5,13},{6,14},{7,15},{8,0},{9,1},... | collective-permute-start | bytes 626696 | tf_op jit(solution)/shard_map/ppermute | solution.py:682
  76.8 1.9 %state.7 = (bf16[512,384]{1,0:T(8,128)(2,1)S(1)}, f32[256,384]{1,0:T(8,128)S(1)}, bf16[272,384]{1,0:T(8,128)(2,1)S(1)}) custom-call(s32[5]{0:T(128)S(1)} %stack.23.place, bf16[128,1024]{1,0:T(8,128)(2,1)S(1)} %get-tuple-element.81.refs_4_.refs_0_, bf16[128,1024]{1,0:T(8,128)(2,1)S(1)} %collective-permute-done.15.refs_1_, ...), custom_call_target="tpu_custom_call" | custom-call | flops 1 | bytes 1 | tf_op jit(solution)/shard_map/state/pallas_call | solution.py:657
  78.7 1.3 %collective-permute-start.20 = (bf16[272,384]{1,0:T(8,128)(2,1)S(1)}, bf16[272,384]{1,0:T(8,128)(2,1)S(1)}, u32[]{:S(2)}, u32[]{:S(2)}) collective-permute-start(bf16[272,384]{1,0:T(8,128)(2,1)S(1)} %get-tuple-element.104.refs_0_.refs_1_), channel_id=1, source_target_pairs={{0,8},{1,9},{2,10},{3,11},{4,12},{5,13},{6,14},{7,15},{8,0},{9,1},... | collective-permute-start | bytes 626696 | tf_op jit(solution)/shard_map/ppermute | solution.py:682
  80.1 1.5 %collective-permute-start.11 = (bf16[272,512]{1,0:T(8,128)(2,1)S(1)}, bf16[272,512]{1,0:T(8,128)(2,1)S(1)}, u32[]{:S(2)}, u32[]{:S(2)}) collective-permute-start(bf16[272,512]{1,0:T(8,128)(2,1)S(1)} %combine.5.refs_10_), channel_id=1, source_target_pairs={{0,16},{1,17},{2,18},{3,19},{4,20},{5,21},{6,22},{7,23},{8,24},{9,... | collective-permute-start | bytes 835592 | tf_op jit(solution)/shard_map/ppermute | solution.py:682
  84.5 2.6 %final.4 = (bf16[256,768]{1,0:T(8,128)(2,1)S(1)}, bf16[256,768]{1,0:T(8,128)(2,1)S(1)}) custom-call(s32[5]{0:T(128)S(1)} %stack.23.place, bf16[272,384]{1,0:T(8,128)(2,1)S(1)} %collective-permute-done.18.refs_0_, bf16[272,384]{1,0:T(8,128)(2,1)S(1)} %collective-permute-done.19.refs_0_.refs_1_, bf16[272,384]{1,0:T(8,128)(2,1)S(1)} %collective-permute-done.21.refs_3_.refs_2_, ...), custom_call_target="tpu_custom_call" | custom-call | flops 1 | bytes 1 | tf_op jit(solution)/shard_map/final/pallas_call | solution.py:657
  87.8 1.3 %collective-permute-start.25 = (bf16[272,384]{1,0:T(8,128)(2,1)S(1)}, bf16[272,384]{1,0:T(8,128)(2,1)S(1)}, u32[]{:S(2)}, u32[]{:S(2)}) collective-permute-start(bf16[272,384]{1,0:T(8,128)(2,1)S(1)} %combine.9.refs_0_), channel_id=1, source_target_pairs={{0,16},{1,17},{2,18},{3,19},{4,20},{5,21},{6,22},{7,23},{8,24},{9,... | collective-permute-start | bytes 626696 | tf_op jit(solution)/shard_map/ppermute | solution.py:682
  89.1 1.7 %collective-permute-start.27 = (bf16[256,768]{1,0:T(8,128)(2,1)S(1)}, bf16[256,768]{1,0:T(8,128)(2,1)S(1)}, u32[]{:S(2)}, u32[]{:S(2)}) collective-permute-start(bf16[256,768]{1,0:T(8,128)(2,1)S(1)} %get-tuple-element.116), channel_id=1, source_target_pairs={{0,4},{1,5},{2,6},{3,7},{4,0},{5,1},{6,2},{7,3},{8,12},{9,13},{10,... | collective-permute-start | bytes 1179656 | tf_op jit(solution)/shard_map/ppermute | solution.py:682
  95.4 2.0 %collective-permute-done.25.refs_1_ = bf16[272,384]{1,0:T(8,128)(2,1)S(1)} collective-permute-done((bf16[272,384]{1,0:T(8,128)(2,1)S(1)}, bf16[272,384]{1,0:T(8,128)(2,1)S(1)}, u32[]{:S(2)}, u32[]{:S(2)}) %collective-permute-start.25) | collective-permute-done | bytes 208928 | tf_op jit(solution)/shard_map/ppermute | solution.py:682
  98.5 2.6 %collective-permute-start.29 = (bf16[256,384]{1,0:T(8,128)(2,1)S(1)}, bf16[256,384]{1,0:T(8,128)(2,1)S(1)}, u32[]{:S(2)}, u32[]{:S(2)}) collective-permute-start(bf16[256,384]{1,0:T(8,128)(2,1)S(1)} %get-tuple-element.118), channel_id=1, source_target_pairs={{0,4},{1,5},{2,6},{3,7},{4,0},{5,1},{6,2},{7,3},{8,12},{9,13},{10,... | collective-permute-start | bytes 589832 | tf_op jit(solution)/shard_map/ppermute | solution.py:682
  102.6 1.9 %place.1 = bf16[256,4096]{1,0:T(8,128)(2,1)} custom-call(s32[5]{0:T(128)S(1)} %stack.23.place, bf16[256,512]{1,0:T(8,128)(2,1)S(1)} %get-tuple-element.110.refs_6_.refs_0_, bf16[256,768]{1,0:T(8,128)(2,1)S(1)} %get-tuple-element.109.refs_2_.refs_1_, bf16[256,384]{1,0:T(8,128)(2,1)S(1)} %get-tuple-element.112.refs_6_.refs_2_, ...), custom_call_target="tpu_custom_call" | custom-call | flops 1 | bytes 1 | tf_op jit(solution)/shard_map/place/pallas_call | solution.py:619
  (75 shorter events, 26.6 us)
Async XLA Ops:
  2.5 2.1 %collective-permute-start = (bf16[64,2048]{1,0:T(8,128)(2,1)S(1)}, bf16[64,2048]{1,0:T(8,128)(2,1)S(1)}, u32[]{:S(2)}, u32[]{:S(2)}) collective-permute-start(bf16[64,2048]{1,0:T(8,128)(2,1)S(1)} %pack_first.1.order), channel_id=1, source_target_pairs={{0,4},{1,5},{2,6},{3,7},{4,0},{5,1},{6,2},{7,3},{8,12},{9,13},{10,... | collective-permute-start | bytes 786440 | tf_op jit(solution)/shard_map/ppermute | solution.py:682
  4.6 3.5 %collective-permute-start.4 = (bf16[64,8448]{1,0:T(8,128)(2,1)S(1)}, bf16[64,8448]{1,0:T(8,128)(2,1)S(1)}, u32[]{:S(2)}, u32[]{:S(2)}) collective-permute-start(bf16[64,8448]{1,0:T(8,128)(2,1)S(1)} %gate.3), channel_id=1, source_target_pairs={{0,4},{1,5},{2,6},{3,7},{4,0},{5,1},{6,2},{7,3},{8,12},{9,13},{10,... | collective-permute-start | bytes 3244040 | tf_op jit(solution)/shard_map/ppermute | solution.py:682
  5.7 12.4 %collective-permute-start.1 = (bf16[128,512]{1,0:T(8,128)(2,1)S(1)}, bf16[128,512]{1,0:T(8,128)(2,1)S(1)}, u32[]{:S(2)}, u32[]{:S(2)}) collective-permute-start(bf16[128,512]{1,0:T(8,128)(2,1)S(1)} %get-tuple-element.63), channel_id=1, source_target_pairs={{0,2},{1,3},{2,0},{3,1},{4,6},{5,7},{6,4},{7,5},{8,10},{9,11},{10,... | collective-permute-start | bytes 393224 | tf_op jit(solution)/shard_map/ppermute | solution.py:682
  8.7 6.0 %collective-permute-start.5 = (bf16[3,10240]{1,0:T(4,128)(2,1)S(1)}, bf16[3,10240]{1,0:T(4,128)(2,1)S(1)}, u32[]{:S(2)}, u32[]{:S(2)}) collective-permute-start(bf16[3,10240]{1,0:T(4,128)(2,1)S(1)} %edge.1), channel_id=1, source_target_pairs={{3,11},{7,15},{11,19},{15,23},{19,27},{23,31}} | collective-permute-start | bytes 184328 | tf_op jit(solution)/shard_map/ppermute | solution.py:682
  9.4 11.5 %collective-permute-start.2 = (bf16[128,512]{1,0:T(8,128)(2,1)S(1)}, bf16[128,512]{1,0:T(8,128)(2,1)S(1)}, u32[]{:S(2)}, u32[]{:S(2)}) collective-permute-start(bf16[128,512]{1,0:T(8,128)(2,1)S(1)} %get-tuple-element.64), channel_id=1, source_target_pairs={{0,3},{1,2},{2,1},{3,0},{4,7},{5,6},{6,5},{7,4},{8,11},{9,10},{10,... | collective-permute-start | bytes 393224 | tf_op jit(solution)/shard_map/ppermute | solution.py:682
  10.0 10.9 %collective-permute-start.3 = (bf16[128,512]{1,0:T(8,128)(2,1)S(1)}, bf16[128,512]{1,0:T(8,128)(2,1)S(1)}, u32[]{:S(2)}, u32[]{:S(2)}) collective-permute-start(bf16[128,512]{1,0:T(8,128)(2,1)S(1)} %get-tuple-element.65), channel_id=1, source_target_pairs={{0,1},{1,0},{2,3},{3,2},{4,5},{5,4},{6,7},{7,6},{8,9},{9,8},{10,11... | collective-permute-start | bytes 393224 | tf_op jit(solution)/shard_map/ppermute | solution.py:682
  15.7 9.8 %collective-permute-start.6 = (bf16[128,384]{1,0:T(8,128)(2,1)S(1)}, bf16[128,384]{1,0:T(8,128)(2,1)S(1)}, u32[]{:S(2)}, u32[]{:S(2)}) collective-permute-start(bf16[128,384]{1,0:T(8,128)(2,1)S(1)} %get-tuple-element.71), channel_id=1, source_target_pairs={{0,2},{1,3},{2,0},{3,1},{4,6},{5,7},{6,4},{7,5},{8,10},{9,11},{10,... | collective-permute-start | bytes 294920 | tf_op jit(solution)/shard_map/ppermute | solution.py:682
  18.1 9.9 %collective-permute-start.7 = (bf16[128,384]{1,0:T(8,128)(2,1)S(1)}, bf16[128,384]{1,0:T(8,128)(2,1)S(1)}, u32[]{:S(2)}, u32[]{:S(2)}) collective-permute-start(bf16[128,384]{1,0:T(8,128)(2,1)S(1)} %get-tuple-element.72), channel_id=1, source_target_pairs={{0,3},{1,2},{2,1},{3,0},{4,7},{5,6},{6,5},{7,4},{8,11},{9,10},{10,... | collective-permute-start | bytes 294920 | tf_op jit(solution)/shard_map/ppermute | solution.py:682
  18.1 9.8 %collective-permute-start.8 = (bf16[128,384]{1,0:T(8,128)(2,1)S(1)}, bf16[128,384]{1,0:T(8,128)(2,1)S(1)}, u32[]{:S(2)}, u32[]{:S(2)}) collective-permute-start(bf16[128,384]{1,0:T(8,128)(2,1)S(1)} %get-tuple-element.73), channel_id=1, source_target_pairs={{0,1},{1,0},{2,3},{3,2},{4,5},{5,4},{6,7},{7,6},{8,9},{9,8},{10,11... | collective-permute-start | bytes 294920 | tf_op jit(solution)/shard_map/ppermute | solution.py:682
  20.8 10.7 %copy-start.5 = (f32[256]{0:T(256)S(1)}, f32[256]{0:T(256)}, u32[]{:S(2)}) copy-start(f32[256]{0:T(256)} %param.11) | copy-start | bytes 3076
  20.8 10.7 %copy-start.6 = (f32[256]{0:T(256)S(1)}, f32[256]{0:T(256)}, u32[]{:S(2)}) copy-start(f32[256]{0:T(256)} %param.12) | copy-start | bytes 3076
  27.9 12.9 %collective-permute-start.12 = (bf16[128,768]{1,0:T(8,128)(2,1)S(1)}, bf16[128,768]{1,0:T(8,128)(2,1)S(1)}, u32[]{:S(2)}, u32[]{:S(2)}) collective-permute-start(bf16[128,768]{1,0:T(8,128)(2,1)S(1)} %get-tuple-element.89), channel_id=1, source_target_pairs={{0,2},{1,3},{2,0},{3,1},{4,6},{5,7},{6,4},{7,5},{8,10},{9,11},{10,... | collective-permute-start | bytes 589832 | tf_op jit(solution)/shard_map/ppermute | solution.py:682
  29.0 19.0 %collective-permute-start.13 = (bf16[128,768]{1,0:T(8,128)(2,1)S(1)}, bf16[128,768]{1,0:T(8,128)(2,1)S(1)}, u32[]{:S(2)}, u32[]{:S(2)}) collective-permute-start(bf16[128,768]{1,0:T(8,128)(2,1)S(1)} %get-tuple-element.90), channel_id=1, source_target_pairs={{0,3},{1,2},{2,1},{3,0},{4,7},{5,6},{6,5},{7,4},{8,11},{9,10},{10,... | collective-permute-start | bytes 589832 | tf_op jit(solution)/shard_map/ppermute | solution.py:682
  30.2 17.8 %collective-permute-start.14 = (bf16[128,768]{1,0:T(8,128)(2,1)S(1)}, bf16[128,768]{1,0:T(8,128)(2,1)S(1)}, u32[]{:S(2)}, u32[]{:S(2)}) collective-permute-start(bf16[128,768]{1,0:T(8,128)(2,1)S(1)} %get-tuple-element.91), channel_id=1, source_target_pairs={{0,1},{1,0},{2,3},{3,2},{4,5},{5,4},{6,7},{7,6},{8,9},{9,8},{10,11... | collective-permute-start | bytes 589832 | tf_op jit(solution)/shard_map/ppermute | solution.py:682
  35.2 16.3 %collective-permute-start.10 = (bf16[272,256]{1,0:T(8,128)(2,1)S(1)}, bf16[272,256]{1,0:T(8,128)(2,1)S(1)}, u32[]{:S(2)}, u32[]{:S(2)}) collective-permute-start(bf16[272,256]{1,0:T(8,128)(2,1)S(1)} %get-tuple-element.80.refs_1_.refs_3_), channel_id=1, source_target_pairs={{0,8},{1,9},{2,10},{3,11},{4,12},{5,13},{6,14},{7,15},{8,0},{9,1},... | collective-permute-start | bytes 417800 | tf_op jit(solution)/shard_map/ppermute | solution.py:682
  38.6 13.0 %collective-permute-start.9 = (bf16[272,256]{1,0:T(8,128)(2,1)S(1)}, bf16[272,256]{1,0:T(8,128)(2,1)S(1)}, u32[]{:S(2)}, u32[]{:S(2)}) collective-permute-start(bf16[272,256]{1,0:T(8,128)(2,1)S(1)} %get-tuple-element.79.refs_0_.refs_2_), channel_id=1, source_target_pairs={{0,8},{1,9},{2,10},{3,11},{4,12},{5,13},{6,14},{7,15},{8,0},{9,1},... | collective-permute-start | bytes 417800 | tf_op jit(solution)/shard_map/ppermute | solution.py:682
  48.0 19.5 %collective-permute-start.15 = (bf16[128,1024]{1,0:T(8,128)(2,1)S(1)}, bf16[128,1024]{1,0:T(8,128)(2,1)S(1)}, u32[]{:S(2)}, u32[]{:S(2)}) collective-permute-start(bf16[128,1024]{1,0:T(8,128)(2,1)S(1)} %get-tuple-element.92), channel_id=1, source_target_pairs={{0,2},{1,3},{2,0},{3,1},{4,6},{5,7},{6,4},{7,5},{8,10},{9,11},{10,... | collective-permute-start | bytes 786440 | tf_op jit(solution)/shard_map/ppermute | solution.py:682
  48.0 22.7 %collective-permute-start.16 = (bf16[128,1024]{1,0:T(8,128)(2,1)S(1)}, bf16[128,1024]{1,0:T(8,128)(2,1)S(1)}, u32[]{:S(2)}, u32[]{:S(2)}) collective-permute-start(bf16[128,1024]{1,0:T(8,128)(2,1)S(1)} %get-tuple-element.93), channel_id=1, source_target_pairs={{0,3},{1,2},{2,1},{3,0},{4,7},{5,6},{6,5},{7,4},{8,11},{9,10},{10,... | collective-permute-start | bytes 786440 | tf_op jit(solution)/shard_map/ppermute | solution.py:682
  48.1 22.7 %collective-permute-start.17 = (bf16[128,1024]{1,0:T(8,128)(2,1)S(1)}, bf16[128,1024]{1,0:T(8,128)(2,1)S(1)}, u32[]{:S(2)}, u32[]{:S(2)}) collective-permute-start(bf16[128,1024]{1,0:T(8,128)(2,1)S(1)} %get-tuple-element.94), channel_id=1, source_target_pairs={{0,1},{1,0},{2,3},{3,2},{4,5},{5,4},{6,7},{7,6},{8,9},{9,8},{10,11... | collective-permute-start | bytes 786440 | tf_op jit(solution)/shard_map/ppermute | solution.py:682
  54.8 6.2 %collective-permute-start.18 = (bf16[272,384]{1,0:T(8,128)(2,1)S(1)}, bf16[272,384]{1,0:T(8,128)(2,1)S(1)}, u32[]{:S(2)}, u32[]{:S(2)}) collective-permute-start(bf16[272,384]{1,0:T(8,128)(2,1)S(1)} %get-tuple-element.95.refs_1_), channel_id=1, source_target_pairs={{0,8},{1,9},{2,10},{3,11},{4,12},{5,13},{6,14},{7,15},{8,0},{9,1},... | collective-permute-start | bytes 626696 | tf_op jit(solution)/shard_map/ppermute | solution.py:682
  58.2 7.4 %collective-permute-start.19 = (bf16[272,384]{1,0:T(8,128)(2,1)S(1)}, bf16[272,384]{1,0:T(8,128)(2,1)S(1)}, u32[]{:S(2)}, u32[]{:S(2)}) collective-permute-start(bf16[272,384]{1,0:T(8,128)(2,1)S(1)} %get-tuple-element.96.refs_1_), channel_id=1, source_target_pairs={{0,8},{1,9},{2,10},{3,11},{4,12},{5,13},{6,14},{7,15},{8,0},{9,1},... | collective-permute-start | bytes 626696 | tf_op jit(solution)/shard_map/ppermute | solution.py:682
  61.7 20.9 %collective-permute-start.21 = (bf16[272,384]{1,0:T(8,128)(2,1)S(1)}, bf16[272,384]{1,0:T(8,128)(2,1)S(1)}, u32[]{:S(2)}, u32[]{:S(2)}) collective-permute-start(bf16[272,384]{1,0:T(8,128)(2,1)S(1)} %combine.6.refs_2_.refs_10_), channel_id=1, source_target_pairs={{0,16},{1,17},{2,18},{3,19},{4,20},{5,21},{6,22},{7,23},{8,24},{9,... | collective-permute-start | bytes 626696 | tf_op jit(solution)/shard_map/ppermute | solution.py:682
  66.2 16.4 %collective-permute-start.22 = (bf16[272,384]{1,0:T(8,128)(2,1)S(1)}, bf16[272,384]{1,0:T(8,128)(2,1)S(1)}, u32[]{:S(2)}, u32[]{:S(2)}) collective-permute-start(bf16[272,384]{1,0:T(8,128)(2,1)S(1)} %combine.7.refs_11_), channel_id=1, source_target_pairs={{0,16},{1,17},{2,18},{3,19},{4,20},{5,21},{6,22},{7,23},{8,24},{9,... | collective-permute-start | bytes 626696 | tf_op jit(solution)/shard_map/ppermute | solution.py:682
  72.7 9.9 %collective-permute-start.23 = (bf16[272,384]{1,0:T(8,128)(2,1)S(1)}, bf16[272,384]{1,0:T(8,128)(2,1)S(1)}, u32[]{:S(2)}, u32[]{:S(2)}) collective-permute-start(bf16[272,384]{1,0:T(8,128)(2,1)S(1)} %get-tuple-element.97.refs_8_.refs_1_), channel_id=1, source_target_pairs={{0,8},{1,9},{2,10},{3,11},{4,12},{5,13},{6,14},{7,15},{8,0},{9,1},... | collective-permute-start | bytes 626696 | tf_op jit(solution)/shard_map/ppermute | solution.py:682
  78.7 8.4 %collective-permute-start.20 = (bf16[272,384]{1,0:T(8,128)(2,1)S(1)}, bf16[272,384]{1,0:T(8,128)(2,1)S(1)}, u32[]{:S(2)}, u32[]{:S(2)}) collective-permute-start(bf16[272,384]{1,0:T(8,128)(2,1)S(1)} %get-tuple-element.104.refs_0_.refs_1_), channel_id=1, source_target_pairs={{0,8},{1,9},{2,10},{3,11},{4,12},{5,13},{6,14},{7,15},{8,0},{9,1},... | collective-permute-start | bytes 626696 | tf_op jit(solution)/shard_map/ppermute | solution.py:682
  80.1 12.3 %collective-permute-start.11 = (bf16[272,512]{1,0:T(8,128)(2,1)S(1)}, bf16[272,512]{1,0:T(8,128)(2,1)S(1)}, u32[]{:S(2)}, u32[]{:S(2)}) collective-permute-start(bf16[272,512]{1,0:T(8,128)(2,1)S(1)} %combine.5.refs_10_), channel_id=1, source_target_pairs={{0,16},{1,17},{2,18},{3,19},{4,20},{5,21},{6,22},{7,23},{8,24},{9,... | collective-permute-start | bytes 835592 | tf_op jit(solution)/shard_map/ppermute | solution.py:682
  83.2 11.1 %collective-permute-start.24 = (bf16[272,384]{1,0:T(8,128)(2,1)S(1)}, bf16[272,384]{1,0:T(8,128)(2,1)S(1)}, u32[]{:S(2)}, u32[]{:S(2)}) collective-permute-start(bf16[272,384]{1,0:T(8,128)(2,1)S(1)} %combine.8.refs_12_), channel_id=1, source_target_pairs={{0,16},{1,17},{2,18},{3,19},{4,20},{5,21},{6,22},{7,23},{8,24},{9,... | collective-permute-start | bytes 626696 | tf_op jit(solution)/shard_map/ppermute | solution.py:682
  87.8 9.6 %collective-permute-start.25 = (bf16[272,384]{1,0:T(8,128)(2,1)S(1)}, bf16[272,384]{1,0:T(8,128)(2,1)S(1)}, u32[]{:S(2)}, u32[]{:S(2)}) collective-permute-start(bf16[272,384]{1,0:T(8,128)(2,1)S(1)} %combine.9.refs_0_), channel_id=1, source_target_pairs={{0,16},{1,17},{2,18},{3,19},{4,20},{5,21},{6,22},{7,23},{8,24},{9,... | collective-permute-start | bytes 626696 | tf_op jit(solution)/shard_map/ppermute | solution.py:682
  89.1 12.1 %collective-permute-start.27 = (bf16[256,768]{1,0:T(8,128)(2,1)S(1)}, bf16[256,768]{1,0:T(8,128)(2,1)S(1)}, u32[]{:S(2)}, u32[]{:S(2)}) collective-permute-start(bf16[256,768]{1,0:T(8,128)(2,1)S(1)} %get-tuple-element.116), channel_id=1, source_target_pairs={{0,4},{1,5},{2,6},{3,7},{4,0},{5,1},{6,2},{7,3},{8,12},{9,13},{10,... | collective-permute-start | bytes 1179656 | tf_op jit(solution)/shard_map/ppermute | solution.py:682
  93.5 7.7 %collective-permute-start.26 = (bf16[256,512]{1,0:T(8,128)(2,1)S(1)}, bf16[256,512]{1,0:T(8,128)(2,1)S(1)}, u32[]{:S(2)}, u32[]{:S(2)}) collective-permute-start(bf16[256,512]{1,0:T(8,128)(2,1)S(1)} %get-tuple-element.115), channel_id=1, source_target_pairs={{0,4},{1,5},{2,6},{3,7},{4,0},{5,1},{6,2},{7,3},{8,12},{9,13},{10,... | collective-permute-start | bytes 786440 | tf_op jit(solution)/shard_map/ppermute | solution.py:682
  98.5 3.7 %collective-permute-start.29 = (bf16[256,384]{1,0:T(8,128)(2,1)S(1)}, bf16[256,384]{1,0:T(8,128)(2,1)S(1)}, u32[]{:S(2)}, u32[]{:S(2)}) collective-permute-start(bf16[256,384]{1,0:T(8,128)(2,1)S(1)} %get-tuple-element.118), channel_id=1, source_target_pairs={{0,4},{1,5},{2,6},{3,7},{4,0},{5,1},{6,2},{7,3},{8,12},{9,13},{10,... | collective-permute-start | bytes 589832 | tf_op jit(solution)/shard_map/ppermute | solution.py:682
  101.1 1.4 %collective-permute-start.28 = (bf16[256,384]{1,0:T(8,128)(2,1)S(1)}, bf16[256,384]{1,0:T(8,128)(2,1)S(1)}, u32[]{:S(2)}, u32[]{:S(2)}) collective-permute-start(bf16[256,384]{1,0:T(8,128)(2,1)S(1)} %get-tuple-element.117), channel_id=1, source_target_pairs={{0,4},{1,5},{2,6},{3,7},{4,0},{5,1},{6,2},{7,3},{8,12},{9,13},{10,... | collective-permute-start | bytes 589832 | tf_op jit(solution)/shard_map/ppermute | solution.py:682
  (6 other events, 24.9 us)

commit v25 on v23

--- a/solution.py
+++ b/solution.py
@@ -838,15 +838,15 @@
     state_of(1, joined[0])
     combine_of(1, [])
     state_of(2, joined[1])
+    state_of(3, sent[2])
     c, score = call(
         functools.partial(score_kernel, shards),
         [((slab, STATE), BF16), ((slab, BLOCK), F32)],
-        [place] + seen(3) + [taps, offset, edge, b] + [Stay(o) for o in sent[2]],
+        [place] + seen(3) + [taps, offset, edge, b] + [Stay(o) for o in sent[3]],
         scratch=[pltpu.VMEM((slab + 8, STATE), F32)],
         name="score",
     )
-    state_of(3, [score])
-    local_of(0, sent[3])
+    local_of(0, [score])
 
     def in_full(i, order):
         wide = [pltpu.VMEM((slab, GROUPED[i][2]), F32)]

time: 104 us -> 104 us (level)
  transfers between devices with their start and end apart: 29 -> 29, of which waited for: 8 -> 9; matrix products, arithmetic and copies ran while one was open for 0% -> 0% of each run, Pallas kernels for 28% -> 28%
where the time goes in v25:
time: 104 us
  starting transfers between devices  46.3 us (45%)
  Pallas kernels  31.6 us (30%)
  waiting for transfers between devices  23.4 us (22%)
  local copies, waits for them, and re-layouts  2.06 us (2%)
    ppermute x29, starting transfers between devices, over(): lax.ppermute(block, axes, [(i, j) for i, j in route if j is not None and...  46.3 us
    pallas_call x26, Pallas kernels, call(): pl.pallas_call(body, out_shape=shapes, in_specs=specs, out_specs=[vmem] *...  29.7 us
    ppermute x29, waiting for transfers between devices, over(): lax.ppermute(block, axes, [(i, j) for i, j in route if j is not None and...  23.4 us
  transfers between devices with their start and end apart: 29, of which 9 were waited for; matrix products, arithmetic and copies ran while one was open for 0% of the time, Pallas kernels for 28%

profile of v25, /device:TPU:13, one launch (start us, length us, event | category | flops | bytes accessed | tf_op | source)
XLA Modules:
  0.0 103.9 jit_solution(1952700106239959262)
XLA Ops:
  0.1 1.7 %copy-done = bf16[64,20480]{1,0:T(8,128)(2,1)S(1)} copy-done((bf16[64,20480]{1,0:T(8,128)(2,1)S(1)}, bf16[64,20480]{1,0:T(8,128)(2,1)}, u32[]{:S(2)}) %copy-start) | copy-done | bytes 2621464
  3.2 1.3 %pack.1 = (bf16[64,8448]{1,0:T(8,128)(2,1)S(1)}, bf16[16,10240]{1,0:T(8,128)(2,1)S(1)}) custom-call(s32[5]{0:T(128)S(1)} %stack.23.place, bf16[64,20480]{1,0:T(8,128)(2,1)S(1)} %copy-done, bf16[64,256]{1,0:T(8,128)(2,1)S(1)} %copy-done.2, bf16[64,2048]{1,0:T(8,128)(2,1)S(1)} %pack_first.1.order), custom_call_target="tpu_custom_call" | custom-call | flops 1 | bytes 1 | tf_op jit(solution)/shard_map/pack/pallas_call | solution.py:658
  5.7 2.4 %collective-permute-start.1 = (bf16[128,512]{1,0:T(8,128)(2,1)S(1)}, bf16[128,512]{1,0:T(8,128)(2,1)S(1)}, u32[]{:S(2)}, u32[]{:S(2)}) collective-permute-start(bf16[128,512]{1,0:T(8,128)(2,1)S(1)} %get-tuple-element.61), channel_id=1, source_target_pairs={{0,2},{1,3},{2,0},{3,1},{4,6},{5,7},{6,4},{7,5},{8,10},{9,11},{10,... | collective-permute-start | bytes 393224 | tf_op jit(solution)/shard_map/ppermute | solution.py:683
  10.0 4.6 %collective-permute-start.3 = (bf16[128,512]{1,0:T(8,128)(2,1)S(1)}, bf16[128,512]{1,0:T(8,128)(2,1)S(1)}, u32[]{:S(2)}, u32[]{:S(2)}) collective-permute-start(bf16[128,512]{1,0:T(8,128)(2,1)S(1)} %get-tuple-element.63), channel_id=1, source_target_pairs={{0,1},{1,0},{2,3},{3,2},{4,5},{5,4},{6,7},{7,6},{8,9},{9,8},{10,11... | collective-permute-start | bytes 393224 | tf_op jit(solution)/shard_map/ppermute | solution.py:683
  15.7 2.4 %collective-permute-start.6 = (bf16[128,384]{1,0:T(8,128)(2,1)S(1)}, bf16[128,384]{1,0:T(8,128)(2,1)S(1)}, u32[]{:S(2)}, u32[]{:S(2)}) collective-permute-start(bf16[128,384]{1,0:T(8,128)(2,1)S(1)} %get-tuple-element.69), channel_id=1, source_target_pairs={{0,2},{1,3},{2,0},{3,1},{4,6},{5,7},{6,4},{7,5},{8,10},{9,11},{10,... | collective-permute-start | bytes 294920 | tf_op jit(solution)/shard_map/ppermute | solution.py:683
  21.0 4.5 %collective-permute-done.6.refs_1_.refs_6_ = bf16[128,384]{1,0:T(8,128)(2,1)S(1)} collective-permute-done((bf16[128,384]{1,0:T(8,128)(2,1)S(1)}, bf16[128,384]{1,0:T(8,128)(2,1)S(1)}, u32[]{:S(2)}, u32[]{:S(2)}) %collective-permute-start.6) | collective-permute-done | bytes 98336 | tf_op jit(solution)/shard_map/ppermute | solution.py:683
  25.5 2.5 %collective-permute-done.7.refs_2_.refs_7_ = bf16[128,384]{1,0:T(8,128)(2,1)S(1)} collective-permute-done((bf16[128,384]{1,0:T(8,128)(2,1)S(1)}, bf16[128,384]{1,0:T(8,128)(2,1)S(1)}, u32[]{:S(2)}, u32[]{:S(2)}) %collective-permute-start.7) | collective-permute-done | bytes 98336 | tf_op jit(solution)/shard_map/ppermute | solution.py:683
  27.9 3.4 %collective-permute-start.12 = (bf16[128,768]{1,0:T(8,128)(2,1)S(1)}, bf16[128,768]{1,0:T(8,128)(2,1)S(1)}, u32[]{:S(2)}, u32[]{:S(2)}) collective-permute-start(bf16[128,768]{1,0:T(8,128)(2,1)S(1)} %get-tuple-element.86), channel_id=1, source_target_pairs={{0,2},{1,3},{2,0},{3,1},{4,6},{5,7},{6,4},{7,5},{8,10},{9,11},{10,... | collective-permute-start | bytes 589832 | tf_op jit(solution)/shard_map/ppermute | solution.py:683
  31.3 1.7 %prep.1 = (bf16[512,256]{1,0:T(8,128)(2,1)S(1)}, f32[4,2560]{1,0:T(4,128)S(1)}, f32[512,128]{1,0:T(8,128)S(1)}, f32[128,512]{1,0:T(8,128)S(1)}, bf16[512,256]{1,...) custom-call(s32[5]{0:T(128)S(1)} %stack.23.place, ...), custom_call_target="tpu_custom_call" | custom-call | flops 1 | bytes 1 | tf_op jit(solution)/shard_map/prep/pallas_call | solution.py:658
  33.0 2.1 %state.4 = (bf16[512,512]{1,0:T(8,128)(2,1)S(1)}, f32[256,512]{1,0:T(8,128)S(1)}, bf16[272,256]{1,0:T(8,128)(2,1)S(1)}, bf16[272,256]{1,0:T(8,128)(2,1)S(1)}) custom-call(s32[5]{0:T(128)S(1)} %stack.23.place, bf16[128,512]{1,0:T(8,128)(2,1)S(1)} %get-tuple-element.60.refs_0_, bf16[128,512]{1,0:T(8,128)(2,1)S(1)} %collective-permute-done.1.refs_1_.refs_3_, ...), custom_call_target="tpu_custom_call" | custom-call | flops 1 | bytes 1 | tf_op jit(solution)/shard_map/state/pallas_call | solution.py:658
  35.1 3.3 %collective-permute-start.10 = (bf16[272,256]{1,0:T(8,128)(2,1)S(1)}, bf16[272,256]{1,0:T(8,128)(2,1)S(1)}, u32[]{:S(2)}, u32[]{:S(2)}) collective-permute-start(bf16[272,256]{1,0:T(8,128)(2,1)S(1)} %get-tuple-element.78.refs_1_.refs_3_), channel_id=1, source_target_pairs={{0,8},{1,9},{2,10},{3,11},{4,12},{5,13},{6,14},{7,15},{8,0},{9,1},... | collective-permute-start | bytes 417800 | tf_op jit(solution)/shard_map/ppermute | solution.py:683
  38.4 1.3 %collective-permute-start.9 = (bf16[272,256]{1,0:T(8,128)(2,1)S(1)}, bf16[272,256]{1,0:T(8,128)(2,1)S(1)}, u32[]{:S(2)}, u32[]{:S(2)}) collective-permute-start(bf16[272,256]{1,0:T(8,128)(2,1)S(1)} %get-tuple-element.77.refs_0_.refs_2_), channel_id=1, source_target_pairs={{0,8},{1,9},{2,10},{3,11},{4,12},{5,13},{6,14},{7,15},{8,0},{9,1},... | collective-permute-start | bytes 417800 | tf_op jit(solution)/shard_map/ppermute | solution.py:683
  40.5 5.0 %collective-permute-done.12.refs_2_.refs_1_ = bf16[128,768]{1,0:T(8,128)(2,1)S(1)} collective-permute-done((bf16[128,768]{1,0:T(8,128)(2,1)S(1)}, bf16[128,768]{1,0:T(8,128)(2,1)S(1)}, u32[]{:S(2)}, u32[]{:S(2)}) %collective-permute-start.12) | collective-permute-done | bytes 196640 | tf_op jit(solution)/shard_map/ppermute | solution.py:683
  45.6 4.4 %collective-permute-start.15 = (bf16[128,1024]{1,0:T(8,128)(2,1)S(1)}, bf16[128,1024]{1,0:T(8,128)(2,1)S(1)}, u32[]{:S(2)}, u32[]{:S(2)}) collective-permute-start(bf16[128,1024]{1,0:T(8,128)(2,1)S(1)} %get-tuple-element.89), channel_id=1, source_target_pairs={{0,2},{1,3},{2,0},{3,1},{4,6},{5,7},{6,4},{7,5},{8,10},{9,11},{10,... | collective-permute-start | bytes 786440 | tf_op jit(solution)/shard_map/ppermute | solution.py:683
  50.0 2.2 %collective-permute-start.16 = (bf16[128,1024]{1,0:T(8,128)(2,1)S(1)}, bf16[128,1024]{1,0:T(8,128)(2,1)S(1)}, u32[]{:S(2)}, u32[]{:S(2)}) collective-permute-start(bf16[128,1024]{1,0:T(8,128)(2,1)S(1)} %get-tuple-element.90), channel_id=1, source_target_pairs={{0,3},{1,2},{2,1},{3,0},{4,7},{5,6},{6,5},{7,4},{8,11},{9,10},{10,... | collective-permute-start | bytes 786440 | tf_op jit(solution)/shard_map/ppermute | solution.py:683
  52.8 2.6 %state.5 = (bf16[512,768]{1,0:T(8,128)(2,1)S(1)}, f32[256,768]{1,0:T(8,128)S(1)}, bf16[272,384]{1,0:T(8,128)(2,1)S(1)}, bf16[272,384]{1,0:T(8,128)(2,1)S(1)}) custom-call(s32[5]{0:T(128)S(1)} %stack.23.place, bf16[128,768]{1,0:T(8,128)(2,1)S(1)} %get-tuple-element.72.refs_9_.refs_0_, bf16[128,768]{1,0:T(8,128)(2,1)S(1)} %collective-permute-done.12.refs_2_.refs_1_, ...), custom_call_target="tpu_custom_call" | custom-call | flops 1 | bytes 1 | tf_op jit(solution)/shard_map/state/pallas_call | solution.py:658
  55.4 3.5 %collective-permute-start.17 = (bf16[272,384]{1,0:T(8,128)(2,1)S(1)}, bf16[272,384]{1,0:T(8,128)(2,1)S(1)}, u32[]{:S(2)}, u32[]{:S(2)}) collective-permute-start(bf16[272,384]{1,0:T(8,128)(2,1)S(1)} %get-tuple-element.91.refs_1_), channel_id=1, source_target_pairs={{0,8},{1,9},{2,10},{3,11},{4,12},{5,13},{6,14},{7,15},{8,0},{9,1},... | collective-permute-start | bytes 626696 | tf_op jit(solution)/shard_map/ppermute | solution.py:683
  58.9 1.3 %collective-permute-start.18 = (bf16[272,384]{1,0:T(8,128)(2,1)S(1)}, bf16[272,384]{1,0:T(8,128)(2,1)S(1)}, u32[]{:S(2)}, u32[]{:S(2)}) collective-permute-start(bf16[272,384]{1,0:T(8,128)(2,1)S(1)} %get-tuple-element.92.refs_1_), channel_id=1, source_target_pairs={{0,8},{1,9},{2,10},{3,11},{4,12},{5,13},{6,14},{7,15},{8,0},{9,1},... | collective-permute-start | bytes 626696 | tf_op jit(solution)/shard_map/ppermute | solution.py:683
  60.2 1.3 %collective-permute-start.11 = (bf16[272,512]{1,0:T(8,128)(2,1)S(1)}, bf16[272,512]{1,0:T(8,128)(2,1)S(1)}, u32[]{:S(2)}, u32[]{:S(2)}) collective-permute-start(bf16[272,512]{1,0:T(8,128)(2,1)S(1)} %combine.5.refs_10_), channel_id=1, source_target_pairs={{0,16},{1,17},{2,18},{3,19},{4,20},{5,21},{6,22},{7,23},{8,24},{9,... | collective-permute-start | bytes 835592 | tf_op jit(solution)/shard_map/ppermute | solution.py:683
  62.2 1.3 %collective-permute-start.20 = (bf16[272,384]{1,0:T(8,128)(2,1)S(1)}, bf16[272,384]{1,0:T(8,128)(2,1)S(1)}, u32[]{:S(2)}, u32[]{:S(2)}) collective-permute-start(bf16[272,384]{1,0:T(8,128)(2,1)S(1)} %combine.6.refs_2_.refs_10_), channel_id=1, source_target_pairs={{0,16},{1,17},{2,18},{3,19},{4,20},{5,21},{6,22},{7,23},{8,24},{9,... | collective-permute-start | bytes 626696 | tf_op jit(solution)/shard_map/ppermute | solution.py:683
  63.5 2.4 %collective-permute-done.18.refs_0_.refs_1_ = bf16[272,384]{1,0:T(8,128)(2,1)S(1)} collective-permute-done((bf16[272,384]{1,0:T(8,128)(2,1)S(1)}, bf16[272,384]{1,0:T(8,128)(2,1)S(1)}, u32[]{:S(2)}, u32[]{:S(2)}) %collective-permute-start.18) | collective-permute-done | bytes 208928 | tf_op jit(solution)/shard_map/ppermute | solution.py:683
  66.6 1.3 %collective-permute-start.21 = (bf16[272,384]{1,0:T(8,128)(2,1)S(1)}, bf16[272,384]{1,0:T(8,128)(2,1)S(1)}, u32[]{:S(2)}, u32[]{:S(2)}) collective-permute-start(bf16[272,384]{1,0:T(8,128)(2,1)S(1)} %combine.7.refs_11_), channel_id=1, source_target_pairs={{0,16},{1,17},{2,18},{3,19},{4,20},{5,21},{6,22},{7,23},{8,24},{9,... | collective-permute-start | bytes 626696 | tf_op jit(solution)/shard_map/ppermute | solution.py:683
  67.9 5.7 %collective-permute-done.16.refs_2_ = bf16[128,1024]{1,0:T(8,128)(2,1)S(1)} collective-permute-done((bf16[128,1024]{1,0:T(8,128)(2,1)S(1)}, bf16[128,1024]{1,0:T(8,128)(2,1)S(1)}, u32[]{:S(2)}, u32[]{:S(2)}) %collective-permute-start.16) | collective-permute-done | bytes 262176 | tf_op jit(solution)/shard_map/ppermute | solution.py:683
  73.6 1.9 %state.6 = (bf16[512,384]{1,0:T(8,128)(2,1)S(1)}, f32[256,384]{1,0:T(8,128)S(1)}, bf16[272,384]{1,0:T(8,128)(2,1)S(1)}) custom-call(s32[5]{0:T(128)S(1)} %stack.23.place, bf16[128,1024]{1,0:T(8,128)(2,1)S(1)} %get-tuple-element.79.refs_4_.refs_0_, bf16[128,1024]{1,0:T(8,128)(2,1)S(1)} %collective-permute-done.15.refs_1_, ...), custom_call_target="tpu_custom_call" | custom-call | flops 1 | bytes 1 | tf_op jit(solution)/shard_map/state/pallas_call | solution.py:658
  75.5 3.4 %collective-permute-start.22 = (bf16[272,384]{1,0:T(8,128)(2,1)S(1)}, bf16[272,384]{1,0:T(8,128)(2,1)S(1)}, u32[]{:S(2)}, u32[]{:S(2)}) collective-permute-start(bf16[272,384]{1,0:T(8,128)(2,1)S(1)} %get-tuple-element.93.refs_10_.refs_1_), channel_id=1, source_target_pairs={{0,8},{1,9},{2,10},{3,11},{4,12},{5,13},{6,14},{7,15},{8,0},{9,1},... | collective-permute-start | bytes 626696 | tf_op jit(solution)/shard_map/ppermute | solution.py:683
  79.0 1.9 %state.7 = (bf16[512,384]{1,0:T(8,128)(2,1)S(1)}, f32[256,384]{1,0:T(8,128)S(1)}, bf16[272,384]{1,0:T(8,128)(2,1)S(1)}) custom-call(s32[5]{0:T(128)S(1)} %stack.23.place, bf16[128,1024]{1,0:T(8,128)(2,1)S(1)} %get-tuple-element.79.refs_4_.refs_0_, bf16[128,1024]{1,0:T(8,128)(2,1)S(1)} %collective-permute-done.15.refs_1_, ...), custom_call_target="tpu_custom_call" | custom-call | flops 1 | bytes 1 | tf_op jit(solution)/shard_map/state/pallas_call | solution.py:658
  80.9 1.5 %collective-permute-start.19 = (bf16[272,384]{1,0:T(8,128)(2,1)S(1)}, bf16[272,384]{1,0:T(8,128)(2,1)S(1)}, u32[]{:S(2)}, u32[]{:S(2)}) collective-permute-start(bf16[272,384]{1,0:T(8,128)(2,1)S(1)} %get-tuple-element.94.refs_8_.refs_1_), channel_id=1, source_target_pairs={{0,8},{1,9},{2,10},{3,11},{4,12},{5,13},{6,14},{7,15},{8,0},{9,1},... | collective-permute-start | bytes 626696 | tf_op jit(solution)/shard_map/ppermute | solution.py:683
  85.2 1.3 %collective-permute-start.23 = (bf16[272,384]{1,0:T(8,128)(2,1)S(1)}, bf16[272,384]{1,0:T(8,128)(2,1)S(1)}, u32[]{:S(2)}, u32[]{:S(2)}) collective-permute-start(bf16[272,384]{1,0:T(8,128)(2,1)S(1)} %combine.8.refs_12_), channel_id=1, source_target_pairs={{0,16},{1,17},{2,18},{3,19},{4,20},{5,21},{6,22},{7,23},{8,24},{9,... | collective-permute-start | bytes 626696 | tf_op jit(solution)/shard_map/ppermute | solution.py:683
  86.5 2.6 %final.4 = (bf16[256,768]{1,0:T(8,128)(2,1)S(1)}, bf16[256,768]{1,0:T(8,128)(2,1)S(1)}) custom-call(s32[5]{0:T(128)S(1)} %stack.23.place, bf16[272,384]{1,0:T(8,128)(2,1)S(1)} %collective-permute-done.17.refs_0_, bf16[272,384]{1,0:T(8,128)(2,1)S(1)} %collective-permute-done.18.refs_0_.refs_1_, bf16[272,384]{1,0:T(8,128)(2,1)S(1)} %collective-permute-done.20.refs_3_.refs_2_, ...), custom_call_target="tpu_custom_call" | custom-call | flops 1 | bytes 1 | tf_op jit(solution)/shard_map/final/pallas_call | solution.py:658
  95.8 1.8 %collective-permute-done.24.refs_1_ = bf16[272,384]{1,0:T(8,128)(2,1)S(1)} collective-permute-done((bf16[272,384]{1,0:T(8,128)(2,1)S(1)}, bf16[272,384]{1,0:T(8,128)(2,1)S(1)}, u32[]{:S(2)}, u32[]{:S(2)}) %collective-permute-start.24) | collective-permute-done | bytes 208928 | tf_op jit(solution)/shard_map/ppermute | solution.py:683
  98.7 1.7 %collective-permute-start.28 = (bf16[256,384]{1,0:T(8,128)(2,1)S(1)}, bf16[256,384]{1,0:T(8,128)(2,1)S(1)}, u32[]{:S(2)}, u32[]{:S(2)}) collective-permute-start(bf16[256,384]{1,0:T(8,128)(2,1)S(1)} %get-tuple-element.114), channel_id=1, source_target_pairs={{0,4},{1,5},{2,6},{3,7},{4,0},{5,1},{6,2},{7,3},{8,12},{9,13},{10,... | collective-permute-start | bytes 589832 | tf_op jit(solution)/shard_map/ppermute | solution.py:683
  101.9 1.9 %place.1 = bf16[256,4096]{1,0:T(8,128)(2,1)} custom-call(s32[5]{0:T(128)S(1)} %stack.23.place, bf16[256,512]{1,0:T(8,128)(2,1)S(1)} %get-tuple-element.106.refs_6_.refs_0_, bf16[256,768]{1,0:T(8,128)(2,1)S(1)} %get-tuple-element.105.refs_2_.refs_1_, bf16[256,384]{1,0:T(8,128)(2,1)S(1)} %get-tuple-element.108.refs_6_.refs_2_, ...), custom_call_target="tpu_custom_call" | custom-call | flops 1 | bytes 1 | tf_op jit(solution)/shard_map/place/pallas_call | solution.py:620
  (73 shorter events, 23.2 us)
Async XLA Ops:
  2.5 2.1 %collective-permute-start = (bf16[64,2048]{1,0:T(8,128)(2,1)S(1)}, bf16[64,2048]{1,0:T(8,128)(2,1)S(1)}, u32[]{:S(2)}, u32[]{:S(2)}) collective-permute-start(bf16[64,2048]{1,0:T(8,128)(2,1)S(1)} %pack_first.1.order), channel_id=1, source_target_pairs={{0,4},{1,5},{2,6},{3,7},{4,0},{5,1},{6,2},{7,3},{8,12},{9,13},{10,... | collective-permute-start | bytes 786440 | tf_op jit(solution)/shard_map/ppermute | solution.py:683
  4.6 3.5 %collective-permute-start.4 = (bf16[64,8448]{1,0:T(8,128)(2,1)S(1)}, bf16[64,8448]{1,0:T(8,128)(2,1)S(1)}, u32[]{:S(2)}, u32[]{:S(2)}) collective-permute-start(bf16[64,8448]{1,0:T(8,128)(2,1)S(1)} %gate.3), channel_id=1, source_target_pairs={{0,4},{1,5},{2,6},{3,7},{4,0},{5,1},{6,2},{7,3},{8,12},{9,13},{10,... | collective-permute-start | bytes 3244040 | tf_op jit(solution)/shard_map/ppermute | solution.py:683
  5.7 12.4 %collective-permute-start.1 = (bf16[128,512]{1,0:T(8,128)(2,1)S(1)}, bf16[128,512]{1,0:T(8,128)(2,1)S(1)}, u32[]{:S(2)}, u32[]{:S(2)}) collective-permute-start(bf16[128,512]{1,0:T(8,128)(2,1)S(1)} %get-tuple-element.61), channel_id=1, source_target_pairs={{0,2},{1,3},{2,0},{3,1},{4,6},{5,7},{6,4},{7,5},{8,10},{9,11},{10,... | collective-permute-start | bytes 393224 | tf_op jit(solution)/shard_map/ppermute | solution.py:683
  8.7 6.0 %collective-permute-start.5 = (bf16[3,10240]{1,0:T(4,128)(2,1)S(1)}, bf16[3,10240]{1,0:T(4,128)(2,1)S(1)}, u32[]{:S(2)}, u32[]{:S(2)}) collective-permute-start(bf16[3,10240]{1,0:T(4,128)(2,1)S(1)} %edge.1), channel_id=1, source_target_pairs={{3,11},{7,15},{11,19},{15,23},{19,27},{23,31}} | collective-permute-start | bytes 184328 | tf_op jit(solution)/shard_map/ppermute | solution.py:683
  9.4 11.6 %collective-permute-start.2 = (bf16[128,512]{1,0:T(8,128)(2,1)S(1)}, bf16[128,512]{1,0:T(8,128)(2,1)S(1)}, u32[]{:S(2)}, u32[]{:S(2)}) collective-permute-start(bf16[128,512]{1,0:T(8,128)(2,1)S(1)} %get-tuple-element.62), channel_id=1, source_target_pairs={{0,3},{1,2},{2,1},{3,0},{4,7},{5,6},{6,5},{7,4},{8,11},{9,10},{10,... | collective-permute-start | bytes 393224 | tf_op jit(solution)/shard_map/ppermute | solution.py:683
  10.0 11.0 %collective-permute-start.3 = (bf16[128,512]{1,0:T(8,128)(2,1)S(1)}, bf16[128,512]{1,0:T(8,128)(2,1)S(1)}, u32[]{:S(2)}, u32[]{:S(2)}) collective-permute-start(bf16[128,512]{1,0:T(8,128)(2,1)S(1)} %get-tuple-element.63), channel_id=1, source_target_pairs={{0,1},{1,0},{2,3},{3,2},{4,5},{5,4},{6,7},{7,6},{8,9},{9,8},{10,11... | collective-permute-start | bytes 393224 | tf_op jit(solution)/shard_map/ppermute | solution.py:683
  15.7 9.8 %collective-permute-start.6 = (bf16[128,384]{1,0:T(8,128)(2,1)S(1)}, bf16[128,384]{1,0:T(8,128)(2,1)S(1)}, u32[]{:S(2)}, u32[]{:S(2)}) collective-permute-start(bf16[128,384]{1,0:T(8,128)(2,1)S(1)} %get-tuple-element.69), channel_id=1, source_target_pairs={{0,2},{1,3},{2,0},{3,1},{4,6},{5,7},{6,4},{7,5},{8,10},{9,11},{10,... | collective-permute-start | bytes 294920 | tf_op jit(solution)/shard_map/ppermute | solution.py:683
  18.1 9.9 %collective-permute-start.7 = (bf16[128,384]{1,0:T(8,128)(2,1)S(1)}, bf16[128,384]{1,0:T(8,128)(2,1)S(1)}, u32[]{:S(2)}, u32[]{:S(2)}) collective-permute-start(bf16[128,384]{1,0:T(8,128)(2,1)S(1)} %get-tuple-element.70), channel_id=1, source_target_pairs={{0,3},{1,2},{2,1},{3,0},{4,7},{5,6},{6,5},{7,4},{8,11},{9,10},{10,... | collective-permute-start | bytes 294920 | tf_op jit(solution)/shard_map/ppermute | solution.py:683
  18.1 9.8 %collective-permute-start.8 = (bf16[128,384]{1,0:T(8,128)(2,1)S(1)}, bf16[128,384]{1,0:T(8,128)(2,1)S(1)}, u32[]{:S(2)}, u32[]{:S(2)}) collective-permute-start(bf16[128,384]{1,0:T(8,128)(2,1)S(1)} %get-tuple-element.71), channel_id=1, source_target_pairs={{0,1},{1,0},{2,3},{3,2},{4,5},{5,4},{6,7},{7,6},{8,9},{9,8},{10,11... | collective-permute-start | bytes 294920 | tf_op jit(solution)/shard_map/ppermute | solution.py:683
  20.9 10.4 %copy-start.5 = (f32[256]{0:T(256)S(1)}, f32[256]{0:T(256)}, u32[]{:S(2)}) copy-start(f32[256]{0:T(256)} %param.11) | copy-start | bytes 3076
  20.9 10.4 %copy-start.6 = (f32[256]{0:T(256)S(1)}, f32[256]{0:T(256)}, u32[]{:S(2)}) copy-start(f32[256]{0:T(256)} %param.12) | copy-start | bytes 3076
  20.9 10.4 %copy-start.7 = (f32[256]{0:T(256)S(1)}, f32[256]{0:T(256)}, u32[]{:S(2)}) copy-start(f32[256]{0:T(256)} %param.13) | copy-start | bytes 3076
  27.9 17.6 %collective-permute-start.14 = (bf16[128,1792]{1,0:T(8,128)(2,1)S(1)}, bf16[128,1792]{1,0:T(8,128)(2,1)S(1)}, u32[]{:S(2)}, u32[]{:S(2)}) collective-permute-start(bf16[128,1792]{1,0:T(8,128)(2,1)S(1)} %get-tuple-element.88), channel_id=1, source_target_pairs={{0,1},{1,0},{2,3},{3,2},{4,5},{5,4},{6,7},{7,6},{8,9},{9,8},{10,11... | collective-permute-start | bytes 1376264 | tf_op jit(solution)/shard_map/ppermute | solution.py:683
  27.9 17.6 %collective-permute-start.12 = (bf16[128,768]{1,0:T(8,128)(2,1)S(1)}, bf16[128,768]{1,0:T(8,128)(2,1)S(1)}, u32[]{:S(2)}, u32[]{:S(2)}) collective-permute-start(bf16[128,768]{1,0:T(8,128)(2,1)S(1)} %get-tuple-element.86), channel_id=1, source_target_pairs={{0,2},{1,3},{2,0},{3,1},{4,6},{5,7},{6,4},{7,5},{8,10},{9,11},{10,... | collective-permute-start | bytes 589832 | tf_op jit(solution)/shard_map/ppermute | solution.py:683
  31.3 14.2 %collective-permute-start.13 = (bf16[128,768]{1,0:T(8,128)(2,1)S(1)}, bf16[128,768]{1,0:T(8,128)(2,1)S(1)}, u32[]{:S(2)}, u32[]{:S(2)}) collective-permute-start(bf16[128,768]{1,0:T(8,128)(2,1)S(1)} %get-tuple-element.87), channel_id=1, source_target_pairs={{0,3},{1,2},{2,1},{3,0},{4,7},{5,6},{6,5},{7,4},{8,11},{9,10},{10,... | collective-permute-start | bytes 589832 | tf_op jit(solution)/shard_map/ppermute | solution.py:683
  35.1 17.0 %collective-permute-start.10 = (bf16[272,256]{1,0:T(8,128)(2,1)S(1)}, bf16[272,256]{1,0:T(8,128)(2,1)S(1)}, u32[]{:S(2)}, u32[]{:S(2)}) collective-permute-start(bf16[272,256]{1,0:T(8,128)(2,1)S(1)} %get-tuple-element.78.refs_1_.refs_3_), channel_id=1, source_target_pairs={{0,8},{1,9},{2,10},{3,11},{4,12},{5,13},{6,14},{7,15},{8,0},{9,1},... | collective-permute-start | bytes 417800 | tf_op jit(solution)/shard_map/ppermute | solution.py:683
  38.4 13.7 %collective-permute-start.9 = (bf16[272,256]{1,0:T(8,128)(2,1)S(1)}, bf16[272,256]{1,0:T(8,128)(2,1)S(1)}, u32[]{:S(2)}, u32[]{:S(2)}) collective-permute-start(bf16[272,256]{1,0:T(8,128)(2,1)S(1)} %get-tuple-element.77.refs_0_.refs_2_), channel_id=1, source_target_pairs={{0,8},{1,9},{2,10},{3,11},{4,12},{5,13},{6,14},{7,15},{8,0},{9,1},... | collective-permute-start | bytes 417800 | tf_op jit(solution)/shard_map/ppermute | solution.py:683
  45.6 22.3 %collective-permute-start.15 = (bf16[128,1024]{1,0:T(8,128)(2,1)S(1)}, bf16[128,1024]{1,0:T(8,128)(2,1)S(1)}, u32[]{:S(2)}, u32[]{:S(2)}) collective-permute-start(bf16[128,1024]{1,0:T(8,128)(2,1)S(1)} %get-tuple-element.89), channel_id=1, source_target_pairs={{0,2},{1,3},{2,0},{3,1},{4,6},{5,7},{6,4},{7,5},{8,10},{9,11},{10,... | collective-permute-start | bytes 786440 | tf_op jit(solution)/shard_map/ppermute | solution.py:683
  50.0 23.6 %collective-permute-start.16 = (bf16[128,1024]{1,0:T(8,128)(2,1)S(1)}, bf16[128,1024]{1,0:T(8,128)(2,1)S(1)}, u32[]{:S(2)}, u32[]{:S(2)}) collective-permute-start(bf16[128,1024]{1,0:T(8,128)(2,1)S(1)} %get-tuple-element.90), channel_id=1, source_target_pairs={{0,3},{1,2},{2,1},{3,0},{4,7},{5,6},{6,5},{7,4},{8,11},{9,10},{10,... | collective-permute-start | bytes 786440 | tf_op jit(solution)/shard_map/ppermute | solution.py:683
  55.4 6.2 %collective-permute-start.17 = (bf16[272,384]{1,0:T(8,128)(2,1)S(1)}, bf16[272,384]{1,0:T(8,128)(2,1)S(1)}, u32[]{:S(2)}, u32[]{:S(2)}) collective-permute-start(bf16[272,384]{1,0:T(8,128)(2,1)S(1)} %get-tuple-element.91.refs_1_), channel_id=1, source_target_pairs={{0,8},{1,9},{2,10},{3,11},{4,12},{5,13},{6,14},{7,15},{8,0},{9,1},... | collective-permute-start | bytes 626696 | tf_op jit(solution)/shard_map/ppermute | solution.py:683
  58.9 7.0 %collective-permute-start.18 = (bf16[272,384]{1,0:T(8,128)(2,1)S(1)}, bf16[272,384]{1,0:T(8,128)(2,1)S(1)}, u32[]{:S(2)}, u32[]{:S(2)}) collective-permute-start(bf16[272,384]{1,0:T(8,128)(2,1)S(1)} %get-tuple-element.92.refs_1_), channel_id=1, source_target_pairs={{0,8},{1,9},{2,10},{3,11},{4,12},{5,13},{6,14},{7,15},{8,0},{9,1},... | collective-permute-start | bytes 626696 | tf_op jit(solution)/shard_map/ppermute | solution.py:683
  60.2 24.4 %collective-permute-start.11 = (bf16[272,512]{1,0:T(8,128)(2,1)S(1)}, bf16[272,512]{1,0:T(8,128)(2,1)S(1)}, u32[]{:S(2)}, u32[]{:S(2)}) collective-permute-start(bf16[272,512]{1,0:T(8,128)(2,1)S(1)} %combine.5.refs_10_), channel_id=1, source_target_pairs={{0,16},{1,17},{2,18},{3,19},{4,20},{5,21},{6,22},{7,23},{8,24},{9,... | collective-permute-start | bytes 835592 | tf_op jit(solution)/shard_map/ppermute | solution.py:683
  62.2 22.3 %collective-permute-start.20 = (bf16[272,384]{1,0:T(8,128)(2,1)S(1)}, bf16[272,384]{1,0:T(8,128)(2,1)S(1)}, u32[]{:S(2)}, u32[]{:S(2)}) collective-permute-start(bf16[272,384]{1,0:T(8,128)(2,1)S(1)} %combine.6.refs_2_.refs_10_), channel_id=1, source_target_pairs={{0,16},{1,17},{2,18},{3,19},{4,20},{5,21},{6,22},{7,23},{8,24},{9,... | collective-permute-start | bytes 626696 | tf_op jit(solution)/shard_map/ppermute | solution.py:683
  66.6 18.0 %collective-permute-start.21 = (bf16[272,384]{1,0:T(8,128)(2,1)S(1)}, bf16[272,384]{1,0:T(8,128)(2,1)S(1)}, u32[]{:S(2)}, u32[]{:S(2)}) collective-permute-start(bf16[272,384]{1,0:T(8,128)(2,1)S(1)} %combine.7.refs_11_), channel_id=1, source_target_pairs={{0,16},{1,17},{2,18},{3,19},{4,20},{5,21},{6,22},{7,23},{8,24},{9,... | collective-permute-start | bytes 626696 | tf_op jit(solution)/shard_map/ppermute | solution.py:683
  75.5 9.1 %collective-permute-start.22 = (bf16[272,384]{1,0:T(8,128)(2,1)S(1)}, bf16[272,384]{1,0:T(8,128)(2,1)S(1)}, u32[]{:S(2)}, u32[]{:S(2)}) collective-permute-start(bf16[272,384]{1,0:T(8,128)(2,1)S(1)} %get-tuple-element.93.refs_10_.refs_1_), channel_id=1, source_target_pairs={{0,8},{1,9},{2,10},{3,11},{4,12},{5,13},{6,14},{7,15},{8,0},{9,1},... | collective-permute-start | bytes 626696 | tf_op jit(solution)/shard_map/ppermute | solution.py:683
  80.9 8.3 %collective-permute-start.19 = (bf16[272,384]{1,0:T(8,128)(2,1)S(1)}, bf16[272,384]{1,0:T(8,128)(2,1)S(1)}, u32[]{:S(2)}, u32[]{:S(2)}) collective-permute-start(bf16[272,384]{1,0:T(8,128)(2,1)S(1)} %get-tuple-element.94.refs_8_.refs_1_), channel_id=1, source_target_pairs={{0,8},{1,9},{2,10},{3,11},{4,12},{5,13},{6,14},{7,15},{8,0},{9,1},... | collective-permute-start | bytes 626696 | tf_op jit(solution)/shard_map/ppermute | solution.py:683
  85.2 9.5 %collective-permute-start.23 = (bf16[272,384]{1,0:T(8,128)(2,1)S(1)}, bf16[272,384]{1,0:T(8,128)(2,1)S(1)}, u32[]{:S(2)}, u32[]{:S(2)}) collective-permute-start(bf16[272,384]{1,0:T(8,128)(2,1)S(1)} %combine.8.refs_12_), channel_id=1, source_target_pairs={{0,16},{1,17},{2,18},{3,19},{4,20},{5,21},{6,22},{7,23},{8,24},{9,... | collective-permute-start | bytes 626696 | tf_op jit(solution)/shard_map/ppermute | solution.py:683
  89.8 7.8 %collective-permute-start.24 = (bf16[272,384]{1,0:T(8,128)(2,1)S(1)}, bf16[272,384]{1,0:T(8,128)(2,1)S(1)}, u32[]{:S(2)}, u32[]{:S(2)}) collective-permute-start(bf16[272,384]{1,0:T(8,128)(2,1)S(1)} %combine.9.refs_0_), channel_id=1, source_target_pairs={{0,16},{1,17},{2,18},{3,19},{4,20},{5,21},{6,22},{7,23},{8,24},{9,... | collective-permute-start | bytes 626696 | tf_op jit(solution)/shard_map/ppermute | solution.py:683
  91.1 9.4 %collective-permute-start.26 = (bf16[256,768]{1,0:T(8,128)(2,1)S(1)}, bf16[256,768]{1,0:T(8,128)(2,1)S(1)}, u32[]{:S(2)}, u32[]{:S(2)}) collective-permute-start(bf16[256,768]{1,0:T(8,128)(2,1)S(1)} %get-tuple-element.112), channel_id=1, source_target_pairs={{0,4},{1,5},{2,6},{3,7},{4,0},{5,1},{6,2},{7,3},{8,12},{9,13},{10,... | collective-permute-start | bytes 1179656 | tf_op jit(solution)/shard_map/ppermute | solution.py:683
  94.7 5.8 %collective-permute-start.25 = (bf16[256,512]{1,0:T(8,128)(2,1)S(1)}, bf16[256,512]{1,0:T(8,128)(2,1)S(1)}, u32[]{:S(2)}, u32[]{:S(2)}) collective-permute-start(bf16[256,512]{1,0:T(8,128)(2,1)S(1)} %get-tuple-element.111), channel_id=1, source_target_pairs={{0,4},{1,5},{2,6},{3,7},{4,0},{5,1},{6,2},{7,3},{8,12},{9,13},{10,... | collective-permute-start | bytes 786440 | tf_op jit(solution)/shard_map/ppermute | solution.py:683
  98.7 2.8 %collective-permute-start.28 = (bf16[256,384]{1,0:T(8,128)(2,1)S(1)}, bf16[256,384]{1,0:T(8,128)(2,1)S(1)}, u32[]{:S(2)}, u32[]{:S(2)}) collective-permute-start(bf16[256,384]{1,0:T(8,128)(2,1)S(1)} %get-tuple-element.114), channel_id=1, source_target_pairs={{0,4},{1,5},{2,6},{3,7},{4,0},{5,1},{6,2},{7,3},{8,12},{9,13},{10,... | collective-permute-start | bytes 589832 | tf_op jit(solution)/shard_map/ppermute | solution.py:683
  100.4 1.4 %collective-permute-start.27 = (bf16[256,384]{1,0:T(8,128)(2,1)S(1)}, bf16[256,384]{1,0:T(8,128)(2,1)S(1)}, u32[]{:S(2)}, u32[]{:S(2)}) collective-permute-start(bf16[256,384]{1,0:T(8,128)(2,1)S(1)} %get-tuple-element.113), channel_id=1, source_target_pairs={{0,4},{1,5},{2,6},{3,7},{4,0},{5,1},{6,2},{7,3},{8,12},{9,13},{10,... | collective-permute-start | bytes 589832 | tf_op jit(solution)/shard_map/ppermute | solution.py:683
  (5 other events, 14.3 us)

commit v26 on v23

--- a/solution.py
+++ b/solution.py
@@ -831,7 +831,7 @@
 
     state_of(0, [])
     own_block, *fourth_blocks = send_on([(r, (3,)) for r in range(shards) if r != NEAR], sent[0])
-    fourth_blocks = gate(fourth_blocks, message[2][1:])
+    fourth_blocks = gate(fourth_blocks, message[2][1:NEAR])
     fourth_blocks = [over(block, lambda i, r=r: i ^ FLIP[r]) for r, block in enumerate(fourth_blocks, 1)]
     message.append([own_block, *fourth_blocks, message[2][NEAR]])
     combine_of(0, [own_block])

time: 104 us -> 104 us (level)
  no operation moved by 1% of the time
where the time goes in v26:
time: 104 us
  starting transfers between devices  46.8 us (45%)
  Pallas kernels  31.5 us (30%)
  waiting for transfers between devices  22.6 us (22%)
  local copies, waits for them, and re-layouts  2.06 us (2%)
    ppermute x29, starting transfers between devices, over(): lax.ppermute(block, axes, [(i, j) for i, j in route if j is not None and...  46.8 us
    pallas_call x26, Pallas kernels, call(): pl.pallas_call(body, out_shape=shapes, in_specs=specs, out_specs=[vmem] *...  29.6 us
    ppermute x29, waiting for transfers between devices, over(): lax.ppermute(block, axes, [(i, j) for i, j in route if j is not None and...  22.6 us
  transfers between devices with their start and end apart: 29, of which 8 were waited for; matrix products, arithmetic and copies ran while one was open for 0% of the time, Pallas kernels for 28%

profile of v26, /device:TPU:13, one launch (start us, length us, event | category | flops | bytes accessed | tf_op | source)
XLA Modules:
  0.0 103.5 jit_solution(17658315023797905846)
XLA Ops:
  0.1 1.7 %copy-done = bf16[64,20480]{1,0:T(8,128)(2,1)S(1)} copy-done((bf16[64,20480]{1,0:T(8,128)(2,1)S(1)}, bf16[64,20480]{1,0:T(8,128)(2,1)}, u32[]{:S(2)}) %copy-start) | copy-done | bytes 2621464
  3.2 1.3 %pack.1 = (bf16[64,8448]{1,0:T(8,128)(2,1)S(1)}, bf16[16,10240]{1,0:T(8,128)(2,1)S(1)}) custom-call(s32[5]{0:T(128)S(1)} %stack.23.place, bf16[64,20480]{1,0:T(8,128)(2,1)S(1)} %copy-done, bf16[64,256]{1,0:T(8,128)(2,1)S(1)} %copy-done.2, bf16[64,2048]{1,0:T(8,128)(2,1)S(1)} %pack_first.1.order), custom_call_target="tpu_custom_call" | custom-call | flops 1 | bytes 1 | tf_op jit(solution)/shard_map/pack/pallas_call | solution.py:658
  5.7 2.4 %collective-permute-start.1 = (bf16[128,512]{1,0:T(8,128)(2,1)S(1)}, bf16[128,512]{1,0:T(8,128)(2,1)S(1)}, u32[]{:S(2)}, u32[]{:S(2)}) collective-permute-start(bf16[128,512]{1,0:T(8,128)(2,1)S(1)} %get-tuple-element.61), channel_id=1, source_target_pairs={{0,2},{1,3},{2,0},{3,1},{4,6},{5,7},{6,4},{7,5},{8,10},{9,11},{10,... | collective-permute-start | bytes 393224 | tf_op jit(solution)/shard_map/ppermute | solution.py:683
  10.0 4.6 %collective-permute-start.3 = (bf16[128,512]{1,0:T(8,128)(2,1)S(1)}, bf16[128,512]{1,0:T(8,128)(2,1)S(1)}, u32[]{:S(2)}, u32[]{:S(2)}) collective-permute-start(bf16[128,512]{1,0:T(8,128)(2,1)S(1)} %get-tuple-element.63), channel_id=1, source_target_pairs={{0,1},{1,0},{2,3},{3,2},{4,5},{5,4},{6,7},{7,6},{8,9},{9,8},{10,11... | collective-permute-start | bytes 393224 | tf_op jit(solution)/shard_map/ppermute | solution.py:683
  15.7 2.4 %collective-permute-start.6 = (bf16[128,384]{1,0:T(8,128)(2,1)S(1)}, bf16[128,384]{1,0:T(8,128)(2,1)S(1)}, u32[]{:S(2)}, u32[]{:S(2)}) collective-permute-start(bf16[128,384]{1,0:T(8,128)(2,1)S(1)} %get-tuple-element.69), channel_id=1, source_target_pairs={{0,2},{1,3},{2,0},{3,1},{4,6},{5,7},{6,4},{7,5},{8,10},{9,11},{10,... | collective-permute-start | bytes 294920 | tf_op jit(solution)/shard_map/ppermute | solution.py:683
  21.0 4.5 %collective-permute-done.6.refs_1_.refs_6_ = bf16[128,384]{1,0:T(8,128)(2,1)S(1)} collective-permute-done((bf16[128,384]{1,0:T(8,128)(2,1)S(1)}, bf16[128,384]{1,0:T(8,128)(2,1)S(1)}, u32[]{:S(2)}, u32[]{:S(2)}) %collective-permute-start.6) | collective-permute-done | bytes 98336 | tf_op jit(solution)/shard_map/ppermute | solution.py:683
  25.5 2.5 %collective-permute-done.7.refs_2_.refs_7_ = bf16[128,384]{1,0:T(8,128)(2,1)S(1)} collective-permute-done((bf16[128,384]{1,0:T(8,128)(2,1)S(1)}, bf16[128,384]{1,0:T(8,128)(2,1)S(1)}, u32[]{:S(2)}, u32[]{:S(2)}) %collective-permute-start.7) | collective-permute-done | bytes 98336 | tf_op jit(solution)/shard_map/ppermute | solution.py:683
  27.9 3.4 %collective-permute-start.12 = (bf16[128,768]{1,0:T(8,128)(2,1)S(1)}, bf16[128,768]{1,0:T(8,128)(2,1)S(1)}, u32[]{:S(2)}, u32[]{:S(2)}) collective-permute-start(bf16[128,768]{1,0:T(8,128)(2,1)S(1)} %get-tuple-element.86), channel_id=1, source_target_pairs={{0,2},{1,3},{2,0},{3,1},{4,6},{5,7},{6,4},{7,5},{8,10},{9,11},{10,... | collective-permute-start | bytes 589832 | tf_op jit(solution)/shard_map/ppermute | solution.py:683
  31.3 1.7 %prep.1 = (bf16[512,256]{1,0:T(8,128)(2,1)S(1)}, f32[4,2560]{1,0:T(4,128)S(1)}, f32[512,128]{1,0:T(8,128)S(1)}, f32[128,512]{1,0:T(8,128)S(1)}, bf16[512,256]{1,...) custom-call(s32[5]{0:T(128)S(1)} %stack.23.place, ...), custom_call_target="tpu_custom_call" | custom-call | flops 1 | bytes 1 | tf_op jit(solution)/shard_map/prep/pallas_call | solution.py:658
  33.0 2.1 %state.4 = (bf16[512,512]{1,0:T(8,128)(2,1)S(1)}, f32[256,512]{1,0:T(8,128)S(1)}, bf16[272,256]{1,0:T(8,128)(2,1)S(1)}, bf16[272,256]{1,0:T(8,128)(2,1)S(1)}) custom-call(s32[5]{0:T(128)S(1)} %stack.23.place, bf16[128,512]{1,0:T(8,128)(2,1)S(1)} %get-tuple-element.60.refs_0_, bf16[128,512]{1,0:T(8,128)(2,1)S(1)} %collective-permute-done.1.refs_1_.refs_3_, ...), custom_call_target="tpu_custom_call" | custom-call | flops 1 | bytes 1 | tf_op jit(solution)/shard_map/state/pallas_call | solution.py:658
  35.1 3.3 %collective-permute-start.9 = (bf16[272,256]{1,0:T(8,128)(2,1)S(1)}, bf16[272,256]{1,0:T(8,128)(2,1)S(1)}, u32[]{:S(2)}, u32[]{:S(2)}) collective-permute-start(bf16[272,256]{1,0:T(8,128)(2,1)S(1)} %get-tuple-element.77.refs_0_.refs_2_), channel_id=1, source_target_pairs={{0,8},{1,9},{2,10},{3,11},{4,12},{5,13},{6,14},{7,15},{8,0},{9,1},... | collective-permute-start | bytes 417800 | tf_op jit(solution)/shard_map/ppermute | solution.py:683
  38.4 1.3 %collective-permute-start.10 = (bf16[272,256]{1,0:T(8,128)(2,1)S(1)}, bf16[272,256]{1,0:T(8,128)(2,1)S(1)}, u32[]{:S(2)}, u32[]{:S(2)}) collective-permute-start(bf16[272,256]{1,0:T(8,128)(2,1)S(1)} %get-tuple-element.78.refs_1_.refs_3_), channel_id=1, source_target_pairs={{0,8},{1,9},{2,10},{3,11},{4,12},{5,13},{6,14},{7,15},{8,0},{9,1},... | collective-permute-start | bytes 417800 | tf_op jit(solution)/shard_map/ppermute | solution.py:683
  40.5 5.0 %collective-permute-done.12.refs_2_.refs_1_ = bf16[128,768]{1,0:T(8,128)(2,1)S(1)} collective-permute-done((bf16[128,768]{1,0:T(8,128)(2,1)S(1)}, bf16[128,768]{1,0:T(8,128)(2,1)S(1)}, u32[]{:S(2)}, u32[]{:S(2)}) %collective-permute-start.12) | collective-permute-done | bytes 196640 | tf_op jit(solution)/shard_map/ppermute | solution.py:683
  45.6 4.4 %collective-permute-start.14 = (bf16[128,1024]{1,0:T(8,128)(2,1)S(1)}, bf16[128,1024]{1,0:T(8,128)(2,1)S(1)}, u32[]{:S(2)}, u32[]{:S(2)}) collective-permute-start(bf16[128,1024]{1,0:T(8,128)(2,1)S(1)} %get-tuple-element.88), channel_id=1, source_target_pairs={{0,2},{1,3},{2,0},{3,1},{4,6},{5,7},{6,4},{7,5},{8,10},{9,11},{10,... | collective-permute-start | bytes 786440 | tf_op jit(solution)/shard_map/ppermute | solution.py:683
  50.0 2.2 %collective-permute-start.15 = (bf16[128,1024]{1,0:T(8,128)(2,1)S(1)}, bf16[128,1024]{1,0:T(8,128)(2,1)S(1)}, u32[]{:S(2)}, u32[]{:S(2)}) collective-permute-start(bf16[128,1024]{1,0:T(8,128)(2,1)S(1)} %get-tuple-element.89), channel_id=1, source_target_pairs={{0,3},{1,2},{2,1},{3,0},{4,7},{5,6},{6,5},{7,4},{8,11},{9,10},{10,... | collective-permute-start | bytes 786440 | tf_op jit(solution)/shard_map/ppermute | solution.py:683
  52.8 2.6 %state.5 = (bf16[512,768]{1,0:T(8,128)(2,1)S(1)}, f32[256,768]{1,0:T(8,128)S(1)}, bf16[272,384]{1,0:T(8,128)(2,1)S(1)}, bf16[272,384]{1,0:T(8,128)(2,1)S(1)}) custom-call(s32[5]{0:T(128)S(1)} %stack.23.place, bf16[128,768]{1,0:T(8,128)(2,1)S(1)} %get-tuple-element.72.refs_9_.refs_0_, bf16[128,768]{1,0:T(8,128)(2,1)S(1)} %collective-permute-done.12.refs_2_.refs_1_, ...), custom_call_target="tpu_custom_call" | custom-call | flops 1 | bytes 1 | tf_op jit(solution)/shard_map/state/pallas_call | solution.py:658
  55.4 3.5 %collective-permute-start.17 = (bf16[272,384]{1,0:T(8,128)(2,1)S(1)}, bf16[272,384]{1,0:T(8,128)(2,1)S(1)}, u32[]{:S(2)}, u32[]{:S(2)}) collective-permute-start(bf16[272,384]{1,0:T(8,128)(2,1)S(1)} %get-tuple-element.91.refs_1_), channel_id=1, source_target_pairs={{0,8},{1,9},{2,10},{3,11},{4,12},{5,13},{6,14},{7,15},{8,0},{9,1},... | collective-permute-start | bytes 626696 | tf_op jit(solution)/shard_map/ppermute | solution.py:683
  58.9 1.3 %collective-permute-start.18 = (bf16[272,384]{1,0:T(8,128)(2,1)S(1)}, bf16[272,384]{1,0:T(8,128)(2,1)S(1)}, u32[]{:S(2)}, u32[]{:S(2)}) collective-permute-start(bf16[272,384]{1,0:T(8,128)(2,1)S(1)} %get-tuple-element.92.refs_1_), channel_id=1, source_target_pairs={{0,8},{1,9},{2,10},{3,11},{4,12},{5,13},{6,14},{7,15},{8,0},{9,1},... | collective-permute-start | bytes 626696 | tf_op jit(solution)/shard_map/ppermute | solution.py:683
  60.2 1.3 %collective-permute-start.11 = (bf16[272,512]{1,0:T(8,128)(2,1)S(1)}, bf16[272,512]{1,0:T(8,128)(2,1)S(1)}, u32[]{:S(2)}, u32[]{:S(2)}) collective-permute-start(bf16[272,512]{1,0:T(8,128)(2,1)S(1)} %combine.5.refs_10_), channel_id=1, source_target_pairs={{0,16},{1,17},{2,18},{3,19},{4,20},{5,21},{6,22},{7,23},{8,24},{9,... | collective-permute-start | bytes 835592 | tf_op jit(solution)/shard_map/ppermute | solution.py:683
  62.2 1.3 %collective-permute-start.20 = (bf16[272,384]{1,0:T(8,128)(2,1)S(1)}, bf16[272,384]{1,0:T(8,128)(2,1)S(1)}, u32[]{:S(2)}, u32[]{:S(2)}) collective-permute-start(bf16[272,384]{1,0:T(8,128)(2,1)S(1)} %combine.6.refs_2_.refs_10_), channel_id=1, source_target_pairs={{0,16},{1,17},{2,18},{3,19},{4,20},{5,21},{6,22},{7,23},{8,24},{9,... | collective-permute-start | bytes 626696 | tf_op jit(solution)/shard_map/ppermute | solution.py:683
  63.5 2.4 %collective-permute-done.18.refs_0_.refs_1_ = bf16[272,384]{1,0:T(8,128)(2,1)S(1)} collective-permute-done((bf16[272,384]{1,0:T(8,128)(2,1)S(1)}, bf16[272,384]{1,0:T(8,128)(2,1)S(1)}, u32[]{:S(2)}, u32[]{:S(2)}) %collective-permute-start.18) | collective-permute-done | bytes 208928 | tf_op jit(solution)/shard_map/ppermute | solution.py:683
  66.6 1.3 %collective-permute-start.21 = (bf16[272,384]{1,0:T(8,128)(2,1)S(1)}, bf16[272,384]{1,0:T(8,128)(2,1)S(1)}, u32[]{:S(2)}, u32[]{:S(2)}) collective-permute-start(bf16[272,384]{1,0:T(8,128)(2,1)S(1)} %combine.7.refs_11_), channel_id=1, source_target_pairs={{0,16},{1,17},{2,18},{3,19},{4,20},{5,21},{6,22},{7,23},{8,24},{9,... | collective-permute-start | bytes 626696 | tf_op jit(solution)/shard_map/ppermute | solution.py:683
  67.9 5.7 %collective-permute-done.15.refs_2_ = bf16[128,1024]{1,0:T(8,128)(2,1)S(1)} collective-permute-done((bf16[128,1024]{1,0:T(8,128)(2,1)S(1)}, bf16[128,1024]{1,0:T(8,128)(2,1)S(1)}, u32[]{:S(2)}, u32[]{:S(2)}) %collective-permute-start.15) | collective-permute-done | bytes 262176 | tf_op jit(solution)/shard_map/ppermute | solution.py:683
  73.6 1.9 %state.6 = (bf16[512,384]{1,0:T(8,128)(2,1)S(1)}, f32[256,384]{1,0:T(8,128)S(1)}, bf16[272,384]{1,0:T(8,128)(2,1)S(1)}) custom-call(s32[5]{0:T(128)S(1)} %stack.23.place, bf16[128,1024]{1,0:T(8,128)(2,1)S(1)} %get-tuple-element.79.refs_4_.refs_0_, bf16[128,1024]{1,0:T(8,128)(2,1)S(1)} %collective-permute-done.14.refs_1_, ...), custom_call_target="tpu_custom_call" | custom-call | flops 1 | bytes 1 | tf_op jit(solution)/shard_map/state/pallas_call | solution.py:658
  75.5 3.4 %collective-permute-start.22 = (bf16[272,384]{1,0:T(8,128)(2,1)S(1)}, bf16[272,384]{1,0:T(8,128)(2,1)S(1)}, u32[]{:S(2)}, u32[]{:S(2)}) collective-permute-start(bf16[272,384]{1,0:T(8,128)(2,1)S(1)} %get-tuple-element.93.refs_8_.refs_1_), channel_id=1, source_target_pairs={{0,8},{1,9},{2,10},{3,11},{4,12},{5,13},{6,14},{7,15},{8,0},{9,1},... | collective-permute-start | bytes 626696 | tf_op jit(solution)/shard_map/ppermute | solution.py:683
  80.1 1.9 %state.7 = (bf16[512,384]{1,0:T(8,128)(2,1)S(1)}, f32[256,384]{1,0:T(8,128)S(1)}, bf16[272,384]{1,0:T(8,128)(2,1)S(1)}) custom-call(s32[5]{0:T(128)S(1)} %stack.23.place, bf16[128,1024]{1,0:T(8,128)(2,1)S(1)} %get-tuple-element.79.refs_4_.refs_0_, bf16[128,1024]{1,0:T(8,128)(2,1)S(1)} %collective-permute-done.14.refs_1_, ...), custom_call_target="tpu_custom_call" | custom-call | flops 1 | bytes 1 | tf_op jit(solution)/shard_map/state/pallas_call | solution.py:658
  82.0 1.5 %collective-permute-start.19 = (bf16[272,384]{1,0:T(8,128)(2,1)S(1)}, bf16[272,384]{1,0:T(8,128)(2,1)S(1)}, u32[]{:S(2)}, u32[]{:S(2)}) collective-permute-start(bf16[272,384]{1,0:T(8,128)(2,1)S(1)} %get-tuple-element.100.refs_0_.refs_1_), channel_id=1, source_target_pairs={{0,8},{1,9},{2,10},{3,11},{4,12},{5,13},{6,14},{7,15},{8,0},{9,1},... | collective-permute-start | bytes 626696 | tf_op jit(solution)/shard_map/ppermute | solution.py:683
  85.2 1.3 %collective-permute-start.23 = (bf16[272,384]{1,0:T(8,128)(2,1)S(1)}, bf16[272,384]{1,0:T(8,128)(2,1)S(1)}, u32[]{:S(2)}, u32[]{:S(2)}) collective-permute-start(bf16[272,384]{1,0:T(8,128)(2,1)S(1)} %combine.8.refs_12_), channel_id=1, source_target_pairs={{0,16},{1,17},{2,18},{3,19},{4,20},{5,21},{6,22},{7,23},{8,24},{9,... | collective-permute-start | bytes 626696 | tf_op jit(solution)/shard_map/ppermute | solution.py:683
  86.5 2.6 %final.4 = (bf16[256,768]{1,0:T(8,128)(2,1)S(1)}, bf16[256,768]{1,0:T(8,128)(2,1)S(1)}) custom-call(s32[5]{0:T(128)S(1)} %stack.23.place, bf16[272,384]{1,0:T(8,128)(2,1)S(1)} %collective-permute-done.17.refs_0_, bf16[272,384]{1,0:T(8,128)(2,1)S(1)} %collective-permute-done.18.refs_0_.refs_1_, bf16[272,384]{1,0:T(8,128)(2,1)S(1)} %collective-permute-done.20.refs_3_.refs_2_, ...), custom_call_target="tpu_custom_call" | custom-call | flops 1 | bytes 1 | tf_op jit(solution)/shard_map/final/pallas_call | solution.py:658
  89.8 1.3 %collective-permute-start.24 = (bf16[272,384]{1,0:T(8,128)(2,1)S(1)}, bf16[272,384]{1,0:T(8,128)(2,1)S(1)}, u32[]{:S(2)}, u32[]{:S(2)}) collective-permute-start(bf16[272,384]{1,0:T(8,128)(2,1)S(1)} %combine.9.refs_0_), channel_id=1, source_target_pairs={{0,16},{1,17},{2,18},{3,19},{4,20},{5,21},{6,22},{7,23},{8,24},{9,... | collective-permute-start | bytes 626696 | tf_op jit(solution)/shard_map/ppermute | solution.py:683
  98.7 1.7 %collective-permute-start.28 = (bf16[256,384]{1,0:T(8,128)(2,1)S(1)}, bf16[256,384]{1,0:T(8,128)(2,1)S(1)}, u32[]{:S(2)}, u32[]{:S(2)}) collective-permute-start(bf16[256,384]{1,0:T(8,128)(2,1)S(1)} %get-tuple-element.114), channel_id=1, source_target_pairs={{0,4},{1,5},{2,6},{3,7},{4,0},{5,1},{6,2},{7,3},{8,12},{9,13},{10,... | collective-permute-start | bytes 589832 | tf_op jit(solution)/shard_map/ppermute | solution.py:683
  101.5 1.9 %place.1 = bf16[256,4096]{1,0:T(8,128)(2,1)} custom-call(s32[5]{0:T(128)S(1)} %stack.23.place, bf16[256,512]{1,0:T(8,128)(2,1)S(1)} %get-tuple-element.106.refs_6_.refs_0_, bf16[256,768]{1,0:T(8,128)(2,1)S(1)} %get-tuple-element.105.refs_2_.refs_1_, bf16[256,384]{1,0:T(8,128)(2,1)S(1)} %get-tuple-element.108.refs_6_.refs_2_, ...), custom_call_target="tpu_custom_call" | custom-call | flops 1 | bytes 1 | tf_op jit(solution)/shard_map/place/pallas_call | solution.py:620
  (73 shorter events, 23.4 us)
Async XLA Ops:
  2.5 2.1 %collective-permute-start = (bf16[64,2048]{1,0:T(8,128)(2,1)S(1)}, bf16[64,2048]{1,0:T(8,128)(2,1)S(1)}, u32[]{:S(2)}, u32[]{:S(2)}) collective-permute-start(bf16[64,2048]{1,0:T(8,128)(2,1)S(1)} %pack_first.1.order), channel_id=1, source_target_pairs={{0,4},{1,5},{2,6},{3,7},{4,0},{5,1},{6,2},{7,3},{8,12},{9,13},{10,... | collective-permute-start | bytes 786440 | tf_op jit(solution)/shard_map/ppermute | solution.py:683
  4.6 3.5 %collective-permute-start.4 = (bf16[64,8448]{1,0:T(8,128)(2,1)S(1)}, bf16[64,8448]{1,0:T(8,128)(2,1)S(1)}, u32[]{:S(2)}, u32[]{:S(2)}) collective-permute-start(bf16[64,8448]{1,0:T(8,128)(2,1)S(1)} %gate.3), channel_id=1, source_target_pairs={{0,4},{1,5},{2,6},{3,7},{4,0},{5,1},{6,2},{7,3},{8,12},{9,13},{10,... | collective-permute-start | bytes 3244040 | tf_op jit(solution)/shard_map/ppermute | solution.py:683
  5.7 12.4 %collective-permute-start.1 = (bf16[128,512]{1,0:T(8,128)(2,1)S(1)}, bf16[128,512]{1,0:T(8,128)(2,1)S(1)}, u32[]{:S(2)}, u32[]{:S(2)}) collective-permute-start(bf16[128,512]{1,0:T(8,128)(2,1)S(1)} %get-tuple-element.61), channel_id=1, source_target_pairs={{0,2},{1,3},{2,0},{3,1},{4,6},{5,7},{6,4},{7,5},{8,10},{9,11},{10,... | collective-permute-start | bytes 393224 | tf_op jit(solution)/shard_map/ppermute | solution.py:683
  8.7 6.0 %collective-permute-start.5 = (bf16[3,10240]{1,0:T(4,128)(2,1)S(1)}, bf16[3,10240]{1,0:T(4,128)(2,1)S(1)}, u32[]{:S(2)}, u32[]{:S(2)}) collective-permute-start(bf16[3,10240]{1,0:T(4,128)(2,1)S(1)} %edge.1), channel_id=1, source_target_pairs={{3,11},{7,15},{11,19},{15,23},{19,27},{23,31}} | collective-permute-start | bytes 184328 | tf_op jit(solution)/shard_map/ppermute | solution.py:683
  9.4 11.6 %collective-permute-start.2 = (bf16[128,512]{1,0:T(8,128)(2,1)S(1)}, bf16[128,512]{1,0:T(8,128)(2,1)S(1)}, u32[]{:S(2)}, u32[]{:S(2)}) collective-permute-start(bf16[128,512]{1,0:T(8,128)(2,1)S(1)} %get-tuple-element.62), channel_id=1, source_target_pairs={{0,3},{1,2},{2,1},{3,0},{4,7},{5,6},{6,5},{7,4},{8,11},{9,10},{10,... | collective-permute-start | bytes 393224 | tf_op jit(solution)/shard_map/ppermute | solution.py:683
  10.0 11.0 %collective-permute-start.3 = (bf16[128,512]{1,0:T(8,128)(2,1)S(1)}, bf16[128,512]{1,0:T(8,128)(2,1)S(1)}, u32[]{:S(2)}, u32[]{:S(2)}) collective-permute-start(bf16[128,512]{1,0:T(8,128)(2,1)S(1)} %get-tuple-element.63), channel_id=1, source_target_pairs={{0,1},{1,0},{2,3},{3,2},{4,5},{5,4},{6,7},{7,6},{8,9},{9,8},{10,11... | collective-permute-start | bytes 393224 | tf_op jit(solution)/shard_map/ppermute | solution.py:683
  15.7 9.8 %collective-permute-start.6 = (bf16[128,384]{1,0:T(8,128)(2,1)S(1)}, bf16[128,384]{1,0:T(8,128)(2,1)S(1)}, u32[]{:S(2)}, u32[]{:S(2)}) collective-permute-start(bf16[128,384]{1,0:T(8,128)(2,1)S(1)} %get-tuple-element.69), channel_id=1, source_target_pairs={{0,2},{1,3},{2,0},{3,1},{4,6},{5,7},{6,4},{7,5},{8,10},{9,11},{10,... | collective-permute-start | bytes 294920 | tf_op jit(solution)/shard_map/ppermute | solution.py:683
  18.1 9.9 %collective-permute-start.7 = (bf16[128,384]{1,0:T(8,128)(2,1)S(1)}, bf16[128,384]{1,0:T(8,128)(2,1)S(1)}, u32[]{:S(2)}, u32[]{:S(2)}) collective-permute-start(bf16[128,384]{1,0:T(8,128)(2,1)S(1)} %get-tuple-element.70), channel_id=1, source_target_pairs={{0,3},{1,2},{2,1},{3,0},{4,7},{5,6},{6,5},{7,4},{8,11},{9,10},{10,... | collective-permute-start | bytes 294920 | tf_op jit(solution)/shard_map/ppermute | solution.py:683
  18.1 9.8 %collective-permute-start.8 = (bf16[128,384]{1,0:T(8,128)(2,1)S(1)}, bf16[128,384]{1,0:T(8,128)(2,1)S(1)}, u32[]{:S(2)}, u32[]{:S(2)}) collective-permute-start(bf16[128,384]{1,0:T(8,128)(2,1)S(1)} %get-tuple-element.71), channel_id=1, source_target_pairs={{0,1},{1,0},{2,3},{3,2},{4,5},{5,4},{6,7},{7,6},{8,9},{9,8},{10,11... | collective-permute-start | bytes 294920 | tf_op jit(solution)/shard_map/ppermute | solution.py:683
  20.9 10.4 %copy-start.5 = (f32[256]{0:T(256)S(1)}, f32[256]{0:T(256)}, u32[]{:S(2)}) copy-start(f32[256]{0:T(256)} %param.11) | copy-start | bytes 3076
  20.9 10.4 %copy-start.6 = (f32[256]{0:T(256)S(1)}, f32[256]{0:T(256)}, u32[]{:S(2)}) copy-start(f32[256]{0:T(256)} %param.12) | copy-start | bytes 3076
  20.9 10.4 %copy-start.7 = (f32[256]{0:T(256)S(1)}, f32[256]{0:T(256)}, u32[]{:S(2)}) copy-start(f32[256]{0:T(256)} %param.13) | copy-start | bytes 3076
  27.9 24.9 %collective-permute-start.16 = (bf16[128,1792]{1,0:T(8,128)(2,1)S(1)}, bf16[128,1792]{1,0:T(8,128)(2,1)S(1)}, u32[]{:S(2)}, u32[]{:S(2)}) collective-permute-start(bf16[128,1792]{1,0:T(8,128)(2,1)S(1)} %get-tuple-element.90), channel_id=1, source_target_pairs={{0,1},{1,0},{2,3},{3,2},{4,5},{5,4},{6,7},{7,6},{8,9},{9,8},{10,11... | collective-permute-start | bytes 1376264 | tf_op jit(solution)/shard_map/ppermute | solution.py:683
  27.9 17.6 %collective-permute-start.12 = (bf16[128,768]{1,0:T(8,128)(2,1)S(1)}, bf16[128,768]{1,0:T(8,128)(2,1)S(1)}, u32[]{:S(2)}, u32[]{:S(2)}) collective-permute-start(bf16[128,768]{1,0:T(8,128)(2,1)S(1)} %get-tuple-element.86), channel_id=1, source_target_pairs={{0,2},{1,3},{2,0},{3,1},{4,6},{5,7},{6,4},{7,5},{8,10},{9,11},{10,... | collective-permute-start | bytes 589832 | tf_op jit(solution)/shard_map/ppermute | solution.py:683
  31.3 14.2 %collective-permute-start.13 = (bf16[128,768]{1,0:T(8,128)(2,1)S(1)}, bf16[128,768]{1,0:T(8,128)(2,1)S(1)}, u32[]{:S(2)}, u32[]{:S(2)}) collective-permute-start(bf16[128,768]{1,0:T(8,128)(2,1)S(1)} %get-tuple-element.87), channel_id=1, source_target_pairs={{0,3},{1,2},{2,1},{3,0},{4,7},{5,6},{6,5},{7,4},{8,11},{9,10},{10,... | collective-permute-start | bytes 589832 | tf_op jit(solution)/shard_map/ppermute | solution.py:683
  35.1 17.0 %collective-permute-start.9 = (bf16[272,256]{1,0:T(8,128)(2,1)S(1)}, bf16[272,256]{1,0:T(8,128)(2,1)S(1)}, u32[]{:S(2)}, u32[]{:S(2)}) collective-permute-start(bf16[272,256]{1,0:T(8,128)(2,1)S(1)} %get-tuple-element.77.refs_0_.refs_2_), channel_id=1, source_target_pairs={{0,8},{1,9},{2,10},{3,11},{4,12},{5,13},{6,14},{7,15},{8,0},{9,1},... | collective-permute-start | bytes 417800 | tf_op jit(solution)/shard_map/ppermute | solution.py:683
  38.4 13.7 %collective-permute-start.10 = (bf16[272,256]{1,0:T(8,128)(2,1)S(1)}, bf16[272,256]{1,0:T(8,128)(2,1)S(1)}, u32[]{:S(2)}, u32[]{:S(2)}) collective-permute-start(bf16[272,256]{1,0:T(8,128)(2,1)S(1)} %get-tuple-element.78.refs_1_.refs_3_), channel_id=1, source_target_pairs={{0,8},{1,9},{2,10},{3,11},{4,12},{5,13},{6,14},{7,15},{8,0},{9,1},... | collective-permute-start | bytes 417800 | tf_op jit(solution)/shard_map/ppermute | solution.py:683
  45.6 22.3 %collective-permute-start.14 = (bf16[128,1024]{1,0:T(8,128)(2,1)S(1)}, bf16[128,1024]{1,0:T(8,128)(2,1)S(1)}, u32[]{:S(2)}, u32[]{:S(2)}) collective-permute-start(bf16[128,1024]{1,0:T(8,128)(2,1)S(1)} %get-tuple-element.88), channel_id=1, source_target_pairs={{0,2},{1,3},{2,0},{3,1},{4,6},{5,7},{6,4},{7,5},{8,10},{9,11},{10,... | collective-permute-start | bytes 786440 | tf_op jit(solution)/shard_map/ppermute | solution.py:683
  50.0 23.6 %collective-permute-start.15 = (bf16[128,1024]{1,0:T(8,128)(2,1)S(1)}, bf16[128,1024]{1,0:T(8,128)(2,1)S(1)}, u32[]{:S(2)}, u32[]{:S(2)}) collective-permute-start(bf16[128,1024]{1,0:T(8,128)(2,1)S(1)} %get-tuple-element.89), channel_id=1, source_target_pairs={{0,3},{1,2},{2,1},{3,0},{4,7},{5,6},{6,5},{7,4},{8,11},{9,10},{10,... | collective-permute-start | bytes 786440 | tf_op jit(solution)/shard_map/ppermute | solution.py:683
  55.4 6.2 %collective-permute-start.17 = (bf16[272,384]{1,0:T(8,128)(2,1)S(1)}, bf16[272,384]{1,0:T(8,128)(2,1)S(1)}, u32[]{:S(2)}, u32[]{:S(2)}) collective-permute-start(bf16[272,384]{1,0:T(8,128)(2,1)S(1)} %get-tuple-element.91.refs_1_), channel_id=1, source_target_pairs={{0,8},{1,9},{2,10},{3,11},{4,12},{5,13},{6,14},{7,15},{8,0},{9,1},... | collective-permute-start | bytes 626696 | tf_op jit(solution)/shard_map/ppermute | solution.py:683
  58.9 7.0 %collective-permute-start.18 = (bf16[272,384]{1,0:T(8,128)(2,1)S(1)}, bf16[272,384]{1,0:T(8,128)(2,1)S(1)}, u32[]{:S(2)}, u32[]{:S(2)}) collective-permute-start(bf16[272,384]{1,0:T(8,128)(2,1)S(1)} %get-tuple-element.92.refs_1_), channel_id=1, source_target_pairs={{0,8},{1,9},{2,10},{3,11},{4,12},{5,13},{6,14},{7,15},{8,0},{9,1},... | collective-permute-start | bytes 626696 | tf_op jit(solution)/shard_map/ppermute | solution.py:683
  60.2 24.4 %collective-permute-start.11 = (bf16[272,512]{1,0:T(8,128)(2,1)S(1)}, bf16[272,512]{1,0:T(8,128)(2,1)S(1)}, u32[]{:S(2)}, u32[]{:S(2)}) collective-permute-start(bf16[272,512]{1,0:T(8,128)(2,1)S(1)} %combine.5.refs_10_), channel_id=1, source_target_pairs={{0,16},{1,17},{2,18},{3,19},{4,20},{5,21},{6,22},{7,23},{8,24},{9,... | collective-permute-start | bytes 835592 | tf_op jit(solution)/shard_map/ppermute | solution.py:683
  62.2 22.3 %collective-permute-start.20 = (bf16[272,384]{1,0:T(8,128)(2,1)S(1)}, bf16[272,384]{1,0:T(8,128)(2,1)S(1)}, u32[]{:S(2)}, u32[]{:S(2)}) collective-permute-start(bf16[272,384]{1,0:T(8,128)(2,1)S(1)} %combine.6.refs_2_.refs_10_), channel_id=1, source_target_pairs={{0,16},{1,17},{2,18},{3,19},{4,20},{5,21},{6,22},{7,23},{8,24},{9,... | collective-permute-start | bytes 626696 | tf_op jit(solution)/shard_map/ppermute | solution.py:683
  66.6 18.0 %collective-permute-start.21 = (bf16[272,384]{1,0:T(8,128)(2,1)S(1)}, bf16[272,384]{1,0:T(8,128)(2,1)S(1)}, u32[]{:S(2)}, u32[]{:S(2)}) collective-permute-start(bf16[272,384]{1,0:T(8,128)(2,1)S(1)} %combine.7.refs_11_), channel_id=1, source_target_pairs={{0,16},{1,17},{2,18},{3,19},{4,20},{5,21},{6,22},{7,23},{8,24},{9,... | collective-permute-start | bytes 626696 | tf_op jit(solution)/shard_map/ppermute | solution.py:683
  75.5 9.1 %collective-permute-start.22 = (bf16[272,384]{1,0:T(8,128)(2,1)S(1)}, bf16[272,384]{1,0:T(8,128)(2,1)S(1)}, u32[]{:S(2)}, u32[]{:S(2)}) collective-permute-start(bf16[272,384]{1,0:T(8,128)(2,1)S(1)} %get-tuple-element.93.refs_8_.refs_1_), channel_id=1, source_target_pairs={{0,8},{1,9},{2,10},{3,11},{4,12},{5,13},{6,14},{7,15},{8,0},{9,1},... | collective-permute-start | bytes 626696 | tf_op jit(solution)/shard_map/ppermute | solution.py:683
  82.0 7.1 %collective-permute-start.19 = (bf16[272,384]{1,0:T(8,128)(2,1)S(1)}, bf16[272,384]{1,0:T(8,128)(2,1)S(1)}, u32[]{:S(2)}, u32[]{:S(2)}) collective-permute-start(bf16[272,384]{1,0:T(8,128)(2,1)S(1)} %get-tuple-element.100.refs_0_.refs_1_), channel_id=1, source_target_pairs={{0,8},{1,9},{2,10},{3,11},{4,12},{5,13},{6,14},{7,15},{8,0},{9,1},... | collective-permute-start | bytes 626696 | tf_op jit(solution)/shard_map/ppermute | solution.py:683
  85.2 9.4 %collective-permute-start.23 = (bf16[272,384]{1,0:T(8,128)(2,1)S(1)}, bf16[272,384]{1,0:T(8,128)(2,1)S(1)}, u32[]{:S(2)}, u32[]{:S(2)}) collective-permute-start(bf16[272,384]{1,0:T(8,128)(2,1)S(1)} %combine.8.refs_12_), channel_id=1, source_target_pairs={{0,16},{1,17},{2,18},{3,19},{4,20},{5,21},{6,22},{7,23},{8,24},{9,... | collective-permute-start | bytes 626696 | tf_op jit(solution)/shard_map/ppermute | solution.py:683
  89.8 7.8 %collective-permute-start.24 = (bf16[272,384]{1,0:T(8,128)(2,1)S(1)}, bf16[272,384]{1,0:T(8,128)(2,1)S(1)}, u32[]{:S(2)}, u32[]{:S(2)}) collective-permute-start(bf16[272,384]{1,0:T(8,128)(2,1)S(1)} %combine.9.refs_0_), channel_id=1, source_target_pairs={{0,16},{1,17},{2,18},{3,19},{4,20},{5,21},{6,22},{7,23},{8,24},{9,... | collective-permute-start | bytes 626696 | tf_op jit(solution)/shard_map/ppermute | solution.py:683
  91.1 9.3 %collective-permute-start.26 = (bf16[256,768]{1,0:T(8,128)(2,1)S(1)}, bf16[256,768]{1,0:T(8,128)(2,1)S(1)}, u32[]{:S(2)}, u32[]{:S(2)}) collective-permute-start(bf16[256,768]{1,0:T(8,128)(2,1)S(1)} %get-tuple-element.112), channel_id=1, source_target_pairs={{0,4},{1,5},{2,6},{3,7},{4,0},{5,1},{6,2},{7,3},{8,12},{9,13},{10,... | collective-permute-start | bytes 1179656 | tf_op jit(solution)/shard_map/ppermute | solution.py:683
  94.6 5.8 %collective-permute-start.25 = (bf16[256,512]{1,0:T(8,128)(2,1)S(1)}, bf16[256,512]{1,0:T(8,128)(2,1)S(1)}, u32[]{:S(2)}, u32[]{:S(2)}) collective-permute-start(bf16[256,512]{1,0:T(8,128)(2,1)S(1)} %get-tuple-element.111), channel_id=1, source_target_pairs={{0,4},{1,5},{2,6},{3,7},{4,0},{5,1},{6,2},{7,3},{8,12},{9,13},{10,... | collective-permute-start | bytes 786440 | tf_op jit(solution)/shard_map/ppermute | solution.py:683
  95.8 4.6 %collective-permute-start.27 = (bf16[256,384]{1,0:T(8,128)(2,1)S(1)}, bf16[256,384]{1,0:T(8,128)(2,1)S(1)}, u32[]{:S(2)}, u32[]{:S(2)}) collective-permute-start(bf16[256,384]{1,0:T(8,128)(2,1)S(1)} %get-tuple-element.113), channel_id=1, source_target_pairs={{0,4},{1,5},{2,6},{3,7},{4,0},{5,1},{6,2},{7,3},{8,12},{9,13},{10,... | collective-permute-start | bytes 589832 | tf_op jit(solution)/shard_map/ppermute | solution.py:683
  98.7 2.8 %collective-permute-start.28 = (bf16[256,384]{1,0:T(8,128)(2,1)S(1)}, bf16[256,384]{1,0:T(8,128)(2,1)S(1)}, u32[]{:S(2)}, u32[]{:S(2)}) collective-permute-start(bf16[256,384]{1,0:T(8,128)(2,1)S(1)} %get-tuple-element.114), channel_id=1, source_target_pairs={{0,4},{1,5},{2,6},{3,7},{4,0},{5,1},{6,2},{7,3},{8,12},{9,13},{10,... | collective-permute-start | bytes 589832 | tf_op jit(solution)/shard_map/ppermute | solution.py:683
  (5 other events, 14.3 us)
